TPU v7x, 32 devices: a whole 2x2x4 slice. The times are simulated.
32 devices in a mesh: groups: 1, replica: 32 (over z, y, x, core).
Axes of the slice: x: 2, y: 2, z: 4, core: 2. Of those that a mesh axis runs over, the one named last changes fastest.
Arguments:
- queries: bfloat16 [8192, 1024], P(('groups', 'replica')), may hold values from -15 to 15
- suffix_kv: bfloat16 [8192, 256], P(('groups', 'replica')), may hold values from -6 to 6
- own_cache: bfloat16 [16384, 256], P(('groups', 'replica')), may hold values from -6 to 6
- ctx_len: int32 [32], P(('groups', 'replica')), may hold values from 64 to 512, as said below
- prefix_cache: bfloat16 [131072, 256], P(('groups', 'replica')), may hold values from -18 to 18
- owners: int32 [2], P('groups'), may hold values from 0 to 31, as said below
- readers: int32 [32], P('groups'), may hold values from 0 to 1
- kv_pool: bfloat16 [1024, 128, 256], P(('groups', 'replica')), may hold values from -6 to 6
- mig_target: int32 [32, 32], P(('groups', 'replica')), may hold values from 0 to 31, as said below
- mig_block: int32 [32, 32], P(('groups', 'replica')), may hold values from 0 to 31, each once within a row
- mig_count: int32 [32], P(('groups', 'replica')), may hold values from 8 to 32, as said below
Outputs:
- attended: bfloat16 [8192, 1024], P(('groups', 'replica'))
Inputs may be any that keep to these rules, and one draw needn't show every extreme that they name: `owners`: 2 different replicas; replica 32 - 1 owns one prefix in every draw. `ctx_len`: the largest value is 512 in every draw. `mig_target`: each row names every replica once, so one source sends at most one block to one target; in every draw one replica is the first entry of every row. `mig_block`: each row names every block of the source's pool once. `mig_count`: the largest value is 32 in every draw.
All inputs are finite; a program needn't handle non-finite values.
Results may differ from a plain program's by a relative error of at most 0.0019.
Values may be sent and summed in bfloat16 or wider, within the bound.
No kernel may reach another device: no remote copies, remote signals or barrier semaphores. Data moves between devices by JAX's collectives and lax.ppermute only.
A program may use at most 128 MiB of HBM per device.

v0:
```python
import jax
import jax.numpy as jnp
from jax import lax
from jax.sharding import PartitionSpec as P


def fold_block(carried, query_rows, key_value, allowed):
    running_max, denominator, numerator = carried
    head_size = key_value.shape[1] // 2
    scores = lax.dot_general(
        query_rows,
        key_value[:, :head_size],
        (((1,), (1,)), ((), ())),
        preferred_element_type=jnp.float32,
    ) * head_size ** (-0.5)
    scores = jnp.where(allowed, scores, -jnp.inf)
    new_max = jnp.maximum(running_max, jnp.max(scores, axis=1))
    shrink = jnp.exp(running_max - new_max)
    weights = jnp.exp(scores - new_max[:, None])
    denominator = denominator * shrink + jnp.sum(weights, axis=1)
    numerator = numerator * shrink[:, None] + jnp.dot(
        weights.astype(jnp.bfloat16), key_value[:, head_size:], preferred_element_type=jnp.float32
    )
    return (new_max, denominator, numerator)


def fold_keys(carried, query_rows, key_value, key_mask):
    key_count = key_value.shape[0]
    if key_count > 1024 and key_count % 1024 == 0:
        blocks = key_value.reshape(key_count // 1024, 1024, key_value.shape[1])
        mask_rows = key_mask.reshape(key_count // 1024, 1024)

        def step_block(partial_value, block_pair):
            return (
                fold_block(partial_value, query_rows, block_pair[0], block_pair[1][None, :]),
                None,
            )

        carried, unused = lax.scan(step_block, carried, (blocks, mask_rows))
        return carried
    return fold_block(carried, query_rows, key_value, key_mask[None, :])


def on_device(
    queries,
    suffix_kv,
    own_cache,
    ctx_len,
    prefix_cache,
    owners,
    readers,
    kv_pool,
    mig_target,
    mig_block,
    mig_count,
):
    replicas = lax.axis_size("replica")
    head_size = suffix_kv.shape[1] // 2
    head_count = queries.shape[1] // head_size
    query_rows = queries.reshape(-1, head_size)
    row_count = query_rows.shape[0]
    suffix_len = suffix_kv.shape[0]
    carried = (
        jnp.full((row_count,), -jnp.inf, jnp.float32),
        jnp.zeros((row_count,), jnp.float32),
        jnp.zeros((row_count, head_size), jnp.float32),
    )
    targets = mig_target[0]
    block_ids = mig_block[0]
    entry_live = jnp.arange(targets.shape[0], dtype=jnp.int32) < mig_count[0]
    matching = (targets[None, :] == jnp.arange(replicas, dtype=jnp.int32)[:, None]) & entry_live[
        None, :
    ]
    slot_ids = jnp.sum(jnp.where(matching, block_ids[None, :], 0), axis=1)
    slot_flags = jnp.any(matching, axis=1).astype(jnp.bfloat16)
    outgoing = kv_pool[slot_ids]
    arrived, arrived_flags = (
        lax.all_to_all(outgoing, "replica", split_axis=0, concat_axis=0, tiled=True),
        lax.all_to_all(slot_flags, "replica", split_axis=0, concat_axis=0, tiled=True),
    )
    pieces = prefix_cache.reshape(replicas, -1, prefix_cache.shape[1])
    spread = lax.all_to_all(pieces, "replica", split_axis=0, concat_axis=0, tiled=True)
    held = spread[owners]
    outgoing_pieces = held[readers]
    collected = lax.all_to_all(outgoing_pieces, "replica", split_axis=0, concat_axis=0, tiled=True)
    shared = collected.reshape(prefix_cache.shape)
    positions = jnp.arange(row_count, dtype=jnp.int32) // head_count
    causal = jnp.arange(suffix_len, dtype=jnp.int32)[None, :] <= positions[:, None]
    carried = fold_block(carried, query_rows, suffix_kv, causal)
    own_mask = jnp.arange(own_cache.shape[0], dtype=jnp.int32) < ctx_len[0]
    carried = fold_keys(carried, query_rows, own_cache, own_mask)
    moved_rows = arrived.reshape(-1, arrived.shape[2])
    moved_mask = jnp.repeat(arrived_flags > 0, arrived.shape[1])
    carried = fold_keys(carried, query_rows, moved_rows, moved_mask)
    carried = fold_keys(carried, query_rows, shared, jnp.ones((shared.shape[0],), bool))
    running_max, denominator, numerator = carried
    return (numerator / denominator[:, None]).astype(jnp.bfloat16).reshape(queries.shape)


def solution(mesh):
    in_specs = (
        P(("groups", "replica"), None),
        P(("groups", "replica"), None),
        P(("groups", "replica"), None),
        P(("groups", "replica")),
        P(("groups", "replica"), None),
        P("groups"),
        P("groups"),
        P(("groups", "replica"), None, None),
        P(("groups", "replica"), None),
        P(("groups", "replica"), None),
        P(("groups", "replica")),
    )
    out_specs = P(("groups", "replica"), None)
    return jax.shard_map(
        on_device, mesh=mesh, in_specs=in_specs, out_specs=out_specs, check_vma=False
    )
```

profile of v0, /device:TPU:0, one launch (start us, length us, event | category | flops | bytes accessed | tf_op | source)
XLA Modules:
  0.0 204.1 jit_solution(16879425851371043175)
XLA Ops:
  1.7 14.3 %all_to_all.21 = bf16[32,1,1]{2,1,0:T(2,128)(2,1)S(1)} all-to-all(bf16[32,1,1]{2,1,0:T(2,128)(2,1)S(1)} %copy.14), channel_id=1, replica_groups=mesh['groups'=1,'replica'=32] {'replica'}, dimensions={0} | all-to-all | bytes 128 | tf_op jit(solution)/shard_map/all_to_all | solution.py:79
  16.0 3.5 %all-to-all-start.2 = ((bf16[32,128,256]{2,1,0:T(8,128)(2,1)}), bf16[32,128,256]{2,1,0:T(8,128)(2,1)}, u32[]{:S(2)}, u32[]{:S(2)}) async-start(bf16[32,128,256]{2,1,0:T(8,128)(2,1)} %bitcast.36), calls=%async_computation.2 | async-start | bytes 4194304 | tf_op jit(solution)/shard_map/all_to_all | solution.py:82
  19.7 2.0 gather_fusion
  21.7 46.7 %all-to-all-done.2 = bf16[32,128,256]{2,1,0:T(8,128)(2,1)} async-done(((bf16[32,128,256]{2,1,0:T(8,128)(2,1)}), bf16[32,128,256]{2,1,0:T(8,128)(2,1)}, u32[]{:S(2)}, u32[]{:S(2)}) %all-to-all-start.2) | async-done | bytes 2097184 | tf_op jit(solution)/shard_map/all_to_all | solution.py:82
  68.4 4.0 %all-to-all-start.1 = ((bf16[32,128,256]{2,1,0:T(8,128)(2,1)}), bf16[32,128,256]{2,1,0:T(8,128)(2,1)}, u32[]{:S(2)}, u32[]{:S(2)}) async-start(bf16[32,128,256]{2,1,0:T(8,128)(2,1)} %gather_fusion), calls=%async_computation.1 | async-start | bytes 4194304 | tf_op jit(solution)/shard_map/all_to_all | solution.py:78
  76.8 2.3 %convolution_add_fusion = f32[2048,128]{1,0:T(8,128)} fusion(f32[2048,128]{1,0:T(8,128)S(1)} %fusion.31, f32[2048,512]{0,1:T(8,128)S(1)} %get-tuple-element.122, f32[2048]{0:T(1024)S(1)} %max.16, pred[512]{0:T(512)(128)(4,1)S(1)} %iota_compare_fusion.2, bf16[512,256]{1,0:T(8,128)(2,1)S(1)} %copy-done.6), kind=kOutput, calls=%fused_computation.42 | convolution fusion | flops 272891904 | bytes 6431232 | tf_op jit(solution)/shard_map/dot_general | solution.py:21
  80.0 2.1 %gather_fusion.1 = bf16[2,128,256]{2,1,0:T(8,128)(2,1)S(1)} fusion(bf16[32,128,256]{2,1,0:T(8,128)(2,1)} %all-to-all-done.2, s32[1024]{0:T(1024)S(1)} %pad_clamp_fusion.1), kind=kCustom, calls=%fused_computation.1 | custom fusion | bytes 262152 | tf_op jit(solution)/shard_map/gather | solution.py:83
  82.1 2.0 gather_fusion.2
  84.1 37.1 %all-to-all-done.1 = bf16[32,128,256]{2,1,0:T(8,128)(2,1)} async-done(((bf16[32,128,256]{2,1,0:T(8,128)(2,1)}), bf16[32,128,256]{2,1,0:T(8,128)(2,1)}, u32[]{:S(2)}, u32[]{:S(2)}) %all-to-all-start.1) | async-done | bytes 2097184 | tf_op jit(solution)/shard_map/all_to_all | solution.py:78
  121.3 4.3 %all-to-all-start.3 = ((bf16[32,128,256]{2,1,0:T(8,128)(2,1)}), bf16[32,128,256]{2,1,0:T(8,128)(2,1)}, u32[]{:S(2)}, u32[]{:S(2)}) async-start(bf16[32,128,256]{2,1,0:T(8,128)(2,1)} %gather_fusion.2), calls=%async_computation.3 | async-start | bytes 4194304 | tf_op jit(solution)/shard_map/all_to_all | solution.py:85
  125.6 34.7 %while.28 = (s32[]{:T(128)}, f32[2048]{0:T(1024)S(1)}, f32[2048]{0:T(1024)S(1)}, f32[2048,128]{1,0:T(8,128)}, pred[4,1024]{1,0:T(4,128)(4,1)S(1)}, /*index=5*/bf...) while((s32[]{:T(128)}, f32[2048]{0:T(1024)S(1)}, f32[2048]{0:T(1024)S(1)}, ...), condition=%wide.region_9.10_spmd, body=%wide.region_6.9_spmd.sunk | while | flops 1097338880 | bytes 37885076 | solution.py:39
  125.6 1.1 dynamic-slice_bitcast_fusion.4
  126.7 1.5 fusion.72
  128.3 2.5 %fusion.73 = f32[2048]{0:T(1024)S(1)} fusion(f32[1024,2048]{1,0:T(8,128)S(1)} %get-tuple-element.206, f32[2048]{0:T(1024)S(1)} %max.19, pred[1024]{0:T(1024)(128)(4,1)S(1)} %dynamic-slice_reduce_fusion.2), kind=kLoop, calls=%fused_computation.22.clone.1 | loop fusion | flops 8386560 | bytes 8406016 | tf_op jit(solution)/shard_map/while/body/eval_jaxpr/reduce_sum | solution.py:20
  130.8 2.5 %fusion.74 = f32[2048,128]{1,0:T(8,128)S(1)} fusion(f32[1024,2048]{1,0:T(8,128)S(1)} %get-tuple-element.206, f32[2048]{0:T(1024)S(1)} %max.19, pred[1024]{0:T(1024)(128)(4,1)S(1)} %dynamic-slice_reduce_fusion.2, f32[2048,128]{1,0:T(8,128)S(1)} %copy-done.1, f32[2048]{0:T(1024)S(1)} %get-tuple-element.208, ...), kind=kOutput, calls=%fused_computation.25.clone.1 | convolution fusion | flops 545783808 | bytes 10765312 | tf_op jit(solution)/shard_map/while/body/eval_jaxpr/dot_general | solution.py:21
  134.3 1.1 dynamic-slice_bitcast_fusion.4
  135.4 1.5 fusion.72
  136.9 2.5 %fusion.73 = f32[2048]{0:T(1024)S(1)} fusion(f32[1024,2048]{1,0:T(8,128)S(1)} %get-tuple-element.206, f32[2048]{0:T(1024)S(1)} %max.19, pred[1024]{0:T(1024)(128)(4,1)S(1)} %dynamic-slice_reduce_fusion.2), kind=kLoop, calls=%fused_computation.22.clone.1 | loop fusion | flops 8386560 | bytes 8406016 | tf_op jit(solution)/shard_map/while/body/eval_jaxpr/reduce_sum | solution.py:20
  139.5 2.5 %fusion.74 = f32[2048,128]{1,0:T(8,128)S(1)} fusion(f32[1024,2048]{1,0:T(8,128)S(1)} %get-tuple-element.206, f32[2048]{0:T(1024)S(1)} %max.19, pred[1024]{0:T(1024)(128)(4,1)S(1)} %dynamic-slice_reduce_fusion.2, f32[2048,128]{1,0:T(8,128)S(1)} %copy-done.1, f32[2048]{0:T(1024)S(1)} %get-tuple-element.208, ...), kind=kOutput, calls=%fused_computation.25.clone.1 | convolution fusion | flops 545783808 | bytes 10765312 | tf_op jit(solution)/shard_map/while/body/eval_jaxpr/dot_general | solution.py:21
  141.9 1.0 copy-done.2
  142.9 1.1 dynamic-slice_bitcast_fusion.4
  144.0 1.5 fusion.72
  145.6 2.5 %fusion.73 = f32[2048]{0:T(1024)S(1)} fusion(f32[1024,2048]{1,0:T(8,128)S(1)} %get-tuple-element.206, f32[2048]{0:T(1024)S(1)} %max.19, pred[1024]{0:T(1024)(128)(4,1)S(1)} %dynamic-slice_reduce_fusion.2), kind=kLoop, calls=%fused_computation.22.clone.1 | loop fusion | flops 8386560 | bytes 8406016 | tf_op jit(solution)/shard_map/while/body/eval_jaxpr/reduce_sum | solution.py:20
  148.1 2.5 %fusion.74 = f32[2048,128]{1,0:T(8,128)S(1)} fusion(f32[1024,2048]{1,0:T(8,128)S(1)} %get-tuple-element.206, f32[2048]{0:T(1024)S(1)} %max.19, pred[1024]{0:T(1024)(128)(4,1)S(1)} %dynamic-slice_reduce_fusion.2, f32[2048,128]{1,0:T(8,128)S(1)} %copy-done.1, f32[2048]{0:T(1024)S(1)} %get-tuple-element.208, ...), kind=kOutput, calls=%fused_computation.25.clone.1 | convolution fusion | flops 545783808 | bytes 10765312 | tf_op jit(solution)/shard_map/while/body/eval_jaxpr/dot_general | solution.py:21
  151.6 1.1 dynamic-slice_bitcast_fusion.4
  152.7 1.6 fusion.72
  154.3 2.5 %fusion.73 = f32[2048]{0:T(1024)S(1)} fusion(f32[1024,2048]{1,0:T(8,128)S(1)} %get-tuple-element.206, f32[2048]{0:T(1024)S(1)} %max.19, pred[1024]{0:T(1024)(128)(4,1)S(1)} %dynamic-slice_reduce_fusion.2), kind=kLoop, calls=%fused_computation.22.clone.1 | loop fusion | flops 8386560 | bytes 8406016 | tf_op jit(solution)/shard_map/while/body/eval_jaxpr/reduce_sum | solution.py:20
  156.8 2.5 %fusion.74 = f32[2048,128]{1,0:T(8,128)S(1)} fusion(f32[1024,2048]{1,0:T(8,128)S(1)} %get-tuple-element.206, f32[2048]{0:T(1024)S(1)} %max.19, pred[1024]{0:T(1024)(128)(4,1)S(1)} %dynamic-slice_reduce_fusion.2, f32[2048,128]{1,0:T(8,128)S(1)} %copy-done.1, f32[2048]{0:T(1024)S(1)} %get-tuple-element.208, ...), kind=kOutput, calls=%fused_computation.25.clone.1 | convolution fusion | flops 545783808 | bytes 10765312 | tf_op jit(solution)/shard_map/while/body/eval_jaxpr/dot_general | solution.py:21
  160.3 14.1 %all-to-all-done.3 = bf16[32,128,256]{2,1,0:T(8,128)(2,1)} async-done(((bf16[32,128,256]{2,1,0:T(8,128)(2,1)}), bf16[32,128,256]{2,1,0:T(8,128)(2,1)}, u32[]{:S(2)}, u32[]{:S(2)}) %all-to-all-start.3) | async-done | bytes 2097184 | tf_op jit(solution)/shard_map/all_to_all | solution.py:85
  174.3 27.1 %while.29 = (s32[]{:T(128)}, f32[2048]{0:T(1024)S(1)}, f32[2048]{0:T(1024)S(1)}, f32[2048,128]{1,0:T(8,128)}, bf16[4,1024,256]{2,1,0:T(8,128)(2,1)}, /*index=5*/bf16[2048,128]{1,0:T(8,128)(2,1)S(1)}, s32[]{:T(128)}) while((s32[]{:T(128)}, f32[2048]{0:T(1024)S(1)}, f32[2048]{0:T(1024)S(1)}, f32[2048,128]{1,0:T(8,128)}, ...), condition=%wide.region_13.14_spmd, body=%wide.region_10.13_spmd.sunk | while | flops 1091047424 | bytes 37879944 | solution.py:39
  174.3 1.1 dynamic-slice_bitcast_fusion.5
  175.4 1.3 multiply_reduce_fusion.2
  176.7 1.4 fusion.78
  178.1 2.0 fusion.79
  181.1 1.1 dynamic-slice_bitcast_fusion.5
  182.2 1.3 multiply_reduce_fusion.2
  183.5 1.4 fusion.78
  184.9 2.0 fusion.79
  187.9 1.1 dynamic-slice_bitcast_fusion.5
  189.0 1.3 multiply_reduce_fusion.2
  190.3 1.4 fusion.78
  191.7 2.0 fusion.79
  194.7 1.1 dynamic-slice_bitcast_fusion.5
  195.8 1.3 multiply_reduce_fusion.2
  197.1 1.4 fusion.78
  198.5 2.0 fusion.79
  201.5 1.6 divide_convert_fusion
  203.1 1.0 reshape.83
  (100 shorter events, 12.8 us)
Async XLA Ops:
  0.0 19.6 %copy-start = (bf16[32,128,256]{2,1,0:T(8,128)(2,1)S(1)}, bf16[32,128,256]{2,1,0:T(8,128)(2,1)}, u32[]{:S(2)}) copy-start(bf16[32,128,256]{2,1,0:T(8,128)(2,1)} %param.22) | copy-start | bytes 6291460
  0.0 19.5 %copy-start.8 = (s32[1,32]{1,0:T(1,128)S(1)}, s32[1,32]{1,0:T(1,128)}, u32[]{:S(2)}) copy-start(s32[1,32]{1,0:T(1,128)} %param.23) | copy-start | bytes 388
  0.0 19.5 %copy-start.9 = (s32[1,32]{1,0:T(1,128)S(1)}, s32[1,32]{1,0:T(1,128)}, u32[]{:S(2)}) copy-start(s32[1,32]{1,0:T(1,128)} %param.24) | copy-start | bytes 388
  16.0 52.4 %all-to-all-start.2 = ((bf16[32,128,256]{2,1,0:T(8,128)(2,1)}), bf16[32,128,256]{2,1,0:T(8,128)(2,1)}, u32[]{:S(2)}, u32[]{:S(2)}) async-start(bf16[32,128,256]{2,1,0:T(8,128)(2,1)} %bitcast.36), calls=%async_computation.2 | async-start | bytes 4194304 | tf_op jit(solution)/shard_map/all_to_all | solution.py:82
  19.6 52.8 %copy-start.5 = (bf16[256,1024]{1,0:T(8,128)(2,1)S(1)}, bf16[256,1024]{1,0:T(8,128)(2,1)}, u32[]{:S(2)}) copy-start(bf16[256,1024]{1,0:T(8,128)(2,1)} %param.15) | copy-start | bytes 1572868
  19.7 53.7 %copy-start.7 = (bf16[256,256]{1,0:T(8,128)(2,1)S(1)}, bf16[256,256]{1,0:T(8,128)(2,1)}, u32[]{:S(2)}) copy-start(bf16[256,256]{1,0:T(8,128)(2,1)} %param.16) | copy-start | bytes 393220
  21.7 52.1 %copy-start.6 = (bf16[512,256]{1,0:T(8,128)(2,1)S(1)}, bf16[512,256]{1,0:T(8,128)(2,1)}, u32[]{:S(2)}) copy-start(bf16[512,256]{1,0:T(8,128)(2,1)} %param.17) | copy-start | bytes 786436
  68.4 52.9 %all-to-all-start.1 = ((bf16[32,128,256]{2,1,0:T(8,128)(2,1)}), bf16[32,128,256]{2,1,0:T(8,128)(2,1)}, u32[]{:S(2)}, u32[]{:S(2)}) async-start(bf16[32,128,256]{2,1,0:T(8,128)(2,1)} %gather_fusion), calls=%async_computation.1 | async-start | bytes 4194304 | tf_op jit(solution)/shard_map/all_to_all | solution.py:78
  72.6 1.9 copy-start.10
  72.6 2.0 copy-start.11
  121.3 53.1 %all-to-all-start.3 = ((bf16[32,128,256]{2,1,0:T(8,128)(2,1)}), bf16[32,128,256]{2,1,0:T(8,128)(2,1)}, u32[]{:S(2)}, u32[]{:S(2)}) async-start(bf16[32,128,256]{2,1,0:T(8,128)(2,1)} %gather_fusion.2), calls=%async_computation.3 | async-start | bytes 4194304 | tf_op jit(solution)/shard_map/all_to_all | solution.py:85
  128.3 2.5 %copy-start.1 = (f32[2048,128]{1,0:T(8,128)S(1)}, f32[2048,128]{1,0:T(8,128)}, u32[]{:S(2)}) copy-start(f32[2048,128]{1,0:T(8,128)} %get-tuple-element.230) | copy-start | bytes 3145732 | tf_op jit(solution)/shard_map/while
  133.3 1.0 copy-start.2
  136.9 2.5 %copy-start.1 = (f32[2048,128]{1,0:T(8,128)S(1)}, f32[2048,128]{1,0:T(8,128)}, u32[]{:S(2)}) copy-start(f32[2048,128]{1,0:T(8,128)} %get-tuple-element.230) | copy-start | bytes 3145732 | tf_op jit(solution)/shard_map/while
  141.9 1.0 copy-start.2
  145.6 2.5 %copy-start.1 = (f32[2048,128]{1,0:T(8,128)S(1)}, f32[2048,128]{1,0:T(8,128)}, u32[]{:S(2)}) copy-start(f32[2048,128]{1,0:T(8,128)} %get-tuple-element.230) | copy-start | bytes 3145732 | tf_op jit(solution)/shard_map/while
  150.6 1.0 copy-start.2
  154.3 2.5 %copy-start.1 = (f32[2048,128]{1,0:T(8,128)S(1)}, f32[2048,128]{1,0:T(8,128)}, u32[]{:S(2)}) copy-start(f32[2048,128]{1,0:T(8,128)} %get-tuple-element.230) | copy-start | bytes 3145732 | tf_op jit(solution)/shard_map/while
  159.2 1.0 copy-start.2
  176.7 1.4 copy-start.3
  180.1 1.0 copy-start.4
  183.5 1.4 copy-start.3
  186.9 1.0 copy-start.4
  190.3 1.4 copy-start.3
  193.7 1.0 copy-start.4
  197.1 1.4 copy-start.3
  200.5 1.0 copy-start.4
where the time goes:
time: 205 us; the launch traced here: 204 us
  waiting for transfers between devices  97.9 us (48%)
  matrix products  33.3 us (16%)
  local copies, waits for them, and re-layouts  24.5 us (12%)
  other arithmetic  20 us (10%)
  blocking collectives  14.3 us (7%)
  starting transfers between devices  11.8 us (6%)
    all_to_all x1, waiting for transfers between devices, on_device(): lax.all_to_all(pieces, 'replica', split_axis=0, concat_axis=0, tiled=True)  46.7 us
    all_to_all x1, waiting for transfers between devices, on_device(): lax.all_to_all(outgoing, 'replica', split_axis=0, concat_axis=0, tiled=True)  37.1 us
    dot_general x10, matrix products, fold_block(): jnp.dot(weights.astype(jnp.bfloat16), key_value[:, head_size:], preferred...  20.9 us
    reduce_sum x10, other arithmetic, fold_block(): denominator = denominator * shrink + jnp.sum(weights, axis=1)  16.7 us
    all_to_all x1, blocking collectives, on_device(): lax.all_to_all(slot_flags, 'replica', split_axis=0, concat_axis=0, tiled=...  14.3 us
    all_to_all x1, waiting for transfers between devices, on_device(): lax.all_to_all(outgoing_pieces, 'replica', split_axis=0, concat_axis=0, t...  14.1 us
    dot_general x10, matrix products, fold_block(): lax.dot_general(query_rows, key_value[:, :head_size], (((1,), (1,)), ((),...  12.4 us
    squeeze x8, local copies, waits for them, and re-layouts, fold_keys(): carried, unused = lax.scan(step_block, carried, (blocks, mask_rows))  8.62 us
  transfers between devices with their start and end apart: 3, of which 3 were waited for; matrix products, arithmetic and copies ran while one was open for 21% of the time, Pallas kernels for 0%

commit v1 on v0

v1 whole, which is shorter than its diff:
```python
import functools

import jax
import jax.numpy as jnp
from jax import lax
from jax.experimental import pallas as pl
from jax.experimental.pallas import tpu as pltpu
from jax.sharding import PartitionSpec as P

LOG2E = 1.4426950408889634
DEAD_MARK = 1024.0
DEAD_ABOVE = 512.0
NEG = -1e30
VMEM_BYTES = 40 * 1024 * 1024


def fold_keys(q_ref, m_ref, acc_ref, keys, values, factor, mask=None):
    heads, tokens, width = acc_ref.shape
    size = keys.shape[1]
    for head in range(heads):
        rows = q_ref[:, head * size:(head + 1) * size]
        scores = lax.dot_general(
            rows, keys, (((1,), (1,)), ((), ())), preferred_element_type=jnp.float32
        )
        if mask is not None:
            scores = jnp.where(mask, scores, NEG)
        old_max = m_ref[head]
        new_max = jnp.maximum(old_max, jnp.max(scores, axis=1, keepdims=True))
        shrink = jnp.exp2((old_max - new_max) * factor)
        weights = jnp.exp2((scores - jnp.tile(new_max, (1, keys.shape[0] // size))) * factor)
        m_ref[head] = new_max
        acc_ref[head] = acc_ref[head] * jnp.tile(shrink, (1, width // size)) + jnp.dot(
            weights.astype(jnp.bfloat16), values, preferred_element_type=jnp.float32
        )


def finish(acc_ref, out_ref):
    heads, tokens, width = acc_ref.shape
    size = width // 2
    for head in range(heads):
        out_ref[:, head * size:(head + 1) * size] = (
            acc_ref[head, :, :size] / acc_ref[head, :, size:]
        ).astype(out_ref.dtype)


def local_kernel(factor, len_ref, q_ref, suffix_ref, own_ref, m_ref, acc_ref, values_ref):
    size = q_ref.shape[1] // acc_ref.shape[0]
    suffix = suffix_ref.shape[0]
    own = own_ref.shape[0]
    m_ref[...] = jnp.full(m_ref.shape, NEG, jnp.float32)
    acc_ref[...] = jnp.zeros(acc_ref.shape, jnp.float32)
    values_ref[:suffix, :size] = suffix_ref[:, size:]
    values_ref[:suffix, size:] = jnp.ones((suffix, size), jnp.bfloat16)
    causal = lax.broadcasted_iota(jnp.int32, (suffix, suffix), 1) <= lax.broadcasted_iota(
        jnp.int32, (suffix, suffix), 0
    )
    fold_keys(
        q_ref, m_ref, acc_ref, suffix_ref[:, :size], values_ref[:suffix, :], factor, causal
    )
    live = lax.broadcasted_iota(jnp.int32, (own, size), 0) < len_ref[0]
    zeros = jnp.zeros((own, size), jnp.float32)
    spare = jnp.broadcast_to(suffix_ref[:1, :size].astype(jnp.float32), (own, size))
    keys = jnp.where(live, own_ref[:, :size].astype(jnp.float32), spare).astype(jnp.bfloat16)
    values_ref[:own, :size] = jnp.where(
        live, own_ref[:, size:].astype(jnp.float32), zeros
    ).astype(jnp.bfloat16)
    values_ref[:own, size:] = jnp.where(live, 1.0, zeros).astype(jnp.bfloat16)
    fold_keys(q_ref, m_ref, acc_ref, keys, values_ref[:own, :], factor)


def prefix_kernel(factor, which_ref, q_ref, kv_ref, m_in, acc_in, m_ref, acc_ref, values_ref):
    size = q_ref.shape[1] // acc_ref.shape[0]

    @pl.when(pl.program_id(0) == 0)
    def _():
        m_ref[...] = m_in[...]
        acc_ref[...] = acc_in[...]

    values_ref[:, :size] = kv_ref[:, size:]
    values_ref[:, size:] = jnp.ones((kv_ref.shape[0], size), jnp.bfloat16)
    fold_keys(q_ref, m_ref, acc_ref, kv_ref[:, :size], values_ref[...], factor)


def moved_kernel(
    factor, q_ref, kv_ref, suffix_ref, m_in, acc_in, out_ref, m_ref, acc_ref, keys_ref, values_ref
):
    size = q_ref.shape[1] // acc_ref.shape[0]

    @pl.when(pl.program_id(0) == 0)
    def _():
        m_ref[...] = m_in[...]
        acc_ref[...] = acc_in[...]

    rows = kv_ref[...].reshape(-1, kv_ref.shape[-1]).astype(jnp.float32)
    live = jnp.broadcast_to(rows[:, size:size + 1] < DEAD_ABOVE, (rows.shape[0], size))
    zeros = jnp.zeros((rows.shape[0], size), jnp.float32)
    spare = jnp.broadcast_to(suffix_ref[:1, :size].astype(jnp.float32), zeros.shape)
    keys_ref[...] = jnp.where(live, rows[:, :size], spare).astype(jnp.bfloat16)
    values_ref[:, :size] = jnp.where(live, rows[:, size:], zeros).astype(jnp.bfloat16)
    values_ref[:, size:] = jnp.where(live, 1.0, zeros).astype(jnp.bfloat16)
    fold_keys(q_ref, m_ref, acc_ref, keys_ref[...], values_ref[...], factor)

    @pl.when(pl.program_id(0) == pl.num_programs(0) - 1)
    def _():
        finish(acc_ref, out_ref)


def whole(shape):
    return pl.BlockSpec(shape, lambda *args: (0,) * len(shape))


def cost(rows, keys, size):
    return pl.CostEstimate(
        flops=6 * rows * keys * size, bytes_accessed=4 * keys * size, transcendentals=rows * keys
    )


def on_device(
    queries,
    suffix_kv,
    own_cache,
    ctx_len,
    prefix_cache,
    owners,
    readers,
    kv_pool,
    mig_target,
    mig_block,
    mig_count,
):
    replicas = lax.axis_size("replica")
    me = lax.axis_index("replica")
    size = suffix_kv.shape[1] // 2
    tokens = queries.shape[0]
    heads = queries.shape[1] // size
    prefixes = owners.shape[0]
    factor = size ** (-0.5) * LOG2E
    row_count = tokens * heads
    state = (
        jax.ShapeDtypeStruct((heads, tokens, size), jnp.float32),
        jax.ShapeDtypeStruct((heads, tokens, 2 * size), jnp.float32),
    )
    state_specs = (whole(state[0].shape), whole(state[1].shape))
    params = pltpu.CompilerParams(vmem_limit_bytes=VMEM_BYTES)

    targets = mig_target[0]
    entry_live = jnp.arange(targets.shape[0], dtype=jnp.int32) < mig_count[0]
    matching = (targets[None, :] == jnp.arange(replicas, dtype=jnp.int32)[:, None]) & entry_live[
        None, :
    ]
    slot_ids = jnp.sum(jnp.where(matching, mig_block[0][None, :], 0), axis=1)
    slot_live = jnp.any(matching, axis=1)
    outgoing = jnp.where(
        slot_live[:, None, None], kv_pool[slot_ids], jnp.asarray(DEAD_MARK, kv_pool.dtype)
    )
    arrived = lax.all_to_all(outgoing, "replica", split_axis=0, concat_axis=0, tiled=True)

    offered = jnp.where(
        (owners == me)[:, None, None], prefix_cache[None], jnp.zeros((), prefix_cache.dtype)
    )
    shared = lax.psum(offered, "replica")

    state_now = pl.pallas_call(
        functools.partial(local_kernel, factor),
        out_shape=state,
        in_specs=[
            pl.BlockSpec(memory_space=pltpu.SMEM),
            whole(queries.shape),
            whole(suffix_kv.shape),
            whole(own_cache.shape),
        ],
        out_specs=state_specs,
        grid=(1,),
        scratch_shapes=[
            pltpu.VMEM((max(tokens, own_cache.shape[0]), 2 * size), jnp.bfloat16)
        ],
        compiler_params=params,
        cost_estimate=cost(row_count, tokens + own_cache.shape[0], size),
        name="local_keys",
    )(ctx_len, queries, suffix_kv, own_cache)

    rows = min(1024, shared.shape[1])
    state_now = pl.pallas_call(
        functools.partial(prefix_kernel, factor),
        out_shape=state,
        grid_spec=pltpu.PrefetchScalarGridSpec(
            num_scalar_prefetch=1,
            grid=(shared.shape[1] // rows,),
            in_specs=[
                whole(queries.shape),
                pl.BlockSpec((None, rows, 2 * size), lambda i, which: (which[0], i, 0)),
                *state_specs,
            ],
            out_specs=state_specs,
            scratch_shapes=[pltpu.VMEM((rows, 2 * size), jnp.bfloat16)],
        ),
        compiler_params=params,
        cost_estimate=cost(row_count, shared.shape[1], size),
        name="prefix_keys",
    )(readers[me][None], queries, shared, *state_now)

    rows = arrived.shape[1]
    group = max(1, 1024 // rows)
    return pl.pallas_call(
        functools.partial(moved_kernel, factor),
        out_shape=jax.ShapeDtypeStruct(queries.shape, queries.dtype),
        grid=(replicas // group,),
        in_specs=[
            whole(queries.shape),
            pl.BlockSpec((group, rows, 2 * size), lambda i: (i, 0, 0)),
            whole(suffix_kv.shape),
            *state_specs,
        ],
        out_specs=whole(queries.shape),
        scratch_shapes=[
            pltpu.VMEM(state[0].shape, jnp.float32),
            pltpu.VMEM(state[1].shape, jnp.float32),
            pltpu.VMEM((group * rows, size), jnp.bfloat16),
            pltpu.VMEM((group * rows, 2 * size), jnp.bfloat16),
        ],
        compiler_params=params,
        cost_estimate=cost(row_count, replicas * rows, size),
        name="moved_keys",
    )(queries, arrived, suffix_kv, *state_now)


def solution(mesh):
    in_specs = (
        P(("groups", "replica"), None),
        P(("groups", "replica"), None),
        P(("groups", "replica"), None),
        P(("groups", "replica")),
        P(("groups", "replica"), None),
        P("groups"),
        P("groups"),
        P(("groups", "replica"), None, None),
        P(("groups", "replica"), None),
        P(("groups", "replica"), None),
        P(("groups", "replica")),
    )
    out_specs = P(("groups", "replica"), None)
    return jax.shard_map(
        on_device, mesh=mesh, in_specs=in_specs, out_specs=out_specs, check_vma=False
    )
```

time: 205 us -> 243 us (1.19)
  waiting for transfers between devices: 97.9 us -> 166 us
  matrix products: 33.3 us -> 0 us
  Pallas kernels: 0 us -> 30 us
  blocking collectives: 14.3 us -> 0 us
  between operations: 1.73 us -> 15 us
  other arithmetic: 20 us -> 8.67 us
  local copies, waits for them, and re-layouts: 24.5 us -> 15.1 us
  starting transfers between devices: 11.8 us -> 7.47 us
    psum x0 -> x1, waiting for transfers between devices: none -> 166 us  [on_device(): shared = lax.psum(offered, 'replica')]
    all_to_all x2 -> x0, waiting for transfers between devices: 60.8 us -> none  [the longest x1 46.7 us: on_device(): lax.all_to_all(pieces, 'replica', split_axis=0, concat_axis=0, tiled=True)]
    all_to_all x1, waiting for transfers between devices: 37.1 us -> 0.01 us  [on_device(): lax.all_to_all(outgoing, 'replica', split_axis=0, concat_axis=0, tiled=True)]
    dot_general x20 -> x0, matrix products: 33.3 us -> none  [the longest x10 20.9 us: fold_block(): jnp.dot(weights.astype(jnp.bfloat16), key_value[:, head_size:], preferred...]
    pallas_call x0 -> x3, Pallas kernels: none -> 30 us  [the longest x1 14.6 us: on_device(): pl.pallas_call(functools.partial(moved_kernel, factor), out_shape=jax.Sha...]
    reduce_sum x11 -> x1, other arithmetic: 16.8 us -> 0.79 us  [on_device(): slot_ids = jnp.sum(jnp.where(matching, mig_block[0][None, :], 0), axis=1)]
    all_to_all x1 -> x0, blocking collectives: 14.3 us -> none  [on_device(): lax.all_to_all(slot_flags, 'replica', split_axis=0, concat_axis=0, tiled=...]
    unnamed x18 -> x30, local copies, waits for them, and re-layouts: 0.13 us -> 12.5 us
  transfers between devices with their start and end apart: 3 -> 2, of which waited for: 3 -> 1; matrix products, arithmetic and copies ran while one was open for 21% -> 2% of each run, Pallas kernels for 0% -> 6%
where the time goes in v1:
time: 243 us
  waiting for transfers between devices  166 us (68%)
  Pallas kernels  30 us (12%)
  local copies, waits for them, and re-layouts  15.1 us (6%)
  between operations  15 us (6%)
  other arithmetic  8.67 us (4%)
  starting transfers between devices  7.47 us (3%)
    psum x1, waiting for transfers between devices, on_device(): shared = lax.psum(offered, 'replica')  166 us
    pallas_call x1, Pallas kernels, on_device(): pl.pallas_call(functools.partial(moved_kernel, factor), out_shape=jax.Sha...  14.6 us
    pallas_call x1, Pallas kernels, on_device(): pl.pallas_call(functools.partial(prefix_kernel, factor), out_shape=state,...  12.9 us
    unnamed x30, local copies, waits for them, and re-layouts  12.5 us
    all_to_all x1, starting transfers between devices, on_device(): lax.all_to_all(outgoing, 'replica', split_axis=0, concat_axis=0, tiled=True)  7.43 us
  transfers between devices with their start and end apart: 2, of which 1 were waited for; matrix products, arithmetic and copies ran while one was open for 2% of the time, Pallas kernels for 6%

profile of v1, /device:TPU:0, one launch (start us, length us, event | category | flops | bytes accessed | tf_op | source)
XLA Modules:
  0.0 242.6 jit_solution(14817230881668799333)
XLA Ops:
  6.5 0.0 copy-start
  7.4 0.8 fusion.1
  8.1 0.8 select_reduce_fusion
  8.9 0.0 copy-done
  8.9 2.0 gather_fusion
  11.0 3.2 %broadcast_select_fusion.1 = bf16[32,128,256]{2,1,0:T(8,128)(2,1)} fusion(bf16[32,128,256]{2,1,0:T(8,128)(2,1)} %gather_fusion, pred[32]{0:T(512)(128)(4,1)S(1)} %fusion.1), kind=kLoop, calls=%fused_computation.2 | loop fusion | flops 1048576 | bytes 4194336 | tf_op jit(solution)/shard_map/jit(_where)/select_n | solution.py:153
  14.1 0.0 copy-start.13
  14.1 7.4 %all-to-all-start = ((bf16[32,128,256]{2,1,0:T(8,128)(2,1)}), bf16[32,128,256]{2,1,0:T(8,128)(2,1)}, u32[]{:S(2)}, u32[]{:S(2)}) async-start(bf16[32,128,256]{2,1,0:T(8,128)(2,1)} %broadcast_select_fusion.1), calls=%async_computation | async-start | bytes 4194304 | tf_op jit(solution)/shard_map/all_to_all | solution.py:156
  21.6 0.0 all-reduce.2.cloned.1.call-start
  21.6 0.0 copy-done.13
  21.6 3.9 %broadcast_select_fusion = bf16[2,4096,256]{2,1,0:T(8,128)(2,1)} fusion(pred[2]{0:T(512)(128)(4,1)S(1)} %broadcast_compare_fusion, bf16[4096,256]{1,0:T(8,128)(2,1)} %param.15), kind=kLoop, calls=%fused_computation.1 | loop fusion | flops 2097152 | bytes 6291458 | tf_op jit(solution)/shard_map/jit(_where)/select_n | solution.py:158
  25.6 0.0 copy-start.14
  25.6 0.0 copy-start.2
  25.6 0.0 copy-start.3
  25.6 0.0 copy-start.4
  25.6 0.0 all-reduce.2.cloned.1.call-update
  26.3 0.0 copy-done.14
  26.3 0.6 dynamic_slice.3.which_ref
  26.9 0.0 copy-done.2
  26.9 0.0 copy-done.3
  26.9 0.0 copy-done.4
  26.9 2.5 %local_keys.1 = (f32[8,256,128]{2,1,0:T(8,128)S(1)}, f32[8,256,256]{2,1,0:T(8,128)S(1)}) custom-call(s32[1]{0:T(128)S(6)} %copy.13.len_ref, bf16[256,1024]{1,0:T(8,128)(2,1)S(1)} %copy-done.2, bf16[256,256]{1,0:T(8,128)(2,1)S(1)} %copy-done.4, bf16[512,256]{1,0:T(8,128)(2,1)S(1)} %copy-done.3), custom_call_target="tpu_custom_call" | custom-call | flops 1207959552 | bytes 393216 | tf_op jit(solution)/shard_map/local_keys/pallas_call | solution.py:163
  29.4 0.0 copy-start.5
  29.4 1.3 copy-done.5
  30.8 0.0 copy-start.7
  30.8 1.0 copy-done.7
  31.7 166.4 %all-reduce.2.cloned.1.call-done.kv_ref = bf16[2,4096,256]{2,1,0:T(8,128)(2,1)} async-done(((bf16[2,4096,256]{2,1,0:T(8,128)(2,1)}), bf16[2,4096,256]{2,1,0:T(8,128)(2,1)}) %all-reduce.2.cloned.1.call-update) | async-done | bytes 4194320 | tf_op jit(solution)/shard_map/psum | solution.py:161
  198.2 0.0 copy-start.1
  198.2 2.2 copy-done.1
  200.3 0.0 copy-start.6
  200.3 1.6 copy-done.6
  201.9 0.0 copy-start.8
  201.9 1.2 copy-done.8
  203.2 12.9 %prefix_keys.1 = (f32[8,256,128]{2,1,0:T(8,128)S(1)}, f32[8,256,256]{2,1,0:T(8,128)S(1)}) custom-call(s32[1]{0:T(128)} %dynamic_slice.3.which_ref, bf16[256,1024]{1,0:T(8,128)(2,1)S(1)} %copy-done.2, bf16[2,4096,256]{2,1,0:T(8,128)(2,1)S(1)} %copy-done.1, f32[8,256,128]{2,1,0:T(8,128)S(1)} %copy-done.8, f32[8,256,256]{2,1,0:T(8,128)S(1)} %copy-done.6), custom_call_target="tpu_custom_call" | custom-call | flops 6442450944 | bytes 2097152 | tf_op jit(solution)/shard_map/prefix_keys/pallas_call | solution.py:183
  216.1 0.0 copy-start.9
  216.1 1.3 copy-done.9
  217.4 0.0 copy-start.11
  217.4 1.0 copy-done.11
  218.4 0.0 all-to-all-done.kv_ref
  218.4 0.0 copy-start.10
  218.4 1.6 copy-done.10
  220.0 0.0 copy-start.12
  220.0 1.2 copy-done.12
  221.2 14.6 %moved_keys.1 = bf16[256,1024]{1,0:T(8,128)(2,1)} custom-call(bf16[256,1024]{1,0:T(8,128)(2,1)S(1)} %copy-done.2, bf16[32,128,256]{2,1,0:T(8,128)(2,1)} %all-to-all-done.kv_ref, bf16[256,256]{1,0:T(8,128)(2,1)S(1)} %copy-done.4, f32[8,256,128]{2,1,0:T(8,128)S(1)} %copy-done.12, f32[8,256,256]{2,1,0:T(8,128)S(1)} %copy-done.10), custom_call_target="tpu_custom_call" | custom-call | flops 6442450944 | bytes 2097152 | tf_op jit(solution)/shard_map/moved_keys/pallas_call | solution.py:204
  (4 shorter events, 0.0 us)
Async XLA Ops:
  6.5 2.4 copy-start
  14.1 7.5 %copy-start.13 = (s32[2]{0:T(128)S(1)}, s32[2]{0:T(128)}, u32[]{:S(2)}) copy-start(s32[2]{0:T(128)} %param.16) | copy-start | bytes 28
  14.1 204.3 %all-to-all-start = ((bf16[32,128,256]{2,1,0:T(8,128)(2,1)}), bf16[32,128,256]{2,1,0:T(8,128)(2,1)}, u32[]{:S(2)}, u32[]{:S(2)}) async-start(bf16[32,128,256]{2,1,0:T(8,128)(2,1)} %broadcast_select_fusion.1), calls=%async_computation | async-start | bytes 4194304 | tf_op jit(solution)/shard_map/all_to_all | solution.py:156
  21.6 176.6 %all-reduce.2.cloned.1.call-start = ((), (), s32[]{:S(2)}) async-start(), calls=%async_computation.1 | async-start | bytes 8388608 | tf_op jit(solution)/shard_map/psum | solution.py:161
  25.6 0.8 copy-start.14
  25.6 1.4 copy-start.2
  25.6 1.4 copy-start.3
  25.6 1.4 copy-start.4
  29.4 1.3 copy-start.5
  30.8 1.0 copy-start.7
  198.2 2.2 copy-start.1
  200.3 1.6 copy-start.6
  201.9 1.2 copy-start.8
  216.1 1.3 copy-start.9
  217.4 1.0 copy-start.11
  218.4 1.6 copy-start.10
  220.0 1.2 copy-start.12
Sparse Core Ops, SparseCore 0:
  27.9 170.1 all-reduce.1

commit v2 on v1

--- a/solution.py
+++ b/solution.py
@@ -68,7 +68,7 @@
     fold_keys(q_ref, m_ref, acc_ref, keys, values_ref[:own, :], factor)
 
 
-def prefix_kernel(factor, which_ref, q_ref, kv_ref, m_in, acc_in, m_ref, acc_ref, values_ref):
+def prefix_kernel(factor, q_ref, kv_ref, m_in, acc_in, m_ref, acc_ref, values_ref):
     size = q_ref.shape[1] // acc_ref.shape[0]
 
     @pl.when(pl.program_id(0) == 0)
@@ -113,6 +113,28 @@
     return pl.CostEstimate(
         flops=6 * rows * keys * size, bytes_accessed=4 * keys * size, transcendentals=rows * keys
     )
+
+
+def multicast(prefix_cache, owners, readers):
+    replicas = lax.axis_size("replica")
+    me = lax.axis_index("replica")
+    half = replicas // 2
+    mine = me // half
+    halves = [list(range(half)), list(range(half, replicas))]
+    exchange = functools.partial(
+        lax.all_to_all,
+        axis_name="replica",
+        split_axis=0,
+        concat_axis=0,
+        axis_index_groups=halves,
+        tiled=True,
+    )
+    pieces = prefix_cache.reshape(half, -1, prefix_cache.shape[1])
+    found = exchange(pieces)[owners % half]
+    passed = lax.ppermute(found, "replica", [(i, (i + half) % replicas) for i in range(replicas)])
+    held = jnp.where((owners // half == mine)[:, None, None], found, passed)
+    wanted = lax.dynamic_slice_in_dim(readers, mine * half, half)
+    return exchange(held[wanted]).reshape(prefix_cache.shape)
 
 
 def on_device(
@@ -129,11 +151,9 @@
     mig_count,
 ):
     replicas = lax.axis_size("replica")
-    me = lax.axis_index("replica")
     size = suffix_kv.shape[1] // 2
     tokens = queries.shape[0]
     heads = queries.shape[1] // size
-    prefixes = owners.shape[0]
     factor = size ** (-0.5) * LOG2E
     row_count = tokens * heads
     state = (
@@ -155,10 +175,7 @@
     )
     arrived = lax.all_to_all(outgoing, "replica", split_axis=0, concat_axis=0, tiled=True)
 
-    offered = jnp.where(
-        (owners == me)[:, None, None], prefix_cache[None], jnp.zeros((), prefix_cache.dtype)
-    )
-    shared = lax.psum(offered, "replica")
+    shared = multicast(prefix_cache, owners, readers)
 
     state_now = pl.pallas_call(
         functools.partial(local_kernel, factor),
@@ -179,25 +196,22 @@
         name="local_keys",
     )(ctx_len, queries, suffix_kv, own_cache)
 
-    rows = min(1024, shared.shape[1])
+    rows = min(1024, shared.shape[0])
     state_now = pl.pallas_call(
         functools.partial(prefix_kernel, factor),
         out_shape=state,
-        grid_spec=pltpu.PrefetchScalarGridSpec(
-            num_scalar_prefetch=1,
-            grid=(shared.shape[1] // rows,),
-            in_specs=[
-                whole(queries.shape),
-                pl.BlockSpec((None, rows, 2 * size), lambda i, which: (which[0], i, 0)),
-                *state_specs,
-            ],
-            out_specs=state_specs,
-            scratch_shapes=[pltpu.VMEM((rows, 2 * size), jnp.bfloat16)],
-        ),
+        grid=(shared.shape[0] // rows,),
+        in_specs=[
+            whole(queries.shape),
+            pl.BlockSpec((rows, 2 * size), lambda i: (i, 0)),
+            *state_specs,
+        ],
+        out_specs=state_specs,
+        scratch_shapes=[pltpu.VMEM((rows, 2 * size), jnp.bfloat16)],
         compiler_params=params,
-        cost_estimate=cost(row_count, shared.shape[1], size),
+        cost_estimate=cost(row_count, shared.shape[0], size),
         name="prefix_keys",
-    )(readers[me][None], queries, shared, *state_now)
+    )(queries, shared, *state_now)
 
     rows = arrived.shape[1]
     group = max(1, 1024 // rows)

time: 243 us -> 162 us (0.67)
  waiting for transfers between devices: 166 us -> 94.2 us
  between operations: 15 us -> 1.46 us
  starting transfers between devices: 7.47 us -> 20.5 us
  other arithmetic: 8.67 us -> 3.66 us
  local copies, waits for them, and re-layouts: 15.1 us -> 11.3 us
    psum x1 -> x0, waiting for transfers between devices: 166 us -> none  [on_device(): shared = lax.psum(offered, 'replica')]
    all_to_all x0 -> x2, waiting for transfers between devices: none -> 52.5 us  [the longest x1 29.3 us: multicast(): found = exchange(pieces)[owners % half]]
    all_to_all x1, waiting for transfers between devices: 0.01 us -> 30 us  [on_device(): lax.all_to_all(outgoing, 'replica', split_axis=0, concat_axis=0, tiled=True)]
    all_to_all x0 -> x2, starting transfers between devices: none -> 11.9 us  [the longest x1 6.49 us: multicast(): found = exchange(pieces)[owners % half]]
    ppermute x0 -> x1, waiting for transfers between devices: none -> 11.7 us  [multicast(): lax.ppermute(found, 'replica', [(i, (i + half) % replicas) for i in range...]
    unnamed x30 -> x24, local copies, waits for them, and re-layouts: 12.5 us -> 5.16 us
    gather x0 -> x2, local copies, waits for them, and re-layouts: none -> 4.17 us  [the longest x1 2.15 us: multicast(): found = exchange(pieces)[owners % half]]
    select_n x1 -> x3, other arithmetic: 3.91 us -> 0.19 us  [the longest x1 0.1 us: multicast(): held = jnp.where((owners // half == mine)[:, None, None], found, passed)]
  transfers between devices with their start and end apart: 2 -> 4, of which waited for: 1 -> 4; matrix products, arithmetic and copies ran while one was open for 2% -> 3% of each run, Pallas kernels for 6% -> 10%
where the time goes in v2:
time: 162 us
  waiting for transfers between devices  94.2 us (58%)
  Pallas kernels  30.4 us (19%)
  starting transfers between devices  20.5 us (13%)
  local copies, waits for them, and re-layouts  11.3 us (7%)
  other arithmetic  3.66 us (2%)
    all_to_all x1, waiting for transfers between devices, on_device(): lax.all_to_all(outgoing, 'replica', split_axis=0, concat_axis=0, tiled=True)  30 us
    all_to_all x1, waiting for transfers between devices, multicast(): found = exchange(pieces)[owners % half]  29.3 us
    all_to_all x1, waiting for transfers between devices, multicast(): return exchange(held[wanted]).reshape(prefix_cache.shape)  23.2 us
    pallas_call x1, Pallas kernels, on_device(): pl.pallas_call(functools.partial(moved_kernel, factor), out_shape=jax.Sha...  14.6 us
    pallas_call x1, Pallas kernels, on_device(): pl.pallas_call(functools.partial(prefix_kernel, factor), out_shape=state,...  13.3 us
    ppermute x1, waiting for transfers between devices, multicast(): lax.ppermute(found, 'replica', [(i, (i + half) % replicas) for i in range...  11.7 us
    all_to_all x1, starting transfers between devices, multicast(): found = exchange(pieces)[owners % half]  6.49 us
    all_to_all x1, starting transfers between devices, on_device(): lax.all_to_all(outgoing, 'replica', split_axis=0, concat_axis=0, tiled=True)  5.96 us
  transfers between devices with their start and end apart: 4, of which 4 were waited for; matrix products, arithmetic and copies ran while one was open for 3% of the time, Pallas kernels for 10%

profile of v2, /device:TPU:0, one launch (start us, length us, event | category | flops | bytes accessed | tf_op | source)
XLA Modules:
  0.0 161.5 jit_solution(18171293341750813979)
XLA Ops:
  0.0 0.0 copy-start
  0.0 0.0 copy-start.10
  0.0 0.0 copy-start.11
  0.0 6.5 %all-to-all-start.1 = ((bf16[16,256,256]{2,1,0:T(8,128)(2,1)}), bf16[16,256,256]{2,1,0:T(8,128)(2,1)}, u32[]{:S(2)}, u32[]{:S(2)}) async-start(bf16[16,256,256]{2,1,0:T(8,128)(2,1)} %bitcast.10), calls=%async_computation.1 | async-start | bytes 4194304 | tf_op jit(solution)/shard_map/all_to_all | solution.py:133
  6.5 0.0 copy-done.10
  6.5 0.1 compare_select_fusion
  6.6 0.0 copy-done.11
  6.6 29.3 %all-to-all-done.1 = bf16[16,256,256]{2,1,0:T(8,128)(2,1)} async-done(((bf16[16,256,256]{2,1,0:T(8,128)(2,1)}), bf16[16,256,256]{2,1,0:T(8,128)(2,1)}, u32[]{:S(2)}, u32[]{:S(2)}) %all-to-all-start.1) | async-done | bytes 2097184 | tf_op jit(solution)/shard_map/all_to_all | solution.py:133
  35.9 2.2 %gather_fusion.1 = bf16[2,256,256]{2,1,0:T(8,128)(2,1)S(1)} fusion(bf16[16,256,256]{2,1,0:T(8,128)(2,1)} %all-to-all-done.1, s32[1024]{0:T(1024)S(1)} %pad_clamp_fusion.1), kind=kCustom, calls=%fused_computation.1 | custom fusion | bytes 524296 | tf_op jit(solution)/shard_map/gather | solution.py:133
  38.0 2.7 %collective-permute-start = (bf16[2,256,256]{2,1,0:T(8,128)(2,1)S(1)}, bf16[2,256,256]{2,1,0:T(8,128)(2,1)S(1)}, u32[]{:S(2)}, u32[]{:S(2)}) collective-permute-start(bf16[2,256,256]{2,1,0:T(8,128)(2,1)S(1)} %gather_fusion.1), channel_id=1, source_target_pairs={{0,16},{1,17},{2,18},{3,19},{4,20},{5,21},{6,22},{7,23},{8,24},{9,... | collective-permute-start | bytes 786440 | tf_op jit(solution)/shard_map/ppermute | solution.py:134
  40.7 11.7 %collective-permute-done = bf16[2,256,256]{2,1,0:T(8,128)(2,1)S(1)} collective-permute-done((bf16[2,256,256]{2,1,0:T(8,128)(2,1)S(1)}, bf16[2,256,256]{2,1,0:T(8,128)(2,1)S(1)}, u32[]{:S(2)}, u32[]{:S(2)}) %collective-permute-start) | collective-permute-done | bytes 262176 | tf_op jit(solution)/shard_map/ppermute | solution.py:134
  52.4 0.1 broadcast_select_fusion.1
  52.5 2.0 %gather_fusion.2 = bf16[16,256,256]{2,1,0:T(8,128)(2,1)} fusion(bf16[2,256,256]{2,1,0:T(8,128)(2,1)S(1)} %broadcast_select_fusion.1, s32[1024]{0:T(1024)S(1)} %pad_clamp_fusion), kind=kCustom, calls=%fused_computation.2 | custom fusion | bytes 4194368 | tf_op jit(solution)/shard_map/gather | solution.py:137
  54.5 0.0 copy-start.8
  54.5 0.0 copy-start.9
  54.6 5.4 %all-to-all-start.2 = ((bf16[16,256,256]{2,1,0:T(8,128)(2,1)}), bf16[16,256,256]{2,1,0:T(8,128)(2,1)}, u32[]{:S(2)}, u32[]{:S(2)}) async-start(bf16[16,256,256]{2,1,0:T(8,128)(2,1)} %gather_fusion.2), calls=%async_computation.2 | async-start | bytes 4194304 | tf_op jit(solution)/shard_map/all_to_all | solution.py:137
  60.6 0.0 copy-done.8
  60.6 0.0 copy-done.9
  60.6 0.1 select_reduce_fusion
  60.7 0.0 copy-done
  60.8 2.0 %gather_fusion = bf16[32,128,256]{2,1,0:T(8,128)(2,1)} fusion(bf16[32,128,256]{2,1,0:T(8,128)(2,1)S(1)} %copy-done, s32[1024]{0:T(1024)S(1)} %pad_clamp_fusion.2), kind=kCustom, calls=%fused_computation | custom fusion | bytes 4194432 | tf_op jit(solution)/shard_map/gather | solution.py:174
  62.8 0.1 fusion.1
  62.9 3.2 %broadcast_select_fusion = bf16[32,128,256]{2,1,0:T(8,128)(2,1)} fusion(bf16[32,128,256]{2,1,0:T(8,128)(2,1)} %gather_fusion, pred[32]{0:T(512)(128)(4,1)S(1)} %fusion.1), kind=kLoop, calls=%fused_computation.3 | loop fusion | flops 1048576 | bytes 4194336 | tf_op jit(solution)/shard_map/jit(_where)/select_n | solution.py:173
  66.1 0.0 copy-start.1
  66.1 0.0 copy-start.2
  66.1 0.0 copy-start.3
  66.1 23.2 %all-to-all-done.2 = bf16[16,256,256]{2,1,0:T(8,128)(2,1)} async-done(((bf16[16,256,256]{2,1,0:T(8,128)(2,1)}), bf16[16,256,256]{2,1,0:T(8,128)(2,1)}, u32[]{:S(2)}, u32[]{:S(2)}) %all-to-all-start.2) | async-done | bytes 2097184 | tf_op jit(solution)/shard_map/all_to_all | solution.py:137
  89.3 6.0 %all-to-all-start = ((bf16[32,128,256]{2,1,0:T(8,128)(2,1)}), bf16[32,128,256]{2,1,0:T(8,128)(2,1)}, u32[]{:S(2)}, u32[]{:S(2)}) async-start(bf16[32,128,256]{2,1,0:T(8,128)(2,1)} %broadcast_select_fusion), calls=%async_computation | async-start | bytes 4194304 | tf_op jit(solution)/shard_map/all_to_all | solution.py:176
  95.9 0.0 copy-done.1
  95.9 0.0 copy-done.2
  95.9 0.0 copy-done.3
  96.0 2.5 %local_keys.1 = (f32[8,256,128]{2,1,0:T(8,128)S(1)}, f32[8,256,256]{2,1,0:T(8,128)S(1)}) custom-call(s32[1]{0:T(128)S(6)} %copy.12.len_ref, bf16[256,1024]{1,0:T(8,128)(2,1)S(1)} %copy-done.1, bf16[256,256]{1,0:T(8,128)(2,1)S(1)} %copy-done.3, bf16[512,256]{1,0:T(8,128)(2,1)S(1)} %copy-done.2), custom_call_target="tpu_custom_call" | custom-call | flops 1207959552 | bytes 393216 | tf_op jit(solution)/shard_map/local_keys/pallas_call | solution.py:180
  98.5 13.3 %prefix_keys.1 = (f32[8,256,128]{2,1,0:T(8,128)S(1)}, f32[8,256,256]{2,1,0:T(8,128)S(1)}) custom-call(bf16[256,1024]{1,0:T(8,128)(2,1)S(1)} %copy-done.1, bf16[4096,256]{1,0:T(8,128)(2,1)} %bitcast.6.kv_ref, f32[8,256,128]{2,1,0:T(8,128)S(1)} %get-tuple-element.9.m_in, f32[8,256,256]{2,1,0:T(8,128)S(1)} %get-tuple-element.10.acc_in), custom_call_target="tpu_custom_call" | custom-call | flops 6442450944 | bytes 2097152 | tf_op jit(solution)/shard_map/prefix_keys/pallas_call | solution.py:200
  111.8 0.0 copy-start.4
  111.8 1.3 copy-done.4
  113.1 0.0 copy-start.6
  113.1 1.0 copy-done.6
  114.1 30.0 %all-to-all-done.kv_ref = bf16[32,128,256]{2,1,0:T(8,128)(2,1)} async-done(((bf16[32,128,256]{2,1,0:T(8,128)(2,1)}), bf16[32,128,256]{2,1,0:T(8,128)(2,1)}, u32[]{:S(2)}, u32[]{:S(2)}) %all-to-all-start) | async-done | bytes 2097184 | tf_op jit(solution)/shard_map/all_to_all | solution.py:176
  144.2 0.0 copy-start.5
  144.2 1.6 copy-done.5
  145.7 0.0 copy-start.7
  145.7 1.2 copy-done.7
  147.0 14.6 %moved_keys.1 = bf16[256,1024]{1,0:T(8,128)(2,1)} custom-call(bf16[256,1024]{1,0:T(8,128)(2,1)S(1)} %copy-done.1, bf16[32,128,256]{2,1,0:T(8,128)(2,1)} %all-to-all-done.kv_ref, bf16[256,256]{1,0:T(8,128)(2,1)S(1)} %copy-done.3, f32[8,256,128]{2,1,0:T(8,128)S(1)} %copy-done.7, f32[8,256,256]{2,1,0:T(8,128)S(1)} %copy-done.5), custom_call_target="tpu_custom_call" | custom-call | flops 6442450944 | bytes 2097152 | tf_op jit(solution)/shard_map/moved_keys/pallas_call | solution.py:218
  (7 shorter events, 0.1 us)
Async XLA Ops:
  0.0 60.7 %copy-start = (bf16[32,128,256]{2,1,0:T(8,128)(2,1)S(1)}, bf16[32,128,256]{2,1,0:T(8,128)(2,1)}, u32[]{:S(2)}) copy-start(bf16[32,128,256]{2,1,0:T(8,128)(2,1)} %param.18) | copy-start | bytes 6291460
  0.0 6.5 %copy-start.10 = (s32[32]{0:T(128)S(1)}, s32[32]{0:T(128)}, u32[]{:S(2)}) copy-start(s32[32]{0:T(128)} %param.17) | copy-start | bytes 388
  0.0 6.6 %copy-start.11 = (s32[2]{0:T(128)S(1)}, s32[2]{0:T(128)}, u32[]{:S(2)}) copy-start(s32[2]{0:T(128)} %param.16) | copy-start | bytes 28
  0.0 35.9 %all-to-all-start.1 = ((bf16[16,256,256]{2,1,0:T(8,128)(2,1)}), bf16[16,256,256]{2,1,0:T(8,128)(2,1)}, u32[]{:S(2)}, u32[]{:S(2)}) async-start(bf16[16,256,256]{2,1,0:T(8,128)(2,1)} %bitcast.10), calls=%async_computation.1 | async-start | bytes 4194304 | tf_op jit(solution)/shard_map/all_to_all | solution.py:133
  38.0 14.4 %collective-permute-start = (bf16[2,256,256]{2,1,0:T(8,128)(2,1)S(1)}, bf16[2,256,256]{2,1,0:T(8,128)(2,1)S(1)}, u32[]{:S(2)}, u32[]{:S(2)}) collective-permute-start(bf16[2,256,256]{2,1,0:T(8,128)(2,1)S(1)} %gather_fusion.1), channel_id=1, source_target_pairs={{0,16},{1,17},{2,18},{3,19},{4,20},{5,21},{6,22},{7,23},{8,24},{9,... | collective-permute-start | bytes 786440 | tf_op jit(solution)/shard_map/ppermute | solution.py:134
  54.5 6.0 %copy-start.8 = (s32[1,32]{1,0:T(1,128)S(1)}, s32[1,32]{1,0:T(1,128)}, u32[]{:S(2)}) copy-start(s32[1,32]{1,0:T(1,128)} %param.20) | copy-start | bytes 388
  54.5 6.0 %copy-start.9 = (s32[1,32]{1,0:T(1,128)S(1)}, s32[1,32]{1,0:T(1,128)}, u32[]{:S(2)}) copy-start(s32[1,32]{1,0:T(1,128)} %param.19) | copy-start | bytes 388
  54.6 34.8 %all-to-all-start.2 = ((bf16[16,256,256]{2,1,0:T(8,128)(2,1)}), bf16[16,256,256]{2,1,0:T(8,128)(2,1)}, u32[]{:S(2)}, u32[]{:S(2)}) async-start(bf16[16,256,256]{2,1,0:T(8,128)(2,1)} %gather_fusion.2), calls=%async_computation.2 | async-start | bytes 4194304 | tf_op jit(solution)/shard_map/all_to_all | solution.py:137
  66.1 29.9 %copy-start.1 = (bf16[256,1024]{1,0:T(8,128)(2,1)S(1)}, bf16[256,1024]{1,0:T(8,128)(2,1)}, u32[]{:S(2)}) copy-start(bf16[256,1024]{1,0:T(8,128)(2,1)} %q_ref.5) | copy-start | bytes 1572868
  66.1 29.9 %copy-start.2 = (bf16[512,256]{1,0:T(8,128)(2,1)S(1)}, bf16[512,256]{1,0:T(8,128)(2,1)}, u32[]{:S(2)}) copy-start(bf16[512,256]{1,0:T(8,128)(2,1)} %own_ref.1) | copy-start | bytes 786436
  66.1 29.9 %copy-start.3 = (bf16[256,256]{1,0:T(8,128)(2,1)S(1)}, bf16[256,256]{1,0:T(8,128)(2,1)}, u32[]{:S(2)}) copy-start(bf16[256,256]{1,0:T(8,128)(2,1)} %suffix_ref.3) | copy-start | bytes 393220
  89.3 54.8 %all-to-all-start = ((bf16[32,128,256]{2,1,0:T(8,128)(2,1)}), bf16[32,128,256]{2,1,0:T(8,128)(2,1)}, u32[]{:S(2)}, u32[]{:S(2)}) async-start(bf16[32,128,256]{2,1,0:T(8,128)(2,1)} %broadcast_select_fusion), calls=%async_computation | async-start | bytes 4194304 | tf_op jit(solution)/shard_map/all_to_all | solution.py:176
  111.8 1.3 copy-start.4
  113.1 1.0 copy-start.6
  144.2 1.6 copy-start.5
  145.7 1.2 copy-start.7

commit v3 on v1

--- a/solution.py
+++ b/solution.py
@@ -68,7 +68,7 @@
     fold_keys(q_ref, m_ref, acc_ref, keys, values_ref[:own, :], factor)
 
 
-def prefix_kernel(factor, which_ref, q_ref, kv_ref, m_in, acc_in, m_ref, acc_ref, values_ref):
+def prefix_kernel(factor, q_ref, kv_ref, m_in, acc_in, m_ref, acc_ref, values_ref):
     size = q_ref.shape[1] // acc_ref.shape[0]
 
     @pl.when(pl.program_id(0) == 0)
@@ -113,6 +113,58 @@
     return pl.CostEstimate(
         flops=6 * rows * keys * size, bytes_accessed=4 * keys * size, transcendentals=rows * keys
     )
+
+
+def multicast(prefix_cache, owners, readers):
+    replicas = lax.axis_size("replica")
+    me = lax.axis_index("replica")
+    half = replicas // 2
+    chips = half // 2
+    core = me % 2
+    chip = me // 2 % chips
+    side = me // half
+    width = prefix_cache.shape[1]
+
+    def swap_cores(rows):
+        return lax.ppermute(rows, "replica", [(i, i ^ 1) for i in range(replicas)])
+
+    def to_peer(rows, step):
+        return lax.ppermute(rows, "replica", [(i, i ^ (2 * step)) for i in range(replicas)])
+
+    split = prefix_cache.reshape(2, chips, -1, width)
+    kept = lax.dynamic_index_in_dim(split, core, 0, keepdims=False)
+    swapped = swap_cores(lax.dynamic_index_in_dim(split, 1 - core, 0, keepdims=False))
+    gathered = []
+    for prefix in range(owners.shape[0]):
+        owner = owners[prefix]
+        own_core = owner % 2 == core
+        held = None
+        for step in range(chips):
+            there = chip ^ step
+            rows = jnp.where(
+                own_core,
+                lax.dynamic_index_in_dim(kept, there, 0, keepdims=False),
+                lax.dynamic_index_in_dim(swapped, there, 0, keepdims=False),
+            )
+            if step:
+                rows = to_peer(rows, step)
+            held = rows if held is None else jnp.where(owner // 2 % chips == there, rows, held)
+        passed = lax.ppermute(
+            held, "replica", [(i, (i + half) % replicas) for i in range(replicas)]
+        )
+        held = jnp.where(owner // half == side, held, passed)
+        gathered.append([held] + [to_peer(held, step) for step in range(1, chips)])
+
+    def pick(wanted):
+        picked = []
+        for step in range(chips):
+            rows = gathered[0][step]
+            for prefix in range(1, owners.shape[0]):
+                rows = jnp.where(wanted == prefix, gathered[prefix][step], rows)
+            picked.append(rows)
+        return jnp.concatenate(picked)
+
+    return pick(readers[me]), swap_cores(pick(readers[me ^ 1]))
 
 
 def on_device(
@@ -129,11 +181,9 @@
     mig_count,
 ):
     replicas = lax.axis_size("replica")
-    me = lax.axis_index("replica")
     size = suffix_kv.shape[1] // 2
     tokens = queries.shape[0]
     heads = queries.shape[1] // size
-    prefixes = owners.shape[0]
     factor = size ** (-0.5) * LOG2E
     row_count = tokens * heads
     state = (
@@ -155,10 +205,7 @@
     )
     arrived = lax.all_to_all(outgoing, "replica", split_axis=0, concat_axis=0, tiled=True)
 
-    offered = jnp.where(
-        (owners == me)[:, None, None], prefix_cache[None], jnp.zeros((), prefix_cache.dtype)
-    )
-    shared = lax.psum(offered, "replica")
+    shared = multicast(prefix_cache, owners, readers)
 
     state_now = pl.pallas_call(
         functools.partial(local_kernel, factor),
@@ -179,25 +226,23 @@
         name="local_keys",
     )(ctx_len, queries, suffix_kv, own_cache)
 
-    rows = min(1024, shared.shape[1])
-    state_now = pl.pallas_call(
-        functools.partial(prefix_kernel, factor),
-        out_shape=state,
-        grid_spec=pltpu.PrefetchScalarGridSpec(
-            num_scalar_prefetch=1,
-            grid=(shared.shape[1] // rows,),
+    for part in shared:
+        rows = min(1024, part.shape[0])
+        state_now = pl.pallas_call(
+            functools.partial(prefix_kernel, factor),
+            out_shape=state,
+            grid=(part.shape[0] // rows,),
             in_specs=[
                 whole(queries.shape),
-                pl.BlockSpec((None, rows, 2 * size), lambda i, which: (which[0], i, 0)),
+                pl.BlockSpec((rows, 2 * size), lambda i: (i, 0)),
                 *state_specs,
             ],
             out_specs=state_specs,
             scratch_shapes=[pltpu.VMEM((rows, 2 * size), jnp.bfloat16)],
-        ),
-        compiler_params=params,
-        cost_estimate=cost(row_count, shared.shape[1], size),
-        name="prefix_keys",
-    )(readers[me][None], queries, shared, *state_now)
+            compiler_params=params,
+            cost_estimate=cost(row_count, part.shape[0], size),
+            name="prefix_keys",
+        )(queries, part, *state_now)
 
     rows = arrived.shape[1]
     group = max(1, 1024 // rows)

time: 243 us -> 168 us (0.69)
  waiting for transfers between devices: 166 us -> 54 us
  starting transfers between devices: 7.47 us -> 55.8 us
  between operations: 15 us -> 8.41 us
  local copies, waits for them, and re-layouts: 15.1 us -> 10.9 us
    psum x1 -> x0, waiting for transfers between devices: 166 us -> none  [on_device(): shared = lax.psum(offered, 'replica')]
    ppermute x0 -> x32, waiting for transfers between devices: none -> 54 us  [the longest x28 44.2 us: to_peer(): lax.ppermute(rows, 'replica', [(i, i ^ 2 * step) for i in range(replicas)])]
    ppermute x0 -> x32, starting transfers between devices: none -> 52 us  [the longest x28 42.2 us: to_peer(): lax.ppermute(rows, 'replica', [(i, i ^ 2 * step) for i in range(replicas)])]
    unnamed x30 -> x24, local copies, waits for them, and re-layouts: 12.5 us -> 5.17 us
    all_to_all x1, starting transfers between devices: 7.43 us -> 3.81 us  [on_device(): lax.all_to_all(outgoing, 'replica', split_axis=0, concat_axis=0, tiled=True)]
    squeeze x0 -> x1, local copies, waits for them, and re-layouts: none -> 2.43 us  [multicast(): lax.dynamic_index_in_dim(split, 1 - core, 0, keepdims=False)]
    pallas_call x1 -> x2, Pallas kernels: 12.9 us -> 12.5 us  [on_device(): pl.pallas_call(functools.partial(prefix_kernel, factor), out_shape=state,...]
  transfers between devices with their start and end apart: 2 -> 33, of which waited for: 1 -> 14; matrix products, arithmetic and copies ran while one was open for 2% -> 6% of each run, Pallas kernels for 6% -> 9%
where the time goes in v3:
time: 168 us
  starting transfers between devices  55.8 us (33%)
  waiting for transfers between devices  54 us (32%)
  Pallas kernels  29.5 us (18%)
  local copies, waits for them, and re-layouts  10.9 us (6%)
  other arithmetic  9.33 us (6%)
  between operations  8.41 us (5%)
    ppermute x28, waiting for transfers between devices, to_peer(): lax.ppermute(rows, 'replica', [(i, i ^ 2 * step) for i in range(replicas)])  44.2 us
    ppermute x28, starting transfers between devices, to_peer(): lax.ppermute(rows, 'replica', [(i, i ^ 2 * step) for i in range(replicas)])  42.2 us
    pallas_call x1, Pallas kernels, on_device(): pl.pallas_call(functools.partial(moved_kernel, factor), out_shape=jax.Sha...  14.6 us
    pallas_call x2, Pallas kernels, on_device(): pl.pallas_call(functools.partial(prefix_kernel, factor), out_shape=state,...  12.5 us
    ppermute x2, waiting for transfers between devices, multicast(): lax.ppermute(held, 'replica', [(i, (i + half) % replicas) for i in range(...  9.75 us
    ppermute x2, starting transfers between devices, multicast(): lax.ppermute(held, 'replica', [(i, (i + half) % replicas) for i in range(...  9.25 us
    unnamed x24, local copies, waits for them, and re-layouts  5.17 us
    all_to_all x1, starting transfers between devices, on_device(): lax.all_to_all(outgoing, 'replica', split_axis=0, concat_axis=0, tiled=True)  3.81 us
  transfers between devices with their start and end apart: 33, of which 14 were waited for; matrix products, arithmetic and copies ran while one was open for 6% of the time, Pallas kernels for 9%

profile of v3, /device:TPU:0, one launch (start us, length us, event | category | flops | bytes accessed | tf_op | source)
XLA Modules:
  0.0 168.0 jit_solution(13848365364206262578)
XLA Ops:
  0.0 2.4 %dynamic-slice_bitcast_fusion = bf16[8,256,256]{2,1,0:T(8,128)(2,1)} fusion(bf16[2,8,256,256]{3,2,1,0:T(8,128)(2,1)} %bitcast.91, s32[]{:T(128)S(6)} %select_n.434), kind=kLoop, calls=%fused_computation.2 | loop fusion | bytes 2097156 | tf_op jit(solution)/shard_map/jit(dynamic_index_in_dim)/squeeze | solution.py:136
  8.5 2.4 %bitcast_select_fusion.3 = (bf16[256,256]{1,0:T(8,128)(2,1)}, bf16[256,256]{1,0:T(8,128)(2,1)S(1)}, bf16[256,256]{1,0:T(8,128)(2,1)}, bf16[256,256]{1,0:T(8,128)...) fusion(pred[]{:T(512)S(6)} %eq.122, ...), kind=kLoop, calls=%fused_computation.20 | loop fusion | flops 917504 | bytes 3670078 | tf_op jit(solution)/shard_map/jit(_where)/select_n | solution.py:144
  10.9 4.5 %collective-permute-start.1 = (bf16[256,256]{1,0:T(8,128)(2,1)}, bf16[256,256]{1,0:T(8,128)(2,1)}, u32[]{:S(2)}, u32[]{:S(2)}) collective-permute-start(bf16[256,256]{1,0:T(8,128)(2,1)} %get-tuple-element.33), channel_id=1, source_target_pairs={{0,14},{1,15},{2,12},{3,13},{4,10},{5,11},{6,8},{7,9},{8,6},{9,7},... | collective-permute-start | bytes 393224 | tf_op jit(solution)/shard_map/ppermute | solution.py:132
  15.7 1.5 collective-permute-start.3
  17.4 2.0 %gather_fusion = bf16[32,128,256]{2,1,0:T(8,128)(2,1)} fusion(bf16[32,128,256]{2,1,0:T(8,128)(2,1)S(1)} %copy-done, s32[1024]{0:T(1024)S(1)} %pad_clamp_fusion), kind=kCustom, calls=%fused_computation | custom fusion | bytes 4194432 | tf_op jit(solution)/shard_map/gather | solution.py:204
  19.6 2.8 %collective-permute-start.5 = (bf16[256,256]{1,0:T(8,128)(2,1)}, bf16[256,256]{1,0:T(8,128)(2,1)}, u32[]{:S(2)}, u32[]{:S(2)}) collective-permute-start(bf16[256,256]{1,0:T(8,128)(2,1)} %get-tuple-element.31), channel_id=1, source_target_pairs={{0,6},{1,7},{2,4},{3,5},{4,2},{5,3},{6,0},{7,1},{8,14},{9,15},{10,... | collective-permute-start | bytes 393224 | tf_op jit(solution)/shard_map/ppermute | solution.py:132
  23.1 1.4 collective-permute-start.7
  24.5 2.4 %collective-permute-done.3 = bf16[256,256]{1,0:T(8,128)(2,1)} collective-permute-done((bf16[256,256]{1,0:T(8,128)(2,1)}, bf16[256,256]{1,0:T(8,128)(2,1)}, u32[]{:S(2)}, u32[]{:S(2)}) %collective-permute-start.3) | collective-permute-done | bytes 131104 | tf_op jit(solution)/shard_map/ppermute | solution.py:132
  26.9 1.5 collective-permute-start.10
  28.5 2.5 %collective-permute-start.11 = (bf16[256,256]{1,0:T(8,128)(2,1)S(1)}, bf16[256,256]{1,0:T(8,128)(2,1)}, u32[]{:S(2)}, u32[]{:S(2)}) collective-permute-start(bf16[256,256]{1,0:T(8,128)(2,1)S(1)} %get-tuple-element.23), channel_id=1, source_target_pairs={{0,10},{1,11},{2,8},{3,9},{4,14},{5,15},{6,12},{7,13},{8,2},{9,3},... | collective-permute-start | bytes 393224 | tf_op jit(solution)/shard_map/ppermute | solution.py:132
  31.0 3.2 %broadcast_select_fusion = bf16[32,128,256]{2,1,0:T(8,128)(2,1)} fusion(bf16[32,128,256]{2,1,0:T(8,128)(2,1)} %gather_fusion, pred[32]{0:T(512)(128)(4,1)S(1)} %fusion.15), kind=kLoop, calls=%fused_computation.1 | loop fusion | flops 1048576 | bytes 4194336 | tf_op jit(solution)/shard_map/jit(_where)/select_n | solution.py:203
  34.2 3.8 %all-to-all-start = ((bf16[32,128,256]{2,1,0:T(8,128)(2,1)}), bf16[32,128,256]{2,1,0:T(8,128)(2,1)}, u32[]{:S(2)}, u32[]{:S(2)}) async-start(bf16[32,128,256]{2,1,0:T(8,128)(2,1)} %broadcast_select_fusion), calls=%async_computation | async-start | bytes 4194304 | tf_op jit(solution)/shard_map/all_to_all | solution.py:206
  39.5 1.8 %collective-permute-start.12 = (bf16[256,256]{1,0:T(8,128)(2,1)}, bf16[256,256]{1,0:T(8,128)(2,1)S(1)}, u32[]{:S(2)}, u32[]{:S(2)}) collective-permute-start(bf16[256,256]{1,0:T(8,128)(2,1)} %get-tuple-element.24), channel_id=1, source_target_pairs={{0,8},{1,9},{2,10},{3,11},{4,12},{5,13},{6,14},{7,15},{8,0},{9,1},... | collective-permute-start | bytes 393224 | tf_op jit(solution)/shard_map/ppermute | solution.py:132
  41.3 2.4 %collective-permute-start.13 = (bf16[256,256]{1,0:T(8,128)(2,1)}, bf16[256,256]{1,0:T(8,128)(2,1)S(1)}, u32[]{:S(2)}, u32[]{:S(2)}) collective-permute-start(bf16[256,256]{1,0:T(8,128)(2,1)} %get-tuple-element.25), channel_id=1, source_target_pairs={{0,6},{1,7},{2,4},{3,5},{4,2},{5,3},{6,0},{7,1},{8,14},{9,15},{10,... | collective-permute-start | bytes 393224 | tf_op jit(solution)/shard_map/ppermute | solution.py:132
  44.8 2.4 %collective-permute-start.9 = (bf16[256,256]{1,0:T(8,128)(2,1)S(1)}, bf16[256,256]{1,0:T(8,128)(2,1)S(1)}, u32[]{:S(2)}, u32[]{:S(2)}) collective-permute-start(bf16[256,256]{1,0:T(8,128)(2,1)S(1)} %get-tuple-element.21), channel_id=1, source_target_pairs={{0,14},{1,15},{2,12},{3,13},{4,10},{5,11},{6,8},{7,9},{8,6},{9,7},... | collective-permute-start | bytes 393224 | tf_op jit(solution)/shard_map/ppermute | solution.py:132
  47.1 1.0 fusion.6
  48.2 28.0 %collective-permute-done.12 = bf16[256,256]{1,0:T(8,128)(2,1)S(1)} collective-permute-done((bf16[256,256]{1,0:T(8,128)(2,1)}, bf16[256,256]{1,0:T(8,128)(2,1)S(1)}, u32[]{:S(2)}, u32[]{:S(2)}) %collective-permute-start.12) | collective-permute-done | bytes 131104 | tf_op jit(solution)/shard_map/ppermute | solution.py:132
  76.2 4.2 %collective-permute-start.8 = (bf16[256,256]{1,0:T(8,128)(2,1)S(1)}, bf16[256,256]{1,0:T(8,128)(2,1)}, u32[]{:S(2)}, u32[]{:S(2)}) collective-permute-start(bf16[256,256]{1,0:T(8,128)(2,1)S(1)} %fusion.6), channel_id=1, source_target_pairs={{0,16},{1,17},{2,18},{3,19},{4,20},{5,21},{6,22},{7,23},{8,24},{9,... | collective-permute-start | bytes 393224 | tf_op jit(solution)/shard_map/ppermute | solution.py:152
  80.4 1.1 fusion.13
  81.5 5.1 %collective-permute-start.16 = (bf16[256,256]{1,0:T(8,128)(2,1)S(1)}, bf16[256,256]{1,0:T(8,128)(2,1)S(1)}, u32[]{:S(2)}, u32[]{:S(2)}) collective-permute-start(bf16[256,256]{1,0:T(8,128)(2,1)S(1)} %fusion.13), channel_id=1, source_target_pairs={{0,16},{1,17},{2,18},{3,19},{4,20},{5,21},{6,22},{7,23},{8,24},{9,... | collective-permute-start | bytes 393224 | tf_op jit(solution)/shard_map/ppermute | solution.py:152
  88.4 7.5 %collective-permute-done.8 = bf16[256,256]{1,0:T(8,128)(2,1)} collective-permute-done((bf16[256,256]{1,0:T(8,128)(2,1)S(1)}, bf16[256,256]{1,0:T(8,128)(2,1)}, u32[]{:S(2)}, u32[]{:S(2)}) %collective-permute-start.8) | collective-permute-done | bytes 131104 | tf_op jit(solution)/shard_map/ppermute | solution.py:152
  96.0 2.2 %collective-permute-done.16 = bf16[256,256]{1,0:T(8,128)(2,1)S(1)} collective-permute-done((bf16[256,256]{1,0:T(8,128)(2,1)S(1)}, bf16[256,256]{1,0:T(8,128)(2,1)S(1)}, u32[]{:S(2)}, u32[]{:S(2)}) %collective-permute-start.16) | collective-permute-done | bytes 131104 | tf_op jit(solution)/shard_map/ppermute | solution.py:152
  98.2 1.0 select_dynamic-update-slice_fusion.7
  99.2 1.3 collective-permute-start.17
  100.5 1.4 collective-permute-start.19
  102.4 0.9 collective-permute-start.20
  103.3 2.1 %collective-permute-start.21 = (bf16[256,256]{1,0:T(8,128)(2,1)S(1)}, bf16[256,256]{1,0:T(8,128)(2,1)S(1)}, u32[]{:S(2)}, u32[]{:S(2)}) collective-permute-start(bf16[256,256]{1,0:T(8,128)(2,1)S(1)} %get-tuple-element.19), channel_id=1, source_target_pairs={{0,6},{1,7},{2,4},{3,5},{4,2},{5,3},{6,0},{7,1},{8,14},{9,15},{10,... | collective-permute-start | bytes 393224 | tf_op jit(solution)/shard_map/ppermute | solution.py:132
  105.4 2.3 %collective-permute-start.22 = (bf16[256,256]{1,0:T(8,128)(2,1)S(1)}, bf16[256,256]{1,0:T(8,128)(2,1)S(1)}, u32[]{:S(2)}, u32[]{:S(2)}) collective-permute-start(bf16[256,256]{1,0:T(8,128)(2,1)S(1)} %get-tuple-element.18), channel_id=1, source_target_pairs={{0,6},{1,7},{2,4},{3,5},{4,2},{5,3},{6,0},{7,1},{8,14},{9,15},{10,... | collective-permute-start | bytes 393224 | tf_op jit(solution)/shard_map/ppermute | solution.py:132
  108.4 2.1 %collective-permute-start.24 = (bf16[256,256]{1,0:T(8,128)(2,1)S(1)}, bf16[256,256]{1,0:T(8,128)(2,1)S(1)}, u32[]{:S(2)}, u32[]{:S(2)}) collective-permute-start(bf16[256,256]{1,0:T(8,128)(2,1)S(1)} %get-tuple-element.18), channel_id=1, source_target_pairs={{0,8},{1,9},{2,10},{3,11},{4,12},{5,13},{6,14},{7,15},{8,0},{9,1},... | collective-permute-start | bytes 393224 | tf_op jit(solution)/shard_map/ppermute | solution.py:132
  110.5 2.8 %collective-permute-done.20 = bf16[256,256]{1,0:T(8,128)(2,1)S(1)} collective-permute-done((bf16[256,256]{1,0:T(8,128)(2,1)S(1)}, bf16[256,256]{1,0:T(8,128)(2,1)S(1)}, u32[]{:S(2)}, u32[]{:S(2)}) %collective-permute-start.20) | collective-permute-done | bytes 131104 | tf_op jit(solution)/shard_map/ppermute | solution.py:132
  113.3 3.0 %collective-permute-start.26 = (bf16[256,256]{1,0:T(8,128)(2,1)S(1)}, bf16[256,256]{1,0:T(8,128)(2,1)S(1)}, u32[]{:S(2)}, u32[]{:S(2)}) collective-permute-start(bf16[256,256]{1,0:T(8,128)(2,1)S(1)} %get-tuple-element.18), channel_id=1, source_target_pairs={{0,10},{1,11},{2,8},{3,9},{4,14},{5,15},{6,12},{7,13},{8,2},{9,3},... | collective-permute-start | bytes 393224 | tf_op jit(solution)/shard_map/ppermute | solution.py:132
  116.3 0.9 collective-permute-start.27
  117.3 2.1 %collective-permute-start.28 = (bf16[256,256]{1,0:T(8,128)(2,1)S(1)}, bf16[256,256]{1,0:T(8,128)(2,1)S(1)}, u32[]{:S(2)}, u32[]{:S(2)}) collective-permute-start(bf16[256,256]{1,0:T(8,128)(2,1)S(1)} %get-tuple-element.18), channel_id=1, source_target_pairs={{0,12},{1,13},{2,14},{3,15},{4,8},{5,9},{6,10},{7,11},{8,4},{9,5},... | collective-permute-start | bytes 393224 | tf_op jit(solution)/shard_map/ppermute | solution.py:132
  120.1 1.1 collective-permute-done.25
  121.3 2.1 %collective-permute-start.30 = (bf16[256,256]{1,0:T(8,128)(2,1)S(1)}, bf16[256,256]{1,0:T(8,128)(2,1)S(1)}, u32[]{:S(2)}, u32[]{:S(2)}) collective-permute-start(bf16[256,256]{1,0:T(8,128)(2,1)S(1)} %get-tuple-element.18), channel_id=1, source_target_pairs={{0,14},{1,15},{2,12},{3,13},{4,10},{5,11},{6,8},{7,9},{8,6},{9,7},... | collective-permute-start | bytes 393224 | tf_op jit(solution)/shard_map/ppermute | solution.py:132
  123.3 0.7 collective-permute-done.26
  124.1 2.4 %collective-permute-done.27 = bf16[256,256]{1,0:T(8,128)(2,1)S(1)} collective-permute-done((bf16[256,256]{1,0:T(8,128)(2,1)S(1)}, bf16[256,256]{1,0:T(8,128)(2,1)S(1)}, u32[]{:S(2)}, u32[]{:S(2)}) %collective-permute-start.27) | collective-permute-done | bytes 131104 | tf_op jit(solution)/shard_map/ppermute | solution.py:132
  126.5 2.5 %collective-permute-done.28 = bf16[256,256]{1,0:T(8,128)(2,1)S(1)} collective-permute-done((bf16[256,256]{1,0:T(8,128)(2,1)S(1)}, bf16[256,256]{1,0:T(8,128)(2,1)S(1)}, u32[]{:S(2)}, u32[]{:S(2)}) %collective-permute-start.28) | collective-permute-done | bytes 131104 | tf_op jit(solution)/shard_map/ppermute | solution.py:132
  129.1 1.9 %collective-permute-done.29 = bf16[256,256]{1,0:T(8,128)(2,1)S(1)} collective-permute-done((bf16[256,256]{1,0:T(8,128)(2,1)S(1)}, bf16[256,256]{1,0:T(8,128)(2,1)S(1)}, u32[]{:S(2)}, u32[]{:S(2)}) %collective-permute-start.29) | collective-permute-done | bytes 131104 | tf_op jit(solution)/shard_map/ppermute | solution.py:132
  131.0 1.4 collective-permute-done.30
  133.2 2.5 %local_keys.1 = (f32[8,256,128]{2,1,0:T(8,128)S(1)}, f32[8,256,256]{2,1,0:T(8,128)S(1)}) custom-call(s32[1]{0:T(128)S(6)} %copy.26.len_ref, bf16[256,1024]{1,0:T(8,128)(2,1)S(1)} %copy-done.1, bf16[256,256]{1,0:T(8,128)(2,1)S(1)} %copy-done.3, bf16[512,256]{1,0:T(8,128)(2,1)S(1)} %copy-done.2), custom_call_target="tpu_custom_call" | custom-call | flops 1207959552 | bytes 393216 | tf_op jit(solution)/shard_map/local_keys/pallas_call | solution.py:210
  135.7 6.2 %prefix_keys.2 = (f32[8,256,128]{2,1,0:T(8,128)S(1)}, f32[8,256,256]{2,1,0:T(8,128)S(1)}) custom-call(bf16[256,1024]{1,0:T(8,128)(2,1)S(1)} %copy-done.1, bf16[2048,256]{1,0:T(8,128)(2,1)S(1)} %get-tuple-element.34.kv_ref, f32[8,256,128]{2,1,0:T(8,128)S(1)} %get-tuple-element.11.m_in, f32[8,256,256]{2,1,0:T(8,128)S(1)} %get-tuple-element.12.acc_in), custom_call_target="tpu_custom_call" | custom-call | flops 3221225472 | bytes 1048576 | tf_op jit(solution)/shard_map/prefix_keys/pallas_call | solution.py:231
  142.0 6.2 %prefix_keys.3 = (f32[8,256,128]{2,1,0:T(8,128)S(1)}, f32[8,256,256]{2,1,0:T(8,128)S(1)}) custom-call(bf16[256,1024]{1,0:T(8,128)(2,1)S(1)} %copy-done.1, bf16[2048,256]{1,0:T(8,128)(2,1)S(1)} %collective-permute-done.31.kv_ref, f32[8,256,128]{2,1,0:T(8,128)S(1)} %get-tuple-element.13.m_in, f32[8,256,256]{2,1,0:T(8,128)S(1)} %get-tuple-element.14.acc_in), custom_call_target="tpu_custom_call" | custom-call | flops 3221225472 | bytes 1048576 | tf_op jit(solution)/shard_map/prefix_keys/pallas_call | solution.py:231
  148.3 1.3 copy-done.4
  149.6 1.0 copy-done.6
  150.6 1.6 copy-done.5
  152.2 1.2 copy-done.7
  153.4 14.6 %moved_keys.1 = bf16[256,1024]{1,0:T(8,128)(2,1)} custom-call(bf16[256,1024]{1,0:T(8,128)(2,1)S(1)} %copy-done.1, bf16[32,128,256]{2,1,0:T(8,128)(2,1)} %all-to-all-done.kv_ref, bf16[256,256]{1,0:T(8,128)(2,1)S(1)} %copy-done.3, f32[8,256,128]{2,1,0:T(8,128)S(1)} %copy-done.7, f32[8,256,256]{2,1,0:T(8,128)S(1)} %copy-done.5), custom_call_target="tpu_custom_call" | custom-call | flops 6442450944 | bytes 2097152 | tf_op jit(solution)/shard_map/moved_keys/pallas_call | solution.py:249
  (68 shorter events, 6.8 us)
Async XLA Ops:
  0.0 17.4 %copy-start = (bf16[32,128,256]{2,1,0:T(8,128)(2,1)S(1)}, bf16[32,128,256]{2,1,0:T(8,128)(2,1)}, u32[]{:S(2)}) copy-start(bf16[32,128,256]{2,1,0:T(8,128)(2,1)} %param.18) | copy-start | bytes 6291460
  0.0 2.9 %copy-start.9 = (s32[2]{0:T(128)S(1)}, s32[2]{0:T(128)}, u32[]{:S(2)}) copy-start(s32[2]{0:T(128)} %param.16) | copy-start | bytes 28
  0.0 8.3 %copy-start.11 = (s32[1,32]{1,0:T(1,128)S(1)}, s32[1,32]{1,0:T(1,128)}, u32[]{:S(2)}) copy-start(s32[1,32]{1,0:T(1,128)} %param.19) | copy-start | bytes 388
  0.0 8.3 %copy-start.10 = (s32[1,32]{1,0:T(1,128)S(1)}, s32[1,32]{1,0:T(1,128)}, u32[]{:S(2)}) copy-start(s32[1,32]{1,0:T(1,128)} %param.20) | copy-start | bytes 388
  2.5 6.0 %collective-permute-start = (bf16[8,256,256]{2,1,0:T(8,128)(2,1)}, bf16[8,256,256]{2,1,0:T(8,128)(2,1)S(1)}, u32[]{:S(2)}, u32[]{:S(2)}) collective-permute-start(bf16[8,256,256]{2,1,0:T(8,128)(2,1)} %dynamic-slice_bitcast_fusion), channel_id=1, source_target_pairs={{0,1},{1,0},{2,3},{3,2},{4,5},{5,4},{6,7},{7,6},{8,9},{9,8},{10,11... | collective-permute-start | bytes 3145736 | tf_op jit(solution)/shard_map/ppermute | solution.py:129
  10.9 11.5 %collective-permute-start.1 = (bf16[256,256]{1,0:T(8,128)(2,1)}, bf16[256,256]{1,0:T(8,128)(2,1)}, u32[]{:S(2)}, u32[]{:S(2)}) collective-permute-start(bf16[256,256]{1,0:T(8,128)(2,1)} %get-tuple-element.33), channel_id=1, source_target_pairs={{0,14},{1,15},{2,12},{3,13},{4,10},{5,11},{6,8},{7,9},{8,6},{9,7},... | collective-permute-start | bytes 393224 | tf_op jit(solution)/shard_map/ppermute | solution.py:132
  15.3 7.8 %collective-permute-start.2 = (bf16[256,256]{1,0:T(8,128)(2,1)}, bf16[256,256]{1,0:T(8,128)(2,1)}, u32[]{:S(2)}, u32[]{:S(2)}) collective-permute-start(bf16[256,256]{1,0:T(8,128)(2,1)} %get-tuple-element.28), channel_id=1, source_target_pairs={{0,12},{1,13},{2,14},{3,15},{4,8},{5,9},{6,10},{7,11},{8,4},{9,5},... | collective-permute-start | bytes 393224 | tf_op jit(solution)/shard_map/ppermute | solution.py:132
  15.7 11.1 %collective-permute-start.3 = (bf16[256,256]{1,0:T(8,128)(2,1)}, bf16[256,256]{1,0:T(8,128)(2,1)}, u32[]{:S(2)}, u32[]{:S(2)}) collective-permute-start(bf16[256,256]{1,0:T(8,128)(2,1)} %get-tuple-element.29), channel_id=1, source_target_pairs={{0,10},{1,11},{2,8},{3,9},{4,14},{5,15},{6,12},{7,13},{8,2},{9,3},... | collective-permute-start | bytes 393224 | tf_op jit(solution)/shard_map/ppermute | solution.py:132
  17.3 11.2 %collective-permute-start.4 = (bf16[256,256]{1,0:T(8,128)(2,1)}, bf16[256,256]{1,0:T(8,128)(2,1)}, u32[]{:S(2)}, u32[]{:S(2)}) collective-permute-start(bf16[256,256]{1,0:T(8,128)(2,1)} %get-tuple-element.30), channel_id=1, source_target_pairs={{0,8},{1,9},{2,10},{3,11},{4,12},{5,13},{6,14},{7,15},{8,0},{9,1},... | collective-permute-start | bytes 393224 | tf_op jit(solution)/shard_map/ppermute | solution.py:132
  19.6 19.9 %collective-permute-start.5 = (bf16[256,256]{1,0:T(8,128)(2,1)}, bf16[256,256]{1,0:T(8,128)(2,1)}, u32[]{:S(2)}, u32[]{:S(2)}) collective-permute-start(bf16[256,256]{1,0:T(8,128)(2,1)} %get-tuple-element.31), channel_id=1, source_target_pairs={{0,6},{1,7},{2,4},{3,5},{4,2},{5,3},{6,0},{7,1},{8,14},{9,15},{10,... | collective-permute-start | bytes 393224 | tf_op jit(solution)/shard_map/ppermute | solution.py:132
  22.4 18.9 %collective-permute-start.6 = (bf16[256,256]{1,0:T(8,128)(2,1)}, bf16[256,256]{1,0:T(8,128)(2,1)}, u32[]{:S(2)}, u32[]{:S(2)}) collective-permute-start(bf16[256,256]{1,0:T(8,128)(2,1)} %get-tuple-element.32), channel_id=1, source_target_pairs={{0,4},{1,5},{2,6},{3,7},{4,0},{5,1},{6,2},{7,3},{8,12},{9,13},{10,... | collective-permute-start | bytes 393224 | tf_op jit(solution)/shard_map/ppermute | solution.py:132
  23.1 20.5 %collective-permute-start.7 = (bf16[256,256]{1,0:T(8,128)(2,1)}, bf16[256,256]{1,0:T(8,128)(2,1)}, u32[]{:S(2)}, u32[]{:S(2)}) collective-permute-start(bf16[256,256]{1,0:T(8,128)(2,1)} %get-tuple-element.20), channel_id=1, source_target_pairs={{0,2},{1,3},{2,0},{3,1},{4,6},{5,7},{6,4},{7,5},{8,10},{9,11},{10,... | collective-permute-start | bytes 393224 | tf_op jit(solution)/shard_map/ppermute | solution.py:132
  26.9 17.3 %collective-permute-start.10 = (bf16[256,256]{1,0:T(8,128)(2,1)}, bf16[256,256]{1,0:T(8,128)(2,1)}, u32[]{:S(2)}, u32[]{:S(2)}) collective-permute-start(bf16[256,256]{1,0:T(8,128)(2,1)} %get-tuple-element.22), channel_id=1, source_target_pairs={{0,12},{1,13},{2,14},{3,15},{4,8},{5,9},{6,10},{7,11},{8,4},{9,5},... | collective-permute-start | bytes 393224 | tf_op jit(solution)/shard_map/ppermute | solution.py:132
  28.5 16.3 %collective-permute-start.11 = (bf16[256,256]{1,0:T(8,128)(2,1)S(1)}, bf16[256,256]{1,0:T(8,128)(2,1)}, u32[]{:S(2)}, u32[]{:S(2)}) collective-permute-start(bf16[256,256]{1,0:T(8,128)(2,1)S(1)} %get-tuple-element.23), channel_id=1, source_target_pairs={{0,10},{1,11},{2,8},{3,9},{4,14},{5,15},{6,12},{7,13},{8,2},{9,3},... | collective-permute-start | bytes 393224 | tf_op jit(solution)/shard_map/ppermute | solution.py:132
  34.2 116.4 %all-to-all-start = ((bf16[32,128,256]{2,1,0:T(8,128)(2,1)}), bf16[32,128,256]{2,1,0:T(8,128)(2,1)}, u32[]{:S(2)}, u32[]{:S(2)}) async-start(bf16[32,128,256]{2,1,0:T(8,128)(2,1)} %broadcast_select_fusion), calls=%async_computation | async-start | bytes 4194304 | tf_op jit(solution)/shard_map/all_to_all | solution.py:206
  38.0 48.5 %copy-start.8 = (s32[32]{0:T(128)S(1)}, s32[32]{0:T(128)}, u32[]{:S(2)}) copy-start(s32[32]{0:T(128)} %param.17) | copy-start | bytes 388
  39.5 36.7 %collective-permute-start.12 = (bf16[256,256]{1,0:T(8,128)(2,1)}, bf16[256,256]{1,0:T(8,128)(2,1)S(1)}, u32[]{:S(2)}, u32[]{:S(2)}) collective-permute-start(bf16[256,256]{1,0:T(8,128)(2,1)} %get-tuple-element.24), channel_id=1, source_target_pairs={{0,8},{1,9},{2,10},{3,11},{4,12},{5,13},{6,14},{7,15},{8,0},{9,1},... | collective-permute-start | bytes 393224 | tf_op jit(solution)/shard_map/ppermute | solution.py:132
  41.3 39.1 %collective-permute-start.13 = (bf16[256,256]{1,0:T(8,128)(2,1)}, bf16[256,256]{1,0:T(8,128)(2,1)S(1)}, u32[]{:S(2)}, u32[]{:S(2)}) collective-permute-start(bf16[256,256]{1,0:T(8,128)(2,1)} %get-tuple-element.25), channel_id=1, source_target_pairs={{0,6},{1,7},{2,4},{3,5},{4,2},{5,3},{6,0},{7,1},{8,14},{9,15},{10,... | collective-permute-start | bytes 393224 | tf_op jit(solution)/shard_map/ppermute | solution.py:132
  43.6 36.7 %collective-permute-start.14 = (bf16[256,256]{1,0:T(8,128)(2,1)}, bf16[256,256]{1,0:T(8,128)(2,1)S(1)}, u32[]{:S(2)}, u32[]{:S(2)}) collective-permute-start(bf16[256,256]{1,0:T(8,128)(2,1)} %get-tuple-element.26), channel_id=1, source_target_pairs={{0,4},{1,5},{2,6},{3,7},{4,0},{5,1},{6,2},{7,3},{8,12},{9,13},{10,... | collective-permute-start | bytes 393224 | tf_op jit(solution)/shard_map/ppermute | solution.py:132
  44.2 36.2 %collective-permute-start.15 = (bf16[256,256]{1,0:T(8,128)(2,1)S(1)}, bf16[256,256]{1,0:T(8,128)(2,1)S(1)}, u32[]{:S(2)}, u32[]{:S(2)}) collective-permute-start(bf16[256,256]{1,0:T(8,128)(2,1)S(1)} %get-tuple-element.27), channel_id=1, source_target_pairs={{0,2},{1,3},{2,0},{3,1},{4,6},{5,7},{6,4},{7,5},{8,10},{9,11},{10,... | collective-permute-start | bytes 393224 | tf_op jit(solution)/shard_map/ppermute | solution.py:132
  44.8 35.6 %collective-permute-start.9 = (bf16[256,256]{1,0:T(8,128)(2,1)S(1)}, bf16[256,256]{1,0:T(8,128)(2,1)S(1)}, u32[]{:S(2)}, u32[]{:S(2)}) collective-permute-start(bf16[256,256]{1,0:T(8,128)(2,1)S(1)} %get-tuple-element.21), channel_id=1, source_target_pairs={{0,14},{1,15},{2,12},{3,13},{4,10},{5,11},{6,8},{7,9},{8,6},{9,7},... | collective-permute-start | bytes 393224 | tf_op jit(solution)/shard_map/ppermute | solution.py:132
  76.2 19.8 %collective-permute-start.8 = (bf16[256,256]{1,0:T(8,128)(2,1)S(1)}, bf16[256,256]{1,0:T(8,128)(2,1)}, u32[]{:S(2)}, u32[]{:S(2)}) collective-permute-start(bf16[256,256]{1,0:T(8,128)(2,1)S(1)} %fusion.6), channel_id=1, source_target_pairs={{0,16},{1,17},{2,18},{3,19},{4,20},{5,21},{6,22},{7,23},{8,24},{9,... | collective-permute-start | bytes 393224 | tf_op jit(solution)/shard_map/ppermute | solution.py:152
  81.5 16.7 %collective-permute-start.16 = (bf16[256,256]{1,0:T(8,128)(2,1)S(1)}, bf16[256,256]{1,0:T(8,128)(2,1)S(1)}, u32[]{:S(2)}, u32[]{:S(2)}) collective-permute-start(bf16[256,256]{1,0:T(8,128)(2,1)S(1)} %fusion.13), channel_id=1, source_target_pairs={{0,16},{1,17},{2,18},{3,19},{4,20},{5,21},{6,22},{7,23},{8,24},{9,... | collective-permute-start | bytes 393224 | tf_op jit(solution)/shard_map/ppermute | solution.py:152
  99.2 34.0 %copy-start.1 = (bf16[256,1024]{1,0:T(8,128)(2,1)S(1)}, bf16[256,1024]{1,0:T(8,128)(2,1)}, u32[]{:S(2)}) copy-start(bf16[256,1024]{1,0:T(8,128)(2,1)} %q_ref.7) | copy-start | bytes 1572868
  99.2 34.0 %copy-start.2 = (bf16[512,256]{1,0:T(8,128)(2,1)S(1)}, bf16[512,256]{1,0:T(8,128)(2,1)}, u32[]{:S(2)}) copy-start(bf16[512,256]{1,0:T(8,128)(2,1)} %own_ref.1) | copy-start | bytes 786436
  99.2 34.0 %copy-start.3 = (bf16[256,256]{1,0:T(8,128)(2,1)S(1)}, bf16[256,256]{1,0:T(8,128)(2,1)}, u32[]{:S(2)}) copy-start(bf16[256,256]{1,0:T(8,128)(2,1)} %suffix_ref.3) | copy-start | bytes 393220
  99.2 6.2 %collective-permute-start.17 = (bf16[256,256]{1,0:T(8,128)(2,1)S(1)}, bf16[256,256]{1,0:T(8,128)(2,1)S(1)}, u32[]{:S(2)}, u32[]{:S(2)}) collective-permute-start(bf16[256,256]{1,0:T(8,128)(2,1)S(1)} %get-tuple-element.19), channel_id=1, source_target_pairs={{0,2},{1,3},{2,0},{3,1},{4,6},{5,7},{6,4},{7,5},{8,10},{9,11},{10,... | collective-permute-start | bytes 393224 | tf_op jit(solution)/shard_map/ppermute | solution.py:132
  100.5 7.8 %collective-permute-start.19 = (bf16[256,256]{1,0:T(8,128)(2,1)S(1)}, bf16[256,256]{1,0:T(8,128)(2,1)S(1)}, u32[]{:S(2)}, u32[]{:S(2)}) collective-permute-start(bf16[256,256]{1,0:T(8,128)(2,1)S(1)} %get-tuple-element.19), channel_id=1, source_target_pairs={{0,4},{1,5},{2,6},{3,7},{4,0},{5,1},{6,2},{7,3},{8,12},{9,13},{10,... | collective-permute-start | bytes 393224 | tf_op jit(solution)/shard_map/ppermute | solution.py:132
  101.9 6.4 %collective-permute-start.18 = (bf16[256,256]{1,0:T(8,128)(2,1)S(1)}, bf16[256,256]{1,0:T(8,128)(2,1)S(1)}, u32[]{:S(2)}, u32[]{:S(2)}) collective-permute-start(bf16[256,256]{1,0:T(8,128)(2,1)S(1)} %get-tuple-element.18), channel_id=1, source_target_pairs={{0,2},{1,3},{2,0},{3,1},{4,6},{5,7},{6,4},{7,5},{8,10},{9,11},{10,... | collective-permute-start | bytes 393224 | tf_op jit(solution)/shard_map/ppermute | solution.py:132
  102.4 10.8 %collective-permute-start.20 = (bf16[256,256]{1,0:T(8,128)(2,1)S(1)}, bf16[256,256]{1,0:T(8,128)(2,1)S(1)}, u32[]{:S(2)}, u32[]{:S(2)}) collective-permute-start(bf16[256,256]{1,0:T(8,128)(2,1)S(1)} %get-tuple-element.18), channel_id=1, source_target_pairs={{0,4},{1,5},{2,6},{3,7},{4,0},{5,1},{6,2},{7,3},{8,12},{9,13},{10,... | collective-permute-start | bytes 393224 | tf_op jit(solution)/shard_map/ppermute | solution.py:132
  103.3 10.0 %collective-permute-start.21 = (bf16[256,256]{1,0:T(8,128)(2,1)S(1)}, bf16[256,256]{1,0:T(8,128)(2,1)S(1)}, u32[]{:S(2)}, u32[]{:S(2)}) collective-permute-start(bf16[256,256]{1,0:T(8,128)(2,1)S(1)} %get-tuple-element.19), channel_id=1, source_target_pairs={{0,6},{1,7},{2,4},{3,5},{4,2},{5,3},{6,0},{7,1},{8,14},{9,15},{10,... | collective-permute-start | bytes 393224 | tf_op jit(solution)/shard_map/ppermute | solution.py:132
  105.4 10.9 %collective-permute-start.22 = (bf16[256,256]{1,0:T(8,128)(2,1)S(1)}, bf16[256,256]{1,0:T(8,128)(2,1)S(1)}, u32[]{:S(2)}, u32[]{:S(2)}) collective-permute-start(bf16[256,256]{1,0:T(8,128)(2,1)S(1)} %get-tuple-element.18), channel_id=1, source_target_pairs={{0,6},{1,7},{2,4},{3,5},{4,2},{5,3},{6,0},{7,1},{8,14},{9,15},{10,... | collective-permute-start | bytes 393224 | tf_op jit(solution)/shard_map/ppermute | solution.py:132
  108.3 8.9 %collective-permute-start.23 = (bf16[256,256]{1,0:T(8,128)(2,1)S(1)}, bf16[256,256]{1,0:T(8,128)(2,1)S(1)}, u32[]{:S(2)}, u32[]{:S(2)}) collective-permute-start(bf16[256,256]{1,0:T(8,128)(2,1)S(1)} %get-tuple-element.19), channel_id=1, source_target_pairs={{0,8},{1,9},{2,10},{3,11},{4,12},{5,13},{6,14},{7,15},{8,0},{9,1},... | collective-permute-start | bytes 393224 | tf_op jit(solution)/shard_map/ppermute | solution.py:132
  108.4 11.0 %collective-permute-start.24 = (bf16[256,256]{1,0:T(8,128)(2,1)S(1)}, bf16[256,256]{1,0:T(8,128)(2,1)S(1)}, u32[]{:S(2)}, u32[]{:S(2)}) collective-permute-start(bf16[256,256]{1,0:T(8,128)(2,1)S(1)} %get-tuple-element.18), channel_id=1, source_target_pairs={{0,8},{1,9},{2,10},{3,11},{4,12},{5,13},{6,14},{7,15},{8,0},{9,1},... | collective-permute-start | bytes 393224 | tf_op jit(solution)/shard_map/ppermute | solution.py:132
  113.2 8.0 %collective-permute-start.25 = (bf16[256,256]{1,0:T(8,128)(2,1)S(1)}, bf16[256,256]{1,0:T(8,128)(2,1)S(1)}, u32[]{:S(2)}, u32[]{:S(2)}) collective-permute-start(bf16[256,256]{1,0:T(8,128)(2,1)S(1)} %get-tuple-element.19), channel_id=1, source_target_pairs={{0,10},{1,11},{2,8},{3,9},{4,14},{5,15},{6,12},{7,13},{8,2},{9,3},... | collective-permute-start | bytes 393224 | tf_op jit(solution)/shard_map/ppermute | solution.py:132
  113.3 10.7 %collective-permute-start.26 = (bf16[256,256]{1,0:T(8,128)(2,1)S(1)}, bf16[256,256]{1,0:T(8,128)(2,1)S(1)}, u32[]{:S(2)}, u32[]{:S(2)}) collective-permute-start(bf16[256,256]{1,0:T(8,128)(2,1)S(1)} %get-tuple-element.18), channel_id=1, source_target_pairs={{0,10},{1,11},{2,8},{3,9},{4,14},{5,15},{6,12},{7,13},{8,2},{9,3},... | collective-permute-start | bytes 393224 | tf_op jit(solution)/shard_map/ppermute | solution.py:132
  116.3 10.2 %collective-permute-start.27 = (bf16[256,256]{1,0:T(8,128)(2,1)S(1)}, bf16[256,256]{1,0:T(8,128)(2,1)S(1)}, u32[]{:S(2)}, u32[]{:S(2)}) collective-permute-start(bf16[256,256]{1,0:T(8,128)(2,1)S(1)} %get-tuple-element.19), channel_id=1, source_target_pairs={{0,12},{1,13},{2,14},{3,15},{4,8},{5,9},{6,10},{7,11},{8,4},{9,5},... | collective-permute-start | bytes 393224 | tf_op jit(solution)/shard_map/ppermute | solution.py:132
  117.3 11.8 %collective-permute-start.28 = (bf16[256,256]{1,0:T(8,128)(2,1)S(1)}, bf16[256,256]{1,0:T(8,128)(2,1)S(1)}, u32[]{:S(2)}, u32[]{:S(2)}) collective-permute-start(bf16[256,256]{1,0:T(8,128)(2,1)S(1)} %get-tuple-element.18), channel_id=1, source_target_pairs={{0,12},{1,13},{2,14},{3,15},{4,8},{5,9},{6,10},{7,11},{8,4},{9,5},... | collective-permute-start | bytes 393224 | tf_op jit(solution)/shard_map/ppermute | solution.py:132
  119.4 11.6 %collective-permute-start.29 = (bf16[256,256]{1,0:T(8,128)(2,1)S(1)}, bf16[256,256]{1,0:T(8,128)(2,1)S(1)}, u32[]{:S(2)}, u32[]{:S(2)}) collective-permute-start(bf16[256,256]{1,0:T(8,128)(2,1)S(1)} %get-tuple-element.19), channel_id=1, source_target_pairs={{0,14},{1,15},{2,12},{3,13},{4,10},{5,11},{6,8},{7,9},{8,6},{9,7},... | collective-permute-start | bytes 393224 | tf_op jit(solution)/shard_map/ppermute | solution.py:132
  121.3 11.2 %collective-permute-start.30 = (bf16[256,256]{1,0:T(8,128)(2,1)S(1)}, bf16[256,256]{1,0:T(8,128)(2,1)S(1)}, u32[]{:S(2)}, u32[]{:S(2)}) collective-permute-start(bf16[256,256]{1,0:T(8,128)(2,1)S(1)} %get-tuple-element.18), channel_id=1, source_target_pairs={{0,14},{1,15},{2,12},{3,13},{4,10},{5,11},{6,8},{7,9},{8,6},{9,7},... | collective-permute-start | bytes 393224 | tf_op jit(solution)/shard_map/ppermute | solution.py:132
  132.5 9.5 %collective-permute-start.31 = (bf16[2048,256]{1,0:T(8,128)(2,1)S(1)}, bf16[2048,256]{1,0:T(8,128)(2,1)S(1)}, u32[]{:S(2)}, u32[]{:S(2)}) collective-permute-start(bf16[2048,256]{1,0:T(8,128)(2,1)S(1)} %get-tuple-element.35), channel_id=1, source_target_pairs={{0,1},{1,0},{2,3},{3,2},{4,5},{5,4},{6,7},{7,6},{8,9},{9,8},{10,11... | collective-permute-start | bytes 3145736 | tf_op jit(solution)/shard_map/ppermute | solution.py:129
  148.2 1.4 copy-start.4
  149.6 1.0 copy-start.6
  150.6 1.6 copy-start.5
  152.2 1.2 copy-start.7

commit v4 on v1

v4 whole, which is shorter than its diff:
```python
import functools

import jax
import jax.numpy as jnp
from jax import lax
from jax.experimental import pallas as pl
from jax.experimental.pallas import tpu as pltpu
from jax.sharding import PartitionSpec as P

LOG2E = 1.4426950408889634
DEAD_MARK = 1024.0
DEAD_ABOVE = 512.0
NEG = -1e30
CHUNK = 1024
PARAMS = pltpu.CompilerParams(vmem_limit_bytes=56 * 1024 * 1024)


def fold_keys(q_ref, m_ref, acc_ref, keys, values, factor, mask=None):
    heads, tokens, width = acc_ref.shape
    size = keys.shape[1]
    for head in range(heads):
        rows = q_ref[:, head * size:(head + 1) * size]
        scores = lax.dot_general(
            rows, keys, (((1,), (1,)), ((), ())), preferred_element_type=jnp.float32
        )
        if mask is not None:
            scores = jnp.where(mask, scores, NEG)
        old_max = m_ref[head]
        new_max = jnp.maximum(old_max, jnp.max(scores, axis=1, keepdims=True))
        shrink = jnp.exp2((old_max - new_max) * factor)
        weights = jnp.exp2((scores - jnp.tile(new_max, (1, keys.shape[0] // size))) * factor)
        m_ref[head] = new_max
        acc_ref[head] = acc_ref[head] * jnp.tile(shrink, (1, width // size)) + jnp.dot(
            weights.astype(jnp.bfloat16), values, preferred_element_type=jnp.float32
        )


def load_state(sums_ref, stat_ref, m_ref, acc_ref):
    heads, tokens, size = m_ref.shape
    for head in range(heads):
        acc_ref[head, :, :size] = sums_ref[head]
        acc_ref[head, :, size:] = jnp.broadcast_to(stat_ref[head, :, :1], (tokens, size))
        m_ref[head] = jnp.broadcast_to(stat_ref[head, :, size - 1:], (tokens, size))


def save_state(m_ref, acc_ref, sums_ref, stat_ref):
    heads, tokens, size = m_ref.shape
    left = lax.broadcasted_iota(jnp.int32, (tokens, size), 1) < size // 2
    for head in range(heads):
        sums_ref[head] = acc_ref[head, :, :size]
        stat_ref[head] = jnp.where(left, acc_ref[head, :, size:], m_ref[head])


def finish(acc_ref, out_ref):
    heads, tokens, width = acc_ref.shape
    size = width // 2
    for head in range(heads):
        out_ref[:, head * size:(head + 1) * size] = (
            acc_ref[head, :, :size] / acc_ref[head, :, size:]
        ).astype(out_ref.dtype)


def stage_live(rows, live, suffix_ref, keys_ref, values_ref):
    size = suffix_ref.shape[1] // 2
    zeros = jnp.zeros((rows.shape[0], size), jnp.float32)
    spare = jnp.broadcast_to(suffix_ref[:1, :size].astype(jnp.float32), zeros.shape)
    keys_ref[:rows.shape[0], :] = jnp.where(live, rows[:, :size], spare).astype(jnp.bfloat16)
    values_ref[:rows.shape[0], :size] = jnp.where(live, rows[:, size:], zeros).astype(jnp.bfloat16)
    values_ref[:rows.shape[0], size:] = jnp.where(live, 1.0, zeros).astype(jnp.bfloat16)


def fold_moved(factor, q_ref, kv_ref, suffix_ref, m_ref, acc_ref, keys_ref, values_ref):
    rows = kv_ref[...].reshape(-1, kv_ref.shape[-1]).astype(jnp.float32)
    size = suffix_ref.shape[1] // 2
    live = jnp.broadcast_to(rows[:, size:size + 1] < DEAD_ABOVE, (rows.shape[0], size))
    stage_live(rows, live, suffix_ref, keys_ref, values_ref)
    fold_keys(
        q_ref, m_ref, acc_ref, keys_ref[:rows.shape[0], :], values_ref[:rows.shape[0], :], factor
    )


def first_kernel(
    factor, len_ref, q_ref, suffix_ref, own_ref, kv_ref, sums_ref, stat_ref, m_ref, acc_ref,
    keys_ref, values_ref
):
    size = suffix_ref.shape[1] // 2
    suffix = suffix_ref.shape[0]
    own = own_ref.shape[0]

    @pl.when(pl.program_id(0) == 0)
    def _():
        m_ref[...] = jnp.full(m_ref.shape, NEG, jnp.float32)
        acc_ref[...] = jnp.zeros(acc_ref.shape, jnp.float32)
        values_ref[:suffix, :size] = suffix_ref[:, size:]
        values_ref[:suffix, size:] = jnp.ones((suffix, size), jnp.bfloat16)
        causal = lax.broadcasted_iota(jnp.int32, (suffix, suffix), 1) <= lax.broadcasted_iota(
            jnp.int32, (suffix, suffix), 0
        )
        fold_keys(
            q_ref, m_ref, acc_ref, suffix_ref[:, :size], values_ref[:suffix, :], factor, causal
        )
        live = lax.broadcasted_iota(jnp.int32, (own, size), 0) < len_ref[0]
        stage_live(own_ref[...].astype(jnp.float32), live, suffix_ref, keys_ref, values_ref)
        fold_keys(q_ref, m_ref, acc_ref, keys_ref[:own, :], values_ref[:own, :], factor)

    fold_moved(factor, q_ref, kv_ref, suffix_ref, m_ref, acc_ref, keys_ref, values_ref)

    @pl.when(pl.program_id(0) == pl.num_programs(0) - 1)
    def _():
        save_state(m_ref, acc_ref, sums_ref, stat_ref)


def moved_kernel(
    factor, q_ref, suffix_ref, kv_ref, sums_in, stat_in, sums_ref, stat_ref, m_ref, acc_ref,
    keys_ref, values_ref
):
    @pl.when(pl.program_id(0) == 0)
    def _():
        load_state(sums_in, stat_in, m_ref, acc_ref)

    fold_moved(factor, q_ref, kv_ref, suffix_ref, m_ref, acc_ref, keys_ref, values_ref)

    @pl.when(pl.program_id(0) == pl.num_programs(0) - 1)
    def _():
        save_state(m_ref, acc_ref, sums_ref, stat_ref)


def prefix_kernel(factor, last, count, which_ref, q_ref, *refs):
    pieces, refs = refs[:count], refs[count:]
    sums_in, stat_in = refs[:2]
    m_ref, acc_ref, keys_ref, values_ref = refs[-4:]
    size = keys_ref.shape[1]
    load_state(sums_in, stat_in, m_ref, acc_ref)
    for place, piece in enumerate(pieces):
        rows = pl.ds(place * piece.shape[0], piece.shape[0])
        keys_ref[rows, :] = piece[:, :size]
        values_ref[rows, :size] = piece[:, size:]
    values_ref[:, size:] = jnp.ones((values_ref.shape[0], size), jnp.bfloat16)
    chunk = min(CHUNK, keys_ref.shape[0])

    @pl.loop(0, keys_ref.shape[0] // chunk)
    def _(step):
        rows = pl.ds(pl.multiple_of(step * chunk, chunk), chunk)
        fold_keys(q_ref, m_ref, acc_ref, keys_ref[rows, :], values_ref[rows, :], factor)

    if last:
        finish(acc_ref, refs[2])
    else:
        save_state(m_ref, acc_ref, refs[2], refs[3])


def pack_kernel(target_ref, block_ref, count_ref, pool_ref, out_ref, mark_ref, sems):
    entries = target_ref.shape[1]
    mark_ref[...] = jnp.full(mark_ref.shape, DEAD_MARK, mark_ref.dtype)

    @pl.loop(0, entries)
    def _(entry):
        slot = out_ref.at[target_ref[0, entry]]
        live = entry < count_ref[0]

        @pl.when(live)
        def _():
            pltpu.make_async_copy(pool_ref.at[block_ref[0, entry]], slot, sems.at[entry]).start()

        @pl.when(jnp.logical_not(live))
        def _():
            pltpu.make_async_copy(mark_ref, slot, sems.at[entry]).start()

    @pl.loop(0, entries)
    def _(entry):
        pltpu.make_async_copy(mark_ref, out_ref.at[0], sems.at[entry]).wait()


def stage_kernel(owner_ref, place_ref, kept_ref, swapped_ref, *refs):
    pieces, sems = refs[:-1], refs[-1]
    core, chip = place_ref[0], place_ref[1]
    prefixes = owner_ref.shape[0]

    def copies(source, step, prefix):
        return pltpu.make_async_copy(
            source.at[core, chip ^ step], pieces[step].at[prefix], sems.at[step, prefix]
        )

    for step in range(len(pieces)):
        for prefix in range(prefixes):
            here = owner_ref[prefix] % 2 == core

            @pl.when(here)
            def _():
                copies(kept_ref, step, prefix).start()

            @pl.when(jnp.logical_not(here))
            def _():
                copies(swapped_ref, step, prefix).start()

    for step in range(len(pieces)):
        for prefix in range(prefixes):
            copies(kept_ref, step, prefix).wait()


def multicast(prefix_cache, owners, outgoing):
    replicas = lax.axis_size("replica")
    me = lax.axis_index("replica")
    half = replicas // 2
    chips = half // 2
    bits = chips.bit_length() - 1
    chip = me // 2 % chips
    width = prefix_cache.shape[1]

    def swap_cores(rows):
        return lax.ppermute(rows, "replica", [(i, i ^ 1) for i in range(replicas)])

    def to_peer(rows, step):
        return lax.ppermute(rows, "replica", [(i, i ^ (2 * step)) for i in range(replicas)])

    split = prefix_cache.reshape(2, chips, -1, width)
    swapped, outgoing = lax.optimization_barrier((swap_cores(prefix_cache), outgoing))
    swapped = swapped.reshape(split.shape)
    piece = jax.ShapeDtypeStruct((owners.shape[0], split.shape[2], width), split.dtype)
    anywhere = pl.BlockSpec(memory_space=pl.ANY)
    staged = pl.pallas_call(
        stage_kernel,
        out_shape=(piece,) * chips,
        in_specs=[pl.BlockSpec(memory_space=pltpu.SMEM)] * 2 + [anywhere] * 2,
        out_specs=(anywhere,) * chips,
        scratch_shapes=[pltpu.SemaphoreType.DMA((chips, owners.shape[0]))],
        compiler_params=PARAMS,
        name="stage_prefix",
    )(owners, jnp.stack([me % 2, chip]), split, swapped)
    away = chip ^ (owners // 2 % chips)
    found = staged[0]
    for step in range(chips - 1, 0, -1):
        rows = to_peer(staged[step], step)
        found = jnp.where((away == step)[:, None, None], rows, found)
    passed = lax.ppermute(found, "replica", [(i, (i + half) % replicas) for i in range(replicas)])
    held = jnp.where((owners // half == me // half)[:, None, None], found, passed)

    gathered = {0: held}
    for step in sorted(range(1, chips), key=lambda step: (step.bit_count(), step)):
        members = [bit for bit in range(bits) if step >> bit & 1]
        linked = [bit for bit in members if step >> ((bit - 1) % bits) & 1]
        last = 1 << min(linked or members)
        gathered[step] = to_peer(gathered[step ^ last], last)
    ours = [gathered[step] for step in range(chips)]
    return ours, [swap_cores(rows) for rows in ours], outgoing


def whole(shape):
    return pl.BlockSpec(shape, lambda *args: (0,) * len(shape))


def cost(rows, keys, size):
    return pl.CostEstimate(
        flops=6 * rows * keys * size, bytes_accessed=4 * keys * size, transcendentals=rows * keys
    )


def on_device(
    queries,
    suffix_kv,
    own_cache,
    ctx_len,
    prefix_cache,
    owners,
    readers,
    kv_pool,
    mig_target,
    mig_block,
    mig_count,
):
    me = lax.axis_index("replica")
    replicas = lax.axis_size("replica")
    size = suffix_kv.shape[1] // 2
    tokens = queries.shape[0]
    heads = queries.shape[1] // size
    factor = size ** (-0.5) * LOG2E
    row_count = tokens * heads
    state = (jax.ShapeDtypeStruct((heads, tokens, size), jnp.float32),) * 2
    state_specs = (whole(state[0].shape),) * 2
    in_smem = pl.BlockSpec(memory_space=pltpu.SMEM)
    anywhere = pl.BlockSpec(memory_space=pl.ANY)

    def scratch(keys):
        return [
            pltpu.VMEM((heads, tokens, size), jnp.float32),
            pltpu.VMEM((heads, tokens, 2 * size), jnp.float32),
            pltpu.VMEM((keys, size), jnp.bfloat16),
            pltpu.VMEM((keys, 2 * size), jnp.bfloat16),
        ]

    outgoing = pl.pallas_call(
        pack_kernel,
        out_shape=jax.ShapeDtypeStruct((replicas, *kv_pool.shape[1:]), kv_pool.dtype),
        in_specs=[in_smem] * 3 + [anywhere],
        out_specs=anywhere,
        scratch_shapes=[
            pltpu.VMEM(kv_pool.shape[1:], kv_pool.dtype),
            pltpu.SemaphoreType.DMA((mig_target.shape[1],)),
        ],
        compiler_params=PARAMS,
        name="pack_moved",
    )(mig_target, mig_block, mig_count, kv_pool)
    ours, theirs, outgoing = multicast(prefix_cache, owners, outgoing)
    arrived = lax.all_to_all(outgoing, "replica", split_axis=0, concat_axis=0, tiled=True)

    rows = arrived.shape[1]
    group = max(1, CHUNK // rows)
    steps = replicas // group
    first = max(1, steps // 2)
    most = max(group * rows, own_cache.shape[0], tokens)
    state_now = pl.pallas_call(
        functools.partial(first_kernel, factor),
        out_shape=state,
        grid=(first,),
        in_specs=[
            in_smem,
            whole(queries.shape),
            whole(suffix_kv.shape),
            whole(own_cache.shape),
            pl.BlockSpec((group, rows, 2 * size), lambda i: (i, 0, 0)),
        ],
        out_specs=state_specs,
        scratch_shapes=scratch(most),
        compiler_params=PARAMS,
        cost_estimate=cost(row_count, tokens + own_cache.shape[0] + first * group * rows, size),
        name="first_keys",
    )(ctx_len, queries, suffix_kv, own_cache, arrived)
    state_now = pl.pallas_call(
        functools.partial(moved_kernel, factor),
        out_shape=state,
        grid=(steps - first,),
        in_specs=[
            whole(queries.shape),
            whole(suffix_kv.shape),
            pl.BlockSpec((group, rows, 2 * size), lambda i: (i + first, 0, 0)),
            *state_specs,
        ],
        out_specs=state_specs,
        scratch_shapes=scratch(most),
        compiler_params=PARAMS,
        cost_estimate=cost(row_count, (steps - first) * group * rows, size),
        name="moved_keys",
    )(queries, suffix_kv, arrived, *state_now)

    for last, pieces in enumerate((ours, theirs)):
        rows = pieces[0].shape[1]
        state_now = pl.pallas_call(
            functools.partial(prefix_kernel, factor, last, len(pieces)),
            out_shape=jax.ShapeDtypeStruct(queries.shape, queries.dtype) if last else state,
            grid_spec=pltpu.PrefetchScalarGridSpec(
                num_scalar_prefetch=1,
                grid=(1,),
                in_specs=[
                    whole(queries.shape),
                    *[pl.BlockSpec((None, rows, 2 * size), lambda i, which: (which[0], 0, 0))]
                    * len(pieces),
                    *state_specs,
                ],
                out_specs=whole(queries.shape) if last else state_specs,
                scratch_shapes=scratch(len(pieces) * rows),
            ),
            compiler_params=PARAMS,
            cost_estimate=cost(row_count, len(pieces) * rows, size),
            name="prefix_keys",
        )(readers[me][None], queries, *pieces, *state_now)
    return state_now


def solution(mesh):
    in_specs = (
        P(("groups", "replica"), None),
        P(("groups", "replica"), None),
        P(("groups", "replica"), None),
        P(("groups", "replica")),
        P(("groups", "replica"), None),
        P("groups"),
        P("groups"),
        P(("groups", "replica"), None, None),
        P(("groups", "replica"), None),
        P(("groups", "replica"), None),
        P(("groups", "replica")),
    )
    out_specs = P(("groups", "replica"), None)
    return jax.shard_map(
        on_device, mesh=mesh, in_specs=in_specs, out_specs=out_specs, check_vma=False
    )
```

time: 243 us -> 243 us (level)
  waiting for transfers between devices: 166 us -> 36.3 us
  Pallas kernels: 30 us -> 155 us
  starting transfers between devices: 7.47 us -> 45 us
  between operations: 15 us -> 1.62 us
  local copies, waits for them, and re-layouts: 15.1 us -> 2.38 us
  other arithmetic: 8.67 us -> 1.84 us
    psum x1 -> x0, waiting for transfers between devices: 166 us -> none  [on_device(): shared = lax.psum(offered, 'replica')]
    pallas_call x3 -> x6, Pallas kernels: 30 us -> 155 us  [the longest x1 65.6 us: multicast(): pl.pallas_call(stage_kernel, out_shape=(piece,) * chips, in_specs=[pl.Blo...]
    ppermute x0 -> x24, waiting for transfers between devices: none -> 36.3 us  [the longest x14 25.6 us: to_peer(): lax.ppermute(rows, 'replica', [(i, i ^ 2 * step) for i in range(replicas)])]
    ppermute x0 -> x24, starting transfers between devices: none -> 20.9 us  [the longest x14 16.7 us: to_peer(): lax.ppermute(rows, 'replica', [(i, i ^ 2 * step) for i in range(replicas)])]
    all_to_all x1, starting transfers between devices: 7.43 us -> 24 us  [on_device(): lax.all_to_all(outgoing, 'replica', split_axis=0, concat_axis=0, tiled=True)]
    unnamed x30 -> x38, local copies, waits for them, and re-layouts: 12.5 us -> 1.78 us
    select_n x3 -> x2, other arithmetic: 7.09 us -> 1.21 us  [the longest x1 1.11 us: multicast(): found = jnp.where((away == step)[:, None, None], rows, found)]
  transfers between devices with their start and end apart: 2 -> 25, of which waited for: 1 -> 8; matrix products, arithmetic and copies ran while one was open for 2% -> 1% of each run, Pallas kernels for 6% -> 60%
where the time goes in v4:
time: 243 us; the launch traced here: 242 us
  Pallas kernels  155 us (64%)
  starting transfers between devices  45 us (19%)
  waiting for transfers between devices  36.3 us (15%)
    pallas_call x1, Pallas kernels, multicast(): pl.pallas_call(stage_kernel, out_shape=(piece,) * chips, in_specs=[pl.Blo...  65.6 us
    pallas_call x1, Pallas kernels, on_device(): pl.pallas_call(pack_kernel, out_shape=jax.ShapeDtypeStruct((replicas, *kv...  45.8 us
    ppermute x14, waiting for transfers between devices, to_peer(): lax.ppermute(rows, 'replica', [(i, i ^ 2 * step) for i in range(replicas)])  25.6 us
    all_to_all x1, starting transfers between devices, on_device(): lax.all_to_all(outgoing, 'replica', split_axis=0, concat_axis=0, tiled=True)  24 us
    pallas_call x2, Pallas kernels, on_device(): pl.pallas_call(functools.partial(prefix_kernel, factor, last, len(pieces)...  21.5 us
    ppermute x14, starting transfers between devices, to_peer(): lax.ppermute(rows, 'replica', [(i, i ^ 2 * step) for i in range(replicas)])  16.7 us
    pallas_call x1, Pallas kernels, on_device(): pl.pallas_call(functools.partial(first_kernel, factor), out_shape=state,...  11.5 us
    ppermute x1, waiting for transfers between devices, multicast(): lax.ppermute(found, 'replica', [(i, (i + half) % replicas) for i in range...  10.7 us
  transfers between devices with their start and end apart: 25, of which 8 were waited for; matrix products, arithmetic and copies ran while one was open for 1% of the time, Pallas kernels for 60%

profile of v4, /device:TPU:0, one launch (start us, length us, event | category | flops | bytes accessed | tf_op | source)
XLA Modules:
  0.0 241.7 jit_solution(16022855521803930084)
XLA Ops:
  0.0 0.5 collective-permute-start
  1.1 45.8 %pack_moved.1 = bf16[32,128,256]{2,1,0:T(8,128)(2,1)} custom-call(s32[1,32]{1,0:T(1,128)} %target_ref.1, s32[1,32]{1,0:T(1,128)} %block_ref.1, s32[1]{0:T(128)S(6)} %copy.13.count_ref, bf16[32,128,256]{2,1,0:T(8,128)(2,1)} %pool_ref.1), custom_call_target="tpu_custom_call" | custom-call | tf_op jit(solution)/shard_map/pack_moved/pallas_call | solution.py:291
  46.9 0.0 collective-permute-done
  46.9 24.0 %all-to-all-start = ((bf16[32,128,256]{2,1,0:T(8,128)(2,1)}), bf16[32,128,256]{2,1,0:T(8,128)(2,1)}, u32[]{:S(2)}, u32[]{:S(2)}) async-start(bf16[32,128,256]{2,1,0:T(8,128)(2,1)} %pack_moved.1), calls=%async_computation | async-start | bytes 4194304 | tf_op jit(solution)/shard_map/all_to_all | solution.py:304
  71.0 0.6 pad_add_fusion.place_ref
  71.6 65.6 %stage_prefix.1 = (bf16[2,256,256]{2,1,0:T(8,128)(2,1)}, bf16[2,256,256]{2,1,0:T(8,128)(2,1)}, bf16[2,256,256]{2,1,0:T(8,128)(2,1)}, bf16[2,256,256]{2,1,0:T(8,1...) custom-call(s32[2]{0:T(128)} %owner_ref.1, ...), custom_call_target="tpu_custom_call" | custom-call | tf_op jit(solution)/shard_map/stage_prefix/pallas_call | solution.py:221
  137.2 0.0 copy-start.18
  137.2 1.8 collective-permute-start.1
  139.0 1.5 collective-permute-start.2
  140.4 0.3 collective-permute-start.3
  140.8 1.7 collective-permute-start.4
  142.4 1.5 collective-permute-start.5
  143.9 2.7 %collective-permute-done.1 = bf16[2,256,256]{2,1,0:T(8,128)(2,1)S(1)} collective-permute-done((bf16[2,256,256]{2,1,0:T(8,128)(2,1)}, bf16[2,256,256]{2,1,0:T(8,128)(2,1)S(1)}, u32[]{:S(2)}, u32[]{:S(2)}) %collective-permute-start.1) | collective-permute-done | bytes 262176 | tf_op jit(solution)/shard_map/ppermute | solution.py:214
  146.6 2.6 %collective-permute-start.6 = (bf16[2,256,256]{2,1,0:T(8,128)(2,1)}, bf16[2,256,256]{2,1,0:T(8,128)(2,1)S(1)}, u32[]{:S(2)}, u32[]{:S(2)}) collective-permute-start(bf16[2,256,256]{2,1,0:T(8,128)(2,1)} %get-tuple-element.27), channel_id=1, source_target_pairs={{0,12},{1,13},{2,14},{3,15},{4,8},{5,9},{6,10},{7,11},{8,4},{9,5},... | collective-permute-start | bytes 786440 | tf_op jit(solution)/shard_map/ppermute | solution.py:214
  149.2 0.3 collective-permute-done.2
  149.5 1.3 collective-permute-start.7
  150.9 8.1 %collective-permute-done.3 = bf16[2,256,256]{2,1,0:T(8,128)(2,1)S(1)} collective-permute-done((bf16[2,256,256]{2,1,0:T(8,128)(2,1)}, bf16[2,256,256]{2,1,0:T(8,128)(2,1)S(1)}, u32[]{:S(2)}, u32[]{:S(2)}) %collective-permute-start.3) | collective-permute-done | bytes 262176 | tf_op jit(solution)/shard_map/ppermute | solution.py:214
  159.0 4.4 %collective-permute-done.6 = bf16[2,256,256]{2,1,0:T(8,128)(2,1)S(1)} collective-permute-done((bf16[2,256,256]{2,1,0:T(8,128)(2,1)}, bf16[2,256,256]{2,1,0:T(8,128)(2,1)S(1)}, u32[]{:S(2)}, u32[]{:S(2)}) %collective-permute-start.6) | collective-permute-done | bytes 262176 | tf_op jit(solution)/shard_map/ppermute | solution.py:214
  163.4 5.2 %collective-permute-done.7 = bf16[2,256,256]{2,1,0:T(8,128)(2,1)S(1)} collective-permute-done((bf16[2,256,256]{2,1,0:T(8,128)(2,1)}, bf16[2,256,256]{2,1,0:T(8,128)(2,1)S(1)}, u32[]{:S(2)}, u32[]{:S(2)}) %collective-permute-start.7) | collective-permute-done | bytes 262176 | tf_op jit(solution)/shard_map/ppermute | solution.py:214
  168.6 1.1 select_select_fusion
  169.7 2.5 %collective-permute-start.8 = (bf16[2,256,256]{2,1,0:T(8,128)(2,1)S(1)}, bf16[2,256,256]{2,1,0:T(8,128)(2,1)S(1)}, u32[]{:S(2)}, u32[]{:S(2)}) collective-permute-start(bf16[2,256,256]{2,1,0:T(8,128)(2,1)S(1)} %select_select_fusion), channel_id=1, source_target_pairs={{0,16},{1,17},{2,18},{3,19},{4,20},{5,21},{6,22},{7,23},{8,24},{9,... | collective-permute-start | bytes 786440 | tf_op jit(solution)/shard_map/ppermute | solution.py:235
  172.1 10.7 %collective-permute-done.8 = bf16[2,256,256]{2,1,0:T(8,128)(2,1)S(1)} collective-permute-done((bf16[2,256,256]{2,1,0:T(8,128)(2,1)S(1)}, bf16[2,256,256]{2,1,0:T(8,128)(2,1)S(1)}, u32[]{:S(2)}, u32[]{:S(2)}) %collective-permute-start.8) | collective-permute-done | bytes 262176 | tf_op jit(solution)/shard_map/ppermute | solution.py:235
  182.8 0.1 broadcast_select_fusion.refs_0_
  183.0 0.0 copy-start.1
  183.0 0.5 collective-permute-start.10
  183.5 1.4 collective-permute-start.12
  185.6 0.6 dynamic_slice.4.which_ref
  186.2 4.1 %collective-permute-done.10.refs_1_ = bf16[2,256,256]{2,1,0:T(8,128)(2,1)S(1)} collective-permute-done((bf16[2,256,256]{2,1,0:T(8,128)(2,1)S(1)}, bf16[2,256,256]{2,1,0:T(8,128)(2,1)S(1)}, u32[]{:S(2)}, u32[]{:S(2)}) %collective-permute-start.10) | collective-permute-done | bytes 262176 | tf_op jit(solution)/shard_map/ppermute | solution.py:214
  190.3 1.1 collective-permute-start.14
  191.4 1.0 collective-permute-start.20
  192.4 11.5 %first_keys.1 = (f32[8,256,128]{2,1,0:T(8,128)}, f32[8,256,128]{2,1,0:T(8,128)}) custom-call(s32[1]{0:T(128)S(6)} %copy.12.len_ref, bf16[256,1024]{1,0:T(8,128)(2,1)} %q_ref.7, bf16[256,256]{1,0:T(8,128)(2,1)} %suffix_ref.3, bf16[512,256]{1,0:T(8,128)(2,1)} %own_ref.1, bf16[32,128,256]{2,1,0:T(8,128)(2,1)} %all-to-all-done.kv_ref), custom_call_target="tpu_custom_call" | custom-call | flops 4429185024 | bytes 1441792 | tf_op jit(solution)/shard_map/first_keys/pallas_call | solution.py:311
  203.9 0.2 collective-permute-start.13
  204.1 1.2 collective-permute-start.18
  205.3 0.8 collective-permute-start.22
  206.2 10.2 %moved_keys.1 = (f32[8,256,128]{2,1,0:T(8,128)}, f32[8,256,128]{2,1,0:T(8,128)}) custom-call(bf16[256,1024]{1,0:T(8,128)(2,1)} %q_ref.7, bf16[256,256]{1,0:T(8,128)(2,1)} %suffix_ref.3, bf16[32,128,256]{2,1,0:T(8,128)(2,1)} %all-to-all-done.kv_ref, f32[8,256,128]{2,1,0:T(8,128)} %get-tuple-element.31.sums_in, f32[8,256,128]{2,1,0:T(8,128)} %get-tuple-element.32.stat_in), custom_call_target="tpu_custom_call" | custom-call | flops 3221225472 | bytes 1048576 | tf_op jit(solution)/shard_map/moved_keys/pallas_call | solution.py:328
  216.4 0.1 collective-permute-start.17
  216.5 0.5 collective-permute-start.21
  217.1 0.1 collective-permute-start.15
  217.2 0.4 collective-permute-start.19
  217.6 0.7 collective-permute-done.22.refs_7_
  218.3 0.7 copy-done.11
  219.0 11.0 %prefix_keys.2 = (f32[8,256,128]{2,1,0:T(8,128)}, f32[8,256,128]{2,1,0:T(8,128)}) custom-call(s32[1]{0:T(128)} %dynamic_slice.4.which_ref, bf16[256,1024]{1,0:T(8,128)(2,1)} %q_ref.7, bf16[2,256,256]{2,1,0:T(8,128)(2,1)} %copy-done.1, bf16[2,256,256]{2,1,0:T(8,128)(2,1)} %copy-done.4, bf16[2,256,256]{2,1,0:T(8,128)(2,1)} %copy-done.5, ...), custom_call_target="tpu_custom_call" | custom-call | flops 3221225472 | bytes 1048576 | tf_op jit(solution)/shard_map/prefix_keys/pallas_call | solution.py:347
  230.2 0.6 copy-done.13
  230.8 0.1 copy-done.15
  230.9 0.1 copy-done.16
  231.0 0.1 copy-done.14
  231.1 0.1 copy-done.17
  231.2 10.5 %prefix_keys.3 = bf16[256,1024]{1,0:T(8,128)(2,1)} custom-call(s32[1]{0:T(128)} %dynamic_slice.4.which_ref, bf16[256,1024]{1,0:T(8,128)(2,1)} %q_ref.7, bf16[2,256,256]{2,1,0:T(8,128)(2,1)} %copy-done.3, bf16[2,256,256]{2,1,0:T(8,128)(2,1)} %copy-done.6, bf16[2,256,256]{2,1,0:T(8,128)(2,1)} %copy-done.10, bf16[2,256,256]{2,1,0:T(8,128)(2,1)} %copy-done.15, ...), custom_call_target="tpu_custom_call" | custom-call | flops 3221225472 | bytes 1048576 | tf_op jit(solution)/shard_map/prefix_keys/pallas_call | solution.py:347
  (52 shorter events, 0.1 us)
Async XLA Ops:
  0.0 46.9 %collective-permute-start = (bf16[4096,256]{1,0:T(8,128)(2,1)}, bf16[4096,256]{1,0:T(8,128)(2,1)S(1)}, u32[]{:S(2)}, u32[]{:S(2)}) collective-permute-start(bf16[4096,256]{1,0:T(8,128)(2,1)} %param.15), channel_id=1, source_target_pairs={{0,1},{1,0},{2,3},{3,2},{4,5},{5,4},{6,7},{7,6},{8,9},{9,8},{10,11... | collective-permute-start | bytes 6291464 | tf_op jit(solution)/shard_map/ppermute | solution.py:211
  46.9 24.1 %copy-start = (bf16[4096,256]{1,0:T(8,128)(2,1)}, bf16[4096,256]{1,0:T(8,128)(2,1)S(1)}, u32[]{:S(2)}) copy-start(bf16[4096,256]{1,0:T(8,128)(2,1)S(1)} %collective-permute-done) | copy-start | bytes 6291460
  46.9 145.5 %all-to-all-start = ((bf16[32,128,256]{2,1,0:T(8,128)(2,1)}), bf16[32,128,256]{2,1,0:T(8,128)(2,1)}, u32[]{:S(2)}, u32[]{:S(2)}) async-start(bf16[32,128,256]{2,1,0:T(8,128)(2,1)} %pack_moved.1), calls=%async_computation | async-start | bytes 4194304 | tf_op jit(solution)/shard_map/all_to_all | solution.py:304
  71.6 79.2 %copy-start.2 = (s32[2]{0:T(128)S(1)}, s32[2]{0:T(128)}, u32[]{:S(2)}) copy-start(s32[2]{0:T(128)} %owner_ref.1) | copy-start | bytes 28
  137.2 48.4 %copy-start.18 = (s32[32]{0:T(128)S(1)}, s32[32]{0:T(128)}, u32[]{:S(2)}) copy-start(s32[32]{0:T(128)} %param.17) | copy-start | bytes 388
  137.2 9.4 %collective-permute-start.1 = (bf16[2,256,256]{2,1,0:T(8,128)(2,1)}, bf16[2,256,256]{2,1,0:T(8,128)(2,1)S(1)}, u32[]{:S(2)}, u32[]{:S(2)}) collective-permute-start(bf16[2,256,256]{2,1,0:T(8,128)(2,1)} %get-tuple-element.22), channel_id=1, source_target_pairs={{0,2},{1,3},{2,0},{3,1},{4,6},{5,7},{6,4},{7,5},{8,10},{9,11},{10,... | collective-permute-start | bytes 786440 | tf_op jit(solution)/shard_map/ppermute | solution.py:214
  139.0 10.6 %collective-permute-start.2 = (bf16[2,256,256]{2,1,0:T(8,128)(2,1)}, bf16[2,256,256]{2,1,0:T(8,128)(2,1)S(1)}, u32[]{:S(2)}, u32[]{:S(2)}) collective-permute-start(bf16[2,256,256]{2,1,0:T(8,128)(2,1)} %get-tuple-element.23), channel_id=1, source_target_pairs={{0,4},{1,5},{2,6},{3,7},{4,0},{5,1},{6,2},{7,3},{8,12},{9,13},{10,... | collective-permute-start | bytes 786440 | tf_op jit(solution)/shard_map/ppermute | solution.py:214
  140.4 18.6 %collective-permute-start.3 = (bf16[2,256,256]{2,1,0:T(8,128)(2,1)}, bf16[2,256,256]{2,1,0:T(8,128)(2,1)S(1)}, u32[]{:S(2)}, u32[]{:S(2)}) collective-permute-start(bf16[2,256,256]{2,1,0:T(8,128)(2,1)} %get-tuple-element.24), channel_id=1, source_target_pairs={{0,6},{1,7},{2,4},{3,5},{4,2},{5,3},{6,0},{7,1},{8,14},{9,15},{10,... | collective-permute-start | bytes 786440 | tf_op jit(solution)/shard_map/ppermute | solution.py:214
  140.8 18.2 %collective-permute-start.4 = (bf16[2,256,256]{2,1,0:T(8,128)(2,1)}, bf16[2,256,256]{2,1,0:T(8,128)(2,1)S(1)}, u32[]{:S(2)}, u32[]{:S(2)}) collective-permute-start(bf16[2,256,256]{2,1,0:T(8,128)(2,1)} %get-tuple-element.25), channel_id=1, source_target_pairs={{0,8},{1,9},{2,10},{3,11},{4,12},{5,13},{6,14},{7,15},{8,0},{9,1},... | collective-permute-start | bytes 786440 | tf_op jit(solution)/shard_map/ppermute | solution.py:214
  142.4 16.5 %collective-permute-start.5 = (bf16[2,256,256]{2,1,0:T(8,128)(2,1)}, bf16[2,256,256]{2,1,0:T(8,128)(2,1)S(1)}, u32[]{:S(2)}, u32[]{:S(2)}) collective-permute-start(bf16[2,256,256]{2,1,0:T(8,128)(2,1)} %get-tuple-element.26), channel_id=1, source_target_pairs={{0,10},{1,11},{2,8},{3,9},{4,14},{5,15},{6,12},{7,13},{8,2},{9,3},... | collective-permute-start | bytes 786440 | tf_op jit(solution)/shard_map/ppermute | solution.py:214
  146.6 16.7 %collective-permute-start.6 = (bf16[2,256,256]{2,1,0:T(8,128)(2,1)}, bf16[2,256,256]{2,1,0:T(8,128)(2,1)S(1)}, u32[]{:S(2)}, u32[]{:S(2)}) collective-permute-start(bf16[2,256,256]{2,1,0:T(8,128)(2,1)} %get-tuple-element.27), channel_id=1, source_target_pairs={{0,12},{1,13},{2,14},{3,15},{4,8},{5,9},{6,10},{7,11},{8,4},{9,5},... | collective-permute-start | bytes 786440 | tf_op jit(solution)/shard_map/ppermute | solution.py:214
  149.5 19.0 %collective-permute-start.7 = (bf16[2,256,256]{2,1,0:T(8,128)(2,1)}, bf16[2,256,256]{2,1,0:T(8,128)(2,1)S(1)}, u32[]{:S(2)}, u32[]{:S(2)}) collective-permute-start(bf16[2,256,256]{2,1,0:T(8,128)(2,1)} %get-tuple-element.28), channel_id=1, source_target_pairs={{0,14},{1,15},{2,12},{3,13},{4,10},{5,11},{6,8},{7,9},{8,6},{9,7},... | collective-permute-start | bytes 786440 | tf_op jit(solution)/shard_map/ppermute | solution.py:214
  169.7 13.2 %collective-permute-start.8 = (bf16[2,256,256]{2,1,0:T(8,128)(2,1)S(1)}, bf16[2,256,256]{2,1,0:T(8,128)(2,1)S(1)}, u32[]{:S(2)}, u32[]{:S(2)}) collective-permute-start(bf16[2,256,256]{2,1,0:T(8,128)(2,1)S(1)} %select_select_fusion), channel_id=1, source_target_pairs={{0,16},{1,17},{2,18},{3,19},{4,20},{5,21},{6,22},{7,23},{8,24},{9,... | collective-permute-start | bytes 786440 | tf_op jit(solution)/shard_map/ppermute | solution.py:235
  183.0 20.9 %copy-start.1 = (bf16[2,256,256]{2,1,0:T(8,128)(2,1)}, bf16[2,256,256]{2,1,0:T(8,128)(2,1)S(1)}, u32[]{:S(2)}) copy-start(bf16[2,256,256]{2,1,0:T(8,128)(2,1)S(1)} %broadcast_select_fusion.refs_0_) | copy-start | bytes 786436
  183.0 7.3 %collective-permute-start.10 = (bf16[2,256,256]{2,1,0:T(8,128)(2,1)S(1)}, bf16[2,256,256]{2,1,0:T(8,128)(2,1)S(1)}, u32[]{:S(2)}, u32[]{:S(2)}) collective-permute-start(bf16[2,256,256]{2,1,0:T(8,128)(2,1)S(1)} %broadcast_select_fusion.refs_0_), channel_id=1, source_target_pairs={{0,2},{1,3},{2,0},{3,1},{4,6},{5,7},{6,4},{7,5},{8,10},{9,11},{10,... | collective-permute-start | bytes 786440 | tf_op jit(solution)/shard_map/ppermute | solution.py:214
  183.5 7.9 %collective-permute-start.12 = (bf16[2,256,256]{2,1,0:T(8,128)(2,1)S(1)}, bf16[2,256,256]{2,1,0:T(8,128)(2,1)S(1)}, u32[]{:S(2)}, u32[]{:S(2)}) collective-permute-start(bf16[2,256,256]{2,1,0:T(8,128)(2,1)S(1)} %broadcast_select_fusion.refs_0_), channel_id=1, source_target_pairs={{0,4},{1,5},{2,6},{3,7},{4,0},{5,1},{6,2},{7,3},{8,12},{9,13},{10,... | collective-permute-start | bytes 786440 | tf_op jit(solution)/shard_map/ppermute | solution.py:214
  186.2 17.7 %collective-permute-start.16 = (bf16[2,256,256]{2,1,0:T(8,128)(2,1)S(1)}, bf16[2,256,256]{2,1,0:T(8,128)(2,1)S(1)}, u32[]{:S(2)}, u32[]{:S(2)}) collective-permute-start(bf16[2,256,256]{2,1,0:T(8,128)(2,1)S(1)} %broadcast_select_fusion.refs_0_), channel_id=1, source_target_pairs={{0,8},{1,9},{2,10},{3,11},{4,12},{5,13},{6,14},{7,15},{8,0},{9,1},... | collective-permute-start | bytes 786440 | tf_op jit(solution)/shard_map/ppermute | solution.py:214
  186.2 18.0 %collective-permute-start.9 = (bf16[2,256,256]{2,1,0:T(8,128)(2,1)S(1)}, bf16[2,256,256]{2,1,0:T(8,128)(2,1)S(1)}, u32[]{:S(2)}, u32[]{:S(2)}) collective-permute-start(bf16[2,256,256]{2,1,0:T(8,128)(2,1)S(1)} %broadcast_select_fusion.refs_0_), channel_id=1, source_target_pairs={{0,1},{1,0},{2,3},{3,2},{4,5},{5,4},{6,7},{7,6},{8,9},{9,8},{10,11... | collective-permute-start | bytes 786440 | tf_op jit(solution)/shard_map/ppermute | solution.py:211
  190.3 13.6 %copy-start.4 = (bf16[2,256,256]{2,1,0:T(8,128)(2,1)}, bf16[2,256,256]{2,1,0:T(8,128)(2,1)S(1)}, u32[]{:S(2)}) copy-start(bf16[2,256,256]{2,1,0:T(8,128)(2,1)S(1)} %collective-permute-done.10.refs_1_) | copy-start | bytes 786436
  190.3 26.1 %collective-permute-start.14 = (bf16[2,256,256]{2,1,0:T(8,128)(2,1)S(1)}, bf16[2,256,256]{2,1,0:T(8,128)(2,1)S(1)}, u32[]{:S(2)}, u32[]{:S(2)}) collective-permute-start(bf16[2,256,256]{2,1,0:T(8,128)(2,1)S(1)} %collective-permute-done.10.refs_1_), channel_id=1, source_target_pairs={{0,4},{1,5},{2,6},{3,7},{4,0},{5,1},{6,2},{7,3},{8,12},{9,13},{10,... | collective-permute-start | bytes 786440 | tf_op jit(solution)/shard_map/ppermute | solution.py:214
  191.4 25.7 %collective-permute-start.11 = (bf16[2,256,256]{2,1,0:T(8,128)(2,1)S(1)}, bf16[2,256,256]{2,1,0:T(8,128)(2,1)S(1)}, u32[]{:S(2)}, u32[]{:S(2)}) collective-permute-start(bf16[2,256,256]{2,1,0:T(8,128)(2,1)S(1)} %collective-permute-done.10.refs_1_), channel_id=1, source_target_pairs={{0,1},{1,0},{2,3},{3,2},{4,5},{5,4},{6,7},{7,6},{8,9},{9,8},{10,11... | collective-permute-start | bytes 786440 | tf_op jit(solution)/shard_map/ppermute | solution.py:211
  191.4 12.5 %copy-start.5 = (bf16[2,256,256]{2,1,0:T(8,128)(2,1)}, bf16[2,256,256]{2,1,0:T(8,128)(2,1)S(1)}, u32[]{:S(2)}) copy-start(bf16[2,256,256]{2,1,0:T(8,128)(2,1)S(1)} %collective-permute-done.12.refs_2_) | copy-start | bytes 786436
  191.4 13.9 %collective-permute-start.20 = (bf16[2,256,256]{2,1,0:T(8,128)(2,1)S(1)}, bf16[2,256,256]{2,1,0:T(8,128)(2,1)S(1)}, u32[]{:S(2)}, u32[]{:S(2)}) collective-permute-start(bf16[2,256,256]{2,1,0:T(8,128)(2,1)S(1)} %collective-permute-done.12.refs_2_), channel_id=1, source_target_pairs={{0,8},{1,9},{2,10},{3,11},{4,12},{5,13},{6,14},{7,15},{8,0},{9,1},... | collective-permute-start | bytes 786440 | tf_op jit(solution)/shard_map/ppermute | solution.py:214
  203.9 12.5 %copy-start.7 = (bf16[2,256,256]{2,1,0:T(8,128)(2,1)}, bf16[2,256,256]{2,1,0:T(8,128)(2,1)S(1)}, u32[]{:S(2)}) copy-start(bf16[2,256,256]{2,1,0:T(8,128)(2,1)S(1)} %collective-permute-done.16.refs_4_) | copy-start | bytes 786436
  203.9 13.3 %collective-permute-start.13 = (bf16[2,256,256]{2,1,0:T(8,128)(2,1)S(1)}, bf16[2,256,256]{2,1,0:T(8,128)(2,1)S(1)}, u32[]{:S(2)}, u32[]{:S(2)}) collective-permute-start(bf16[2,256,256]{2,1,0:T(8,128)(2,1)S(1)} %collective-permute-done.12.refs_2_), channel_id=1, source_target_pairs={{0,1},{1,0},{2,3},{3,2},{4,5},{5,4},{6,7},{7,6},{8,9},{9,8},{10,11... | collective-permute-start | bytes 786440 | tf_op jit(solution)/shard_map/ppermute | solution.py:211
  204.1 12.3 %copy-start.3 = (bf16[2,256,256]{2,1,0:T(8,128)(2,1)}, bf16[2,256,256]{2,1,0:T(8,128)(2,1)S(1)}, u32[]{:S(2)}) copy-start(bf16[2,256,256]{2,1,0:T(8,128)(2,1)S(1)} %collective-permute-done.9.refs_0_) | copy-start | bytes 786436
  204.1 12.4 %collective-permute-start.18 = (bf16[2,256,256]{2,1,0:T(8,128)(2,1)S(1)}, bf16[2,256,256]{2,1,0:T(8,128)(2,1)S(1)}, u32[]{:S(2)}, u32[]{:S(2)}) collective-permute-start(bf16[2,256,256]{2,1,0:T(8,128)(2,1)S(1)} %collective-permute-done.16.refs_4_), channel_id=1, source_target_pairs={{0,2},{1,3},{2,0},{3,1},{4,6},{5,7},{6,4},{7,5},{8,10},{9,11},{10,... | collective-permute-start | bytes 786440 | tf_op jit(solution)/shard_map/ppermute | solution.py:214
  205.3 11.2 %copy-start.9 = (bf16[2,256,256]{2,1,0:T(8,128)(2,1)}, bf16[2,256,256]{2,1,0:T(8,128)(2,1)S(1)}, u32[]{:S(2)}) copy-start(bf16[2,256,256]{2,1,0:T(8,128)(2,1)S(1)} %collective-permute-done.20.refs_6_) | copy-start | bytes 786436
  205.3 13.0 %collective-permute-start.22 = (bf16[2,256,256]{2,1,0:T(8,128)(2,1)S(1)}, bf16[2,256,256]{2,1,0:T(8,128)(2,1)S(1)}, u32[]{:S(2)}, u32[]{:S(2)}) collective-permute-start(bf16[2,256,256]{2,1,0:T(8,128)(2,1)S(1)} %collective-permute-done.20.refs_6_), channel_id=1, source_target_pairs={{0,2},{1,3},{2,0},{3,1},{4,6},{5,7},{6,4},{7,5},{8,10},{9,11},{10,... | collective-permute-start | bytes 786440 | tf_op jit(solution)/shard_map/ppermute | solution.py:214
  216.4 1.9 copy-start.8
  216.4 13.7 %collective-permute-start.17 = (bf16[2,256,256]{2,1,0:T(8,128)(2,1)S(1)}, bf16[2,256,256]{2,1,0:T(8,128)(2,1)S(1)}, u32[]{:S(2)}, u32[]{:S(2)}) collective-permute-start(bf16[2,256,256]{2,1,0:T(8,128)(2,1)S(1)} %collective-permute-done.16.refs_4_), channel_id=1, source_target_pairs={{0,1},{1,0},{2,3},{3,2},{4,5},{5,4},{6,7},{7,6},{8,9},{9,8},{10,11... | collective-permute-start | bytes 786440 | tf_op jit(solution)/shard_map/ppermute | solution.py:211
  216.5 1.8 copy-start.12
  216.5 13.6 %collective-permute-start.21 = (bf16[2,256,256]{2,1,0:T(8,128)(2,1)S(1)}, bf16[2,256,256]{2,1,0:T(8,128)(2,1)S(1)}, u32[]{:S(2)}, u32[]{:S(2)}) collective-permute-start(bf16[2,256,256]{2,1,0:T(8,128)(2,1)S(1)} %collective-permute-done.20.refs_6_), channel_id=1, source_target_pairs={{0,1},{1,0},{2,3},{3,2},{4,5},{5,4},{6,7},{7,6},{8,9},{9,8},{10,11... | collective-permute-start | bytes 786440 | tf_op jit(solution)/shard_map/ppermute | solution.py:211
  217.1 13.0 %copy-start.6 = (bf16[2,256,256]{2,1,0:T(8,128)(2,1)}, bf16[2,256,256]{2,1,0:T(8,128)(2,1)S(1)}, u32[]{:S(2)}) copy-start(bf16[2,256,256]{2,1,0:T(8,128)(2,1)S(1)} %collective-permute-done.11.refs_1_) | copy-start | bytes 786436
  217.1 13.0 %collective-permute-start.15 = (bf16[2,256,256]{2,1,0:T(8,128)(2,1)S(1)}, bf16[2,256,256]{2,1,0:T(8,128)(2,1)S(1)}, u32[]{:S(2)}, u32[]{:S(2)}) collective-permute-start(bf16[2,256,256]{2,1,0:T(8,128)(2,1)S(1)} %collective-permute-done.14.refs_3_), channel_id=1, source_target_pairs={{0,1},{1,0},{2,3},{3,2},{4,5},{5,4},{6,7},{7,6},{8,9},{9,8},{10,11... | collective-permute-start | bytes 786440 | tf_op jit(solution)/shard_map/ppermute | solution.py:211
  217.2 12.9 %copy-start.10 = (bf16[2,256,256]{2,1,0:T(8,128)(2,1)}, bf16[2,256,256]{2,1,0:T(8,128)(2,1)S(1)}, u32[]{:S(2)}) copy-start(bf16[2,256,256]{2,1,0:T(8,128)(2,1)S(1)} %collective-permute-done.13.refs_2_) | copy-start | bytes 786436
  217.2 13.0 %collective-permute-start.19 = (bf16[2,256,256]{2,1,0:T(8,128)(2,1)S(1)}, bf16[2,256,256]{2,1,0:T(8,128)(2,1)S(1)}, u32[]{:S(2)}, u32[]{:S(2)}) collective-permute-start(bf16[2,256,256]{2,1,0:T(8,128)(2,1)S(1)} %collective-permute-done.18.refs_5_), channel_id=1, source_target_pairs={{0,1},{1,0},{2,3},{3,2},{4,5},{5,4},{6,7},{7,6},{8,9},{9,8},{10,11... | collective-permute-start | bytes 786440 | tf_op jit(solution)/shard_map/ppermute | solution.py:211
  218.3 0.7 copy-start.11
  218.3 11.8 %collective-permute-start.23 = (bf16[2,256,256]{2,1,0:T(8,128)(2,1)S(1)}, bf16[2,256,256]{2,1,0:T(8,128)(2,1)S(1)}, u32[]{:S(2)}, u32[]{:S(2)}) collective-permute-start(bf16[2,256,256]{2,1,0:T(8,128)(2,1)S(1)} %collective-permute-done.22.refs_7_), channel_id=1, source_target_pairs={{0,1},{1,0},{2,3},{3,2},{4,5},{5,4},{6,7},{7,6},{8,9},{9,8},{10,11... | collective-permute-start | bytes 786440 | tf_op jit(solution)/shard_map/ppermute | solution.py:211
  230.1 0.7 copy-start.13
  230.1 0.8 copy-start.15
  230.1 0.9 copy-start.16
  230.1 1.0 copy-start.14
  230.2 1.0 copy-start.17

commit v5 on v4

--- a/solution.py
+++ b/solution.py
@@ -12,7 +12,7 @@
 DEAD_ABOVE = 512.0
 NEG = -1e30
 CHUNK = 1024
-PARAMS = pltpu.CompilerParams(vmem_limit_bytes=56 * 1024 * 1024)
+PARAMS = pltpu.CompilerParams(vmem_limit_bytes=40 * 1024 * 1024)
 
 
 def fold_keys(q_ref, m_ref, acc_ref, keys, values, factor, mask=None):
@@ -35,22 +35,6 @@
         )
 
 
-def load_state(sums_ref, stat_ref, m_ref, acc_ref):
-    heads, tokens, size = m_ref.shape
-    for head in range(heads):
-        acc_ref[head, :, :size] = sums_ref[head]
-        acc_ref[head, :, size:] = jnp.broadcast_to(stat_ref[head, :, :1], (tokens, size))
-        m_ref[head] = jnp.broadcast_to(stat_ref[head, :, size - 1:], (tokens, size))
-
-
-def save_state(m_ref, acc_ref, sums_ref, stat_ref):
-    heads, tokens, size = m_ref.shape
-    left = lax.broadcasted_iota(jnp.int32, (tokens, size), 1) < size // 2
-    for head in range(heads):
-        sums_ref[head] = acc_ref[head, :, :size]
-        stat_ref[head] = jnp.where(left, acc_ref[head, :, size:], m_ref[head])
-
-
 def finish(acc_ref, out_ref):
     heads, tokens, width = acc_ref.shape
     size = width // 2
@@ -80,8 +64,7 @@
 
 
 def first_kernel(
-    factor, len_ref, q_ref, suffix_ref, own_ref, kv_ref, sums_ref, stat_ref, m_ref, acc_ref,
-    keys_ref, values_ref
+    factor, len_ref, q_ref, suffix_ref, own_ref, kv_ref, m_ref, acc_ref, keys_ref, values_ref
 ):
     size = suffix_ref.shape[1] // 2
     suffix = suffix_ref.shape[0]
@@ -105,70 +88,59 @@
 
     fold_moved(factor, q_ref, kv_ref, suffix_ref, m_ref, acc_ref, keys_ref, values_ref)
 
-    @pl.when(pl.program_id(0) == pl.num_programs(0) - 1)
-    def _():
-        save_state(m_ref, acc_ref, sums_ref, stat_ref)
-
-
-def moved_kernel(
-    factor, q_ref, suffix_ref, kv_ref, sums_in, stat_in, sums_ref, stat_ref, m_ref, acc_ref,
-    keys_ref, values_ref
-):
-    @pl.when(pl.program_id(0) == 0)
-    def _():
-        load_state(sums_in, stat_in, m_ref, acc_ref)
-
-    fold_moved(factor, q_ref, kv_ref, suffix_ref, m_ref, acc_ref, keys_ref, values_ref)
-
-    @pl.when(pl.program_id(0) == pl.num_programs(0) - 1)
-    def _():
-        save_state(m_ref, acc_ref, sums_ref, stat_ref)
-
 
 def prefix_kernel(factor, last, count, which_ref, q_ref, *refs):
     pieces, refs = refs[:count], refs[count:]
-    sums_in, stat_in = refs[:2]
+    m_in, acc_in, out_ref = refs[:3]
     m_ref, acc_ref, keys_ref, values_ref = refs[-4:]
     size = keys_ref.shape[1]
-    load_state(sums_in, stat_in, m_ref, acc_ref)
-    for place, piece in enumerate(pieces):
-        rows = pl.ds(place * piece.shape[0], piece.shape[0])
-        keys_ref[rows, :] = piece[:, :size]
-        values_ref[rows, :size] = piece[:, size:]
-    values_ref[:, size:] = jnp.ones((values_ref.shape[0], size), jnp.bfloat16)
     chunk = min(CHUNK, keys_ref.shape[0])
-
-    @pl.loop(0, keys_ref.shape[0] // chunk)
-    def _(step):
-        rows = pl.ds(pl.multiple_of(step * chunk, chunk), chunk)
-        fold_keys(q_ref, m_ref, acc_ref, keys_ref[rows, :], values_ref[rows, :], factor)
-
+    step = pl.program_id(0)
+
+    @pl.when(step == 0)
+    def _():
+        m_ref[...] = m_in[...]
+        acc_ref[...] = acc_in[...]
+        for place, piece in enumerate(pieces):
+            rows = pl.ds(place * piece.shape[0], piece.shape[0])
+            keys_ref[rows, :] = piece[:, :size]
+            values_ref[rows, :size] = piece[:, size:]
+        values_ref[:, size:] = jnp.ones((values_ref.shape[0], size), jnp.bfloat16)
+
+    rows = pl.ds(pl.multiple_of(step * chunk, chunk), chunk)
+    fold_keys(q_ref, m_ref, acc_ref, keys_ref[rows, :], values_ref[rows, :], factor)
     if last:
-        finish(acc_ref, refs[2])
-    else:
-        save_state(m_ref, acc_ref, refs[2], refs[3])
-
-
-def pack_kernel(target_ref, block_ref, count_ref, pool_ref, out_ref, mark_ref, sems):
+
+        @pl.when(step == pl.num_programs(0) - 1)
+        def _():
+            finish(acc_ref, out_ref)
+
+
+def pack_kernel(target_ref, block_ref, count_ref, pool_ref, out_ref, sems):
     entries = target_ref.shape[1]
-    mark_ref[...] = jnp.full(mark_ref.shape, DEAD_MARK, mark_ref.dtype)
+
+    def block(entry):
+        return pltpu.make_async_copy(
+            pool_ref.at[block_ref[0, entry]], out_ref.at[target_ref[0, entry]], sems.at[entry]
+        )
 
     @pl.loop(0, entries)
     def _(entry):
-        slot = out_ref.at[target_ref[0, entry]]
         live = entry < count_ref[0]
 
         @pl.when(live)
         def _():
-            pltpu.make_async_copy(pool_ref.at[block_ref[0, entry]], slot, sems.at[entry]).start()
+            block(entry).start()
 
         @pl.when(jnp.logical_not(live))
         def _():
-            pltpu.make_async_copy(mark_ref, slot, sems.at[entry]).start()
+            out_ref[target_ref[0, entry]] = jnp.full(out_ref.shape[1:], DEAD_MARK, out_ref.dtype)
 
     @pl.loop(0, entries)
     def _(entry):
-        pltpu.make_async_copy(mark_ref, out_ref.at[0], sems.at[entry]).wait()
+        @pl.when(entry < count_ref[0])
+        def _():
+            block(entry).wait()
 
 
 def stage_kernel(owner_ref, place_ref, kept_ref, swapped_ref, *refs):
@@ -222,7 +194,8 @@
         stage_kernel,
         out_shape=(piece,) * chips,
         in_specs=[pl.BlockSpec(memory_space=pltpu.SMEM)] * 2 + [anywhere] * 2,
-        out_specs=(anywhere,) * chips,
+        out_specs=(whole(piece.shape),) * chips,
+        grid=(1,),
         scratch_shapes=[pltpu.SemaphoreType.DMA((chips, owners.shape[0]))],
         compiler_params=PARAMS,
         name="stage_prefix",
@@ -241,8 +214,10 @@
         linked = [bit for bit in members if step >> ((bit - 1) % bits) & 1]
         last = 1 << min(linked or members)
         gathered[step] = to_peer(gathered[step ^ last], last)
-    ours = [gathered[step] for step in range(chips)]
-    return ours, [swap_cores(rows) for rows in ours], outgoing
+    parts = [[], []]
+    for step, rows in gathered.items():
+        parts[step.bit_count() > 1].extend((rows, swap_cores(rows)))
+    return parts, outgoing
 
 
 def whole(shape):
@@ -275,15 +250,16 @@
     heads = queries.shape[1] // size
     factor = size ** (-0.5) * LOG2E
     row_count = tokens * heads
-    state = (jax.ShapeDtypeStruct((heads, tokens, size), jnp.float32),) * 2
-    state_specs = (whole(state[0].shape),) * 2
+    state = (
+        jax.ShapeDtypeStruct((heads, tokens, size), jnp.float32),
+        jax.ShapeDtypeStruct((heads, tokens, 2 * size), jnp.float32),
+    )
+    state_specs = (whole(state[0].shape), whole(state[1].shape))
     in_smem = pl.BlockSpec(memory_space=pltpu.SMEM)
     anywhere = pl.BlockSpec(memory_space=pl.ANY)
 
     def scratch(keys):
         return [
-            pltpu.VMEM((heads, tokens, size), jnp.float32),
-            pltpu.VMEM((heads, tokens, 2 * size), jnp.float32),
             pltpu.VMEM((keys, size), jnp.bfloat16),
             pltpu.VMEM((keys, 2 * size), jnp.bfloat16),
         ]
@@ -292,26 +268,21 @@
         pack_kernel,
         out_shape=jax.ShapeDtypeStruct((replicas, *kv_pool.shape[1:]), kv_pool.dtype),
         in_specs=[in_smem] * 3 + [anywhere],
-        out_specs=anywhere,
-        scratch_shapes=[
-            pltpu.VMEM(kv_pool.shape[1:], kv_pool.dtype),
-            pltpu.SemaphoreType.DMA((mig_target.shape[1],)),
-        ],
+        out_specs=whole((replicas, *kv_pool.shape[1:])),
+        grid=(1,),
+        scratch_shapes=[pltpu.SemaphoreType.DMA((mig_target.shape[1],))],
         compiler_params=PARAMS,
         name="pack_moved",
     )(mig_target, mig_block, mig_count, kv_pool)
-    ours, theirs, outgoing = multicast(prefix_cache, owners, outgoing)
+    shared, outgoing = multicast(prefix_cache, owners, outgoing)
     arrived = lax.all_to_all(outgoing, "replica", split_axis=0, concat_axis=0, tiled=True)
 
     rows = arrived.shape[1]
     group = max(1, CHUNK // rows)
-    steps = replicas // group
-    first = max(1, steps // 2)
-    most = max(group * rows, own_cache.shape[0], tokens)
     state_now = pl.pallas_call(
         functools.partial(first_kernel, factor),
         out_shape=state,
-        grid=(first,),
+        grid=(replicas // group,),
         in_specs=[
             in_smem,
             whole(queries.shape),
@@ -320,36 +291,21 @@
             pl.BlockSpec((group, rows, 2 * size), lambda i: (i, 0, 0)),
         ],
         out_specs=state_specs,
-        scratch_shapes=scratch(most),
+        scratch_shapes=scratch(max(group * rows, own_cache.shape[0], tokens)),
         compiler_params=PARAMS,
-        cost_estimate=cost(row_count, tokens + own_cache.shape[0] + first * group * rows, size),
-        name="first_keys",
+        cost_estimate=cost(row_count, tokens + own_cache.shape[0] + replicas * rows, size),
+        name="moved_keys",
     )(ctx_len, queries, suffix_kv, own_cache, arrived)
-    state_now = pl.pallas_call(
-        functools.partial(moved_kernel, factor),
-        out_shape=state,
-        grid=(steps - first,),
-        in_specs=[
-            whole(queries.shape),
-            whole(suffix_kv.shape),
-            pl.BlockSpec((group, rows, 2 * size), lambda i: (i + first, 0, 0)),
-            *state_specs,
-        ],
-        out_specs=state_specs,
-        scratch_shapes=scratch(most),
-        compiler_params=PARAMS,
-        cost_estimate=cost(row_count, (steps - first) * group * rows, size),
-        name="moved_keys",
-    )(queries, suffix_kv, arrived, *state_now)
-
-    for last, pieces in enumerate((ours, theirs)):
+
+    for last, pieces in enumerate(shared):
         rows = pieces[0].shape[1]
+        keys = len(pieces) * rows
         state_now = pl.pallas_call(
             functools.partial(prefix_kernel, factor, last, len(pieces)),
             out_shape=jax.ShapeDtypeStruct(queries.shape, queries.dtype) if last else state,
             grid_spec=pltpu.PrefetchScalarGridSpec(
                 num_scalar_prefetch=1,
-                grid=(1,),
+                grid=(max(1, keys // CHUNK),),
                 in_specs=[
                     whole(queries.shape),
                     *[pl.BlockSpec((None, rows, 2 * size), lambda i, which: (which[0], 0, 0))]
@@ -357,10 +313,11 @@
                     *state_specs,
                 ],
                 out_specs=whole(queries.shape) if last else state_specs,
-                scratch_shapes=scratch(len(pieces) * rows),
+                scratch_shapes=[pltpu.VMEM(part.shape, part.dtype) for part in state] * last
+                + scratch(keys),
             ),
             compiler_params=PARAMS,
-            cost_estimate=cost(row_count, len(pieces) * rows, size),
+            cost_estimate=cost(row_count, keys, size),
             name="prefix_keys",
         )(readers[me][None], queries, *pieces, *state_now)
     return state_now

time: 243 us -> 146 us (0.60)
  Pallas kernels: 155 us -> 44.5 us
  waiting for transfers between devices: 36.3 us -> 63.6 us
  starting transfers between devices: 45 us -> 28.2 us
  local copies, waits for them, and re-layouts: 2.38 us -> 7.24 us
    pallas_call x1, Pallas kernels: 65.6 us -> 4.46 us  [multicast(): pl.pallas_call(stage_kernel, out_shape=(piece,) * chips, in_specs=[pl.Blo...]
    pallas_call x1, Pallas kernels: 45.8 us -> 5.83 us  [on_device(): pl.pallas_call(pack_kernel, out_shape=jax.ShapeDtypeStruct((replicas, *kv...]
    ppermute x14, waiting for transfers between devices: 25.6 us -> 51.8 us  [to_peer(): lax.ppermute(rows, 'replica', [(i, i ^ 2 * step) for i in range(replicas)])]
    all_to_all x1, starting transfers between devices: 24 us -> 6.21 us  [on_device(): lax.all_to_all(outgoing, 'replica', split_axis=0, concat_axis=0, tiled=True)]
    pallas_call x1 -> x0, Pallas kernels: 10.2 us -> none  [on_device(): pl.pallas_call(functools.partial(moved_kernel, factor), out_shape=state,...]
    pallas_call x1, Pallas kernels: 11.5 us -> 16.8 us  [on_device(): pl.pallas_call(functools.partial(first_kernel, factor), out_shape=state,...]
    unnamed x38 -> x24, local copies, waits for them, and re-layouts: 1.78 us -> 6.58 us
    pallas_call x2, Pallas kernels: 21.5 us -> 17.4 us  [on_device(): pl.pallas_call(functools.partial(prefix_kernel, factor, last, len(pieces)...]
  transfers between devices with their start and end apart: 25 -> 25, of which waited for: 8 -> 11; matrix products, arithmetic and copies ran while one was open for 1% -> 1% of each run, Pallas kernels for 60% -> 24%
where the time goes in v5:
time: 146 us; the launch traced here: 145 us
  waiting for transfers between devices  63.6 us (44%)
  Pallas kernels  44.5 us (30%)
  starting transfers between devices  28.2 us (19%)
  local copies, waits for them, and re-layouts  7.24 us (5%)
  between operations  1.56 us (1%)
    ppermute x14, waiting for transfers between devices, to_peer(): lax.ppermute(rows, 'replica', [(i, i ^ 2 * step) for i in range(replicas)])  51.8 us
    pallas_call x2, Pallas kernels, on_device(): pl.pallas_call(functools.partial(prefix_kernel, factor, last, len(pieces)...  17.4 us
    pallas_call x1, Pallas kernels, on_device(): pl.pallas_call(functools.partial(first_kernel, factor), out_shape=state,...  16.8 us
    ppermute x14, starting transfers between devices, to_peer(): lax.ppermute(rows, 'replica', [(i, i ^ 2 * step) for i in range(replicas)])  16.5 us
    ppermute x1, waiting for transfers between devices, multicast(): lax.ppermute(found, 'replica', [(i, (i + half) % replicas) for i in range...  11.7 us
    unnamed x24, local copies, waits for them, and re-layouts  6.58 us
    all_to_all x1, starting transfers between devices, on_device(): lax.all_to_all(outgoing, 'replica', split_axis=0, concat_axis=0, tiled=True)  6.21 us
    pallas_call x1, Pallas kernels, on_device(): pl.pallas_call(pack_kernel, out_shape=jax.ShapeDtypeStruct((replicas, *kv...  5.83 us
  transfers between devices with their start and end apart: 25, of which 11 were waited for; matrix products, arithmetic and copies ran while one was open for 1% of the time, Pallas kernels for 24%

profile of v5, /device:TPU:0, one launch (start us, length us, event | category | flops | bytes accessed | tf_op | source)
XLA Modules:
  0.0 145.4 jit_solution(17021020620333176845)
XLA Ops:
  0.0 0.5 collective-permute-start
  1.1 1.6 %copy-done = bf16[32,128,256]{2,1,0:T(8,128)(2,1)S(1)} copy-done((bf16[32,128,256]{2,1,0:T(8,128)(2,1)S(1)}, bf16[32,128,256]{2,1,0:T(8,128)(2,1)}, u32[]{:S(2)}) %copy-start) | copy-done | bytes 2097176
  2.7 0.7 copy-done.5
  3.4 0.7 copy-done.6
  4.0 5.8 %pack_moved.1 = bf16[32,128,256]{2,1,0:T(8,128)(2,1)} custom-call(s32[1,32]{1,0:T(1,128)S(1)} %copy-done.5, s32[1,32]{1,0:T(1,128)S(1)} %copy-done.6, s32[1]{0:T(128)S(6)} %copy.13.count_ref, bf16[32,128,256]{2,1,0:T(8,128)(2,1)S(1)} %copy-done), custom_call_target="tpu_custom_call" | custom-call | tf_op jit(solution)/shard_map/pack_moved/pallas_call | solution.py:267
  9.8 0.0 copy-start.1
  9.9 0.0 copy-start.4
  9.9 1.4 copy-done.2
  11.3 6.2 %all-to-all-start = ((bf16[32,128,256]{2,1,0:T(8,128)(2,1)}), bf16[32,128,256]{2,1,0:T(8,128)(2,1)}, u32[]{:S(2)}, u32[]{:S(2)}) async-start(bf16[32,128,256]{2,1,0:T(8,128)(2,1)} %pack_moved.1), calls=%async_computation | async-start | bytes 4194304 | tf_op jit(solution)/shard_map/all_to_all | solution.py:278
  17.5 0.1 pad_add_fusion.place_ref
  17.6 1.6 %copy-done.3 = bf16[4096,256]{1,0:T(8,128)(2,1)S(1)} copy-done((bf16[4096,256]{1,0:T(8,128)(2,1)S(1)}, bf16[4096,256]{1,0:T(8,128)(2,1)}, u32[]{:S(2)}) %copy-start.3) | copy-done | bytes 2097176
  19.2 4.5 %stage_prefix.1 = (bf16[2,256,256]{2,1,0:T(8,128)(2,1)S(1)}, bf16[2,256,256]{2,1,0:T(8,128)(2,1)}, bf16[2,256,256]{2,1,0:T(8,128)(2,1)}, bf16[2,256,256]{2,1,0:T...) custom-call(s32[2]{0:T(128)S(1)} %copy-done.4, ...), custom_call_target="tpu_custom_call" | custom-call | tf_op jit(solution)/shard_map/stage_prefix/pallas_call | solution.py:193
  23.7 0.7 copy-done.9
  24.4 1.8 %collective-permute-start.1 = (bf16[2,256,256]{2,1,0:T(8,128)(2,1)}, bf16[2,256,256]{2,1,0:T(8,128)(2,1)S(1)}, u32[]{:S(2)}, u32[]{:S(2)}) collective-permute-start(bf16[2,256,256]{2,1,0:T(8,128)(2,1)} %get-tuple-element.20), channel_id=1, source_target_pairs={{0,2},{1,3},{2,0},{3,1},{4,6},{5,7},{6,4},{7,5},{8,10},{9,11},{10,... | collective-permute-start | bytes 786440 | tf_op jit(solution)/shard_map/ppermute | solution.py:186
  26.1 1.5 %collective-permute-start.2 = (bf16[2,256,256]{2,1,0:T(8,128)(2,1)}, bf16[2,256,256]{2,1,0:T(8,128)(2,1)S(1)}, u32[]{:S(2)}, u32[]{:S(2)}) collective-permute-start(bf16[2,256,256]{2,1,0:T(8,128)(2,1)} %get-tuple-element.21), channel_id=1, source_target_pairs={{0,4},{1,5},{2,6},{3,7},{4,0},{5,1},{6,2},{7,3},{8,12},{9,13},{10,... | collective-permute-start | bytes 786440 | tf_op jit(solution)/shard_map/ppermute | solution.py:186
  27.6 0.3 collective-permute-start.3
  27.9 1.7 %collective-permute-start.4 = (bf16[2,256,256]{2,1,0:T(8,128)(2,1)S(1)}, bf16[2,256,256]{2,1,0:T(8,128)(2,1)S(1)}, u32[]{:S(2)}, u32[]{:S(2)}) collective-permute-start(bf16[2,256,256]{2,1,0:T(8,128)(2,1)S(1)} %get-tuple-element.23), channel_id=1, source_target_pairs={{0,8},{1,9},{2,10},{3,11},{4,12},{5,13},{6,14},{7,15},{8,0},{9,1},... | collective-permute-start | bytes 786440 | tf_op jit(solution)/shard_map/ppermute | solution.py:186
  29.6 1.5 %collective-permute-start.5 = (bf16[2,256,256]{2,1,0:T(8,128)(2,1)S(1)}, bf16[2,256,256]{2,1,0:T(8,128)(2,1)S(1)}, u32[]{:S(2)}, u32[]{:S(2)}) collective-permute-start(bf16[2,256,256]{2,1,0:T(8,128)(2,1)S(1)} %get-tuple-element.24), channel_id=1, source_target_pairs={{0,10},{1,11},{2,8},{3,9},{4,14},{5,15},{6,12},{7,13},{8,2},{9,3},... | collective-permute-start | bytes 786440 | tf_op jit(solution)/shard_map/ppermute | solution.py:186
  31.1 8.5 %collective-permute-done.1 = bf16[2,256,256]{2,1,0:T(8,128)(2,1)S(1)} collective-permute-done((bf16[2,256,256]{2,1,0:T(8,128)(2,1)}, bf16[2,256,256]{2,1,0:T(8,128)(2,1)S(1)}, u32[]{:S(2)}, u32[]{:S(2)}) %collective-permute-start.1) | collective-permute-done | bytes 262176 | tf_op jit(solution)/shard_map/ppermute | solution.py:186
  39.6 4.0 %collective-permute-start.6 = (bf16[2,256,256]{2,1,0:T(8,128)(2,1)S(1)}, bf16[2,256,256]{2,1,0:T(8,128)(2,1)S(1)}, u32[]{:S(2)}, u32[]{:S(2)}) collective-permute-start(bf16[2,256,256]{2,1,0:T(8,128)(2,1)S(1)} %get-tuple-element.25), channel_id=1, source_target_pairs={{0,12},{1,13},{2,14},{3,15},{4,8},{5,9},{6,10},{7,11},{8,4},{9,5},... | collective-permute-start | bytes 786440 | tf_op jit(solution)/shard_map/ppermute | solution.py:186
  43.6 0.9 collective-permute-done.2
  44.5 2.5 %collective-permute-start.7 = (bf16[2,256,256]{2,1,0:T(8,128)(2,1)S(1)}, bf16[2,256,256]{2,1,0:T(8,128)(2,1)S(1)}, u32[]{:S(2)}, u32[]{:S(2)}) collective-permute-start(bf16[2,256,256]{2,1,0:T(8,128)(2,1)S(1)} %get-tuple-element.26), channel_id=1, source_target_pairs={{0,14},{1,15},{2,12},{3,13},{4,10},{5,11},{6,8},{7,9},{8,6},{9,7},... | collective-permute-start | bytes 786440 | tf_op jit(solution)/shard_map/ppermute | solution.py:186
  47.0 5.1 %collective-permute-done.3 = bf16[2,256,256]{2,1,0:T(8,128)(2,1)S(1)} collective-permute-done((bf16[2,256,256]{2,1,0:T(8,128)(2,1)}, bf16[2,256,256]{2,1,0:T(8,128)(2,1)S(1)}, u32[]{:S(2)}, u32[]{:S(2)}) %collective-permute-start.3) | collective-permute-done | bytes 262176 | tf_op jit(solution)/shard_map/ppermute | solution.py:186
  52.1 6.2 %collective-permute-done.4 = bf16[2,256,256]{2,1,0:T(8,128)(2,1)S(1)} collective-permute-done((bf16[2,256,256]{2,1,0:T(8,128)(2,1)S(1)}, bf16[2,256,256]{2,1,0:T(8,128)(2,1)S(1)}, u32[]{:S(2)}, u32[]{:S(2)}) %collective-permute-start.4) | collective-permute-done | bytes 262176 | tf_op jit(solution)/shard_map/ppermute | solution.py:186
  58.4 7.7 %collective-permute-done.5 = bf16[2,256,256]{2,1,0:T(8,128)(2,1)S(1)} collective-permute-done((bf16[2,256,256]{2,1,0:T(8,128)(2,1)S(1)}, bf16[2,256,256]{2,1,0:T(8,128)(2,1)S(1)}, u32[]{:S(2)}, u32[]{:S(2)}) %collective-permute-start.5) | collective-permute-done | bytes 262176 | tf_op jit(solution)/shard_map/ppermute | solution.py:186
  66.0 6.2 %collective-permute-done.6 = bf16[2,256,256]{2,1,0:T(8,128)(2,1)S(1)} collective-permute-done((bf16[2,256,256]{2,1,0:T(8,128)(2,1)S(1)}, bf16[2,256,256]{2,1,0:T(8,128)(2,1)S(1)}, u32[]{:S(2)}, u32[]{:S(2)}) %collective-permute-start.6) | collective-permute-done | bytes 262176 | tf_op jit(solution)/shard_map/ppermute | solution.py:186
  72.2 6.0 %collective-permute-done.7 = bf16[2,256,256]{2,1,0:T(8,128)(2,1)S(1)} collective-permute-done((bf16[2,256,256]{2,1,0:T(8,128)(2,1)S(1)}, bf16[2,256,256]{2,1,0:T(8,128)(2,1)S(1)}, u32[]{:S(2)}, u32[]{:S(2)}) %collective-permute-start.7) | collective-permute-done | bytes 262176 | tf_op jit(solution)/shard_map/ppermute | solution.py:186
  78.2 0.2 select_select_fusion
  78.3 3.5 %collective-permute-start.8 = (bf16[2,256,256]{2,1,0:T(8,128)(2,1)S(1)}, bf16[2,256,256]{2,1,0:T(8,128)(2,1)S(1)}, u32[]{:S(2)}, u32[]{:S(2)}) collective-permute-start(bf16[2,256,256]{2,1,0:T(8,128)(2,1)S(1)} %select_select_fusion), channel_id=1, source_target_pairs={{0,16},{1,17},{2,18},{3,19},{4,20},{5,21},{6,22},{7,23},{8,24},{9,... | collective-permute-start | bytes 786440 | tf_op jit(solution)/shard_map/ppermute | solution.py:208
  81.8 11.7 %collective-permute-done.8 = bf16[2,256,256]{2,1,0:T(8,128)(2,1)S(1)} collective-permute-done((bf16[2,256,256]{2,1,0:T(8,128)(2,1)S(1)}, bf16[2,256,256]{2,1,0:T(8,128)(2,1)S(1)}, u32[]{:S(2)}, u32[]{:S(2)}) %collective-permute-start.8) | collective-permute-done | bytes 262176 | tf_op jit(solution)/shard_map/ppermute | solution.py:208
  93.6 0.1 broadcast_select_fusion.refs_0_
  93.7 0.5 collective-permute-start.9
  94.2 0.7 collective-permute-start.15
  94.9 6.1 %collective-permute-done.9.refs_2_ = bf16[2,256,256]{2,1,0:T(8,128)(2,1)S(1)} collective-permute-done((bf16[2,256,256]{2,1,0:T(8,128)(2,1)S(1)}, bf16[2,256,256]{2,1,0:T(8,128)(2,1)S(1)}, u32[]{:S(2)}, u32[]{:S(2)}) %collective-permute-start.9) | collective-permute-done | bytes 262176 | tf_op jit(solution)/shard_map/ppermute | solution.py:186
  101.0 0.1 collective-permute-done.15.refs_4_
  101.7 0.7 dynamic_slice.4.which_ref
  102.4 0.4 collective-permute-start.22
  102.8 0.4 collective-permute-start.10
  103.2 1.5 %collective-permute-start.13 = (bf16[2,256,256]{2,1,0:T(8,128)(2,1)S(1)}, bf16[2,256,256]{2,1,0:T(8,128)(2,1)S(1)}, u32[]{:S(2)}, u32[]{:S(2)}) collective-permute-start(bf16[2,256,256]{2,1,0:T(8,128)(2,1)S(1)} %collective-permute-done.12.refs_6_), channel_id=1, source_target_pairs={{0,2},{1,3},{2,0},{3,1},{4,6},{5,7},{6,4},{7,5},{8,10},{9,11},{10,... | collective-permute-start | bytes 786440 | tf_op jit(solution)/shard_map/ppermute | solution.py:186
  104.7 5.1 %collective-permute-done.16.refs_4_ = bf16[2,256,256]{2,1,0:T(8,128)(2,1)S(1)} collective-permute-done((bf16[2,256,256]{2,1,0:T(8,128)(2,1)S(1)}, bf16[2,256,256]{2,1,0:T(8,128)(2,1)S(1)}, u32[]{:S(2)}, u32[]{:S(2)}) %collective-permute-start.16) | collective-permute-done | bytes 262176 | tf_op jit(solution)/shard_map/ppermute | solution.py:186
  109.7 0.3 collective-permute-start.18
  110.1 16.8 %moved_keys.1 = (f32[8,256,128]{2,1,0:T(8,128)S(1)}, f32[8,256,256]{2,1,0:T(8,128)S(1)}) custom-call(s32[1]{0:T(128)S(6)} %copy.12.len_ref, bf16[256,1024]{1,0:T(8,128)(2,1)S(1)} %copy-done.7, bf16[256,256]{1,0:T(8,128)(2,1)S(1)} %copy-done.10, bf16[512,256]{1,0:T(8,128)(2,1)S(1)} %copy-done.8, bf16[32,128,256]{2,1,0:T(8,128)(2,1)} %all-to-all-done.kv_ref), custom_call_target="tpu_custom_call" | custom-call | flops 7650410496 | bytes 2490368 | tf_op jit(solution)/shard_map/moved_keys/pallas_call | solution.py:282
  126.9 0.1 collective-permute-start.17
  126.9 0.5 collective-permute-start.11
  127.4 0.1 collective-permute-start.14
  127.5 0.4 collective-permute-start.19
  128.0 8.3 %prefix_keys.2 = (f32[8,256,128]{2,1,0:T(8,128)S(1)}, f32[8,256,256]{2,1,0:T(8,128)S(1)}) custom-call(s32[1]{0:T(128)} %dynamic_slice.4.which_ref, bf16[256,1024]{1,0:T(8,128)(2,1)S(1)} %copy-done.7, bf16[2,256,256]{2,1,0:T(8,128)(2,1)S(1)} %broadcast_select_fusion.refs_0_, bf16[2,256,256]{2,1,0:T(8,128)(2,1)S(1)} %collective-permute-done.20.refs_1_, ...), custom_call_target="tpu_custom_call" | custom-call | flops 3221225472 | bytes 1048576 | tf_op jit(solution)/shard_map/prefix_keys/pallas_call | solution.py:303
  136.3 9.1 %prefix_keys.3 = bf16[256,1024]{1,0:T(8,128)(2,1)} custom-call(s32[1]{0:T(128)} %dynamic_slice.4.which_ref, bf16[256,1024]{1,0:T(8,128)(2,1)S(1)} %copy-done.7, bf16[2,256,256]{2,1,0:T(8,128)(2,1)S(1)} %collective-permute-done.10.refs_0_, bf16[2,256,256]{2,1,0:T(8,128)(2,1)S(1)} %collective-permute-done.11.refs_1_, ...), custom_call_target="tpu_custom_call" | custom-call | flops 3221225472 | bytes 1048576 | tf_op jit(solution)/shard_map/prefix_keys/pallas_call | solution.py:303
  (37 shorter events, 0.1 us)
Async XLA Ops:
  0.0 9.9 %collective-permute-start = (bf16[4096,256]{1,0:T(8,128)(2,1)}, bf16[4096,256]{1,0:T(8,128)(2,1)S(1)}, u32[]{:S(2)}, u32[]{:S(2)}) collective-permute-start(bf16[4096,256]{1,0:T(8,128)(2,1)} %param.15), channel_id=1, source_target_pairs={{0,1},{1,0},{2,3},{3,2},{4,5},{5,4},{6,7},{7,6},{8,9},{9,8},{10,11... | collective-permute-start | bytes 6291464 | tf_op jit(solution)/shard_map/ppermute | solution.py:183
  1.1 1.6 %copy-start = (bf16[32,128,256]{2,1,0:T(8,128)(2,1)S(1)}, bf16[32,128,256]{2,1,0:T(8,128)(2,1)}, u32[]{:S(2)}) copy-start(bf16[32,128,256]{2,1,0:T(8,128)(2,1)} %pool_ref.1) | copy-start | bytes 6291460
  2.7 0.7 copy-start.5
  3.4 0.7 copy-start.6
  9.8 7.7 %copy-start.1 = (bf16[4096,256]{1,0:T(8,128)(2,1)S(1)}, bf16[4096,256]{1,0:T(8,128)(2,1)}, u32[]{:S(2)}) copy-start(bf16[4096,256]{1,0:T(8,128)(2,1)} %param.15) | copy-start | bytes 6291460
  9.9 7.7 %copy-start.4 = (s32[2]{0:T(128)S(1)}, s32[2]{0:T(128)}, u32[]{:S(2)}) copy-start(s32[2]{0:T(128)} %owner_ref.1) | copy-start | bytes 28
  9.9 1.4 copy-start.2
  11.3 98.8 %all-to-all-start = ((bf16[32,128,256]{2,1,0:T(8,128)(2,1)}), bf16[32,128,256]{2,1,0:T(8,128)(2,1)}, u32[]{:S(2)}, u32[]{:S(2)}) async-start(bf16[32,128,256]{2,1,0:T(8,128)(2,1)} %pack_moved.1), calls=%async_computation | async-start | bytes 4194304 | tf_op jit(solution)/shard_map/all_to_all | solution.py:278
  17.6 1.6 %copy-start.3 = (bf16[4096,256]{1,0:T(8,128)(2,1)S(1)}, bf16[4096,256]{1,0:T(8,128)(2,1)}, u32[]{:S(2)}) copy-start(bf16[4096,256]{1,0:T(8,128)(2,1)} %copy-done.2) | copy-start | bytes 6291460
  23.6 0.7 copy-start.9
  24.4 77.4 %copy-start.11 = (s32[32]{0:T(128)S(1)}, s32[32]{0:T(128)}, u32[]{:S(2)}) copy-start(s32[32]{0:T(128)} %param.17) | copy-start | bytes 388
  24.4 85.7 %copy-start.7 = (bf16[256,1024]{1,0:T(8,128)(2,1)S(1)}, bf16[256,1024]{1,0:T(8,128)(2,1)}, u32[]{:S(2)}) copy-start(bf16[256,1024]{1,0:T(8,128)(2,1)} %q_ref.5) | copy-start | bytes 1572868
  24.4 85.7 %copy-start.8 = (bf16[512,256]{1,0:T(8,128)(2,1)S(1)}, bf16[512,256]{1,0:T(8,128)(2,1)}, u32[]{:S(2)}) copy-start(bf16[512,256]{1,0:T(8,128)(2,1)} %own_ref.1) | copy-start | bytes 786436
  24.4 85.7 %copy-start.10 = (bf16[256,256]{1,0:T(8,128)(2,1)S(1)}, bf16[256,256]{1,0:T(8,128)(2,1)}, u32[]{:S(2)}) copy-start(bf16[256,256]{1,0:T(8,128)(2,1)} %suffix_ref.1) | copy-start | bytes 393220
  24.4 15.2 %collective-permute-start.1 = (bf16[2,256,256]{2,1,0:T(8,128)(2,1)}, bf16[2,256,256]{2,1,0:T(8,128)(2,1)S(1)}, u32[]{:S(2)}, u32[]{:S(2)}) collective-permute-start(bf16[2,256,256]{2,1,0:T(8,128)(2,1)} %get-tuple-element.20), channel_id=1, source_target_pairs={{0,2},{1,3},{2,0},{3,1},{4,6},{5,7},{6,4},{7,5},{8,10},{9,11},{10,... | collective-permute-start | bytes 786440 | tf_op jit(solution)/shard_map/ppermute | solution.py:186
  26.1 18.3 %collective-permute-start.2 = (bf16[2,256,256]{2,1,0:T(8,128)(2,1)}, bf16[2,256,256]{2,1,0:T(8,128)(2,1)S(1)}, u32[]{:S(2)}, u32[]{:S(2)}) collective-permute-start(bf16[2,256,256]{2,1,0:T(8,128)(2,1)} %get-tuple-element.21), channel_id=1, source_target_pairs={{0,4},{1,5},{2,6},{3,7},{4,0},{5,1},{6,2},{7,3},{8,12},{9,13},{10,... | collective-permute-start | bytes 786440 | tf_op jit(solution)/shard_map/ppermute | solution.py:186
  27.6 24.5 %collective-permute-start.3 = (bf16[2,256,256]{2,1,0:T(8,128)(2,1)}, bf16[2,256,256]{2,1,0:T(8,128)(2,1)S(1)}, u32[]{:S(2)}, u32[]{:S(2)}) collective-permute-start(bf16[2,256,256]{2,1,0:T(8,128)(2,1)} %copy-done.9), channel_id=1, source_target_pairs={{0,6},{1,7},{2,4},{3,5},{4,2},{5,3},{6,0},{7,1},{8,14},{9,15},{10,... | collective-permute-start | bytes 786440 | tf_op jit(solution)/shard_map/ppermute | solution.py:186
  27.9 30.4 %collective-permute-start.4 = (bf16[2,256,256]{2,1,0:T(8,128)(2,1)S(1)}, bf16[2,256,256]{2,1,0:T(8,128)(2,1)S(1)}, u32[]{:S(2)}, u32[]{:S(2)}) collective-permute-start(bf16[2,256,256]{2,1,0:T(8,128)(2,1)S(1)} %get-tuple-element.23), channel_id=1, source_target_pairs={{0,8},{1,9},{2,10},{3,11},{4,12},{5,13},{6,14},{7,15},{8,0},{9,1},... | collective-permute-start | bytes 786440 | tf_op jit(solution)/shard_map/ppermute | solution.py:186
  29.6 36.4 %collective-permute-start.5 = (bf16[2,256,256]{2,1,0:T(8,128)(2,1)S(1)}, bf16[2,256,256]{2,1,0:T(8,128)(2,1)S(1)}, u32[]{:S(2)}, u32[]{:S(2)}) collective-permute-start(bf16[2,256,256]{2,1,0:T(8,128)(2,1)S(1)} %get-tuple-element.24), channel_id=1, source_target_pairs={{0,10},{1,11},{2,8},{3,9},{4,14},{5,15},{6,12},{7,13},{8,2},{9,3},... | collective-permute-start | bytes 786440 | tf_op jit(solution)/shard_map/ppermute | solution.py:186
  39.6 32.6 %collective-permute-start.6 = (bf16[2,256,256]{2,1,0:T(8,128)(2,1)S(1)}, bf16[2,256,256]{2,1,0:T(8,128)(2,1)S(1)}, u32[]{:S(2)}, u32[]{:S(2)}) collective-permute-start(bf16[2,256,256]{2,1,0:T(8,128)(2,1)S(1)} %get-tuple-element.25), channel_id=1, source_target_pairs={{0,12},{1,13},{2,14},{3,15},{4,8},{5,9},{6,10},{7,11},{8,4},{9,5},... | collective-permute-start | bytes 786440 | tf_op jit(solution)/shard_map/ppermute | solution.py:186
  44.5 33.7 %collective-permute-start.7 = (bf16[2,256,256]{2,1,0:T(8,128)(2,1)S(1)}, bf16[2,256,256]{2,1,0:T(8,128)(2,1)S(1)}, u32[]{:S(2)}, u32[]{:S(2)}) collective-permute-start(bf16[2,256,256]{2,1,0:T(8,128)(2,1)S(1)} %get-tuple-element.26), channel_id=1, source_target_pairs={{0,14},{1,15},{2,12},{3,13},{4,10},{5,11},{6,8},{7,9},{8,6},{9,7},... | collective-permute-start | bytes 786440 | tf_op jit(solution)/shard_map/ppermute | solution.py:186
  78.3 15.2 %collective-permute-start.8 = (bf16[2,256,256]{2,1,0:T(8,128)(2,1)S(1)}, bf16[2,256,256]{2,1,0:T(8,128)(2,1)S(1)}, u32[]{:S(2)}, u32[]{:S(2)}) collective-permute-start(bf16[2,256,256]{2,1,0:T(8,128)(2,1)S(1)} %select_select_fusion), channel_id=1, source_target_pairs={{0,16},{1,17},{2,18},{3,19},{4,20},{5,21},{6,22},{7,23},{8,24},{9,... | collective-permute-start | bytes 786440 | tf_op jit(solution)/shard_map/ppermute | solution.py:208
  93.7 7.3 %collective-permute-start.9 = (bf16[2,256,256]{2,1,0:T(8,128)(2,1)S(1)}, bf16[2,256,256]{2,1,0:T(8,128)(2,1)S(1)}, u32[]{:S(2)}, u32[]{:S(2)}) collective-permute-start(bf16[2,256,256]{2,1,0:T(8,128)(2,1)S(1)} %broadcast_select_fusion.refs_0_), channel_id=1, source_target_pairs={{0,2},{1,3},{2,0},{3,1},{4,6},{5,7},{6,4},{7,5},{8,10},{9,11},{10,... | collective-permute-start | bytes 786440 | tf_op jit(solution)/shard_map/ppermute | solution.py:186
  94.2 6.9 %collective-permute-start.15 = (bf16[2,256,256]{2,1,0:T(8,128)(2,1)S(1)}, bf16[2,256,256]{2,1,0:T(8,128)(2,1)S(1)}, u32[]{:S(2)}, u32[]{:S(2)}) collective-permute-start(bf16[2,256,256]{2,1,0:T(8,128)(2,1)S(1)} %broadcast_select_fusion.refs_0_), channel_id=1, source_target_pairs={{0,4},{1,5},{2,6},{3,7},{4,0},{5,1},{6,2},{7,3},{8,12},{9,13},{10,... | collective-permute-start | bytes 786440 | tf_op jit(solution)/shard_map/ppermute | solution.py:186
  94.8 8.0 %collective-permute-start.12 = (bf16[2,256,256]{2,1,0:T(8,128)(2,1)S(1)}, bf16[2,256,256]{2,1,0:T(8,128)(2,1)S(1)}, u32[]{:S(2)}, u32[]{:S(2)}) collective-permute-start(bf16[2,256,256]{2,1,0:T(8,128)(2,1)S(1)} %broadcast_select_fusion.refs_0_), channel_id=1, source_target_pairs={{0,8},{1,9},{2,10},{3,11},{4,12},{5,13},{6,14},{7,15},{8,0},{9,1},... | collective-permute-start | bytes 786440 | tf_op jit(solution)/shard_map/ppermute | solution.py:186
  94.8 8.3 %collective-permute-start.20 = (bf16[2,256,256]{2,1,0:T(8,128)(2,1)S(1)}, bf16[2,256,256]{2,1,0:T(8,128)(2,1)S(1)}, u32[]{:S(2)}, u32[]{:S(2)}) collective-permute-start(bf16[2,256,256]{2,1,0:T(8,128)(2,1)S(1)} %broadcast_select_fusion.refs_0_), channel_id=1, source_target_pairs={{0,1},{1,0},{2,3},{3,2},{4,5},{5,4},{6,7},{7,6},{8,9},{9,8},{10,11... | collective-permute-start | bytes 786440 | tf_op jit(solution)/shard_map/ppermute | solution.py:183
  101.0 2.2 %collective-permute-start.21 = (bf16[2,256,256]{2,1,0:T(8,128)(2,1)S(1)}, bf16[2,256,256]{2,1,0:T(8,128)(2,1)S(1)}, u32[]{:S(2)}, u32[]{:S(2)}) collective-permute-start(bf16[2,256,256]{2,1,0:T(8,128)(2,1)S(1)} %collective-permute-done.9.refs_2_), channel_id=1, source_target_pairs={{0,1},{1,0},{2,3},{3,2},{4,5},{5,4},{6,7},{7,6},{8,9},{9,8},{10,11... | collective-permute-start | bytes 786440 | tf_op jit(solution)/shard_map/ppermute | solution.py:183
  101.1 8.6 %collective-permute-start.16 = (bf16[2,256,256]{2,1,0:T(8,128)(2,1)S(1)}, bf16[2,256,256]{2,1,0:T(8,128)(2,1)S(1)}, u32[]{:S(2)}, u32[]{:S(2)}) collective-permute-start(bf16[2,256,256]{2,1,0:T(8,128)(2,1)S(1)} %collective-permute-done.15.refs_4_), channel_id=1, source_target_pairs={{0,8},{1,9},{2,10},{3,11},{4,12},{5,13},{6,14},{7,15},{8,0},{9,1},... | collective-permute-start | bytes 786440 | tf_op jit(solution)/shard_map/ppermute | solution.py:186
  102.4 24.5 %collective-permute-start.22 = (bf16[2,256,256]{2,1,0:T(8,128)(2,1)S(1)}, bf16[2,256,256]{2,1,0:T(8,128)(2,1)S(1)}, u32[]{:S(2)}, u32[]{:S(2)}) collective-permute-start(bf16[2,256,256]{2,1,0:T(8,128)(2,1)S(1)} %collective-permute-done.15.refs_4_), channel_id=1, source_target_pairs={{0,1},{1,0},{2,3},{3,2},{4,5},{5,4},{6,7},{7,6},{8,9},{9,8},{10,11... | collective-permute-start | bytes 786440 | tf_op jit(solution)/shard_map/ppermute | solution.py:183
  102.8 24.1 %collective-permute-start.10 = (bf16[2,256,256]{2,1,0:T(8,128)(2,1)S(1)}, bf16[2,256,256]{2,1,0:T(8,128)(2,1)S(1)}, u32[]{:S(2)}, u32[]{:S(2)}) collective-permute-start(bf16[2,256,256]{2,1,0:T(8,128)(2,1)S(1)} %collective-permute-done.9.refs_2_), channel_id=1, source_target_pairs={{0,4},{1,5},{2,6},{3,7},{4,0},{5,1},{6,2},{7,3},{8,12},{9,13},{10,... | collective-permute-start | bytes 786440 | tf_op jit(solution)/shard_map/ppermute | solution.py:186
  103.2 24.8 %collective-permute-start.23 = (bf16[2,256,256]{2,1,0:T(8,128)(2,1)S(1)}, bf16[2,256,256]{2,1,0:T(8,128)(2,1)}, u32[]{:S(2)}, u32[]{:S(2)}) collective-permute-start(bf16[2,256,256]{2,1,0:T(8,128)(2,1)S(1)} %collective-permute-done.12.refs_6_), channel_id=1, source_target_pairs={{0,1},{1,0},{2,3},{3,2},{4,5},{5,4},{6,7},{7,6},{8,9},{9,8},{10,11... | collective-permute-start | bytes 786440 | tf_op jit(solution)/shard_map/ppermute | solution.py:183
  103.2 24.2 %collective-permute-start.13 = (bf16[2,256,256]{2,1,0:T(8,128)(2,1)S(1)}, bf16[2,256,256]{2,1,0:T(8,128)(2,1)S(1)}, u32[]{:S(2)}, u32[]{:S(2)}) collective-permute-start(bf16[2,256,256]{2,1,0:T(8,128)(2,1)S(1)} %collective-permute-done.12.refs_6_), channel_id=1, source_target_pairs={{0,2},{1,3},{2,0},{3,1},{4,6},{5,7},{6,4},{7,5},{8,10},{9,11},{10,... | collective-permute-start | bytes 786440 | tf_op jit(solution)/shard_map/ppermute | solution.py:186
  109.7 17.8 %collective-permute-start.18 = (bf16[2,256,256]{2,1,0:T(8,128)(2,1)S(1)}, bf16[2,256,256]{2,1,0:T(8,128)(2,1)}, u32[]{:S(2)}, u32[]{:S(2)}) collective-permute-start(bf16[2,256,256]{2,1,0:T(8,128)(2,1)S(1)} %collective-permute-done.16.refs_4_), channel_id=1, source_target_pairs={{0,2},{1,3},{2,0},{3,1},{4,6},{5,7},{6,4},{7,5},{8,10},{9,11},{10,... | collective-permute-start | bytes 786440 | tf_op jit(solution)/shard_map/ppermute | solution.py:186
  126.9 9.4 %collective-permute-start.17 = (bf16[2,256,256]{2,1,0:T(8,128)(2,1)S(1)}, bf16[2,256,256]{2,1,0:T(8,128)(2,1)S(1)}, u32[]{:S(2)}, u32[]{:S(2)}) collective-permute-start(bf16[2,256,256]{2,1,0:T(8,128)(2,1)S(1)} %collective-permute-done.16.refs_4_), channel_id=1, source_target_pairs={{0,1},{1,0},{2,3},{3,2},{4,5},{5,4},{6,7},{7,6},{8,9},{9,8},{10,11... | collective-permute-start | bytes 786440 | tf_op jit(solution)/shard_map/ppermute | solution.py:183
  126.9 9.3 %collective-permute-start.11 = (bf16[2,256,256]{2,1,0:T(8,128)(2,1)S(1)}, bf16[2,256,256]{2,1,0:T(8,128)(2,1)S(1)}, u32[]{:S(2)}, u32[]{:S(2)}) collective-permute-start(bf16[2,256,256]{2,1,0:T(8,128)(2,1)S(1)} %collective-permute-done.10.refs_0_), channel_id=1, source_target_pairs={{0,1},{1,0},{2,3},{3,2},{4,5},{5,4},{6,7},{7,6},{8,9},{9,8},{10,11... | collective-permute-start | bytes 786440 | tf_op jit(solution)/shard_map/ppermute | solution.py:183
  127.4 8.9 %collective-permute-start.14 = (bf16[2,256,256]{2,1,0:T(8,128)(2,1)S(1)}, bf16[2,256,256]{2,1,0:T(8,128)(2,1)S(1)}, u32[]{:S(2)}, u32[]{:S(2)}) collective-permute-start(bf16[2,256,256]{2,1,0:T(8,128)(2,1)S(1)} %collective-permute-done.13.refs_2_), channel_id=1, source_target_pairs={{0,1},{1,0},{2,3},{3,2},{4,5},{5,4},{6,7},{7,6},{8,9},{9,8},{10,11... | collective-permute-start | bytes 786440 | tf_op jit(solution)/shard_map/ppermute | solution.py:183
  127.5 8.8 %collective-permute-start.19 = (bf16[2,256,256]{2,1,0:T(8,128)(2,1)}, bf16[2,256,256]{2,1,0:T(8,128)(2,1)S(1)}, u32[]{:S(2)}, u32[]{:S(2)}) collective-permute-start(bf16[2,256,256]{2,1,0:T(8,128)(2,1)} %collective-permute-done.18.refs_6_), channel_id=1, source_target_pairs={{0,1},{1,0},{2,3},{3,2},{4,5},{5,4},{6,7},{7,6},{8,9},{9,8},{10,11... | collective-permute-start | bytes 786440 | tf_op jit(solution)/shard_map/ppermute | solution.py:183

commit v6 on v5

--- a/solution.py
+++ b/solution.py
@@ -13,6 +13,7 @@
 NEG = -1e30
 CHUNK = 1024
 PARAMS = pltpu.CompilerParams(vmem_limit_bytes=40 * 1024 * 1024)
+COPY_PARAMS = pltpu.CompilerParams(vmem_limit_bytes=56 * 1024 * 1024)
 
 
 def fold_keys(q_ref, m_ref, acc_ref, keys, values, factor, mask=None):
@@ -53,49 +54,49 @@
     values_ref[:rows.shape[0], size:] = jnp.where(live, 1.0, zeros).astype(jnp.bfloat16)
 
 
-def fold_moved(factor, q_ref, kv_ref, suffix_ref, m_ref, acc_ref, keys_ref, values_ref):
+def local_kernel(
+    factor, len_ref, q_ref, suffix_ref, own_ref, m_ref, acc_ref, keys_ref, values_ref
+):
+    size = suffix_ref.shape[1] // 2
+    suffix = suffix_ref.shape[0]
+    own = own_ref.shape[0]
+    m_ref[...] = jnp.full(m_ref.shape, NEG, jnp.float32)
+    acc_ref[...] = jnp.zeros(acc_ref.shape, jnp.float32)
+    values_ref[:suffix, :size] = suffix_ref[:, size:]
+    values_ref[:suffix, size:] = jnp.ones((suffix, size), jnp.bfloat16)
+    causal = lax.broadcasted_iota(jnp.int32, (suffix, suffix), 1) <= lax.broadcasted_iota(
+        jnp.int32, (suffix, suffix), 0
+    )
+    fold_keys(
+        q_ref, m_ref, acc_ref, suffix_ref[:, :size], values_ref[:suffix, :], factor, causal
+    )
+    live = lax.broadcasted_iota(jnp.int32, (own, size), 0) < len_ref[0]
+    stage_live(own_ref[...].astype(jnp.float32), live, suffix_ref, keys_ref, values_ref)
+    fold_keys(q_ref, m_ref, acc_ref, keys_ref[:own, :], values_ref[:own, :], factor)
+
+
+def moved_kernel(
+    factor, q_ref, suffix_ref, kv_ref, m_in, acc_in, m_ref, acc_ref, keys_ref, values_ref
+):
+    @pl.when(pl.program_id(0) == 0)
+    def _():
+        m_ref[...] = m_in[...]
+        acc_ref[...] = acc_in[...]
+
     rows = kv_ref[...].reshape(-1, kv_ref.shape[-1]).astype(jnp.float32)
     size = suffix_ref.shape[1] // 2
     live = jnp.broadcast_to(rows[:, size:size + 1] < DEAD_ABOVE, (rows.shape[0], size))
     stage_live(rows, live, suffix_ref, keys_ref, values_ref)
-    fold_keys(
-        q_ref, m_ref, acc_ref, keys_ref[:rows.shape[0], :], values_ref[:rows.shape[0], :], factor
-    )
-
-
-def first_kernel(
-    factor, len_ref, q_ref, suffix_ref, own_ref, kv_ref, m_ref, acc_ref, keys_ref, values_ref
-):
-    size = suffix_ref.shape[1] // 2
-    suffix = suffix_ref.shape[0]
-    own = own_ref.shape[0]
-
-    @pl.when(pl.program_id(0) == 0)
-    def _():
-        m_ref[...] = jnp.full(m_ref.shape, NEG, jnp.float32)
-        acc_ref[...] = jnp.zeros(acc_ref.shape, jnp.float32)
-        values_ref[:suffix, :size] = suffix_ref[:, size:]
-        values_ref[:suffix, size:] = jnp.ones((suffix, size), jnp.bfloat16)
-        causal = lax.broadcasted_iota(jnp.int32, (suffix, suffix), 1) <= lax.broadcasted_iota(
-            jnp.int32, (suffix, suffix), 0
-        )
-        fold_keys(
-            q_ref, m_ref, acc_ref, suffix_ref[:, :size], values_ref[:suffix, :], factor, causal
-        )
-        live = lax.broadcasted_iota(jnp.int32, (own, size), 0) < len_ref[0]
-        stage_live(own_ref[...].astype(jnp.float32), live, suffix_ref, keys_ref, values_ref)
-        fold_keys(q_ref, m_ref, acc_ref, keys_ref[:own, :], values_ref[:own, :], factor)
-
-    fold_moved(factor, q_ref, kv_ref, suffix_ref, m_ref, acc_ref, keys_ref, values_ref)
-
-
-def prefix_kernel(factor, last, count, which_ref, q_ref, *refs):
+    fold_keys(q_ref, m_ref, acc_ref, keys_ref[...], values_ref[...], factor)
+
+
+def prefix_kernel(factor, last, count, steps, which_ref, q_ref, *refs):
     pieces, refs = refs[:count], refs[count:]
     m_in, acc_in, out_ref = refs[:3]
     m_ref, acc_ref, keys_ref, values_ref = refs[-4:]
     size = keys_ref.shape[1]
-    chunk = min(CHUNK, keys_ref.shape[0])
     step = pl.program_id(0)
+    chunk = keys_ref.shape[0] // steps
 
     @pl.when(step == 0)
     def _():
@@ -111,7 +112,7 @@
     fold_keys(q_ref, m_ref, acc_ref, keys_ref[rows, :], values_ref[rows, :], factor)
     if last:
 
-        @pl.when(step == pl.num_programs(0) - 1)
+        @pl.when(step == steps - 1)
         def _():
             finish(acc_ref, out_ref)
 
@@ -145,68 +146,100 @@
 
 def stage_kernel(owner_ref, place_ref, kept_ref, swapped_ref, *refs):
     pieces, sems = refs[:-1], refs[-1]
-    core, chip = place_ref[0], place_ref[1]
-    prefixes = owner_ref.shape[0]
-
-    def copies(source, step, prefix):
+    core, chip, is_last = place_ref[0], place_ref[1], place_ref[2]
+    sought = owner_ref.shape[0]
+    chips = len(pieces) // 2
+
+    def copy(source, step, prefix):
+        target = pieces[step].at[prefix] if prefix < sought else pieces[chips + step]
         return pltpu.make_async_copy(
-            source.at[core, chip ^ step], pieces[step].at[prefix], sems.at[step, prefix]
+            source.at[core, chip ^ step], target, sems.at[step, prefix]
         )
 
-    for step in range(len(pieces)):
-        for prefix in range(prefixes):
-            here = owner_ref[prefix] % 2 == core
-
-            @pl.when(here)
-            def _():
-                copies(kept_ref, step, prefix).start()
-
-            @pl.when(jnp.logical_not(here))
-            def _():
-                copies(swapped_ref, step, prefix).start()
-
-    for step in range(len(pieces)):
-        for prefix in range(prefixes):
-            copies(kept_ref, step, prefix).wait()
-
-
-def multicast(prefix_cache, owners, outgoing):
+    def each(do):
+        for step in range(chips):
+            for prefix in range(sought):
+                do(step, prefix, owner_ref[prefix] % 2 == core)
+
+        @pl.when(is_last == 1)
+        def _():
+            for step in range(chips):
+                do(step, sought, core == 1)
+
+    def start(step, prefix, here):
+        @pl.when(here)
+        def _():
+            copy(kept_ref, step, prefix).start()
+
+        @pl.when(jnp.logical_not(here))
+        def _():
+            copy(swapped_ref, step, prefix).start()
+
+    each(start)
+    each(lambda step, prefix, here: copy(kept_ref, step, prefix).wait())
+
+
+def multicast(prefix_cache, owners, readers, outgoing):
     replicas = lax.axis_size("replica")
     me = lax.axis_index("replica")
     half = replicas // 2
     chips = half // 2
     bits = chips.bit_length() - 1
     chip = me // 2 % chips
+    side = me // half
     width = prefix_cache.shape[1]
+    ids = jnp.arange(owners.shape[0], dtype=jnp.int32)
+    known = jnp.sum(jnp.where(owners == replicas - 1, ids, 0))
+    sought = jnp.where(ids[:-1] >= known, owners[1:], owners[:-1])
 
     def swap_cores(rows):
         return lax.ppermute(rows, "replica", [(i, i ^ 1) for i in range(replicas)])
 
     def to_peer(rows, step):
         return lax.ppermute(rows, "replica", [(i, i ^ (2 * step)) for i in range(replicas)])
+
+    def from_last(rows, step):
+        pair = (replicas - 2, replicas - 1)
+        return lax.ppermute(rows, "replica", [(i, i ^ (2 * step)) for i in pair])
 
     split = prefix_cache.reshape(2, chips, -1, width)
     swapped, outgoing = lax.optimization_barrier((swap_cores(prefix_cache), outgoing))
     swapped = swapped.reshape(split.shape)
-    piece = jax.ShapeDtypeStruct((owners.shape[0], split.shape[2], width), split.dtype)
+    piece = jax.ShapeDtypeStruct(split.shape[2:], split.dtype)
+    pieces = jax.ShapeDtypeStruct((owners.shape[0] - 1, *piece.shape), split.dtype)
     anywhere = pl.BlockSpec(memory_space=pl.ANY)
     staged = pl.pallas_call(
         stage_kernel,
-        out_shape=(piece,) * chips,
+        out_shape=(pieces,) * chips + (piece,) * chips,
         in_specs=[pl.BlockSpec(memory_space=pltpu.SMEM)] * 2 + [anywhere] * 2,
-        out_specs=(whole(piece.shape),) * chips,
+        out_specs=(whole(pieces.shape),) * chips + (whole(piece.shape),) * chips,
         grid=(1,),
         scratch_shapes=[pltpu.SemaphoreType.DMA((chips, owners.shape[0]))],
-        compiler_params=PARAMS,
+        compiler_params=COPY_PARAMS,
         name="stage_prefix",
-    )(owners, jnp.stack([me % 2, chip]), split, swapped)
-    away = chip ^ (owners // 2 % chips)
+    )(
+        sought,
+        jnp.stack([me % 2, chip, (me // 2 == replicas // 2 - 1).astype(jnp.int32)]),
+        split,
+        swapped,
+    )
+    staged, staged_known = staged[:chips], staged[chips:]
+
+    away = chip ^ (chips - 1)
+    found = staged_known[0]
+    for step in range(1, chips):
+        found = jnp.where(away == step, from_last(staged_known[step], step), found)
+    passed = lax.ppermute(found, "replica", [(i + half, i) for i in range(half)])
+    held_known = jnp.where(side == 1, found, passed)
+
+    away = chip ^ (sought // 2 % chips)
     found = staged[0]
     for step in range(chips - 1, 0, -1):
         rows = to_peer(staged[step], step)
         found = jnp.where((away == step)[:, None, None], rows, found)
     passed = lax.ppermute(found, "replica", [(i, (i + half) % replicas) for i in range(replicas)])
-    held = jnp.where((owners // half == me // half)[:, None, None], found, passed)
+    held = jnp.where((sought // half == side)[:, None, None], found, passed)
+    held = jnp.concatenate([held_known[None], held])
 
     gathered = {0: held}
     for step in sorted(range(1, chips), key=lambda step: (step.bit_count(), step)):
@@ -217,7 +250,9 @@
     parts = [[], []]
     for step, rows in gathered.items():
         parts[step.bit_count() > 1].extend((rows, swap_cores(rows)))
-    return parts, outgoing
+    wanted = readers[me]
+    place = jnp.where(wanted == known, 0, wanted + (wanted < known))
+    return parts, place[None], outgoing
 
 
 def whole(shape):
@@ -243,7 +278,6 @@
     mig_block,
     mig_count,
 ):
-    me = lax.axis_index("replica")
     replicas = lax.axis_size("replica")
     size = suffix_kv.shape[1] // 2
     tokens = queries.shape[0]
@@ -271,41 +305,62 @@
         out_specs=whole((replicas, *kv_pool.shape[1:])),
         grid=(1,),
         scratch_shapes=[pltpu.SemaphoreType.DMA((mig_target.shape[1],))],
-        compiler_params=PARAMS,
+        compiler_params=COPY_PARAMS,
         name="pack_moved",
     )(mig_target, mig_block, mig_count, kv_pool)
-    shared, outgoing = multicast(prefix_cache, owners, outgoing)
+    shared, place, outgoing = multicast(prefix_cache, owners, readers, outgoing)
     arrived = lax.all_to_all(outgoing, "replica", split_axis=0, concat_axis=0, tiled=True)
 
-    rows = arrived.shape[1]
-    group = max(1, CHUNK // rows)
     state_now = pl.pallas_call(
-        functools.partial(first_kernel, factor),
+        functools.partial(local_kernel, factor),
         out_shape=state,
-        grid=(replicas // group,),
+        grid=(1,),
         in_specs=[
             in_smem,
             whole(queries.shape),
             whole(suffix_kv.shape),
             whole(own_cache.shape),
-            pl.BlockSpec((group, rows, 2 * size), lambda i: (i, 0, 0)),
         ],
         out_specs=state_specs,
-        scratch_shapes=scratch(max(group * rows, own_cache.shape[0], tokens)),
+        scratch_shapes=scratch(max(own_cache.shape[0], tokens)),
         compiler_params=PARAMS,
-        cost_estimate=cost(row_count, tokens + own_cache.shape[0] + replicas * rows, size),
-        name="moved_keys",
-    )(ctx_len, queries, suffix_kv, own_cache, arrived)
+        cost_estimate=cost(row_count, tokens + own_cache.shape[0], size),
+        name="local_keys",
+    )(ctx_len, queries, suffix_kv, own_cache)
+
+    rows = arrived.shape[1]
+    group = max(1, CHUNK // rows)
+    steps = replicas // group
+    for begin, end in ((0, steps // 2), (steps // 2, steps)):
+        state_now = pl.pallas_call(
+            functools.partial(moved_kernel, factor),
+            out_shape=state,
+            grid=(end - begin,),
+            in_specs=[
+                whole(queries.shape),
+                whole(suffix_kv.shape),
+                pl.BlockSpec((group, rows, 2 * size), lambda i, begin=begin: (i + begin, 0, 0)),
+                *state_specs,
+            ],
+            out_specs=state_specs,
+            scratch_shapes=scratch(group * rows),
+            compiler_params=PARAMS,
+            cost_estimate=cost(row_count, (end - begin) * group * rows, size),
+            name="moved_keys",
+        )(queries, suffix_kv, arrived, *state_now)
 
     for last, pieces in enumerate(shared):
         rows = pieces[0].shape[1]
         keys = len(pieces) * rows
+        steps = max(1, keys // CHUNK)
+        while keys % (steps * size):
+            steps -= 1
         state_now = pl.pallas_call(
-            functools.partial(prefix_kernel, factor, last, len(pieces)),
+            functools.partial(prefix_kernel, factor, last, len(pieces), steps),
             out_shape=jax.ShapeDtypeStruct(queries.shape, queries.dtype) if last else state,
             grid_spec=pltpu.PrefetchScalarGridSpec(
                 num_scalar_prefetch=1,
-                grid=(max(1, keys // CHUNK),),
+                grid=(steps,),
                 in_specs=[
                     whole(queries.shape),
                     *[pl.BlockSpec((None, rows, 2 * size), lambda i, which: (which[0], 0, 0))]
@@ -319,7 +374,7 @@
             compiler_params=PARAMS,
             cost_estimate=cost(row_count, keys, size),
             name="prefix_keys",
-        )(readers[me][None], queries, *pieces, *state_now)
+        )(place, queries, *pieces, *state_now)
     return state_now
 
 

time: 146 us -> 142 us (0.973)
  waiting for transfers between devices: 63.6 us -> 32.5 us
  starting transfers between devices: 28.2 us -> 53.9 us
  Pallas kernels: 44.5 us -> 37.5 us
  between operations: 1.56 us -> 6.74 us
  other arithmetic: 0.35 us -> 3.25 us
    ppermute x14, waiting for transfers between devices: 51.8 us -> 27.6 us  [to_peer(): lax.ppermute(rows, 'replica', [(i, i ^ 2 * step) for i in range(replicas)])]
    ppermute x1, starting transfers between devices: 3.48 us -> 20.4 us  [multicast(): lax.ppermute(found, 'replica', [(i, (i + half) % replicas) for i in range...]
    ppermute x0 -> x8, starting transfers between devices: none -> 8.66 us  [the longest x7 7.38 us: from_last(): return lax.ppermute(rows, 'replica', [(i, i ^ 2 * step) for i in pair])]
    ppermute x1, waiting for transfers between devices: 11.7 us -> 4.78 us  [multicast(): lax.ppermute(found, 'replica', [(i, (i + half) % replicas) for i in range...]
    pallas_call x2 -> x4, Pallas kernels: 21.2 us -> 18.6 us  [the longest x2 12.7 us: on_device(): pl.pallas_call(functools.partial(moved_kernel, factor), out_shape=state,...]
    pallas_call x2, Pallas kernels: 17.4 us -> 15.1 us  [on_device(): pl.pallas_call(functools.partial(prefix_kernel, factor, last, len(pieces)...]
    pallas_call x1, Pallas kernels: 5.83 us -> 3.83 us  [on_device(): pl.pallas_call(pack_kernel, out_shape=jax.ShapeDtypeStruct((replicas, *kv...]
    unnamed x24 -> x20, local copies, waits for them, and re-layouts: 6.58 us -> 6.51 us
  transfers between devices with their start and end apart: 25 -> 33, of which waited for: 11 -> 8; matrix products, arithmetic and copies ran while one was open for 1% -> 3% of each run, Pallas kernels for 24% -> 21%
where the time goes in v6:
time: 142 us
  starting transfers between devices  53.9 us (38%)
  Pallas kernels  37.5 us (26%)
  waiting for transfers between devices  32.5 us (23%)
  local copies, waits for them, and re-layouts  7.67 us (5%)
  between operations  6.74 us (5%)
  other arithmetic  3.25 us (2%)
    ppermute x14, waiting for transfers between devices, to_peer(): lax.ppermute(rows, 'replica', [(i, i ^ 2 * step) for i in range(replicas)])  27.6 us
    ppermute x1, starting transfers between devices, multicast(): lax.ppermute(found, 'replica', [(i, (i + half) % replicas) for i in range...  20.4 us
    ppermute x14, starting transfers between devices, to_peer(): lax.ppermute(rows, 'replica', [(i, i ^ 2 * step) for i in range(replicas)])  16.2 us
    pallas_call x2, Pallas kernels, on_device(): pl.pallas_call(functools.partial(prefix_kernel, factor, last, len(pieces)...  15.1 us
    pallas_call x2, Pallas kernels, on_device(): pl.pallas_call(functools.partial(moved_kernel, factor), out_shape=state,...  12.7 us
    ppermute x7, starting transfers between devices, from_last(): return lax.ppermute(rows, 'replica', [(i, i ^ 2 * step) for i in pair])  7.38 us
    all_to_all x1, starting transfers between devices, on_device(): lax.all_to_all(outgoing, 'replica', split_axis=0, concat_axis=0, tiled=True)  6.83 us
    unnamed x20, local copies, waits for them, and re-layouts  6.51 us
  transfers between devices with their start and end apart: 33, of which 8 were waited for; matrix products, arithmetic and copies ran while one was open for 3% of the time, Pallas kernels for 21%

profile of v6, /device:TPU:0, one launch (start us, length us, event | category | flops | bytes accessed | tf_op | source)
XLA Modules:
  0.0 141.5 jit_solution(1659564673683123362)
XLA Ops:
  0.0 0.5 collective-permute-start
  1.1 3.8 %pack_moved.1 = bf16[32,128,256]{2,1,0:T(8,128)(2,1)} custom-call(s32[1,32]{1,0:T(1,128)} %target_ref.1, s32[1,32]{1,0:T(1,128)} %block_ref.1, s32[1]{0:T(128)S(6)} %copy.13.count_ref, bf16[32,128,256]{2,1,0:T(8,128)(2,1)} %pool_ref.1), custom_call_target="tpu_custom_call" | custom-call | tf_op jit(solution)/shard_map/pack_moved/pallas_call | solution.py:301
  5.0 1.3 copy-done.7
  6.3 6.8 %all-to-all-start = ((bf16[32,128,256]{2,1,0:T(8,128)(2,1)}), bf16[32,128,256]{2,1,0:T(8,128)(2,1)S(1)}, u32[]{:S(2)}, u32[]{:S(2)}) async-start(bf16[32,128,256]{2,1,0:T(8,128)(2,1)} %pack_moved.1), calls=%async_computation | async-start | bytes 4194304 | tf_op jit(solution)/shard_map/all_to_all | solution.py:312
  13.2 0.6 fusion
  14.5 0.6 fusion.1
  16.3 0.6 pad_add_fusion.place_ref
  16.9 3.4 %stage_prefix.1 = (bf16[1,256,256]{2,1,0:T(8,128)(2,1)}, bf16[1,256,256]{2,1,0:T(8,128)(2,1)}, bf16[1,256,256]{2,1,0:T(8,128)(2,1)}, bf16[1,256,256]{2,1,0:T(8,1...) custom-call(s32[1]{0:T(128)S(6)} %select_n.130.owner_ref, ...), custom_call_target="tpu_custom_call" | custom-call | tf_op jit(solution)/shard_map/stage_prefix/pallas_call | solution.py:211
  20.4 0.8 collective-permute-start.1
  21.2 0.7 collective-permute-start.2
  21.8 0.7 collective-permute-start.3
  22.5 1.3 collective-permute-start.4
  23.8 1.3 collective-permute-start.5
  25.2 1.3 collective-permute-start.6
  26.5 1.3 collective-permute-start.7
  27.8 1.8 %collective-permute-start.10 = (bf16[1,256,256]{2,1,0:T(8,128)(2,1)}, bf16[1,256,256]{2,1,0:T(8,128)(2,1)S(1)}, u32[]{:S(2)}, u32[]{:S(2)}) collective-permute-start(bf16[1,256,256]{2,1,0:T(8,128)(2,1)} %get-tuple-element.41), channel_id=1, source_target_pairs={{0,4},{1,5},{2,6},{3,7},{4,0},{5,1},{6,2},{7,3},{8,12},{9,13},{10,... | collective-permute-start | bytes 393224 | tf_op jit(solution)/shard_map/ppermute | solution.py:199
  29.6 1.5 %collective-permute-start.11 = (bf16[1,256,256]{2,1,0:T(8,128)(2,1)}, bf16[1,256,256]{2,1,0:T(8,128)(2,1)}, u32[]{:S(2)}, u32[]{:S(2)}) collective-permute-start(bf16[1,256,256]{2,1,0:T(8,128)(2,1)} %get-tuple-element.42), channel_id=1, source_target_pairs={{0,6},{1,7},{2,4},{3,5},{4,2},{5,3},{6,0},{7,1},{8,14},{9,15},{10,... | collective-permute-start | bytes 393224 | tf_op jit(solution)/shard_map/ppermute | solution.py:199
  31.0 1.5 %collective-permute-start.12 = (bf16[1,256,256]{2,1,0:T(8,128)(2,1)}, bf16[1,256,256]{2,1,0:T(8,128)(2,1)S(1)}, u32[]{:S(2)}, u32[]{:S(2)}) collective-permute-start(bf16[1,256,256]{2,1,0:T(8,128)(2,1)} %get-tuple-element.43), channel_id=1, source_target_pairs={{0,8},{1,9},{2,10},{3,11},{4,12},{5,13},{6,14},{7,15},{8,0},{9,1},... | collective-permute-start | bytes 393224 | tf_op jit(solution)/shard_map/ppermute | solution.py:199
  32.7 2.7 %collective-permute-start.14 = (bf16[1,256,256]{2,1,0:T(8,128)(2,1)}, bf16[1,256,256]{2,1,0:T(8,128)(2,1)S(1)}, u32[]{:S(2)}, u32[]{:S(2)}) collective-permute-start(bf16[1,256,256]{2,1,0:T(8,128)(2,1)} %get-tuple-element.45), channel_id=1, source_target_pairs={{0,12},{1,13},{2,14},{3,15},{4,8},{5,9},{6,10},{7,11},{8,4},{9,5},... | collective-permute-start | bytes 393224 | tf_op jit(solution)/shard_map/ppermute | solution.py:199
  35.4 6.7 %collective-permute-done.10 = bf16[1,256,256]{2,1,0:T(8,128)(2,1)S(1)} collective-permute-done((bf16[1,256,256]{2,1,0:T(8,128)(2,1)}, bf16[1,256,256]{2,1,0:T(8,128)(2,1)S(1)}, u32[]{:S(2)}, u32[]{:S(2)}) %collective-permute-start.10) | collective-permute-done | bytes 131104 | tf_op jit(solution)/shard_map/ppermute | solution.py:199
  42.2 1.4 %collective-permute-start.15 = (bf16[1,256,256]{2,1,0:T(8,128)(2,1)}, bf16[1,256,256]{2,1,0:T(8,128)(2,1)S(1)}, u32[]{:S(2)}, u32[]{:S(2)}) collective-permute-start(bf16[1,256,256]{2,1,0:T(8,128)(2,1)} %get-tuple-element.46), channel_id=1, source_target_pairs={{0,14},{1,15},{2,12},{3,13},{4,10},{5,11},{6,8},{7,9},{8,6},{9,7},... | collective-permute-start | bytes 393224 | tf_op jit(solution)/shard_map/ppermute | solution.py:199
  43.7 1.0 select_select_fusion.1
  44.6 6.8 %collective-permute-done.12 = bf16[1,256,256]{2,1,0:T(8,128)(2,1)S(1)} collective-permute-done((bf16[1,256,256]{2,1,0:T(8,128)(2,1)}, bf16[1,256,256]{2,1,0:T(8,128)(2,1)S(1)}, u32[]{:S(2)}, u32[]{:S(2)}) %collective-permute-start.12) | collective-permute-done | bytes 131104 | tf_op jit(solution)/shard_map/ppermute | solution.py:199
  51.4 1.3 collective-permute-start.8
  52.7 1.5 %collective-permute-done.13 = bf16[1,256,256]{2,1,0:T(8,128)(2,1)S(1)} collective-permute-done((bf16[1,256,256]{2,1,0:T(8,128)(2,1)}, bf16[1,256,256]{2,1,0:T(8,128)(2,1)S(1)}, u32[]{:S(2)}, u32[]{:S(2)}) %collective-permute-start.13) | collective-permute-done | bytes 131104 | tf_op jit(solution)/shard_map/ppermute | solution.py:199
  54.2 2.8 %collective-permute-done.14 = bf16[1,256,256]{2,1,0:T(8,128)(2,1)S(1)} collective-permute-done((bf16[1,256,256]{2,1,0:T(8,128)(2,1)}, bf16[1,256,256]{2,1,0:T(8,128)(2,1)S(1)}, u32[]{:S(2)}, u32[]{:S(2)}) %collective-permute-start.14) | collective-permute-done | bytes 131104 | tf_op jit(solution)/shard_map/ppermute | solution.py:199
  57.0 4.4 %collective-permute-done.15 = bf16[1,256,256]{2,1,0:T(8,128)(2,1)S(1)} collective-permute-done((bf16[1,256,256]{2,1,0:T(8,128)(2,1)}, bf16[1,256,256]{2,1,0:T(8,128)(2,1)S(1)}, u32[]{:S(2)}, u32[]{:S(2)}) %collective-permute-start.15) | collective-permute-done | bytes 131104 | tf_op jit(solution)/shard_map/ppermute | solution.py:199
  61.5 1.0 select_select_fusion
  62.4 20.4 %collective-permute-start.16 = (bf16[1,256,256]{2,1,0:T(8,128)(2,1)S(1)}, bf16[1,256,256]{2,1,0:T(8,128)(2,1)S(1)}, u32[]{:S(2)}, u32[]{:S(2)}) collective-permute-start(bf16[1,256,256]{2,1,0:T(8,128)(2,1)S(1)} %select_select_fusion), channel_id=1, source_target_pairs={{0,16},{1,17},{2,18},{3,19},{4,20},{5,21},{6,22},{7,23},{8,24},{9,... | collective-permute-start | bytes 393224 | tf_op jit(solution)/shard_map/ppermute | solution.py:240
  82.9 4.8 %collective-permute-done.16 = bf16[1,256,256]{2,1,0:T(8,128)(2,1)S(1)} collective-permute-done((bf16[1,256,256]{2,1,0:T(8,128)(2,1)S(1)}, bf16[1,256,256]{2,1,0:T(8,128)(2,1)S(1)}, u32[]{:S(2)}, u32[]{:S(2)}) %collective-permute-start.16) | collective-permute-done | bytes 131104 | tf_op jit(solution)/shard_map/ppermute | solution.py:240
  87.8 1.7 %collective-permute-start.17 = (bf16[2,256,256]{2,1,0:T(8,128)(2,1)S(1)}, bf16[2,256,256]{2,1,0:T(8,128)(2,1)}, u32[]{:S(2)}, u32[]{:S(2)}) collective-permute-start(bf16[2,256,256]{2,1,0:T(8,128)(2,1)S(1)} %pad_maximum_fusion.refs_0_), channel_id=1, source_target_pairs={{0,2},{1,3},{2,0},{3,1},{4,6},{5,7},{6,4},{7,5},{8,10},{9,11},{10,... | collective-permute-start | bytes 786440 | tf_op jit(solution)/shard_map/ppermute | solution.py:199
  89.5 0.6 dynamic_slice.3
  94.0 2.5 %local_keys.1 = (f32[8,256,128]{2,1,0:T(8,128)S(1)}, f32[8,256,256]{2,1,0:T(8,128)S(1)}) custom-call(s32[1]{0:T(128)S(6)} %copy.12.len_ref, bf16[256,1024]{1,0:T(8,128)(2,1)S(1)} %copy-done, bf16[256,256]{1,0:T(8,128)(2,1)S(1)} %copy-done.2, bf16[512,256]{1,0:T(8,128)(2,1)S(1)} %copy-done.1), custom_call_target="tpu_custom_call" | custom-call | flops 1207959552 | bytes 393216 | tf_op jit(solution)/shard_map/local_keys/pallas_call | solution.py:314
  96.5 1.3 copy-done.3
  97.8 1.0 copy-done.5
  98.8 0.5 collective-permute-start.30
  99.3 2.0 %collective-permute-start.24 = (bf16[2,256,256]{2,1,0:T(8,128)(2,1)S(1)}, bf16[2,256,256]{2,1,0:T(8,128)(2,1)S(1)}, u32[]{:S(2)}, u32[]{:S(2)}) collective-permute-start(bf16[2,256,256]{2,1,0:T(8,128)(2,1)S(1)} %collective-permute-done.23.refs_4_), channel_id=1, source_target_pairs={{0,8},{1,9},{2,10},{3,11},{4,12},{5,13},{6,14},{7,15},{8,0},{9,1},... | collective-permute-start | bytes 786440 | tf_op jit(solution)/shard_map/ppermute | solution.py:199
  101.4 1.6 %copy-done.4 = f32[8,256,256]{2,1,0:T(8,128)S(1)} copy-done((f32[8,256,256]{2,1,0:T(8,128)S(1)}, f32[8,256,256]{2,1,0:T(8,128)}, u32[]{:S(2)}) %copy-start.4) | copy-done | bytes 2097176
  103.0 1.2 copy-done.6
  104.2 6.4 %moved_keys.2 = (f32[8,256,128]{2,1,0:T(8,128)S(1)}, f32[8,256,256]{2,1,0:T(8,128)S(1)}) custom-call(bf16[256,1024]{1,0:T(8,128)(2,1)S(1)} %copy-done, bf16[256,256]{1,0:T(8,128)(2,1)S(1)} %copy-done.2, bf16[32,128,256]{2,1,0:T(8,128)(2,1)S(1)} %all-to-all-done.kv_ref, f32[8,256,128]{2,1,0:T(8,128)S(1)} %copy-done.6, f32[8,256,256]{2,1,0:T(8,128)S(1)} %copy-done.4), custom_call_target="tpu_custom_call" | custom-call | flops 3221225472 | bytes 1048576 | tf_op jit(solution)/shard_map/moved_keys/pallas_call | solution.py:335
  110.6 1.2 collective-permute-start.18
  112.0 1.1 collective-permute-start.21
  113.2 0.9 collective-permute-start.26
  114.1 6.4 %moved_keys.3 = (f32[8,256,128]{2,1,0:T(8,128)S(1)}, f32[8,256,256]{2,1,0:T(8,128)S(1)}) custom-call(bf16[256,1024]{1,0:T(8,128)(2,1)S(1)} %copy-done, bf16[256,256]{1,0:T(8,128)(2,1)S(1)} %copy-done.2, bf16[32,128,256]{2,1,0:T(8,128)(2,1)S(1)} %all-to-all-done.kv_ref, f32[8,256,128]{2,1,0:T(8,128)S(1)} %get-tuple-element.51.m_in, ...), custom_call_target="tpu_custom_call" | custom-call | flops 3221225472 | bytes 1048576 | tf_op jit(solution)/shard_map/moved_keys/pallas_call | solution.py:335
  120.5 0.5 collective-permute-start.19
  121.4 5.0 %collective-permute-done.26.refs_6_ = bf16[2,256,256]{2,1,0:T(8,128)(2,1)S(1)} collective-permute-done((bf16[2,256,256]{2,1,0:T(8,128)(2,1)S(1)}, bf16[2,256,256]{2,1,0:T(8,128)(2,1)S(1)}, u32[]{:S(2)}, u32[]{:S(2)}) %collective-permute-start.26) | collective-permute-done | bytes 262176 | tf_op jit(solution)/shard_map/ppermute | solution.py:199
  126.4 7.6 %prefix_keys.2 = (f32[8,256,128]{2,1,0:T(8,128)S(1)}, f32[8,256,256]{2,1,0:T(8,128)S(1)}) custom-call(s32[1]{0:T(128)} %bitcast.1.which_ref, bf16[256,1024]{1,0:T(8,128)(2,1)S(1)} %copy-done, bf16[2,256,256]{2,1,0:T(8,128)(2,1)S(1)} %pad_maximum_fusion.refs_0_, bf16[2,256,256]{2,1,0:T(8,128)(2,1)} %collective-permute-done.28.refs_1_, ...), custom_call_target="tpu_custom_call" | custom-call | flops 3221225472 | bytes 1048576 | tf_op jit(solution)/shard_map/prefix_keys/pallas_call | solution.py:358
  134.0 7.6 %prefix_keys.3 = bf16[256,1024]{1,0:T(8,128)(2,1)} custom-call(s32[1]{0:T(128)} %bitcast.1.which_ref, bf16[256,1024]{1,0:T(8,128)(2,1)S(1)} %copy-done, bf16[2,256,256]{2,1,0:T(8,128)(2,1)S(1)} %collective-permute-done.18.refs_0_, bf16[2,256,256]{2,1,0:T(8,128)(2,1)S(1)} %collective-permute-done.19.refs_1_, ...), custom_call_target="tpu_custom_call" | custom-call | flops 3221225472 | bytes 1048576 | tf_op jit(solution)/shard_map/prefix_keys/pallas_call | solution.py:358
  (55 shorter events, 1.2 us)
Async XLA Ops:
  0.0 5.0 %collective-permute-start = (bf16[4096,256]{1,0:T(8,128)(2,1)}, bf16[4096,256]{1,0:T(8,128)(2,1)S(1)}, u32[]{:S(2)}, u32[]{:S(2)}) collective-permute-start(bf16[4096,256]{1,0:T(8,128)(2,1)} %param.15), channel_id=1, source_target_pairs={{0,1},{1,0},{2,3},{3,2},{4,5},{5,4},{6,7},{7,6},{8,9},{9,8},{10,11... | collective-permute-start | bytes 6291464 | tf_op jit(solution)/shard_map/ppermute | solution.py:196
  4.9 8.2 %copy-start.8 = (s32[2]{0:T(128)S(1)}, s32[2]{0:T(128)}, u32[]{:S(2)}) copy-start(s32[2]{0:T(128)} %param.16) | copy-start | bytes 28
  5.0 1.3 copy-start.7
  6.3 95.1 %all-to-all-start = ((bf16[32,128,256]{2,1,0:T(8,128)(2,1)}), bf16[32,128,256]{2,1,0:T(8,128)(2,1)S(1)}, u32[]{:S(2)}, u32[]{:S(2)}) async-start(bf16[32,128,256]{2,1,0:T(8,128)(2,1)} %pack_moved.1), calls=%async_computation | async-start | bytes 4194304 | tf_op jit(solution)/shard_map/all_to_all | solution.py:312
  20.3 69.2 %copy-start.9 = (s32[32]{0:T(128)S(1)}, s32[32]{0:T(128)}, u32[]{:S(2)}) copy-start(s32[32]{0:T(128)} %param.17) | copy-start | bytes 388
  20.3 73.6 %copy-start = (bf16[256,1024]{1,0:T(8,128)(2,1)S(1)}, bf16[256,1024]{1,0:T(8,128)(2,1)}, u32[]{:S(2)}) copy-start(bf16[256,1024]{1,0:T(8,128)(2,1)} %q_ref.9) | copy-start | bytes 1572868
  20.3 73.6 %copy-start.1 = (bf16[512,256]{1,0:T(8,128)(2,1)S(1)}, bf16[512,256]{1,0:T(8,128)(2,1)}, u32[]{:S(2)}) copy-start(bf16[512,256]{1,0:T(8,128)(2,1)} %own_ref.1) | copy-start | bytes 786436
  20.4 73.6 %copy-start.2 = (bf16[256,256]{1,0:T(8,128)(2,1)S(1)}, bf16[256,256]{1,0:T(8,128)(2,1)}, u32[]{:S(2)}) copy-start(bf16[256,256]{1,0:T(8,128)(2,1)} %suffix_ref.5) | copy-start | bytes 393220
  20.4 4.8 %collective-permute-start.1 = (bf16[256,256]{1,0:T(8,128)(2,1)}, bf16[256,256]{1,0:T(8,128)(2,1)S(1)}, u32[]{:S(2)}, u32[]{:S(2)}) collective-permute-start(bf16[256,256]{1,0:T(8,128)(2,1)} %get-tuple-element.32), channel_id=1, source_target_pairs={{30,16},{31,17}} | collective-permute-start | bytes 393224 | tf_op jit(solution)/shard_map/ppermute | solution.py:203
  21.2 5.3 %collective-permute-start.2 = (bf16[256,256]{1,0:T(8,128)(2,1)}, bf16[256,256]{1,0:T(8,128)(2,1)S(1)}, u32[]{:S(2)}, u32[]{:S(2)}) collective-permute-start(bf16[256,256]{1,0:T(8,128)(2,1)} %get-tuple-element.33), channel_id=1, source_target_pairs={{30,18},{31,19}} | collective-permute-start | bytes 393224 | tf_op jit(solution)/shard_map/ppermute | solution.py:203
  21.8 5.9 %collective-permute-start.3 = (bf16[256,256]{1,0:T(8,128)(2,1)}, bf16[256,256]{1,0:T(8,128)(2,1)S(1)}, u32[]{:S(2)}, u32[]{:S(2)}) collective-permute-start(bf16[256,256]{1,0:T(8,128)(2,1)} %get-tuple-element.34), channel_id=1, source_target_pairs={{30,20},{31,21}} | collective-permute-start | bytes 393224 | tf_op jit(solution)/shard_map/ppermute | solution.py:203
  22.5 7.0 %collective-permute-start.4 = (bf16[256,256]{1,0:T(8,128)(2,1)}, bf16[256,256]{1,0:T(8,128)(2,1)}, u32[]{:S(2)}, u32[]{:S(2)}) collective-permute-start(bf16[256,256]{1,0:T(8,128)(2,1)} %get-tuple-element.35), channel_id=1, source_target_pairs={{30,22},{31,23}} | collective-permute-start | bytes 393224 | tf_op jit(solution)/shard_map/ppermute | solution.py:203
  23.8 7.2 %collective-permute-start.5 = (bf16[256,256]{1,0:T(8,128)(2,1)}, bf16[256,256]{1,0:T(8,128)(2,1)}, u32[]{:S(2)}, u32[]{:S(2)}) collective-permute-start(bf16[256,256]{1,0:T(8,128)(2,1)} %get-tuple-element.36), channel_id=1, source_target_pairs={{30,24},{31,25}} | collective-permute-start | bytes 393224 | tf_op jit(solution)/shard_map/ppermute | solution.py:203
  25.2 7.3 %collective-permute-start.6 = (bf16[256,256]{1,0:T(8,128)(2,1)}, bf16[256,256]{1,0:T(8,128)(2,1)}, u32[]{:S(2)}, u32[]{:S(2)}) collective-permute-start(bf16[256,256]{1,0:T(8,128)(2,1)} %get-tuple-element.37), channel_id=1, source_target_pairs={{30,26},{31,27}} | collective-permute-start | bytes 393224 | tf_op jit(solution)/shard_map/ppermute | solution.py:203
  26.5 6.3 %collective-permute-start.7 = (bf16[256,256]{1,0:T(8,128)(2,1)}, bf16[256,256]{1,0:T(8,128)(2,1)}, u32[]{:S(2)}, u32[]{:S(2)}) collective-permute-start(bf16[256,256]{1,0:T(8,128)(2,1)} %get-tuple-element.38), channel_id=1, source_target_pairs={{30,28},{31,29}} | collective-permute-start | bytes 393224 | tf_op jit(solution)/shard_map/ppermute | solution.py:203
  27.8 14.4 %collective-permute-start.10 = (bf16[1,256,256]{2,1,0:T(8,128)(2,1)}, bf16[1,256,256]{2,1,0:T(8,128)(2,1)S(1)}, u32[]{:S(2)}, u32[]{:S(2)}) collective-permute-start(bf16[1,256,256]{2,1,0:T(8,128)(2,1)} %get-tuple-element.41), channel_id=1, source_target_pairs={{0,4},{1,5},{2,6},{3,7},{4,0},{5,1},{6,2},{7,3},{8,12},{9,13},{10,... | collective-permute-start | bytes 393224 | tf_op jit(solution)/shard_map/ppermute | solution.py:199
  29.6 14.1 %collective-permute-start.11 = (bf16[1,256,256]{2,1,0:T(8,128)(2,1)}, bf16[1,256,256]{2,1,0:T(8,128)(2,1)}, u32[]{:S(2)}, u32[]{:S(2)}) collective-permute-start(bf16[1,256,256]{2,1,0:T(8,128)(2,1)} %get-tuple-element.42), channel_id=1, source_target_pairs={{0,6},{1,7},{2,4},{3,5},{4,2},{5,3},{6,0},{7,1},{8,14},{9,15},{10,... | collective-permute-start | bytes 393224 | tf_op jit(solution)/shard_map/ppermute | solution.py:199
  31.0 20.4 %collective-permute-start.12 = (bf16[1,256,256]{2,1,0:T(8,128)(2,1)}, bf16[1,256,256]{2,1,0:T(8,128)(2,1)S(1)}, u32[]{:S(2)}, u32[]{:S(2)}) collective-permute-start(bf16[1,256,256]{2,1,0:T(8,128)(2,1)} %get-tuple-element.43), channel_id=1, source_target_pairs={{0,8},{1,9},{2,10},{3,11},{4,12},{5,13},{6,14},{7,15},{8,0},{9,1},... | collective-permute-start | bytes 393224 | tf_op jit(solution)/shard_map/ppermute | solution.py:199
  32.5 21.8 %collective-permute-start.13 = (bf16[1,256,256]{2,1,0:T(8,128)(2,1)}, bf16[1,256,256]{2,1,0:T(8,128)(2,1)S(1)}, u32[]{:S(2)}, u32[]{:S(2)}) collective-permute-start(bf16[1,256,256]{2,1,0:T(8,128)(2,1)} %get-tuple-element.44), channel_id=1, source_target_pairs={{0,10},{1,11},{2,8},{3,9},{4,14},{5,15},{6,12},{7,13},{8,2},{9,3},... | collective-permute-start | bytes 393224 | tf_op jit(solution)/shard_map/ppermute | solution.py:199
  32.7 24.3 %collective-permute-start.14 = (bf16[1,256,256]{2,1,0:T(8,128)(2,1)}, bf16[1,256,256]{2,1,0:T(8,128)(2,1)S(1)}, u32[]{:S(2)}, u32[]{:S(2)}) collective-permute-start(bf16[1,256,256]{2,1,0:T(8,128)(2,1)} %get-tuple-element.45), channel_id=1, source_target_pairs={{0,12},{1,13},{2,14},{3,15},{4,8},{5,9},{6,10},{7,11},{8,4},{9,5},... | collective-permute-start | bytes 393224 | tf_op jit(solution)/shard_map/ppermute | solution.py:199
  42.2 19.3 %collective-permute-start.15 = (bf16[1,256,256]{2,1,0:T(8,128)(2,1)}, bf16[1,256,256]{2,1,0:T(8,128)(2,1)S(1)}, u32[]{:S(2)}, u32[]{:S(2)}) collective-permute-start(bf16[1,256,256]{2,1,0:T(8,128)(2,1)} %get-tuple-element.46), channel_id=1, source_target_pairs={{0,14},{1,15},{2,12},{3,13},{4,10},{5,11},{6,8},{7,9},{8,6},{9,7},... | collective-permute-start | bytes 393224 | tf_op jit(solution)/shard_map/ppermute | solution.py:199
  43.6 17.9 %collective-permute-start.9 = (bf16[1,256,256]{2,1,0:T(8,128)(2,1)}, bf16[1,256,256]{2,1,0:T(8,128)(2,1)S(1)}, u32[]{:S(2)}, u32[]{:S(2)}) collective-permute-start(bf16[1,256,256]{2,1,0:T(8,128)(2,1)} %get-tuple-element.40), channel_id=1, source_target_pairs={{0,2},{1,3},{2,0},{3,1},{4,6},{5,7},{6,4},{7,5},{8,10},{9,11},{10,... | collective-permute-start | bytes 393224 | tf_op jit(solution)/shard_map/ppermute | solution.py:199
  51.4 31.5 %collective-permute-start.8 = (bf16[256,256]{1,0:T(8,128)(2,1)S(1)}, bf16[256,256]{1,0:T(8,128)(2,1)S(1)}, u32[]{:S(2)}, u32[]{:S(2)}) collective-permute-start(bf16[256,256]{1,0:T(8,128)(2,1)S(1)} %select_select_fusion.1), channel_id=1, source_target_pairs={{16,0},{17,1},{18,2},{19,3},{20,4},{21,5},{22,6},{23,7},{24,8},{25... | collective-permute-start | bytes 393224 | tf_op jit(solution)/shard_map/ppermute | solution.py:232
  62.4 25.2 %collective-permute-start.16 = (bf16[1,256,256]{2,1,0:T(8,128)(2,1)S(1)}, bf16[1,256,256]{2,1,0:T(8,128)(2,1)S(1)}, u32[]{:S(2)}, u32[]{:S(2)}) collective-permute-start(bf16[1,256,256]{2,1,0:T(8,128)(2,1)S(1)} %select_select_fusion), channel_id=1, source_target_pairs={{0,16},{1,17},{2,18},{3,19},{4,20},{5,21},{6,22},{7,23},{8,24},{9,... | collective-permute-start | bytes 393224 | tf_op jit(solution)/shard_map/ppermute | solution.py:240
  87.7 11.1 %collective-permute-start.23 = (bf16[2,256,256]{2,1,0:T(8,128)(2,1)S(1)}, bf16[2,256,256]{2,1,0:T(8,128)(2,1)S(1)}, u32[]{:S(2)}, u32[]{:S(2)}) collective-permute-start(bf16[2,256,256]{2,1,0:T(8,128)(2,1)S(1)} %pad_maximum_fusion.refs_0_), channel_id=1, source_target_pairs={{0,4},{1,5},{2,6},{3,7},{4,0},{5,1},{6,2},{7,3},{8,12},{9,13},{10,... | collective-permute-start | bytes 786440 | tf_op jit(solution)/shard_map/ppermute | solution.py:199
  87.8 13.5 %collective-permute-start.17 = (bf16[2,256,256]{2,1,0:T(8,128)(2,1)S(1)}, bf16[2,256,256]{2,1,0:T(8,128)(2,1)}, u32[]{:S(2)}, u32[]{:S(2)}) collective-permute-start(bf16[2,256,256]{2,1,0:T(8,128)(2,1)S(1)} %pad_maximum_fusion.refs_0_), channel_id=1, source_target_pairs={{0,2},{1,3},{2,0},{3,1},{4,6},{5,7},{6,4},{7,5},{8,10},{9,11},{10,... | collective-permute-start | bytes 786440 | tf_op jit(solution)/shard_map/ppermute | solution.py:199
  96.5 1.3 copy-start.3
  97.8 1.0 copy-start.5
  98.8 11.7 %collective-permute-start.20 = (bf16[2,256,256]{2,1,0:T(8,128)(2,1)S(1)}, bf16[2,256,256]{2,1,0:T(8,128)(2,1)}, u32[]{:S(2)}, u32[]{:S(2)}) collective-permute-start(bf16[2,256,256]{2,1,0:T(8,128)(2,1)S(1)} %pad_maximum_fusion.refs_0_), channel_id=1, source_target_pairs={{0,8},{1,9},{2,10},{3,11},{4,12},{5,13},{6,14},{7,15},{8,0},{9,1},... | collective-permute-start | bytes 786440 | tf_op jit(solution)/shard_map/ppermute | solution.py:199
  98.8 13.0 %collective-permute-start.28 = (bf16[2,256,256]{2,1,0:T(8,128)(2,1)S(1)}, bf16[2,256,256]{2,1,0:T(8,128)(2,1)}, u32[]{:S(2)}, u32[]{:S(2)}) collective-permute-start(bf16[2,256,256]{2,1,0:T(8,128)(2,1)S(1)} %pad_maximum_fusion.refs_0_), channel_id=1, source_target_pairs={{0,1},{1,0},{2,3},{3,2},{4,5},{5,4},{6,7},{7,6},{8,9},{9,8},{10,11... | collective-permute-start | bytes 786440 | tf_op jit(solution)/shard_map/ppermute | solution.py:196
  98.8 21.6 %collective-permute-start.30 = (bf16[2,256,256]{2,1,0:T(8,128)(2,1)S(1)}, bf16[2,256,256]{2,1,0:T(8,128)(2,1)}, u32[]{:S(2)}, u32[]{:S(2)}) collective-permute-start(bf16[2,256,256]{2,1,0:T(8,128)(2,1)S(1)} %collective-permute-done.23.refs_4_), channel_id=1, source_target_pairs={{0,1},{1,0},{2,3},{3,2},{4,5},{5,4},{6,7},{7,6},{8,9},{9,8},{10,11... | collective-permute-start | bytes 786440 | tf_op jit(solution)/shard_map/ppermute | solution.py:196
  99.3 13.8 %collective-permute-start.24 = (bf16[2,256,256]{2,1,0:T(8,128)(2,1)S(1)}, bf16[2,256,256]{2,1,0:T(8,128)(2,1)S(1)}, u32[]{:S(2)}, u32[]{:S(2)}) collective-permute-start(bf16[2,256,256]{2,1,0:T(8,128)(2,1)S(1)} %collective-permute-done.23.refs_4_), channel_id=1, source_target_pairs={{0,8},{1,9},{2,10},{3,11},{4,12},{5,13},{6,14},{7,15},{8,0},{9,1},... | collective-permute-start | bytes 786440 | tf_op jit(solution)/shard_map/ppermute | solution.py:199
  101.4 10.7 %collective-permute-start.29 = (bf16[2,256,256]{2,1,0:T(8,128)(2,1)}, bf16[2,256,256]{2,1,0:T(8,128)(2,1)}, u32[]{:S(2)}, u32[]{:S(2)}) collective-permute-start(bf16[2,256,256]{2,1,0:T(8,128)(2,1)} %collective-permute-done.17.refs_2_), channel_id=1, source_target_pairs={{0,1},{1,0},{2,3},{3,2},{4,5},{5,4},{6,7},{7,6},{8,9},{9,8},{10,11... | collective-permute-start | bytes 786440 | tf_op jit(solution)/shard_map/ppermute | solution.py:196
  101.4 1.6 %copy-start.4 = (f32[8,256,256]{2,1,0:T(8,128)S(1)}, f32[8,256,256]{2,1,0:T(8,128)}, u32[]{:S(2)}) copy-start(f32[8,256,256]{2,1,0:T(8,128)} %copy-done.3) | copy-start | bytes 6291460
  103.0 1.2 copy-start.6
  110.6 9.9 %collective-permute-start.18 = (bf16[2,256,256]{2,1,0:T(8,128)(2,1)}, bf16[2,256,256]{2,1,0:T(8,128)(2,1)S(1)}, u32[]{:S(2)}, u32[]{:S(2)}) collective-permute-start(bf16[2,256,256]{2,1,0:T(8,128)(2,1)} %collective-permute-done.17.refs_2_), channel_id=1, source_target_pairs={{0,4},{1,5},{2,6},{3,7},{4,0},{5,1},{6,2},{7,3},{8,12},{9,13},{10,... | collective-permute-start | bytes 786440 | tf_op jit(solution)/shard_map/ppermute | solution.py:199
  111.8 14.6 %collective-permute-start.31 = (bf16[2,256,256]{2,1,0:T(8,128)(2,1)}, bf16[2,256,256]{2,1,0:T(8,128)(2,1)S(1)}, u32[]{:S(2)}, u32[]{:S(2)}) collective-permute-start(bf16[2,256,256]{2,1,0:T(8,128)(2,1)} %collective-permute-done.20.refs_6_), channel_id=1, source_target_pairs={{0,1},{1,0},{2,3},{3,2},{4,5},{5,4},{6,7},{7,6},{8,9},{9,8},{10,11... | collective-permute-start | bytes 786440 | tf_op jit(solution)/shard_map/ppermute | solution.py:196
  112.0 9.3 %collective-permute-start.21 = (bf16[2,256,256]{2,1,0:T(8,128)(2,1)}, bf16[2,256,256]{2,1,0:T(8,128)(2,1)S(1)}, u32[]{:S(2)}, u32[]{:S(2)}) collective-permute-start(bf16[2,256,256]{2,1,0:T(8,128)(2,1)} %collective-permute-done.20.refs_6_), channel_id=1, source_target_pairs={{0,2},{1,3},{2,0},{3,1},{4,6},{5,7},{6,4},{7,5},{8,10},{9,11},{10,... | collective-permute-start | bytes 786440 | tf_op jit(solution)/shard_map/ppermute | solution.py:199
  113.2 13.2 %collective-permute-start.26 = (bf16[2,256,256]{2,1,0:T(8,128)(2,1)S(1)}, bf16[2,256,256]{2,1,0:T(8,128)(2,1)S(1)}, u32[]{:S(2)}, u32[]{:S(2)}) collective-permute-start(bf16[2,256,256]{2,1,0:T(8,128)(2,1)S(1)} %collective-permute-done.24.refs_4_), channel_id=1, source_target_pairs={{0,2},{1,3},{2,0},{3,1},{4,6},{5,7},{6,4},{7,5},{8,10},{9,11},{10,... | collective-permute-start | bytes 786440 | tf_op jit(solution)/shard_map/ppermute | solution.py:199
  120.4 13.5 %collective-permute-start.25 = (bf16[2,256,256]{2,1,0:T(8,128)(2,1)S(1)}, bf16[2,256,256]{2,1,0:T(8,128)(2,1)S(1)}, u32[]{:S(2)}, u32[]{:S(2)}) collective-permute-start(bf16[2,256,256]{2,1,0:T(8,128)(2,1)S(1)} %collective-permute-done.24.refs_4_), channel_id=1, source_target_pairs={{0,1},{1,0},{2,3},{3,2},{4,5},{5,4},{6,7},{7,6},{8,9},{9,8},{10,11... | collective-permute-start | bytes 786440 | tf_op jit(solution)/shard_map/ppermute | solution.py:196
  120.5 13.4 %collective-permute-start.19 = (bf16[2,256,256]{2,1,0:T(8,128)(2,1)S(1)}, bf16[2,256,256]{2,1,0:T(8,128)(2,1)S(1)}, u32[]{:S(2)}, u32[]{:S(2)}) collective-permute-start(bf16[2,256,256]{2,1,0:T(8,128)(2,1)S(1)} %collective-permute-done.18.refs_0_), channel_id=1, source_target_pairs={{0,1},{1,0},{2,3},{3,2},{4,5},{5,4},{6,7},{7,6},{8,9},{9,8},{10,11... | collective-permute-start | bytes 786440 | tf_op jit(solution)/shard_map/ppermute | solution.py:196
  121.4 12.6 %collective-permute-start.22 = (bf16[2,256,256]{2,1,0:T(8,128)(2,1)S(1)}, bf16[2,256,256]{2,1,0:T(8,128)(2,1)S(1)}, u32[]{:S(2)}, u32[]{:S(2)}) collective-permute-start(bf16[2,256,256]{2,1,0:T(8,128)(2,1)S(1)} %collective-permute-done.21.refs_2_), channel_id=1, source_target_pairs={{0,1},{1,0},{2,3},{3,2},{4,5},{5,4},{6,7},{7,6},{8,9},{9,8},{10,11... | collective-permute-start | bytes 786440 | tf_op jit(solution)/shard_map/ppermute | solution.py:196
  126.4 7.6 %collective-permute-start.27 = (bf16[2,256,256]{2,1,0:T(8,128)(2,1)S(1)}, bf16[2,256,256]{2,1,0:T(8,128)(2,1)S(1)}, u32[]{:S(2)}, u32[]{:S(2)}) collective-permute-start(bf16[2,256,256]{2,1,0:T(8,128)(2,1)S(1)} %collective-permute-done.26.refs_6_), channel_id=1, source_target_pairs={{0,1},{1,0},{2,3},{3,2},{4,5},{5,4},{6,7},{7,6},{8,9},{9,8},{10,11... | collective-permute-start | bytes 786440 | tf_op jit(solution)/shard_map/ppermute | solution.py:196

commit v7 on v6

v7 whole, which is shorter than its diff:
```python
import functools

import jax
import jax.numpy as jnp
from jax import lax
from jax.experimental import pallas as pl
from jax.experimental.pallas import tpu as pltpu
from jax.sharding import PartitionSpec as P

LOG2E = 1.4426950408889634
DEAD_MARK = 1024.0
DEAD_ABOVE = 512.0
NEG = -1e30
CHUNK = 1024
PARAMS = pltpu.CompilerParams(vmem_limit_bytes=40 * 1024 * 1024)
COPY_PARAMS = pltpu.CompilerParams(vmem_limit_bytes=56 * 1024 * 1024)

IN_SMEM = pl.BlockSpec(memory_space=pltpu.SMEM)
IN_HBM = pl.BlockSpec(memory_space=pltpu.HBM)
MOVED_PARTS = 2


def fold_keys(q_ref, m_ref, acc_ref, keys, values, factor, mask=None):
    heads, tokens, width = acc_ref.shape
    size = keys.shape[1]
    for head in range(heads):
        rows = q_ref[:, head * size:(head + 1) * size]
        scores = lax.dot_general(
            rows, keys, (((1,), (1,)), ((), ())), preferred_element_type=jnp.float32
        )
        if mask is not None:
            scores = jnp.where(mask, scores, NEG)
        old_max = m_ref[head]
        new_max = jnp.maximum(old_max, jnp.max(scores, axis=1, keepdims=True))
        shrink = jnp.exp2((old_max - new_max) * factor)
        weights = jnp.exp2((scores - jnp.tile(new_max, (1, keys.shape[0] // size))) * factor)
        m_ref[head] = new_max
        acc_ref[head] = acc_ref[head] * jnp.tile(shrink, (1, width // size)) + jnp.dot(
            weights.astype(jnp.bfloat16), values, preferred_element_type=jnp.float32
        )


def finish(acc_ref, out_ref):
    heads, tokens, width = acc_ref.shape
    size = width // 2
    for head in range(heads):
        out_ref[:, head * size:(head + 1) * size] = (
            acc_ref[head, :, :size] / acc_ref[head, :, size:]
        ).astype(out_ref.dtype)


def stage_live(rows, live, suffix_ref, keys_ref, values_ref):
    size = suffix_ref.shape[1] // 2
    zeros = jnp.zeros((rows.shape[0], size), jnp.float32)
    spare = jnp.broadcast_to(suffix_ref[:1, :size].astype(jnp.float32), zeros.shape)
    keys_ref[:rows.shape[0], :] = jnp.where(live, rows[:, :size], spare).astype(jnp.bfloat16)
    values_ref[:rows.shape[0], :size] = jnp.where(live, rows[:, size:], zeros).astype(jnp.bfloat16)
    values_ref[:rows.shape[0], size:] = jnp.where(live, 1.0, zeros).astype(jnp.bfloat16)


def state_copies(state_here, state_there, sems):
    return [
        pltpu.make_async_copy(source, target, sems.at[place])
        for place, (source, target) in enumerate(zip(state_here, state_there))
    ]


def start_all(copies):
    for copy in copies:
        copy.start()


def wait_all(copies):
    for copy in copies:
        copy.wait()


def fold_local(factor, len_ref, q_ref, suffix_ref, own_ref, m_ref, acc_ref, keys_ref, values_ref):
    size = suffix_ref.shape[1] // 2
    suffix = suffix_ref.shape[0]
    own = own_ref.shape[0]
    m_ref[...] = jnp.full(m_ref.shape, NEG, jnp.float32)
    acc_ref[...] = jnp.zeros(acc_ref.shape, jnp.float32)
    values_ref[:suffix, :size] = suffix_ref[:, size:]
    values_ref[:suffix, size:] = jnp.ones((suffix, size), jnp.bfloat16)
    causal = lax.broadcasted_iota(jnp.int32, (suffix, suffix), 1) <= lax.broadcasted_iota(
        jnp.int32, (suffix, suffix), 0
    )
    fold_keys(
        q_ref, m_ref, acc_ref, suffix_ref[:, :size], values_ref[:suffix, :], factor, causal
    )
    live = lax.broadcasted_iota(jnp.int32, (own, size), 0) < len_ref[0]
    stage_live(own_ref[...].astype(jnp.float32), live, suffix_ref, keys_ref, values_ref)
    fold_keys(q_ref, m_ref, acc_ref, keys_ref[:own, :], values_ref[:own, :], factor)


def moved_kernel(factor, local, steps, *refs):
    q_ref, suffix_ref, kv_ref = refs[:3]
    state_out = refs[-7:-5]
    m_ref, acc_ref, keys_ref, values_ref, sems = refs[-5:]
    step = pl.program_id(0)

    if local:

        @pl.when(step == 0)
        def _():
            fold_local(factor, refs[3], q_ref, suffix_ref, refs[4], *refs[-5:-1])

    else:
        loads = state_copies(refs[3:5], (m_ref, acc_ref), sems)
        pl.when(step == 0)(lambda: start_all(loads))

    rows = kv_ref[...].reshape(-1, kv_ref.shape[-1]).astype(jnp.float32)
    size = suffix_ref.shape[1] // 2
    live = jnp.broadcast_to(rows[:, size:size + 1] < DEAD_ABOVE, (rows.shape[0], size))
    stage_live(rows, live, suffix_ref, keys_ref, values_ref)
    if not local:
        pl.when(step == 0)(lambda: wait_all(loads))
    count = rows.shape[0]
    fold_keys(q_ref, m_ref, acc_ref, keys_ref[:count, :], values_ref[:count, :], factor)

    @pl.when(step == steps - 1)
    def _():
        saves = state_copies((m_ref, acc_ref), state_out, sems)
        start_all(saves)
        wait_all(saves)


def prefix_kernel(factor, last, count, steps, which_ref, q_ref, *refs):
    pieces, refs = refs[:count], refs[count:]
    m_ref, acc_ref, keys_ref, values_ref, sems = refs[-5:]
    size = keys_ref.shape[1]
    step = pl.program_id(0)
    chunk = keys_ref.shape[0] // steps

    @pl.when(step == 0)
    def _():
        loads = state_copies(refs[:2], (m_ref, acc_ref), sems)
        start_all(loads)
        for place, piece in enumerate(pieces):
            rows = pl.ds(place * piece.shape[0], piece.shape[0])
            keys_ref[rows, :] = piece[:, :size]
            values_ref[rows, :size] = piece[:, size:]
        values_ref[:, size:] = jnp.ones((values_ref.shape[0], size), jnp.bfloat16)
        wait_all(loads)

    rows = pl.ds(pl.multiple_of(step * chunk, chunk), chunk)
    fold_keys(q_ref, m_ref, acc_ref, keys_ref[rows, :], values_ref[rows, :], factor)

    @pl.when(step == steps - 1)
    def _():
        if last:
            finish(acc_ref, refs[2])
        else:
            saves = state_copies((m_ref, acc_ref), refs[2:4], sems)
            start_all(saves)
            wait_all(saves)


def pack_kernel(target_ref, block_ref, count_ref, pool_ref, *refs):
    parts = refs[:-4]
    held_ref, mark_ref, in_sems, out_sems = refs[-4:]
    entries = target_ref.shape[1]
    mark_ref[...] = jnp.full(mark_ref.shape, DEAD_MARK, mark_ref.dtype)

    def load(entry):
        return pltpu.make_async_copy(
            pool_ref.at[block_ref[0, entry]], held_ref.at[entry], in_sems.at[entry]
        )

    def stores(entry, source):
        rows = parts[0].shape[1]
        return [
            pltpu.make_async_copy(
                source.at[pl.ds(place * rows, rows)],
                part.at[target_ref[0, entry]],
                out_sems.at[place, entry],
            )
            for place, part in enumerate(parts)
        ]

    @pl.loop(0, entries)
    def _(entry):
        live = entry < count_ref[0]
        pl.when(live)(lambda: load(entry).start())
        pl.when(jnp.logical_not(live))(lambda: start_all(stores(entry, mark_ref)))

    @pl.loop(0, entries)
    def _(entry):
        @pl.when(entry < count_ref[0])
        def _():
            load(entry).wait()
            start_all(stores(entry, held_ref.at[entry]))

    @pl.loop(0, entries)
    def _(entry):
        wait_all(stores(entry, mark_ref))


def stage_kernel(owner_ref, place_ref, kept_ref, swapped_ref, *refs):
    outs, (sought_ref, known_ref, in_sems, out_sems) = refs[:-4], refs[-4:]
    core, chip, is_last = place_ref[0], place_ref[1], place_ref[2]
    chips, sought = sought_ref.shape[:2]
    bits = chips.bit_length() - 1

    def load(source, step, prefix):
        if prefix < sought:
            place, target = chip ^ step, sought_ref.at[step, prefix]
        else:
            mirrored = sum((step >> bit & 1) << (bits - 1 - bit) for bit in range(bits))
            place, target = step, known_ref.at[mirrored]
        return pltpu.make_async_copy(source.at[core, place], target, in_sems.at[step, prefix])

    def start(step, prefix, here):
        pl.when(here)(lambda: load(kept_ref, step, prefix).start())
        pl.when(jnp.logical_not(here))(lambda: load(swapped_ref, step, prefix).start())

    def store(place):
        half = chips // 2
        if place < chips:
            source = sought_ref.at[place]
        else:
            source = known_ref.at[pl.ds((place - chips) * half, half)]
        return pltpu.make_async_copy(source, outs[place], out_sems.at[place])

    for step in range(chips):
        for prefix in range(sought):
            start(step, prefix, owner_ref[prefix] % 2 == core)

    @pl.when(is_last == 1)
    def _():
        for step in range(chips):
            start(step, sought, core == 1)

    for step in range(chips):
        for prefix in range(sought):
            load(kept_ref, step, prefix).wait()
        store(step).start()

    @pl.when(is_last == 1)
    def _():
        for step in range(chips):
            load(kept_ref, step, sought).wait()

    for place in range(chips, chips + 2):
        store(place).start()
    for place in range(chips + 2):
        store(place).wait()


def multicast(prefix_cache, owners, readers, outgoing):
    replicas = lax.axis_size("replica")
    me = lax.axis_index("replica")
    half = replicas // 2
    chips = half // 2
    bits = chips.bit_length() - 1
    chip = me // 2 % chips
    side = me // half
    width = prefix_cache.shape[1]
    ids = jnp.arange(owners.shape[0], dtype=jnp.int32)
    known = jnp.sum(jnp.where(owners == replicas - 1, ids, 0))
    sought = jnp.where(ids[:-1] >= known, owners[1:], owners[:-1])

    def swap_cores(rows):
        return lax.ppermute(rows, "replica", [(i, i ^ 1) for i in range(replicas)])

    def to_peer(rows, step):
        return lax.ppermute(rows, "replica", [(i, i ^ (2 * step)) for i in range(replicas)])

    split = prefix_cache.reshape(2, chips, -1, width)
    swapped, *outgoing = lax.optimization_barrier((swap_cores(prefix_cache), *outgoing))
    swapped = swapped.reshape(split.shape)
    rows = split.shape[2]
    pieces = jax.ShapeDtypeStruct((owners.shape[0] - 1, rows, width), split.dtype)
    known_pieces = jax.ShapeDtypeStruct((chips // 2, rows, width), split.dtype)
    staged = pl.pallas_call(
        stage_kernel,
        out_shape=(pieces,) * chips + (known_pieces,) * 2,
        in_specs=[IN_SMEM] * 2 + [IN_HBM] * 2,
        out_specs=(IN_HBM,) * (chips + 2),
        scratch_shapes=[
            pltpu.VMEM((chips, *pieces.shape), split.dtype),
            pltpu.VMEM((chips, rows, width), split.dtype),
            pltpu.SemaphoreType.DMA((chips, owners.shape[0])),
            pltpu.SemaphoreType.DMA((chips + 2,)),
        ],
        compiler_params=COPY_PARAMS,
        name="stage_prefix",
    )(
        sought,
        jnp.stack([me % 2, chip, (me // 2 == replicas // 2 - 1).astype(jnp.int32)]),
        split,
        swapped,
    )

    away = chip ^ (sought // 2 % chips)
    found = staged[0]
    for step in range(chips - 1, 0, -1):
        rows = to_peer(staged[step], step)
        found = jnp.where((away == step)[:, None, None], rows, found)
    passed = lax.ppermute(found, "replica", [(i, (i + half) % replicas) for i in range(replicas)])
    passed, *later = lax.optimization_barrier((passed, *outgoing[1:]))
    held = jnp.where((sought // half == side)[:, None, None], found, passed)

    sent, known_held = staged[chips], staged[chips + 1]
    for bit in range(bits):
        senders = [
            i for i in range(half, replicas) if (i // 2 % chips) >> bit == (chips - 1) >> bit
        ]
        passed = lax.ppermute(sent, "replica", [(i, i ^ (2 << bit)) for i in senders])
        known_held = jnp.where(chip >> bit & 1 == 1, known_held, passed)
        left = known_held.shape[0] // 2
        sent, known_held = known_held[:left], known_held[left:] if left else known_held
    passed = lax.ppermute(known_held, "replica", [(i + half, i) for i in range(half)])
    held = jnp.concatenate([jnp.where(side == 1, known_held, passed), held])

    gathered = {0: held}
    for step in sorted(range(1, chips), key=lambda step: (step.bit_count(), step)):
        members = [bit for bit in range(bits) if step >> bit & 1]
        linked = [bit for bit in members if step >> ((bit - 1) % bits) & 1]
        last = 1 << min(linked or members)
        gathered[step] = to_peer(gathered[step ^ last], last)
    parts = [[], []]
    for step, rows in gathered.items():
        parts[step.bit_count() > 1].extend((rows, swap_cores(rows)))
    wanted = readers[me]
    place = jnp.where(wanted == known, 0, wanted + (wanted < known))
    return parts, place[None], (outgoing[0], *later)


def whole(shape):
    return pl.BlockSpec(shape, lambda *args: (0,) * len(shape))


def cost(rows, keys, size):
    return pl.CostEstimate(
        flops=12 * rows * keys * size, bytes_accessed=4 * keys * size, transcendentals=rows * keys
    )


def on_device(
    queries,
    suffix_kv,
    own_cache,
    ctx_len,
    prefix_cache,
    owners,
    readers,
    kv_pool,
    mig_target,
    mig_block,
    mig_count,
):
    replicas = lax.axis_size("replica")
    size = suffix_kv.shape[1] // 2
    tokens = queries.shape[0]
    heads = queries.shape[1] // size
    factor = size ** (-0.5) * LOG2E
    row_count = tokens * heads
    state = (
        jax.ShapeDtypeStruct((heads, tokens, size), jnp.float32),
        jax.ShapeDtypeStruct((heads, tokens, 2 * size), jnp.float32),
    )
    def scratch(keys):
        return [
            *[pltpu.VMEM(part.shape, part.dtype) for part in state],
            pltpu.VMEM((keys, size), jnp.bfloat16),
            pltpu.VMEM((keys, 2 * size), jnp.bfloat16),
            pltpu.SemaphoreType.DMA((2,)),
        ]

    entries = mig_target.shape[1]
    rows = kv_pool.shape[1] // MOVED_PARTS
    part = jax.ShapeDtypeStruct((replicas, rows, kv_pool.shape[2]), kv_pool.dtype)
    outgoing = pl.pallas_call(
        pack_kernel,
        out_shape=(part,) * MOVED_PARTS,
        in_specs=[IN_SMEM] * 3 + [IN_HBM],
        out_specs=(IN_HBM,) * MOVED_PARTS,
        scratch_shapes=[
            pltpu.VMEM((entries, *kv_pool.shape[1:]), kv_pool.dtype),
            pltpu.VMEM(kv_pool.shape[1:], kv_pool.dtype),
            pltpu.SemaphoreType.DMA((entries,)),
            pltpu.SemaphoreType.DMA((MOVED_PARTS, entries)),
        ],
        compiler_params=COPY_PARAMS,
        name="pack_moved",
    )(mig_target, mig_block, mig_count, kv_pool)
    shared, place, outgoing = multicast(prefix_cache, owners, readers, outgoing)

    state_now = ()
    for count, part in enumerate(outgoing):
        arrived = lax.all_to_all(part, "replica", split_axis=0, concat_axis=0, tiled=True)
        local = count == 0
        group = min(replicas, max(1, CHUNK // rows))
        steps = replicas // group
        most = max(group * rows, own_cache.shape[0], tokens) if local else group * rows
        keys = replicas * rows + (tokens + own_cache.shape[0]) * local
        state_now = pl.pallas_call(
            functools.partial(moved_kernel, factor, local, steps),
            out_shape=state,
            grid=(steps,),
            in_specs=[
                whole(queries.shape),
                whole(suffix_kv.shape),
                pl.BlockSpec((group, rows, 2 * size), lambda i: (i, 0, 0)),
                *([IN_SMEM, whole(own_cache.shape)] if local else [IN_HBM, IN_HBM]),
            ],
            out_specs=(IN_HBM, IN_HBM),
            scratch_shapes=scratch(most),
            compiler_params=PARAMS,
            cost_estimate=cost(row_count, keys, size),
            name="moved_keys",
        )(queries, suffix_kv, arrived, *((ctx_len, own_cache) if local else state_now))

    for last, pieces in enumerate(shared):
        rows = pieces[0].shape[1]
        keys = len(pieces) * rows
        steps = max(1, keys // CHUNK)
        while keys % (steps * size):
            steps -= 1
        state_now = pl.pallas_call(
            functools.partial(prefix_kernel, factor, last, len(pieces), steps),
            out_shape=jax.ShapeDtypeStruct(queries.shape, queries.dtype) if last else state,
            grid_spec=pltpu.PrefetchScalarGridSpec(
                num_scalar_prefetch=1,
                grid=(steps,),
                in_specs=[
                    whole(queries.shape),
                    *[pl.BlockSpec((None, rows, 2 * size), lambda i, which: (which[0], 0, 0))]
                    * len(pieces),
                    IN_HBM,
                    IN_HBM,
                ],
                out_specs=whole(queries.shape) if last else (IN_HBM, IN_HBM),
                scratch_shapes=scratch(keys),
            ),
            compiler_params=PARAMS,
            cost_estimate=cost(row_count, keys, size),
            name="prefix_keys",
        )(place, queries, *pieces, *state_now)
    return state_now


def solution(mesh):
    in_specs = (
        P(("groups", "replica"), None),
        P(("groups", "replica"), None),
        P(("groups", "replica"), None),
        P(("groups", "replica")),
        P(("groups", "replica"), None),
        P("groups"),
        P("groups"),
        P(("groups", "replica"), None, None),
        P(("groups", "replica"), None),
        P(("groups", "replica"), None),
        P(("groups", "replica")),
    )
    out_specs = P(("groups", "replica"), None)
    return jax.shard_map(
        on_device, mesh=mesh, in_specs=in_specs, out_specs=out_specs, check_vma=False
    )
```

time: 142 us -> 149 us (1.049)
  waiting for transfers between devices: 32.5 us -> 47.4 us
  starting transfers between devices: 53.9 us -> 43.6 us
    ppermute x8 -> x4, waiting for transfers between devices: 0.02 us -> 29.4 us  [the longest x1 29.4 us: multicast(): lax.ppermute(known_held, 'replica', [(i + half, i) for i in range(half)])]
    ppermute x1, starting transfers between devices: 20.4 us -> 3.12 us  [multicast(): lax.ppermute(found, 'replica', [(i, (i + half) % replicas) for i in range...]
    ppermute x14, waiting for transfers between devices: 27.6 us -> 17.1 us  [to_peer(): lax.ppermute(rows, 'replica', [(i, i ^ 2 * step) for i in range(replicas)])]
    all_to_all x1 -> x2, starting transfers between devices: 6.83 us -> 15.2 us  [on_device(): lax.all_to_all(part, 'replica', split_axis=0, concat_axis=0, tiled=True)]
    ppermute x8 -> x4, starting transfers between devices: 8.66 us -> 4.28 us  [the longest x3 2.81 us: multicast(): passed = lax.ppermute(sent, 'replica', [(i, i ^ 2 << bit) for i in senders])]
    ppermute x1, waiting for transfers between devices: 4.78 us -> 0.89 us  [multicast(): lax.ppermute(found, 'replica', [(i, (i + half) % replicas) for i in range...]
    ppermute x14, starting transfers between devices: 16.2 us -> 19.4 us  [to_peer(): lax.ppermute(rows, 'replica', [(i, i ^ 2 * step) for i in range(replicas)])]
    pallas_call x5 -> x4, Pallas kernels: 22.4 us -> 22.8 us  [the longest x2 15.7 us: on_device(): pl.pallas_call(functools.partial(moved_kernel, factor, local, steps), out...]
  transfers between devices with their start and end apart: 33 -> 30, of which waited for: 8 -> 8; matrix products, arithmetic and copies ran while one was open for 3% -> 3% of each run, Pallas kernels for 21% -> 21%
where the time goes in v7:
time: 149 us; the launch traced here: 148 us
  waiting for transfers between devices  47.4 us (32%)
  starting transfers between devices  43.6 us (29%)
  Pallas kernels  38.9 us (26%)
  local copies, waits for them, and re-layouts  8.42 us (6%)
  between operations  7.09 us (5%)
  other arithmetic  2.4 us (2%)
    ppermute x1, waiting for transfers between devices, multicast(): lax.ppermute(known_held, 'replica', [(i + half, i) for i in range(half)])  29.4 us
    ppermute x14, starting transfers between devices, to_peer(): lax.ppermute(rows, 'replica', [(i, i ^ 2 * step) for i in range(replicas)])  19.4 us
    ppermute x14, waiting for transfers between devices, to_peer(): lax.ppermute(rows, 'replica', [(i, i ^ 2 * step) for i in range(replicas)])  17.1 us
    pallas_call x2, Pallas kernels, on_device(): pl.pallas_call(functools.partial(prefix_kernel, factor, last, len(pieces)...  16.2 us
    pallas_call x2, Pallas kernels, on_device(): pl.pallas_call(functools.partial(moved_kernel, factor, local, steps), out...  15.7 us
    all_to_all x2, starting transfers between devices, on_device(): lax.all_to_all(part, 'replica', split_axis=0, concat_axis=0, tiled=True)  15.2 us
    unnamed x30, local copies, waits for them, and re-layouts  6.6 us
    pallas_call x1, Pallas kernels, on_device(): pl.pallas_call(pack_kernel, out_shape=(part,) * MOVED_PARTS, in_specs=[IN...  3.86 us
  transfers between devices with their start and end apart: 30, of which 8 were waited for; matrix products, arithmetic and copies ran while one was open for 3% of the time, Pallas kernels for 21%

profile of v7, /device:TPU:0, one launch (start us, length us, event | category | flops | bytes accessed | tf_op | source)
XLA Modules:
  0.0 147.9 jit_solution(622842430859610834)
XLA Ops:
  0.0 0.5 collective-permute-start
  1.1 3.9 %pack_moved.1 = (bf16[32,64,256]{2,1,0:T(8,128)(2,1)}, bf16[32,64,256]{2,1,0:T(8,128)(2,1)}) custom-call(s32[1,32]{1,0:T(1,128)} %target_ref.1, s32[1,32]{1,0:T(1,128)} %block_ref.1, s32[1]{0:T(128)S(6)} %copy.13.count_ref, bf16[32,128,256]{2,1,0:T(8,128)(2,1)} %pool_ref.1), custom_call_target="tpu_custom_call" | custom-call | tf_op jit(solution)/shard_map/pack_moved/pallas_call | solution.py:375
  5.0 7.1 %all-to-all-start.1 = ((bf16[32,64,256]{2,1,0:T(8,128)(2,1)}), bf16[32,64,256]{2,1,0:T(8,128)(2,1)S(1)}, u32[]{:S(2)}, u32[]{:S(2)}) async-start(bf16[32,64,256]{2,1,0:T(8,128)(2,1)} %get-tuple-element.44), calls=%async_computation.1 | async-start | bytes 2097152 | tf_op jit(solution)/shard_map/all_to_all | solution.py:393
  12.2 0.7 fusion
  13.5 0.6 fusion.1
  15.3 0.6 pad_add_fusion.place_ref
  15.9 3.2 %stage_prefix.1 = (bf16[1,256,256]{2,1,0:T(8,128)(2,1)}, bf16[1,256,256]{2,1,0:T(8,128)(2,1)}, bf16[1,256,256]{2,1,0:T(8,128)(2,1)}, bf16[1,256,256]{2,1,0:T(8,1...) custom-call(s32[1]{0:T(128)S(6)} %select_n.112.owner_ref, ...), custom_call_target="tpu_custom_call" | custom-call | tf_op jit(solution)/shard_map/stage_prefix/pallas_call | solution.py:276
  19.1 0.8 collective-permute-start.1
  19.9 2.7 %collective-permute-start.10 = (bf16[1,256,256]{2,1,0:T(8,128)(2,1)}, bf16[1,256,256]{2,1,0:T(8,128)(2,1)S(1)}, u32[]{:S(2)}, u32[]{:S(2)}) collective-permute-start(bf16[1,256,256]{2,1,0:T(8,128)(2,1)} %get-tuple-element.38), channel_id=1, source_target_pairs={{0,12},{1,13},{2,14},{3,15},{4,8},{5,9},{6,10},{7,11},{8,4},{9,5},... | collective-permute-start | bytes 393224 | tf_op jit(solution)/shard_map/ppermute | solution.py:268
  22.7 1.5 collective-permute-start.11
  24.1 0.3 collective-permute-start.5
  24.4 1.8 %collective-permute-start.6 = (bf16[1,256,256]{2,1,0:T(8,128)(2,1)}, bf16[1,256,256]{2,1,0:T(8,128)(2,1)S(1)}, u32[]{:S(2)}, u32[]{:S(2)}) collective-permute-start(bf16[1,256,256]{2,1,0:T(8,128)(2,1)} %get-tuple-element.34), channel_id=1, source_target_pairs={{0,4},{1,5},{2,6},{3,7},{4,0},{5,1},{6,2},{7,3},{8,12},{9,13},{10,... | collective-permute-start | bytes 393224 | tf_op jit(solution)/shard_map/ppermute | solution.py:268
  26.2 7.0 %collective-permute-done.10 = bf16[1,256,256]{2,1,0:T(8,128)(2,1)S(1)} collective-permute-done((bf16[1,256,256]{2,1,0:T(8,128)(2,1)}, bf16[1,256,256]{2,1,0:T(8,128)(2,1)S(1)}, u32[]{:S(2)}, u32[]{:S(2)}) %collective-permute-start.10) | collective-permute-done | bytes 131104 | tf_op jit(solution)/shard_map/ppermute | solution.py:268
  33.2 2.6 %collective-permute-start.7 = (bf16[1,256,256]{2,1,0:T(8,128)(2,1)}, bf16[1,256,256]{2,1,0:T(8,128)(2,1)S(1)}, u32[]{:S(2)}, u32[]{:S(2)}) collective-permute-start(bf16[1,256,256]{2,1,0:T(8,128)(2,1)} %get-tuple-element.35), channel_id=1, source_target_pairs={{0,6},{1,7},{2,4},{3,5},{4,2},{5,3},{6,0},{7,1},{8,14},{9,15},{10,... | collective-permute-start | bytes 393224 | tf_op jit(solution)/shard_map/ppermute | solution.py:268
  35.8 2.5 %collective-permute-done.11 = bf16[1,256,256]{2,1,0:T(8,128)(2,1)S(1)} collective-permute-done((bf16[1,256,256]{2,1,0:T(8,128)(2,1)}, bf16[1,256,256]{2,1,0:T(8,128)(2,1)S(1)}, u32[]{:S(2)}, u32[]{:S(2)}) %collective-permute-start.11) | collective-permute-done | bytes 131104 | tf_op jit(solution)/shard_map/ppermute | solution.py:268
  38.3 3.0 %collective-permute-start.8 = (bf16[1,256,256]{2,1,0:T(8,128)(2,1)}, bf16[1,256,256]{2,1,0:T(8,128)(2,1)S(1)}, u32[]{:S(2)}, u32[]{:S(2)}) collective-permute-start(bf16[1,256,256]{2,1,0:T(8,128)(2,1)} %get-tuple-element.36), channel_id=1, source_target_pairs={{0,8},{1,9},{2,10},{3,11},{4,12},{5,13},{6,14},{7,15},{8,0},{9,1},... | collective-permute-start | bytes 393224 | tf_op jit(solution)/shard_map/ppermute | solution.py:268
  41.5 0.7 collective-permute-start.2
  42.2 3.7 %collective-permute-done.8 = bf16[1,256,256]{2,1,0:T(8,128)(2,1)S(1)} collective-permute-done((bf16[1,256,256]{2,1,0:T(8,128)(2,1)}, bf16[1,256,256]{2,1,0:T(8,128)(2,1)S(1)}, u32[]{:S(2)}, u32[]{:S(2)}) %collective-permute-start.8) | collective-permute-done | bytes 131104 | tf_op jit(solution)/shard_map/ppermute | solution.py:268
  46.0 1.5 %collective-permute-done.9 = bf16[1,256,256]{2,1,0:T(8,128)(2,1)S(1)} collective-permute-done((bf16[1,256,256]{2,1,0:T(8,128)(2,1)}, bf16[1,256,256]{2,1,0:T(8,128)(2,1)S(1)}, u32[]{:S(2)}, u32[]{:S(2)}) %collective-permute-start.9) | collective-permute-done | bytes 131104 | tf_op jit(solution)/shard_map/ppermute | solution.py:268
  47.5 3.1 %collective-permute-start.12 = (bf16[1,256,256]{2,1,0:T(8,128)(2,1)S(1)}, bf16[1,256,256]{2,1,0:T(8,128)(2,1)S(1)}, u32[]{:S(2)}, u32[]{:S(2)}) collective-permute-start(bf16[1,256,256]{2,1,0:T(8,128)(2,1)S(1)} %select_select_fusion), channel_id=1, source_target_pairs={{0,16},{1,17},{2,18},{3,19},{4,20},{5,21},{6,22},{7,23},{8,24},{9,... | collective-permute-start | bytes 393224 | tf_op jit(solution)/shard_map/ppermute | solution.py:301
  50.7 0.7 slice.31
  51.4 1.3 collective-permute-start.3
  52.7 0.9 collective-permute-done.12
  53.6 8.1 %all-to-all-start = ((bf16[32,64,256]{2,1,0:T(8,128)(2,1)}), bf16[32,64,256]{2,1,0:T(8,128)(2,1)S(1)}, u32[]{:S(2)}, u32[]{:S(2)}) async-start(bf16[32,64,256]{2,1,0:T(8,128)(2,1)} %get-tuple-element.43), calls=%async_computation | async-start | bytes 2097152 | tf_op jit(solution)/shard_map/all_to_all | solution.py:393
  61.7 0.9 slice_select_fusion.1
  62.7 1.5 collective-permute-start.4
  64.2 29.4 %collective-permute-done.4 = bf16[1,256,256]{2,1,0:T(8,128)(2,1)S(1)} collective-permute-done((bf16[1,256,256]{2,1,0:T(8,128)(2,1)S(1)}, bf16[1,256,256]{2,1,0:T(8,128)(2,1)S(1)}, u32[]{:S(2)}, u32[]{:S(2)}) %collective-permute-start.4) | collective-permute-done | bytes 131104 | tf_op jit(solution)/shard_map/ppermute | solution.py:314
  93.6 1.5 %collective-permute-start.19 = (bf16[2,256,256]{2,1,0:T(8,128)(2,1)S(1)}, bf16[2,256,256]{2,1,0:T(8,128)(2,1)S(1)}, u32[]{:S(2)}, u32[]{:S(2)}) collective-permute-start(bf16[2,256,256]{2,1,0:T(8,128)(2,1)S(1)} %pad_maximum_fusion.refs_0_), channel_id=1, source_target_pairs={{0,4},{1,5},{2,6},{3,7},{4,0},{5,1},{6,2},{7,3},{8,12},{9,13},{10,... | collective-permute-start | bytes 786440 | tf_op jit(solution)/shard_map/ppermute | solution.py:268
  95.1 1.5 %collective-permute-start.13 = (bf16[2,256,256]{2,1,0:T(8,128)(2,1)S(1)}, bf16[2,256,256]{2,1,0:T(8,128)(2,1)}, u32[]{:S(2)}, u32[]{:S(2)}) collective-permute-start(bf16[2,256,256]{2,1,0:T(8,128)(2,1)S(1)} %pad_maximum_fusion.refs_0_), channel_id=1, source_target_pairs={{0,2},{1,3},{2,0},{3,1},{4,6},{5,7},{6,4},{7,5},{8,10},{9,11},{10,... | collective-permute-start | bytes 786440 | tf_op jit(solution)/shard_map/ppermute | solution.py:268
  96.6 0.6 dynamic_slice.3
  101.2 0.3 collective-permute-done.19.refs_4_
  101.5 0.2 collective-permute-start.26
  101.7 1.9 %collective-permute-start.20 = (bf16[2,256,256]{2,1,0:T(8,128)(2,1)S(1)}, bf16[2,256,256]{2,1,0:T(8,128)(2,1)}, u32[]{:S(2)}, u32[]{:S(2)}) collective-permute-start(bf16[2,256,256]{2,1,0:T(8,128)(2,1)S(1)} %collective-permute-done.19.refs_4_), channel_id=1, source_target_pairs={{0,8},{1,9},{2,10},{3,11},{4,12},{5,13},{6,14},{7,15},{8,0},{9,1},... | collective-permute-start | bytes 786440 | tf_op jit(solution)/shard_map/ppermute | solution.py:268
  103.7 8.9 %moved_keys.2 = (f32[8,256,128]{2,1,0:T(8,128)S(1)}, f32[8,256,256]{2,1,0:T(8,128)S(1)}) custom-call(bf16[256,1024]{1,0:T(8,128)(2,1)S(1)} %copy-done, bf16[256,256]{1,0:T(8,128)(2,1)S(1)} %copy-done.6, bf16[32,64,256]{2,1,0:T(8,128)(2,1)S(1)} %all-to-all-done.1.refs_2_, s32[1]{0:T(128)S(6)} %copy.12.refs_3_, bf16[512,256]{1,0:T(8,128)(2,1)S(1)} %copy-done.1), custom_call_target="tpu_custom_call" | custom-call | flops 8858370048 | bytes 1441792 | tf_op jit(solution)/shard_map/moved_keys/pallas_call | solution.py:399
  112.6 1.3 copy-done.7
  114.0 1.0 copy-done.9
  114.9 0.5 collective-permute-start.14
  115.5 0.7 copy-done.2
  116.4 0.7 copy-done.4
  117.1 0.6 collective-permute-start.17
  117.7 1.4 collective-permute-start.22
  119.1 1.6 %copy-done.8 = f32[8,256,256]{2,1,0:T(8,128)S(1)} copy-done((f32[8,256,256]{2,1,0:T(8,128)S(1)}, f32[8,256,256]{2,1,0:T(8,128)}, u32[]{:S(2)}) %copy-start.8) | copy-done | bytes 2097176
  120.7 1.2 copy-done.10
  122.0 6.8 %moved_keys.3 = (f32[8,256,128]{2,1,0:T(8,128)S(1)}, f32[8,256,256]{2,1,0:T(8,128)S(1)}) custom-call(bf16[256,1024]{1,0:T(8,128)(2,1)S(1)} %copy-done, bf16[256,256]{1,0:T(8,128)(2,1)S(1)} %copy-done.6, bf16[32,64,256]{2,1,0:T(8,128)(2,1)S(1)} %all-to-all-done.refs_2_, f32[8,256,128]{2,1,0:T(8,128)S(1)} %copy-done.10, f32[8,256,256]{2,1,0:T(8,128)S(1)} %copy-done.8), custom_call_target="tpu_custom_call" | custom-call | flops 6442450944 | bytes 1048576 | tf_op jit(solution)/shard_map/moved_keys/pallas_call | solution.py:399
  128.9 0.5 collective-permute-start.15
  129.4 2.0 %collective-permute-done.22.refs_6_ = bf16[2,256,256]{2,1,0:T(8,128)(2,1)S(1)} collective-permute-done((bf16[2,256,256]{2,1,0:T(8,128)(2,1)}, bf16[2,256,256]{2,1,0:T(8,128)(2,1)S(1)}, u32[]{:S(2)}, u32[]{:S(2)}) %collective-permute-start.22) | collective-permute-done | bytes 262176 | tf_op jit(solution)/shard_map/ppermute | solution.py:268
  131.5 7.9 %prefix_keys.2 = (f32[8,256,128]{2,1,0:T(8,128)S(1)}, f32[8,256,256]{2,1,0:T(8,128)S(1)}) custom-call(s32[1]{0:T(128)} %bitcast.1.which_ref, bf16[256,1024]{1,0:T(8,128)(2,1)S(1)} %copy-done, bf16[2,256,256]{2,1,0:T(8,128)(2,1)S(1)} %pad_maximum_fusion.refs_0_, bf16[2,256,256]{2,1,0:T(8,128)(2,1)S(1)} %copy-done.3, ...), custom_call_target="tpu_custom_call" | custom-call | flops 6442450944 | bytes 1048576 | tf_op jit(solution)/shard_map/prefix_keys/pallas_call | solution.py:422
  139.4 8.3 %prefix_keys.3 = bf16[256,1024]{1,0:T(8,128)(2,1)} custom-call(s32[1]{0:T(128)} %bitcast.1.which_ref, bf16[256,1024]{1,0:T(8,128)(2,1)S(1)} %copy-done, bf16[2,256,256]{2,1,0:T(8,128)(2,1)S(1)} %collective-permute-done.14.refs_0_, bf16[2,256,256]{2,1,0:T(8,128)(2,1)S(1)} %collective-permute-done.15.refs_1_, ...), custom_call_target="tpu_custom_call" | custom-call | flops 6442450944 | bytes 1048576 | tf_op jit(solution)/shard_map/prefix_keys/pallas_call | solution.py:422
  (62 shorter events, 0.8 us)
Async XLA Ops:
  0.0 5.0 %collective-permute-start = (bf16[4096,256]{1,0:T(8,128)(2,1)}, bf16[4096,256]{1,0:T(8,128)(2,1)S(1)}, u32[]{:S(2)}, u32[]{:S(2)}) collective-permute-start(bf16[4096,256]{1,0:T(8,128)(2,1)} %param.15), channel_id=1, source_target_pairs={{0,1},{1,0},{2,3},{3,2},{4,5},{5,4},{6,7},{7,6},{8,9},{9,8},{10,11... | collective-permute-start | bytes 6291464 | tf_op jit(solution)/shard_map/ppermute | solution.py:265
  1.1 11.1 %copy-start.13 = (s32[2]{0:T(128)S(1)}, s32[2]{0:T(128)}, u32[]{:S(2)}) copy-start(s32[2]{0:T(128)} %param.16) | copy-start | bytes 28
  5.0 10.9 %copy-start.11 = (bf16[4096,256]{1,0:T(8,128)(2,1)}, bf16[4096,256]{1,0:T(8,128)(2,1)S(1)}, u32[]{:S(2)}) copy-start(bf16[4096,256]{1,0:T(8,128)(2,1)S(1)} %collective-permute-done) | copy-start | bytes 6291460
  5.0 48.6 %all-to-all-start.1 = ((bf16[32,64,256]{2,1,0:T(8,128)(2,1)}), bf16[32,64,256]{2,1,0:T(8,128)(2,1)S(1)}, u32[]{:S(2)}, u32[]{:S(2)}) async-start(bf16[32,64,256]{2,1,0:T(8,128)(2,1)} %get-tuple-element.44), calls=%async_computation.1 | async-start | bytes 2097152 | tf_op jit(solution)/shard_map/all_to_all | solution.py:393
  19.1 28.3 %copy-start.12 = (bf16[1,256,256]{2,1,0:T(8,128)(2,1)S(1)}, bf16[1,256,256]{2,1,0:T(8,128)(2,1)}, u32[]{:S(2)}) copy-start(bf16[1,256,256]{2,1,0:T(8,128)(2,1)} %get-tuple-element.40) | copy-start | bytes 393220
  19.1 22.2 %collective-permute-start.1 = (bf16[4,256,256]{2,1,0:T(8,128)(2,1)}, bf16[4,256,256]{2,1,0:T(8,128)(2,1)S(1)}, u32[]{:S(2)}, u32[]{:S(2)}) collective-permute-start(bf16[4,256,256]{2,1,0:T(8,128)(2,1)} %get-tuple-element.32), channel_id=1, source_target_pairs={{30,28},{31,29}} | collective-permute-start | bytes 1572872 | tf_op jit(solution)/shard_map/ppermute | solution.py:310
  19.9 13.3 %collective-permute-start.10 = (bf16[1,256,256]{2,1,0:T(8,128)(2,1)}, bf16[1,256,256]{2,1,0:T(8,128)(2,1)S(1)}, u32[]{:S(2)}, u32[]{:S(2)}) collective-permute-start(bf16[1,256,256]{2,1,0:T(8,128)(2,1)} %get-tuple-element.38), channel_id=1, source_target_pairs={{0,12},{1,13},{2,14},{3,15},{4,8},{5,9},{6,10},{7,11},{8,4},{9,5},... | collective-permute-start | bytes 393224 | tf_op jit(solution)/shard_map/ppermute | solution.py:268
  22.7 15.6 %collective-permute-start.11 = (bf16[1,256,256]{2,1,0:T(8,128)(2,1)}, bf16[1,256,256]{2,1,0:T(8,128)(2,1)S(1)}, u32[]{:S(2)}, u32[]{:S(2)}) collective-permute-start(bf16[1,256,256]{2,1,0:T(8,128)(2,1)} %get-tuple-element.39), channel_id=1, source_target_pairs={{0,14},{1,15},{2,12},{3,13},{4,10},{5,11},{6,8},{7,9},{8,6},{9,7},... | collective-permute-start | bytes 393224 | tf_op jit(solution)/shard_map/ppermute | solution.py:268
  24.1 17.3 %collective-permute-start.5 = (bf16[1,256,256]{2,1,0:T(8,128)(2,1)}, bf16[1,256,256]{2,1,0:T(8,128)(2,1)S(1)}, u32[]{:S(2)}, u32[]{:S(2)}) collective-permute-start(bf16[1,256,256]{2,1,0:T(8,128)(2,1)} %get-tuple-element.33), channel_id=1, source_target_pairs={{0,2},{1,3},{2,0},{3,1},{4,6},{5,7},{6,4},{7,5},{8,10},{9,11},{10,... | collective-permute-start | bytes 393224 | tf_op jit(solution)/shard_map/ppermute | solution.py:268
  24.4 17.8 %collective-permute-start.6 = (bf16[1,256,256]{2,1,0:T(8,128)(2,1)}, bf16[1,256,256]{2,1,0:T(8,128)(2,1)S(1)}, u32[]{:S(2)}, u32[]{:S(2)}) collective-permute-start(bf16[1,256,256]{2,1,0:T(8,128)(2,1)} %get-tuple-element.34), channel_id=1, source_target_pairs={{0,4},{1,5},{2,6},{3,7},{4,0},{5,1},{6,2},{7,3},{8,12},{9,13},{10,... | collective-permute-start | bytes 393224 | tf_op jit(solution)/shard_map/ppermute | solution.py:268
  33.2 9.0 %collective-permute-start.7 = (bf16[1,256,256]{2,1,0:T(8,128)(2,1)}, bf16[1,256,256]{2,1,0:T(8,128)(2,1)S(1)}, u32[]{:S(2)}, u32[]{:S(2)}) collective-permute-start(bf16[1,256,256]{2,1,0:T(8,128)(2,1)} %get-tuple-element.35), channel_id=1, source_target_pairs={{0,6},{1,7},{2,4},{3,5},{4,2},{5,3},{6,0},{7,1},{8,14},{9,15},{10,... | collective-permute-start | bytes 393224 | tf_op jit(solution)/shard_map/ppermute | solution.py:268
  38.3 7.6 %collective-permute-start.8 = (bf16[1,256,256]{2,1,0:T(8,128)(2,1)}, bf16[1,256,256]{2,1,0:T(8,128)(2,1)S(1)}, u32[]{:S(2)}, u32[]{:S(2)}) collective-permute-start(bf16[1,256,256]{2,1,0:T(8,128)(2,1)} %get-tuple-element.36), channel_id=1, source_target_pairs={{0,8},{1,9},{2,10},{3,11},{4,12},{5,13},{6,14},{7,15},{8,0},{9,1},... | collective-permute-start | bytes 393224 | tf_op jit(solution)/shard_map/ppermute | solution.py:268
  41.4 6.1 %collective-permute-start.9 = (bf16[1,256,256]{2,1,0:T(8,128)(2,1)}, bf16[1,256,256]{2,1,0:T(8,128)(2,1)S(1)}, u32[]{:S(2)}, u32[]{:S(2)}) collective-permute-start(bf16[1,256,256]{2,1,0:T(8,128)(2,1)} %get-tuple-element.37), channel_id=1, source_target_pairs={{0,10},{1,11},{2,8},{3,9},{4,14},{5,15},{6,12},{7,13},{8,2},{9,3},... | collective-permute-start | bytes 393224 | tf_op jit(solution)/shard_map/ppermute | solution.py:268
  41.5 9.2 %collective-permute-start.2 = (bf16[2,256,256]{2,1,0:T(8,128)(2,1)S(1)}, bf16[2,256,256]{2,1,0:T(8,128)(2,1)S(1)}, u32[]{:S(2)}, u32[]{:S(2)}) collective-permute-start(bf16[2,256,256]{2,1,0:T(8,128)(2,1)S(1)} %slice.29), channel_id=1, source_target_pairs={{28,24},{29,25},{30,26},{31,27}} | collective-permute-start | bytes 786440 | tf_op jit(solution)/shard_map/ppermute | solution.py:310
  47.5 6.1 %collective-permute-start.12 = (bf16[1,256,256]{2,1,0:T(8,128)(2,1)S(1)}, bf16[1,256,256]{2,1,0:T(8,128)(2,1)S(1)}, u32[]{:S(2)}, u32[]{:S(2)}) collective-permute-start(bf16[1,256,256]{2,1,0:T(8,128)(2,1)S(1)} %select_select_fusion), channel_id=1, source_target_pairs={{0,16},{1,17},{2,18},{3,19},{4,20},{5,21},{6,22},{7,23},{8,24},{9,... | collective-permute-start | bytes 393224 | tf_op jit(solution)/shard_map/ppermute | solution.py:301
  50.7 46.0 %copy-start.14 = (s32[32]{0:T(128)S(1)}, s32[32]{0:T(128)}, u32[]{:S(2)}) copy-start(s32[32]{0:T(128)} %param.17) | copy-start | bytes 388
  50.7 53.0 %copy-start = (bf16[256,1024]{1,0:T(8,128)(2,1)S(1)}, bf16[256,1024]{1,0:T(8,128)(2,1)}, u32[]{:S(2)}) copy-start(bf16[256,1024]{1,0:T(8,128)(2,1)} %q_ref.3) | copy-start | bytes 1572868
  50.7 53.0 %copy-start.1 = (bf16[512,256]{1,0:T(8,128)(2,1)S(1)}, bf16[512,256]{1,0:T(8,128)(2,1)}, u32[]{:S(2)}) copy-start(bf16[512,256]{1,0:T(8,128)(2,1)} %refs_4_.1) | copy-start | bytes 786436
  50.7 53.0 %copy-start.6 = (bf16[256,256]{1,0:T(8,128)(2,1)S(1)}, bf16[256,256]{1,0:T(8,128)(2,1)}, u32[]{:S(2)}) copy-start(bf16[256,256]{1,0:T(8,128)(2,1)} %refs_1_.3) | copy-start | bytes 393220
  51.4 10.4 %collective-permute-start.3 = (bf16[1,256,256]{2,1,0:T(8,128)(2,1)}, bf16[1,256,256]{2,1,0:T(8,128)(2,1)}, u32[]{:S(2)}, u32[]{:S(2)}) collective-permute-start(bf16[1,256,256]{2,1,0:T(8,128)(2,1)} %slice.31), channel_id=1, source_target_pairs={{24,16},{25,17},{26,18},{27,19},{28,20},{29,21},{30,22},{31,23}} | collective-permute-start | bytes 393224 | tf_op jit(solution)/shard_map/ppermute | solution.py:310
  53.6 65.6 %all-to-all-start = ((bf16[32,64,256]{2,1,0:T(8,128)(2,1)}), bf16[32,64,256]{2,1,0:T(8,128)(2,1)S(1)}, u32[]{:S(2)}, u32[]{:S(2)}) async-start(bf16[32,64,256]{2,1,0:T(8,128)(2,1)} %get-tuple-element.43), calls=%async_computation | async-start | bytes 2097152 | tf_op jit(solution)/shard_map/all_to_all | solution.py:393
  62.7 30.9 %collective-permute-start.4 = (bf16[1,256,256]{2,1,0:T(8,128)(2,1)S(1)}, bf16[1,256,256]{2,1,0:T(8,128)(2,1)S(1)}, u32[]{:S(2)}, u32[]{:S(2)}) collective-permute-start(bf16[1,256,256]{2,1,0:T(8,128)(2,1)S(1)} %slice_select_fusion.1), channel_id=1, source_target_pairs={{16,0},{17,1},{18,2},{19,3},{20,4},{21,5},{22,6},{23,7},{24,8},{25... | collective-permute-start | bytes 393224 | tf_op jit(solution)/shard_map/ppermute | solution.py:314
  93.6 7.9 %collective-permute-start.19 = (bf16[2,256,256]{2,1,0:T(8,128)(2,1)S(1)}, bf16[2,256,256]{2,1,0:T(8,128)(2,1)S(1)}, u32[]{:S(2)}, u32[]{:S(2)}) collective-permute-start(bf16[2,256,256]{2,1,0:T(8,128)(2,1)S(1)} %pad_maximum_fusion.refs_0_), channel_id=1, source_target_pairs={{0,4},{1,5},{2,6},{3,7},{4,0},{5,1},{6,2},{7,3},{8,12},{9,13},{10,... | collective-permute-start | bytes 786440 | tf_op jit(solution)/shard_map/ppermute | solution.py:268
  95.1 8.5 %collective-permute-start.13 = (bf16[2,256,256]{2,1,0:T(8,128)(2,1)S(1)}, bf16[2,256,256]{2,1,0:T(8,128)(2,1)}, u32[]{:S(2)}, u32[]{:S(2)}) collective-permute-start(bf16[2,256,256]{2,1,0:T(8,128)(2,1)S(1)} %pad_maximum_fusion.refs_0_), channel_id=1, source_target_pairs={{0,2},{1,3},{2,0},{3,1},{4,6},{5,7},{6,4},{7,5},{8,10},{9,11},{10,... | collective-permute-start | bytes 786440 | tf_op jit(solution)/shard_map/ppermute | solution.py:268
  101.1 13.9 %collective-permute-start.16 = (bf16[2,256,256]{2,1,0:T(8,128)(2,1)S(1)}, bf16[2,256,256]{2,1,0:T(8,128)(2,1)}, u32[]{:S(2)}, u32[]{:S(2)}) collective-permute-start(bf16[2,256,256]{2,1,0:T(8,128)(2,1)S(1)} %pad_maximum_fusion.refs_0_), channel_id=1, source_target_pairs={{0,8},{1,9},{2,10},{3,11},{4,12},{5,13},{6,14},{7,15},{8,0},{9,1},... | collective-permute-start | bytes 786440 | tf_op jit(solution)/shard_map/ppermute | solution.py:268
  101.1 14.3 %collective-permute-start.24 = (bf16[2,256,256]{2,1,0:T(8,128)(2,1)S(1)}, bf16[2,256,256]{2,1,0:T(8,128)(2,1)S(1)}, u32[]{:S(2)}, u32[]{:S(2)}) collective-permute-start(bf16[2,256,256]{2,1,0:T(8,128)(2,1)S(1)} %pad_maximum_fusion.refs_0_), channel_id=1, source_target_pairs={{0,1},{1,0},{2,3},{3,2},{4,5},{5,4},{6,7},{7,6},{8,9},{9,8},{10,11... | collective-permute-start | bytes 786440 | tf_op jit(solution)/shard_map/ppermute | solution.py:265
  101.5 27.3 %collective-permute-start.26 = (bf16[2,256,256]{2,1,0:T(8,128)(2,1)S(1)}, bf16[2,256,256]{2,1,0:T(8,128)(2,1)}, u32[]{:S(2)}, u32[]{:S(2)}) collective-permute-start(bf16[2,256,256]{2,1,0:T(8,128)(2,1)S(1)} %collective-permute-done.19.refs_4_), channel_id=1, source_target_pairs={{0,1},{1,0},{2,3},{3,2},{4,5},{5,4},{6,7},{7,6},{8,9},{9,8},{10,11... | collective-permute-start | bytes 786440 | tf_op jit(solution)/shard_map/ppermute | solution.py:265
  101.7 16.0 %collective-permute-start.20 = (bf16[2,256,256]{2,1,0:T(8,128)(2,1)S(1)}, bf16[2,256,256]{2,1,0:T(8,128)(2,1)}, u32[]{:S(2)}, u32[]{:S(2)}) collective-permute-start(bf16[2,256,256]{2,1,0:T(8,128)(2,1)S(1)} %collective-permute-done.19.refs_4_), channel_id=1, source_target_pairs={{0,8},{1,9},{2,10},{3,11},{4,12},{5,13},{6,14},{7,15},{8,0},{9,1},... | collective-permute-start | bytes 786440 | tf_op jit(solution)/shard_map/ppermute | solution.py:268
  103.7 12.7 %collective-permute-start.25 = (bf16[2,256,256]{2,1,0:T(8,128)(2,1)}, bf16[2,256,256]{2,1,0:T(8,128)(2,1)S(1)}, u32[]{:S(2)}, u32[]{:S(2)}) collective-permute-start(bf16[2,256,256]{2,1,0:T(8,128)(2,1)} %collective-permute-done.13.refs_2_), channel_id=1, source_target_pairs={{0,1},{1,0},{2,3},{3,2},{4,5},{5,4},{6,7},{7,6},{8,9},{9,8},{10,11... | collective-permute-start | bytes 786440 | tf_op jit(solution)/shard_map/ppermute | solution.py:265
  112.6 1.3 copy-start.7
  114.0 1.0 copy-start.9
  114.9 13.9 %collective-permute-start.14 = (bf16[2,256,256]{2,1,0:T(8,128)(2,1)}, bf16[2,256,256]{2,1,0:T(8,128)(2,1)S(1)}, u32[]{:S(2)}, u32[]{:S(2)}) collective-permute-start(bf16[2,256,256]{2,1,0:T(8,128)(2,1)} %collective-permute-done.13.refs_2_), channel_id=1, source_target_pairs={{0,4},{1,5},{2,6},{3,7},{4,0},{5,1},{6,2},{7,3},{8,12},{9,13},{10,... | collective-permute-start | bytes 786440 | tf_op jit(solution)/shard_map/ppermute | solution.py:268
  115.5 0.7 copy-start.2
  116.2 15.3 %collective-permute-start.27 = (bf16[2,256,256]{2,1,0:T(8,128)(2,1)}, bf16[2,256,256]{2,1,0:T(8,128)(2,1)S(1)}, u32[]{:S(2)}, u32[]{:S(2)}) collective-permute-start(bf16[2,256,256]{2,1,0:T(8,128)(2,1)} %collective-permute-done.16.refs_6_), channel_id=1, source_target_pairs={{0,1},{1,0},{2,3},{3,2},{4,5},{5,4},{6,7},{7,6},{8,9},{9,8},{10,11... | collective-permute-start | bytes 786440 | tf_op jit(solution)/shard_map/ppermute | solution.py:265
  116.4 0.7 copy-start.4
  117.1 12.3 %collective-permute-start.17 = (bf16[2,256,256]{2,1,0:T(8,128)(2,1)}, bf16[2,256,256]{2,1,0:T(8,128)(2,1)S(1)}, u32[]{:S(2)}, u32[]{:S(2)}) collective-permute-start(bf16[2,256,256]{2,1,0:T(8,128)(2,1)} %collective-permute-done.16.refs_6_), channel_id=1, source_target_pairs={{0,2},{1,3},{2,0},{3,1},{4,6},{5,7},{6,4},{7,5},{8,10},{9,11},{10,... | collective-permute-start | bytes 786440 | tf_op jit(solution)/shard_map/ppermute | solution.py:268
  117.7 13.7 %collective-permute-start.22 = (bf16[2,256,256]{2,1,0:T(8,128)(2,1)}, bf16[2,256,256]{2,1,0:T(8,128)(2,1)S(1)}, u32[]{:S(2)}, u32[]{:S(2)}) collective-permute-start(bf16[2,256,256]{2,1,0:T(8,128)(2,1)} %collective-permute-done.20.refs_4_), channel_id=1, source_target_pairs={{0,2},{1,3},{2,0},{3,1},{4,6},{5,7},{6,4},{7,5},{8,10},{9,11},{10,... | collective-permute-start | bytes 786440 | tf_op jit(solution)/shard_map/ppermute | solution.py:268
  119.1 1.6 %copy-start.8 = (f32[8,256,256]{2,1,0:T(8,128)S(1)}, f32[8,256,256]{2,1,0:T(8,128)}, u32[]{:S(2)}) copy-start(f32[8,256,256]{2,1,0:T(8,128)} %copy-done.7) | copy-start | bytes 6291460
  120.7 1.2 copy-start.10
  122.0 9.5 %copy-start.3 = (bf16[2,256,256]{2,1,0:T(8,128)(2,1)S(1)}, bf16[2,256,256]{2,1,0:T(8,128)(2,1)}, u32[]{:S(2)}) copy-start(bf16[2,256,256]{2,1,0:T(8,128)(2,1)} %copy-done.2) | copy-start | bytes 786436
  122.0 9.5 %copy-start.5 = (bf16[2,256,256]{2,1,0:T(8,128)(2,1)S(1)}, bf16[2,256,256]{2,1,0:T(8,128)(2,1)}, u32[]{:S(2)}) copy-start(bf16[2,256,256]{2,1,0:T(8,128)(2,1)} %copy-done.4) | copy-start | bytes 786436
  128.8 10.6 %collective-permute-start.21 = (bf16[2,256,256]{2,1,0:T(8,128)(2,1)}, bf16[2,256,256]{2,1,0:T(8,128)(2,1)S(1)}, u32[]{:S(2)}, u32[]{:S(2)}) collective-permute-start(bf16[2,256,256]{2,1,0:T(8,128)(2,1)} %collective-permute-done.20.refs_4_), channel_id=1, source_target_pairs={{0,1},{1,0},{2,3},{3,2},{4,5},{5,4},{6,7},{7,6},{8,9},{9,8},{10,11... | collective-permute-start | bytes 786440 | tf_op jit(solution)/shard_map/ppermute | solution.py:265
  128.9 10.5 %collective-permute-start.15 = (bf16[2,256,256]{2,1,0:T(8,128)(2,1)S(1)}, bf16[2,256,256]{2,1,0:T(8,128)(2,1)S(1)}, u32[]{:S(2)}, u32[]{:S(2)}) collective-permute-start(bf16[2,256,256]{2,1,0:T(8,128)(2,1)S(1)} %collective-permute-done.14.refs_0_), channel_id=1, source_target_pairs={{0,1},{1,0},{2,3},{3,2},{4,5},{5,4},{6,7},{7,6},{8,9},{9,8},{10,11... | collective-permute-start | bytes 786440 | tf_op jit(solution)/shard_map/ppermute | solution.py:265
  129.4 10.0 %collective-permute-start.18 = (bf16[2,256,256]{2,1,0:T(8,128)(2,1)S(1)}, bf16[2,256,256]{2,1,0:T(8,128)(2,1)S(1)}, u32[]{:S(2)}, u32[]{:S(2)}) collective-permute-start(bf16[2,256,256]{2,1,0:T(8,128)(2,1)S(1)} %collective-permute-done.17.refs_2_), channel_id=1, source_target_pairs={{0,1},{1,0},{2,3},{3,2},{4,5},{5,4},{6,7},{7,6},{8,9},{9,8},{10,11... | collective-permute-start | bytes 786440 | tf_op jit(solution)/shard_map/ppermute | solution.py:265
  131.4 8.0 %collective-permute-start.23 = (bf16[2,256,256]{2,1,0:T(8,128)(2,1)S(1)}, bf16[2,256,256]{2,1,0:T(8,128)(2,1)S(1)}, u32[]{:S(2)}, u32[]{:S(2)}) collective-permute-start(bf16[2,256,256]{2,1,0:T(8,128)(2,1)S(1)} %collective-permute-done.22.refs_6_), channel_id=1, source_target_pairs={{0,1},{1,0},{2,3},{3,2},{4,5},{5,4},{6,7},{7,6},{8,9},{9,8},{10,11... | collective-permute-start | bytes 786440 | tf_op jit(solution)/shard_map/ppermute | solution.py:265

commit v8 on v7

v8 whole, which is shorter than its diff:
```python
import functools

import jax
import jax.numpy as jnp
from jax import lax
from jax.experimental import pallas as pl
from jax.experimental.pallas import tpu as pltpu
from jax.sharding import PartitionSpec as P

LOG2E = 1.4426950408889634
DEAD_MARK = 1024.0
DEAD_ABOVE = 512.0
NEG = -1e30
CHUNK = 1024
PARAMS = pltpu.CompilerParams(vmem_limit_bytes=40 * 1024 * 1024)
COPY_PARAMS = pltpu.CompilerParams(vmem_limit_bytes=56 * 1024 * 1024)

IN_SMEM = pl.BlockSpec(memory_space=pltpu.SMEM)
IN_HBM = pl.BlockSpec(memory_space=pltpu.HBM)
MOVED_PARTS = 2
ONE_ROWS = 16
MAX_ROWS = 8


def fold_keys(qt_ref, state_ref, tokens, keys, values, factor, mask=None):
    high = values.shape[0]
    heads = qt_ref.shape[1] // tokens

    def score(head):
        columns = slice(head * tokens, (head + 1) * tokens)
        scores = jnp.dot(keys, qt_ref[:, columns], preferred_element_type=jnp.float32)
        return scores if mask is None else jnp.where(mask, scores, NEG)

    following = score(0)
    for head in range(heads):
        scores, following = following, score(head + 1) if head + 1 < heads else None
        columns = slice(head * tokens, (head + 1) * tokens)
        old_max = state_ref[high:high + 1, columns]
        new_max = jnp.maximum(old_max, jnp.max(scores, axis=0, keepdims=True))
        shrink = jnp.exp2((old_max - new_max) * factor)
        weights = jnp.exp2((scores - new_max) * factor).astype(jnp.bfloat16)
        state_ref[high:, columns] = jnp.broadcast_to(new_max, (MAX_ROWS, tokens))
        state_ref[:high, columns] = state_ref[:high, columns] * shrink + jnp.dot(
            values, weights, preferred_element_type=jnp.float32
        )


def finish(state_ref, out_ref):
    tokens, width = out_ref.shape
    size = state_ref.shape[0] - ONE_ROWS - MAX_ROWS
    for head in range(width // size):
        columns = slice(head * tokens, (head + 1) * tokens)
        attended = state_ref[:size, columns] / state_ref[size:size + 1, columns]
        out_ref[:, head * size:(head + 1) * size] = attended.T.astype(out_ref.dtype)


def stage_rows(rows, place, keys_ref, values_ref):
    size = keys_ref.shape[1]
    count = rows.shape[0]
    columns = pl.ds(place, count)
    keys_ref[columns, :] = rows[:, :size]
    values_ref[:size, columns] = rows[:, size:].astype(jnp.float32).T.astype(jnp.bfloat16)
    values_ref[size:, columns] = jnp.ones((ONE_ROWS, count), jnp.bfloat16)


def stage_live(rows, live, suffix_ref, keys_ref, values_ref):
    size = suffix_ref.shape[1] // 2
    count = rows.shape[0]
    zeros = jnp.zeros((count, size), jnp.float32)
    spare = jnp.broadcast_to(suffix_ref[:1, :size].astype(jnp.float32), zeros.shape)
    keys_ref[:count, :] = jnp.where(live, rows[:, :size], spare).astype(jnp.bfloat16)
    values_ref[:size, :count] = jnp.where(live, rows[:, size:], zeros).T.astype(jnp.bfloat16)
    ones = jnp.where(live, 1.0, zeros).T
    values_ref[size:, :count] = ones[:ONE_ROWS].astype(jnp.bfloat16)


def start_all(copies):
    for copy in copies:
        copy.start()


def wait_all(copies):
    for copy in copies:
        copy.wait()


def fold_local(factor, len_ref, qt_ref, suffix_ref, own_ref, state_ref, keys_ref, values_ref):
    size = suffix_ref.shape[1] // 2
    suffix = suffix_ref.shape[0]
    own = own_ref.shape[0]
    high = values_ref.shape[0]
    state_ref[:high] = jnp.zeros((high, state_ref.shape[1]), jnp.float32)
    state_ref[high:] = jnp.full((MAX_ROWS, state_ref.shape[1]), NEG, jnp.float32)
    stage_rows(suffix_ref[...], 0, keys_ref, values_ref)
    causal = lax.broadcasted_iota(jnp.int32, (suffix, suffix), 0) <= lax.broadcasted_iota(
        jnp.int32, (suffix, suffix), 1
    )
    fold_keys(
        qt_ref, state_ref, suffix, keys_ref[:suffix, :], values_ref[:, :suffix], factor, causal
    )
    live = lax.broadcasted_iota(jnp.int32, (own, size), 0) < len_ref[0]
    stage_live(own_ref[...].astype(jnp.float32), live, suffix_ref, keys_ref, values_ref)
    fold_keys(qt_ref, state_ref, suffix, keys_ref[:own, :], values_ref[:, :own], factor)


def moved_kernel(factor, local, steps, *refs):
    qt_ref, suffix_ref, kv_ref = refs[:3]
    state_out, state_ref, keys_ref, values_ref, sem = refs[-5:]
    step = pl.program_id(0)

    if local:

        @pl.when(step == 0)
        def _():
            fold_local(
                factor, refs[3], qt_ref, suffix_ref, refs[4], state_ref, keys_ref, values_ref
            )

    else:
        load = pltpu.make_async_copy(refs[3], state_ref, sem)
        pl.when(step == 0)(lambda: load.start())

    rows = kv_ref[...].reshape(-1, kv_ref.shape[-1]).astype(jnp.float32)
    count, size = rows.shape[0], rows.shape[1] // 2
    live = jnp.broadcast_to(rows[:, size:size + 1] < DEAD_ABOVE, (count, size))
    stage_live(rows, live, suffix_ref, keys_ref, values_ref)
    if not local:
        pl.when(step == 0)(lambda: load.wait())
    fold_keys(
        qt_ref, state_ref, suffix_ref.shape[0], keys_ref[:count, :], values_ref[:, :count], factor
    )

    @pl.when(step == steps - 1)
    def _():
        save = pltpu.make_async_copy(state_ref, state_out, sem)
        save.start()
        save.wait()


def prefix_kernel(factor, last, count, steps, tokens, which_ref, qt_ref, *refs):
    pieces, refs = refs[:count], refs[count:]
    state_in, out_ref, state_ref, keys_ref, values_ref, sem = refs
    step = pl.program_id(0)
    chunk = keys_ref.shape[0] // steps

    @pl.when(step == 0)
    def _():
        load = pltpu.make_async_copy(state_in, state_ref, sem)
        load.start()
        place = 0
        for piece in pieces:
            stage_rows(piece[...], place, keys_ref, values_ref)
            place += piece.shape[0]
        load.wait()

    rows = pl.ds(pl.multiple_of(step * chunk, keys_ref.shape[1]), chunk)
    fold_keys(qt_ref, state_ref, tokens, keys_ref[rows, :], values_ref[:, rows], factor)

    @pl.when(step == steps - 1)
    def _():
        if last:
            finish(state_ref, out_ref)
        else:
            save = pltpu.make_async_copy(state_ref, out_ref, sem)
            save.start()
            save.wait()


def pick_kernel(which_ref, *refs):
    pieces, out_ref = refs[:-1], refs[-1]
    for place, piece in enumerate(pieces):
        out_ref[pl.ds(place * piece.shape[0], piece.shape[0]), :] = piece[...]


def pack_kernel(target_ref, block_ref, count_ref, pool_ref, *refs):
    parts = refs[:-4]
    held_ref, mark_ref, in_sems, out_sems = refs[-4:]
    entries = target_ref.shape[1]
    mark_ref[...] = jnp.full(mark_ref.shape, DEAD_MARK, mark_ref.dtype)

    def load(entry):
        return pltpu.make_async_copy(
            pool_ref.at[block_ref[0, entry]], held_ref.at[entry], in_sems.at[entry]
        )

    def stores(entry, source):
        rows = parts[0].shape[1]
        return [
            pltpu.make_async_copy(
                source.at[pl.ds(place * rows, rows)],
                part.at[target_ref[0, entry]],
                out_sems.at[place, entry],
            )
            for place, part in enumerate(parts)
        ]

    @pl.loop(0, entries)
    def _(entry):
        live = entry < count_ref[0]
        pl.when(live)(lambda: load(entry).start())
        pl.when(jnp.logical_not(live))(lambda: start_all(stores(entry, mark_ref)))

    @pl.loop(0, entries)
    def _(entry):
        @pl.when(entry < count_ref[0])
        def _():
            load(entry).wait()
            start_all(stores(entry, held_ref.at[entry]))

    @pl.loop(0, entries)
    def _(entry):
        wait_all(stores(entry, mark_ref))


def placed(step, order):
    return sum((step >> bit & 1) << (len(order) - 1 - rank) for rank, bit in enumerate(order))


def stage_kernel(orders, owner_ref, place_ref, kept_ref, swapped_ref, *refs):
    outs, (sought_ref, known_ref, in_sems, out_sems) = refs[:-4], refs[-4:]
    core, chip, is_last = place_ref[0], place_ref[1], place_ref[2]
    chips, sought = sought_ref.shape[:2]

    def load(source, step, prefix):
        if prefix < sought:
            target = sought_ref.at[placed(step, orders[0]), prefix]
        else:
            target = known_ref.at[placed(step, orders[1]), 0]
        return pltpu.make_async_copy(source.at[core, chip ^ step], target, in_sems.at[step, prefix])

    def start(step, prefix, here):
        pl.when(here)(lambda: load(kept_ref, step, prefix).start())
        pl.when(jnp.logical_not(here))(lambda: load(swapped_ref, step, prefix).start())

    def stores(held_ref, first):
        half = chips // 2
        return [
            pltpu.make_async_copy(
                held_ref.at[pl.ds((1 - place) * half, half)],
                outs[first + place],
                out_sems.at[first + place],
            )
            for place in range(2)
        ]

    for step in range(chips):
        for prefix in range(sought):
            start(step, prefix, owner_ref[prefix] % 2 == core)

    @pl.when(is_last == 1)
    def _():
        for step in range(chips):
            start(step, sought, core == 1)

    for step in range(chips):
        for prefix in range(sought):
            load(kept_ref, step, prefix).wait()
    start_all(stores(sought_ref, 0))

    @pl.when(is_last == 1)
    def _():
        for step in range(chips):
            load(kept_ref, step, sought).wait()

    start_all(stores(known_ref, 2))
    wait_all(stores(sought_ref, 0) + stores(known_ref, 2))


def multicast(prefix_cache, owners, readers, outgoing):
    replicas = lax.axis_size("replica")
    me = lax.axis_index("replica")
    half = replicas // 2
    chips = half // 2
    bits = chips.bit_length() - 1
    chip = me // 2 % chips
    side = me // half
    width = prefix_cache.shape[1]
    ids = jnp.arange(owners.shape[0], dtype=jnp.int32)
    known = jnp.sum(jnp.where(owners == replicas - 1, ids, 0))
    sought = jnp.where(ids[:-1] >= known, owners[1:], owners[:-1])
    orders = ([*range(1, bits), 0], [*range(bits)])

    split = prefix_cache.reshape(2, chips, -1, width)
    swapped, *outgoing = lax.optimization_barrier((swap_cores(prefix_cache), *outgoing))
    swapped = swapped.reshape(split.shape)
    rows = split.shape[2]
    shares = [
        jax.ShapeDtypeStruct((chips // 2, count, rows, width), split.dtype)
        for count in (owners.shape[0] - 1, 1)
    ]
    staged = pl.pallas_call(
        functools.partial(stage_kernel, orders),
        out_shape=(shares[0],) * 2 + (shares[1],) * 2,
        in_specs=[IN_SMEM] * 2 + [IN_HBM] * 2,
        out_specs=(IN_HBM,) * 4,
        scratch_shapes=[
            *[pltpu.VMEM((chips, *share.shape[1:]), split.dtype) for share in shares],
            pltpu.SemaphoreType.DMA((chips, owners.shape[0])),
            pltpu.SemaphoreType.DMA((4,)),
        ],
        compiler_params=COPY_PARAMS,
        name="stage_prefix",
    )(
        sought,
        jnp.stack([me % 2, chip, (me // 2 == replicas // 2 - 1).astype(jnp.int32)]),
        split,
        swapped,
    )

    def scatter(sent, kept, source, order, senders):
        for rank, bit in enumerate(order):
            pairs = [(i, i ^ (2 << bit)) for i in range(replicas) if senders(i, order[rank:])]
            passed = lax.ppermute(sent, "replica", pairs)
            away = (source >> bit ^ chip >> bit) & 1 == 1
            kept = jnp.where(away[None, :, None, None], passed, kept)
            left = kept.shape[0] // 2
            if left:
                kept, sent = kept[:left], kept[left:]
        return kept[0]

    def holds(i, ahead):
        return i >= half and all(i // 2 >> bit & 1 for bit in ahead)

    found = scatter(*staged[:2], sought // 2 % chips, orders[0], lambda i, ahead: True)
    passed = lax.ppermute(found, "replica", [(i, (i + half) % replicas) for i in range(replicas)])
    held = jnp.where((sought // half == side)[:, None, None], found, passed)
    last_chip = jnp.full((1,), chips - 1, jnp.int32)
    found = scatter(*staged[2:], last_chip, orders[1], holds)
    passed = lax.ppermute(found, "replica", [(i + half, i) for i in range(half)])
    held = jnp.concatenate([jnp.where(side == 1, found, passed), held])
    wanted = jnp.stack([readers[me], readers[me ^ 1]])
    return held, jnp.where(wanted == known, 0, wanted + (wanted < known)), outgoing


def swap_cores(rows):
    return lax.ppermute(rows, "replica", [(i, i ^ 1) for i in range(lax.axis_size("replica"))])


def gather(held, place):
    replicas = lax.axis_size("replica")
    chips = replicas // 4
    bits = chips.bit_length() - 1
    gathered = {0: held}
    for step in sorted(range(1, chips), key=lambda step: (step.bit_count(), step)):
        members = [bit for bit in range(bits) if step >> bit & 1]
        linked = [bit for bit in members if step >> ((bit - 1) % bits) & 1]
        last = min(linked or members)
        gathered[step] = lax.ppermute(
            gathered[step ^ 1 << last], "replica", [(i, i ^ (2 << last)) for i in range(replicas)]
        )
    parts = []
    for late in (False, True):
        pieces = [gathered[step] for step in gathered if (step.bit_count() > 1) == late]
        rows, width = pieces[0].shape[1:]
        spec = pl.BlockSpec((None, rows, width), lambda i, which: (which[1], 0, 0))
        picked = pl.pallas_call(
            pick_kernel,
            out_shape=jax.ShapeDtypeStruct((len(pieces) * rows, width), held.dtype),
            grid_spec=pltpu.PrefetchScalarGridSpec(
                num_scalar_prefetch=1,
                grid=(1,),
                in_specs=[spec] * len(pieces),
                out_specs=pl.BlockSpec((len(pieces) * rows, width), lambda i, which: (0, 0)),
            ),
            compiler_params=PARAMS,
            name="pick_other",
        )(place, *pieces)
        parts.append((pieces, swap_cores(picked)))
    return parts


def whole(shape):
    return pl.BlockSpec(shape, lambda *args: (0,) * len(shape))


def cost(rows, keys, size):
    return pl.CostEstimate(
        flops=12 * rows * keys * size, bytes_accessed=4 * keys * size, transcendentals=rows * keys
    )


def on_device(
    queries,
    suffix_kv,
    own_cache,
    ctx_len,
    prefix_cache,
    owners,
    readers,
    kv_pool,
    mig_target,
    mig_block,
    mig_count,
):
    replicas = lax.axis_size("replica")
    size = suffix_kv.shape[1] // 2
    tokens = queries.shape[0]
    heads = queries.shape[1] // size
    factor = size ** (-0.5) * LOG2E
    row_count = tokens * heads
    state = jax.ShapeDtypeStruct((size + ONE_ROWS + MAX_ROWS, row_count), jnp.float32)
    columns = queries.reshape(tokens, heads, size).transpose(2, 1, 0).reshape(size, row_count)

    def scratch(keys):
        return [
            pltpu.VMEM(state.shape, state.dtype),
            pltpu.VMEM((keys, size), jnp.bfloat16),
            pltpu.VMEM((size + ONE_ROWS, keys), jnp.bfloat16),
            pltpu.SemaphoreType.DMA,
        ]

    entries = mig_target.shape[1]
    rows = kv_pool.shape[1] // MOVED_PARTS
    part = jax.ShapeDtypeStruct((replicas, rows, kv_pool.shape[2]), kv_pool.dtype)
    outgoing = pl.pallas_call(
        pack_kernel,
        out_shape=(part,) * MOVED_PARTS,
        in_specs=[IN_SMEM] * 3 + [IN_HBM],
        out_specs=(IN_HBM,) * MOVED_PARTS,
        scratch_shapes=[
            pltpu.VMEM((entries, *kv_pool.shape[1:]), kv_pool.dtype),
            pltpu.VMEM(kv_pool.shape[1:], kv_pool.dtype),
            pltpu.SemaphoreType.DMA((entries,)),
            pltpu.SemaphoreType.DMA((MOVED_PARTS, entries)),
        ],
        compiler_params=COPY_PARAMS,
        name="pack_moved",
    )(mig_target, mig_block, mig_count, kv_pool)
    held, place, outgoing = multicast(prefix_cache, owners, readers, outgoing)

    def fold_moved(part, state_now):
        arrived = lax.all_to_all(part, "replica", split_axis=0, concat_axis=0, tiled=True)
        local = state_now is None
        group = min(replicas, max(1, CHUNK // rows))
        steps = replicas // group
        most = max(group * rows, own_cache.shape[0], tokens) if local else group * rows
        keys = replicas * rows + (tokens + own_cache.shape[0]) * local
        return pl.pallas_call(
            functools.partial(moved_kernel, factor, local, steps),
            out_shape=state,
            grid=(steps,),
            in_specs=[
                whole(columns.shape),
                whole(suffix_kv.shape),
                pl.BlockSpec((group, rows, 2 * size), lambda i: (i, 0, 0)),
                *([IN_SMEM, whole(own_cache.shape)] if local else [IN_HBM]),
            ],
            out_specs=IN_HBM,
            scratch_shapes=scratch(most),
            compiler_params=PARAMS,
            cost_estimate=cost(row_count, keys, size),
            name="moved_keys",
        )(columns, suffix_kv, arrived, *((ctx_len, own_cache) if local else (state_now,)))

    state_now = fold_moved(outgoing[0], None)
    held, state_now, *later = lax.optimization_barrier((held, state_now, *outgoing[1:]))
    for part in later:
        state_now = fold_moved(part, state_now)

    for last, (pieces, others) in enumerate(gather(held, place)):
        piece_rows = pieces[0].shape[1]
        keys = 2 * len(pieces) * piece_rows
        steps = max(1, keys // CHUNK)
        while keys % (steps * size):
            steps -= 1
        state_now = pl.pallas_call(
            functools.partial(prefix_kernel, factor, last, len(pieces) + 1, steps, tokens),
            out_shape=jax.ShapeDtypeStruct(queries.shape, queries.dtype) if last else state,
            grid_spec=pltpu.PrefetchScalarGridSpec(
                num_scalar_prefetch=1,
                grid=(steps,),
                in_specs=[
                    whole(columns.shape),
                    *[pl.BlockSpec((None, piece_rows, 2 * size), lambda i, which: (which[0], 0, 0))]
                    * len(pieces),
                    whole(others.shape),
                    IN_HBM,
                ],
                out_specs=whole(queries.shape) if last else IN_HBM,
                scratch_shapes=scratch(keys),
            ),
            compiler_params=PARAMS,
            cost_estimate=cost(row_count, keys, size),
            name="prefix_keys",
        )(place, columns, *pieces, others, state_now)
    return state_now


def solution(mesh):
    in_specs = (
        P(("groups", "replica"), None),
        P(("groups", "replica"), None),
        P(("groups", "replica"), None),
        P(("groups", "replica")),
        P(("groups", "replica"), None),
        P("groups"),
        P("groups"),
        P(("groups", "replica"), None, None),
        P(("groups", "replica"), None),
        P(("groups", "replica"), None),
        P(("groups", "replica")),
    )
    out_specs = P(("groups", "replica"), None)
    return jax.shard_map(
        on_device, mesh=mesh, in_specs=in_specs, out_specs=out_specs, check_vma=False
    )
```

time: 149 us -> 156 us (1.047)
  starting transfers between devices: 43.6 us -> 35.8 us
  Pallas kernels: 38.9 us -> 46.3 us
  waiting for transfers between devices: 47.4 us -> 53.4 us
  other arithmetic: 2.4 us -> 6.22 us
  between operations: 7.09 us -> 3.86 us
  local copies, waits for them, and re-layouts: 8.42 us -> 10.1 us
    all_to_all x2, starting transfers between devices: 15.2 us -> 9.5 us  [fold_moved(): lax.all_to_all(part, 'replica', split_axis=0, concat_axis=0, tiled=True)]
    pallas_call x3 -> x5, Pallas kernels: 18.9 us -> 23.5 us  [the longest x2 17.9 us: fold_moved(): pl.pallas_call(functools.partial(moved_kernel, factor, local, steps), out...]
    ppermute x27 -> x17, waiting for transfers between devices: 46.5 us -> 50.7 us  [the longest x7 25.6 us: gather(): lax.ppermute(gathered[step ^ 1 << last], 'replica', [(i, i ^ 2 << last) f...]
    ppermute x27 -> x17, starting transfers between devices: 25.3 us -> 21.6 us  [the longest x6 9.89 us: scatter(): passed = lax.ppermute(sent, 'replica', pairs)]
    select_n x5 -> x6, other arithmetic: 1.08 us -> 4.22 us  [the longest x4 2.29 us: scatter(): kept = jnp.where(away[None, :, None, None], passed, kept)]
    pallas_call x2, Pallas kernels: 16.2 us -> 18.9 us  [on_device(): pl.pallas_call(functools.partial(prefix_kernel, factor, last, len(pieces)...]
    ppermute x1, waiting for transfers between devices: 0.89 us -> 2.7 us  [multicast(): lax.ppermute(found, 'replica', [(i, (i + half) % replicas) for i in range...]
    ppermute x1, starting transfers between devices: 3.12 us -> 4.72 us  [multicast(): lax.ppermute(found, 'replica', [(i, (i + half) % replicas) for i in range...]
  transfers between devices with their start and end apart: 30 -> 20, of which waited for: 8 -> 10; matrix products, arithmetic and copies ran while one was open for 3% -> 7% of each run, Pallas kernels for 21% -> 15%
where the time goes in v8:
time: 156 us
  waiting for transfers between devices  53.4 us (34%)
  Pallas kernels  46.3 us (30%)
  starting transfers between devices  35.8 us (23%)
  local copies, waits for them, and re-layouts  10.1 us (6%)
  other arithmetic  6.22 us (4%)
  between operations  3.86 us (2%)
    ppermute x7, waiting for transfers between devices, gather(): lax.ppermute(gathered[step ^ 1 << last], 'replica', [(i, i ^ 2 << last) f...  25.6 us
    pallas_call x2, Pallas kernels, on_device(): pl.pallas_call(functools.partial(prefix_kernel, factor, last, len(pieces)...  18.9 us
    pallas_call x2, Pallas kernels, fold_moved(): pl.pallas_call(functools.partial(moved_kernel, factor, local, steps), out...  17.9 us
    ppermute x6, waiting for transfers between devices, scatter(): passed = lax.ppermute(sent, 'replica', pairs)  17.6 us
    ppermute x6, starting transfers between devices, scatter(): passed = lax.ppermute(sent, 'replica', pairs)  9.89 us
    ppermute x7, starting transfers between devices, gather(): lax.ppermute(gathered[step ^ 1 << last], 'replica', [(i, i ^ 2 << last) f...  9.82 us
    all_to_all x2, starting transfers between devices, fold_moved(): lax.all_to_all(part, 'replica', split_axis=0, concat_axis=0, tiled=True)  9.5 us
    ppermute x1, waiting for transfers between devices, multicast(): lax.ppermute(found, 'replica', [(i + half, i) for i in range(half)])  7.42 us
  transfers between devices with their start and end apart: 20, of which 10 were waited for; matrix products, arithmetic and copies ran while one was open for 7% of the time, Pallas kernels for 15%

profile of v8, /device:TPU:0, one launch (start us, length us, event | category | flops | bytes accessed | tf_op | source)
XLA Modules:
  0.0 155.7 jit_solution(851895679933402895)
XLA Ops:
  1.1 1.4 fusion.3
  3.1 1.4 fusion.4
  5.9 3.9 %pack_moved.1 = (bf16[32,64,256]{2,1,0:T(8,128)(2,1)}, bf16[32,64,256]{2,1,0:T(8,128)(2,1)}) custom-call(s32[1,32]{1,0:T(1,128)} %target_ref.1, s32[1,32]{1,0:T(1,128)} %block_ref.1, s32[1]{0:T(128)S(6)} %copy.16.count_ref, bf16[32,128,256]{2,1,0:T(8,128)(2,1)} %pool_ref.1), custom_call_target="tpu_custom_call" | custom-call | tf_op jit(solution)/shard_map/pack_moved/pallas_call | solution.py:415
  9.8 0.6 pad_add_fusion.place_ref
  10.3 1.4 copy-done.9
  11.7 3.4 %stage_prefix.1 = (bf16[4,1,256,256]{3,2,1,0:T(8,128)(2,1)}, bf16[4,1,256,256]{3,2,1,0:T(8,128)(2,1)}, bf16[4,1,256,256]{3,2,1,0:T(8,128)(2,1)}, bf16[4,1,256,256]{3,2,1,0:T(8,128)(2,1)}) custom-call(s32[1]{0:T(128)S(6)} %select_n.91.owner_ref, s32[3]{0:T(128)} %pad_add_fusion.place_ref, bf16[2,8,256,256]{3,2,1,0:T(8,128)(2,1)} %bitcast.31, ...), custom_call_target="tpu_custom_call" | custom-call | tf_op jit(solution)/shard_map/stage_prefix/pallas_call | solution.py:291
  15.1 1.6 %collective-permute-start.1 = (bf16[4,1,256,256]{3,2,1,0:T(8,128)(2,1)}, bf16[4,1,256,256]{3,2,1,0:T(8,128)(2,1)}, u32[]{:S(2)}, u32[]{:S(2)}) collective-permute-start(bf16[4,1,256,256]{3,2,1,0:T(8,128)(2,1)} %get-tuple-element.20), channel_id=1, source_target_pairs={{30,28},{31,29}} | collective-permute-start | bytes 1572872 | tf_op jit(solution)/shard_map/ppermute | solution.py:313
  16.8 2.4 %collective-permute-start.5 = (bf16[4,1,256,256]{3,2,1,0:T(8,128)(2,1)}, bf16[4,1,256,256]{3,2,1,0:T(8,128)(2,1)}, u32[]{:S(2)}, u32[]{:S(2)}) collective-permute-start(bf16[4,1,256,256]{3,2,1,0:T(8,128)(2,1)} %get-tuple-element.22), channel_id=1, source_target_pairs={{0,4},{1,5},{2,6},{3,7},{4,0},{5,1},{6,2},{7,3},{8,12},{9,13},{10,... | collective-permute-start | bytes 1572872 | tf_op jit(solution)/shard_map/ppermute | solution.py:313
  19.2 6.7 %all-to-all-start = ((bf16[32,64,256]{2,1,0:T(8,128)(2,1)}), bf16[32,64,256]{2,1,0:T(8,128)(2,1)S(1)}, u32[]{:S(2)}, u32[]{:S(2)}) async-start(bf16[32,64,256]{2,1,0:T(8,128)(2,1)} %get-tuple-element.24), calls=%async_computation | async-start | bytes 2097152 | tf_op jit(solution)/shard_map/all_to_all | solution.py:432
  25.9 1.2 broadcast_select_fusion.1
  27.1 1.4 collective-permute-start.2
  28.5 9.8 %collective-permute-done.5 = bf16[4,1,256,256]{3,2,1,0:T(8,128)(2,1)} collective-permute-done((bf16[4,1,256,256]{3,2,1,0:T(8,128)(2,1)}, bf16[4,1,256,256]{3,2,1,0:T(8,128)(2,1)}, u32[]{:S(2)}, u32[]{:S(2)}) %collective-permute-start.5) | collective-permute-done | bytes 524320 | tf_op jit(solution)/shard_map/ppermute | solution.py:313
  38.3 0.7 slice.48
  39.0 0.6 collective-permute-start.6
  39.7 1.4 copy.12
  41.1 1.1 copy.14
  43.0 1.0 slice_select_fusion.1
  44.0 0.7 collective-permute-start.3
  44.7 6.2 %collective-permute-done.6 = bf16[2,1,256,256]{3,2,1,0:T(8,128)(2,1)} collective-permute-done((bf16[2,1,256,256]{3,2,1,0:T(8,128)(2,1)}, bf16[2,1,256,256]{3,2,1,0:T(8,128)(2,1)}, u32[]{:S(2)}, u32[]{:S(2)}) %collective-permute-start.6) | collective-permute-done | bytes 262176 | tf_op jit(solution)/shard_map/ppermute | solution.py:313
  50.9 3.2 %collective-permute-start.7 = (bf16[1,1,256,256]{3,2,1,0:T(8,128)(2,1)S(1)}, bf16[1,1,256,256]{3,2,1,0:T(8,128)(2,1)S(1)}, u32[]{:S(2)}, u32[]{:S(2)}) collective-permute-start(bf16[1,1,256,256]{3,2,1,0:T(8,128)(2,1)S(1)} %slice.50), channel_id=1, source_target_pairs={{0,2},{1,3},{2,0},{3,1},{4,6},{5,7},{6,4},{7,5},{8,10},{9,11},{10,... | collective-permute-start | bytes 393224 | tf_op jit(solution)/shard_map/ppermute | solution.py:313
  54.2 1.3 collective-permute-start.4
  55.5 1.6 %collective-permute-done.7 = bf16[1,1,256,256]{3,2,1,0:T(8,128)(2,1)S(1)} collective-permute-done((bf16[1,1,256,256]{3,2,1,0:T(8,128)(2,1)S(1)}, bf16[1,1,256,256]{3,2,1,0:T(8,128)(2,1)S(1)}, u32[]{:S(2)}, u32[]{:S(2)}) %collective-permute-start.7) | collective-permute-done | bytes 131104 | tf_op jit(solution)/shard_map/ppermute | solution.py:313
  57.1 4.7 %collective-permute-start.8 = (bf16[1,256,256]{2,1,0:T(8,128)(2,1)S(1)}, bf16[1,256,256]{2,1,0:T(8,128)(2,1)S(1)}, u32[]{:S(2)}, u32[]{:S(2)}) collective-permute-start(bf16[1,256,256]{2,1,0:T(8,128)(2,1)S(1)} %fusion), channel_id=1, source_target_pairs={{0,16},{1,17},{2,18},{3,19},{4,20},{5,21},{6,22},{7,23},{8,24},{9,... | collective-permute-start | bytes 393224 | tf_op jit(solution)/shard_map/ppermute | solution.py:325
  61.8 7.4 %collective-permute-done.4 = bf16[1,256,256]{2,1,0:T(8,128)(2,1)S(1)} collective-permute-done((bf16[1,256,256]{2,1,0:T(8,128)(2,1)S(1)}, bf16[1,256,256]{2,1,0:T(8,128)(2,1)S(1)}, u32[]{:S(2)}, u32[]{:S(2)}) %collective-permute-start.4) | collective-permute-done | bytes 131104 | tf_op jit(solution)/shard_map/ppermute | solution.py:329
  69.3 2.7 %collective-permute-done.8 = bf16[1,256,256]{2,1,0:T(8,128)(2,1)S(1)} collective-permute-done((bf16[1,256,256]{2,1,0:T(8,128)(2,1)S(1)}, bf16[1,256,256]{2,1,0:T(8,128)(2,1)S(1)}, u32[]{:S(2)}, u32[]{:S(2)}) %collective-permute-start.8) | collective-permute-done | bytes 131104 | tf_op jit(solution)/shard_map/ppermute | solution.py:325
  72.0 10.0 %moved_keys.2.refs_3_ = f32[152,2048]{1,0:T(8,128)S(1)} custom-call(bf16[128,2048]{1,0:T(8,128)(2,1)S(1)} %bitcast.27, bf16[256,256]{1,0:T(8,128)(2,1)S(1)} %copy-done.6, bf16[32,64,256]{2,1,0:T(8,128)(2,1)S(1)} %all-to-all-done.refs_2_, s32[1]{0:T(128)S(6)} %copy.15.refs_3_, bf16[512,256]{1,0:T(8,128)(2,1)S(1)} %copy-done.5), custom_call_target="tpu_custom_call" | custom-call | flops 8858370048 | bytes 1441792 | tf_op jit(solution)/shard_map/moved_keys/pallas_call | solution.py:438
  82.1 1.0 copy-done.7
  83.1 2.8 %all-to-all-start.1 = ((bf16[32,64,256]{2,1,0:T(8,128)(2,1)}), bf16[32,64,256]{2,1,0:T(8,128)(2,1)S(1)}, u32[]{:S(2)}, u32[]{:S(2)}) async-start(bf16[32,64,256]{2,1,0:T(8,128)(2,1)} %get-tuple-element.27), calls=%async_computation.1 | async-start | bytes 2097152 | tf_op jit(solution)/shard_map/all_to_all | solution.py:432
  85.9 1.5 collective-permute-start.13
  87.5 1.5 collective-permute-start.9
  89.0 1.5 collective-permute-start.11
  90.5 12.5 %collective-permute-done.13.refs_2_ = bf16[2,256,256]{2,1,0:T(8,128)(2,1)S(1)} collective-permute-done((bf16[2,256,256]{2,1,0:T(8,128)(2,1)S(1)}, bf16[2,256,256]{2,1,0:T(8,128)(2,1)S(1)}, u32[]{:S(2)}, u32[]{:S(2)}) %collective-permute-start.13) | collective-permute-done | bytes 262176 | tf_op jit(solution)/shard_map/ppermute | solution.py:348
  103.0 0.8 collective-permute-start.14
  103.8 1.2 collective-permute-start.10
  105.0 5.1 %collective-permute-done.11.refs_3_ = bf16[2,256,256]{2,1,0:T(8,128)(2,1)S(1)} collective-permute-done((bf16[2,256,256]{2,1,0:T(8,128)(2,1)S(1)}, bf16[2,256,256]{2,1,0:T(8,128)(2,1)S(1)}, u32[]{:S(2)}, u32[]{:S(2)}) %collective-permute-start.11) | collective-permute-done | bytes 262176 | tf_op jit(solution)/shard_map/ppermute | solution.py:348
  110.1 1.8 %collective-permute-start.12 = (bf16[2,256,256]{2,1,0:T(8,128)(2,1)S(1)}, bf16[2,256,256]{2,1,0:T(8,128)(2,1)}, u32[]{:S(2)}, u32[]{:S(2)}) collective-permute-start(bf16[2,256,256]{2,1,0:T(8,128)(2,1)S(1)} %collective-permute-done.11.refs_3_), channel_id=1, source_target_pairs={{0,2},{1,3},{2,0},{3,1},{4,6},{5,7},{6,4},{7,5},{8,10},{9,11},{10,... | collective-permute-start | bytes 786440 | tf_op jit(solution)/shard_map/ppermute | solution.py:348
  111.9 4.7 %collective-permute-done.14.refs_2_ = bf16[2,256,256]{2,1,0:T(8,128)(2,1)S(1)} collective-permute-done((bf16[2,256,256]{2,1,0:T(8,128)(2,1)S(1)}, bf16[2,256,256]{2,1,0:T(8,128)(2,1)S(1)}, u32[]{:S(2)}, u32[]{:S(2)}) %collective-permute-start.14) | collective-permute-done | bytes 262176 | tf_op jit(solution)/shard_map/ppermute | solution.py:348
  116.6 1.5 collective-permute-start.15
  118.1 0.6 fusion.5
  118.8 1.9 %compare_select_fusion.which_ref = s32[2]{0:T(128)S(1)} fusion(s32[1]{0:T(128)} %get-tuple-element.32, s32[1]{0:T(128)} %get-tuple-element.31, s32[]{:T(128)} %fusion.3), kind=kLoop, calls=%fused_computation.12 | loop fusion | flops 12 | bytes 20 | tf_op jit(solution)/shard_map/jit(_where)/select_n | solution.py:332
  120.7 0.6 pick_other.3
  121.4 3.3 %collective-permute-done.15.refs_3_ = bf16[2,256,256]{2,1,0:T(8,128)(2,1)} collective-permute-done((bf16[2,256,256]{2,1,0:T(8,128)(2,1)S(1)}, bf16[2,256,256]{2,1,0:T(8,128)(2,1)}, u32[]{:S(2)}, u32[]{:S(2)}) %collective-permute-start.15) | collective-permute-done | bytes 262176 | tf_op jit(solution)/shard_map/ppermute | solution.py:348
  124.7 0.9 copy-done.1
  125.6 1.6 %pick_other.2 = bf16[1024,256]{1,0:T(8,128)(2,1)S(1)} custom-call(s32[2]{0:T(128)S(1)} %compare_select_fusion.which_ref, bf16[2,256,256]{2,1,0:T(8,128)(2,1)} %collective-permute-done.10.refs_0_, bf16[2,256,256]{2,1,0:T(8,128)(2,1)} %collective-permute-done.12.refs_1_, bf16[2,256,256]{2,1,0:T(8,128)(2,1)S(1)} %copy-done.1, ...), custom_call_target="tpu_custom_call" | custom-call | tf_op jit(solution)/shard_map/pick_other/pallas_call | solution.py:356
  127.4 1.3 copy-done.8
  128.6 7.9 %moved_keys.3.refs_5_ = f32[152,2048]{1,0:T(8,128)S(1)} custom-call(bf16[128,2048]{1,0:T(8,128)(2,1)S(1)} %bitcast.28, bf16[256,256]{1,0:T(8,128)(2,1)S(1)} %copy-done.6, bf16[32,64,256]{2,1,0:T(8,128)(2,1)S(1)} %all-to-all-done.1.refs_2_, f32[152,2048]{1,0:T(8,128)S(1)} %copy-done.8), custom_call_target="tpu_custom_call" | custom-call | flops 6442450944 | bytes 1048576 | tf_op jit(solution)/shard_map/moved_keys/pallas_call | solution.py:438
  136.5 9.0 %prefix_keys.2.refs_5_ = f32[152,2048]{1,0:T(8,128)S(1)} custom-call(s32[2]{0:T(128)S(1)} %compare_select_fusion.which_ref, bf16[128,2048]{1,0:T(8,128)(2,1)S(1)} %bitcast.29, bf16[2,256,256]{2,1,0:T(8,128)(2,1)S(1)} %pad_maximum_fusion.refs_0_, bf16[2,256,256]{2,1,0:T(8,128)(2,1)S(1)} %collective-permute-done.9.refs_1_, ...), custom_call_target="tpu_custom_call" | custom-call | flops 6442450944 | bytes 1048576 | tf_op jit(solution)/shard_map/prefix_keys/pallas_call | solution.py:466
  145.6 9.9 %prefix_keys.3 = bf16[256,1024]{1,0:T(8,128)(2,1)} custom-call(s32[2]{0:T(128)S(1)} %compare_select_fusion.which_ref, bf16[128,2048]{1,0:T(8,128)(2,1)S(1)} %bitcast.30, bf16[2,256,256]{2,1,0:T(8,128)(2,1)} %collective-permute-done.10.refs_0_, bf16[2,256,256]{2,1,0:T(8,128)(2,1)} %collective-permute-done.12.refs_1_, bf16[2,256,256]{2,1,0:T(8,128)(2,1)S(1)} %copy-done.2, ...), custom_call_target="tpu_custom_call" | custom-call | flops 6442450944 | bytes 1048576 | tf_op jit(solution)/shard_map/prefix_keys/pallas_call | solution.py:466
  (50 shorter events, 1.1 us)
Async XLA Ops:
  0.0 10.3 %collective-permute-start = (bf16[4096,256]{1,0:T(8,128)(2,1)}, bf16[4096,256]{1,0:T(8,128)(2,1)S(1)}, u32[]{:S(2)}, u32[]{:S(2)}) collective-permute-start(bf16[4096,256]{1,0:T(8,128)(2,1)} %param.15), channel_id=1, source_target_pairs={{0,1},{1,0},{2,3},{3,2},{4,5},{5,4},{6,7},{7,6},{8,9},{9,8},{10,11... | collective-permute-start | bytes 6291464 | tf_op jit(solution)/shard_map/ppermute | solution.py:336
  10.3 1.4 copy-start.9
  15.1 10.7 %copy-start.12 = (bf16[4,1,256,256]{3,2,1,0:T(8,128)(2,1)S(1)}, bf16[4,1,256,256]{3,2,1,0:T(8,128)(2,1)}, u32[]{:S(2)}) copy-start(bf16[4,1,256,256]{3,2,1,0:T(8,128)(2,1)} %get-tuple-element.21) | copy-start | bytes 1572868
  15.1 10.7 %collective-permute-start.1 = (bf16[4,1,256,256]{3,2,1,0:T(8,128)(2,1)}, bf16[4,1,256,256]{3,2,1,0:T(8,128)(2,1)}, u32[]{:S(2)}, u32[]{:S(2)}) collective-permute-start(bf16[4,1,256,256]{3,2,1,0:T(8,128)(2,1)} %get-tuple-element.20), channel_id=1, source_target_pairs={{30,28},{31,29}} | collective-permute-start | bytes 1572872 | tf_op jit(solution)/shard_map/ppermute | solution.py:313
  16.8 21.5 %collective-permute-start.5 = (bf16[4,1,256,256]{3,2,1,0:T(8,128)(2,1)}, bf16[4,1,256,256]{3,2,1,0:T(8,128)(2,1)}, u32[]{:S(2)}, u32[]{:S(2)}) collective-permute-start(bf16[4,1,256,256]{3,2,1,0:T(8,128)(2,1)} %get-tuple-element.22), channel_id=1, source_target_pairs={{0,4},{1,5},{2,6},{3,7},{4,0},{5,1},{6,2},{7,3},{8,12},{9,13},{10,... | collective-permute-start | bytes 1572872 | tf_op jit(solution)/shard_map/ppermute | solution.py:313
  19.2 19.1 %copy-start.11 = (bf16[4,1,256,256]{3,2,1,0:T(8,128)(2,1)S(1)}, bf16[4,1,256,256]{3,2,1,0:T(8,128)(2,1)}, u32[]{:S(2)}) copy-start(bf16[4,1,256,256]{3,2,1,0:T(8,128)(2,1)} %get-tuple-element.23) | copy-start | bytes 1572868
  19.2 52.8 %all-to-all-start = ((bf16[32,64,256]{2,1,0:T(8,128)(2,1)}), bf16[32,64,256]{2,1,0:T(8,128)(2,1)S(1)}, u32[]{:S(2)}, u32[]{:S(2)}) async-start(bf16[32,64,256]{2,1,0:T(8,128)(2,1)} %get-tuple-element.24), calls=%async_computation | async-start | bytes 2097152 | tf_op jit(solution)/shard_map/all_to_all | solution.py:432
  25.9 13.8 %copy-start.10 = (bf16[256,1024]{1,0:T(8,128)(2,1)S(1)}, bf16[256,1024]{1,0:T(8,128)(2,1)}, u32[]{:S(2)}) copy-start(bf16[256,1024]{1,0:T(8,128)(2,1)} %param.11) | copy-start | bytes 1572868
  27.1 15.8 %collective-permute-start.2 = (bf16[2,1,256,256]{3,2,1,0:T(8,128)(2,1)S(1)}, bf16[2,1,256,256]{3,2,1,0:T(8,128)(2,1)}, u32[]{:S(2)}, u32[]{:S(2)}) collective-permute-start(bf16[2,1,256,256]{3,2,1,0:T(8,128)(2,1)S(1)} %slice.44), channel_id=1, source_target_pairs={{28,24},{29,25},{30,26},{31,27}} | collective-permute-start | bytes 786440 | tf_op jit(solution)/shard_map/ppermute | solution.py:313
  39.0 11.8 %collective-permute-start.6 = (bf16[2,1,256,256]{3,2,1,0:T(8,128)(2,1)}, bf16[2,1,256,256]{3,2,1,0:T(8,128)(2,1)}, u32[]{:S(2)}, u32[]{:S(2)}) collective-permute-start(bf16[2,1,256,256]{3,2,1,0:T(8,128)(2,1)} %slice.48), channel_id=1, source_target_pairs={{0,8},{1,9},{2,10},{3,11},{4,12},{5,13},{6,14},{7,15},{8,0},{9,1},... | collective-permute-start | bytes 786440 | tf_op jit(solution)/shard_map/ppermute | solution.py:313
  42.9 29.1 %copy-start.5 = (bf16[512,256]{1,0:T(8,128)(2,1)S(1)}, bf16[512,256]{1,0:T(8,128)(2,1)}, u32[]{:S(2)}) copy-start(bf16[512,256]{1,0:T(8,128)(2,1)} %refs_4_.1) | copy-start | bytes 786436
  43.0 29.1 %copy-start.6 = (bf16[256,256]{1,0:T(8,128)(2,1)S(1)}, bf16[256,256]{1,0:T(8,128)(2,1)}, u32[]{:S(2)}) copy-start(bf16[256,256]{1,0:T(8,128)(2,1)} %refs_1_.3) | copy-start | bytes 393220
  44.0 10.1 %collective-permute-start.3 = (bf16[1,1,256,256]{3,2,1,0:T(8,128)(2,1)S(1)}, bf16[1,1,256,256]{3,2,1,0:T(8,128)(2,1)S(1)}, u32[]{:S(2)}, u32[]{:S(2)}) collective-permute-start(bf16[1,1,256,256]{3,2,1,0:T(8,128)(2,1)S(1)} %slice.46), channel_id=1, source_target_pairs={{24,16},{25,17},{26,18},{27,19},{28,20},{29,21},{30,22},{31,23}} | collective-permute-start | bytes 393224 | tf_op jit(solution)/shard_map/ppermute | solution.py:313
  50.9 6.2 %collective-permute-start.7 = (bf16[1,1,256,256]{3,2,1,0:T(8,128)(2,1)S(1)}, bf16[1,1,256,256]{3,2,1,0:T(8,128)(2,1)S(1)}, u32[]{:S(2)}, u32[]{:S(2)}) collective-permute-start(bf16[1,1,256,256]{3,2,1,0:T(8,128)(2,1)S(1)} %slice.50), channel_id=1, source_target_pairs={{0,2},{1,3},{2,0},{3,1},{4,6},{5,7},{6,4},{7,5},{8,10},{9,11},{10,... | collective-permute-start | bytes 393224 | tf_op jit(solution)/shard_map/ppermute | solution.py:313
  54.2 15.1 %collective-permute-start.4 = (bf16[1,256,256]{2,1,0:T(8,128)(2,1)S(1)}, bf16[1,256,256]{2,1,0:T(8,128)(2,1)S(1)}, u32[]{:S(2)}, u32[]{:S(2)}) collective-permute-start(bf16[1,256,256]{2,1,0:T(8,128)(2,1)S(1)} %fusion.1), channel_id=1, source_target_pairs={{16,0},{17,1},{18,2},{19,3},{20,4},{21,5},{22,6},{23,7},{24,8},{25... | collective-permute-start | bytes 393224 | tf_op jit(solution)/shard_map/ppermute | solution.py:329
  57.1 14.9 %collective-permute-start.8 = (bf16[1,256,256]{2,1,0:T(8,128)(2,1)S(1)}, bf16[1,256,256]{2,1,0:T(8,128)(2,1)S(1)}, u32[]{:S(2)}, u32[]{:S(2)}) collective-permute-start(bf16[1,256,256]{2,1,0:T(8,128)(2,1)S(1)} %fusion), channel_id=1, source_target_pairs={{0,16},{1,17},{2,18},{3,19},{4,20},{5,21},{6,22},{7,23},{8,24},{9,... | collective-permute-start | bytes 393224 | tf_op jit(solution)/shard_map/ppermute | solution.py:325
  82.1 1.1 copy-start.7
  82.1 36.1 %copy-start.13 = (s32[32]{0:T(128)S(1)}, s32[32]{0:T(128)}, u32[]{:S(2)}) copy-start(s32[32]{0:T(128)} %param.17) | copy-start | bytes 388
  83.1 44.2 %all-to-all-start.1 = ((bf16[32,64,256]{2,1,0:T(8,128)(2,1)}), bf16[32,64,256]{2,1,0:T(8,128)(2,1)S(1)}, u32[]{:S(2)}, u32[]{:S(2)}) async-start(bf16[32,64,256]{2,1,0:T(8,128)(2,1)} %get-tuple-element.27), calls=%async_computation.1 | async-start | bytes 2097152 | tf_op jit(solution)/shard_map/all_to_all | solution.py:432
  85.9 17.0 %collective-permute-start.13 = (bf16[2,256,256]{2,1,0:T(8,128)(2,1)S(1)}, bf16[2,256,256]{2,1,0:T(8,128)(2,1)S(1)}, u32[]{:S(2)}, u32[]{:S(2)}) collective-permute-start(bf16[2,256,256]{2,1,0:T(8,128)(2,1)S(1)} %pad_maximum_fusion.refs_0_), channel_id=1, source_target_pairs={{0,4},{1,5},{2,6},{3,7},{4,0},{5,1},{6,2},{7,3},{8,12},{9,13},{10,... | collective-permute-start | bytes 786440 | tf_op jit(solution)/shard_map/ppermute | solution.py:348
  87.5 16.3 %collective-permute-start.9 = (bf16[2,256,256]{2,1,0:T(8,128)(2,1)S(1)}, bf16[2,256,256]{2,1,0:T(8,128)(2,1)S(1)}, u32[]{:S(2)}, u32[]{:S(2)}) collective-permute-start(bf16[2,256,256]{2,1,0:T(8,128)(2,1)S(1)} %pad_maximum_fusion.refs_0_), channel_id=1, source_target_pairs={{0,2},{1,3},{2,0},{3,1},{4,6},{5,7},{6,4},{7,5},{8,10},{9,11},{10,... | collective-permute-start | bytes 786440 | tf_op jit(solution)/shard_map/ppermute | solution.py:348
  89.0 21.1 %collective-permute-start.11 = (bf16[2,256,256]{2,1,0:T(8,128)(2,1)S(1)}, bf16[2,256,256]{2,1,0:T(8,128)(2,1)S(1)}, u32[]{:S(2)}, u32[]{:S(2)}) collective-permute-start(bf16[2,256,256]{2,1,0:T(8,128)(2,1)S(1)} %pad_maximum_fusion.refs_0_), channel_id=1, source_target_pairs={{0,8},{1,9},{2,10},{3,11},{4,12},{5,13},{6,14},{7,15},{8,0},{9,1},... | collective-permute-start | bytes 786440 | tf_op jit(solution)/shard_map/ppermute | solution.py:348
  103.0 13.7 %collective-permute-start.14 = (bf16[2,256,256]{2,1,0:T(8,128)(2,1)S(1)}, bf16[2,256,256]{2,1,0:T(8,128)(2,1)S(1)}, u32[]{:S(2)}, u32[]{:S(2)}) collective-permute-start(bf16[2,256,256]{2,1,0:T(8,128)(2,1)S(1)} %collective-permute-done.13.refs_2_), channel_id=1, source_target_pairs={{0,8},{1,9},{2,10},{3,11},{4,12},{5,13},{6,14},{7,15},{8,0},{9,1},... | collective-permute-start | bytes 786440 | tf_op jit(solution)/shard_map/ppermute | solution.py:348
  103.8 17.5 %collective-permute-start.10 = (bf16[2,256,256]{2,1,0:T(8,128)(2,1)S(1)}, bf16[2,256,256]{2,1,0:T(8,128)(2,1)}, u32[]{:S(2)}, u32[]{:S(2)}) collective-permute-start(bf16[2,256,256]{2,1,0:T(8,128)(2,1)S(1)} %collective-permute-done.9.refs_1_), channel_id=1, source_target_pairs={{0,4},{1,5},{2,6},{3,7},{4,0},{5,1},{6,2},{7,3},{8,12},{9,13},{10,... | collective-permute-start | bytes 786440 | tf_op jit(solution)/shard_map/ppermute | solution.py:348
  110.1 11.3 %copy-start.3 = (bf16[2,256,256]{2,1,0:T(8,128)(2,1)}, bf16[2,256,256]{2,1,0:T(8,128)(2,1)S(1)}, u32[]{:S(2)}) copy-start(bf16[2,256,256]{2,1,0:T(8,128)(2,1)S(1)} %collective-permute-done.11.refs_3_) | copy-start | bytes 786436
  110.1 11.3 %collective-permute-start.12 = (bf16[2,256,256]{2,1,0:T(8,128)(2,1)S(1)}, bf16[2,256,256]{2,1,0:T(8,128)(2,1)}, u32[]{:S(2)}, u32[]{:S(2)}) collective-permute-start(bf16[2,256,256]{2,1,0:T(8,128)(2,1)S(1)} %collective-permute-done.11.refs_3_), channel_id=1, source_target_pairs={{0,2},{1,3},{2,0},{3,1},{4,6},{5,7},{6,4},{7,5},{8,10},{9,11},{10,... | collective-permute-start | bytes 786440 | tf_op jit(solution)/shard_map/ppermute | solution.py:348
  116.6 4.8 %copy-start = (bf16[2,256,256]{2,1,0:T(8,128)(2,1)}, bf16[2,256,256]{2,1,0:T(8,128)(2,1)S(1)}, u32[]{:S(2)}) copy-start(bf16[2,256,256]{2,1,0:T(8,128)(2,1)S(1)} %collective-permute-done.14.refs_2_) | copy-start | bytes 786436
  116.6 8.1 %collective-permute-start.15 = (bf16[2,256,256]{2,1,0:T(8,128)(2,1)S(1)}, bf16[2,256,256]{2,1,0:T(8,128)(2,1)}, u32[]{:S(2)}, u32[]{:S(2)}) collective-permute-start(bf16[2,256,256]{2,1,0:T(8,128)(2,1)S(1)} %collective-permute-done.14.refs_2_), channel_id=1, source_target_pairs={{0,2},{1,3},{2,0},{3,1},{4,6},{5,7},{6,4},{7,5},{8,10},{9,11},{10,... | collective-permute-start | bytes 786440 | tf_op jit(solution)/shard_map/ppermute | solution.py:348
  121.3 15.3 %collective-permute-start.17 = (bf16[1024,256]{1,0:T(8,128)(2,1)S(1)}, bf16[1024,256]{1,0:T(8,128)(2,1)}, u32[]{:S(2)}, u32[]{:S(2)}) collective-permute-start(bf16[1024,256]{1,0:T(8,128)(2,1)S(1)} %pick_other.3), channel_id=1, source_target_pairs={{0,1},{1,0},{2,3},{3,2},{4,5},{5,4},{6,7},{7,6},{8,9},{9,8},{10,11... | collective-permute-start | bytes 1572872 | tf_op jit(solution)/shard_map/ppermute | solution.py:336
  124.7 1.0 copy-start.1
  127.3 18.3 %collective-permute-start.16 = (bf16[1024,256]{1,0:T(8,128)(2,1)S(1)}, bf16[1024,256]{1,0:T(8,128)(2,1)}, u32[]{:S(2)}, u32[]{:S(2)}) collective-permute-start(bf16[1024,256]{1,0:T(8,128)(2,1)S(1)} %pick_other.2), channel_id=1, source_target_pairs={{0,1},{1,0},{2,3},{3,2},{4,5},{5,4},{6,7},{7,6},{8,9},{9,8},{10,11... | collective-permute-start | bytes 1572872 | tf_op jit(solution)/shard_map/ppermute | solution.py:336
  127.3 1.3 copy-start.8
  128.6 7.9 %copy-start.4 = (bf16[2,256,256]{2,1,0:T(8,128)(2,1)S(1)}, bf16[2,256,256]{2,1,0:T(8,128)(2,1)}, u32[]{:S(2)}) copy-start(bf16[2,256,256]{2,1,0:T(8,128)(2,1)} %copy-done.3) | copy-start | bytes 786436
  136.5 9.1 %copy-start.2 = (bf16[2,256,256]{2,1,0:T(8,128)(2,1)S(1)}, bf16[2,256,256]{2,1,0:T(8,128)(2,1)}, u32[]{:S(2)}) copy-start(bf16[2,256,256]{2,1,0:T(8,128)(2,1)} %copy-done) | copy-start | bytes 786436

commit v9 on v7

v9 whole, which is shorter than its diff:
```python
import functools

import jax
import jax.numpy as jnp
from jax import lax
from jax.experimental import pallas as pl
from jax.experimental.pallas import tpu as pltpu
from jax.sharding import PartitionSpec as P

LOG2E = 1.4426950408889634
DEAD_MARK = 1024.0
DEAD_ABOVE = 512.0
NEG = -1e30
CHUNK = 2048
PARAMS = pltpu.CompilerParams(vmem_limit_bytes=62 * 1024 * 1024)

IN_SMEM = pl.BlockSpec(memory_space=pltpu.SMEM)
IN_HBM = pl.BlockSpec(memory_space=pltpu.HBM)


def fold_keys(q_ref, max_ref, sums_ref, keys, values, factor, mask=None):
    heads, tokens, width = sums_ref.shape
    size = keys.shape[1]

    def score(head):
        scores = lax.dot_general(
            q_ref[:, head * size:(head + 1) * size],
            keys,
            (((1,), (1,)), ((), ())),
            preferred_element_type=jnp.float32,
        )
        return scores if mask is None else jnp.where(mask, scores, NEG)

    following = score(0)
    for head in range(heads):
        scores, following = following, score(head + 1) if head + 1 < heads else None
        old_max = max_ref[head]
        new_max = jnp.maximum(old_max, jnp.max(scores, axis=1, keepdims=True))
        shrink = jnp.exp2((old_max - new_max) * factor)
        weights = jnp.exp2((scores - jnp.tile(new_max, (1, keys.shape[0] // size))) * factor)
        max_ref[head] = new_max
        sums_ref[head] = sums_ref[head] * jnp.tile(shrink, (1, width // size)) + jnp.dot(
            weights.astype(jnp.bfloat16), values, preferred_element_type=jnp.float32
        )


def finish(sums_ref, out_ref):
    heads, tokens, width = sums_ref.shape
    size = width // 2
    for head in range(heads):
        out_ref[:, head * size:(head + 1) * size] = (
            sums_ref[head, :, :size] / sums_ref[head, :, size:]
        ).astype(out_ref.dtype)


def stage_rows(rows, place, keys_ref, values_ref):
    size = keys_ref.shape[1]
    here = pl.ds(place, rows.shape[0])
    keys_ref[here, :] = rows[:, :size]
    values_ref[here, :size] = rows[:, size:]
    values_ref[here, size:] = jnp.ones((rows.shape[0], size), jnp.bfloat16)


def stage_live(rows, live, suffix_ref, keys_ref, values_ref):
    size = suffix_ref.shape[1] // 2
    count = rows.shape[0]
    zeros = jnp.zeros((count, size), jnp.float32)
    spare = jnp.broadcast_to(suffix_ref[:1, :size].astype(jnp.float32), zeros.shape)
    keys_ref[:count, :] = jnp.where(live, rows[:, :size], spare).astype(jnp.bfloat16)
    values_ref[:count, :size] = jnp.where(live, rows[:, size:], zeros).astype(jnp.bfloat16)
    values_ref[:count, size:] = jnp.where(live, 1.0, zeros).astype(jnp.bfloat16)


def start_all(copies):
    for copy in copies:
        copy.start()


def wait_all(copies):
    for copy in copies:
        copy.wait()


def state_copies(state_here, state_there, sems):
    return [
        pltpu.make_async_copy(source, target, sems.at[place])
        for place, (source, target) in enumerate(zip(state_here, state_there))
    ]


def fold_local(
    factor, len_ref, q_ref, suffix_ref, own_ref, max_ref, sums_ref, keys_ref, values_ref
):
    size = suffix_ref.shape[1] // 2
    suffix = suffix_ref.shape[0]
    own = own_ref.shape[0]
    max_ref[...] = jnp.full(max_ref.shape, NEG, jnp.float32)
    sums_ref[...] = jnp.zeros(sums_ref.shape, jnp.float32)
    stage_rows(suffix_ref[...], 0, keys_ref, values_ref)
    causal = lax.broadcasted_iota(jnp.int32, (suffix, suffix), 1) <= lax.broadcasted_iota(
        jnp.int32, (suffix, suffix), 0
    )
    fold_keys(
        q_ref, max_ref, sums_ref, keys_ref[:suffix, :], values_ref[:suffix, :], factor, causal
    )
    live = lax.broadcasted_iota(jnp.int32, (own, size), 0) < len_ref[0]
    stage_live(own_ref[...].astype(jnp.float32), live, suffix_ref, keys_ref, values_ref)
    fold_keys(q_ref, max_ref, sums_ref, keys_ref[:own, :], values_ref[:own, :], factor)


def moved_kernel(factor, local, steps, *refs):
    q_ref, suffix_ref, kv_ref = refs[:3]
    state_out = refs[-7:-5]
    max_ref, sums_ref, keys_ref, values_ref, sems = refs[-5:]
    step = pl.program_id(0)

    if local:

        @pl.when(step == 0)
        def _():
            fold_local(factor, refs[3], q_ref, suffix_ref, refs[4], *refs[-5:-1])

    else:
        loads = state_copies(refs[3:5], (max_ref, sums_ref), sems)
        pl.when(step == 0)(lambda: start_all(loads))

    rows = kv_ref[...].reshape(-1, kv_ref.shape[-1]).astype(jnp.float32)
    count, size = rows.shape[0], rows.shape[1] // 2
    live = jnp.broadcast_to(rows[:, size:size + 1] < DEAD_ABOVE, (count, size))
    stage_live(rows, live, suffix_ref, keys_ref, values_ref)
    if not local:
        pl.when(step == 0)(lambda: wait_all(loads))
    fold_keys(q_ref, max_ref, sums_ref, keys_ref[:count, :], values_ref[:count, :], factor)

    @pl.when(step == steps - 1)
    def _():
        saves = state_copies((max_ref, sums_ref), state_out, sems)
        start_all(saves)
        wait_all(saves)


def prefix_kernel(factor, last, count, steps, which_ref, q_ref, *refs):
    pieces, refs = refs[:count], refs[count:]
    max_ref, sums_ref, keys_ref, values_ref, sems = refs[-5:]
    step = pl.program_id(0)
    chunk = keys_ref.shape[0] // steps

    @pl.when(step == 0)
    def _():
        loads = state_copies(refs[:2], (max_ref, sums_ref), sems)
        start_all(loads)
        place = 0
        for piece in pieces:
            stage_rows(piece[...], place, keys_ref, values_ref)
            place += piece.shape[0]
        wait_all(loads)

    rows = pl.ds(pl.multiple_of(step * chunk, keys_ref.shape[1]), chunk)
    fold_keys(q_ref, max_ref, sums_ref, keys_ref[rows, :], values_ref[rows, :], factor)

    @pl.when(step == steps - 1)
    def _():
        if last:
            finish(sums_ref, refs[2])
        else:
            saves = state_copies((max_ref, sums_ref), refs[2:4], sems)
            start_all(saves)
            wait_all(saves)


def pick_kernel(which_ref, *refs):
    pieces, out_ref = refs[:-1], refs[-1]
    for place, piece in enumerate(pieces):
        out_ref[pl.ds(place * piece.shape[0], piece.shape[0]), :] = piece[...]


def pack_kernel(target_ref, block_ref, count_ref, pool_ref, *refs):
    parts = refs[:-4]
    held_ref, mark_ref, in_sems, out_sems = refs[-4:]
    entries = target_ref.shape[1]
    mark_ref[...] = jnp.full(mark_ref.shape, DEAD_MARK, mark_ref.dtype)

    def load(entry):
        return pltpu.make_async_copy(
            pool_ref.at[block_ref[0, entry]], held_ref.at[entry], in_sems.at[entry]
        )

    def stores(entry, source):
        copies = []
        first = 0
        for place, part in enumerate(parts):
            rows = part.shape[1]
            copies.append(
                pltpu.make_async_copy(
                    source.at[pl.ds(first, rows)],
                    part.at[target_ref[0, entry]],
                    out_sems.at[place, entry],
                )
            )
            first += rows
        return copies

    @pl.loop(0, entries)
    def _(entry):
        live = entry < count_ref[0]
        pl.when(live)(lambda: load(entry).start())
        pl.when(jnp.logical_not(live))(lambda: start_all(stores(entry, mark_ref)))

    @pl.loop(0, entries)
    def _(entry):
        @pl.when(entry < count_ref[0])
        def _():
            load(entry).wait()
            start_all(stores(entry, held_ref.at[entry]))

    @pl.loop(0, entries)
    def _(entry):
        wait_all(stores(entry, mark_ref))


def placed(step, order):
    return sum((step >> bit & 1) << (len(order) - 1 - rank) for rank, bit in enumerate(order))


def stage_kernel(order, owner_ref, place_ref, kept_ref, swapped_ref, *refs):
    outs, (sought_ref, known_ref, in_sems, out_sems) = refs[:-4], refs[-4:]
    core, chip, is_last = place_ref[0], place_ref[1], place_ref[2]
    chips, sought = sought_ref.shape[:2]

    def load(source, step, prefix):
        if prefix < sought:
            target = sought_ref.at[step, prefix]
        else:
            target = known_ref.at[placed(step, order), 0]
        return pltpu.make_async_copy(source.at[core, chip ^ step], target, in_sems.at[step, prefix])

    def start(step, prefix, here):
        pl.when(here)(lambda: load(kept_ref, step, prefix).start())
        pl.when(jnp.logical_not(here))(lambda: load(swapped_ref, step, prefix).start())

    def store(place):
        half = chips // 2
        if place < chips:
            source = sought_ref.at[place]
        else:
            source = known_ref.at[pl.ds((chips + 1 - place) * half, half)]
        return pltpu.make_async_copy(source, outs[place], out_sems.at[place])

    for step in range(chips):
        for prefix in range(sought):
            start(step, prefix, owner_ref[prefix] % 2 == core)

    @pl.when(is_last == 1)
    def _():
        for step in range(chips):
            start(step, sought, core == 1)

    for step in range(chips):
        for prefix in range(sought):
            load(kept_ref, step, prefix).wait()
        store(step).start()

    @pl.when(is_last == 1)
    def _():
        for step in range(chips):
            load(kept_ref, step, sought).wait()

    store(chips).start()
    store(chips + 1).start()
    wait_all([store(place) for place in range(chips + 2)])


def multicast(prefix_cache, owners, readers, outgoing):
    replicas = lax.axis_size("replica")
    me = lax.axis_index("replica")
    half = replicas // 2
    chips = half // 2
    bits = chips.bit_length() - 1
    chip = me // 2 % chips
    side = me // half
    width = prefix_cache.shape[1]
    ids = jnp.arange(owners.shape[0], dtype=jnp.int32)
    known = jnp.sum(jnp.where(owners == replicas - 1, ids, 0))
    sought = jnp.where(ids[:-1] >= known, owners[1:], owners[:-1])
    order = [*range(bits)]

    split = prefix_cache.reshape(2, chips, -1, width)
    swapped, *outgoing = lax.optimization_barrier((swap_cores(prefix_cache), *outgoing))
    swapped = swapped.reshape(split.shape)
    rows = split.shape[2]
    pieces = jax.ShapeDtypeStruct((owners.shape[0] - 1, rows, width), split.dtype)
    share = jax.ShapeDtypeStruct((chips // 2, 1, rows, width), split.dtype)
    staged = pl.pallas_call(
        functools.partial(stage_kernel, order),
        out_shape=(pieces,) * chips + (share,) * 2,
        in_specs=[IN_SMEM] * 2 + [IN_HBM] * 2,
        out_specs=(IN_HBM,) * (chips + 2),
        scratch_shapes=[
            pltpu.VMEM((chips, *pieces.shape), split.dtype),
            pltpu.VMEM((chips, *share.shape[1:]), split.dtype),
            pltpu.SemaphoreType.DMA((chips, owners.shape[0])),
            pltpu.SemaphoreType.DMA((chips + 2,)),
        ],
        compiler_params=PARAMS,
        name="stage_prefix",
    )(
        sought,
        jnp.stack([me % 2, chip, (me // 2 == replicas // 2 - 1).astype(jnp.int32)]),
        split,
        swapped,
    )

    away = chip ^ (sought // 2 % chips)
    found = staged[0]
    for step in range(chips - 1, 0, -1):
        passed = lax.ppermute(
            staged[step], "replica", [(i, i ^ (2 * step)) for i in range(replicas)]
        )
        found = jnp.where((away == step)[:, None, None], passed, found)
    passed = lax.ppermute(found, "replica", [(i, (i + half) % replicas) for i in range(replicas)])
    held = jnp.where((sought // half == side)[:, None, None], found, passed)

    sent, kept = staged[chips:]
    for rank, bit in enumerate(order):
        senders = [
            i for i in range(half, replicas) if all(i // 2 >> ahead & 1 for ahead in order[rank:])
        ]
        passed = lax.ppermute(sent, "replica", [(i, i ^ (2 << bit)) for i in senders])
        kept = jnp.where(chip >> bit & 1 == 1, kept, passed)
        left = kept.shape[0] // 2
        if left:
            kept, sent = kept[:left], kept[left:]
    passed = lax.ppermute(kept[0], "replica", [(i + half, i) for i in range(half)])
    held = jnp.concatenate([jnp.where(side == 1, kept[0], passed), held])
    wanted = jnp.stack([readers[me], readers[me ^ 1]])
    return held, jnp.where(wanted == known, 0, wanted + (wanted < known)), outgoing


def swap_cores(rows):
    return lax.ppermute(rows, "replica", [(i, i ^ 1) for i in range(lax.axis_size("replica"))])


def gather_step(gathered, step):
    replicas = lax.axis_size("replica")
    bits = (replicas // 4).bit_length() - 1
    members = [bit for bit in range(bits) if step >> bit & 1]
    linked = [bit for bit in members if step >> ((bit - 1) % bits) & 1]
    last = min(linked or members)
    pairs = [(i, i ^ (2 << last)) for i in range(replicas)]
    return lax.ppermute(gathered[step ^ 1 << last], "replica", pairs)


def from_other(pieces, place):
    rows, width = pieces[0].shape[1:]
    spec = pl.BlockSpec((None, rows, width), lambda i, which: (which[1], 0, 0))
    picked = pl.pallas_call(
        pick_kernel,
        out_shape=jax.ShapeDtypeStruct((len(pieces) * rows, width), pieces[0].dtype),
        grid_spec=pltpu.PrefetchScalarGridSpec(
            num_scalar_prefetch=1,
            grid=(1,),
            in_specs=[spec] * len(pieces),
            out_specs=pl.BlockSpec((len(pieces) * rows, width), lambda i, which: (0, 0)),
        ),
        compiler_params=PARAMS,
        name="pick_other",
    )(place, *pieces)
    return swap_cores(picked)


def whole(shape):
    return pl.BlockSpec(shape, lambda *args: (0,) * len(shape))


def cost(rows, keys, size):
    return pl.CostEstimate(
        flops=12 * rows * keys * size, bytes_accessed=4 * keys * size, transcendentals=rows * keys
    )


def on_device(
    queries,
    suffix_kv,
    own_cache,
    ctx_len,
    prefix_cache,
    owners,
    readers,
    kv_pool,
    mig_target,
    mig_block,
    mig_count,
):
    replicas = lax.axis_size("replica")
    size = suffix_kv.shape[1] // 2
    tokens = queries.shape[0]
    heads = queries.shape[1] // size
    factor = size ** (-0.5) * LOG2E
    row_count = tokens * heads
    state = (
        jax.ShapeDtypeStruct((heads, tokens, size), jnp.float32),
        jax.ShapeDtypeStruct((heads, tokens, 2 * size), jnp.float32),
    )

    def scratch(keys):
        return [
            *[pltpu.VMEM(part.shape, part.dtype) for part in state],
            pltpu.VMEM((keys, size), jnp.bfloat16),
            pltpu.VMEM((keys, 2 * size), jnp.bfloat16),
            pltpu.SemaphoreType.DMA((2,)),
        ]

    entries = mig_target.shape[1]
    block = kv_pool.shape[1]
    early = block * 3 // 4
    parts = tuple(
        jax.ShapeDtypeStruct((replicas, rows, kv_pool.shape[2]), kv_pool.dtype)
        for rows in (early, block - early)
    )
    outgoing = pl.pallas_call(
        pack_kernel,
        out_shape=parts,
        in_specs=[IN_SMEM] * 3 + [IN_HBM],
        out_specs=(IN_HBM,) * len(parts),
        scratch_shapes=[
            pltpu.VMEM((entries, *kv_pool.shape[1:]), kv_pool.dtype),
            pltpu.VMEM(kv_pool.shape[1:], kv_pool.dtype),
            pltpu.SemaphoreType.DMA((entries,)),
            pltpu.SemaphoreType.DMA((len(parts), entries)),
        ],
        compiler_params=PARAMS,
        name="pack_moved",
    )(mig_target, mig_block, mig_count, kv_pool)
    held, place, outgoing = multicast(prefix_cache, owners, readers, outgoing)

    def fold_moved(part, state_now):
        arrived = lax.all_to_all(part, "replica", split_axis=0, concat_axis=0, tiled=True)
        local = state_now is None
        rows = part.shape[1]
        group = max(n for n in range(1, replicas + 1) if replicas % n == 0 and n * rows <= CHUNK)
        steps = replicas // group
        most = max(group * rows, own_cache.shape[0], tokens) if local else group * rows
        keys = replicas * rows + (tokens + own_cache.shape[0]) * local
        return pl.pallas_call(
            functools.partial(moved_kernel, factor, local, steps),
            out_shape=state,
            grid=(steps,),
            in_specs=[
                whole(queries.shape),
                whole(suffix_kv.shape),
                pl.BlockSpec((group, rows, 2 * size), lambda i: (i, 0, 0)),
                *([IN_SMEM, whole(own_cache.shape)] if local else [IN_HBM] * 2),
            ],
            out_specs=(IN_HBM,) * 2,
            scratch_shapes=scratch(most),
            compiler_params=PARAMS,
            cost_estimate=cost(row_count, keys, size),
            name="moved_keys",
        )(queries, suffix_kv, arrived, *((ctx_len, own_cache) if local else state_now))

    def fold_prefix(pieces, state_now, last):
        others = from_other(pieces, place)
        rows = pieces[0].shape[1]
        keys = 2 * len(pieces) * rows
        steps = max(1, keys // CHUNK)
        while keys % (steps * size):
            steps -= 1
        return pl.pallas_call(
            functools.partial(prefix_kernel, factor, last, len(pieces) + 1, steps),
            out_shape=jax.ShapeDtypeStruct(queries.shape, queries.dtype) if last else state,
            grid_spec=pltpu.PrefetchScalarGridSpec(
                num_scalar_prefetch=1,
                grid=(steps,),
                in_specs=[
                    whole(queries.shape),
                    *[pl.BlockSpec((None, rows, 2 * size), lambda i, which: (which[0], 0, 0))]
                    * len(pieces),
                    whole(others.shape),
                    IN_HBM,
                    IN_HBM,
                ],
                out_specs=whole(queries.shape) if last else (IN_HBM, IN_HBM),
                scratch_shapes=scratch(keys),
            ),
            compiler_params=PARAMS,
            cost_estimate=cost(row_count, keys, size),
            name="prefix_keys",
        )(place, queries, *pieces, others, *state_now)

    state_now = fold_moved(outgoing[0], None)
    held, *later = lax.optimization_barrier((held, *outgoing[1:]))
    chips = replicas // 4
    gathered = {0: held}
    for step in (step for step in range(1, chips) if step.bit_count() == 1):
        gathered[step] = gather_step(gathered, step)
    state_now = fold_prefix(list(gathered.values()), state_now, False)
    late = sorted(
        (step for step in range(1, chips) if step.bit_count() > 1),
        key=lambda step: (step.bit_count(), step),
    )
    for step in late:
        if step == late[-1]:
            source, *state_now = lax.optimization_barrier((gathered, *state_now))
        else:
            source = gathered
        gathered[step] = gather_step(source, step)
    for part in later:
        state_now = fold_moved(part, state_now)
    return fold_prefix([gathered[step] for step in late], state_now, True)


def solution(mesh):
    in_specs = (
        P(("groups", "replica"), None),
        P(("groups", "replica"), None),
        P(("groups", "replica"), None),
        P(("groups", "replica")),
        P(("groups", "replica"), None),
        P("groups"),
        P("groups"),
        P(("groups", "replica"), None, None),
        P(("groups", "replica"), None),
        P(("groups", "replica"), None),
        P(("groups", "replica")),
    )
    out_specs = P(("groups", "replica"), None)
    return jax.shard_map(
        on_device, mesh=mesh, in_specs=in_specs, out_specs=out_specs, check_vma=False
    )
```

time: 149 us -> 152 us (1.020)
  Pallas kernels: 38.9 us -> 53.9 us
  waiting for transfers between devices: 47.4 us -> 37.9 us
  local copies, waits for them, and re-layouts: 8.42 us -> 3.82 us
  starting transfers between devices: 43.6 us -> 47.6 us
  between operations: 7.09 us -> 3.74 us
  other arithmetic: 2.4 us -> 3.99 us
    ppermute x24 -> x18, waiting for transfers between devices: 46.5 us -> 31.4 us  [the longest x7 22.1 us: multicast(): lax.ppermute(staged[step], 'replica', [(i, i ^ 2 * step) for i in range(r...]
    pallas_call x6 -> x8, Pallas kernels: 38.9 us -> 53.9 us  [the longest x2 21 us: fold_moved(): pl.pallas_call(functools.partial(moved_kernel, factor, local, steps), out...]
    ppermute x1, starting transfers between devices: 3.12 us -> 12.6 us  [multicast(): lax.ppermute(found, 'replica', [(i, (i + half) % replicas) for i in range...]
    ppermute x1, waiting for transfers between devices: 0.89 us -> 6.47 us  [multicast(): lax.ppermute(found, 'replica', [(i, (i + half) % replicas) for i in range...]
    all_to_all x2, starting transfers between devices: 15.2 us -> 10.3 us  [fold_moved(): lax.all_to_all(part, 'replica', split_axis=0, concat_axis=0, tiled=True)]
    unnamed x30 -> x28, local copies, waits for them, and re-layouts: 6.6 us -> 2.57 us
    select_n x5, other arithmetic: 1.08 us -> 2.67 us  [the longest x1 2.49 us: multicast(): jnp.where(wanted == known, 0, wanted + (wanted < known))]
    ppermute x24 -> x18, starting transfers between devices: 22.5 us -> 22.6 us  [the longest x7 13 us: multicast(): lax.ppermute(staged[step], 'replica', [(i, i ^ 2 * step) for i in range(r...]
  transfers between devices with their start and end apart: 30 -> 24, of which waited for: 8 -> 9; matrix products, arithmetic and copies ran while one was open for 3% -> 3% of each run, Pallas kernels for 21% -> 29%
where the time goes in v9:
time: 152 us; the launch traced here: 151 us
  Pallas kernels  53.9 us (35%)
  starting transfers between devices  47.6 us (31%)
  waiting for transfers between devices  37.9 us (25%)
  other arithmetic  3.99 us (3%)
  local copies, waits for them, and re-layouts  3.82 us (3%)
  between operations  3.74 us (2%)
    ppermute x7, waiting for transfers between devices, multicast(): lax.ppermute(staged[step], 'replica', [(i, i ^ 2 * step) for i in range(r...  22.1 us
    pallas_call x2, Pallas kernels, fold_moved(): pl.pallas_call(functools.partial(moved_kernel, factor, local, steps), out...  21 us
    pallas_call x2, Pallas kernels, fold_prefix(): pl.pallas_call(functools.partial(prefix_kernel, factor, last, len(pieces)...  20.6 us
    ppermute x7, starting transfers between devices, multicast(): lax.ppermute(staged[step], 'replica', [(i, i ^ 2 * step) for i in range(r...  13 us
    ppermute x1, starting transfers between devices, multicast(): lax.ppermute(found, 'replica', [(i, (i + half) % replicas) for i in range...  12.6 us
    all_to_all x2, starting transfers between devices, fold_moved(): lax.all_to_all(part, 'replica', split_axis=0, concat_axis=0, tiled=True)  10.3 us
    ppermute x7, waiting for transfers between devices, gather_step(): return lax.ppermute(gathered[step ^ 1 << last], 'replica', pairs)  7.97 us
    ppermute x7, starting transfers between devices, gather_step(): return lax.ppermute(gathered[step ^ 1 << last], 'replica', pairs)  7.82 us
  transfers between devices with their start and end apart: 24, of which 9 were waited for; matrix products, arithmetic and copies ran while one was open for 3% of the time, Pallas kernels for 29%

profile of v9, /device:TPU:0, one launch (start us, length us, event | category | flops | bytes accessed | tf_op | source)
XLA Modules:
  0.0 150.9 jit_solution(13022262016350396299)
XLA Ops:
  0.0 0.5 collective-permute-start
  1.1 3.9 %pack_moved.1 = (bf16[32,96,256]{2,1,0:T(8,128)(2,1)}, bf16[32,32,256]{2,1,0:T(8,128)(2,1)}) custom-call(s32[1,32]{1,0:T(1,128)} %target_ref.1, s32[1,32]{1,0:T(1,128)} %block_ref.1, s32[1]{0:T(128)S(6)} %copy.13.count_ref, bf16[32,128,256]{2,1,0:T(8,128)(2,1)} %pool_ref.1), custom_call_target="tpu_custom_call" | custom-call | tf_op jit(solution)/shard_map/pack_moved/pallas_call | solution.py:420
  5.0 6.9 %all-to-all-start = ((bf16[32,96,256]{2,1,0:T(8,128)(2,1)}), bf16[32,96,256]{2,1,0:T(8,128)(2,1)S(1)}, u32[]{:S(2)}, u32[]{:S(2)}) async-start(bf16[32,96,256]{2,1,0:T(8,128)(2,1)} %get-tuple-element.46), calls=%async_computation | async-start | bytes 3145728 | tf_op jit(solution)/shard_map/all_to_all | solution.py:437
  12.0 0.6 fusion.2
  13.3 0.6 fusion.3
  15.2 0.6 pad_add_fusion.place_ref
  15.8 3.2 %stage_prefix.1 = (bf16[1,256,256]{2,1,0:T(8,128)(2,1)}, bf16[1,256,256]{2,1,0:T(8,128)(2,1)}, bf16[1,256,256]{2,1,0:T(8,128)(2,1)}, bf16[1,256,256]{2,1,0:T(8,1...) custom-call(s32[1]{0:T(128)S(6)} %select_n.118.owner_ref, ...), custom_call_target="tpu_custom_call" | custom-call | tf_op jit(solution)/shard_map/stage_prefix/pallas_call | solution.py:293
  19.1 0.8 collective-permute-start.1
  19.9 0.1 broadcast_select_fusion
  20.0 0.7 collective-permute-start.2
  20.7 2.7 %collective-permute-start.10 = (bf16[1,256,256]{2,1,0:T(8,128)(2,1)}, bf16[1,256,256]{2,1,0:T(8,128)(2,1)S(1)}, u32[]{:S(2)}, u32[]{:S(2)}) collective-permute-start(bf16[1,256,256]{2,1,0:T(8,128)(2,1)} %get-tuple-element.41), channel_id=1, source_target_pairs={{0,12},{1,13},{2,14},{3,15},{4,8},{5,9},{6,10},{7,11},{8,4},{9,5},... | collective-permute-start | bytes 393224 | tf_op jit(solution)/shard_map/ppermute | solution.py:316
  23.4 2.5 %collective-permute-start.11 = (bf16[1,256,256]{2,1,0:T(8,128)(2,1)}, bf16[1,256,256]{2,1,0:T(8,128)(2,1)S(1)}, u32[]{:S(2)}, u32[]{:S(2)}) collective-permute-start(bf16[1,256,256]{2,1,0:T(8,128)(2,1)} %get-tuple-element.42), channel_id=1, source_target_pairs={{0,14},{1,15},{2,12},{3,13},{4,10},{5,11},{6,8},{7,9},{8,6},{9,7},... | collective-permute-start | bytes 393224 | tf_op jit(solution)/shard_map/ppermute | solution.py:316
  25.9 1.5 collective-permute-start.6
  27.4 14.6 %collective-permute-done.10 = bf16[1,256,256]{2,1,0:T(8,128)(2,1)S(1)} collective-permute-done((bf16[1,256,256]{2,1,0:T(8,128)(2,1)}, bf16[1,256,256]{2,1,0:T(8,128)(2,1)S(1)}, u32[]{:S(2)}, u32[]{:S(2)}) %collective-permute-start.10) | collective-permute-done | bytes 131104 | tf_op jit(solution)/shard_map/ppermute | solution.py:316
  42.0 2.0 %collective-permute-start.7 = (bf16[1,256,256]{2,1,0:T(8,128)(2,1)S(1)}, bf16[1,256,256]{2,1,0:T(8,128)(2,1)S(1)}, u32[]{:S(2)}, u32[]{:S(2)}) collective-permute-start(bf16[1,256,256]{2,1,0:T(8,128)(2,1)S(1)} %copy-done.12), channel_id=1, source_target_pairs={{0,6},{1,7},{2,4},{3,5},{4,2},{5,3},{6,0},{7,1},{8,14},{9,15},{10,... | collective-permute-start | bytes 393224 | tf_op jit(solution)/shard_map/ppermute | solution.py:316
  44.0 1.2 collective-permute-done.11
  45.2 3.9 %collective-permute-start.8 = (bf16[1,256,256]{2,1,0:T(8,128)(2,1)S(1)}, bf16[1,256,256]{2,1,0:T(8,128)(2,1)S(1)}, u32[]{:S(2)}, u32[]{:S(2)}) collective-permute-start(bf16[1,256,256]{2,1,0:T(8,128)(2,1)S(1)} %copy-done.11), channel_id=1, source_target_pairs={{0,8},{1,9},{2,10},{3,11},{4,12},{5,13},{6,14},{7,15},{8,0},{9,1},... | collective-permute-start | bytes 393224 | tf_op jit(solution)/shard_map/ppermute | solution.py:316
  49.2 0.4 collective-permute-start.9
  49.6 0.7 collective-permute-start.3
  50.3 3.2 %collective-permute-done.8 = bf16[1,256,256]{2,1,0:T(8,128)(2,1)S(1)} collective-permute-done((bf16[1,256,256]{2,1,0:T(8,128)(2,1)S(1)}, bf16[1,256,256]{2,1,0:T(8,128)(2,1)S(1)}, u32[]{:S(2)}, u32[]{:S(2)}) %collective-permute-start.8) | collective-permute-done | bytes 131104 | tf_op jit(solution)/shard_map/ppermute | solution.py:316
  53.5 3.1 %collective-permute-done.9 = bf16[1,256,256]{2,1,0:T(8,128)(2,1)S(1)} collective-permute-done((bf16[1,256,256]{2,1,0:T(8,128)(2,1)S(1)}, bf16[1,256,256]{2,1,0:T(8,128)(2,1)S(1)}, u32[]{:S(2)}, u32[]{:S(2)}) %collective-permute-start.9) | collective-permute-done | bytes 131104 | tf_op jit(solution)/shard_map/ppermute | solution.py:316
  56.6 0.1 select_select_fusion
  56.6 12.6 %collective-permute-start.12 = (bf16[1,256,256]{2,1,0:T(8,128)(2,1)S(1)}, bf16[1,256,256]{2,1,0:T(8,128)(2,1)S(1)}, u32[]{:S(2)}, u32[]{:S(2)}) collective-permute-start(bf16[1,256,256]{2,1,0:T(8,128)(2,1)S(1)} %select_select_fusion), channel_id=1, source_target_pairs={{0,16},{1,17},{2,18},{3,19},{4,20},{5,21},{6,22},{7,23},{8,24},{9,... | collective-permute-start | bytes 393224 | tf_op jit(solution)/shard_map/ppermute | solution.py:320
  69.2 1.3 collective-permute-start.4
  70.5 6.5 %collective-permute-done.12 = bf16[1,256,256]{2,1,0:T(8,128)(2,1)S(1)} collective-permute-done((bf16[1,256,256]{2,1,0:T(8,128)(2,1)S(1)}, bf16[1,256,256]{2,1,0:T(8,128)(2,1)S(1)}, u32[]{:S(2)}, u32[]{:S(2)}) %collective-permute-start.12) | collective-permute-done | bytes 131104 | tf_op jit(solution)/shard_map/ppermute | solution.py:320
  77.0 1.4 collective-permute-done.4
  78.5 0.9 collective-permute-start.13
  79.3 1.6 %collective-permute-start.17 = (bf16[2,256,256]{2,1,0:T(8,128)(2,1)S(1)}, bf16[2,256,256]{2,1,0:T(8,128)(2,1)}, u32[]{:S(2)}, u32[]{:S(2)}) collective-permute-start(bf16[2,256,256]{2,1,0:T(8,128)(2,1)S(1)} %pad_maximum_fusion.refs_0_), channel_id=1, source_target_pairs={{0,4},{1,5},{2,6},{3,7},{4,0},{5,1},{6,2},{7,3},{8,12},{9,13},{10,... | collective-permute-start | bytes 786440 | tf_op jit(solution)/shard_map/ppermute | solution.py:350
  81.6 0.6 fusion.4
  82.2 2.5 %compare_select_fusion.which_ref = s32[2]{0:T(128)} fusion(s32[1]{0:T(128)} %get-tuple-element.60, s32[1]{0:T(128)} %get-tuple-element.59, s32[]{:T(128)} %fusion.2), kind=kLoop, calls=%fused_computation.9 | loop fusion | flops 12 | bytes 20 | tf_op jit(solution)/shard_map/jit(_where)/select_n | solution.py:336
  84.7 0.7 collective-permute-done.13.refs_1_
  85.4 0.4 collective-permute-done.15.refs_3_
  85.8 0.3 copy-done.2
  86.1 0.7 copy-done.3
  86.8 2.6 %pick_other.2 = bf16[1024,256]{1,0:T(8,128)(2,1)} custom-call(s32[2]{0:T(128)} %compare_select_fusion.which_ref, bf16[2,256,256]{2,1,0:T(8,128)(2,1)} %copy-done.1, bf16[2,256,256]{2,1,0:T(8,128)(2,1)} %copy-done.2, bf16[2,256,256]{2,1,0:T(8,128)(2,1)} %collective-permute-done.17.refs_2_, bf16[2,256,256]{2,1,0:T(8,128)(2,1)} %copy-done.3), custom_call_target="tpu_custom_call" | custom-call | tf_op jit(solution)/shard_map/pick_other/pallas_call | solution.py:356
  89.4 1.8 %collective-permute-start.14 = (bf16[2,256,256]{2,1,0:T(8,128)(2,1)}, bf16[2,256,256]{2,1,0:T(8,128)(2,1)S(1)}, u32[]{:S(2)}, u32[]{:S(2)}) collective-permute-start(bf16[2,256,256]{2,1,0:T(8,128)(2,1)} %copy-done.2), channel_id=1, source_target_pairs={{0,4},{1,5},{2,6},{3,7},{4,0},{5,1},{6,2},{7,3},{8,12},{9,13},{10,... | collective-permute-start | bytes 786440 | tf_op jit(solution)/shard_map/ppermute | solution.py:350
  91.2 1.0 collective-permute-start.16
  92.2 0.9 collective-permute-start.18
  93.1 3.3 %all-to-all-start.1 = ((bf16[32,32,256]{2,1,0:T(8,128)(2,1)}), bf16[32,32,256]{2,1,0:T(8,128)(2,1)}, u32[]{:S(2)}, u32[]{:S(2)}) async-start(bf16[32,32,256]{2,1,0:T(8,128)(2,1)} %get-tuple-element.52), calls=%async_computation.1 | async-start | bytes 1048576 | tf_op jit(solution)/shard_map/all_to_all | solution.py:437
  96.5 13.6 %moved_keys.2 = (f32[8,256,128]{2,1,0:T(8,128)}, f32[8,256,256]{2,1,0:T(8,128)}) custom-call(bf16[256,1024]{1,0:T(8,128)(2,1)} %q_ref.3, bf16[256,256]{1,0:T(8,128)(2,1)} %refs_1_.3, bf16[32,96,256]{2,1,0:T(8,128)(2,1)} %copy-done, s32[1]{0:T(128)S(6)} %copy.12.refs_3_, bf16[512,256]{1,0:T(8,128)(2,1)} %refs_4_.1), custom_call_target="tpu_custom_call" | custom-call | flops 12079595520 | bytes 1966080 | tf_op jit(solution)/shard_map/moved_keys/pallas_call | solution.py:444
  110.1 10.6 %prefix_keys.2 = (f32[8,256,128]{2,1,0:T(8,128)}, f32[8,256,256]{2,1,0:T(8,128)}) custom-call(s32[2]{0:T(128)} %compare_select_fusion.which_ref, bf16[256,1024]{1,0:T(8,128)(2,1)} %q_ref.3, bf16[2,256,256]{2,1,0:T(8,128)(2,1)} %copy-done.1, bf16[2,256,256]{2,1,0:T(8,128)(2,1)} %copy-done.2, bf16[2,256,256]{2,1,0:T(8,128)(2,1)} %collective-permute-done.17.refs_2_, ...), custom_call_target="tpu_custom_call" | custom-call | flops 6442450944 | bytes 1048576 | tf_op jit(solution)/shard_map/prefix_keys/pallas_call | solution.py:468
  120.7 1.6 %collective-permute-start.20 = (bf16[2,256,256]{2,1,0:T(8,128)(2,1)}, bf16[2,256,256]{2,1,0:T(8,128)(2,1)S(1)}, u32[]{:S(2)}, u32[]{:S(2)}) collective-permute-start(bf16[2,256,256]{2,1,0:T(8,128)(2,1)} %collective-permute-done.18.refs_2_), channel_id=1, source_target_pairs={{0,2},{1,3},{2,0},{3,1},{4,6},{5,7},{6,4},{7,5},{8,10},{9,11},{10,... | collective-permute-start | bytes 786440 | tf_op jit(solution)/shard_map/ppermute | solution.py:350
  122.4 6.9 %collective-permute-done.20.refs_3_ = bf16[2,256,256]{2,1,0:T(8,128)(2,1)S(1)} collective-permute-done((bf16[2,256,256]{2,1,0:T(8,128)(2,1)}, bf16[2,256,256]{2,1,0:T(8,128)(2,1)S(1)}, u32[]{:S(2)}, u32[]{:S(2)}) %collective-permute-start.20) | collective-permute-done | bytes 262176 | tf_op jit(solution)/shard_map/ppermute | solution.py:350
  129.3 0.7 copy-done.5
  130.0 2.6 %pick_other.3 = bf16[1024,256]{1,0:T(8,128)(2,1)} custom-call(s32[2]{0:T(128)} %compare_select_fusion.which_ref, bf16[2,256,256]{2,1,0:T(8,128)(2,1)} %copy-done.4, bf16[2,256,256]{2,1,0:T(8,128)(2,1)} %collective-permute-done.16.refs_1_, bf16[2,256,256]{2,1,0:T(8,128)(2,1)} %collective-permute-done.18.refs_2_, bf16[2,256,256]{2,1,0:T(8,128)(2,1)} %copy-done.5), custom_call_target="tpu_custom_call" | custom-call | tf_op jit(solution)/shard_map/pick_other/pallas_call | solution.py:356
  132.6 7.3 %moved_keys.3 = (f32[8,256,128]{2,1,0:T(8,128)}, f32[8,256,256]{2,1,0:T(8,128)}) custom-call(bf16[256,1024]{1,0:T(8,128)(2,1)} %q_ref.3, bf16[256,256]{1,0:T(8,128)(2,1)} %refs_1_.3, bf16[32,32,256]{2,1,0:T(8,128)(2,1)} %all-to-all-done.1.refs_2_, f32[8,256,128]{2,1,0:T(8,128)} %get-tuple-element.53.refs_3_, f32[8,256,256]{2,1,0:T(8,128)} %get-tuple-element.54.refs_4_), custom_call_target="tpu_custom_call" | custom-call | flops 3221225472 | bytes 524288 | tf_op jit(solution)/shard_map/moved_keys/pallas_call | solution.py:444
  139.9 0.8 copy-done.9
  140.7 10.0 %prefix_keys.3 = bf16[256,1024]{1,0:T(8,128)(2,1)} custom-call(s32[2]{0:T(128)} %compare_select_fusion.which_ref, bf16[256,1024]{1,0:T(8,128)(2,1)} %q_ref.3, bf16[2,256,256]{2,1,0:T(8,128)(2,1)} %copy-done.4, bf16[2,256,256]{2,1,0:T(8,128)(2,1)} %collective-permute-done.16.refs_1_, bf16[2,256,256]{2,1,0:T(8,128)(2,1)} %collective-permute-done.18.refs_2_, ...), custom_call_target="tpu_custom_call" | custom-call | flops 6442450944 | bytes 1048576 | tf_op jit(solution)/shard_map/prefix_keys/pallas_call | solution.py:468
  (51 shorter events, 0.2 us)
Async XLA Ops:
  0.0 5.0 %collective-permute-start = (bf16[4096,256]{1,0:T(8,128)(2,1)}, bf16[4096,256]{1,0:T(8,128)(2,1)}, u32[]{:S(2)}, u32[]{:S(2)}) collective-permute-start(bf16[4096,256]{1,0:T(8,128)(2,1)} %param.15), channel_id=1, source_target_pairs={{0,1},{1,0},{2,3},{3,2},{4,5},{5,4},{6,7},{7,6},{8,9},{9,8},{10,11... | collective-permute-start | bytes 6291464 | tf_op jit(solution)/shard_map/ppermute | solution.py:340
  5.0 7.0 %copy-start.8 = (s32[2]{0:T(128)S(1)}, s32[2]{0:T(128)}, u32[]{:S(2)}) copy-start(s32[2]{0:T(128)} %param.16) | copy-start | bytes 28
  5.0 88.1 %all-to-all-start = ((bf16[32,96,256]{2,1,0:T(8,128)(2,1)}), bf16[32,96,256]{2,1,0:T(8,128)(2,1)S(1)}, u32[]{:S(2)}, u32[]{:S(2)}) async-start(bf16[32,96,256]{2,1,0:T(8,128)(2,1)} %get-tuple-element.46), calls=%async_computation | async-start | bytes 3145728 | tf_op jit(solution)/shard_map/all_to_all | solution.py:437
  19.0 6.9 %copy-start.13 = (bf16[1,256,256]{2,1,0:T(8,128)(2,1)S(1)}, bf16[1,256,256]{2,1,0:T(8,128)(2,1)}, u32[]{:S(2)}) copy-start(bf16[1,256,256]{2,1,0:T(8,128)(2,1)} %get-tuple-element.37) | copy-start | bytes 393220
  19.0 22.9 %copy-start.12 = (bf16[1,256,256]{2,1,0:T(8,128)(2,1)S(1)}, bf16[1,256,256]{2,1,0:T(8,128)(2,1)}, u32[]{:S(2)}) copy-start(bf16[1,256,256]{2,1,0:T(8,128)(2,1)} %get-tuple-element.38) | copy-start | bytes 393220
  19.0 26.2 %copy-start.11 = (bf16[1,256,256]{2,1,0:T(8,128)(2,1)S(1)}, bf16[1,256,256]{2,1,0:T(8,128)(2,1)}, u32[]{:S(2)}) copy-start(bf16[1,256,256]{2,1,0:T(8,128)(2,1)} %get-tuple-element.39) | copy-start | bytes 393220
  19.0 30.1 %copy-start.10 = (bf16[1,256,256]{2,1,0:T(8,128)(2,1)S(1)}, bf16[1,256,256]{2,1,0:T(8,128)(2,1)}, u32[]{:S(2)}) copy-start(bf16[1,256,256]{2,1,0:T(8,128)(2,1)} %get-tuple-element.40) | copy-start | bytes 393220
  19.1 37.5 %copy-start.6 = (bf16[1,256,256]{2,1,0:T(8,128)(2,1)S(1)}, bf16[1,256,256]{2,1,0:T(8,128)(2,1)}, u32[]{:S(2)}) copy-start(bf16[1,256,256]{2,1,0:T(8,128)(2,1)} %get-tuple-element.43) | copy-start | bytes 393220
  19.1 0.8 collective-permute-start.1
  20.0 61.6 %copy-start.7 = (s32[32]{0:T(128)S(1)}, s32[32]{0:T(128)}, u32[]{:S(2)}) copy-start(s32[32]{0:T(128)} %param.17) | copy-start | bytes 388
  20.0 29.1 %collective-permute-start.2 = (bf16[2,1,256,256]{3,2,1,0:T(8,128)(2,1)S(1)}, bf16[2,1,256,256]{3,2,1,0:T(8,128)(2,1)S(1)}, u32[]{:S(2)}, u32[]{:S(2)}) collective-permute-start(bf16[2,1,256,256]{3,2,1,0:T(8,128)(2,1)S(1)} %slice.29), channel_id=1, source_target_pairs={{28,24},{29,25},{30,26},{31,27}} | collective-permute-start | bytes 786440 | tf_op jit(solution)/shard_map/ppermute | solution.py:328
  20.7 21.3 %collective-permute-start.10 = (bf16[1,256,256]{2,1,0:T(8,128)(2,1)}, bf16[1,256,256]{2,1,0:T(8,128)(2,1)S(1)}, u32[]{:S(2)}, u32[]{:S(2)}) collective-permute-start(bf16[1,256,256]{2,1,0:T(8,128)(2,1)} %get-tuple-element.41), channel_id=1, source_target_pairs={{0,12},{1,13},{2,14},{3,15},{4,8},{5,9},{6,10},{7,11},{8,4},{9,5},... | collective-permute-start | bytes 393224 | tf_op jit(solution)/shard_map/ppermute | solution.py:316
  23.4 21.8 %collective-permute-start.11 = (bf16[1,256,256]{2,1,0:T(8,128)(2,1)}, bf16[1,256,256]{2,1,0:T(8,128)(2,1)S(1)}, u32[]{:S(2)}, u32[]{:S(2)}) collective-permute-start(bf16[1,256,256]{2,1,0:T(8,128)(2,1)} %get-tuple-element.42), channel_id=1, source_target_pairs={{0,14},{1,15},{2,12},{3,13},{4,10},{5,11},{6,8},{7,9},{8,6},{9,7},... | collective-permute-start | bytes 393224 | tf_op jit(solution)/shard_map/ppermute | solution.py:316
  25.9 23.6 %collective-permute-start.5 = (bf16[1,256,256]{2,1,0:T(8,128)(2,1)}, bf16[1,256,256]{2,1,0:T(8,128)(2,1)S(1)}, u32[]{:S(2)}, u32[]{:S(2)}) collective-permute-start(bf16[1,256,256]{2,1,0:T(8,128)(2,1)} %get-tuple-element.36), channel_id=1, source_target_pairs={{0,2},{1,3},{2,0},{3,1},{4,6},{5,7},{6,4},{7,5},{8,10},{9,11},{10,... | collective-permute-start | bytes 393224 | tf_op jit(solution)/shard_map/ppermute | solution.py:316
  25.9 24.3 %collective-permute-start.6 = (bf16[1,256,256]{2,1,0:T(8,128)(2,1)S(1)}, bf16[1,256,256]{2,1,0:T(8,128)(2,1)S(1)}, u32[]{:S(2)}, u32[]{:S(2)}) collective-permute-start(bf16[1,256,256]{2,1,0:T(8,128)(2,1)S(1)} %copy-done.13), channel_id=1, source_target_pairs={{0,4},{1,5},{2,6},{3,7},{4,0},{5,1},{6,2},{7,3},{8,12},{9,13},{10,... | collective-permute-start | bytes 393224 | tf_op jit(solution)/shard_map/ppermute | solution.py:316
  42.0 8.3 %collective-permute-start.7 = (bf16[1,256,256]{2,1,0:T(8,128)(2,1)S(1)}, bf16[1,256,256]{2,1,0:T(8,128)(2,1)S(1)}, u32[]{:S(2)}, u32[]{:S(2)}) collective-permute-start(bf16[1,256,256]{2,1,0:T(8,128)(2,1)S(1)} %copy-done.12), channel_id=1, source_target_pairs={{0,6},{1,7},{2,4},{3,5},{4,2},{5,3},{6,0},{7,1},{8,14},{9,15},{10,... | collective-permute-start | bytes 393224 | tf_op jit(solution)/shard_map/ppermute | solution.py:316
  45.2 8.3 %collective-permute-start.8 = (bf16[1,256,256]{2,1,0:T(8,128)(2,1)S(1)}, bf16[1,256,256]{2,1,0:T(8,128)(2,1)S(1)}, u32[]{:S(2)}, u32[]{:S(2)}) collective-permute-start(bf16[1,256,256]{2,1,0:T(8,128)(2,1)S(1)} %copy-done.11), channel_id=1, source_target_pairs={{0,8},{1,9},{2,10},{3,11},{4,12},{5,13},{6,14},{7,15},{8,0},{9,1},... | collective-permute-start | bytes 393224 | tf_op jit(solution)/shard_map/ppermute | solution.py:316
  49.2 7.4 %collective-permute-start.9 = (bf16[1,256,256]{2,1,0:T(8,128)(2,1)S(1)}, bf16[1,256,256]{2,1,0:T(8,128)(2,1)S(1)}, u32[]{:S(2)}, u32[]{:S(2)}) collective-permute-start(bf16[1,256,256]{2,1,0:T(8,128)(2,1)S(1)} %copy-done.10), channel_id=1, source_target_pairs={{0,10},{1,11},{2,8},{3,9},{4,14},{5,15},{6,12},{7,13},{8,2},{9,3},... | collective-permute-start | bytes 393224 | tf_op jit(solution)/shard_map/ppermute | solution.py:316
  49.6 19.6 %collective-permute-start.3 = (bf16[1,1,256,256]{3,2,1,0:T(8,128)(2,1)S(1)}, bf16[1,1,256,256]{3,2,1,0:T(8,128)(2,1)S(1)}, u32[]{:S(2)}, u32[]{:S(2)}) collective-permute-start(bf16[1,1,256,256]{3,2,1,0:T(8,128)(2,1)S(1)} %slice.31), channel_id=1, source_target_pairs={{24,16},{25,17},{26,18},{27,19},{28,20},{29,21},{30,22},{31,23}} | collective-permute-start | bytes 393224 | tf_op jit(solution)/shard_map/ppermute | solution.py:328
  56.6 20.4 %collective-permute-start.12 = (bf16[1,256,256]{2,1,0:T(8,128)(2,1)S(1)}, bf16[1,256,256]{2,1,0:T(8,128)(2,1)S(1)}, u32[]{:S(2)}, u32[]{:S(2)}) collective-permute-start(bf16[1,256,256]{2,1,0:T(8,128)(2,1)S(1)} %select_select_fusion), channel_id=1, source_target_pairs={{0,16},{1,17},{2,18},{3,19},{4,20},{5,21},{6,22},{7,23},{8,24},{9,... | collective-permute-start | bytes 393224 | tf_op jit(solution)/shard_map/ppermute | solution.py:320
  69.2 9.2 %collective-permute-start.4 = (bf16[1,256,256]{2,1,0:T(8,128)(2,1)S(1)}, bf16[1,256,256]{2,1,0:T(8,128)(2,1)S(1)}, u32[]{:S(2)}, u32[]{:S(2)}) collective-permute-start(bf16[1,256,256]{2,1,0:T(8,128)(2,1)S(1)} %fusion), channel_id=1, source_target_pairs={{16,0},{17,1},{18,2},{19,3},{20,4},{21,5},{22,6},{23,7},{24,8},{25... | collective-permute-start | bytes 393224 | tf_op jit(solution)/shard_map/ppermute | solution.py:333
  78.4 8.4 %copy-start.1 = (bf16[2,256,256]{2,1,0:T(8,128)(2,1)}, bf16[2,256,256]{2,1,0:T(8,128)(2,1)S(1)}, u32[]{:S(2)}) copy-start(bf16[2,256,256]{2,1,0:T(8,128)(2,1)S(1)} %pad_maximum_fusion.refs_0_) | copy-start | bytes 786436
  78.5 6.9 %collective-permute-start.13 = (bf16[2,256,256]{2,1,0:T(8,128)(2,1)S(1)}, bf16[2,256,256]{2,1,0:T(8,128)(2,1)S(1)}, u32[]{:S(2)}, u32[]{:S(2)}) collective-permute-start(bf16[2,256,256]{2,1,0:T(8,128)(2,1)S(1)} %pad_maximum_fusion.refs_0_), channel_id=1, source_target_pairs={{0,2},{1,3},{2,0},{3,1},{4,6},{5,7},{6,4},{7,5},{8,10},{9,11},{10,... | collective-permute-start | bytes 786440 | tf_op jit(solution)/shard_map/ppermute | solution.py:350
  79.3 6.5 %collective-permute-start.15 = (bf16[2,256,256]{2,1,0:T(8,128)(2,1)S(1)}, bf16[2,256,256]{2,1,0:T(8,128)(2,1)S(1)}, u32[]{:S(2)}, u32[]{:S(2)}) collective-permute-start(bf16[2,256,256]{2,1,0:T(8,128)(2,1)S(1)} %pad_maximum_fusion.refs_0_), channel_id=1, source_target_pairs={{0,8},{1,9},{2,10},{3,11},{4,12},{5,13},{6,14},{7,15},{8,0},{9,1},... | collective-permute-start | bytes 786440 | tf_op jit(solution)/shard_map/ppermute | solution.py:350
  79.3 7.5 %collective-permute-start.17 = (bf16[2,256,256]{2,1,0:T(8,128)(2,1)S(1)}, bf16[2,256,256]{2,1,0:T(8,128)(2,1)}, u32[]{:S(2)}, u32[]{:S(2)}) collective-permute-start(bf16[2,256,256]{2,1,0:T(8,128)(2,1)S(1)} %pad_maximum_fusion.refs_0_), channel_id=1, source_target_pairs={{0,4},{1,5},{2,6},{3,7},{4,0},{5,1},{6,2},{7,3},{8,12},{9,13},{10,... | collective-permute-start | bytes 786440 | tf_op jit(solution)/shard_map/ppermute | solution.py:350
  85.4 0.7 copy-start.2
  86.1 0.7 copy-start.3
  89.4 20.7 %collective-permute-start.19 = (bf16[1024,256]{1,0:T(8,128)(2,1)}, bf16[1024,256]{1,0:T(8,128)(2,1)}, u32[]{:S(2)}, u32[]{:S(2)}) collective-permute-start(bf16[1024,256]{1,0:T(8,128)(2,1)} %pick_other.2), channel_id=1, source_target_pairs={{0,1},{1,0},{2,3},{3,2},{4,5},{5,4},{6,7},{7,6},{8,9},{9,8},{10,11... | collective-permute-start | bytes 1572872 | tf_op jit(solution)/shard_map/ppermute | solution.py:340
  89.4 31.3 %collective-permute-start.14 = (bf16[2,256,256]{2,1,0:T(8,128)(2,1)}, bf16[2,256,256]{2,1,0:T(8,128)(2,1)S(1)}, u32[]{:S(2)}, u32[]{:S(2)}) collective-permute-start(bf16[2,256,256]{2,1,0:T(8,128)(2,1)} %copy-done.2), channel_id=1, source_target_pairs={{0,4},{1,5},{2,6},{3,7},{4,0},{5,1},{6,2},{7,3},{8,12},{9,13},{10,... | collective-permute-start | bytes 786440 | tf_op jit(solution)/shard_map/ppermute | solution.py:350
  91.2 29.5 %collective-permute-start.16 = (bf16[2,256,256]{2,1,0:T(8,128)(2,1)}, bf16[2,256,256]{2,1,0:T(8,128)(2,1)}, u32[]{:S(2)}, u32[]{:S(2)}) collective-permute-start(bf16[2,256,256]{2,1,0:T(8,128)(2,1)} %copy-done.3), channel_id=1, source_target_pairs={{0,2},{1,3},{2,0},{3,1},{4,6},{5,7},{6,4},{7,5},{8,10},{9,11},{10,... | collective-permute-start | bytes 786440 | tf_op jit(solution)/shard_map/ppermute | solution.py:350
  92.2 28.5 %collective-permute-start.18 = (bf16[2,256,256]{2,1,0:T(8,128)(2,1)}, bf16[2,256,256]{2,1,0:T(8,128)(2,1)}, u32[]{:S(2)}, u32[]{:S(2)}) collective-permute-start(bf16[2,256,256]{2,1,0:T(8,128)(2,1)} %collective-permute-done.17.refs_2_), channel_id=1, source_target_pairs={{0,8},{1,9},{2,10},{3,11},{4,12},{5,13},{6,14},{7,15},{8,0},{9,1},... | collective-permute-start | bytes 786440 | tf_op jit(solution)/shard_map/ppermute | solution.py:350
  93.1 3.3 %copy-start = (bf16[32,96,256]{2,1,0:T(8,128)(2,1)}, bf16[32,96,256]{2,1,0:T(8,128)(2,1)S(1)}, u32[]{:S(2)}) copy-start(bf16[32,96,256]{2,1,0:T(8,128)(2,1)S(1)} %all-to-all-done.refs_2_) | copy-start | bytes 4718596
  93.1 39.5 %all-to-all-start.1 = ((bf16[32,32,256]{2,1,0:T(8,128)(2,1)}), bf16[32,32,256]{2,1,0:T(8,128)(2,1)}, u32[]{:S(2)}, u32[]{:S(2)}) async-start(bf16[32,32,256]{2,1,0:T(8,128)(2,1)} %get-tuple-element.52), calls=%async_computation.1 | async-start | bytes 1048576 | tf_op jit(solution)/shard_map/all_to_all | solution.py:437
  120.7 8.6 %copy-start.4 = (bf16[2,256,256]{2,1,0:T(8,128)(2,1)}, bf16[2,256,256]{2,1,0:T(8,128)(2,1)S(1)}, u32[]{:S(2)}) copy-start(bf16[2,256,256]{2,1,0:T(8,128)(2,1)S(1)} %collective-permute-done.14.refs_0_) | copy-start | bytes 786436
  120.7 8.5 %collective-permute-start.20 = (bf16[2,256,256]{2,1,0:T(8,128)(2,1)}, bf16[2,256,256]{2,1,0:T(8,128)(2,1)S(1)}, u32[]{:S(2)}, u32[]{:S(2)}) collective-permute-start(bf16[2,256,256]{2,1,0:T(8,128)(2,1)} %collective-permute-done.18.refs_2_), channel_id=1, source_target_pairs={{0,2},{1,3},{2,0},{3,1},{4,6},{5,7},{6,4},{7,5},{8,10},{9,11},{10,... | collective-permute-start | bytes 786440 | tf_op jit(solution)/shard_map/ppermute | solution.py:350
  129.3 0.7 copy-start.5
  132.6 7.3 %collective-permute-start.21 = (bf16[1024,256]{1,0:T(8,128)(2,1)}, bf16[1024,256]{1,0:T(8,128)(2,1)S(1)}, u32[]{:S(2)}, u32[]{:S(2)}) collective-permute-start(bf16[1024,256]{1,0:T(8,128)(2,1)} %pick_other.3), channel_id=1, source_target_pairs={{0,1},{1,0},{2,3},{3,2},{4,5},{5,4},{6,7},{7,6},{8,9},{9,8},{10,11... | collective-permute-start | bytes 1572872 | tf_op jit(solution)/shard_map/ppermute | solution.py:340
  139.9 0.8 copy-start.9

commit v10 on v9

--- a/solution.py
+++ b/solution.py
@@ -11,20 +11,24 @@
 DEAD_MARK = 1024.0
 DEAD_ABOVE = 512.0
 NEG = -1e30
-CHUNK = 2048
-PARAMS = pltpu.CompilerParams(vmem_limit_bytes=62 * 1024 * 1024)
+CHUNK = 1024
+ROWS = 512
+PARAMS = pltpu.CompilerParams(vmem_limit_bytes=44 * 1024 * 1024)
+COPY_PARAMS = pltpu.CompilerParams(vmem_limit_bytes=60 * 1024 * 1024)
 
 IN_SMEM = pl.BlockSpec(memory_space=pltpu.SMEM)
 IN_HBM = pl.BlockSpec(memory_space=pltpu.HBM)
 
 
-def fold_keys(q_ref, max_ref, sums_ref, keys, values, factor, mask=None):
-    heads, tokens, width = sums_ref.shape
+def fold_keys(work, keys, values, factor, mask=None):
+    q_ref, max_ref, sums_ref = work
+    count, width = sums_ref.shape
     size = keys.shape[1]
-
-    def score(head):
+    block = min(ROWS, count)
+
+    def score(first):
         scores = lax.dot_general(
-            q_ref[:, head * size:(head + 1) * size],
+            q_ref[first:first + block, :],
             keys,
             (((1,), (1,)), ((), ())),
             preferred_element_type=jnp.float32,
@@ -32,24 +36,47 @@
         return scores if mask is None else jnp.where(mask, scores, NEG)
 
     following = score(0)
-    for head in range(heads):
-        scores, following = following, score(head + 1) if head + 1 < heads else None
-        old_max = max_ref[head]
+    for first in range(0, count, block):
+        here = slice(first, first + block)
+        scores, following = following, score(first + block) if first + block < count else None
+        old_max = max_ref[here]
         new_max = jnp.maximum(old_max, jnp.max(scores, axis=1, keepdims=True))
         shrink = jnp.exp2((old_max - new_max) * factor)
         weights = jnp.exp2((scores - jnp.tile(new_max, (1, keys.shape[0] // size))) * factor)
-        max_ref[head] = new_max
-        sums_ref[head] = sums_ref[head] * jnp.tile(shrink, (1, width // size)) + jnp.dot(
+        max_ref[here] = new_max
+        sums_ref[here] = sums_ref[here] * jnp.tile(shrink, (1, width // size)) + jnp.dot(
             weights.astype(jnp.bfloat16), values, preferred_element_type=jnp.float32
         )
 
 
+def stack_queries(q_ref, stacked_ref):
+    tokens, width = q_ref.shape
+    size = stacked_ref.shape[1]
+    for head in range(width // size):
+        stacked_ref[head * tokens:(head + 1) * tokens, :] = q_ref[:, head * size:(head + 1) * size]
+
+
+def load_state(loaded_ref, max_ref, sums_ref):
+    count, size = max_ref.shape
+    sums_ref[:, :size] = loaded_ref[0]
+    sums_ref[:, size:] = jnp.broadcast_to(loaded_ref[1, :, :1], (count, size))
+    max_ref[...] = jnp.broadcast_to(loaded_ref[1, :, size - 1:], (count, size))
+
+
+def save_state(max_ref, sums_ref, saved_ref):
+    count, size = max_ref.shape
+    left = lax.broadcasted_iota(jnp.int32, (count, size), 1) < size // 2
+    saved_ref[0] = sums_ref[:, :size]
+    saved_ref[1] = jnp.where(left, sums_ref[:, size:], max_ref[...])
+
+
 def finish(sums_ref, out_ref):
-    heads, tokens, width = sums_ref.shape
-    size = width // 2
-    for head in range(heads):
+    tokens = out_ref.shape[0]
+    size = sums_ref.shape[1] // 2
+    for head in range(out_ref.shape[1] // size):
+        here = slice(head * tokens, (head + 1) * tokens)
         out_ref[:, head * size:(head + 1) * size] = (
-            sums_ref[head, :, :size] / sums_ref[head, :, size:]
+            sums_ref[here, :size] / sums_ref[here, size:]
         ).astype(out_ref.dtype)
 
 
@@ -81,91 +108,71 @@
         copy.wait()
 
 
-def state_copies(state_here, state_there, sems):
-    return [
-        pltpu.make_async_copy(source, target, sems.at[place])
-        for place, (source, target) in enumerate(zip(state_here, state_there))
-    ]
-
-
-def fold_local(
-    factor, len_ref, q_ref, suffix_ref, own_ref, max_ref, sums_ref, keys_ref, values_ref
-):
+def fold_local(factor, len_ref, suffix_ref, own_ref, work, keys_ref, values_ref):
+    q_ref, max_ref, sums_ref = work
     size = suffix_ref.shape[1] // 2
     suffix = suffix_ref.shape[0]
     own = own_ref.shape[0]
     max_ref[...] = jnp.full(max_ref.shape, NEG, jnp.float32)
     sums_ref[...] = jnp.zeros(sums_ref.shape, jnp.float32)
     stage_rows(suffix_ref[...], 0, keys_ref, values_ref)
-    causal = lax.broadcasted_iota(jnp.int32, (suffix, suffix), 1) <= lax.broadcasted_iota(
-        jnp.int32, (suffix, suffix), 0
-    )
-    fold_keys(
-        q_ref, max_ref, sums_ref, keys_ref[:suffix, :], values_ref[:suffix, :], factor, causal
-    )
+    block = min(ROWS, sums_ref.shape[0])
+    token = lax.broadcasted_iota(jnp.int32, (block, suffix), 0) % suffix
+    causal = lax.broadcasted_iota(jnp.int32, (block, suffix), 1) <= token
+    fold_keys(work, keys_ref[:suffix, :], values_ref[:suffix, :], factor, causal)
     live = lax.broadcasted_iota(jnp.int32, (own, size), 0) < len_ref[0]
     stage_live(own_ref[...].astype(jnp.float32), live, suffix_ref, keys_ref, values_ref)
-    fold_keys(q_ref, max_ref, sums_ref, keys_ref[:own, :], values_ref[:own, :], factor)
+    fold_keys(work, keys_ref[:own, :], values_ref[:own, :], factor)
 
 
 def moved_kernel(factor, local, steps, *refs):
     q_ref, suffix_ref, kv_ref = refs[:3]
-    state_out = refs[-7:-5]
-    max_ref, sums_ref, keys_ref, values_ref, sems = refs[-5:]
+    out_ref, *work, keys_ref, values_ref = refs[-6:]
     step = pl.program_id(0)
 
-    if local:
-
-        @pl.when(step == 0)
-        def _():
-            fold_local(factor, refs[3], q_ref, suffix_ref, refs[4], *refs[-5:-1])
-
-    else:
-        loads = state_copies(refs[3:5], (max_ref, sums_ref), sems)
-        pl.when(step == 0)(lambda: start_all(loads))
+    @pl.when(step == 0)
+    def _():
+        stack_queries(q_ref, work[0])
+        if local:
+            fold_local(factor, refs[3], suffix_ref, refs[4], work, keys_ref, values_ref)
+        else:
+            load_state(refs[3], *work[1:])
 
     rows = kv_ref[...].reshape(-1, kv_ref.shape[-1]).astype(jnp.float32)
     count, size = rows.shape[0], rows.shape[1] // 2
     live = jnp.broadcast_to(rows[:, size:size + 1] < DEAD_ABOVE, (count, size))
     stage_live(rows, live, suffix_ref, keys_ref, values_ref)
-    if not local:
-        pl.when(step == 0)(lambda: wait_all(loads))
-    fold_keys(q_ref, max_ref, sums_ref, keys_ref[:count, :], values_ref[:count, :], factor)
+    fold_keys(work, keys_ref[:count, :], values_ref[:count, :], factor)
 
     @pl.when(step == steps - 1)
     def _():
-        saves = state_copies((max_ref, sums_ref), state_out, sems)
-        start_all(saves)
-        wait_all(saves)
-
-
-def prefix_kernel(factor, last, count, steps, which_ref, q_ref, *refs):
-    pieces, refs = refs[:count], refs[count:]
-    max_ref, sums_ref, keys_ref, values_ref, sems = refs[-5:]
+        if local:
+            save_state(*work[1:], out_ref)
+        else:
+            finish(work[2], out_ref)
+
+
+def prefix_kernel(factor, count, steps, which_ref, q_ref, *refs):
+    pieces = refs[:count]
+    loaded_ref, out_ref, *work, keys_ref, values_ref = refs[count:]
     step = pl.program_id(0)
     chunk = keys_ref.shape[0] // steps
 
     @pl.when(step == 0)
     def _():
-        loads = state_copies(refs[:2], (max_ref, sums_ref), sems)
-        start_all(loads)
+        stack_queries(q_ref, work[0])
         place = 0
         for piece in pieces:
             stage_rows(piece[...], place, keys_ref, values_ref)
             place += piece.shape[0]
-        wait_all(loads)
+        load_state(loaded_ref, *work[1:])
 
     rows = pl.ds(pl.multiple_of(step * chunk, keys_ref.shape[1]), chunk)
-    fold_keys(q_ref, max_ref, sums_ref, keys_ref[rows, :], values_ref[rows, :], factor)
+    fold_keys(work, keys_ref[rows, :], values_ref[rows, :], factor)
 
     @pl.when(step == steps - 1)
     def _():
-        if last:
-            finish(sums_ref, refs[2])
-        else:
-            saves = state_copies((max_ref, sums_ref), refs[2:4], sems)
-            start_all(saves)
-            wait_all(saves)
+        save_state(*work[1:], out_ref)
 
 
 def pick_kernel(which_ref, *refs):
@@ -301,7 +308,7 @@
             pltpu.SemaphoreType.DMA((chips, owners.shape[0])),
             pltpu.SemaphoreType.DMA((chips + 2,)),
         ],
-        compiler_params=PARAMS,
+        compiler_params=COPY_PARAMS,
         name="stage_prefix",
     )(
         sought,
@@ -397,22 +404,21 @@
     heads = queries.shape[1] // size
     factor = size ** (-0.5) * LOG2E
     row_count = tokens * heads
-    state = (
-        jax.ShapeDtypeStruct((heads, tokens, size), jnp.float32),
-        jax.ShapeDtypeStruct((heads, tokens, 2 * size), jnp.float32),
-    )
+    state = jax.ShapeDtypeStruct((2, row_count, size), jnp.float32)
+    result = jax.ShapeDtypeStruct(queries.shape, queries.dtype)
 
     def scratch(keys):
         return [
-            *[pltpu.VMEM(part.shape, part.dtype) for part in state],
+            pltpu.VMEM((row_count, size), queries.dtype),
+            pltpu.VMEM((row_count, size), jnp.float32),
+            pltpu.VMEM((row_count, 2 * size), jnp.float32),
             pltpu.VMEM((keys, size), jnp.bfloat16),
             pltpu.VMEM((keys, 2 * size), jnp.bfloat16),
-            pltpu.SemaphoreType.DMA((2,)),
         ]
 
     entries = mig_target.shape[1]
     block = kv_pool.shape[1]
-    early = block * 3 // 4
+    early = block // 2
     parts = tuple(
         jax.ShapeDtypeStruct((replicas, rows, kv_pool.shape[2]), kv_pool.dtype)
         for rows in (early, block - early)
@@ -428,7 +434,7 @@
             pltpu.SemaphoreType.DMA((entries,)),
             pltpu.SemaphoreType.DMA((len(parts), entries)),
         ],
-        compiler_params=PARAMS,
+        compiler_params=COPY_PARAMS,
         name="pack_moved",
     )(mig_target, mig_block, mig_count, kv_pool)
     held, place, outgoing = multicast(prefix_cache, owners, readers, outgoing)
@@ -443,70 +449,57 @@
         keys = replicas * rows + (tokens + own_cache.shape[0]) * local
         return pl.pallas_call(
             functools.partial(moved_kernel, factor, local, steps),
-            out_shape=state,
+            out_shape=state if local else result,
             grid=(steps,),
             in_specs=[
                 whole(queries.shape),
                 whole(suffix_kv.shape),
                 pl.BlockSpec((group, rows, 2 * size), lambda i: (i, 0, 0)),
-                *([IN_SMEM, whole(own_cache.shape)] if local else [IN_HBM] * 2),
+                *([IN_SMEM, whole(own_cache.shape)] if local else [whole(state.shape)]),
             ],
-            out_specs=(IN_HBM,) * 2,
+            out_specs=whole(state.shape if local else queries.shape),
             scratch_shapes=scratch(most),
             compiler_params=PARAMS,
             cost_estimate=cost(row_count, keys, size),
             name="moved_keys",
-        )(queries, suffix_kv, arrived, *((ctx_len, own_cache) if local else state_now))
-
-    def fold_prefix(pieces, state_now, last):
-        others = from_other(pieces, place)
-        rows = pieces[0].shape[1]
-        keys = 2 * len(pieces) * rows
+        )(queries, suffix_kv, arrived, *((ctx_len, own_cache) if local else (state_now,)))
+
+    def fold_prefix(gathered, state_now):
+        near = [gathered[step] for step in gathered if step.bit_count() < 2]
+        far = [gathered[step] for step in gathered if step.bit_count() > 1]
+        others = [from_other(near, place), from_other(far, place)]
+        rows = near[0].shape[1]
+        keys = 2 * len(gathered) * rows
         steps = max(1, keys // CHUNK)
         while keys % (steps * size):
             steps -= 1
         return pl.pallas_call(
-            functools.partial(prefix_kernel, factor, last, len(pieces) + 1, steps),
-            out_shape=jax.ShapeDtypeStruct(queries.shape, queries.dtype) if last else state,
+            functools.partial(prefix_kernel, factor, len(gathered) + 2, steps),
+            out_shape=state,
             grid_spec=pltpu.PrefetchScalarGridSpec(
                 num_scalar_prefetch=1,
                 grid=(steps,),
                 in_specs=[
                     whole(queries.shape),
                     *[pl.BlockSpec((None, rows, 2 * size), lambda i, which: (which[0], 0, 0))]
-                    * len(pieces),
-                    whole(others.shape),
-                    IN_HBM,
-                    IN_HBM,
+                    * len(gathered),
+                    *[whole(part.shape) for part in others],
+                    whole(state.shape),
                 ],
-                out_specs=whole(queries.shape) if last else (IN_HBM, IN_HBM),
+                out_specs=whole(state.shape),
                 scratch_shapes=scratch(keys),
             ),
             compiler_params=PARAMS,
             cost_estimate=cost(row_count, keys, size),
             name="prefix_keys",
-        )(place, queries, *pieces, others, *state_now)
+        )(place, queries, *near, *far, *others, state_now)
 
     state_now = fold_moved(outgoing[0], None)
-    held, *later = lax.optimization_barrier((held, *outgoing[1:]))
-    chips = replicas // 4
     gathered = {0: held}
-    for step in (step for step in range(1, chips) if step.bit_count() == 1):
+    for step in sorted(range(1, replicas // 4), key=lambda step: (step.bit_count(), step)):
         gathered[step] = gather_step(gathered, step)
-    state_now = fold_prefix(list(gathered.values()), state_now, False)
-    late = sorted(
-        (step for step in range(1, chips) if step.bit_count() > 1),
-        key=lambda step: (step.bit_count(), step),
-    )
-    for step in late:
-        if step == late[-1]:
-            source, *state_now = lax.optimization_barrier((gathered, *state_now))
-        else:
-            source = gathered
-        gathered[step] = gather_step(source, step)
-    for part in later:
-        state_now = fold_moved(part, state_now)
-    return fold_prefix([gathered[step] for step in late], state_now, True)
+    gathered[1], last_part = lax.optimization_barrier((gathered[1], outgoing[1]))
+    return fold_moved(last_part, fold_prefix(gathered, state_now))
 
 
 def solution(mesh):

time: 152 us -> 151 us (level)
  Pallas kernels: 53.9 us -> 38.8 us
  local copies, waits for them, and re-layouts: 3.82 us -> 11.7 us
  waiting for transfers between devices: 37.9 us -> 44.7 us
    all_to_all x2, starting transfers between devices: 10.3 us -> 22 us  [fold_moved(): lax.all_to_all(part, 'replica', split_axis=0, concat_axis=0, tiled=True)]
    ppermute x1, starting transfers between devices: 12.6 us -> 3.21 us  [multicast(): lax.ppermute(found, 'replica', [(i, (i + half) % replicas) for i in range...]
    unnamed x28 -> x60, local copies, waits for them, and re-layouts: 2.57 us -> 9.66 us
    pallas_call x2 -> x1, Pallas kernels: 20.6 us -> 14 us  [fold_prefix(): pl.pallas_call(functools.partial(prefix_kernel, factor, len(gathered) + 2...]
    pallas_call x2, Pallas kernels: 21 us -> 15.6 us  [fold_moved(): pl.pallas_call(functools.partial(moved_kernel, factor, local, steps), out...]
    ppermute x7, starting transfers between devices: 7.82 us -> 4.39 us  [gather_step(): return lax.ppermute(gathered[step ^ 1 << last], 'replica', pairs)]
    pallas_call x2, Pallas kernels: 5.17 us -> 2.06 us  [from_other(): pl.pallas_call(pick_kernel, out_shape=jax.ShapeDtypeStruct((len(pieces) *...]
    ppermute x7, waiting for transfers between devices: 7.97 us -> 11 us  [gather_step(): return lax.ppermute(gathered[step ^ 1 << last], 'replica', pairs)]
  transfers between devices with their start and end apart: 24 -> 24, of which waited for: 9 -> 12; matrix products, arithmetic and copies ran while one was open for 3% -> 4% of each run, Pallas kernels for 29% -> 19%
where the time goes in v10:
time: 151 us
  starting transfers between devices  47.6 us (32%)
  waiting for transfers between devices  44.7 us (30%)
  Pallas kernels  38.8 us (26%)
  local copies, waits for them, and re-layouts  11.7 us (8%)
  other arithmetic  4.13 us (3%)
  between operations  3.71 us (2%)
    ppermute x7, waiting for transfers between devices, multicast(): lax.ppermute(staged[step], 'replica', [(i, i ^ 2 * step) for i in range(r...  23.5 us
    all_to_all x2, starting transfers between devices, fold_moved(): lax.all_to_all(part, 'replica', split_axis=0, concat_axis=0, tiled=True)  22 us
    pallas_call x2, Pallas kernels, fold_moved(): pl.pallas_call(functools.partial(moved_kernel, factor, local, steps), out...  15.6 us
    pallas_call x1, Pallas kernels, fold_prefix(): pl.pallas_call(functools.partial(prefix_kernel, factor, len(gathered) + 2...  14 us
    ppermute x7, starting transfers between devices, multicast(): lax.ppermute(staged[step], 'replica', [(i, i ^ 2 * step) for i in range(r...  13.7 us
    ppermute x7, waiting for transfers between devices, gather_step(): return lax.ppermute(gathered[step ^ 1 << last], 'replica', pairs)  11 us
    unnamed x60, local copies, waits for them, and re-layouts  9.66 us
    ppermute x1, waiting for transfers between devices, multicast(): lax.ppermute(found, 'replica', [(i, (i + half) % replicas) for i in range...  7.86 us
  transfers between devices with their start and end apart: 24, of which 12 were waited for; matrix products, arithmetic and copies ran while one was open for 4% of the time, Pallas kernels for 19%

profile of v10, /device:TPU:0, one launch (start us, length us, event | category | flops | bytes accessed | tf_op | source)
XLA Modules:
  0.0 150.7 jit_solution(11818335949105210211)
XLA Ops:
  1.1 1.3 fusion.2
  3.1 1.3 fusion.4
  5.8 3.9 %pack_moved.1 = (bf16[32,64,256]{2,1,0:T(8,128)(2,1)}, bf16[32,64,256]{2,1,0:T(8,128)(2,1)}) custom-call(s32[1,32]{1,0:T(1,128)} %target_ref.1, s32[1,32]{1,0:T(1,128)} %block_ref.1, s32[1]{0:T(128)S(6)} %copy.13.count_ref, bf16[32,128,256]{2,1,0:T(8,128)(2,1)} %pool_ref.1), custom_call_target="tpu_custom_call" | custom-call | tf_op jit(solution)/shard_map/pack_moved/pallas_call | solution.py:426
  9.7 0.6 pad_add_fusion.place_ref
  10.3 1.3 copy-done.20
  11.6 3.2 %stage_prefix.1 = (bf16[1,256,256]{2,1,0:T(8,128)(2,1)}, bf16[1,256,256]{2,1,0:T(8,128)(2,1)}, bf16[1,256,256]{2,1,0:T(8,128)(2,1)}, bf16[1,256,256]{2,1,0:T(8,1...) custom-call(s32[1]{0:T(128)S(6)} %select_n.115.owner_ref, ...), custom_call_target="tpu_custom_call" | custom-call | tf_op jit(solution)/shard_map/stage_prefix/pallas_call | solution.py:300
  14.9 0.8 collective-permute-start.1
  15.9 0.8 collective-permute-start.2
  16.7 3.7 %collective-permute-start.5 = (bf16[1,256,256]{2,1,0:T(8,128)(2,1)S(1)}, bf16[1,256,256]{2,1,0:T(8,128)(2,1)S(1)}, u32[]{:S(2)}, u32[]{:S(2)}) collective-permute-start(bf16[1,256,256]{2,1,0:T(8,128)(2,1)S(1)} %copy-done.29), channel_id=1, source_target_pairs={{0,2},{1,3},{2,0},{3,1},{4,6},{5,7},{6,4},{7,5},{8,10},{9,11},{10,... | collective-permute-start | bytes 393224 | tf_op jit(solution)/shard_map/ppermute | solution.py:323
  20.4 1.4 collective-permute-start.6
  21.8 19.2 %all-to-all-start.1 = ((bf16[32,64,256]{2,1,0:T(8,128)(2,1)}), bf16[32,64,256]{2,1,0:T(8,128)(2,1)S(1)}, u32[]{:S(2)}, u32[]{:S(2)}) async-start(bf16[32,64,256]{2,1,0:T(8,128)(2,1)} %get-tuple-element.38), calls=%async_computation.1 | async-start | bytes 2097152 | tf_op jit(solution)/shard_map/all_to_all | solution.py:443
  41.0 2.7 %collective-permute-start.7 = (bf16[1,256,256]{2,1,0:T(8,128)(2,1)S(1)}, bf16[1,256,256]{2,1,0:T(8,128)(2,1)S(1)}, u32[]{:S(2)}, u32[]{:S(2)}) collective-permute-start(bf16[1,256,256]{2,1,0:T(8,128)(2,1)S(1)} %copy-done.27), channel_id=1, source_target_pairs={{0,6},{1,7},{2,4},{3,5},{4,2},{5,3},{6,0},{7,1},{8,14},{9,15},{10,... | collective-permute-start | bytes 393224 | tf_op jit(solution)/shard_map/ppermute | solution.py:323
  43.8 1.5 collective-permute-start.8
  45.2 0.6 collective-permute-start.9
  45.8 1.5 collective-permute-start.10
  47.3 2.4 %collective-permute-start.11 = (bf16[1,256,256]{2,1,0:T(8,128)(2,1)S(1)}, bf16[1,256,256]{2,1,0:T(8,128)(2,1)S(1)}, u32[]{:S(2)}, u32[]{:S(2)}) collective-permute-start(bf16[1,256,256]{2,1,0:T(8,128)(2,1)S(1)} %copy-done.23), channel_id=1, source_target_pairs={{0,14},{1,15},{2,12},{3,13},{4,10},{5,11},{6,8},{7,9},{8,6},{9,7},... | collective-permute-start | bytes 393224 | tf_op jit(solution)/shard_map/ppermute | solution.py:323
  49.7 6.7 %collective-permute-done.7 = bf16[1,256,256]{2,1,0:T(8,128)(2,1)S(1)} collective-permute-done((bf16[1,256,256]{2,1,0:T(8,128)(2,1)S(1)}, bf16[1,256,256]{2,1,0:T(8,128)(2,1)S(1)}, u32[]{:S(2)}, u32[]{:S(2)}) %collective-permute-start.7) | collective-permute-done | bytes 131104 | tf_op jit(solution)/shard_map/ppermute | solution.py:323
  56.4 0.7 collective-permute-start.3
  57.0 4.8 %collective-permute-done.8 = bf16[1,256,256]{2,1,0:T(8,128)(2,1)S(1)} collective-permute-done((bf16[1,256,256]{2,1,0:T(8,128)(2,1)S(1)}, bf16[1,256,256]{2,1,0:T(8,128)(2,1)S(1)}, u32[]{:S(2)}, u32[]{:S(2)}) %collective-permute-start.8) | collective-permute-done | bytes 131104 | tf_op jit(solution)/shard_map/ppermute | solution.py:323
  61.8 4.9 %collective-permute-done.9 = bf16[1,256,256]{2,1,0:T(8,128)(2,1)S(1)} collective-permute-done((bf16[1,256,256]{2,1,0:T(8,128)(2,1)S(1)}, bf16[1,256,256]{2,1,0:T(8,128)(2,1)S(1)}, u32[]{:S(2)}, u32[]{:S(2)}) %collective-permute-start.9) | collective-permute-done | bytes 131104 | tf_op jit(solution)/shard_map/ppermute | solution.py:323
  66.7 3.9 %collective-permute-done.10 = bf16[1,256,256]{2,1,0:T(8,128)(2,1)S(1)} collective-permute-done((bf16[1,256,256]{2,1,0:T(8,128)(2,1)S(1)}, bf16[1,256,256]{2,1,0:T(8,128)(2,1)S(1)}, u32[]{:S(2)}, u32[]{:S(2)}) %collective-permute-start.10) | collective-permute-done | bytes 131104 | tf_op jit(solution)/shard_map/ppermute | solution.py:323
  70.6 3.3 %collective-permute-done.11 = bf16[1,256,256]{2,1,0:T(8,128)(2,1)S(1)} collective-permute-done((bf16[1,256,256]{2,1,0:T(8,128)(2,1)S(1)}, bf16[1,256,256]{2,1,0:T(8,128)(2,1)S(1)}, u32[]{:S(2)}, u32[]{:S(2)}) %collective-permute-start.11) | collective-permute-done | bytes 131104 | tf_op jit(solution)/shard_map/ppermute | solution.py:323
  73.9 3.2 %collective-permute-start.12 = (bf16[1,256,256]{2,1,0:T(8,128)(2,1)S(1)}, bf16[1,256,256]{2,1,0:T(8,128)(2,1)S(1)}, u32[]{:S(2)}, u32[]{:S(2)}) collective-permute-start(bf16[1,256,256]{2,1,0:T(8,128)(2,1)S(1)} %select_select_fusion), channel_id=1, source_target_pairs={{0,16},{1,17},{2,18},{3,19},{4,20},{5,21},{6,22},{7,23},{8,24},{9,... | collective-permute-start | bytes 393224 | tf_op jit(solution)/shard_map/ppermute | solution.py:327
  77.1 1.3 collective-permute-start.4
  78.4 7.9 %collective-permute-done.12 = bf16[1,256,256]{2,1,0:T(8,128)(2,1)S(1)} collective-permute-done((bf16[1,256,256]{2,1,0:T(8,128)(2,1)S(1)}, bf16[1,256,256]{2,1,0:T(8,128)(2,1)S(1)}, u32[]{:S(2)}, u32[]{:S(2)}) %collective-permute-start.12) | collective-permute-done | bytes 131104 | tf_op jit(solution)/shard_map/ppermute | solution.py:327
  86.3 2.1 %collective-permute-done.4 = bf16[1,256,256]{2,1,0:T(8,128)(2,1)S(1)} collective-permute-done((bf16[1,256,256]{2,1,0:T(8,128)(2,1)S(1)}, bf16[1,256,256]{2,1,0:T(8,128)(2,1)S(1)}, u32[]{:S(2)}, u32[]{:S(2)}) %collective-permute-start.4) | collective-permute-done | bytes 131104 | tf_op jit(solution)/shard_map/ppermute | solution.py:340
  88.4 0.5 collective-permute-start.14
  88.9 0.6 collective-permute-start.13
  89.5 6.6 %collective-permute-done.14.refs_2_ = bf16[2,256,256]{2,1,0:T(8,128)(2,1)S(1)} collective-permute-done((bf16[2,256,256]{2,1,0:T(8,128)(2,1)S(1)}, bf16[2,256,256]{2,1,0:T(8,128)(2,1)S(1)}, u32[]{:S(2)}, u32[]{:S(2)}) %collective-permute-start.14) | collective-permute-done | bytes 262176 | tf_op jit(solution)/shard_map/ppermute | solution.py:357
  96.8 2.1 %collective-permute-start.16 = (bf16[2,256,256]{2,1,0:T(8,128)(2,1)S(1)}, bf16[2,256,256]{2,1,0:T(8,128)(2,1)S(1)}, u32[]{:S(2)}, u32[]{:S(2)}) collective-permute-start(bf16[2,256,256]{2,1,0:T(8,128)(2,1)S(1)} %collective-permute-done.13.refs_1_), channel_id=1, source_target_pairs={{0,4},{1,5},{2,6},{3,7},{4,0},{5,1},{6,2},{7,3},{8,12},{9,13},{10,... | collective-permute-start | bytes 786440 | tf_op jit(solution)/shard_map/ppermute | solution.py:357
  98.9 3.8 %collective-permute-done.18.refs_2_.refs_6_ = bf16[2,256,256]{2,1,0:T(8,128)(2,1)S(1)} collective-permute-done((bf16[2,256,256]{2,1,0:T(8,128)(2,1)S(1)}, bf16[2,256,256]{2,1,0:T(8,128)(2,1)S(1)}, u32[]{:S(2)}, u32[]{:S(2)}) %collective-permute-start.18) | collective-permute-done | bytes 262176 | tf_op jit(solution)/shard_map/ppermute | solution.py:357
  102.8 0.7 collective-permute-start.19
  104.1 0.7 fusion.3
  104.8 2.0 %compare_select_fusion.which_ref = s32[2]{0:T(128)S(1)} fusion(s32[1]{0:T(128)} %get-tuple-element.40, s32[1]{0:T(128)} %get-tuple-element.39, s32[]{:T(128)} %fusion.2), kind=kLoop, calls=%fused_computation.9 | loop fusion | flops 12 | bytes 20 | tf_op jit(solution)/shard_map/jit(_where)/select_n | solution.py:343
  106.8 0.6 pick_other.2
  107.4 0.7 copy-done.8
  108.2 0.7 copy-done.11
  109.2 0.9 copy-done.9
  110.2 0.9 copy-done.12
  111.1 1.5 pick_other.3
  112.8 2.8 %all-to-all-start = ((bf16[32,64,256]{2,1,0:T(8,128)(2,1)}), bf16[32,64,256]{2,1,0:T(8,128)(2,1)S(1)}, u32[]{:S(2)}, u32[]{:S(2)}) async-start(bf16[32,64,256]{2,1,0:T(8,128)(2,1)} %get-tuple-element.36), calls=%async_computation | async-start | bytes 2097152 | tf_op jit(solution)/shard_map/all_to_all | solution.py:443
  115.7 1.0 copy-done.14
  116.7 0.9 copy-done.16
  117.7 8.3 %moved_keys.2.refs_10_ = f32[2,2048,128]{2,1,0:T(8,128)S(1)} custom-call(bf16[256,1024]{1,0:T(8,128)(2,1)S(1)} %copy-done.14, bf16[256,256]{1,0:T(8,128)(2,1)S(1)} %copy-done.17, bf16[32,64,256]{2,1,0:T(8,128)(2,1)S(1)} %all-to-all-done.1.refs_2_, s32[1]{0:T(128)S(6)} %copy.12.refs_3_, bf16[512,256]{1,0:T(8,128)(2,1)S(1)} %copy-done.16), custom_call_target="tpu_custom_call" | custom-call | flops 8858370048 | bytes 1441792 | tf_op jit(solution)/shard_map/moved_keys/pallas_call | solution.py:450
  126.1 14.0 %prefix_keys.1.refs_3_ = f32[2,2048,128]{2,1,0:T(8,128)S(1)} custom-call(s32[2]{0:T(128)S(1)} %compare_select_fusion.which_ref, bf16[256,1024]{1,0:T(8,128)(2,1)S(1)} %copy-done.14, bf16[2,256,256]{2,1,0:T(8,128)(2,1)S(1)} %pad_maximum_fusion.refs_0_, bf16[2,256,256]{2,1,0:T(8,128)(2,1)S(1)} %copy-done.5, bf16[2,256,256]{2,1,0:T(8,128)(2,1)S(1)} %copy-done.1, ...), custom_call_target="tpu_custom_call" | custom-call | flops 12884901888 | bytes 2097152 | tf_op jit(solution)/shard_map/prefix_keys/pallas_call | solution.py:476
  140.1 1.3 copy-done.18
  141.7 1.6 %copy-done.19 = f32[2,2048,128]{2,1,0:T(8,128)S(1)} copy-done((f32[2,2048,128]{2,1,0:T(8,128)S(1)}, f32[2,2048,128]{2,1,0:T(8,128)}, u32[]{:S(2)}) %copy-start.19) | copy-done | bytes 2097176
  143.3 7.3 %moved_keys.3 = bf16[256,1024]{1,0:T(8,128)(2,1)} custom-call(bf16[256,1024]{1,0:T(8,128)(2,1)S(1)} %copy-done.15, bf16[256,256]{1,0:T(8,128)(2,1)S(1)} %copy-done.17, bf16[32,64,256]{2,1,0:T(8,128)(2,1)S(1)} %all-to-all-done.refs_2_, f32[2,2048,128]{2,1,0:T(8,128)S(1)} %copy-done.19), custom_call_target="tpu_custom_call" | custom-call | flops 6442450944 | bytes 1048576 | tf_op jit(solution)/shard_map/moved_keys/pallas_call | solution.py:450
  (82 shorter events, 2.5 us)
Async XLA Ops:
  0.0 10.3 %collective-permute-start = (bf16[4096,256]{1,0:T(8,128)(2,1)}, bf16[4096,256]{1,0:T(8,128)(2,1)S(1)}, u32[]{:S(2)}, u32[]{:S(2)}) collective-permute-start(bf16[4096,256]{1,0:T(8,128)(2,1)} %param.15), channel_id=1, source_target_pairs={{0,1},{1,0},{2,3},{3,2},{4,5},{5,4},{6,7},{7,6},{8,9},{9,8},{10,11... | collective-permute-start | bytes 6291464 | tf_op jit(solution)/shard_map/ppermute | solution.py:347
  10.3 1.3 copy-start.20
  14.8 1.8 %copy-start.29 = (bf16[1,256,256]{2,1,0:T(8,128)(2,1)S(1)}, bf16[1,256,256]{2,1,0:T(8,128)(2,1)}, u32[]{:S(2)}) copy-start(bf16[1,256,256]{2,1,0:T(8,128)(2,1)} %get-tuple-element.27) | copy-start | bytes 393220
  14.8 5.5 %copy-start.28 = (bf16[1,256,256]{2,1,0:T(8,128)(2,1)S(1)}, bf16[1,256,256]{2,1,0:T(8,128)(2,1)}, u32[]{:S(2)}) copy-start(bf16[1,256,256]{2,1,0:T(8,128)(2,1)} %get-tuple-element.28) | copy-start | bytes 393220
  14.9 0.8 collective-permute-start.1
  15.7 25.3 %copy-start.27 = (bf16[1,256,256]{2,1,0:T(8,128)(2,1)S(1)}, bf16[1,256,256]{2,1,0:T(8,128)(2,1)}, u32[]{:S(2)}) copy-start(bf16[1,256,256]{2,1,0:T(8,128)(2,1)} %get-tuple-element.29) | copy-start | bytes 393220
  15.7 28.1 %copy-start.26 = (bf16[1,256,256]{2,1,0:T(8,128)(2,1)S(1)}, bf16[1,256,256]{2,1,0:T(8,128)(2,1)}, u32[]{:S(2)}) copy-start(bf16[1,256,256]{2,1,0:T(8,128)(2,1)} %get-tuple-element.30) | copy-start | bytes 393220
  15.7 29.5 %copy-start.25 = (bf16[1,256,256]{2,1,0:T(8,128)(2,1)S(1)}, bf16[1,256,256]{2,1,0:T(8,128)(2,1)}, u32[]{:S(2)}) copy-start(bf16[1,256,256]{2,1,0:T(8,128)(2,1)} %get-tuple-element.31) | copy-start | bytes 393220
  15.7 30.1 %copy-start.24 = (bf16[1,256,256]{2,1,0:T(8,128)(2,1)S(1)}, bf16[1,256,256]{2,1,0:T(8,128)(2,1)}, u32[]{:S(2)}) copy-start(bf16[1,256,256]{2,1,0:T(8,128)(2,1)} %get-tuple-element.32) | copy-start | bytes 393220
  15.7 31.5 %copy-start.23 = (bf16[1,256,256]{2,1,0:T(8,128)(2,1)S(1)}, bf16[1,256,256]{2,1,0:T(8,128)(2,1)}, u32[]{:S(2)}) copy-start(bf16[1,256,256]{2,1,0:T(8,128)(2,1)} %get-tuple-element.33) | copy-start | bytes 393220
  15.8 58.0 %copy-start.21 = (bf16[1,256,256]{2,1,0:T(8,128)(2,1)S(1)}, bf16[1,256,256]{2,1,0:T(8,128)(2,1)}, u32[]{:S(2)}) copy-start(bf16[1,256,256]{2,1,0:T(8,128)(2,1)} %get-tuple-element.34) | copy-start | bytes 393220
  15.9 31.4 %collective-permute-start.2 = (bf16[2,1,256,256]{3,2,1,0:T(8,128)(2,1)S(1)}, bf16[2,1,256,256]{3,2,1,0:T(8,128)(2,1)S(1)}, u32[]{:S(2)}, u32[]{:S(2)}) collective-permute-start(bf16[2,1,256,256]{3,2,1,0:T(8,128)(2,1)S(1)} %slice.29), channel_id=1, source_target_pairs={{28,24},{29,25},{30,26},{31,27}} | collective-permute-start | bytes 786440 | tf_op jit(solution)/shard_map/ppermute | solution.py:335
  16.7 28.5 %collective-permute-start.5 = (bf16[1,256,256]{2,1,0:T(8,128)(2,1)S(1)}, bf16[1,256,256]{2,1,0:T(8,128)(2,1)S(1)}, u32[]{:S(2)}, u32[]{:S(2)}) collective-permute-start(bf16[1,256,256]{2,1,0:T(8,128)(2,1)S(1)} %copy-done.29), channel_id=1, source_target_pairs={{0,2},{1,3},{2,0},{3,1},{4,6},{5,7},{6,4},{7,5},{8,10},{9,11},{10,... | collective-permute-start | bytes 393224 | tf_op jit(solution)/shard_map/ppermute | solution.py:323
  20.4 25.4 %collective-permute-start.6 = (bf16[1,256,256]{2,1,0:T(8,128)(2,1)S(1)}, bf16[1,256,256]{2,1,0:T(8,128)(2,1)S(1)}, u32[]{:S(2)}, u32[]{:S(2)}) collective-permute-start(bf16[1,256,256]{2,1,0:T(8,128)(2,1)S(1)} %copy-done.28), channel_id=1, source_target_pairs={{0,4},{1,5},{2,6},{3,7},{4,0},{5,1},{6,2},{7,3},{8,12},{9,13},{10,... | collective-permute-start | bytes 393224 | tf_op jit(solution)/shard_map/ppermute | solution.py:323
  21.8 91.0 %all-to-all-start.1 = ((bf16[32,64,256]{2,1,0:T(8,128)(2,1)}), bf16[32,64,256]{2,1,0:T(8,128)(2,1)S(1)}, u32[]{:S(2)}, u32[]{:S(2)}) async-start(bf16[32,64,256]{2,1,0:T(8,128)(2,1)} %get-tuple-element.38), calls=%async_computation.1 | async-start | bytes 2097152 | tf_op jit(solution)/shard_map/all_to_all | solution.py:443
  41.0 63.1 %copy-start.22 = (s32[32]{0:T(128)S(1)}, s32[32]{0:T(128)}, u32[]{:S(2)}) copy-start(s32[32]{0:T(128)} %param.17) | copy-start | bytes 388
  41.0 15.3 %collective-permute-start.7 = (bf16[1,256,256]{2,1,0:T(8,128)(2,1)S(1)}, bf16[1,256,256]{2,1,0:T(8,128)(2,1)S(1)}, u32[]{:S(2)}, u32[]{:S(2)}) collective-permute-start(bf16[1,256,256]{2,1,0:T(8,128)(2,1)S(1)} %copy-done.27), channel_id=1, source_target_pairs={{0,6},{1,7},{2,4},{3,5},{4,2},{5,3},{6,0},{7,1},{8,14},{9,15},{10,... | collective-permute-start | bytes 393224 | tf_op jit(solution)/shard_map/ppermute | solution.py:323
  43.8 18.0 %collective-permute-start.8 = (bf16[1,256,256]{2,1,0:T(8,128)(2,1)S(1)}, bf16[1,256,256]{2,1,0:T(8,128)(2,1)S(1)}, u32[]{:S(2)}, u32[]{:S(2)}) collective-permute-start(bf16[1,256,256]{2,1,0:T(8,128)(2,1)S(1)} %copy-done.26), channel_id=1, source_target_pairs={{0,8},{1,9},{2,10},{3,11},{4,12},{5,13},{6,14},{7,15},{8,0},{9,1},... | collective-permute-start | bytes 393224 | tf_op jit(solution)/shard_map/ppermute | solution.py:323
  45.2 21.4 %collective-permute-start.9 = (bf16[1,256,256]{2,1,0:T(8,128)(2,1)S(1)}, bf16[1,256,256]{2,1,0:T(8,128)(2,1)S(1)}, u32[]{:S(2)}, u32[]{:S(2)}) collective-permute-start(bf16[1,256,256]{2,1,0:T(8,128)(2,1)S(1)} %copy-done.25), channel_id=1, source_target_pairs={{0,10},{1,11},{2,8},{3,9},{4,14},{5,15},{6,12},{7,13},{8,2},{9,3},... | collective-permute-start | bytes 393224 | tf_op jit(solution)/shard_map/ppermute | solution.py:323
  45.8 24.8 %collective-permute-start.10 = (bf16[1,256,256]{2,1,0:T(8,128)(2,1)S(1)}, bf16[1,256,256]{2,1,0:T(8,128)(2,1)S(1)}, u32[]{:S(2)}, u32[]{:S(2)}) collective-permute-start(bf16[1,256,256]{2,1,0:T(8,128)(2,1)S(1)} %copy-done.24), channel_id=1, source_target_pairs={{0,12},{1,13},{2,14},{3,15},{4,8},{5,9},{6,10},{7,11},{8,4},{9,5},... | collective-permute-start | bytes 393224 | tf_op jit(solution)/shard_map/ppermute | solution.py:323
  47.3 26.6 %collective-permute-start.11 = (bf16[1,256,256]{2,1,0:T(8,128)(2,1)S(1)}, bf16[1,256,256]{2,1,0:T(8,128)(2,1)S(1)}, u32[]{:S(2)}, u32[]{:S(2)}) collective-permute-start(bf16[1,256,256]{2,1,0:T(8,128)(2,1)S(1)} %copy-done.23), channel_id=1, source_target_pairs={{0,14},{1,15},{2,12},{3,13},{4,10},{5,11},{6,8},{7,9},{8,6},{9,7},... | collective-permute-start | bytes 393224 | tf_op jit(solution)/shard_map/ppermute | solution.py:323
  56.4 20.8 %collective-permute-start.3 = (bf16[1,1,256,256]{3,2,1,0:T(8,128)(2,1)S(1)}, bf16[1,1,256,256]{3,2,1,0:T(8,128)(2,1)S(1)}, u32[]{:S(2)}, u32[]{:S(2)}) collective-permute-start(bf16[1,1,256,256]{3,2,1,0:T(8,128)(2,1)S(1)} %slice.31), channel_id=1, source_target_pairs={{24,16},{25,17},{26,18},{27,19},{28,20},{29,21},{30,22},{31,23}} | collective-permute-start | bytes 393224 | tf_op jit(solution)/shard_map/ppermute | solution.py:335
  73.9 12.4 %collective-permute-start.12 = (bf16[1,256,256]{2,1,0:T(8,128)(2,1)S(1)}, bf16[1,256,256]{2,1,0:T(8,128)(2,1)S(1)}, u32[]{:S(2)}, u32[]{:S(2)}) collective-permute-start(bf16[1,256,256]{2,1,0:T(8,128)(2,1)S(1)} %select_select_fusion), channel_id=1, source_target_pairs={{0,16},{1,17},{2,18},{3,19},{4,20},{5,21},{6,22},{7,23},{8,24},{9,... | collective-permute-start | bytes 393224 | tf_op jit(solution)/shard_map/ppermute | solution.py:327
  77.1 11.2 %collective-permute-start.4 = (bf16[1,256,256]{2,1,0:T(8,128)(2,1)S(1)}, bf16[1,256,256]{2,1,0:T(8,128)(2,1)S(1)}, u32[]{:S(2)}, u32[]{:S(2)}) collective-permute-start(bf16[1,256,256]{2,1,0:T(8,128)(2,1)S(1)} %fusion), channel_id=1, source_target_pairs={{16,0},{17,1},{18,2},{19,3},{20,4},{21,5},{22,6},{23,7},{24,8},{25... | collective-permute-start | bytes 393224 | tf_op jit(solution)/shard_map/ppermute | solution.py:340
  88.4 7.7 %collective-permute-start.14 = (bf16[2,256,256]{2,1,0:T(8,128)(2,1)S(1)}, bf16[2,256,256]{2,1,0:T(8,128)(2,1)S(1)}, u32[]{:S(2)}, u32[]{:S(2)}) collective-permute-start(bf16[2,256,256]{2,1,0:T(8,128)(2,1)S(1)} %pad_maximum_fusion.refs_0_), channel_id=1, source_target_pairs={{0,4},{1,5},{2,6},{3,7},{4,0},{5,1},{6,2},{7,3},{8,12},{9,13},{10,... | collective-permute-start | bytes 786440 | tf_op jit(solution)/shard_map/ppermute | solution.py:357
  88.9 7.4 %collective-permute-start.15 = (bf16[2,256,256]{2,1,0:T(8,128)(2,1)S(1)}, bf16[2,256,256]{2,1,0:T(8,128)(2,1)S(1)}, u32[]{:S(2)}, u32[]{:S(2)}) collective-permute-start(bf16[2,256,256]{2,1,0:T(8,128)(2,1)S(1)} %pad_maximum_fusion.refs_0_), channel_id=1, source_target_pairs={{0,8},{1,9},{2,10},{3,11},{4,12},{5,13},{6,14},{7,15},{8,0},{9,1},... | collective-permute-start | bytes 786440 | tf_op jit(solution)/shard_map/ppermute | solution.py:357
  88.9 7.8 %collective-permute-start.13 = (bf16[2,256,256]{2,1,0:T(8,128)(2,1)S(1)}, bf16[2,256,256]{2,1,0:T(8,128)(2,1)S(1)}, u32[]{:S(2)}, u32[]{:S(2)}) collective-permute-start(bf16[2,256,256]{2,1,0:T(8,128)(2,1)S(1)} %pad_maximum_fusion.refs_0_), channel_id=1, source_target_pairs={{0,2},{1,3},{2,0},{3,1},{4,6},{5,7},{6,4},{7,5},{8,10},{9,11},{10,... | collective-permute-start | bytes 786440 | tf_op jit(solution)/shard_map/ppermute | solution.py:357
  96.1 16.7 %copy-start = (bf16[2,256,256]{2,1,0:T(8,128)(2,1)}, bf16[2,256,256]{2,1,0:T(8,128)(2,1)S(1)}, u32[]{:S(2)}) copy-start(bf16[2,256,256]{2,1,0:T(8,128)(2,1)S(1)} %collective-permute-done.14.refs_2_) | copy-start | bytes 786436
  96.1 6.7 %collective-permute-start.18 = (bf16[2,256,256]{2,1,0:T(8,128)(2,1)S(1)}, bf16[2,256,256]{2,1,0:T(8,128)(2,1)S(1)}, u32[]{:S(2)}, u32[]{:S(2)}) collective-permute-start(bf16[2,256,256]{2,1,0:T(8,128)(2,1)S(1)} %collective-permute-done.14.refs_2_), channel_id=1, source_target_pairs={{0,8},{1,9},{2,10},{3,11},{4,12},{5,13},{6,14},{7,15},{8,0},{9,1},... | collective-permute-start | bytes 786440 | tf_op jit(solution)/shard_map/ppermute | solution.py:357
  96.3 16.5 %copy-start.2 = (bf16[2,256,256]{2,1,0:T(8,128)(2,1)}, bf16[2,256,256]{2,1,0:T(8,128)(2,1)S(1)}, u32[]{:S(2)}) copy-start(bf16[2,256,256]{2,1,0:T(8,128)(2,1)S(1)} %collective-permute-done.15.refs_3_) | copy-start | bytes 786436
  96.3 11.1 %collective-permute-start.17 = (bf16[2,256,256]{2,1,0:T(8,128)(2,1)S(1)}, bf16[2,256,256]{2,1,0:T(8,128)(2,1)S(1)}, u32[]{:S(2)}, u32[]{:S(2)}) collective-permute-start(bf16[2,256,256]{2,1,0:T(8,128)(2,1)S(1)} %collective-permute-done.15.refs_3_), channel_id=1, source_target_pairs={{0,2},{1,3},{2,0},{3,1},{4,6},{5,7},{6,4},{7,5},{8,10},{9,11},{10,... | collective-permute-start | bytes 786440 | tf_op jit(solution)/shard_map/ppermute | solution.py:357
  96.8 16.0 %copy-start.4 = (bf16[2,256,256]{2,1,0:T(8,128)(2,1)}, bf16[2,256,256]{2,1,0:T(8,128)(2,1)S(1)}, u32[]{:S(2)}) copy-start(bf16[2,256,256]{2,1,0:T(8,128)(2,1)S(1)} %collective-permute-done.13.refs_1_) | copy-start | bytes 786436
  96.8 11.4 %collective-permute-start.16 = (bf16[2,256,256]{2,1,0:T(8,128)(2,1)S(1)}, bf16[2,256,256]{2,1,0:T(8,128)(2,1)S(1)}, u32[]{:S(2)}, u32[]{:S(2)}) collective-permute-start(bf16[2,256,256]{2,1,0:T(8,128)(2,1)S(1)} %collective-permute-done.13.refs_1_), channel_id=1, source_target_pairs={{0,4},{1,5},{2,6},{3,7},{4,0},{5,1},{6,2},{7,3},{8,12},{9,13},{10,... | collective-permute-start | bytes 786440 | tf_op jit(solution)/shard_map/ppermute | solution.py:357
  102.8 10.1 %copy-start.6 = (bf16[2,256,256]{2,1,0:T(8,128)(2,1)}, bf16[2,256,256]{2,1,0:T(8,128)(2,1)S(1)}, u32[]{:S(2)}) copy-start(bf16[2,256,256]{2,1,0:T(8,128)(2,1)S(1)} %collective-permute-done.18.refs_2_.refs_6_) | copy-start | bytes 786436
  102.8 6.5 %collective-permute-start.19 = (bf16[2,256,256]{2,1,0:T(8,128)(2,1)S(1)}, bf16[2,256,256]{2,1,0:T(8,128)(2,1)}, u32[]{:S(2)}, u32[]{:S(2)}) collective-permute-start(bf16[2,256,256]{2,1,0:T(8,128)(2,1)S(1)} %collective-permute-done.18.refs_2_.refs_6_), channel_id=1, source_target_pairs={{0,2},{1,3},{2,0},{3,1},{4,6},{5,7},{6,4},{7,5},{8,10},{9,11},{10,... | collective-permute-start | bytes 786440 | tf_op jit(solution)/shard_map/ppermute | solution.py:357
  106.8 8.9 %copy-start.17 = (bf16[256,256]{1,0:T(8,128)(2,1)S(1)}, bf16[256,256]{1,0:T(8,128)(2,1)}, u32[]{:S(2)}) copy-start(bf16[256,256]{1,0:T(8,128)(2,1)} %refs_1_.3) | copy-start | bytes 393220
  107.3 18.7 %collective-permute-start.20 = (bf16[1024,256]{1,0:T(8,128)(2,1)S(1)}, bf16[1024,256]{1,0:T(8,128)(2,1)}, u32[]{:S(2)}, u32[]{:S(2)}) collective-permute-start(bf16[1024,256]{1,0:T(8,128)(2,1)S(1)} %pick_other.2), channel_id=1, source_target_pairs={{0,1},{1,0},{2,3},{3,2},{4,5},{5,4},{6,7},{7,6},{8,9},{9,8},{10,11... | collective-permute-start | bytes 1572872 | tf_op jit(solution)/shard_map/ppermute | solution.py:347
  112.6 13.4 %collective-permute-start.21 = (bf16[1024,256]{1,0:T(8,128)(2,1)S(1)}, bf16[1024,256]{1,0:T(8,128)(2,1)}, u32[]{:S(2)}, u32[]{:S(2)}) collective-permute-start(bf16[1024,256]{1,0:T(8,128)(2,1)S(1)} %pick_other.3), channel_id=1, source_target_pairs={{0,1},{1,0},{2,3},{3,2},{4,5},{5,4},{6,7},{7,6},{8,9},{9,8},{10,11... | collective-permute-start | bytes 1572872 | tf_op jit(solution)/shard_map/ppermute | solution.py:347
  112.8 28.9 %all-to-all-start = ((bf16[32,64,256]{2,1,0:T(8,128)(2,1)}), bf16[32,64,256]{2,1,0:T(8,128)(2,1)S(1)}, u32[]{:S(2)}, u32[]{:S(2)}) async-start(bf16[32,64,256]{2,1,0:T(8,128)(2,1)} %get-tuple-element.36), calls=%async_computation | async-start | bytes 2097152 | tf_op jit(solution)/shard_map/all_to_all | solution.py:443
  117.7 8.4 %copy-start.1 = (bf16[2,256,256]{2,1,0:T(8,128)(2,1)S(1)}, bf16[2,256,256]{2,1,0:T(8,128)(2,1)}, u32[]{:S(2)}) copy-start(bf16[2,256,256]{2,1,0:T(8,128)(2,1)} %copy-done) | copy-start | bytes 786436
  117.7 8.4 %copy-start.3 = (bf16[2,256,256]{2,1,0:T(8,128)(2,1)S(1)}, bf16[2,256,256]{2,1,0:T(8,128)(2,1)}, u32[]{:S(2)}) copy-start(bf16[2,256,256]{2,1,0:T(8,128)(2,1)} %copy-done.2) | copy-start | bytes 786436
  117.7 8.4 %copy-start.5 = (bf16[2,256,256]{2,1,0:T(8,128)(2,1)S(1)}, bf16[2,256,256]{2,1,0:T(8,128)(2,1)}, u32[]{:S(2)}) copy-start(bf16[2,256,256]{2,1,0:T(8,128)(2,1)} %copy-done.4) | copy-start | bytes 786436
  117.7 8.4 %copy-start.7 = (bf16[2,256,256]{2,1,0:T(8,128)(2,1)S(1)}, bf16[2,256,256]{2,1,0:T(8,128)(2,1)}, u32[]{:S(2)}) copy-start(bf16[2,256,256]{2,1,0:T(8,128)(2,1)} %copy-done.6) | copy-start | bytes 786436
  117.7 8.4 %copy-start.10 = (bf16[2,256,256]{2,1,0:T(8,128)(2,1)S(1)}, bf16[2,256,256]{2,1,0:T(8,128)(2,1)}, u32[]{:S(2)}) copy-start(bf16[2,256,256]{2,1,0:T(8,128)(2,1)} %copy-done.8) | copy-start | bytes 786436
  117.7 8.4 %copy-start.13 = (bf16[2,256,256]{2,1,0:T(8,128)(2,1)S(1)}, bf16[2,256,256]{2,1,0:T(8,128)(2,1)}, u32[]{:S(2)}) copy-start(bf16[2,256,256]{2,1,0:T(8,128)(2,1)} %copy-done.11) | copy-start | bytes 786436
  126.0 15.7 %copy-start.15 = (bf16[256,1024]{1,0:T(8,128)(2,1)S(1)}, bf16[256,1024]{1,0:T(8,128)(2,1)}, u32[]{:S(2)}) copy-start(bf16[256,1024]{1,0:T(8,128)(2,1)} %refs_0_.3) | copy-start | bytes 1572868
  140.1 1.3 copy-start.18
  141.7 1.6 %copy-start.19 = (f32[2,2048,128]{2,1,0:T(8,128)S(1)}, f32[2,2048,128]{2,1,0:T(8,128)}, u32[]{:S(2)}) copy-start(f32[2,2048,128]{2,1,0:T(8,128)} %copy-done.18) | copy-start | bytes 6291460
  (6 other events, 5.3 us)

commit v11 on v10

--- a/solution.py
+++ b/solution.py
@@ -146,10 +146,7 @@
 
     @pl.when(step == steps - 1)
     def _():
-        if local:
-            save_state(*work[1:], out_ref)
-        else:
-            finish(work[2], out_ref)
+        save_state(*work[1:], out_ref)
 
 
 def prefix_kernel(factor, count, steps, which_ref, q_ref, *refs):
@@ -172,7 +169,7 @@
 
     @pl.when(step == steps - 1)
     def _():
-        save_state(*work[1:], out_ref)
+        finish(work[2], out_ref)
 
 
 def pick_kernel(which_ref, *refs):
@@ -277,7 +274,7 @@
     wait_all([store(place) for place in range(chips + 2)])
 
 
-def multicast(prefix_cache, owners, readers, outgoing):
+def multicast(prefix_cache, owners, readers, outgoing, fold_first):
     replicas = lax.axis_size("replica")
     me = lax.axis_index("replica")
     half = replicas // 2
@@ -324,6 +321,7 @@
             staged[step], "replica", [(i, i ^ (2 * step)) for i in range(replicas)]
         )
         found = jnp.where((away == step)[:, None, None], passed, found)
+    found, state_now = lax.optimization_barrier((found, fold_first(outgoing[0])))
     passed = lax.ppermute(found, "replica", [(i, (i + half) % replicas) for i in range(replicas)])
     held = jnp.where((sought // half == side)[:, None, None], found, passed)
 
@@ -340,7 +338,9 @@
     passed = lax.ppermute(kept[0], "replica", [(i + half, i) for i in range(half)])
     held = jnp.concatenate([jnp.where(side == 1, kept[0], passed), held])
     wanted = jnp.stack([readers[me], readers[me ^ 1]])
-    return held, jnp.where(wanted == known, 0, wanted + (wanted < known)), outgoing
+    place = jnp.where(wanted == known, 0, wanted + (wanted < known))
+    held, last_part = lax.optimization_barrier((held, outgoing[1]))
+    return held, place, state_now, last_part
 
 
 def swap_cores(rows):
@@ -437,9 +437,7 @@
         compiler_params=COPY_PARAMS,
         name="pack_moved",
     )(mig_target, mig_block, mig_count, kv_pool)
-    held, place, outgoing = multicast(prefix_cache, owners, readers, outgoing)
-
-    def fold_moved(part, state_now):
+    def fold_moved(part, state_now=None):
         arrived = lax.all_to_all(part, "replica", split_axis=0, concat_axis=0, tiled=True)
         local = state_now is None
         rows = part.shape[1]
@@ -449,7 +447,7 @@
         keys = replicas * rows + (tokens + own_cache.shape[0]) * local
         return pl.pallas_call(
             functools.partial(moved_kernel, factor, local, steps),
-            out_shape=state if local else result,
+            out_shape=state,
             grid=(steps,),
             in_specs=[
                 whole(queries.shape),
@@ -457,14 +455,14 @@
                 pl.BlockSpec((group, rows, 2 * size), lambda i: (i, 0, 0)),
                 *([IN_SMEM, whole(own_cache.shape)] if local else [whole(state.shape)]),
             ],
-            out_specs=whole(state.shape if local else queries.shape),
+            out_specs=whole(state.shape),
             scratch_shapes=scratch(most),
             compiler_params=PARAMS,
             cost_estimate=cost(row_count, keys, size),
             name="moved_keys",
         )(queries, suffix_kv, arrived, *((ctx_len, own_cache) if local else (state_now,)))
 
-    def fold_prefix(gathered, state_now):
+    def fold_prefix(gathered, place, state_now):
         near = [gathered[step] for step in gathered if step.bit_count() < 2]
         far = [gathered[step] for step in gathered if step.bit_count() > 1]
         others = [from_other(near, place), from_other(far, place)]
@@ -475,7 +473,7 @@
             steps -= 1
         return pl.pallas_call(
             functools.partial(prefix_kernel, factor, len(gathered) + 2, steps),
-            out_shape=state,
+            out_shape=result,
             grid_spec=pltpu.PrefetchScalarGridSpec(
                 num_scalar_prefetch=1,
                 grid=(steps,),
@@ -486,7 +484,7 @@
                     *[whole(part.shape) for part in others],
                     whole(state.shape),
                 ],
-                out_specs=whole(state.shape),
+                out_specs=whole(queries.shape),
                 scratch_shapes=scratch(keys),
             ),
             compiler_params=PARAMS,
@@ -494,12 +492,13 @@
             name="prefix_keys",
         )(place, queries, *near, *far, *others, state_now)
 
-    state_now = fold_moved(outgoing[0], None)
+    held, place, state_now, last_part = multicast(
+        prefix_cache, owners, readers, outgoing, fold_moved
+    )
     gathered = {0: held}
     for step in sorted(range(1, replicas // 4), key=lambda step: (step.bit_count(), step)):
         gathered[step] = gather_step(gathered, step)
-    gathered[1], last_part = lax.optimization_barrier((gathered[1], outgoing[1]))
-    return fold_moved(last_part, fold_prefix(gathered, state_now))
+    return fold_prefix(gathered, place, fold_moved(last_part, state_now))
 
 
 def solution(mesh):

time: 151 us -> 151 us (level)
  starting transfers between devices: 47.6 us -> 54.7 us
  waiting for transfers between devices: 44.7 us -> 40.5 us
  local copies, waits for them, and re-layouts: 11.7 us -> 8.58 us
    ppermute x1, starting transfers between devices: 3.21 us -> 17.7 us  [multicast(): lax.ppermute(found, 'replica', [(i, (i + half) % replicas) for i in range...]
    ppermute x7, waiting for transfers between devices: 11 us -> 24.5 us  [gather_step(): return lax.ppermute(gathered[step ^ 1 << last], 'replica', pairs)]
    all_to_all x2, starting transfers between devices: 22 us -> 11.1 us  [fold_moved(): lax.all_to_all(part, 'replica', split_axis=0, concat_axis=0, tiled=True)]
    ppermute x7, waiting for transfers between devices: 23.5 us -> 12.7 us  [multicast(): lax.ppermute(staged[step], 'replica', [(i, i ^ 2 * step) for i in range(r...]
    ppermute x7, starting transfers between devices: 4.39 us -> 9.64 us  [gather_step(): return lax.ppermute(gathered[step ^ 1 << last], 'replica', pairs)]
    ppermute x1, waiting for transfers between devices: 7.86 us -> 3.31 us  [multicast(): lax.ppermute(found, 'replica', [(i, (i + half) % replicas) for i in range...]
    unnamed x60 -> x34, local copies, waits for them, and re-layouts: 9.66 us -> 7.32 us
    ppermute x1, waiting for transfers between devices: 2.05 us -> 0.01 us  [multicast(): lax.ppermute(kept[0], 'replica', [(i + half, i) for i in range(half)])]
  transfers between devices with their start and end apart: 24 -> 24, of which waited for: 12 -> 10; matrix products, arithmetic and copies ran while one was open for 4% -> 3% of each run, Pallas kernels for 19% -> 16%
where the time goes in v11:
time: 151 us; the launch traced here: 150 us
  starting transfers between devices  54.7 us (36%)
  waiting for transfers between devices  40.5 us (27%)
  Pallas kernels  38.8 us (26%)
  local copies, waits for them, and re-layouts  8.58 us (6%)
  between operations  3.7 us (2%)
  other arithmetic  3.43 us (2%)
    ppermute x7, waiting for transfers between devices, gather_step(): return lax.ppermute(gathered[step ^ 1 << last], 'replica', pairs)  24.5 us
    ppermute x1, starting transfers between devices, multicast(): lax.ppermute(found, 'replica', [(i, (i + half) % replicas) for i in range...  17.7 us
    pallas_call x2, Pallas kernels, fold_moved(): pl.pallas_call(functools.partial(moved_kernel, factor, local, steps), out...  14.8 us
    pallas_call x1, Pallas kernels, fold_prefix(): pl.pallas_call(functools.partial(prefix_kernel, factor, len(gathered) + 2...  14.7 us
    ppermute x7, waiting for transfers between devices, multicast(): lax.ppermute(staged[step], 'replica', [(i, i ^ 2 * step) for i in range(r...  12.7 us
    ppermute x7, starting transfers between devices, multicast(): lax.ppermute(staged[step], 'replica', [(i, i ^ 2 * step) for i in range(r...  12.1 us
    all_to_all x2, starting transfers between devices, fold_moved(): lax.all_to_all(part, 'replica', split_axis=0, concat_axis=0, tiled=True)  11.1 us
    ppermute x7, starting transfers between devices, gather_step(): return lax.ppermute(gathered[step ^ 1 << last], 'replica', pairs)  9.64 us
  transfers between devices with their start and end apart: 24, of which 10 were waited for; matrix products, arithmetic and copies ran while one was open for 3% of the time, Pallas kernels for 16%

profile of v11, /device:TPU:0, one launch (start us, length us, event | category | flops | bytes accessed | tf_op | source)
XLA Modules:
  0.0 149.8 jit_solution(447443151391496228)
XLA Ops:
  0.0 0.5 collective-permute-start
  1.1 4.0 %pack_moved.1 = (bf16[32,64,256]{2,1,0:T(8,128)(2,1)}, bf16[32,64,256]{2,1,0:T(8,128)(2,1)}) custom-call(s32[1,32]{1,0:T(1,128)} %target_ref.1, s32[1,32]{1,0:T(1,128)} %block_ref.1, s32[1]{0:T(128)S(6)} %copy.13.count_ref, bf16[32,128,256]{2,1,0:T(8,128)(2,1)} %pool_ref.1), custom_call_target="tpu_custom_call" | custom-call | tf_op jit(solution)/shard_map/pack_moved/pallas_call | solution.py:426
  5.1 7.0 %all-to-all-start = ((bf16[32,64,256]{2,1,0:T(8,128)(2,1)}), bf16[32,64,256]{2,1,0:T(8,128)(2,1)S(1)}, u32[]{:S(2)}, u32[]{:S(2)}) async-start(bf16[32,64,256]{2,1,0:T(8,128)(2,1)} %get-tuple-element.37), calls=%async_computation | async-start | bytes 2097152 | tf_op jit(solution)/shard_map/all_to_all | solution.py:441
  12.1 0.7 fusion.2
  13.5 0.6 fusion.3
  15.5 0.6 pad_add_fusion.place_ref
  16.0 3.2 %stage_prefix.1 = (bf16[1,256,256]{2,1,0:T(8,128)(2,1)}, bf16[1,256,256]{2,1,0:T(8,128)(2,1)}, bf16[1,256,256]{2,1,0:T(8,128)(2,1)}, bf16[1,256,256]{2,1,0:T(8,1...) custom-call(s32[1]{0:T(128)S(6)} %select_n.118.owner_ref, ...), custom_call_target="tpu_custom_call" | custom-call | tf_op jit(solution)/shard_map/stage_prefix/pallas_call | solution.py:297
  19.3 0.8 collective-permute-start.1
  20.3 0.8 collective-permute-start.2
  21.1 2.7 %collective-permute-start.10 = (bf16[1,256,256]{2,1,0:T(8,128)(2,1)}, bf16[1,256,256]{2,1,0:T(8,128)(2,1)S(1)}, u32[]{:S(2)}, u32[]{:S(2)}) collective-permute-start(bf16[1,256,256]{2,1,0:T(8,128)(2,1)} %get-tuple-element.34), channel_id=1, source_target_pairs={{0,12},{1,13},{2,14},{3,15},{4,8},{5,9},{6,10},{7,11},{8,4},{9,5},... | collective-permute-start | bytes 393224 | tf_op jit(solution)/shard_map/ppermute | solution.py:320
  23.8 2.4 %collective-permute-start.11 = (bf16[1,256,256]{2,1,0:T(8,128)(2,1)}, bf16[1,256,256]{2,1,0:T(8,128)(2,1)S(1)}, u32[]{:S(2)}, u32[]{:S(2)}) collective-permute-start(bf16[1,256,256]{2,1,0:T(8,128)(2,1)} %get-tuple-element.35), channel_id=1, source_target_pairs={{0,14},{1,15},{2,12},{3,13},{4,10},{5,11},{6,8},{7,9},{8,6},{9,7},... | collective-permute-start | bytes 393224 | tf_op jit(solution)/shard_map/ppermute | solution.py:320
  27.0 1.5 %collective-permute-start.6 = (bf16[1,256,256]{2,1,0:T(8,128)(2,1)}, bf16[1,256,256]{2,1,0:T(8,128)(2,1)S(1)}, u32[]{:S(2)}, u32[]{:S(2)}) collective-permute-start(bf16[1,256,256]{2,1,0:T(8,128)(2,1)} %get-tuple-element.30), channel_id=1, source_target_pairs={{0,4},{1,5},{2,6},{3,7},{4,0},{5,1},{6,2},{7,3},{8,12},{9,13},{10,... | collective-permute-start | bytes 393224 | tf_op jit(solution)/shard_map/ppermute | solution.py:320
  28.5 4.7 %collective-permute-done.10 = bf16[1,256,256]{2,1,0:T(8,128)(2,1)S(1)} collective-permute-done((bf16[1,256,256]{2,1,0:T(8,128)(2,1)}, bf16[1,256,256]{2,1,0:T(8,128)(2,1)S(1)}, u32[]{:S(2)}, u32[]{:S(2)}) %collective-permute-start.10) | collective-permute-done | bytes 131104 | tf_op jit(solution)/shard_map/ppermute | solution.py:320
  33.2 2.6 %collective-permute-start.7 = (bf16[1,256,256]{2,1,0:T(8,128)(2,1)}, bf16[1,256,256]{2,1,0:T(8,128)(2,1)S(1)}, u32[]{:S(2)}, u32[]{:S(2)}) collective-permute-start(bf16[1,256,256]{2,1,0:T(8,128)(2,1)} %get-tuple-element.31), channel_id=1, source_target_pairs={{0,6},{1,7},{2,4},{3,5},{4,2},{5,3},{6,0},{7,1},{8,14},{9,15},{10,... | collective-permute-start | bytes 393224 | tf_op jit(solution)/shard_map/ppermute | solution.py:320
  35.8 2.9 %collective-permute-done.11 = bf16[1,256,256]{2,1,0:T(8,128)(2,1)S(1)} collective-permute-done((bf16[1,256,256]{2,1,0:T(8,128)(2,1)}, bf16[1,256,256]{2,1,0:T(8,128)(2,1)S(1)}, u32[]{:S(2)}, u32[]{:S(2)}) %collective-permute-start.11) | collective-permute-done | bytes 131104 | tf_op jit(solution)/shard_map/ppermute | solution.py:320
  38.7 2.8 %collective-permute-start.8 = (bf16[1,256,256]{2,1,0:T(8,128)(2,1)}, bf16[1,256,256]{2,1,0:T(8,128)(2,1)S(1)}, u32[]{:S(2)}, u32[]{:S(2)}) collective-permute-start(bf16[1,256,256]{2,1,0:T(8,128)(2,1)} %get-tuple-element.32), channel_id=1, source_target_pairs={{0,8},{1,9},{2,10},{3,11},{4,12},{5,13},{6,14},{7,15},{8,0},{9,1},... | collective-permute-start | bytes 393224 | tf_op jit(solution)/shard_map/ppermute | solution.py:320
  41.5 0.7 collective-permute-start.3
  42.2 3.8 %collective-permute-done.8 = bf16[1,256,256]{2,1,0:T(8,128)(2,1)S(1)} collective-permute-done((bf16[1,256,256]{2,1,0:T(8,128)(2,1)}, bf16[1,256,256]{2,1,0:T(8,128)(2,1)S(1)}, u32[]{:S(2)}, u32[]{:S(2)}) %collective-permute-start.8) | collective-permute-done | bytes 131104 | tf_op jit(solution)/shard_map/ppermute | solution.py:320
  46.0 1.3 collective-permute-done.9
  47.4 1.3 collective-permute-start.4
  48.8 8.3 %moved_keys.2.refs_3_ = f32[2,2048,128]{2,1,0:T(8,128)S(1)} custom-call(bf16[256,1024]{1,0:T(8,128)(2,1)S(1)} %copy-done.6, bf16[256,256]{1,0:T(8,128)(2,1)S(1)} %copy-done.9, bf16[32,64,256]{2,1,0:T(8,128)(2,1)S(1)} %all-to-all-done.refs_2_, s32[1]{0:T(128)S(6)} %copy.12.refs_3_, bf16[512,256]{1,0:T(8,128)(2,1)S(1)} %copy-done.8), custom_call_target="tpu_custom_call" | custom-call | flops 8858370048 | bytes 1441792 | tf_op jit(solution)/shard_map/moved_keys/pallas_call | solution.py:448
  57.1 1.3 copy-done.10
  58.4 17.7 %collective-permute-start.12 = (bf16[1,256,256]{2,1,0:T(8,128)(2,1)S(1)}, bf16[1,256,256]{2,1,0:T(8,128)(2,1)S(1)}, u32[]{:S(2)}, u32[]{:S(2)}) collective-permute-start(bf16[1,256,256]{2,1,0:T(8,128)(2,1)S(1)} %select_select_fusion), channel_id=1, source_target_pairs={{0,16},{1,17},{2,18},{3,19},{4,20},{5,21},{6,22},{7,23},{8,24},{9,... | collective-permute-start | bytes 393224 | tf_op jit(solution)/shard_map/ppermute | solution.py:325
  76.2 3.3 %collective-permute-done.12 = bf16[1,256,256]{2,1,0:T(8,128)(2,1)S(1)} collective-permute-done((bf16[1,256,256]{2,1,0:T(8,128)(2,1)S(1)}, bf16[1,256,256]{2,1,0:T(8,128)(2,1)S(1)}, u32[]{:S(2)}, u32[]{:S(2)}) %collective-permute-start.12) | collective-permute-done | bytes 131104 | tf_op jit(solution)/shard_map/ppermute | solution.py:325
  79.5 4.0 %all-to-all-start.1 = ((bf16[32,64,256]{2,1,0:T(8,128)(2,1)}), bf16[32,64,256]{2,1,0:T(8,128)(2,1)S(1)}, u32[]{:S(2)}, u32[]{:S(2)}) async-start(bf16[32,64,256]{2,1,0:T(8,128)(2,1)} %get-tuple-element.41), calls=%async_computation.1 | async-start | bytes 2097152 | tf_op jit(solution)/shard_map/all_to_all | solution.py:441
  83.6 1.7 %collective-permute-start.14 = (bf16[2,256,256]{2,1,0:T(8,128)(2,1)S(1)}, bf16[2,256,256]{2,1,0:T(8,128)(2,1)S(1)}, u32[]{:S(2)}, u32[]{:S(2)}) collective-permute-start(bf16[2,256,256]{2,1,0:T(8,128)(2,1)S(1)} %pad_maximum_fusion.refs_0_), channel_id=1, source_target_pairs={{0,4},{1,5},{2,6},{3,7},{4,0},{5,1},{6,2},{7,3},{8,12},{9,13},{10,... | collective-permute-start | bytes 786440 | tf_op jit(solution)/shard_map/ppermute | solution.py:357
  85.3 1.5 collective-permute-start.13
  86.7 1.5 collective-permute-start.15
  88.2 12.6 %collective-permute-done.14.refs_2_ = bf16[2,256,256]{2,1,0:T(8,128)(2,1)S(1)} collective-permute-done((bf16[2,256,256]{2,1,0:T(8,128)(2,1)S(1)}, bf16[2,256,256]{2,1,0:T(8,128)(2,1)S(1)}, u32[]{:S(2)}, u32[]{:S(2)}) %collective-permute-start.14) | collective-permute-done | bytes 262176 | tf_op jit(solution)/shard_map/ppermute | solution.py:357
  100.7 0.7 collective-permute-start.18
  101.7 1.1 collective-permute-start.16
  102.8 5.0 %collective-permute-done.15.refs_3_ = bf16[2,256,256]{2,1,0:T(8,128)(2,1)S(1)} collective-permute-done((bf16[2,256,256]{2,1,0:T(8,128)(2,1)S(1)}, bf16[2,256,256]{2,1,0:T(8,128)(2,1)S(1)}, u32[]{:S(2)}, u32[]{:S(2)}) %collective-permute-start.15) | collective-permute-done | bytes 262176 | tf_op jit(solution)/shard_map/ppermute | solution.py:357
  107.9 1.8 %collective-permute-start.17 = (bf16[2,256,256]{2,1,0:T(8,128)(2,1)S(1)}, bf16[2,256,256]{2,1,0:T(8,128)(2,1)S(1)}, u32[]{:S(2)}, u32[]{:S(2)}) collective-permute-start(bf16[2,256,256]{2,1,0:T(8,128)(2,1)S(1)} %collective-permute-done.15.refs_3_), channel_id=1, source_target_pairs={{0,2},{1,3},{2,0},{3,1},{4,6},{5,7},{6,4},{7,5},{8,10},{9,11},{10,... | collective-permute-start | bytes 786440 | tf_op jit(solution)/shard_map/ppermute | solution.py:357
  109.6 4.7 %collective-permute-done.18.refs_2_.refs_6_ = bf16[2,256,256]{2,1,0:T(8,128)(2,1)S(1)} collective-permute-done((bf16[2,256,256]{2,1,0:T(8,128)(2,1)S(1)}, bf16[2,256,256]{2,1,0:T(8,128)(2,1)S(1)}, u32[]{:S(2)}, u32[]{:S(2)}) %collective-permute-start.18) | collective-permute-done | bytes 262176 | tf_op jit(solution)/shard_map/ppermute | solution.py:357
  114.4 1.5 collective-permute-start.19
  115.8 0.6 fusion.4
  116.4 1.9 %compare_select_fusion.which_ref = s32[2]{0:T(128)S(1)} fusion(s32[1]{0:T(128)} %get-tuple-element.46, s32[1]{0:T(128)} %get-tuple-element.45, s32[]{:T(128)} %fusion.2), kind=kLoop, calls=%fused_computation.9 | loop fusion | flops 12 | bytes 20 | tf_op jit(solution)/shard_map/jit(_where)/select_n | solution.py:341
  118.3 0.6 pick_other.2
  119.0 0.7 copy-done
  119.7 0.7 copy-done.3
  120.4 1.9 %collective-permute-done.19.refs_3_.refs_7_ = bf16[2,256,256]{2,1,0:T(8,128)(2,1)} collective-permute-done((bf16[2,256,256]{2,1,0:T(8,128)(2,1)S(1)}, bf16[2,256,256]{2,1,0:T(8,128)(2,1)}, u32[]{:S(2)}, u32[]{:S(2)}) %collective-permute-start.19) | collective-permute-done | bytes 262176 | tf_op jit(solution)/shard_map/ppermute | solution.py:357
  122.3 0.9 copy-done.1
  123.3 0.9 copy-done.4
  124.2 1.5 pick_other.3
  125.8 1.0 copy-done.7
  126.8 1.6 %copy-done.11 = f32[2,2048,128]{2,1,0:T(8,128)S(1)} copy-done((f32[2,2048,128]{2,1,0:T(8,128)S(1)}, f32[2,2048,128]{2,1,0:T(8,128)}, u32[]{:S(2)}) %copy-start.11) | copy-done | bytes 2097176
  128.4 6.6 %moved_keys.3.refs_10_ = f32[2,2048,128]{2,1,0:T(8,128)S(1)} custom-call(bf16[256,1024]{1,0:T(8,128)(2,1)S(1)} %copy-done.7, bf16[256,256]{1,0:T(8,128)(2,1)S(1)} %copy-done.9, bf16[32,64,256]{2,1,0:T(8,128)(2,1)S(1)} %all-to-all-done.1.refs_2_, f32[2,2048,128]{2,1,0:T(8,128)S(1)} %copy-done.11), custom_call_target="tpu_custom_call" | custom-call | flops 6442450944 | bytes 1048576 | tf_op jit(solution)/shard_map/moved_keys/pallas_call | solution.py:448
  135.1 14.7 %prefix_keys.1 = bf16[256,1024]{1,0:T(8,128)(2,1)} custom-call(s32[2]{0:T(128)S(1)} %compare_select_fusion.which_ref, bf16[256,1024]{1,0:T(8,128)(2,1)S(1)} %copy-done.7, bf16[2,256,256]{2,1,0:T(8,128)(2,1)S(1)} %pad_maximum_fusion.refs_0_, bf16[2,256,256]{2,1,0:T(8,128)(2,1)S(1)} %collective-permute-done.13.refs_1_, ...), custom_call_target="tpu_custom_call" | custom-call | flops 12884901888 | bytes 2097152 | tf_op jit(solution)/shard_map/prefix_keys/pallas_call | solution.py:474
  (56 shorter events, 0.9 us)
Async XLA Ops:
  0.0 5.1 %collective-permute-start = (bf16[4096,256]{1,0:T(8,128)(2,1)}, bf16[4096,256]{1,0:T(8,128)(2,1)S(1)}, u32[]{:S(2)}, u32[]{:S(2)}) collective-permute-start(bf16[4096,256]{1,0:T(8,128)(2,1)} %param.15), channel_id=1, source_target_pairs={{0,1},{1,0},{2,3},{3,2},{4,5},{5,4},{6,7},{7,6},{8,9},{9,8},{10,11... | collective-permute-start | bytes 6291464 | tf_op jit(solution)/shard_map/ppermute | solution.py:347
  1.1 11.0 %copy-start.15 = (s32[2]{0:T(128)S(1)}, s32[2]{0:T(128)}, u32[]{:S(2)}) copy-start(s32[2]{0:T(128)} %param.16) | copy-start | bytes 28
  5.1 10.9 %copy-start.12 = (bf16[4096,256]{1,0:T(8,128)(2,1)}, bf16[4096,256]{1,0:T(8,128)(2,1)S(1)}, u32[]{:S(2)}) copy-start(bf16[4096,256]{1,0:T(8,128)(2,1)S(1)} %collective-permute-done) | copy-start | bytes 6291460
  5.1 43.6 %all-to-all-start = ((bf16[32,64,256]{2,1,0:T(8,128)(2,1)}), bf16[32,64,256]{2,1,0:T(8,128)(2,1)S(1)}, u32[]{:S(2)}, u32[]{:S(2)}) async-start(bf16[32,64,256]{2,1,0:T(8,128)(2,1)} %get-tuple-element.37), calls=%async_computation | async-start | bytes 2097152 | tf_op jit(solution)/shard_map/all_to_all | solution.py:441
  19.2 22.2 %copy-start.16 = (bf16[1,256,256]{2,1,0:T(8,128)(2,1)S(1)}, bf16[1,256,256]{2,1,0:T(8,128)(2,1)}, u32[]{:S(2)}) copy-start(bf16[1,256,256]{2,1,0:T(8,128)(2,1)} %get-tuple-element.33) | copy-start | bytes 393220
  19.3 28.1 %copy-start.13 = (bf16[1,256,256]{2,1,0:T(8,128)(2,1)S(1)}, bf16[1,256,256]{2,1,0:T(8,128)(2,1)}, u32[]{:S(2)}) copy-start(bf16[1,256,256]{2,1,0:T(8,128)(2,1)} %get-tuple-element.36) | copy-start | bytes 393220
  19.3 0.8 collective-permute-start.1
  20.1 28.6 %copy-start.6 = (bf16[256,1024]{1,0:T(8,128)(2,1)S(1)}, bf16[256,1024]{1,0:T(8,128)(2,1)}, u32[]{:S(2)}) copy-start(bf16[256,1024]{1,0:T(8,128)(2,1)} %q_ref.1) | copy-start | bytes 1572868
  20.1 28.6 %copy-start.8 = (bf16[512,256]{1,0:T(8,128)(2,1)S(1)}, bf16[512,256]{1,0:T(8,128)(2,1)}, u32[]{:S(2)}) copy-start(bf16[512,256]{1,0:T(8,128)(2,1)} %refs_4_.1) | copy-start | bytes 786436
  20.1 28.6 %copy-start.9 = (bf16[256,256]{1,0:T(8,128)(2,1)S(1)}, bf16[256,256]{1,0:T(8,128)(2,1)}, u32[]{:S(2)}) copy-start(bf16[256,256]{1,0:T(8,128)(2,1)} %refs_1_.3) | copy-start | bytes 393220
  20.3 21.2 %collective-permute-start.2 = (bf16[2,1,256,256]{3,2,1,0:T(8,128)(2,1)S(1)}, bf16[2,1,256,256]{3,2,1,0:T(8,128)(2,1)S(1)}, u32[]{:S(2)}, u32[]{:S(2)}) collective-permute-start(bf16[2,1,256,256]{3,2,1,0:T(8,128)(2,1)S(1)} %slice.29), channel_id=1, source_target_pairs={{28,24},{29,25},{30,26},{31,27}} | collective-permute-start | bytes 786440 | tf_op jit(solution)/shard_map/ppermute | solution.py:333
  21.1 12.1 %collective-permute-start.10 = (bf16[1,256,256]{2,1,0:T(8,128)(2,1)}, bf16[1,256,256]{2,1,0:T(8,128)(2,1)S(1)}, u32[]{:S(2)}, u32[]{:S(2)}) collective-permute-start(bf16[1,256,256]{2,1,0:T(8,128)(2,1)} %get-tuple-element.34), channel_id=1, source_target_pairs={{0,12},{1,13},{2,14},{3,15},{4,8},{5,9},{6,10},{7,11},{8,4},{9,5},... | collective-permute-start | bytes 393224 | tf_op jit(solution)/shard_map/ppermute | solution.py:320
  23.8 14.9 %collective-permute-start.11 = (bf16[1,256,256]{2,1,0:T(8,128)(2,1)}, bf16[1,256,256]{2,1,0:T(8,128)(2,1)S(1)}, u32[]{:S(2)}, u32[]{:S(2)}) collective-permute-start(bf16[1,256,256]{2,1,0:T(8,128)(2,1)} %get-tuple-element.35), channel_id=1, source_target_pairs={{0,14},{1,15},{2,12},{3,13},{4,10},{5,11},{6,8},{7,9},{8,6},{9,7},... | collective-permute-start | bytes 393224 | tf_op jit(solution)/shard_map/ppermute | solution.py:320
  26.9 14.6 %collective-permute-start.5 = (bf16[1,256,256]{2,1,0:T(8,128)(2,1)}, bf16[1,256,256]{2,1,0:T(8,128)(2,1)S(1)}, u32[]{:S(2)}, u32[]{:S(2)}) collective-permute-start(bf16[1,256,256]{2,1,0:T(8,128)(2,1)} %get-tuple-element.29), channel_id=1, source_target_pairs={{0,2},{1,3},{2,0},{3,1},{4,6},{5,7},{6,4},{7,5},{8,10},{9,11},{10,... | collective-permute-start | bytes 393224 | tf_op jit(solution)/shard_map/ppermute | solution.py:320
  27.0 15.2 %collective-permute-start.6 = (bf16[1,256,256]{2,1,0:T(8,128)(2,1)}, bf16[1,256,256]{2,1,0:T(8,128)(2,1)S(1)}, u32[]{:S(2)}, u32[]{:S(2)}) collective-permute-start(bf16[1,256,256]{2,1,0:T(8,128)(2,1)} %get-tuple-element.30), channel_id=1, source_target_pairs={{0,4},{1,5},{2,6},{3,7},{4,0},{5,1},{6,2},{7,3},{8,12},{9,13},{10,... | collective-permute-start | bytes 393224 | tf_op jit(solution)/shard_map/ppermute | solution.py:320
  33.2 9.0 %collective-permute-start.7 = (bf16[1,256,256]{2,1,0:T(8,128)(2,1)}, bf16[1,256,256]{2,1,0:T(8,128)(2,1)S(1)}, u32[]{:S(2)}, u32[]{:S(2)}) collective-permute-start(bf16[1,256,256]{2,1,0:T(8,128)(2,1)} %get-tuple-element.31), channel_id=1, source_target_pairs={{0,6},{1,7},{2,4},{3,5},{4,2},{5,3},{6,0},{7,1},{8,14},{9,15},{10,... | collective-permute-start | bytes 393224 | tf_op jit(solution)/shard_map/ppermute | solution.py:320
  38.7 7.4 %collective-permute-start.8 = (bf16[1,256,256]{2,1,0:T(8,128)(2,1)}, bf16[1,256,256]{2,1,0:T(8,128)(2,1)S(1)}, u32[]{:S(2)}, u32[]{:S(2)}) collective-permute-start(bf16[1,256,256]{2,1,0:T(8,128)(2,1)} %get-tuple-element.32), channel_id=1, source_target_pairs={{0,8},{1,9},{2,10},{3,11},{4,12},{5,13},{6,14},{7,15},{8,0},{9,1},... | collective-permute-start | bytes 393224 | tf_op jit(solution)/shard_map/ppermute | solution.py:320
  41.4 5.9 %collective-permute-start.9 = (bf16[1,256,256]{2,1,0:T(8,128)(2,1)S(1)}, bf16[1,256,256]{2,1,0:T(8,128)(2,1)S(1)}, u32[]{:S(2)}, u32[]{:S(2)}) collective-permute-start(bf16[1,256,256]{2,1,0:T(8,128)(2,1)S(1)} %copy-done.16), channel_id=1, source_target_pairs={{0,10},{1,11},{2,8},{3,9},{4,14},{5,15},{6,12},{7,13},{8,2},{9,3},... | collective-permute-start | bytes 393224 | tf_op jit(solution)/shard_map/ppermute | solution.py:320
  41.5 5.9 %collective-permute-start.3 = (bf16[1,1,256,256]{3,2,1,0:T(8,128)(2,1)S(1)}, bf16[1,1,256,256]{3,2,1,0:T(8,128)(2,1)S(1)}, u32[]{:S(2)}, u32[]{:S(2)}) collective-permute-start(bf16[1,1,256,256]{3,2,1,0:T(8,128)(2,1)S(1)} %slice.31), channel_id=1, source_target_pairs={{24,16},{25,17},{26,18},{27,19},{28,20},{29,21},{30,22},{31,23}} | collective-permute-start | bytes 393224 | tf_op jit(solution)/shard_map/ppermute | solution.py:333
  47.4 28.7 %collective-permute-start.4 = (bf16[1,256,256]{2,1,0:T(8,128)(2,1)S(1)}, bf16[1,256,256]{2,1,0:T(8,128)(2,1)S(1)}, u32[]{:S(2)}, u32[]{:S(2)}) collective-permute-start(bf16[1,256,256]{2,1,0:T(8,128)(2,1)S(1)} %fusion), channel_id=1, source_target_pairs={{16,0},{17,1},{18,2},{19,3},{20,4},{21,5},{22,6},{23,7},{24,8},{25... | collective-permute-start | bytes 393224 | tf_op jit(solution)/shard_map/ppermute | solution.py:338
  57.1 1.4 copy-start.10
  58.4 57.4 %copy-start.14 = (s32[32]{0:T(128)S(1)}, s32[32]{0:T(128)}, u32[]{:S(2)}) copy-start(s32[32]{0:T(128)} %param.17) | copy-start | bytes 388
  58.4 21.1 %collective-permute-start.12 = (bf16[1,256,256]{2,1,0:T(8,128)(2,1)S(1)}, bf16[1,256,256]{2,1,0:T(8,128)(2,1)S(1)}, u32[]{:S(2)}, u32[]{:S(2)}) collective-permute-start(bf16[1,256,256]{2,1,0:T(8,128)(2,1)S(1)} %select_select_fusion), channel_id=1, source_target_pairs={{0,16},{1,17},{2,18},{3,19},{4,20},{5,21},{6,22},{7,23},{8,24},{9,... | collective-permute-start | bytes 393224 | tf_op jit(solution)/shard_map/ppermute | solution.py:325
  79.5 46.2 %all-to-all-start.1 = ((bf16[32,64,256]{2,1,0:T(8,128)(2,1)}), bf16[32,64,256]{2,1,0:T(8,128)(2,1)S(1)}, u32[]{:S(2)}, u32[]{:S(2)}) async-start(bf16[32,64,256]{2,1,0:T(8,128)(2,1)} %get-tuple-element.41), calls=%async_computation.1 | async-start | bytes 2097152 | tf_op jit(solution)/shard_map/all_to_all | solution.py:441
  83.6 17.2 %collective-permute-start.14 = (bf16[2,256,256]{2,1,0:T(8,128)(2,1)S(1)}, bf16[2,256,256]{2,1,0:T(8,128)(2,1)S(1)}, u32[]{:S(2)}, u32[]{:S(2)}) collective-permute-start(bf16[2,256,256]{2,1,0:T(8,128)(2,1)S(1)} %pad_maximum_fusion.refs_0_), channel_id=1, source_target_pairs={{0,4},{1,5},{2,6},{3,7},{4,0},{5,1},{6,2},{7,3},{8,12},{9,13},{10,... | collective-permute-start | bytes 786440 | tf_op jit(solution)/shard_map/ppermute | solution.py:357
  85.3 16.5 %collective-permute-start.13 = (bf16[2,256,256]{2,1,0:T(8,128)(2,1)S(1)}, bf16[2,256,256]{2,1,0:T(8,128)(2,1)S(1)}, u32[]{:S(2)}, u32[]{:S(2)}) collective-permute-start(bf16[2,256,256]{2,1,0:T(8,128)(2,1)S(1)} %pad_maximum_fusion.refs_0_), channel_id=1, source_target_pairs={{0,2},{1,3},{2,0},{3,1},{4,6},{5,7},{6,4},{7,5},{8,10},{9,11},{10,... | collective-permute-start | bytes 786440 | tf_op jit(solution)/shard_map/ppermute | solution.py:357
  86.7 21.1 %collective-permute-start.15 = (bf16[2,256,256]{2,1,0:T(8,128)(2,1)S(1)}, bf16[2,256,256]{2,1,0:T(8,128)(2,1)S(1)}, u32[]{:S(2)}, u32[]{:S(2)}) collective-permute-start(bf16[2,256,256]{2,1,0:T(8,128)(2,1)S(1)} %pad_maximum_fusion.refs_0_), channel_id=1, source_target_pairs={{0,8},{1,9},{2,10},{3,11},{4,12},{5,13},{6,14},{7,15},{8,0},{9,1},... | collective-permute-start | bytes 786440 | tf_op jit(solution)/shard_map/ppermute | solution.py:357
  100.7 13.6 %collective-permute-start.18 = (bf16[2,256,256]{2,1,0:T(8,128)(2,1)S(1)}, bf16[2,256,256]{2,1,0:T(8,128)(2,1)S(1)}, u32[]{:S(2)}, u32[]{:S(2)}) collective-permute-start(bf16[2,256,256]{2,1,0:T(8,128)(2,1)S(1)} %collective-permute-done.14.refs_2_), channel_id=1, source_target_pairs={{0,8},{1,9},{2,10},{3,11},{4,12},{5,13},{6,14},{7,15},{8,0},{9,1},... | collective-permute-start | bytes 786440 | tf_op jit(solution)/shard_map/ppermute | solution.py:357
  101.7 17.3 %collective-permute-start.16 = (bf16[2,256,256]{2,1,0:T(8,128)(2,1)S(1)}, bf16[2,256,256]{2,1,0:T(8,128)(2,1)S(1)}, u32[]{:S(2)}, u32[]{:S(2)}) collective-permute-start(bf16[2,256,256]{2,1,0:T(8,128)(2,1)S(1)} %collective-permute-done.13.refs_1_), channel_id=1, source_target_pairs={{0,4},{1,5},{2,6},{3,7},{4,0},{5,1},{6,2},{7,3},{8,12},{9,13},{10,... | collective-permute-start | bytes 786440 | tf_op jit(solution)/shard_map/ppermute | solution.py:357
  107.9 11.9 %collective-permute-start.17 = (bf16[2,256,256]{2,1,0:T(8,128)(2,1)S(1)}, bf16[2,256,256]{2,1,0:T(8,128)(2,1)S(1)}, u32[]{:S(2)}, u32[]{:S(2)}) collective-permute-start(bf16[2,256,256]{2,1,0:T(8,128)(2,1)S(1)} %collective-permute-done.15.refs_3_), channel_id=1, source_target_pairs={{0,2},{1,3},{2,0},{3,1},{4,6},{5,7},{6,4},{7,5},{8,10},{9,11},{10,... | collective-permute-start | bytes 786440 | tf_op jit(solution)/shard_map/ppermute | solution.py:357
  114.4 8.0 %collective-permute-start.19 = (bf16[2,256,256]{2,1,0:T(8,128)(2,1)S(1)}, bf16[2,256,256]{2,1,0:T(8,128)(2,1)}, u32[]{:S(2)}, u32[]{:S(2)}) collective-permute-start(bf16[2,256,256]{2,1,0:T(8,128)(2,1)S(1)} %collective-permute-done.18.refs_2_.refs_6_), channel_id=1, source_target_pairs={{0,2},{1,3},{2,0},{3,1},{4,6},{5,7},{6,4},{7,5},{8,10},{9,11},{10,... | collective-permute-start | bytes 786440 | tf_op jit(solution)/shard_map/ppermute | solution.py:357
  118.9 16.1 %collective-permute-start.20 = (bf16[1024,256]{1,0:T(8,128)(2,1)S(1)}, bf16[1024,256]{1,0:T(8,128)(2,1)}, u32[]{:S(2)}, u32[]{:S(2)}) collective-permute-start(bf16[1024,256]{1,0:T(8,128)(2,1)S(1)} %pick_other.2), channel_id=1, source_target_pairs={{0,1},{1,0},{2,3},{3,2},{4,5},{5,4},{6,7},{7,6},{8,9},{9,8},{10,11... | collective-permute-start | bytes 1572872 | tf_op jit(solution)/shard_map/ppermute | solution.py:347
  119.0 0.7 copy-start
  119.7 0.7 copy-start.3
  122.3 1.0 copy-start.1
  123.3 0.9 copy-start.4
  125.7 9.3 %collective-permute-start.21 = (bf16[1024,256]{1,0:T(8,128)(2,1)S(1)}, bf16[1024,256]{1,0:T(8,128)(2,1)}, u32[]{:S(2)}, u32[]{:S(2)}) collective-permute-start(bf16[1024,256]{1,0:T(8,128)(2,1)S(1)} %pick_other.3), channel_id=1, source_target_pairs={{0,1},{1,0},{2,3},{3,2},{4,5},{5,4},{6,7},{7,6},{8,9},{9,8},{10,11... | collective-permute-start | bytes 1572872 | tf_op jit(solution)/shard_map/ppermute | solution.py:347
  125.8 1.0 copy-start.7
  126.8 1.6 %copy-start.11 = (f32[2,2048,128]{2,1,0:T(8,128)S(1)}, f32[2,2048,128]{2,1,0:T(8,128)}, u32[]{:S(2)}) copy-start(f32[2,2048,128]{2,1,0:T(8,128)} %copy-done.10) | copy-start | bytes 6291460
  128.4 6.6 %copy-start.2 = (bf16[2,256,256]{2,1,0:T(8,128)(2,1)S(1)}, bf16[2,256,256]{2,1,0:T(8,128)(2,1)}, u32[]{:S(2)}) copy-start(bf16[2,256,256]{2,1,0:T(8,128)(2,1)} %copy-done) | copy-start | bytes 786436
  128.4 6.6 %copy-start.5 = (bf16[2,256,256]{2,1,0:T(8,128)(2,1)S(1)}, bf16[2,256,256]{2,1,0:T(8,128)(2,1)}, u32[]{:S(2)}) copy-start(bf16[2,256,256]{2,1,0:T(8,128)(2,1)} %copy-done.3) | copy-start | bytes 786436

commit v12 on v11

v12 whole, which is shorter than its diff:
```python
import functools

import jax
import jax.numpy as jnp
from jax import lax
from jax.experimental import pallas as pl
from jax.experimental.pallas import tpu as pltpu
from jax.sharding import PartitionSpec as P

LOG2E = 1.4426950408889634
DEAD_MARK = 1024.0
DEAD_ABOVE = 512.0
NEG = -1e30
CHUNK = 1024
ROWS = 512
PARAMS = pltpu.CompilerParams(vmem_limit_bytes=44 * 1024 * 1024)
COPY_PARAMS = pltpu.CompilerParams(vmem_limit_bytes=60 * 1024 * 1024)

IN_SMEM = pl.BlockSpec(memory_space=pltpu.SMEM)
IN_HBM = pl.BlockSpec(memory_space=pltpu.HBM)


def fold_keys(work, keys, values, factor, bias=None):
    q_ref, max_ref, lanes_ref, sums_ref = work
    count, size = sums_ref.shape
    block = min(ROWS, count)
    groups = keys.shape[0] // size

    def score(first):
        scores = lax.dot_general(
            q_ref[first:first + block, :],
            keys,
            (((1,), (1,)), ((), ())),
            preferred_element_type=jnp.float32,
        )
        return scores if bias is None else scores + bias

    following = score(0)
    for first in range(0, count, block):
        here = slice(first, first + block)
        scores, following = following, score(first + block) if first + block < count else None
        old_max = max_ref[here]
        new_max = jnp.maximum(old_max, jnp.max(scores, axis=1, keepdims=True))
        shrink = jnp.exp2((old_max - new_max) * factor)
        weights = jnp.exp2((scores - jnp.tile(new_max, (1, groups))) * factor)
        lanes = weights[:, :size]
        for group in range(1, groups):
            lanes += weights[:, group * size:(group + 1) * size]
        max_ref[here] = new_max
        lanes_ref[here] = lanes_ref[here] * shrink + lanes
        sums_ref[here] = sums_ref[here] * shrink + jnp.dot(
            weights.astype(jnp.bfloat16), values, preferred_element_type=jnp.float32
        )


def stack_queries(q_ref, stacked_ref):
    tokens, width = q_ref.shape
    size = stacked_ref.shape[1]
    for head in range(width // size):
        stacked_ref[head * tokens:(head + 1) * tokens, :] = q_ref[:, head * size:(head + 1) * size]


def load_state(loaded_ref, max_ref, lanes_ref, sums_ref):
    count, size = max_ref.shape
    lane = lax.broadcasted_iota(jnp.int32, (count, size), 1)
    sums_ref[...] = loaded_ref[0]
    lanes_ref[...] = jnp.where(lane == 0, loaded_ref[1], 0.0)
    max_ref[...] = jnp.broadcast_to(loaded_ref[1, :, size - 1:], (count, size))


def save_state(max_ref, lanes_ref, sums_ref, saved_ref):
    count, size = max_ref.shape
    left = lax.broadcasted_iota(jnp.int32, (count, size), 1) < size // 2
    saved_ref[0] = sums_ref[...]
    saved_ref[1] = jnp.where(left, jnp.sum(lanes_ref[...], axis=1, keepdims=True), max_ref[...])


def finish(lanes_ref, sums_ref, out_ref):
    tokens = out_ref.shape[0]
    size = sums_ref.shape[1]
    for head in range(out_ref.shape[1] // size):
        here = slice(head * tokens, (head + 1) * tokens)
        out_ref[:, head * size:(head + 1) * size] = (
            sums_ref[here] / jnp.sum(lanes_ref[here], axis=1, keepdims=True)
        ).astype(out_ref.dtype)


def local_kernel(factor, len_ref, q_ref, suffix_ref, own_ref, out_ref, *work):
    q_stacked, max_ref, lanes_ref, sums_ref = work
    size = sums_ref.shape[1]
    suffix, own = suffix_ref.shape[0], own_ref.shape[0]
    stack_queries(q_ref, q_stacked)
    max_ref[...] = jnp.full(max_ref.shape, NEG, jnp.float32)
    lanes_ref[...] = jnp.zeros(lanes_ref.shape, jnp.float32)
    sums_ref[...] = jnp.zeros(sums_ref.shape, jnp.float32)
    block = min(ROWS, sums_ref.shape[0])
    token = lax.broadcasted_iota(jnp.int32, (block, suffix), 0) % suffix
    key = lax.broadcasted_iota(jnp.int32, (block, suffix), 1)
    causal = jnp.where(key <= token, 0.0, NEG)
    fold_keys(work, suffix_ref[:, :size], suffix_ref[:, size:], factor, causal)
    dead = jnp.where(lax.broadcasted_iota(jnp.int32, (1, own), 1) < len_ref[0], 0.0, NEG)
    fold_keys(work, own_ref[:, :size], own_ref[:, size:], factor, dead)
    save_state(max_ref, lanes_ref, sums_ref, out_ref)


def moved_kernel(factor, steps, q_ref, kv_ref, loaded_ref, out_ref, *work):
    step = pl.program_id(0)
    size = work[3].shape[1]

    @pl.when(step == 0)
    def _():
        stack_queries(q_ref, work[0])
        load_state(loaded_ref, *work[1:])

    rows = kv_ref[...].reshape(-1, kv_ref.shape[-1])
    dead = jnp.where(rows[:, size:].astype(jnp.float32) > DEAD_ABOVE, NEG, 0.0).T[:1]
    fold_keys(work, rows[:, :size], rows[:, size:], factor, dead)

    @pl.when(step == steps - 1)
    def _():
        save_state(*work[1:], out_ref)


def prefix_kernel(factor, count, steps, which_ref, q_ref, *refs):
    pieces = refs[:count]
    loaded_ref, out_ref, *work, rows_ref = refs[count:]
    step = pl.program_id(0)
    size = work[3].shape[1]
    chunk = rows_ref.shape[0] // steps

    @pl.when(step == 0)
    def _():
        stack_queries(q_ref, work[0])
        place = 0
        for piece in pieces:
            rows_ref[pl.ds(place, piece.shape[0]), :] = piece[...]
            place += piece.shape[0]
        load_state(loaded_ref, *work[1:])

    rows = pl.ds(pl.multiple_of(step * chunk, size), chunk)
    fold_keys(work, rows_ref[rows, :size], rows_ref[rows, size:], factor)

    @pl.when(step == steps - 1)
    def _():
        finish(*work[2:], out_ref)


def wait_all(copies):
    for copy in copies:
        copy.wait()


def pick_kernel(which_ref, *refs):
    pieces, out_ref = refs[:-1], refs[-1]
    for place, piece in enumerate(pieces):
        out_ref[pl.ds(place * piece.shape[0], piece.shape[0]), :] = piece[...]


def pack_kernel(target_ref, block_ref, count_ref, pool_ref, out_ref, held_ref, mark_ref, *sems):
    in_sems, out_sems = sems
    entries = target_ref.shape[1]
    mark_ref[...] = jnp.full(mark_ref.shape, DEAD_MARK, mark_ref.dtype)

    def load(entry):
        return pltpu.make_async_copy(
            pool_ref.at[block_ref[0, entry]], held_ref.at[entry], in_sems.at[entry]
        )

    def store(entry, source):
        return pltpu.make_async_copy(
            source, out_ref.at[target_ref[0, entry]], out_sems.at[entry]
        )

    @pl.loop(0, entries)
    def _(entry):
        live = entry < count_ref[0]
        pl.when(live)(lambda: load(entry).start())
        pl.when(jnp.logical_not(live))(lambda: store(entry, mark_ref).start())

    @pl.loop(0, entries)
    def _(entry):
        @pl.when(entry < count_ref[0])
        def _():
            load(entry).wait()
            store(entry, held_ref.at[entry]).start()

    @pl.loop(0, entries)
    def _(entry):
        store(entry, mark_ref).wait()


def stage_kernel(owner_ref, place_ref, kept_ref, swapped_ref, *refs):
    outs, (sought_ref, known_ref, in_sems, out_sems) = refs[:-4], refs[-4:]
    core, chip, is_last = place_ref[0], place_ref[1], place_ref[2]
    chips, sought = sought_ref.shape[:2]

    def load(source, step, prefix):
        target = sought_ref.at[step, prefix] if prefix < sought else known_ref.at[step, 0]
        return pltpu.make_async_copy(source.at[core, chip ^ step], target, in_sems.at[step, prefix])

    def start(step, prefix, here):
        pl.when(here)(lambda: load(kept_ref, step, prefix).start())
        pl.when(jnp.logical_not(here))(lambda: load(swapped_ref, step, prefix).start())

    def store(place):
        source = sought_ref.at[place] if place < chips else known_ref.at[place - chips]
        return pltpu.make_async_copy(source, outs[place], out_sems.at[place])

    for step in range(chips):
        for prefix in range(sought):
            start(step, prefix, owner_ref[prefix] % 2 == core)

    @pl.when(is_last == 1)
    def _():
        for step in range(chips):
            start(step, sought, core == 1)

    for step in range(chips):
        for prefix in range(sought):
            load(kept_ref, step, prefix).wait()
        store(step).start()

    @pl.when(is_last == 1)
    def _():
        for step in range(chips):
            load(kept_ref, step, sought).wait()
            store(chips + step).start()
        wait_all([store(chips + step) for step in range(chips)])

    wait_all([store(step) for step in range(chips)])


def multicast(prefix_cache, owners, readers, outgoing, local):
    replicas = lax.axis_size("replica")
    me = lax.axis_index("replica")
    half = replicas // 2
    chips = half // 2
    chip = me // 2 % chips
    width = prefix_cache.shape[1]
    ids = jnp.arange(owners.shape[0], dtype=jnp.int32)
    known = jnp.sum(jnp.where(owners == replicas - 1, ids, 0))
    sought = jnp.where(ids[:-1] >= known, owners[1:], owners[:-1])

    split = prefix_cache.reshape(2, chips, -1, width)
    swapped, outgoing = lax.optimization_barrier((swap_cores(prefix_cache), outgoing))
    arrived = lax.all_to_all(outgoing, "replica", split_axis=0, concat_axis=0, tiled=True)
    swapped = swapped.reshape(split.shape)
    pieces = jax.ShapeDtypeStruct((owners.shape[0] - 1, *split.shape[2:]), split.dtype)
    piece = jax.ShapeDtypeStruct((1, *split.shape[2:]), split.dtype)
    staged = pl.pallas_call(
        stage_kernel,
        out_shape=(pieces,) * chips + (piece,) * chips,
        in_specs=[IN_SMEM] * 2 + [IN_HBM] * 2,
        out_specs=(IN_HBM,) * (2 * chips),
        scratch_shapes=[
            pltpu.VMEM((chips, *pieces.shape), split.dtype),
            pltpu.VMEM((chips, *piece.shape), split.dtype),
            pltpu.SemaphoreType.DMA((chips, owners.shape[0])),
            pltpu.SemaphoreType.DMA((2 * chips,)),
        ],
        compiler_params=COPY_PARAMS,
        name="stage_prefix",
    )(
        sought,
        jnp.stack([me % 2, chip, (me // 2 == replicas // 2 - 1).astype(jnp.int32)]),
        split,
        swapped,
    )

    def to_peers(staged, senders):
        return [
            lax.ppermute(rows, "replica", [(i, i ^ (2 * step)) for i in senders])
            for step, rows in enumerate(staged)
            if step
        ]

    def choose(own, passed, source):
        away = chip ^ source
        for step, rows in enumerate(passed, 1):
            own = jnp.where((away == step)[:, None, None], rows, own)
        return own

    passed = to_peers(staged[:chips], range(replicas))
    passed[0], local, *known_staged = lax.optimization_barrier((passed[0], local, *staged[chips:]))
    passed_known = to_peers(known_staged, (replicas - 2, replicas - 1))
    last_chip = jnp.full((1,), chips - 1, jnp.int32)
    found = jnp.concatenate(
        [
            choose(known_staged[0], passed_known, last_chip),
            choose(staged[0], passed, sought // 2 % chips),
        ]
    )
    source = jnp.concatenate([jnp.full((1,), replicas - 1, jnp.int32), sought])
    passed = lax.ppermute(found, "replica", [(i, (i + half) % replicas) for i in range(replicas)])
    held = jnp.where((source // half == me // half)[:, None, None], found, passed)
    wanted = jnp.stack([readers[me], readers[me ^ 1]])
    place = jnp.where(wanted == known, 0, wanted + (wanted < known))
    return held, place, local, arrived


def swap_cores(rows):
    return lax.ppermute(rows, "replica", [(i, i ^ 1) for i in range(lax.axis_size("replica"))])


def gather_step(gathered, step):
    replicas = lax.axis_size("replica")
    bits = (replicas // 4).bit_length() - 1
    members = [bit for bit in range(bits) if step >> bit & 1]
    linked = [bit for bit in members if step >> ((bit - 1) % bits) & 1]
    last = min(linked or members)
    pairs = [(i, i ^ (2 << last)) for i in range(replicas)]
    return lax.ppermute(gathered[step ^ 1 << last], "replica", pairs)


def from_other(pieces, place):
    rows, width = pieces[0].shape[1:]
    spec = pl.BlockSpec((None, rows, width), lambda i, which: (which[1], 0, 0))
    picked = pl.pallas_call(
        pick_kernel,
        out_shape=jax.ShapeDtypeStruct((len(pieces) * rows, width), pieces[0].dtype),
        grid_spec=pltpu.PrefetchScalarGridSpec(
            num_scalar_prefetch=1,
            grid=(1,),
            in_specs=[spec] * len(pieces),
            out_specs=pl.BlockSpec((len(pieces) * rows, width), lambda i, which: (0, 0)),
        ),
        compiler_params=PARAMS,
        name="pick_other",
    )(place, *pieces)
    return swap_cores(picked)


def whole(shape):
    return pl.BlockSpec(shape, lambda *args: (0,) * len(shape))


def cost(rows, keys, size):
    return pl.CostEstimate(
        flops=12 * rows * keys * size, bytes_accessed=4 * keys * size, transcendentals=rows * keys
    )


def on_device(
    queries,
    suffix_kv,
    own_cache,
    ctx_len,
    prefix_cache,
    owners,
    readers,
    kv_pool,
    mig_target,
    mig_block,
    mig_count,
):
    replicas = lax.axis_size("replica")
    size = suffix_kv.shape[1] // 2
    tokens = queries.shape[0]
    heads = queries.shape[1] // size
    factor = size ** (-0.5) * LOG2E
    row_count = tokens * heads
    state = jax.ShapeDtypeStruct((2, row_count, size), jnp.float32)
    result = jax.ShapeDtypeStruct(queries.shape, queries.dtype)

    work = [
        pltpu.VMEM((row_count, size), queries.dtype),
        *[pltpu.VMEM((row_count, size), jnp.float32)] * 3,
    ]

    entries = mig_target.shape[1]
    slots = jax.ShapeDtypeStruct((replicas, *kv_pool.shape[1:]), kv_pool.dtype)
    outgoing = pl.pallas_call(
        pack_kernel,
        out_shape=slots,
        in_specs=[IN_SMEM] * 3 + [IN_HBM],
        out_specs=IN_HBM,
        scratch_shapes=[
            pltpu.VMEM((entries, *kv_pool.shape[1:]), kv_pool.dtype),
            pltpu.VMEM(kv_pool.shape[1:], kv_pool.dtype),
            pltpu.SemaphoreType.DMA((entries,)),
            pltpu.SemaphoreType.DMA((entries,)),
        ],
        compiler_params=COPY_PARAMS,
        name="pack_moved",
    )(mig_target, mig_block, mig_count, kv_pool)
    local = pl.pallas_call(
        functools.partial(local_kernel, factor),
        out_shape=state,
        grid=(1,),
        in_specs=[IN_SMEM, whole(queries.shape), whole(suffix_kv.shape), whole(own_cache.shape)],
        out_specs=whole(state.shape),
        scratch_shapes=work,
        compiler_params=PARAMS,
        cost_estimate=cost(row_count, tokens + own_cache.shape[0], size),
        name="local_keys",
    )(ctx_len, queries, suffix_kv, own_cache)
    held, place, state_now, arrived = multicast(prefix_cache, owners, readers, outgoing, local)

    rows = arrived.shape[1]
    group = max(n for n in range(1, replicas + 1) if replicas % n == 0 and n * rows <= CHUNK)
    steps = max(1, replicas // group // 2)
    for first in range(0, replicas // group, steps):
        state_now = pl.pallas_call(
            functools.partial(moved_kernel, factor, steps),
            out_shape=state,
            grid=(steps,),
            in_specs=[
                whole(queries.shape),
                pl.BlockSpec((group, rows, 2 * size), lambda i, first=first: (first + i, 0, 0)),
                whole(state.shape),
            ],
            out_specs=whole(state.shape),
            scratch_shapes=work,
            compiler_params=PARAMS,
            cost_estimate=cost(row_count, steps * group * rows, size),
            name="moved_keys",
        )(queries, arrived, state_now)

    gathered = {0: held}
    for step in sorted(range(1, replicas // 4), key=lambda step: (step.bit_count(), step)):
        gathered[step] = gather_step(gathered, step)
    pieces = list(gathered.values())
    others = from_other(pieces, place)
    rows = held.shape[1]
    keys = 2 * len(pieces) * rows
    steps = max(1, keys // CHUNK)
    while keys % (steps * size):
        steps -= 1
    return pl.pallas_call(
        functools.partial(prefix_kernel, factor, len(pieces) + 1, steps),
        out_shape=result,
        grid_spec=pltpu.PrefetchScalarGridSpec(
            num_scalar_prefetch=1,
            grid=(steps,),
            in_specs=[
                whole(queries.shape),
                *[pl.BlockSpec((None, rows, 2 * size), lambda i, which: (which[0], 0, 0))]
                * len(pieces),
                whole(others.shape),
                whole(state.shape),
            ],
            out_specs=whole(queries.shape),
            scratch_shapes=[*work, pltpu.VMEM((keys, 2 * size), jnp.bfloat16)],
        ),
        compiler_params=PARAMS,
        cost_estimate=cost(row_count, keys, size),
        name="prefix_keys",
    )(place, queries, *pieces, others, state_now)


def solution(mesh):
    in_specs = (
        P(("groups", "replica"), None),
        P(("groups", "replica"), None),
        P(("groups", "replica"), None),
        P(("groups", "replica")),
        P(("groups", "replica"), None),
        P("groups"),
        P("groups"),
        P(("groups", "replica"), None, None),
        P(("groups", "replica"), None),
        P(("groups", "replica"), None),
        P(("groups", "replica")),
    )
    out_specs = P(("groups", "replica"), None)
    return jax.shard_map(
        on_device, mesh=mesh, in_specs=in_specs, out_specs=out_specs, check_vma=False
    )
```

time: 151 us -> 150 us (level)
  starting transfers between devices: 54.7 us -> 44.7 us
  local copies, waits for them, and re-layouts: 8.58 us -> 14.9 us
  waiting for transfers between devices: 40.5 us -> 43.1 us
    ppermute x7, waiting for transfers between devices: 24.5 us -> 12.3 us  [gather_step(): return lax.ppermute(gathered[step ^ 1 << last], 'replica', pairs)]
    ppermute x1, starting transfers between devices: 17.7 us -> 7.8 us  [multicast(): lax.ppermute(found, 'replica', [(i, (i + half) % replicas) for i in range...]
    ppermute x11 -> x14, waiting for transfers between devices: 12.7 us -> 20.9 us  [to_peers(): lax.ppermute(rows, 'replica', [(i, i ^ 2 * step) for i in senders])]
    ppermute x1, waiting for transfers between devices: 3.31 us -> 9.88 us  [multicast(): lax.ppermute(found, 'replica', [(i, (i + half) % replicas) for i in range...]
    unnamed x34 -> x72, local copies, waits for them, and re-layouts: 7.32 us -> 13.8 us
    all_to_all x2 -> x1, starting transfers between devices: 11.1 us -> 6.99 us  [multicast(): lax.all_to_all(outgoing, 'replica', split_axis=0, concat_axis=0, tiled=True)]
    ppermute x11 -> x14, starting transfers between devices: 15.7 us -> 18.5 us  [to_peers(): lax.ppermute(rows, 'replica', [(i, i ^ 2 * step) for i in senders])]
    pallas_call x5 -> x6, Pallas kernels: 36.7 us -> 37.8 us  [the longest x1 14.8 us: on_device(): pl.pallas_call(functools.partial(prefix_kernel, factor, len(pieces) + 1,...]
  transfers between devices with their start and end apart: 24 -> 25, of which waited for: 10 -> 9; matrix products, arithmetic and copies ran while one was open for 3% -> 3% of each run, Pallas kernels for 16% -> 16%
where the time goes in v12:
time: 150 us; the launch traced here: 149 us
  starting transfers between devices  44.7 us (30%)
  waiting for transfers between devices  43.1 us (29%)
  Pallas kernels  39.4 us (26%)
  local copies, waits for them, and re-layouts  14.9 us (10%)
  between operations  3.71 us (2%)
  other arithmetic  3.37 us (2%)
    ppermute x14, waiting for transfers between devices, to_peers(): lax.ppermute(rows, 'replica', [(i, i ^ 2 * step) for i in senders])  20.9 us
    ppermute x14, starting transfers between devices, to_peers(): lax.ppermute(rows, 'replica', [(i, i ^ 2 * step) for i in senders])  18.5 us
    pallas_call x1, Pallas kernels, on_device(): pl.pallas_call(functools.partial(prefix_kernel, factor, len(pieces) + 1,...  14.8 us
    pallas_call x2, Pallas kernels, on_device(): pl.pallas_call(functools.partial(moved_kernel, factor, steps), out_shape=...  13.9 us
    unnamed x72, local copies, waits for them, and re-layouts  13.8 us
    ppermute x7, waiting for transfers between devices, gather_step(): return lax.ppermute(gathered[step ^ 1 << last], 'replica', pairs)  12.3 us
    ppermute x7, starting transfers between devices, gather_step(): return lax.ppermute(gathered[step ^ 1 << last], 'replica', pairs)  10.9 us
    ppermute x1, waiting for transfers between devices, multicast(): lax.ppermute(found, 'replica', [(i, (i + half) % replicas) for i in range...  9.88 us
  transfers between devices with their start and end apart: 25, of which 9 were waited for; matrix products, arithmetic and copies ran while one was open for 3% of the time, Pallas kernels for 16%

profile of v12, /device:TPU:0, one launch (start us, length us, event | category | flops | bytes accessed | tf_op | source)
XLA Modules:
  0.0 149.1 jit_solution(11805538533652455707)
XLA Ops:
  1.1 3.6 %pack_moved.1 = bf16[32,128,256]{2,1,0:T(8,128)(2,1)} custom-call(s32[1,32]{1,0:T(1,128)} %target_ref.1, s32[1,32]{1,0:T(1,128)} %block_ref.1, s32[1]{0:T(128)S(6)} %copy.13.count_ref, bf16[32,128,256]{2,1,0:T(8,128)(2,1)} %pool_ref.1), custom_call_target="tpu_custom_call" | custom-call | tf_op jit(solution)/shard_map/pack_moved/pallas_call | solution.py:372
  4.7 1.4 copy-done.21
  6.1 7.0 %all-to-all-start = ((bf16[32,128,256]{2,1,0:T(8,128)(2,1)}), bf16[32,128,256]{2,1,0:T(8,128)(2,1)S(1)}, u32[]{:S(2)}, u32[]{:S(2)}) async-start(bf16[32,128,256]{2,1,0:T(8,128)(2,1)} %pack_moved.1), calls=%async_computation | async-start | bytes 4194304 | tf_op jit(solution)/shard_map/all_to_all | solution.py:246
  17.3 3.0 %stage_prefix.1 = (bf16[1,256,256]{2,1,0:T(8,128)(2,1)}, bf16[1,256,256]{2,1,0:T(8,128)(2,1)}, bf16[1,256,256]{2,1,0:T(8,128)(2,1)}, bf16[1,256,256]{2,1,0:T(8,1...) custom-call(s32[1]{0:T(128)S(6)} %select_n.107.owner_ref, ...), custom_call_target="tpu_custom_call" | custom-call | tf_op jit(solution)/shard_map/stage_prefix/pallas_call | solution.py:250
  20.4 1.8 %collective-permute-start.1 = (bf16[1,256,256]{2,1,0:T(8,128)(2,1)}, bf16[1,256,256]{2,1,0:T(8,128)(2,1)S(1)}, u32[]{:S(2)}, u32[]{:S(2)}) collective-permute-start(bf16[1,256,256]{2,1,0:T(8,128)(2,1)} %get-tuple-element.34), channel_id=1, source_target_pairs={{0,2},{1,3},{2,0},{3,1},{4,6},{5,7},{6,4},{7,5},{8,10},{9,11},{10,... | collective-permute-start | bytes 393224 | tf_op jit(solution)/shard_map/ppermute | solution.py:272
  22.2 2.4 %collective-permute-start.10 = (bf16[1,256,256]{2,1,0:T(8,128)(2,1)}, bf16[1,256,256]{2,1,0:T(8,128)(2,1)S(1)}, u32[]{:S(2)}, u32[]{:S(2)}) collective-permute-start(bf16[1,256,256]{2,1,0:T(8,128)(2,1)} %get-tuple-element.52), channel_id=1, source_target_pairs={{0,12},{1,13},{2,14},{3,15},{4,8},{5,9},{6,10},{7,11},{8,4},{9,5},... | collective-permute-start | bytes 393224 | tf_op jit(solution)/shard_map/ppermute | solution.py:272
  25.2 1.5 %collective-permute-start.12 = (bf16[1,256,256]{2,1,0:T(8,128)(2,1)}, bf16[1,256,256]{2,1,0:T(8,128)(2,1)S(1)}, u32[]{:S(2)}, u32[]{:S(2)}) collective-permute-start(bf16[1,256,256]{2,1,0:T(8,128)(2,1)} %get-tuple-element.54), channel_id=1, source_target_pairs={{0,8},{1,9},{2,10},{3,11},{4,12},{5,13},{6,14},{7,15},{8,0},{9,1},... | collective-permute-start | bytes 393224 | tf_op jit(solution)/shard_map/ppermute | solution.py:272
  26.7 2.5 %local_keys.1.loaded_ref = f32[2,2048,128]{2,1,0:T(8,128)S(1)} custom-call(s32[1]{0:T(128)S(6)} %copy.12.len_ref, bf16[256,1024]{1,0:T(8,128)(2,1)S(1)} %copy-done.15, bf16[256,256]{1,0:T(8,128)(2,1)S(1)} %copy-done.18, bf16[512,256]{1,0:T(8,128)(2,1)S(1)} %copy-done.17), custom_call_target="tpu_custom_call" | custom-call | flops 2415919104 | bytes 393216 | tf_op jit(solution)/shard_map/local_keys/pallas_call | solution.py:386
  29.3 1.4 copy-done.19
  30.7 1.5 collective-permute-start.13
  32.1 1.5 collective-permute-start.14
  33.6 18.1 %collective-permute-done.10 = bf16[1,256,256]{2,1,0:T(8,128)(2,1)S(1)} collective-permute-done((bf16[1,256,256]{2,1,0:T(8,128)(2,1)}, bf16[1,256,256]{2,1,0:T(8,128)(2,1)S(1)}, u32[]{:S(2)}, u32[]{:S(2)}) %collective-permute-start.10) | collective-permute-done | bytes 131104 | tf_op jit(solution)/shard_map/ppermute | solution.py:272
  51.7 4.6 %collective-permute-start.9 = (bf16[1,256,256]{2,1,0:T(8,128)(2,1)S(1)}, bf16[1,256,256]{2,1,0:T(8,128)(2,1)S(1)}, u32[]{:S(2)}, u32[]{:S(2)}) collective-permute-start(bf16[1,256,256]{2,1,0:T(8,128)(2,1)S(1)} %copy-done.33), channel_id=1, source_target_pairs={{0,14},{1,15},{2,12},{3,13},{4,10},{5,11},{6,8},{7,9},{8,6},{9,7},... | collective-permute-start | bytes 393224 | tf_op jit(solution)/shard_map/ppermute | solution.py:272
  56.3 0.7 collective-permute-start.2
  58.1 0.7 collective-permute-start.4
  58.8 0.7 collective-permute-start.5
  59.5 2.4 %collective-permute-done.9 = bf16[1,256,256]{2,1,0:T(8,128)(2,1)S(1)} collective-permute-done((bf16[1,256,256]{2,1,0:T(8,128)(2,1)S(1)}, bf16[1,256,256]{2,1,0:T(8,128)(2,1)S(1)}, u32[]{:S(2)}, u32[]{:S(2)}) %collective-permute-start.9) | collective-permute-done | bytes 131104 | tf_op jit(solution)/shard_map/ppermute | solution.py:272
  61.8 0.7 collective-permute-start.6
  62.5 0.7 collective-permute-start.7
  63.2 0.7 collective-permute-start.8
  64.1 7.8 %collective-permute-start.15 = (bf16[2,256,256]{2,1,0:T(8,128)(2,1)S(1)}, bf16[2,256,256]{2,1,0:T(8,128)(2,1)S(1)}, u32[]{:S(2)}, u32[]{:S(2)}) collective-permute-start(bf16[2,256,256]{2,1,0:T(8,128)(2,1)S(1)} %pad_maximum_fusion), channel_id=1, source_target_pairs={{0,16},{1,17},{2,18},{3,19},{4,20},{5,21},{6,22},{7,23},{8,24},{9,... | collective-permute-start | bytes 786440 | tf_op jit(solution)/shard_map/ppermute | solution.py:294
  72.0 9.9 %collective-permute-done.15 = bf16[2,256,256]{2,1,0:T(8,128)(2,1)S(1)} collective-permute-done((bf16[2,256,256]{2,1,0:T(8,128)(2,1)S(1)}, bf16[2,256,256]{2,1,0:T(8,128)(2,1)S(1)}, u32[]{:S(2)}, u32[]{:S(2)}) %collective-permute-start.15) | collective-permute-done | bytes 262176 | tf_op jit(solution)/shard_map/ppermute | solution.py:294
  82.0 4.7 %collective-permute-start.17 = (bf16[2,256,256]{2,1,0:T(8,128)(2,1)S(1)}, bf16[2,256,256]{2,1,0:T(8,128)(2,1)S(1)}, u32[]{:S(2)}, u32[]{:S(2)}) collective-permute-start(bf16[2,256,256]{2,1,0:T(8,128)(2,1)S(1)} %broadcast_select_fusion.refs_0_), channel_id=1, source_target_pairs={{0,4},{1,5},{2,6},{3,7},{4,0},{5,1},{6,2},{7,3},{8,12},{9,13},{10,... | collective-permute-start | bytes 786440 | tf_op jit(solution)/shard_map/ppermute | solution.py:312
  86.7 2.7 %collective-permute-start.16 = (bf16[2,256,256]{2,1,0:T(8,128)(2,1)S(1)}, bf16[2,256,256]{2,1,0:T(8,128)(2,1)S(1)}, u32[]{:S(2)}, u32[]{:S(2)}) collective-permute-start(bf16[2,256,256]{2,1,0:T(8,128)(2,1)S(1)} %broadcast_select_fusion.refs_0_), channel_id=1, source_target_pairs={{0,2},{1,3},{2,0},{3,1},{4,6},{5,7},{6,4},{7,5},{8,10},{9,11},{10,... | collective-permute-start | bytes 786440 | tf_op jit(solution)/shard_map/ppermute | solution.py:312
  89.4 1.7 %collective-permute-done.17.refs_2_ = bf16[2,256,256]{2,1,0:T(8,128)(2,1)S(1)} collective-permute-done((bf16[2,256,256]{2,1,0:T(8,128)(2,1)S(1)}, bf16[2,256,256]{2,1,0:T(8,128)(2,1)S(1)}, u32[]{:S(2)}, u32[]{:S(2)}) %collective-permute-start.17) | collective-permute-done | bytes 262176 | tf_op jit(solution)/shard_map/ppermute | solution.py:312
  91.0 1.9 %collective-permute-start.21 = (bf16[2,256,256]{2,1,0:T(8,128)(2,1)S(1)}, bf16[2,256,256]{2,1,0:T(8,128)(2,1)S(1)}, u32[]{:S(2)}, u32[]{:S(2)}) collective-permute-start(bf16[2,256,256]{2,1,0:T(8,128)(2,1)S(1)} %collective-permute-done.17.refs_2_), channel_id=1, source_target_pairs={{0,8},{1,9},{2,10},{3,11},{4,12},{5,13},{6,14},{7,15},{8,0},{9,1},... | collective-permute-start | bytes 786440 | tf_op jit(solution)/shard_map/ppermute | solution.py:312
  92.9 0.7 copy-done
  93.6 1.9 %collective-permute-done.16.refs_1_ = bf16[2,256,256]{2,1,0:T(8,128)(2,1)S(1)} collective-permute-done((bf16[2,256,256]{2,1,0:T(8,128)(2,1)S(1)}, bf16[2,256,256]{2,1,0:T(8,128)(2,1)S(1)}, u32[]{:S(2)}, u32[]{:S(2)}) %collective-permute-start.16) | collective-permute-done | bytes 262176 | tf_op jit(solution)/shard_map/ppermute | solution.py:312
  95.9 0.7 copy-done.3
  96.6 2.0 %collective-permute-done.18.refs_3_ = bf16[2,256,256]{2,1,0:T(8,128)(2,1)S(1)} collective-permute-done((bf16[2,256,256]{2,1,0:T(8,128)(2,1)S(1)}, bf16[2,256,256]{2,1,0:T(8,128)(2,1)S(1)}, u32[]{:S(2)}, u32[]{:S(2)}) %collective-permute-start.18) | collective-permute-done | bytes 262176 | tf_op jit(solution)/shard_map/ppermute | solution.py:312
  99.0 0.7 copy-done.6
  99.7 2.9 %collective-permute-done.21.refs_6_ = bf16[2,256,256]{2,1,0:T(8,128)(2,1)S(1)} collective-permute-done((bf16[2,256,256]{2,1,0:T(8,128)(2,1)S(1)}, bf16[2,256,256]{2,1,0:T(8,128)(2,1)S(1)}, u32[]{:S(2)}, u32[]{:S(2)}) %collective-permute-start.21) | collective-permute-done | bytes 262176 | tf_op jit(solution)/shard_map/ppermute | solution.py:312
  102.6 0.9 collective-permute-start.22
  103.5 0.7 copy-done.9
  104.9 1.9 %compare_select_fusion.which_ref = s32[2]{0:T(128)S(1)} fusion(s32[1]{0:T(128)} %get-tuple-element.64, s32[1]{0:T(128)} %get-tuple-element.63, s32[]{:T(128)} %fusion.1), kind=kLoop, calls=%fused_computation.6 | loop fusion | flops 12 | bytes 20 | tf_op jit(solution)/shard_map/jit(_where)/select_n | solution.py:297
  106.8 3.8 %collective-permute-done.22.refs_7_ = bf16[2,256,256]{2,1,0:T(8,128)(2,1)S(1)} collective-permute-done((bf16[2,256,256]{2,1,0:T(8,128)(2,1)S(1)}, bf16[2,256,256]{2,1,0:T(8,128)(2,1)S(1)}, u32[]{:S(2)}, u32[]{:S(2)}) %collective-permute-start.22) | collective-permute-done | bytes 262176 | tf_op jit(solution)/shard_map/ppermute | solution.py:312
  110.6 0.7 copy-done.12
  111.3 0.9 copy-done.1
  112.2 0.9 copy-done.4
  113.2 0.9 copy-done.7
  114.1 0.9 copy-done.10
  115.1 0.9 copy-done.13
  116.0 1.6 %pick_other.1 = bf16[2048,256]{1,0:T(8,128)(2,1)S(1)} custom-call(s32[2]{0:T(128)S(1)} %compare_select_fusion.which_ref, bf16[2,256,256]{2,1,0:T(8,128)(2,1)S(1)} %broadcast_select_fusion.refs_0_, bf16[2,256,256]{2,1,0:T(8,128)(2,1)S(1)} %copy-done.4, bf16[2,256,256]{2,1,0:T(8,128)(2,1)S(1)} %copy-done.1, bf16[2,256,256]{2,1,0:T(8,128)(2,1)S(1)} %copy-done.7, ...), custom_call_target="tpu_custom_call" | custom-call | tf_op jit(solution)/shard_map/pick_other/pallas_call | solution.py:318
  117.7 1.0 copy-done.16
  118.8 1.6 %copy-done.20 = f32[2,2048,128]{2,1,0:T(8,128)S(1)} copy-done((f32[2,2048,128]{2,1,0:T(8,128)S(1)}, f32[2,2048,128]{2,1,0:T(8,128)}, u32[]{:S(2)}) %copy-start.20) | copy-done | bytes 2097176
  120.3 6.9 %moved_keys.2.loaded_ref = f32[2,2048,128]{2,1,0:T(8,128)S(1)} custom-call(bf16[256,1024]{1,0:T(8,128)(2,1)S(1)} %copy-done.16, bf16[32,128,256]{2,1,0:T(8,128)(2,1)S(1)} %all-to-all-done.kv_ref, f32[2,2048,128]{2,1,0:T(8,128)S(1)} %copy-done.20), custom_call_target="tpu_custom_call" | custom-call | flops 6442450944 | bytes 1048576 | tf_op jit(solution)/shard_map/moved_keys/pallas_call | solution.py:403
  127.3 6.9 %moved_keys.3.refs_9_ = f32[2,2048,128]{2,1,0:T(8,128)S(1)} custom-call(bf16[256,1024]{1,0:T(8,128)(2,1)S(1)} %copy-done.16, bf16[32,128,256]{2,1,0:T(8,128)(2,1)S(1)} %all-to-all-done.kv_ref, f32[2,2048,128]{2,1,0:T(8,128)S(1)} %moved_keys.2.loaded_ref), custom_call_target="tpu_custom_call" | custom-call | flops 6442450944 | bytes 1048576 | tf_op jit(solution)/shard_map/moved_keys/pallas_call | solution.py:403
  134.3 14.8 %prefix_keys.1 = bf16[256,1024]{1,0:T(8,128)(2,1)} custom-call(s32[2]{0:T(128)S(1)} %compare_select_fusion.which_ref, bf16[256,1024]{1,0:T(8,128)(2,1)S(1)} %copy-done.16, bf16[2,256,256]{2,1,0:T(8,128)(2,1)S(1)} %broadcast_select_fusion.refs_0_, bf16[2,256,256]{2,1,0:T(8,128)(2,1)S(1)} %copy-done.5, bf16[2,256,256]{2,1,0:T(8,128)(2,1)S(1)} %copy-done.2, ...), custom_call_target="tpu_custom_call" | custom-call | flops 12884901888 | bytes 2097152 | tf_op jit(solution)/shard_map/prefix_keys/pallas_call | solution.py:429
  (92 shorter events, 5.7 us)
Async XLA Ops:
  0.0 4.7 %collective-permute-start = (bf16[4096,256]{1,0:T(8,128)(2,1)}, bf16[4096,256]{1,0:T(8,128)(2,1)S(1)}, u32[]{:S(2)}, u32[]{:S(2)}) collective-permute-start(bf16[4096,256]{1,0:T(8,128)(2,1)} %param.15), channel_id=1, source_target_pairs={{0,1},{1,0},{2,3},{3,2},{4,5},{5,4},{6,7},{7,6},{8,9},{9,8},{10,11... | collective-permute-start | bytes 6291464 | tf_op jit(solution)/shard_map/ppermute | solution.py:302
  4.7 9.1 %copy-start.25 = (s32[2]{0:T(128)S(1)}, s32[2]{0:T(128)}, u32[]{:S(2)}) copy-start(s32[2]{0:T(128)} %param.16) | copy-start | bytes 28
  6.1 111.6 %all-to-all-start = ((bf16[32,128,256]{2,1,0:T(8,128)(2,1)}), bf16[32,128,256]{2,1,0:T(8,128)(2,1)S(1)}, u32[]{:S(2)}, u32[]{:S(2)}) async-start(bf16[32,128,256]{2,1,0:T(8,128)(2,1)} %pack_moved.1), calls=%async_computation | async-start | bytes 4194304 | tf_op jit(solution)/shard_map/all_to_all | solution.py:246
  17.3 9.4 %copy-start.15 = (bf16[256,1024]{1,0:T(8,128)(2,1)S(1)}, bf16[256,1024]{1,0:T(8,128)(2,1)}, u32[]{:S(2)}) copy-start(bf16[256,1024]{1,0:T(8,128)(2,1)} %q_ref.7) | copy-start | bytes 1572868
  17.3 9.4 %copy-start.17 = (bf16[512,256]{1,0:T(8,128)(2,1)S(1)}, bf16[512,256]{1,0:T(8,128)(2,1)}, u32[]{:S(2)}) copy-start(bf16[512,256]{1,0:T(8,128)(2,1)} %own_ref.1) | copy-start | bytes 786436
  17.3 9.4 %copy-start.18 = (bf16[256,256]{1,0:T(8,128)(2,1)S(1)}, bf16[256,256]{1,0:T(8,128)(2,1)}, u32[]{:S(2)}) copy-start(bf16[256,256]{1,0:T(8,128)(2,1)} %suffix_ref.1) | copy-start | bytes 393220
  20.4 11.8 %collective-permute-start.1 = (bf16[1,256,256]{2,1,0:T(8,128)(2,1)}, bf16[1,256,256]{2,1,0:T(8,128)(2,1)S(1)}, u32[]{:S(2)}, u32[]{:S(2)}) collective-permute-start(bf16[1,256,256]{2,1,0:T(8,128)(2,1)} %get-tuple-element.34), channel_id=1, source_target_pairs={{0,2},{1,3},{2,0},{3,1},{4,6},{5,7},{6,4},{7,5},{8,10},{9,11},{10,... | collective-permute-start | bytes 393224 | tf_op jit(solution)/shard_map/ppermute | solution.py:272
  22.2 29.5 %collective-permute-start.10 = (bf16[1,256,256]{2,1,0:T(8,128)(2,1)}, bf16[1,256,256]{2,1,0:T(8,128)(2,1)S(1)}, u32[]{:S(2)}, u32[]{:S(2)}) collective-permute-start(bf16[1,256,256]{2,1,0:T(8,128)(2,1)} %get-tuple-element.52), channel_id=1, source_target_pairs={{0,12},{1,13},{2,14},{3,15},{4,8},{5,9},{6,10},{7,11},{8,4},{9,5},... | collective-permute-start | bytes 393224 | tf_op jit(solution)/shard_map/ppermute | solution.py:272
  24.6 31.7 %collective-permute-start.11 = (bf16[1,256,256]{2,1,0:T(8,128)(2,1)}, bf16[1,256,256]{2,1,0:T(8,128)(2,1)S(1)}, u32[]{:S(2)}, u32[]{:S(2)}) collective-permute-start(bf16[1,256,256]{2,1,0:T(8,128)(2,1)} %get-tuple-element.53), channel_id=1, source_target_pairs={{0,10},{1,11},{2,8},{3,9},{4,14},{5,15},{6,12},{7,13},{8,2},{9,3},... | collective-permute-start | bytes 393224 | tf_op jit(solution)/shard_map/ppermute | solution.py:272
  25.1 5.5 %copy-start.35 = (bf16[1,256,256]{2,1,0:T(8,128)(2,1)S(1)}, bf16[1,256,256]{2,1,0:T(8,128)(2,1)}, u32[]{:S(2)}) copy-start(bf16[1,256,256]{2,1,0:T(8,128)(2,1)} %get-tuple-element.55) | copy-start | bytes 393220
  25.1 7.0 %copy-start.34 = (bf16[1,256,256]{2,1,0:T(8,128)(2,1)S(1)}, bf16[1,256,256]{2,1,0:T(8,128)(2,1)}, u32[]{:S(2)}) copy-start(bf16[1,256,256]{2,1,0:T(8,128)(2,1)} %get-tuple-element.56) | copy-start | bytes 393220
  25.1 26.6 %copy-start.33 = (bf16[1,256,256]{2,1,0:T(8,128)(2,1)S(1)}, bf16[1,256,256]{2,1,0:T(8,128)(2,1)}, u32[]{:S(2)}) copy-start(bf16[1,256,256]{2,1,0:T(8,128)(2,1)} %get-tuple-element.51) | copy-start | bytes 393220
  25.1 31.2 %copy-start.32 = (bf16[1,256,256]{2,1,0:T(8,128)(2,1)S(1)}, bf16[1,256,256]{2,1,0:T(8,128)(2,1)}, u32[]{:S(2)}) copy-start(bf16[1,256,256]{2,1,0:T(8,128)(2,1)} %get-tuple-element.43) | copy-start | bytes 393220
  25.1 32.2 %copy-start.31 = (bf16[1,256,256]{2,1,0:T(8,128)(2,1)S(1)}, bf16[1,256,256]{2,1,0:T(8,128)(2,1)}, u32[]{:S(2)}) copy-start(bf16[1,256,256]{2,1,0:T(8,128)(2,1)} %get-tuple-element.44) | copy-start | bytes 393220
  25.1 32.9 %copy-start.30 = (bf16[1,256,256]{2,1,0:T(8,128)(2,1)S(1)}, bf16[1,256,256]{2,1,0:T(8,128)(2,1)}, u32[]{:S(2)}) copy-start(bf16[1,256,256]{2,1,0:T(8,128)(2,1)} %get-tuple-element.45) | copy-start | bytes 393220
  25.1 33.6 %copy-start.29 = (bf16[1,256,256]{2,1,0:T(8,128)(2,1)S(1)}, bf16[1,256,256]{2,1,0:T(8,128)(2,1)}, u32[]{:S(2)}) copy-start(bf16[1,256,256]{2,1,0:T(8,128)(2,1)} %get-tuple-element.46) | copy-start | bytes 393220
  25.2 36.7 %copy-start.28 = (bf16[1,256,256]{2,1,0:T(8,128)(2,1)S(1)}, bf16[1,256,256]{2,1,0:T(8,128)(2,1)}, u32[]{:S(2)}) copy-start(bf16[1,256,256]{2,1,0:T(8,128)(2,1)} %get-tuple-element.47) | copy-start | bytes 393220
  25.2 37.3 %copy-start.27 = (bf16[1,256,256]{2,1,0:T(8,128)(2,1)S(1)}, bf16[1,256,256]{2,1,0:T(8,128)(2,1)}, u32[]{:S(2)}) copy-start(bf16[1,256,256]{2,1,0:T(8,128)(2,1)} %get-tuple-element.48) | copy-start | bytes 393220
  25.2 38.0 %copy-start.26 = (bf16[1,256,256]{2,1,0:T(8,128)(2,1)S(1)}, bf16[1,256,256]{2,1,0:T(8,128)(2,1)}, u32[]{:S(2)}) copy-start(bf16[1,256,256]{2,1,0:T(8,128)(2,1)} %get-tuple-element.49) | copy-start | bytes 393220
  25.2 38.7 %copy-start.23 = (bf16[1,256,256]{2,1,0:T(8,128)(2,1)S(1)}, bf16[1,256,256]{2,1,0:T(8,128)(2,1)}, u32[]{:S(2)}) copy-start(bf16[1,256,256]{2,1,0:T(8,128)(2,1)} %get-tuple-element.58) | copy-start | bytes 393220
  25.2 38.8 %copy-start.22 = (bf16[1,256,256]{2,1,0:T(8,128)(2,1)S(1)}, bf16[1,256,256]{2,1,0:T(8,128)(2,1)}, u32[]{:S(2)}) copy-start(bf16[1,256,256]{2,1,0:T(8,128)(2,1)} %get-tuple-element.50) | copy-start | bytes 393220
  25.2 32.1 %collective-permute-start.12 = (bf16[1,256,256]{2,1,0:T(8,128)(2,1)}, bf16[1,256,256]{2,1,0:T(8,128)(2,1)S(1)}, u32[]{:S(2)}, u32[]{:S(2)}) collective-permute-start(bf16[1,256,256]{2,1,0:T(8,128)(2,1)} %get-tuple-element.54), channel_id=1, source_target_pairs={{0,8},{1,9},{2,10},{3,11},{4,12},{5,13},{6,14},{7,15},{8,0},{9,1},... | collective-permute-start | bytes 393224 | tf_op jit(solution)/shard_map/ppermute | solution.py:272
  30.6 73.6 %copy-start.24 = (s32[32]{0:T(128)S(1)}, s32[32]{0:T(128)}, u32[]{:S(2)}) copy-start(s32[32]{0:T(128)} %param.17) | copy-start | bytes 388
  30.7 27.4 %collective-permute-start.13 = (bf16[1,256,256]{2,1,0:T(8,128)(2,1)S(1)}, bf16[1,256,256]{2,1,0:T(8,128)(2,1)S(1)}, u32[]{:S(2)}, u32[]{:S(2)}) collective-permute-start(bf16[1,256,256]{2,1,0:T(8,128)(2,1)S(1)} %copy-done.35), channel_id=1, source_target_pairs={{0,6},{1,7},{2,4},{3,5},{4,2},{5,3},{6,0},{7,1},{8,14},{9,15},{10,... | collective-permute-start | bytes 393224 | tf_op jit(solution)/shard_map/ppermute | solution.py:272
  32.1 26.6 %collective-permute-start.14 = (bf16[1,256,256]{2,1,0:T(8,128)(2,1)S(1)}, bf16[1,256,256]{2,1,0:T(8,128)(2,1)S(1)}, u32[]{:S(2)}, u32[]{:S(2)}) collective-permute-start(bf16[1,256,256]{2,1,0:T(8,128)(2,1)S(1)} %copy-done.34), channel_id=1, source_target_pairs={{0,4},{1,5},{2,6},{3,7},{4,0},{5,1},{6,2},{7,3},{8,12},{9,13},{10,... | collective-permute-start | bytes 393224 | tf_op jit(solution)/shard_map/ppermute | solution.py:272
  51.7 10.1 %collective-permute-start.9 = (bf16[1,256,256]{2,1,0:T(8,128)(2,1)S(1)}, bf16[1,256,256]{2,1,0:T(8,128)(2,1)S(1)}, u32[]{:S(2)}, u32[]{:S(2)}) collective-permute-start(bf16[1,256,256]{2,1,0:T(8,128)(2,1)S(1)} %copy-done.33), channel_id=1, source_target_pairs={{0,14},{1,15},{2,12},{3,13},{4,10},{5,11},{6,8},{7,9},{8,6},{9,7},... | collective-permute-start | bytes 393224 | tf_op jit(solution)/shard_map/ppermute | solution.py:272
  56.3 6.2 %collective-permute-start.2 = (bf16[1,256,256]{2,1,0:T(8,128)(2,1)S(1)}, bf16[1,256,256]{2,1,0:T(8,128)(2,1)S(1)}, u32[]{:S(2)}, u32[]{:S(2)}) collective-permute-start(bf16[1,256,256]{2,1,0:T(8,128)(2,1)S(1)} %copy-done.32), channel_id=1, source_target_pairs={{30,16},{31,17}} | collective-permute-start | bytes 393224 | tf_op jit(solution)/shard_map/ppermute | solution.py:272
  57.3 5.9 %collective-permute-start.3 = (bf16[1,256,256]{2,1,0:T(8,128)(2,1)S(1)}, bf16[1,256,256]{2,1,0:T(8,128)(2,1)S(1)}, u32[]{:S(2)}, u32[]{:S(2)}) collective-permute-start(bf16[1,256,256]{2,1,0:T(8,128)(2,1)S(1)} %copy-done.31), channel_id=1, source_target_pairs={{30,18},{31,19}} | collective-permute-start | bytes 393224 | tf_op jit(solution)/shard_map/ppermute | solution.py:272
  58.1 5.9 %collective-permute-start.4 = (bf16[1,256,256]{2,1,0:T(8,128)(2,1)S(1)}, bf16[1,256,256]{2,1,0:T(8,128)(2,1)S(1)}, u32[]{:S(2)}, u32[]{:S(2)}) collective-permute-start(bf16[1,256,256]{2,1,0:T(8,128)(2,1)S(1)} %copy-done.30), channel_id=1, source_target_pairs={{30,20},{31,21}} | collective-permute-start | bytes 393224 | tf_op jit(solution)/shard_map/ppermute | solution.py:272
  58.8 5.2 %collective-permute-start.5 = (bf16[1,256,256]{2,1,0:T(8,128)(2,1)S(1)}, bf16[1,256,256]{2,1,0:T(8,128)(2,1)S(1)}, u32[]{:S(2)}, u32[]{:S(2)}) collective-permute-start(bf16[1,256,256]{2,1,0:T(8,128)(2,1)S(1)} %copy-done.29), channel_id=1, source_target_pairs={{30,22},{31,23}} | collective-permute-start | bytes 393224 | tf_op jit(solution)/shard_map/ppermute | solution.py:272
  61.8 2.2 %collective-permute-start.6 = (bf16[1,256,256]{2,1,0:T(8,128)(2,1)S(1)}, bf16[1,256,256]{2,1,0:T(8,128)(2,1)S(1)}, u32[]{:S(2)}, u32[]{:S(2)}) collective-permute-start(bf16[1,256,256]{2,1,0:T(8,128)(2,1)S(1)} %copy-done.28), channel_id=1, source_target_pairs={{30,24},{31,25}} | collective-permute-start | bytes 393224 | tf_op jit(solution)/shard_map/ppermute | solution.py:272
  62.5 1.5 collective-permute-start.7
  63.2 0.8 collective-permute-start.8
  64.1 17.8 %collective-permute-start.15 = (bf16[2,256,256]{2,1,0:T(8,128)(2,1)S(1)}, bf16[2,256,256]{2,1,0:T(8,128)(2,1)S(1)}, u32[]{:S(2)}, u32[]{:S(2)}) collective-permute-start(bf16[2,256,256]{2,1,0:T(8,128)(2,1)S(1)} %pad_maximum_fusion), channel_id=1, source_target_pairs={{0,16},{1,17},{2,18},{3,19},{4,20},{5,21},{6,22},{7,23},{8,24},{9,... | collective-permute-start | bytes 786440 | tf_op jit(solution)/shard_map/ppermute | solution.py:294
  82.0 9.1 %collective-permute-start.17 = (bf16[2,256,256]{2,1,0:T(8,128)(2,1)S(1)}, bf16[2,256,256]{2,1,0:T(8,128)(2,1)S(1)}, u32[]{:S(2)}, u32[]{:S(2)}) collective-permute-start(bf16[2,256,256]{2,1,0:T(8,128)(2,1)S(1)} %broadcast_select_fusion.refs_0_), channel_id=1, source_target_pairs={{0,4},{1,5},{2,6},{3,7},{4,0},{5,1},{6,2},{7,3},{8,12},{9,13},{10,... | collective-permute-start | bytes 786440 | tf_op jit(solution)/shard_map/ppermute | solution.py:312
  86.7 8.9 %collective-permute-start.16 = (bf16[2,256,256]{2,1,0:T(8,128)(2,1)S(1)}, bf16[2,256,256]{2,1,0:T(8,128)(2,1)S(1)}, u32[]{:S(2)}, u32[]{:S(2)}) collective-permute-start(bf16[2,256,256]{2,1,0:T(8,128)(2,1)S(1)} %broadcast_select_fusion.refs_0_), channel_id=1, source_target_pairs={{0,2},{1,3},{2,0},{3,1},{4,6},{5,7},{6,4},{7,5},{8,10},{9,11},{10,... | collective-permute-start | bytes 786440 | tf_op jit(solution)/shard_map/ppermute | solution.py:312
  89.3 9.2 %collective-permute-start.18 = (bf16[2,256,256]{2,1,0:T(8,128)(2,1)S(1)}, bf16[2,256,256]{2,1,0:T(8,128)(2,1)S(1)}, u32[]{:S(2)}, u32[]{:S(2)}) collective-permute-start(bf16[2,256,256]{2,1,0:T(8,128)(2,1)S(1)} %broadcast_select_fusion.refs_0_), channel_id=1, source_target_pairs={{0,8},{1,9},{2,10},{3,11},{4,12},{5,13},{6,14},{7,15},{8,0},{9,1},... | collective-permute-start | bytes 786440 | tf_op jit(solution)/shard_map/ppermute | solution.py:312
  91.0 11.6 %collective-permute-start.21 = (bf16[2,256,256]{2,1,0:T(8,128)(2,1)S(1)}, bf16[2,256,256]{2,1,0:T(8,128)(2,1)S(1)}, u32[]{:S(2)}, u32[]{:S(2)}) collective-permute-start(bf16[2,256,256]{2,1,0:T(8,128)(2,1)S(1)} %collective-permute-done.17.refs_2_), channel_id=1, source_target_pairs={{0,8},{1,9},{2,10},{3,11},{4,12},{5,13},{6,14},{7,15},{8,0},{9,1},... | collective-permute-start | bytes 786440 | tf_op jit(solution)/shard_map/ppermute | solution.py:312
  95.6 11.2 %collective-permute-start.19 = (bf16[2,256,256]{2,1,0:T(8,128)(2,1)S(1)}, bf16[2,256,256]{2,1,0:T(8,128)(2,1)}, u32[]{:S(2)}, u32[]{:S(2)}) collective-permute-start(bf16[2,256,256]{2,1,0:T(8,128)(2,1)S(1)} %collective-permute-done.16.refs_1_), channel_id=1, source_target_pairs={{0,4},{1,5},{2,6},{3,7},{4,0},{5,1},{6,2},{7,3},{8,12},{9,13},{10,... | collective-permute-start | bytes 786440 | tf_op jit(solution)/shard_map/ppermute | solution.py:312
  98.6 8.2 %collective-permute-start.20 = (bf16[2,256,256]{2,1,0:T(8,128)(2,1)S(1)}, bf16[2,256,256]{2,1,0:T(8,128)(2,1)}, u32[]{:S(2)}, u32[]{:S(2)}) collective-permute-start(bf16[2,256,256]{2,1,0:T(8,128)(2,1)S(1)} %collective-permute-done.18.refs_3_), channel_id=1, source_target_pairs={{0,2},{1,3},{2,0},{3,1},{4,6},{5,7},{6,4},{7,5},{8,10},{9,11},{10,... | collective-permute-start | bytes 786440 | tf_op jit(solution)/shard_map/ppermute | solution.py:312
  102.6 7.9 %collective-permute-start.22 = (bf16[2,256,256]{2,1,0:T(8,128)(2,1)S(1)}, bf16[2,256,256]{2,1,0:T(8,128)(2,1)S(1)}, u32[]{:S(2)}, u32[]{:S(2)}) collective-permute-start(bf16[2,256,256]{2,1,0:T(8,128)(2,1)S(1)} %collective-permute-done.21.refs_6_), channel_id=1, source_target_pairs={{0,2},{1,3},{2,0},{3,1},{4,6},{5,7},{6,4},{7,5},{8,10},{9,11},{10,... | collective-permute-start | bytes 786440 | tf_op jit(solution)/shard_map/ppermute | solution.py:312
  117.6 16.7 %collective-permute-start.23 = (bf16[2048,256]{1,0:T(8,128)(2,1)S(1)}, bf16[2048,256]{1,0:T(8,128)(2,1)}, u32[]{:S(2)}, u32[]{:S(2)}) collective-permute-start(bf16[2048,256]{1,0:T(8,128)(2,1)S(1)} %pick_other.1), channel_id=1, source_target_pairs={{0,1},{1,0},{2,3},{3,2},{4,5},{5,4},{6,7},{7,6},{8,9},{9,8},{10,11... | collective-permute-start | bytes 3145736 | tf_op jit(solution)/shard_map/ppermute | solution.py:302
  118.8 1.6 %copy-start.20 = (f32[2,2048,128]{2,1,0:T(8,128)S(1)}, f32[2,2048,128]{2,1,0:T(8,128)}, u32[]{:S(2)}) copy-start(f32[2,2048,128]{2,1,0:T(8,128)} %copy-done.19) | copy-start | bytes 6291460
  127.3 7.0 %copy-start.2 = (bf16[2,256,256]{2,1,0:T(8,128)(2,1)S(1)}, bf16[2,256,256]{2,1,0:T(8,128)(2,1)}, u32[]{:S(2)}) copy-start(bf16[2,256,256]{2,1,0:T(8,128)(2,1)} %copy-done) | copy-start | bytes 786436
  127.3 7.0 %copy-start.5 = (bf16[2,256,256]{2,1,0:T(8,128)(2,1)S(1)}, bf16[2,256,256]{2,1,0:T(8,128)(2,1)}, u32[]{:S(2)}) copy-start(bf16[2,256,256]{2,1,0:T(8,128)(2,1)} %copy-done.3) | copy-start | bytes 786436
  127.3 7.0 %copy-start.8 = (bf16[2,256,256]{2,1,0:T(8,128)(2,1)S(1)}, bf16[2,256,256]{2,1,0:T(8,128)(2,1)}, u32[]{:S(2)}) copy-start(bf16[2,256,256]{2,1,0:T(8,128)(2,1)} %copy-done.6) | copy-start | bytes 786436
  127.3 7.0 %copy-start.11 = (bf16[2,256,256]{2,1,0:T(8,128)(2,1)S(1)}, bf16[2,256,256]{2,1,0:T(8,128)(2,1)}, u32[]{:S(2)}) copy-start(bf16[2,256,256]{2,1,0:T(8,128)(2,1)} %copy-done.9) | copy-start | bytes 786436
  127.3 7.0 %copy-start.14 = (bf16[2,256,256]{2,1,0:T(8,128)(2,1)S(1)}, bf16[2,256,256]{2,1,0:T(8,128)(2,1)}, u32[]{:S(2)}) copy-start(bf16[2,256,256]{2,1,0:T(8,128)(2,1)} %copy-done.12) | copy-start | bytes 786436
  (13 other events, 12.1 us)

commit v13 on v12

--- a/solution.py
+++ b/solution.py
@@ -121,7 +121,7 @@
         save_state(*work[1:], out_ref)
 
 
-def prefix_kernel(factor, count, steps, which_ref, q_ref, *refs):
+def prefix_kernel(factor, last, count, steps, which_ref, q_ref, *refs):
     pieces = refs[:count]
     loaded_ref, out_ref, *work, rows_ref = refs[count:]
     step = pl.program_id(0)
@@ -142,7 +142,10 @@
 
     @pl.when(step == steps - 1)
     def _():
-        finish(*work[2:], out_ref)
+        if last:
+            finish(*work[2:], out_ref)
+        else:
+            save_state(*work[1:], out_ref)
 
 
 def wait_all(copies):
@@ -189,10 +192,17 @@
         store(entry, mark_ref).wait()
 
 
-def stage_kernel(owner_ref, place_ref, kept_ref, swapped_ref, *refs):
+def stage_kernel(owner_ref, kept_ref, swapped_ref, *refs):
     outs, (sought_ref, known_ref, in_sems, out_sems) = refs[:-4], refs[-4:]
-    core, chip, is_last = place_ref[0], place_ref[1], place_ref[2]
     chips, sought = sought_ref.shape[:2]
+    replicas = 4 * chips
+    me = lax.axis_index("replica")
+    core, chip, is_last = me % 2, me // 2 % chips, me // 2 == replicas // 2 - 1
+    owners = [owner_ref[prefix] for prefix in range(sought + 1)]
+    after = False
+    for prefix in range(sought):
+        after |= owners[prefix] == replicas - 1
+        owners[prefix] = jnp.where(after, owners[prefix + 1], owners[prefix])
 
     def load(source, step, prefix):
         target = sought_ref.at[step, prefix] if prefix < sought else known_ref.at[step, 0]
@@ -208,9 +218,9 @@
 
     for step in range(chips):
         for prefix in range(sought):
-            start(step, prefix, owner_ref[prefix] % 2 == core)
-
-    @pl.when(is_last == 1)
+            start(step, prefix, owners[prefix] % 2 == core)
+
+    @pl.when(is_last)
     def _():
         for step in range(chips):
             start(step, sought, core == 1)
@@ -220,7 +230,7 @@
             load(kept_ref, step, prefix).wait()
         store(step).start()
 
-    @pl.when(is_last == 1)
+    @pl.when(is_last)
     def _():
         for step in range(chips):
             load(kept_ref, step, sought).wait()
@@ -230,7 +240,7 @@
     wait_all([store(step) for step in range(chips)])
 
 
-def multicast(prefix_cache, owners, readers, outgoing, local):
+def multicast(prefix_cache, owners, readers, outgoing, local, fold_moved):
     replicas = lax.axis_size("replica")
     me = lax.axis_index("replica")
     half = replicas // 2
@@ -250,7 +260,7 @@
     staged = pl.pallas_call(
         stage_kernel,
         out_shape=(pieces,) * chips + (piece,) * chips,
-        in_specs=[IN_SMEM] * 2 + [IN_HBM] * 2,
+        in_specs=[IN_SMEM] + [IN_HBM] * 2,
         out_specs=(IN_HBM,) * (2 * chips),
         scratch_shapes=[
             pltpu.VMEM((chips, *pieces.shape), split.dtype),
@@ -260,12 +270,7 @@
         ],
         compiler_params=COPY_PARAMS,
         name="stage_prefix",
-    )(
-        sought,
-        jnp.stack([me % 2, chip, (me // 2 == replicas // 2 - 1).astype(jnp.int32)]),
-        split,
-        swapped,
-    )
+    )(owners, split, swapped)
 
     def to_peers(staged, senders):
         return [
@@ -281,7 +286,11 @@
         return own
 
     passed = to_peers(staged[:chips], range(replicas))
-    passed[0], local, *known_staged = lax.optimization_barrier((passed[0], local, *staged[chips:]))
+    wanted = jnp.stack([readers[me], readers[me ^ 1]])
+    place = jnp.where(wanted == known, 0, wanted + (wanted < known))
+    passed[0], local, place, *known_staged = lax.optimization_barrier(
+        (passed[0], local, place, *staged[chips:])
+    )
     passed_known = to_peers(known_staged, (replicas - 2, replicas - 1))
     last_chip = jnp.full((1,), chips - 1, jnp.int32)
     found = jnp.concatenate(
@@ -292,10 +301,9 @@
     )
     source = jnp.concatenate([jnp.full((1,), replicas - 1, jnp.int32), sought])
     passed = lax.ppermute(found, "replica", [(i, (i + half) % replicas) for i in range(replicas)])
+    passed, state_now = lax.optimization_barrier((passed, fold_moved(arrived, local)))
     held = jnp.where((source // half == me // half)[:, None, None], found, passed)
-    wanted = jnp.stack([readers[me], readers[me ^ 1]])
-    place = jnp.where(wanted == known, 0, wanted + (wanted < known))
-    return held, place, local, arrived
+    return held, place, state_now
 
 
 def swap_cores(rows):
@@ -394,58 +402,68 @@
         cost_estimate=cost(row_count, tokens + own_cache.shape[0], size),
         name="local_keys",
     )(ctx_len, queries, suffix_kv, own_cache)
-    held, place, state_now, arrived = multicast(prefix_cache, owners, readers, outgoing, local)
-
-    rows = arrived.shape[1]
-    group = max(n for n in range(1, replicas + 1) if replicas % n == 0 and n * rows <= CHUNK)
-    steps = max(1, replicas // group // 2)
-    for first in range(0, replicas // group, steps):
-        state_now = pl.pallas_call(
-            functools.partial(moved_kernel, factor, steps),
-            out_shape=state,
-            grid=(steps,),
-            in_specs=[
-                whole(queries.shape),
-                pl.BlockSpec((group, rows, 2 * size), lambda i, first=first: (first + i, 0, 0)),
-                whole(state.shape),
-            ],
-            out_specs=whole(state.shape),
-            scratch_shapes=work,
+    def fold_moved(arrived, state_now):
+        rows = arrived.shape[1]
+        group = max(n for n in range(1, replicas + 1) if replicas % n == 0 and n * rows <= CHUNK)
+        steps = max(1, replicas // group // 2)
+        for first in range(0, replicas // group, steps):
+            state_now = pl.pallas_call(
+                functools.partial(moved_kernel, factor, steps),
+                out_shape=state,
+                grid=(steps,),
+                in_specs=[
+                    whole(queries.shape),
+                    pl.BlockSpec((group, rows, 2 * size), lambda i, first=first: (first + i, 0, 0)),
+                    whole(state.shape),
+                ],
+                out_specs=whole(state.shape),
+                scratch_shapes=work,
+                compiler_params=PARAMS,
+                cost_estimate=cost(row_count, steps * group * rows, size),
+                name="moved_keys",
+            )(queries, arrived, state_now)
+        return state_now
+
+    def fold_prefix(pieces, others, state_now, last):
+        rows = pieces[0].shape[1]
+        keys = 2 * len(pieces) * rows
+        steps = max(1, keys // CHUNK)
+        while keys % (steps * size):
+            steps -= 1
+        target = result if last else state
+        return pl.pallas_call(
+            functools.partial(prefix_kernel, factor, last, len(pieces) + 1, steps),
+            out_shape=target,
+            grid_spec=pltpu.PrefetchScalarGridSpec(
+                num_scalar_prefetch=1,
+                grid=(steps,),
+                in_specs=[
+                    whole(queries.shape),
+                    *[pl.BlockSpec((None, rows, 2 * size), lambda i, which: (which[0], 0, 0))]
+                    * len(pieces),
+                    whole(others.shape),
+                    whole(state.shape),
+                ],
+                out_specs=whole(target.shape),
+                scratch_shapes=[*work, pltpu.VMEM((keys, 2 * size), jnp.bfloat16)],
+            ),
             compiler_params=PARAMS,
-            cost_estimate=cost(row_count, steps * group * rows, size),
-            name="moved_keys",
-        )(queries, arrived, state_now)
-
+            cost_estimate=cost(row_count, keys, size),
+            name="prefix_keys",
+        )(place, queries, *pieces, others, state_now)
+
+    held, place, state_now = multicast(
+        prefix_cache, owners, readers, outgoing, local, fold_moved
+    )
     gathered = {0: held}
-    for step in sorted(range(1, replicas // 4), key=lambda step: (step.bit_count(), step)):
+    steps = sorted(range(1, replicas // 4), key=lambda step: (step.bit_count(), step))
+    for step in steps:
         gathered[step] = gather_step(gathered, step)
-    pieces = list(gathered.values())
-    others = from_other(pieces, place)
-    rows = held.shape[1]
-    keys = 2 * len(pieces) * rows
-    steps = max(1, keys // CHUNK)
-    while keys % (steps * size):
-        steps -= 1
-    return pl.pallas_call(
-        functools.partial(prefix_kernel, factor, len(pieces) + 1, steps),
-        out_shape=result,
-        grid_spec=pltpu.PrefetchScalarGridSpec(
-            num_scalar_prefetch=1,
-            grid=(steps,),
-            in_specs=[
-                whole(queries.shape),
-                *[pl.BlockSpec((None, rows, 2 * size), lambda i, which: (which[0], 0, 0))]
-                * len(pieces),
-                whole(others.shape),
-                whole(state.shape),
-            ],
-            out_specs=whole(queries.shape),
-            scratch_shapes=[*work, pltpu.VMEM((keys, 2 * size), jnp.bfloat16)],
-        ),
-        compiler_params=PARAMS,
-        cost_estimate=cost(row_count, keys, size),
-        name="prefix_keys",
-    )(place, queries, *pieces, others, state_now)
+    near = [rows for step, rows in gathered.items() if step.bit_count() < 2]
+    state_now = fold_prefix(near, from_other(near, place), state_now, False)
+    gathered[steps[-1]], state_now = lax.optimization_barrier((gathered[steps[-1]], state_now))
+    far = [rows for step, rows in gathered.items() if step.bit_count() > 1]
+    return fold_prefix(far, from_other(far, place), state_now, True)
 
 
 def solution(mesh):

time: 150 us -> 132 us (0.88)
  waiting for transfers between devices: 43.1 us -> 32.4 us
  local copies, waits for them, and re-layouts: 14.9 us -> 5.59 us
    ppermute x1, waiting for transfers between devices: 9.88 us -> 0.01 us  [multicast(): lax.ppermute(found, 'replica', [(i, (i + half) % replicas) for i in range...]
    unnamed x72 -> x16, local copies, waits for them, and re-layouts: 13.8 us -> 4.31 us
    ppermute x2 -> x3, waiting for transfers between devices: 0.01 us -> 1.9 us  [swap_cores(): lax.ppermute(rows, 'replica', [(i, i ^ 1) for i in range(lax.axis_size('r...]
    select_n x2, other arithmetic: 0.11 us -> 2 us  [choose(): own = jnp.where((away == step)[:, None, None], rows, own)]
    ppermute x14, waiting for transfers between devices: 20.9 us -> 19.3 us  [to_peers(): lax.ppermute(rows, 'replica', [(i, i ^ 2 * step) for i in senders])]
    pallas_call x3 -> x4, Pallas kernels: 28.7 us -> 29.1 us  [the longest x2 15.3 us: fold_prefix(): pl.pallas_call(functools.partial(prefix_kernel, factor, last, len(pieces)...]
  transfers between devices with their start and end apart: 25 -> 26, of which waited for: 9 -> 7; matrix products, arithmetic and copies ran while one was open for 3% -> 5% of each run, Pallas kernels for 16% -> 23%
where the time goes in v13:
time: 132 us; the launch traced here: 131 us
  starting transfers between devices  45.3 us (34%)
  Pallas kernels  39.5 us (30%)
  waiting for transfers between devices  32.4 us (25%)
  local copies, waits for them, and re-layouts  5.59 us (4%)
  other arithmetic  4.83 us (4%)
  between operations  3.68 us (3%)
    ppermute x14, waiting for transfers between devices, to_peers(): lax.ppermute(rows, 'replica', [(i, i ^ 2 * step) for i in senders])  19.3 us
    ppermute x14, starting transfers between devices, to_peers(): lax.ppermute(rows, 'replica', [(i, i ^ 2 * step) for i in senders])  18 us
    pallas_call x2, Pallas kernels, fold_prefix(): pl.pallas_call(functools.partial(prefix_kernel, factor, last, len(pieces)...  15.3 us
    pallas_call x2, Pallas kernels, fold_moved(): pl.pallas_call(functools.partial(moved_kernel, factor, steps), out_shape=...  13.9 us
    ppermute x7, starting transfers between devices, gather_step(): return lax.ppermute(gathered[step ^ 1 << last], 'replica', pairs)  12.1 us
    ppermute x7, waiting for transfers between devices, gather_step(): return lax.ppermute(gathered[step ^ 1 << last], 'replica', pairs)  11.2 us
    ppermute x1, starting transfers between devices, multicast(): lax.ppermute(found, 'replica', [(i, (i + half) % replicas) for i in range...  7.7 us
    all_to_all x1, starting transfers between devices, multicast(): lax.all_to_all(outgoing, 'replica', split_axis=0, concat_axis=0, tiled=True)  6.92 us
  transfers between devices with their start and end apart: 26, of which 7 were waited for; matrix products, arithmetic and copies ran while one was open for 5% of the time, Pallas kernels for 23%

profile of v13, /device:TPU:0, one launch (start us, length us, event | category | flops | bytes accessed | tf_op | source)
XLA Modules:
  0.0 131.3 jit_solution(2408172866499157918)
XLA Ops:
  0.0 0.5 collective-permute-start
  1.1 3.6 %pack_moved.1 = bf16[32,128,256]{2,1,0:T(8,128)(2,1)} custom-call(s32[1,32]{1,0:T(1,128)} %target_ref.1, s32[1,32]{1,0:T(1,128)} %block_ref.1, s32[1]{0:T(128)S(6)} %copy.13.count_ref, bf16[32,128,256]{2,1,0:T(8,128)(2,1)} %pool_ref.1), custom_call_target="tpu_custom_call" | custom-call | tf_op jit(solution)/shard_map/pack_moved/pallas_call | solution.py:380
  4.8 1.4 %copy-done.5 = bf16[4096,256]{1,0:T(8,128)(2,1)} copy-done((bf16[4096,256]{1,0:T(8,128)(2,1)}, bf16[4096,256]{1,0:T(8,128)(2,1)S(1)}, u32[]{:S(2)}) %copy-start.5) | copy-done | bytes 2097176
  6.1 6.9 %all-to-all-start = ((bf16[32,128,256]{2,1,0:T(8,128)(2,1)}), bf16[32,128,256]{2,1,0:T(8,128)(2,1)S(1)}, u32[]{:S(2)}, u32[]{:S(2)}) async-start(bf16[32,128,256]{2,1,0:T(8,128)(2,1)} %pack_moved.1), calls=%async_computation | async-start | bytes 4194304 | tf_op jit(solution)/shard_map/all_to_all | solution.py:256
  13.7 2.6 %local_keys.1.loaded_ref = f32[2,2048,128]{2,1,0:T(8,128)S(1)} custom-call(s32[1]{0:T(128)S(6)} %copy.12.len_ref, bf16[256,1024]{1,0:T(8,128)(2,1)S(1)} %copy-done, bf16[256,256]{1,0:T(8,128)(2,1)S(1)} %copy-done.2, bf16[512,256]{1,0:T(8,128)(2,1)S(1)} %copy-done.1), custom_call_target="tpu_custom_call" | custom-call | flops 2415919104 | bytes 393216 | tf_op jit(solution)/shard_map/local_keys/pallas_call | solution.py:394
  16.3 1.3 %copy-done.3 = f32[2,2048,128]{2,1,0:T(8,128)} copy-done((f32[2,2048,128]{2,1,0:T(8,128)}, f32[2,2048,128]{2,1,0:T(8,128)S(1)}, u32[]{:S(2)}) %copy-start.3) | copy-done | bytes 2097176
  17.7 3.0 %stage_prefix.1 = (bf16[1,256,256]{2,1,0:T(8,128)(2,1)}, bf16[1,256,256]{2,1,0:T(8,128)(2,1)}, bf16[1,256,256]{2,1,0:T(8,128)(2,1)}, bf16[1,256,256]{2,1,0:T(8,1...) custom-call(s32[2]{0:T(128)} %owner_ref.1, ...), custom_call_target="tpu_custom_call" | custom-call | tf_op jit(solution)/shard_map/stage_prefix/pallas_call | solution.py:260
  20.7 1.8 %collective-permute-start.1 = (bf16[1,256,256]{2,1,0:T(8,128)(2,1)}, bf16[1,256,256]{2,1,0:T(8,128)(2,1)S(1)}, u32[]{:S(2)}, u32[]{:S(2)}) collective-permute-start(bf16[1,256,256]{2,1,0:T(8,128)(2,1)} %get-tuple-element.39), channel_id=1, source_target_pairs={{0,2},{1,3},{2,0},{3,1},{4,6},{5,7},{6,4},{7,5},{8,10},{9,11},{10,... | collective-permute-start | bytes 393224 | tf_op jit(solution)/shard_map/ppermute | solution.py:277
  22.5 2.4 %collective-permute-start.10 = (bf16[1,256,256]{2,1,0:T(8,128)(2,1)}, bf16[1,256,256]{2,1,0:T(8,128)(2,1)S(1)}, u32[]{:S(2)}, u32[]{:S(2)}) collective-permute-start(bf16[1,256,256]{2,1,0:T(8,128)(2,1)} %get-tuple-element.58), channel_id=1, source_target_pairs={{0,12},{1,13},{2,14},{3,15},{4,8},{5,9},{6,10},{7,11},{8,4},{9,5},... | collective-permute-start | bytes 393224 | tf_op jit(solution)/shard_map/ppermute | solution.py:277
  24.9 0.6 collective-permute-start.11
  25.5 1.5 %collective-permute-start.12 = (bf16[1,256,256]{2,1,0:T(8,128)(2,1)}, bf16[1,256,256]{2,1,0:T(8,128)(2,1)S(1)}, u32[]{:S(2)}, u32[]{:S(2)}) collective-permute-start(bf16[1,256,256]{2,1,0:T(8,128)(2,1)} %get-tuple-element.60), channel_id=1, source_target_pairs={{0,8},{1,9},{2,10},{3,11},{4,12},{5,13},{6,14},{7,15},{8,0},{9,1},... | collective-permute-start | bytes 393224 | tf_op jit(solution)/shard_map/ppermute | solution.py:277
  26.9 0.7 fusion.1
  27.6 0.6 fusion.4
  28.2 2.0 %compare_select_fusion.which_ref = s32[2]{0:T(128)S(1)} fusion(s32[1]{0:T(128)} %get-tuple-element.74, s32[1]{0:T(128)} %get-tuple-element.73, s32[]{:T(128)} %fusion.1), kind=kLoop, calls=%fused_computation.6 | loop fusion | flops 12 | bytes 20 | tf_op jit(solution)/shard_map/jit(_where)/select_n | solution.py:290
  30.2 1.5 %collective-permute-start.13 = (bf16[1,256,256]{2,1,0:T(8,128)(2,1)}, bf16[1,256,256]{2,1,0:T(8,128)(2,1)}, u32[]{:S(2)}, u32[]{:S(2)}) collective-permute-start(bf16[1,256,256]{2,1,0:T(8,128)(2,1)} %get-tuple-element.61), channel_id=1, source_target_pairs={{0,6},{1,7},{2,4},{3,5},{4,2},{5,3},{6,0},{7,1},{8,14},{9,15},{10,... | collective-permute-start | bytes 393224 | tf_op jit(solution)/shard_map/ppermute | solution.py:277
  31.7 0.4 collective-permute-done.1
  32.1 1.1 collective-permute-start.14
  33.1 18.5 %collective-permute-done.10 = bf16[1,256,256]{2,1,0:T(8,128)(2,1)S(1)} collective-permute-done((bf16[1,256,256]{2,1,0:T(8,128)(2,1)}, bf16[1,256,256]{2,1,0:T(8,128)(2,1)S(1)}, u32[]{:S(2)}, u32[]{:S(2)}) %collective-permute-start.10) | collective-permute-done | bytes 131104 | tf_op jit(solution)/shard_map/ppermute | solution.py:277
  51.7 4.6 %collective-permute-start.9 = (bf16[1,256,256]{2,1,0:T(8,128)(2,1)}, bf16[1,256,256]{2,1,0:T(8,128)(2,1)}, u32[]{:S(2)}, u32[]{:S(2)}) collective-permute-start(bf16[1,256,256]{2,1,0:T(8,128)(2,1)} %get-tuple-element.57), channel_id=1, source_target_pairs={{0,14},{1,15},{2,12},{3,13},{4,10},{5,11},{6,8},{7,9},{8,6},{9,7},... | collective-permute-start | bytes 393224 | tf_op jit(solution)/shard_map/ppermute | solution.py:277
  56.3 0.7 collective-permute-start.2
  56.9 0.4 collective-permute-done.12
  57.3 0.7 collective-permute-start.3
  58.0 0.6 fusion.3
  60.7 0.7 collective-permute-start.4
  61.4 0.7 collective-permute-start.5
  62.1 0.7 collective-permute-start.6
  62.8 0.7 collective-permute-start.7
  63.5 0.7 collective-permute-start.8
  64.1 1.0 select_select_fusion
  65.2 1.0 select_select_fusion.1
  66.2 7.7 %collective-permute-start.15 = (bf16[2,256,256]{2,1,0:T(8,128)(2,1)S(1)}, bf16[2,256,256]{2,1,0:T(8,128)(2,1)S(1)}, u32[]{:S(2)}, u32[]{:S(2)}) collective-permute-start(bf16[2,256,256]{2,1,0:T(8,128)(2,1)S(1)} %pad_maximum_fusion), channel_id=1, source_target_pairs={{0,16},{1,17},{2,18},{3,19},{4,20},{5,21},{6,22},{7,23},{8,24},{9,... | collective-permute-start | bytes 786440 | tf_op jit(solution)/shard_map/ppermute | solution.py:303
  73.9 1.6 %copy-done.4 = f32[2,2048,128]{2,1,0:T(8,128)S(1)} copy-done((f32[2,2048,128]{2,1,0:T(8,128)S(1)}, f32[2,2048,128]{2,1,0:T(8,128)}, u32[]{:S(2)}) %copy-start.4) | copy-done | bytes 2097176
  75.5 6.9 %moved_keys.2.loaded_ref = f32[2,2048,128]{2,1,0:T(8,128)S(1)} custom-call(bf16[256,1024]{1,0:T(8,128)(2,1)S(1)} %copy-done, bf16[32,128,256]{2,1,0:T(8,128)(2,1)S(1)} %all-to-all-done.kv_ref, f32[2,2048,128]{2,1,0:T(8,128)S(1)} %copy-done.4), custom_call_target="tpu_custom_call" | custom-call | flops 6442450944 | bytes 1048576 | tf_op jit(solution)/shard_map/moved_keys/pallas_call | solution.py:410
  82.5 6.9 %moved_keys.3.refs_5_ = f32[2,2048,128]{2,1,0:T(8,128)S(1)} custom-call(bf16[256,1024]{1,0:T(8,128)(2,1)S(1)} %copy-done, bf16[32,128,256]{2,1,0:T(8,128)(2,1)S(1)} %all-to-all-done.kv_ref, f32[2,2048,128]{2,1,0:T(8,128)S(1)} %moved_keys.2.loaded_ref), custom_call_target="tpu_custom_call" | custom-call | flops 6442450944 | bytes 1048576 | tf_op jit(solution)/shard_map/moved_keys/pallas_call | solution.py:410
  89.5 1.5 %collective-permute-start.16 = (bf16[2,256,256]{2,1,0:T(8,128)(2,1)S(1)}, bf16[2,256,256]{2,1,0:T(8,128)(2,1)S(1)}, u32[]{:S(2)}, u32[]{:S(2)}) collective-permute-start(bf16[2,256,256]{2,1,0:T(8,128)(2,1)S(1)} %broadcast_select_fusion.refs_0_), channel_id=1, source_target_pairs={{0,2},{1,3},{2,0},{3,1},{4,6},{5,7},{6,4},{7,5},{8,10},{9,11},{10,... | collective-permute-start | bytes 786440 | tf_op jit(solution)/shard_map/ppermute | solution.py:320
  91.0 5.9 %collective-permute-start.18 = (bf16[2,256,256]{2,1,0:T(8,128)(2,1)S(1)}, bf16[2,256,256]{2,1,0:T(8,128)(2,1)S(1)}, u32[]{:S(2)}, u32[]{:S(2)}) collective-permute-start(bf16[2,256,256]{2,1,0:T(8,128)(2,1)S(1)} %broadcast_select_fusion.refs_0_), channel_id=1, source_target_pairs={{0,8},{1,9},{2,10},{3,11},{4,12},{5,13},{6,14},{7,15},{8,0},{9,1},... | collective-permute-start | bytes 786440 | tf_op jit(solution)/shard_map/ppermute | solution.py:320
  96.9 1.1 collective-permute-start.20
  98.1 3.2 %collective-permute-done.18.refs_3_ = bf16[2,256,256]{2,1,0:T(8,128)(2,1)S(1)} collective-permute-done((bf16[2,256,256]{2,1,0:T(8,128)(2,1)S(1)}, bf16[2,256,256]{2,1,0:T(8,128)(2,1)S(1)}, u32[]{:S(2)}, u32[]{:S(2)}) %collective-permute-start.18) | collective-permute-done | bytes 262176 | tf_op jit(solution)/shard_map/ppermute | solution.py:320
  101.3 2.0 %collective-permute-done.20.refs_2_ = bf16[2,256,256]{2,1,0:T(8,128)(2,1)S(1)} collective-permute-done((bf16[2,256,256]{2,1,0:T(8,128)(2,1)S(1)}, bf16[2,256,256]{2,1,0:T(8,128)(2,1)S(1)}, u32[]{:S(2)}, u32[]{:S(2)}) %collective-permute-start.20) | collective-permute-done | bytes 262176 | tf_op jit(solution)/shard_map/ppermute | solution.py:320
  103.3 0.6 pick_other.2
  104.0 1.2 collective-permute-start.17
  105.2 1.5 %collective-permute-start.19 = (bf16[2,256,256]{2,1,0:T(8,128)(2,1)S(1)}, bf16[2,256,256]{2,1,0:T(8,128)(2,1)S(1)}, u32[]{:S(2)}, u32[]{:S(2)}) collective-permute-start(bf16[2,256,256]{2,1,0:T(8,128)(2,1)S(1)} %collective-permute-done.18.refs_3_), channel_id=1, source_target_pairs={{0,2},{1,3},{2,0},{3,1},{4,6},{5,7},{6,4},{7,5},{8,10},{9,11},{10,... | collective-permute-start | bytes 786440 | tf_op jit(solution)/shard_map/ppermute | solution.py:320
  106.7 5.9 %collective-permute-done.21.refs_2_ = bf16[2,256,256]{2,1,0:T(8,128)(2,1)S(1)} collective-permute-done((bf16[2,256,256]{2,1,0:T(8,128)(2,1)S(1)}, bf16[2,256,256]{2,1,0:T(8,128)(2,1)S(1)}, u32[]{:S(2)}, u32[]{:S(2)}) %collective-permute-start.21) | collective-permute-done | bytes 262176 | tf_op jit(solution)/shard_map/ppermute | solution.py:320
  112.7 0.8 collective-permute-start.22
  113.4 7.3 %prefix_keys.2.refs_5_ = f32[2,2048,128]{2,1,0:T(8,128)S(1)} custom-call(s32[2]{0:T(128)S(1)} %compare_select_fusion.which_ref, bf16[256,1024]{1,0:T(8,128)(2,1)S(1)} %copy-done, bf16[2,256,256]{2,1,0:T(8,128)(2,1)S(1)} %broadcast_select_fusion.refs_0_, bf16[2,256,256]{2,1,0:T(8,128)(2,1)S(1)} %collective-permute-done.16.refs_1_, ...), custom_call_target="tpu_custom_call" | custom-call | flops 6442450944 | bytes 1048576 | tf_op jit(solution)/shard_map/prefix_keys/pallas_call | solution.py:434
  120.8 0.6 pick_other.3
  121.5 1.9 %collective-permute-done.24.refs_4_ = bf16[1024,256]{1,0:T(8,128)(2,1)S(1)} collective-permute-done((bf16[1024,256]{1,0:T(8,128)(2,1)S(1)}, bf16[1024,256]{1,0:T(8,128)(2,1)S(1)}, u32[]{:S(2)}, u32[]{:S(2)}) %collective-permute-start.24) | collective-permute-done | bytes 524320 | tf_op jit(solution)/shard_map/ppermute | solution.py:310
  123.4 7.9 %prefix_keys.3 = bf16[256,1024]{1,0:T(8,128)(2,1)} custom-call(s32[2]{0:T(128)S(1)} %compare_select_fusion.which_ref, bf16[256,1024]{1,0:T(8,128)(2,1)S(1)} %copy-done, bf16[2,256,256]{2,1,0:T(8,128)(2,1)S(1)} %collective-permute-done.17.refs_0_, bf16[2,256,256]{2,1,0:T(8,128)(2,1)S(1)} %collective-permute-done.19.refs_1_, ...), custom_call_target="tpu_custom_call" | custom-call | flops 6442450944 | bytes 1048576 | tf_op jit(solution)/shard_map/prefix_keys/pallas_call | solution.py:434
  (39 shorter events, 0.5 us)
Async XLA Ops:
  0.0 4.7 %collective-permute-start = (bf16[4096,256]{1,0:T(8,128)(2,1)}, bf16[4096,256]{1,0:T(8,128)(2,1)S(1)}, u32[]{:S(2)}, u32[]{:S(2)}) collective-permute-start(bf16[4096,256]{1,0:T(8,128)(2,1)} %param.15), channel_id=1, source_target_pairs={{0,1},{1,0},{2,3},{3,2},{4,5},{5,4},{6,7},{7,6},{8,9},{9,8},{10,11... | collective-permute-start | bytes 6291464 | tf_op jit(solution)/shard_map/ppermute | solution.py:310
  4.7 9.0 %copy-start = (bf16[256,1024]{1,0:T(8,128)(2,1)S(1)}, bf16[256,1024]{1,0:T(8,128)(2,1)}, u32[]{:S(2)}) copy-start(bf16[256,1024]{1,0:T(8,128)(2,1)} %q_ref.9) | copy-start | bytes 1572868
  4.7 9.0 %copy-start.1 = (bf16[512,256]{1,0:T(8,128)(2,1)S(1)}, bf16[512,256]{1,0:T(8,128)(2,1)}, u32[]{:S(2)}) copy-start(bf16[512,256]{1,0:T(8,128)(2,1)} %own_ref.1) | copy-start | bytes 786436
  4.7 9.0 %copy-start.2 = (bf16[256,256]{1,0:T(8,128)(2,1)S(1)}, bf16[256,256]{1,0:T(8,128)(2,1)}, u32[]{:S(2)}) copy-start(bf16[256,256]{1,0:T(8,128)(2,1)} %suffix_ref.1) | copy-start | bytes 393220
  4.7 1.4 %copy-start.5 = (bf16[4096,256]{1,0:T(8,128)(2,1)}, bf16[4096,256]{1,0:T(8,128)(2,1)S(1)}, u32[]{:S(2)}) copy-start(bf16[4096,256]{1,0:T(8,128)(2,1)S(1)} %collective-permute-done) | copy-start | bytes 6291460
  6.1 67.8 %all-to-all-start = ((bf16[32,128,256]{2,1,0:T(8,128)(2,1)}), bf16[32,128,256]{2,1,0:T(8,128)(2,1)S(1)}, u32[]{:S(2)}, u32[]{:S(2)}) async-start(bf16[32,128,256]{2,1,0:T(8,128)(2,1)} %pack_moved.1), calls=%async_computation | async-start | bytes 4194304 | tf_op jit(solution)/shard_map/all_to_all | solution.py:256
  16.3 1.3 %copy-start.3 = (f32[2,2048,128]{2,1,0:T(8,128)}, f32[2,2048,128]{2,1,0:T(8,128)S(1)}, u32[]{:S(2)}) copy-start(f32[2,2048,128]{2,1,0:T(8,128)S(1)} %local_keys.1.loaded_ref) | copy-start | bytes 6291460
  17.7 9.3 %copy-start.6 = (s32[2]{0:T(128)S(1)}, s32[2]{0:T(128)}, u32[]{:S(2)}) copy-start(s32[2]{0:T(128)} %owner_ref.1) | copy-start | bytes 28
  17.7 9.9 %copy-start.7 = (s32[32]{0:T(128)S(1)}, s32[32]{0:T(128)}, u32[]{:S(2)}) copy-start(s32[32]{0:T(128)} %param.17) | copy-start | bytes 388
  20.7 11.4 %collective-permute-start.1 = (bf16[1,256,256]{2,1,0:T(8,128)(2,1)}, bf16[1,256,256]{2,1,0:T(8,128)(2,1)S(1)}, u32[]{:S(2)}, u32[]{:S(2)}) collective-permute-start(bf16[1,256,256]{2,1,0:T(8,128)(2,1)} %get-tuple-element.39), channel_id=1, source_target_pairs={{0,2},{1,3},{2,0},{3,1},{4,6},{5,7},{6,4},{7,5},{8,10},{9,11},{10,... | collective-permute-start | bytes 393224 | tf_op jit(solution)/shard_map/ppermute | solution.py:277
  22.5 29.1 %collective-permute-start.10 = (bf16[1,256,256]{2,1,0:T(8,128)(2,1)}, bf16[1,256,256]{2,1,0:T(8,128)(2,1)S(1)}, u32[]{:S(2)}, u32[]{:S(2)}) collective-permute-start(bf16[1,256,256]{2,1,0:T(8,128)(2,1)} %get-tuple-element.58), channel_id=1, source_target_pairs={{0,12},{1,13},{2,14},{3,15},{4,8},{5,9},{6,10},{7,11},{8,4},{9,5},... | collective-permute-start | bytes 393224 | tf_op jit(solution)/shard_map/ppermute | solution.py:277
  24.9 31.3 %collective-permute-start.11 = (bf16[1,256,256]{2,1,0:T(8,128)(2,1)}, bf16[1,256,256]{2,1,0:T(8,128)(2,1)S(1)}, u32[]{:S(2)}, u32[]{:S(2)}) collective-permute-start(bf16[1,256,256]{2,1,0:T(8,128)(2,1)} %get-tuple-element.59), channel_id=1, source_target_pairs={{0,10},{1,11},{2,8},{3,9},{4,14},{5,15},{6,12},{7,13},{8,2},{9,3},... | collective-permute-start | bytes 393224 | tf_op jit(solution)/shard_map/ppermute | solution.py:277
  25.5 31.8 %collective-permute-start.12 = (bf16[1,256,256]{2,1,0:T(8,128)(2,1)}, bf16[1,256,256]{2,1,0:T(8,128)(2,1)S(1)}, u32[]{:S(2)}, u32[]{:S(2)}) collective-permute-start(bf16[1,256,256]{2,1,0:T(8,128)(2,1)} %get-tuple-element.60), channel_id=1, source_target_pairs={{0,8},{1,9},{2,10},{3,11},{4,12},{5,13},{6,14},{7,15},{8,0},{9,1},... | collective-permute-start | bytes 393224 | tf_op jit(solution)/shard_map/ppermute | solution.py:277
  30.2 30.5 %collective-permute-start.13 = (bf16[1,256,256]{2,1,0:T(8,128)(2,1)}, bf16[1,256,256]{2,1,0:T(8,128)(2,1)}, u32[]{:S(2)}, u32[]{:S(2)}) collective-permute-start(bf16[1,256,256]{2,1,0:T(8,128)(2,1)} %get-tuple-element.61), channel_id=1, source_target_pairs={{0,6},{1,7},{2,4},{3,5},{4,2},{5,3},{6,0},{7,1},{8,14},{9,15},{10,... | collective-permute-start | bytes 393224 | tf_op jit(solution)/shard_map/ppermute | solution.py:277
  32.1 29.3 %collective-permute-start.14 = (bf16[1,256,256]{2,1,0:T(8,128)(2,1)}, bf16[1,256,256]{2,1,0:T(8,128)(2,1)}, u32[]{:S(2)}, u32[]{:S(2)}) collective-permute-start(bf16[1,256,256]{2,1,0:T(8,128)(2,1)} %get-tuple-element.62), channel_id=1, source_target_pairs={{0,4},{1,5},{2,6},{3,7},{4,0},{5,1},{6,2},{7,3},{8,12},{9,13},{10,... | collective-permute-start | bytes 393224 | tf_op jit(solution)/shard_map/ppermute | solution.py:277
  51.7 10.4 %collective-permute-start.9 = (bf16[1,256,256]{2,1,0:T(8,128)(2,1)}, bf16[1,256,256]{2,1,0:T(8,128)(2,1)}, u32[]{:S(2)}, u32[]{:S(2)}) collective-permute-start(bf16[1,256,256]{2,1,0:T(8,128)(2,1)} %get-tuple-element.57), channel_id=1, source_target_pairs={{0,14},{1,15},{2,12},{3,13},{4,10},{5,11},{6,8},{7,9},{8,6},{9,7},... | collective-permute-start | bytes 393224 | tf_op jit(solution)/shard_map/ppermute | solution.py:277
  56.3 6.5 %collective-permute-start.2 = (bf16[1,256,256]{2,1,0:T(8,128)(2,1)}, bf16[1,256,256]{2,1,0:T(8,128)(2,1)S(1)}, u32[]{:S(2)}, u32[]{:S(2)}) collective-permute-start(bf16[1,256,256]{2,1,0:T(8,128)(2,1)} %get-tuple-element.49), channel_id=1, source_target_pairs={{30,16},{31,17}} | collective-permute-start | bytes 393224 | tf_op jit(solution)/shard_map/ppermute | solution.py:277
  57.3 6.2 %collective-permute-start.3 = (bf16[1,256,256]{2,1,0:T(8,128)(2,1)}, bf16[1,256,256]{2,1,0:T(8,128)(2,1)S(1)}, u32[]{:S(2)}, u32[]{:S(2)}) collective-permute-start(bf16[1,256,256]{2,1,0:T(8,128)(2,1)} %get-tuple-element.50), channel_id=1, source_target_pairs={{30,18},{31,19}} | collective-permute-start | bytes 393224 | tf_op jit(solution)/shard_map/ppermute | solution.py:277
  60.7 4.4 %collective-permute-start.4 = (bf16[1,256,256]{2,1,0:T(8,128)(2,1)}, bf16[1,256,256]{2,1,0:T(8,128)(2,1)S(1)}, u32[]{:S(2)}, u32[]{:S(2)}) collective-permute-start(bf16[1,256,256]{2,1,0:T(8,128)(2,1)} %get-tuple-element.51), channel_id=1, source_target_pairs={{30,20},{31,21}} | collective-permute-start | bytes 393224 | tf_op jit(solution)/shard_map/ppermute | solution.py:277
  61.4 3.8 %collective-permute-start.5 = (bf16[1,256,256]{2,1,0:T(8,128)(2,1)}, bf16[1,256,256]{2,1,0:T(8,128)(2,1)S(1)}, u32[]{:S(2)}, u32[]{:S(2)}) collective-permute-start(bf16[1,256,256]{2,1,0:T(8,128)(2,1)} %get-tuple-element.52), channel_id=1, source_target_pairs={{30,22},{31,23}} | collective-permute-start | bytes 393224 | tf_op jit(solution)/shard_map/ppermute | solution.py:277
  62.1 3.1 %collective-permute-start.6 = (bf16[1,256,256]{2,1,0:T(8,128)(2,1)}, bf16[1,256,256]{2,1,0:T(8,128)(2,1)S(1)}, u32[]{:S(2)}, u32[]{:S(2)}) collective-permute-start(bf16[1,256,256]{2,1,0:T(8,128)(2,1)} %get-tuple-element.53), channel_id=1, source_target_pairs={{30,24},{31,25}} | collective-permute-start | bytes 393224 | tf_op jit(solution)/shard_map/ppermute | solution.py:277
  62.8 2.4 %collective-permute-start.7 = (bf16[1,256,256]{2,1,0:T(8,128)(2,1)}, bf16[1,256,256]{2,1,0:T(8,128)(2,1)S(1)}, u32[]{:S(2)}, u32[]{:S(2)}) collective-permute-start(bf16[1,256,256]{2,1,0:T(8,128)(2,1)} %get-tuple-element.54), channel_id=1, source_target_pairs={{30,26},{31,27}} | collective-permute-start | bytes 393224 | tf_op jit(solution)/shard_map/ppermute | solution.py:277
  63.5 1.7 %collective-permute-start.8 = (bf16[1,256,256]{2,1,0:T(8,128)(2,1)}, bf16[1,256,256]{2,1,0:T(8,128)(2,1)S(1)}, u32[]{:S(2)}, u32[]{:S(2)}) collective-permute-start(bf16[1,256,256]{2,1,0:T(8,128)(2,1)} %get-tuple-element.55), channel_id=1, source_target_pairs={{30,28},{31,29}} | collective-permute-start | bytes 393224 | tf_op jit(solution)/shard_map/ppermute | solution.py:277
  66.2 23.2 %collective-permute-start.15 = (bf16[2,256,256]{2,1,0:T(8,128)(2,1)S(1)}, bf16[2,256,256]{2,1,0:T(8,128)(2,1)S(1)}, u32[]{:S(2)}, u32[]{:S(2)}) collective-permute-start(bf16[2,256,256]{2,1,0:T(8,128)(2,1)S(1)} %pad_maximum_fusion), channel_id=1, source_target_pairs={{0,16},{1,17},{2,18},{3,19},{4,20},{5,21},{6,22},{7,23},{8,24},{9,... | collective-permute-start | bytes 786440 | tf_op jit(solution)/shard_map/ppermute | solution.py:303
  73.9 1.6 %copy-start.4 = (f32[2,2048,128]{2,1,0:T(8,128)S(1)}, f32[2,2048,128]{2,1,0:T(8,128)}, u32[]{:S(2)}) copy-start(f32[2,2048,128]{2,1,0:T(8,128)} %copy-done.3) | copy-start | bytes 6291460
  89.5 8.5 %collective-permute-start.16 = (bf16[2,256,256]{2,1,0:T(8,128)(2,1)S(1)}, bf16[2,256,256]{2,1,0:T(8,128)(2,1)S(1)}, u32[]{:S(2)}, u32[]{:S(2)}) collective-permute-start(bf16[2,256,256]{2,1,0:T(8,128)(2,1)S(1)} %broadcast_select_fusion.refs_0_), channel_id=1, source_target_pairs={{0,2},{1,3},{2,0},{3,1},{4,6},{5,7},{6,4},{7,5},{8,10},{9,11},{10,... | collective-permute-start | bytes 786440 | tf_op jit(solution)/shard_map/ppermute | solution.py:320
  91.0 10.3 %collective-permute-start.18 = (bf16[2,256,256]{2,1,0:T(8,128)(2,1)S(1)}, bf16[2,256,256]{2,1,0:T(8,128)(2,1)S(1)}, u32[]{:S(2)}, u32[]{:S(2)}) collective-permute-start(bf16[2,256,256]{2,1,0:T(8,128)(2,1)S(1)} %broadcast_select_fusion.refs_0_), channel_id=1, source_target_pairs={{0,8},{1,9},{2,10},{3,11},{4,12},{5,13},{6,14},{7,15},{8,0},{9,1},... | collective-permute-start | bytes 786440 | tf_op jit(solution)/shard_map/ppermute | solution.py:320
  96.9 6.4 %collective-permute-start.20 = (bf16[2,256,256]{2,1,0:T(8,128)(2,1)S(1)}, bf16[2,256,256]{2,1,0:T(8,128)(2,1)S(1)}, u32[]{:S(2)}, u32[]{:S(2)}) collective-permute-start(bf16[2,256,256]{2,1,0:T(8,128)(2,1)S(1)} %broadcast_select_fusion.refs_0_), channel_id=1, source_target_pairs={{0,4},{1,5},{2,6},{3,7},{4,0},{5,1},{6,2},{7,3},{8,12},{9,13},{10,... | collective-permute-start | bytes 786440 | tf_op jit(solution)/shard_map/ppermute | solution.py:320
  103.9 9.6 %collective-permute-start.23 = (bf16[1024,256]{1,0:T(8,128)(2,1)S(1)}, bf16[1024,256]{1,0:T(8,128)(2,1)S(1)}, u32[]{:S(2)}, u32[]{:S(2)}) collective-permute-start(bf16[1024,256]{1,0:T(8,128)(2,1)S(1)} %pick_other.2), channel_id=1, source_target_pairs={{0,1},{1,0},{2,3},{3,2},{4,5},{5,4},{6,7},{7,6},{8,9},{9,8},{10,11... | collective-permute-start | bytes 1572872 | tf_op jit(solution)/shard_map/ppermute | solution.py:310
  104.0 8.7 %collective-permute-start.21 = (bf16[2,256,256]{2,1,0:T(8,128)(2,1)S(1)}, bf16[2,256,256]{2,1,0:T(8,128)(2,1)S(1)}, u32[]{:S(2)}, u32[]{:S(2)}) collective-permute-start(bf16[2,256,256]{2,1,0:T(8,128)(2,1)S(1)} %collective-permute-done.20.refs_2_), channel_id=1, source_target_pairs={{0,8},{1,9},{2,10},{3,11},{4,12},{5,13},{6,14},{7,15},{8,0},{9,1},... | collective-permute-start | bytes 786440 | tf_op jit(solution)/shard_map/ppermute | solution.py:320
  104.0 16.8 %collective-permute-start.17 = (bf16[2,256,256]{2,1,0:T(8,128)(2,1)S(1)}, bf16[2,256,256]{2,1,0:T(8,128)(2,1)S(1)}, u32[]{:S(2)}, u32[]{:S(2)}) collective-permute-start(bf16[2,256,256]{2,1,0:T(8,128)(2,1)S(1)} %collective-permute-done.16.refs_1_), channel_id=1, source_target_pairs={{0,4},{1,5},{2,6},{3,7},{4,0},{5,1},{6,2},{7,3},{8,12},{9,13},{10,... | collective-permute-start | bytes 786440 | tf_op jit(solution)/shard_map/ppermute | solution.py:320
  105.2 15.6 %collective-permute-start.19 = (bf16[2,256,256]{2,1,0:T(8,128)(2,1)S(1)}, bf16[2,256,256]{2,1,0:T(8,128)(2,1)S(1)}, u32[]{:S(2)}, u32[]{:S(2)}) collective-permute-start(bf16[2,256,256]{2,1,0:T(8,128)(2,1)S(1)} %collective-permute-done.18.refs_3_), channel_id=1, source_target_pairs={{0,2},{1,3},{2,0},{3,1},{4,6},{5,7},{6,4},{7,5},{8,10},{9,11},{10,... | collective-permute-start | bytes 786440 | tf_op jit(solution)/shard_map/ppermute | solution.py:320
  112.7 8.1 %collective-permute-start.22 = (bf16[2,256,256]{2,1,0:T(8,128)(2,1)S(1)}, bf16[2,256,256]{2,1,0:T(8,128)(2,1)S(1)}, u32[]{:S(2)}, u32[]{:S(2)}) collective-permute-start(bf16[2,256,256]{2,1,0:T(8,128)(2,1)S(1)} %collective-permute-done.21.refs_2_), channel_id=1, source_target_pairs={{0,2},{1,3},{2,0},{3,1},{4,6},{5,7},{6,4},{7,5},{8,10},{9,11},{10,... | collective-permute-start | bytes 786440 | tf_op jit(solution)/shard_map/ppermute | solution.py:320
  121.4 2.0 %collective-permute-start.24 = (bf16[1024,256]{1,0:T(8,128)(2,1)S(1)}, bf16[1024,256]{1,0:T(8,128)(2,1)S(1)}, u32[]{:S(2)}, u32[]{:S(2)}) collective-permute-start(bf16[1024,256]{1,0:T(8,128)(2,1)S(1)} %pick_other.3), channel_id=1, source_target_pairs={{0,1},{1,0},{2,3},{3,2},{4,5},{5,4},{6,7},{7,6},{8,9},{9,8},{10,11... | collective-permute-start | bytes 1572872 | tf_op jit(solution)/shard_map/ppermute | solution.py:310

commit v14 on v13

--- a/solution.py
+++ b/solution.py
@@ -13,8 +13,8 @@
 NEG = -1e30
 CHUNK = 1024
 ROWS = 512
-PARAMS = pltpu.CompilerParams(vmem_limit_bytes=44 * 1024 * 1024)
-COPY_PARAMS = pltpu.CompilerParams(vmem_limit_bytes=60 * 1024 * 1024)
+PARAMS = pltpu.CompilerParams(vmem_limit_bytes=58 * 1024 * 1024)
+COPY_PARAMS = pltpu.CompilerParams(vmem_limit_bytes=62 * 1024 * 1024)
 
 IN_SMEM = pl.BlockSpec(memory_space=pltpu.SMEM)
 IN_HBM = pl.BlockSpec(memory_space=pltpu.HBM)
@@ -240,7 +240,7 @@
     wait_all([store(step) for step in range(chips)])
 
 
-def multicast(prefix_cache, owners, readers, outgoing, local, fold_moved):
+def multicast(prefix_cache, owners, readers, ctx_len, outgoing, fold_local, fold_moved):
     replicas = lax.axis_size("replica")
     me = lax.axis_index("replica")
     half = replicas // 2
@@ -271,6 +271,7 @@
         compiler_params=COPY_PARAMS,
         name="stage_prefix",
     )(owners, split, swapped)
+    staged = list(staged)
 
     def to_peers(staged, senders):
         return [
@@ -285,11 +286,12 @@
             own = jnp.where((away == step)[:, None, None], rows, own)
         return own
 
+    staged[0], ctx_len = lax.optimization_barrier((staged[0], ctx_len))
     passed = to_peers(staged[:chips], range(replicas))
     wanted = jnp.stack([readers[me], readers[me ^ 1]])
     place = jnp.where(wanted == known, 0, wanted + (wanted < known))
     passed[0], local, place, *known_staged = lax.optimization_barrier(
-        (passed[0], local, place, *staged[chips:])
+        (passed[0], fold_local(ctx_len), place, *staged[chips:])
     )
     passed_known = to_peers(known_staged, (replicas - 2, replicas - 1))
     last_chip = jnp.full((1,), chips - 1, jnp.int32)
@@ -301,9 +303,9 @@
     )
     source = jnp.concatenate([jnp.full((1,), replicas - 1, jnp.int32), sought])
     passed = lax.ppermute(found, "replica", [(i, (i + half) % replicas) for i in range(replicas)])
-    passed, state_now = lax.optimization_barrier((passed, fold_moved(arrived, local)))
+    passed, state_now = lax.optimization_barrier((passed, fold_moved(arrived, local, 0)))
     held = jnp.where((source // half == me // half)[:, None, None], found, passed)
-    return held, place, state_now
+    return held, place, state_now, arrived
 
 
 def swap_cores(rows):
@@ -391,40 +393,46 @@
         compiler_params=COPY_PARAMS,
         name="pack_moved",
     )(mig_target, mig_block, mig_count, kv_pool)
-    local = pl.pallas_call(
-        functools.partial(local_kernel, factor),
-        out_shape=state,
-        grid=(1,),
-        in_specs=[IN_SMEM, whole(queries.shape), whole(suffix_kv.shape), whole(own_cache.shape)],
-        out_specs=whole(state.shape),
-        scratch_shapes=work,
-        compiler_params=PARAMS,
-        cost_estimate=cost(row_count, tokens + own_cache.shape[0], size),
-        name="local_keys",
-    )(ctx_len, queries, suffix_kv, own_cache)
-    def fold_moved(arrived, state_now):
+    def fold_local(ctx_len):
+        return pl.pallas_call(
+            functools.partial(local_kernel, factor),
+            out_shape=state,
+            grid=(1,),
+            in_specs=[
+                IN_SMEM,
+                whole(queries.shape),
+                whole(suffix_kv.shape),
+                whole(own_cache.shape),
+            ],
+            out_specs=whole(state.shape),
+            scratch_shapes=work,
+            compiler_params=PARAMS,
+            cost_estimate=cost(row_count, tokens + own_cache.shape[0], size),
+            name="local_keys",
+        )(ctx_len, queries, suffix_kv, own_cache)
+
+    def fold_moved(arrived, state_now, part):
         rows = arrived.shape[1]
         group = max(n for n in range(1, replicas + 1) if replicas % n == 0 and n * rows <= CHUNK)
-        steps = max(1, replicas // group // 2)
-        for first in range(0, replicas // group, steps):
-            state_now = pl.pallas_call(
-                functools.partial(moved_kernel, factor, steps),
-                out_shape=state,
-                grid=(steps,),
-                in_specs=[
-                    whole(queries.shape),
-                    pl.BlockSpec((group, rows, 2 * size), lambda i, first=first: (first + i, 0, 0)),
-                    whole(state.shape),
-                ],
-                out_specs=whole(state.shape),
-                scratch_shapes=work,
-                compiler_params=PARAMS,
-                cost_estimate=cost(row_count, steps * group * rows, size),
-                name="moved_keys",
-            )(queries, arrived, state_now)
-        return state_now
-
-    def fold_prefix(pieces, others, state_now, last):
+        steps = replicas // group // 2
+        return pl.pallas_call(
+            functools.partial(moved_kernel, factor, steps),
+            out_shape=state,
+            grid=(steps,),
+            in_specs=[
+                whole(queries.shape),
+                pl.BlockSpec((group, rows, 2 * size), lambda i: (part * steps + i, 0, 0)),
+                whole(state.shape),
+            ],
+            out_specs=whole(state.shape),
+            scratch_shapes=work,
+            compiler_params=PARAMS,
+            cost_estimate=cost(row_count, steps * group * rows, size),
+            name="moved_keys",
+        )(queries, arrived, state_now)
+
+    def fold_prefix(pieces, state_now, last=False):
+        others = from_other(pieces, place)
         rows = pieces[0].shape[1]
         keys = 2 * len(pieces) * rows
         steps = max(1, keys // CHUNK)
@@ -452,18 +460,24 @@
             name="prefix_keys",
         )(place, queries, *pieces, others, state_now)
 
-    held, place, state_now = multicast(
-        prefix_cache, owners, readers, outgoing, local, fold_moved
+    held, place, state_now, arrived = multicast(
+        prefix_cache, owners, readers, ctx_len, outgoing, fold_local, fold_moved
     )
     gathered = {0: held}
-    steps = sorted(range(1, replicas // 4), key=lambda step: (step.bit_count(), step))
-    for step in steps:
-        gathered[step] = gather_step(gathered, step)
-    near = [rows for step, rows in gathered.items() if step.bit_count() < 2]
-    state_now = fold_prefix(near, from_other(near, place), state_now, False)
-    gathered[steps[-1]], state_now = lax.optimization_barrier((gathered[steps[-1]], state_now))
-    far = [rows for step, rows in gathered.items() if step.bit_count() > 1]
-    return fold_prefix(far, from_other(far, place), state_now, True)
+    ready = [held]
+    rounds = (replicas // 4).bit_length() - 1
+    for near in range(1, rounds + 1):
+        steps = [step for step in range(1, replicas // 4) if step.bit_count() == near]
+        coming = [gather_step(gathered, step) for step in steps]
+        if near == 1:
+            state_now = fold_moved(arrived, state_now, 1)
+        else:
+            state_now = fold_prefix(ready, state_now)
+            ready = []
+        *coming, state_now = lax.optimization_barrier((*coming, state_now))
+        gathered.update(zip(steps, coming))
+        ready += coming
+    return fold_prefix(ready, state_now, True)
 
 
 def solution(mesh):

time: 132 us -> 146 us (1.11)
  Pallas kernels: 39.5 us -> 63.7 us
  waiting for transfers between devices: 32.4 us -> 19.6 us
  local copies, waits for them, and re-layouts: 5.59 us -> 7.17 us
    ppermute x7, waiting for transfers between devices: 11.2 us -> 0.02 us  [gather_step(): return lax.ppermute(gathered[step ^ 1 << last], 'replica', pairs)]
    pallas_call x2 -> x3, Pallas kernels: 15.3 us -> 24.4 us  [fold_prefix(): pl.pallas_call(functools.partial(prefix_kernel, factor, last, len(pieces)...]
    pallas_call x2, Pallas kernels: 13.9 us -> 20.5 us  [fold_moved(): pl.pallas_call(functools.partial(moved_kernel, factor, steps), out_shape=...]
    pallas_call x2 -> x3, Pallas kernels: 1.16 us -> 7.28 us  [from_other(): pl.pallas_call(pick_kernel, out_shape=jax.ShapeDtypeStruct((len(pieces) *...]
    pallas_call x1, Pallas kernels: 2.59 us -> 5.09 us  [fold_local(): pl.pallas_call(functools.partial(local_kernel, factor), out_shape=state,...]
    ppermute x14, waiting for transfers between devices: 19.3 us -> 17.2 us  [to_peers(): lax.ppermute(rows, 'replica', [(i, i ^ 2 * step) for i in senders])]
    unnamed x16 -> x26, local copies, waits for them, and re-layouts: 4.31 us -> 5.91 us
  transfers between devices with their start and end apart: 26 -> 27, of which waited for: 7 -> 6; matrix products, arithmetic and copies ran while one was open for 5% -> 4% of each run, Pallas kernels for 23% -> 35%
where the time goes in v14:
time: 146 us; the launch traced here: 145 us
  Pallas kernels  63.7 us (44%)
  starting transfers between devices  45.8 us (31%)
  waiting for transfers between devices  19.6 us (13%)
  local copies, waits for them, and re-layouts  7.17 us (5%)
  other arithmetic  5.25 us (4%)
  between operations  3.6 us (2%)
    pallas_call x3, Pallas kernels, fold_prefix(): pl.pallas_call(functools.partial(prefix_kernel, factor, last, len(pieces)...  24.4 us
    pallas_call x2, Pallas kernels, fold_moved(): pl.pallas_call(functools.partial(moved_kernel, factor, steps), out_shape=...  20.5 us
    ppermute x14, starting transfers between devices, to_peers(): lax.ppermute(rows, 'replica', [(i, i ^ 2 * step) for i in senders])  18.3 us
    ppermute x14, waiting for transfers between devices, to_peers(): lax.ppermute(rows, 'replica', [(i, i ^ 2 * step) for i in senders])  17.2 us
    ppermute x7, starting transfers between devices, gather_step(): return lax.ppermute(gathered[step ^ 1 << last], 'replica', pairs)  11.7 us
    ppermute x1, starting transfers between devices, multicast(): lax.ppermute(found, 'replica', [(i, (i + half) % replicas) for i in range...  7.68 us
    all_to_all x1, starting transfers between devices, multicast(): lax.all_to_all(outgoing, 'replica', split_axis=0, concat_axis=0, tiled=True)  7.35 us
    pallas_call x3, Pallas kernels, from_other(): pl.pallas_call(pick_kernel, out_shape=jax.ShapeDtypeStruct((len(pieces) *...  7.28 us
  transfers between devices with their start and end apart: 27, of which 6 were waited for; matrix products, arithmetic and copies ran while one was open for 4% of the time, Pallas kernels for 35%

profile of v14, /device:TPU:0, one launch (start us, length us, event | category | flops | bytes accessed | tf_op | source)
XLA Modules:
  0.0 145.1 jit_solution(15517497642848544713)
XLA Ops:
  1.1 3.4 %pack_moved.1 = bf16[32,128,256]{2,1,0:T(8,128)(2,1)} custom-call(s32[1,32]{1,0:T(1,128)} %target_ref.1, s32[1,32]{1,0:T(1,128)} %block_ref.1, s32[1]{0:T(128)S(6)} %copy.13.count_ref, bf16[32,128,256]{2,1,0:T(8,128)(2,1)} %pool_ref.1), custom_call_target="tpu_custom_call" | custom-call | tf_op jit(solution)/shard_map/pack_moved/pallas_call | solution.py:382
  4.6 7.3 %all-to-all-start = ((bf16[32,128,256]{2,1,0:T(8,128)(2,1)}), bf16[32,128,256]{2,1,0:T(8,128)(2,1)}, u32[]{:S(2)}, u32[]{:S(2)}) async-start(bf16[32,128,256]{2,1,0:T(8,128)(2,1)} %pack_moved.1), calls=%async_computation | async-start | bytes 4194304 | tf_op jit(solution)/shard_map/all_to_all | solution.py:256
  12.6 5.1 %local_keys.1.loaded_ref = f32[2,2048,128]{2,1,0:T(8,128)} custom-call(s32[1]{0:T(128)S(6)} %copy.12.len_ref, bf16[256,1024]{1,0:T(8,128)(2,1)} %q_ref.11, bf16[256,256]{1,0:T(8,128)(2,1)} %suffix_ref.1, bf16[512,256]{1,0:T(8,128)(2,1)} %own_ref.1), custom_call_target="tpu_custom_call" | custom-call | flops 2415919104 | bytes 393216 | tf_op jit(solution)/shard_map/local_keys/pallas_call | solution.py:397
  17.7 3.0 %stage_prefix.1 = (bf16[1,256,256]{2,1,0:T(8,128)(2,1)}, bf16[1,256,256]{2,1,0:T(8,128)(2,1)}, bf16[1,256,256]{2,1,0:T(8,128)(2,1)}, bf16[1,256,256]{2,1,0:T(8,1...) custom-call(s32[2]{0:T(128)} %owner_ref.1, ...), custom_call_target="tpu_custom_call" | custom-call | tf_op jit(solution)/shard_map/stage_prefix/pallas_call | solution.py:260
  20.7 1.8 %collective-permute-start.1 = (bf16[1,256,256]{2,1,0:T(8,128)(2,1)}, bf16[1,256,256]{2,1,0:T(8,128)(2,1)S(1)}, u32[]{:S(2)}, u32[]{:S(2)}) collective-permute-start(bf16[1,256,256]{2,1,0:T(8,128)(2,1)} %get-tuple-element.49), channel_id=1, source_target_pairs={{0,2},{1,3},{2,0},{3,1},{4,6},{5,7},{6,4},{7,5},{8,10},{9,11},{10,... | collective-permute-start | bytes 393224 | tf_op jit(solution)/shard_map/ppermute | solution.py:278
  22.5 2.4 %collective-permute-start.10 = (bf16[1,256,256]{2,1,0:T(8,128)(2,1)}, bf16[1,256,256]{2,1,0:T(8,128)(2,1)S(1)}, u32[]{:S(2)}, u32[]{:S(2)}) collective-permute-start(bf16[1,256,256]{2,1,0:T(8,128)(2,1)} %get-tuple-element.70), channel_id=1, source_target_pairs={{0,12},{1,13},{2,14},{3,15},{4,8},{5,9},{6,10},{7,11},{8,4},{9,5},... | collective-permute-start | bytes 393224 | tf_op jit(solution)/shard_map/ppermute | solution.py:278
  25.4 1.5 %collective-permute-start.12 = (bf16[1,256,256]{2,1,0:T(8,128)(2,1)}, bf16[1,256,256]{2,1,0:T(8,128)(2,1)S(1)}, u32[]{:S(2)}, u32[]{:S(2)}) collective-permute-start(bf16[1,256,256]{2,1,0:T(8,128)(2,1)} %get-tuple-element.72), channel_id=1, source_target_pairs={{0,8},{1,9},{2,10},{3,11},{4,12},{5,13},{6,14},{7,15},{8,0},{9,1},... | collective-permute-start | bytes 393224 | tf_op jit(solution)/shard_map/ppermute | solution.py:278
  26.9 0.7 fusion.1
  27.5 0.6 fusion.4
  28.2 2.4 %compare_select_fusion.which_ref = s32[2]{0:T(128)} fusion(s32[1]{0:T(128)} %get-tuple-element.94, s32[1]{0:T(128)} %get-tuple-element.93, s32[]{:T(128)} %fusion.1), kind=kLoop, calls=%fused_computation.6 | loop fusion | flops 12 | bytes 20 | tf_op jit(solution)/shard_map/jit(_where)/select_n | solution.py:292
  30.6 1.5 %collective-permute-start.13 = (bf16[1,256,256]{2,1,0:T(8,128)(2,1)}, bf16[1,256,256]{2,1,0:T(8,128)(2,1)S(1)}, u32[]{:S(2)}, u32[]{:S(2)}) collective-permute-start(bf16[1,256,256]{2,1,0:T(8,128)(2,1)} %get-tuple-element.73), channel_id=1, source_target_pairs={{0,6},{1,7},{2,4},{3,5},{4,2},{5,3},{6,0},{7,1},{8,14},{9,15},{10,... | collective-permute-start | bytes 393224 | tf_op jit(solution)/shard_map/ppermute | solution.py:278
  32.1 1.5 %collective-permute-start.14 = (bf16[1,256,256]{2,1,0:T(8,128)(2,1)}, bf16[1,256,256]{2,1,0:T(8,128)(2,1)S(1)}, u32[]{:S(2)}, u32[]{:S(2)}) collective-permute-start(bf16[1,256,256]{2,1,0:T(8,128)(2,1)} %get-tuple-element.74), channel_id=1, source_target_pairs={{0,4},{1,5},{2,6},{3,7},{4,0},{5,1},{6,2},{7,3},{8,12},{9,13},{10,... | collective-permute-start | bytes 393224 | tf_op jit(solution)/shard_map/ppermute | solution.py:278
  33.6 16.8 %collective-permute-done.10 = bf16[1,256,256]{2,1,0:T(8,128)(2,1)S(1)} collective-permute-done((bf16[1,256,256]{2,1,0:T(8,128)(2,1)}, bf16[1,256,256]{2,1,0:T(8,128)(2,1)S(1)}, u32[]{:S(2)}, u32[]{:S(2)}) %collective-permute-start.10) | collective-permute-done | bytes 131104 | tf_op jit(solution)/shard_map/ppermute | solution.py:278
  50.3 4.6 %collective-permute-start.9 = (bf16[1,256,256]{2,1,0:T(8,128)(2,1)}, bf16[1,256,256]{2,1,0:T(8,128)(2,1)S(1)}, u32[]{:S(2)}, u32[]{:S(2)}) collective-permute-start(bf16[1,256,256]{2,1,0:T(8,128)(2,1)} %get-tuple-element.69), channel_id=1, source_target_pairs={{0,14},{1,15},{2,12},{3,13},{4,10},{5,11},{6,8},{7,9},{8,6},{9,7},... | collective-permute-start | bytes 393224 | tf_op jit(solution)/shard_map/ppermute | solution.py:278
  54.9 0.7 collective-permute-start.2
  56.0 0.7 collective-permute-start.3
  56.6 0.6 fusion.3
  59.4 0.7 collective-permute-start.4
  60.1 0.7 collective-permute-start.5
  60.8 0.7 collective-permute-start.6
  61.5 0.7 collective-permute-start.7
  62.1 0.7 collective-permute-start.8
  62.8 1.0 select_select_fusion
  63.8 1.0 select_select_fusion.1
  64.9 7.7 %collective-permute-start.15 = (bf16[2,256,256]{2,1,0:T(8,128)(2,1)S(1)}, bf16[2,256,256]{2,1,0:T(8,128)(2,1)S(1)}, u32[]{:S(2)}, u32[]{:S(2)}) collective-permute-start(bf16[2,256,256]{2,1,0:T(8,128)(2,1)S(1)} %pad_maximum_fusion), channel_id=1, source_target_pairs={{0,16},{1,17},{2,18},{3,19},{4,20},{5,21},{6,22},{7,23},{8,24},{9,... | collective-permute-start | bytes 786440 | tf_op jit(solution)/shard_map/ppermute | solution.py:305
  72.5 10.3 %moved_keys.2.loaded_ref = f32[2,2048,128]{2,1,0:T(8,128)} custom-call(bf16[256,1024]{1,0:T(8,128)(2,1)} %q_ref.11, bf16[32,128,256]{2,1,0:T(8,128)(2,1)} %all-to-all-done.kv_ref, f32[2,2048,128]{2,1,0:T(8,128)} %local_keys.1.loaded_ref), custom_call_target="tpu_custom_call" | custom-call | flops 6442450944 | bytes 1048576 | tf_op jit(solution)/shard_map/moved_keys/pallas_call | solution.py:418
  82.9 2.3 %collective-permute-start.16 = (bf16[2,256,256]{2,1,0:T(8,128)(2,1)S(1)}, bf16[2,256,256]{2,1,0:T(8,128)(2,1)S(1)}, u32[]{:S(2)}, u32[]{:S(2)}) collective-permute-start(bf16[2,256,256]{2,1,0:T(8,128)(2,1)S(1)} %broadcast_select_fusion.refs_0_), channel_id=1, source_target_pairs={{0,2},{1,3},{2,0},{3,1},{4,6},{5,7},{6,4},{7,5},{8,10},{9,11},{10,... | collective-permute-start | bytes 786440 | tf_op jit(solution)/shard_map/ppermute | solution.py:322
  85.2 3.8 %collective-permute-start.17 = (bf16[2,256,256]{2,1,0:T(8,128)(2,1)S(1)}, bf16[2,256,256]{2,1,0:T(8,128)(2,1)S(1)}, u32[]{:S(2)}, u32[]{:S(2)}) collective-permute-start(bf16[2,256,256]{2,1,0:T(8,128)(2,1)S(1)} %broadcast_select_fusion.refs_0_), channel_id=1, source_target_pairs={{0,4},{1,5},{2,6},{3,7},{4,0},{5,1},{6,2},{7,3},{8,12},{9,13},{10,... | collective-permute-start | bytes 786440 | tf_op jit(solution)/shard_map/ppermute | solution.py:322
  89.0 2.5 %collective-permute-start.18 = (bf16[2,256,256]{2,1,0:T(8,128)(2,1)S(1)}, bf16[2,256,256]{2,1,0:T(8,128)(2,1)S(1)}, u32[]{:S(2)}, u32[]{:S(2)}) collective-permute-start(bf16[2,256,256]{2,1,0:T(8,128)(2,1)S(1)} %broadcast_select_fusion.refs_0_), channel_id=1, source_target_pairs={{0,8},{1,9},{2,10},{3,11},{4,12},{5,13},{6,14},{7,15},{8,0},{9,1},... | collective-permute-start | bytes 786440 | tf_op jit(solution)/shard_map/ppermute | solution.py:322
  91.6 10.2 %moved_keys.3.refs_5_ = f32[2,2048,128]{2,1,0:T(8,128)} custom-call(bf16[256,1024]{1,0:T(8,128)(2,1)} %q_ref.11, bf16[32,128,256]{2,1,0:T(8,128)(2,1)} %all-to-all-done.kv_ref, f32[2,2048,128]{2,1,0:T(8,128)} %moved_keys.2.loaded_ref), custom_call_target="tpu_custom_call" | custom-call | flops 6442450944 | bytes 1048576 | tf_op jit(solution)/shard_map/moved_keys/pallas_call | solution.py:418
  101.8 0.7 copy-done.3
  102.6 0.7 copy-done.5
  103.3 2.6 %pick_other.3 = bf16[1024,256]{1,0:T(8,128)(2,1)} custom-call(s32[2]{0:T(128)} %compare_select_fusion.which_ref, bf16[2,256,256]{2,1,0:T(8,128)(2,1)} %copy-done, bf16[2,256,256]{2,1,0:T(8,128)(2,1)} %copy-done.3, bf16[2,256,256]{2,1,0:T(8,128)(2,1)} %copy-done.2, bf16[2,256,256]{2,1,0:T(8,128)(2,1)} %copy-done.5), custom_call_target="tpu_custom_call" | custom-call | tf_op jit(solution)/shard_map/pick_other/pallas_call | solution.py:328
  105.9 0.9 collective-permute-start.19
  106.8 0.6 collective-permute-start.20
  108.1 0.8 copy-done.10
  108.8 10.6 %prefix_keys.3.refs_4_ = f32[2,2048,128]{2,1,0:T(8,128)} custom-call(s32[2]{0:T(128)} %compare_select_fusion.which_ref, bf16[256,1024]{1,0:T(8,128)(2,1)} %q_ref.11, bf16[2,256,256]{2,1,0:T(8,128)(2,1)} %copy-done, bf16[2,256,256]{2,1,0:T(8,128)(2,1)} %copy-done.3, bf16[2,256,256]{2,1,0:T(8,128)(2,1)} %copy-done.2, bf16[2,256,256]{2,1,0:T(8,128)(2,1)} %copy-done.5, ...), custom_call_target="tpu_custom_call" | custom-call | flops 6442450944 | bytes 1048576 | tf_op jit(solution)/shard_map/prefix_keys/pallas_call | solution.py:442
  119.5 0.7 copy-done.4
  120.2 0.7 copy-done.7
  121.0 2.5 %pick_other.4 = bf16[768,256]{1,0:T(8,128)(2,1)} custom-call(s32[2]{0:T(128)} %compare_select_fusion.which_ref, bf16[2,256,256]{2,1,0:T(8,128)(2,1)} %copy-done.4, bf16[2,256,256]{2,1,0:T(8,128)(2,1)} %copy-done.6, bf16[2,256,256]{2,1,0:T(8,128)(2,1)} %copy-done.7), custom_call_target="tpu_custom_call" | custom-call | tf_op jit(solution)/shard_map/pick_other/pallas_call | solution.py:328
  123.6 1.5 %collective-permute-start.23 = (bf16[2,256,256]{2,1,0:T(8,128)(2,1)}, bf16[2,256,256]{2,1,0:T(8,128)(2,1)S(1)}, u32[]{:S(2)}, u32[]{:S(2)}) collective-permute-start(bf16[2,256,256]{2,1,0:T(8,128)(2,1)} %copy-done.7), channel_id=1, source_target_pairs={{0,2},{1,3},{2,0},{3,1},{4,6},{5,7},{6,4},{7,5},{8,10},{9,11},{10,... | collective-permute-start | bytes 786440 | tf_op jit(solution)/shard_map/ppermute | solution.py:322
  125.4 0.7 copy-done.11
  126.1 8.5 %prefix_keys.4.refs_2_ = f32[2,2048,128]{2,1,0:T(8,128)} custom-call(s32[2]{0:T(128)} %compare_select_fusion.which_ref, bf16[256,1024]{1,0:T(8,128)(2,1)} %q_ref.11, bf16[2,256,256]{2,1,0:T(8,128)(2,1)} %copy-done.4, bf16[2,256,256]{2,1,0:T(8,128)(2,1)} %copy-done.6, bf16[2,256,256]{2,1,0:T(8,128)(2,1)} %copy-done.7, bf16[768,256]{1,0:T(8,128)(2,1)} %copy-done.11, ...), custom_call_target="tpu_custom_call" | custom-call | flops 4831838208 | bytes 786432 | tf_op jit(solution)/shard_map/prefix_keys/pallas_call | solution.py:442
  134.6 0.7 copy-done.1
  135.3 2.2 %pick_other.5 = bf16[256,256]{1,0:T(8,128)(2,1)} custom-call(s32[2]{0:T(128)} %compare_select_fusion.which_ref, bf16[2,256,256]{2,1,0:T(8,128)(2,1)} %copy-done.1), custom_call_target="tpu_custom_call" | custom-call | tf_op jit(solution)/shard_map/pick_other/pallas_call | solution.py:328
  137.7 1.4 collective-permute-done.25.refs_1_
  139.1 0.7 copy-done.12
  139.7 5.3 %prefix_keys.5 = bf16[256,1024]{1,0:T(8,128)(2,1)} custom-call(s32[2]{0:T(128)} %compare_select_fusion.which_ref, bf16[256,1024]{1,0:T(8,128)(2,1)} %q_ref.11, bf16[2,256,256]{2,1,0:T(8,128)(2,1)} %copy-done.1, bf16[256,256]{1,0:T(8,128)(2,1)} %copy-done.12, f32[2,2048,128]{2,1,0:T(8,128)} %prefix_keys.4.refs_2_), custom_call_target="tpu_custom_call" | custom-call | flops 1610612736 | bytes 262144 | tf_op jit(solution)/shard_map/prefix_keys/pallas_call | solution.py:442
  (53 shorter events, 3.2 us)
Async XLA Ops:
  0.0 4.6 %collective-permute-start = (bf16[4096,256]{1,0:T(8,128)(2,1)}, bf16[4096,256]{1,0:T(8,128)(2,1)}, u32[]{:S(2)}, u32[]{:S(2)}) collective-permute-start(bf16[4096,256]{1,0:T(8,128)(2,1)} %param.15), channel_id=1, source_target_pairs={{0,1},{1,0},{2,3},{3,2},{4,5},{5,4},{6,7},{7,6},{8,9},{9,8},{10,11... | collective-permute-start | bytes 6291464 | tf_op jit(solution)/shard_map/ppermute | solution.py:312
  4.6 68.0 %all-to-all-start = ((bf16[32,128,256]{2,1,0:T(8,128)(2,1)}), bf16[32,128,256]{2,1,0:T(8,128)(2,1)}, u32[]{:S(2)}, u32[]{:S(2)}) async-start(bf16[32,128,256]{2,1,0:T(8,128)(2,1)} %pack_moved.1), calls=%async_computation | async-start | bytes 4194304 | tf_op jit(solution)/shard_map/all_to_all | solution.py:256
  17.7 9.2 %copy-start.8 = (s32[2]{0:T(128)S(1)}, s32[2]{0:T(128)}, u32[]{:S(2)}) copy-start(s32[2]{0:T(128)} %owner_ref.1) | copy-start | bytes 28
  17.7 9.9 %copy-start.9 = (s32[32]{0:T(128)S(1)}, s32[32]{0:T(128)}, u32[]{:S(2)}) copy-start(s32[32]{0:T(128)} %param.17) | copy-start | bytes 388
  20.7 11.4 %collective-permute-start.1 = (bf16[1,256,256]{2,1,0:T(8,128)(2,1)}, bf16[1,256,256]{2,1,0:T(8,128)(2,1)S(1)}, u32[]{:S(2)}, u32[]{:S(2)}) collective-permute-start(bf16[1,256,256]{2,1,0:T(8,128)(2,1)} %get-tuple-element.49), channel_id=1, source_target_pairs={{0,2},{1,3},{2,0},{3,1},{4,6},{5,7},{6,4},{7,5},{8,10},{9,11},{10,... | collective-permute-start | bytes 393224 | tf_op jit(solution)/shard_map/ppermute | solution.py:278
  22.5 27.8 %collective-permute-start.10 = (bf16[1,256,256]{2,1,0:T(8,128)(2,1)}, bf16[1,256,256]{2,1,0:T(8,128)(2,1)S(1)}, u32[]{:S(2)}, u32[]{:S(2)}) collective-permute-start(bf16[1,256,256]{2,1,0:T(8,128)(2,1)} %get-tuple-element.70), channel_id=1, source_target_pairs={{0,12},{1,13},{2,14},{3,15},{4,8},{5,9},{6,10},{7,11},{8,4},{9,5},... | collective-permute-start | bytes 393224 | tf_op jit(solution)/shard_map/ppermute | solution.py:278
  24.9 30.1 %collective-permute-start.11 = (bf16[1,256,256]{2,1,0:T(8,128)(2,1)}, bf16[1,256,256]{2,1,0:T(8,128)(2,1)S(1)}, u32[]{:S(2)}, u32[]{:S(2)}) collective-permute-start(bf16[1,256,256]{2,1,0:T(8,128)(2,1)} %get-tuple-element.71), channel_id=1, source_target_pairs={{0,10},{1,11},{2,8},{3,9},{4,14},{5,15},{6,12},{7,13},{8,2},{9,3},... | collective-permute-start | bytes 393224 | tf_op jit(solution)/shard_map/ppermute | solution.py:278
  25.4 30.5 %collective-permute-start.12 = (bf16[1,256,256]{2,1,0:T(8,128)(2,1)}, bf16[1,256,256]{2,1,0:T(8,128)(2,1)S(1)}, u32[]{:S(2)}, u32[]{:S(2)}) collective-permute-start(bf16[1,256,256]{2,1,0:T(8,128)(2,1)} %get-tuple-element.72), channel_id=1, source_target_pairs={{0,8},{1,9},{2,10},{3,11},{4,12},{5,13},{6,14},{7,15},{8,0},{9,1},... | collective-permute-start | bytes 393224 | tf_op jit(solution)/shard_map/ppermute | solution.py:278
  30.6 28.7 %collective-permute-start.13 = (bf16[1,256,256]{2,1,0:T(8,128)(2,1)}, bf16[1,256,256]{2,1,0:T(8,128)(2,1)S(1)}, u32[]{:S(2)}, u32[]{:S(2)}) collective-permute-start(bf16[1,256,256]{2,1,0:T(8,128)(2,1)} %get-tuple-element.73), channel_id=1, source_target_pairs={{0,6},{1,7},{2,4},{3,5},{4,2},{5,3},{6,0},{7,1},{8,14},{9,15},{10,... | collective-permute-start | bytes 393224 | tf_op jit(solution)/shard_map/ppermute | solution.py:278
  32.1 27.9 %collective-permute-start.14 = (bf16[1,256,256]{2,1,0:T(8,128)(2,1)}, bf16[1,256,256]{2,1,0:T(8,128)(2,1)S(1)}, u32[]{:S(2)}, u32[]{:S(2)}) collective-permute-start(bf16[1,256,256]{2,1,0:T(8,128)(2,1)} %get-tuple-element.74), channel_id=1, source_target_pairs={{0,4},{1,5},{2,6},{3,7},{4,0},{5,1},{6,2},{7,3},{8,12},{9,13},{10,... | collective-permute-start | bytes 393224 | tf_op jit(solution)/shard_map/ppermute | solution.py:278
  50.3 10.5 %collective-permute-start.9 = (bf16[1,256,256]{2,1,0:T(8,128)(2,1)}, bf16[1,256,256]{2,1,0:T(8,128)(2,1)S(1)}, u32[]{:S(2)}, u32[]{:S(2)}) collective-permute-start(bf16[1,256,256]{2,1,0:T(8,128)(2,1)} %get-tuple-element.69), channel_id=1, source_target_pairs={{0,14},{1,15},{2,12},{3,13},{4,10},{5,11},{6,8},{7,9},{8,6},{9,7},... | collective-permute-start | bytes 393224 | tf_op jit(solution)/shard_map/ppermute | solution.py:278
  54.9 6.5 %collective-permute-start.2 = (bf16[1,256,256]{2,1,0:T(8,128)(2,1)}, bf16[1,256,256]{2,1,0:T(8,128)(2,1)S(1)}, u32[]{:S(2)}, u32[]{:S(2)}) collective-permute-start(bf16[1,256,256]{2,1,0:T(8,128)(2,1)} %get-tuple-element.61), channel_id=1, source_target_pairs={{30,16},{31,17}} | collective-permute-start | bytes 393224 | tf_op jit(solution)/shard_map/ppermute | solution.py:278
  56.0 6.2 %collective-permute-start.3 = (bf16[1,256,256]{2,1,0:T(8,128)(2,1)}, bf16[1,256,256]{2,1,0:T(8,128)(2,1)S(1)}, u32[]{:S(2)}, u32[]{:S(2)}) collective-permute-start(bf16[1,256,256]{2,1,0:T(8,128)(2,1)} %get-tuple-element.62), channel_id=1, source_target_pairs={{30,18},{31,19}} | collective-permute-start | bytes 393224 | tf_op jit(solution)/shard_map/ppermute | solution.py:278
  59.4 4.4 %collective-permute-start.4 = (bf16[1,256,256]{2,1,0:T(8,128)(2,1)}, bf16[1,256,256]{2,1,0:T(8,128)(2,1)S(1)}, u32[]{:S(2)}, u32[]{:S(2)}) collective-permute-start(bf16[1,256,256]{2,1,0:T(8,128)(2,1)} %get-tuple-element.63), channel_id=1, source_target_pairs={{30,20},{31,21}} | collective-permute-start | bytes 393224 | tf_op jit(solution)/shard_map/ppermute | solution.py:278
  60.1 3.7 %collective-permute-start.5 = (bf16[1,256,256]{2,1,0:T(8,128)(2,1)}, bf16[1,256,256]{2,1,0:T(8,128)(2,1)S(1)}, u32[]{:S(2)}, u32[]{:S(2)}) collective-permute-start(bf16[1,256,256]{2,1,0:T(8,128)(2,1)} %get-tuple-element.64), channel_id=1, source_target_pairs={{30,22},{31,23}} | collective-permute-start | bytes 393224 | tf_op jit(solution)/shard_map/ppermute | solution.py:278
  60.8 3.0 %collective-permute-start.6 = (bf16[1,256,256]{2,1,0:T(8,128)(2,1)}, bf16[1,256,256]{2,1,0:T(8,128)(2,1)S(1)}, u32[]{:S(2)}, u32[]{:S(2)}) collective-permute-start(bf16[1,256,256]{2,1,0:T(8,128)(2,1)} %get-tuple-element.65), channel_id=1, source_target_pairs={{30,24},{31,25}} | collective-permute-start | bytes 393224 | tf_op jit(solution)/shard_map/ppermute | solution.py:278
  61.5 2.4 %collective-permute-start.7 = (bf16[1,256,256]{2,1,0:T(8,128)(2,1)}, bf16[1,256,256]{2,1,0:T(8,128)(2,1)S(1)}, u32[]{:S(2)}, u32[]{:S(2)}) collective-permute-start(bf16[1,256,256]{2,1,0:T(8,128)(2,1)} %get-tuple-element.66), channel_id=1, source_target_pairs={{30,26},{31,27}} | collective-permute-start | bytes 393224 | tf_op jit(solution)/shard_map/ppermute | solution.py:278
  62.1 1.7 %collective-permute-start.8 = (bf16[1,256,256]{2,1,0:T(8,128)(2,1)}, bf16[1,256,256]{2,1,0:T(8,128)(2,1)S(1)}, u32[]{:S(2)}, u32[]{:S(2)}) collective-permute-start(bf16[1,256,256]{2,1,0:T(8,128)(2,1)} %get-tuple-element.67), channel_id=1, source_target_pairs={{30,28},{31,29}} | collective-permute-start | bytes 393224 | tf_op jit(solution)/shard_map/ppermute | solution.py:278
  64.9 18.0 %collective-permute-start.15 = (bf16[2,256,256]{2,1,0:T(8,128)(2,1)S(1)}, bf16[2,256,256]{2,1,0:T(8,128)(2,1)S(1)}, u32[]{:S(2)}, u32[]{:S(2)}) collective-permute-start(bf16[2,256,256]{2,1,0:T(8,128)(2,1)S(1)} %pad_maximum_fusion), channel_id=1, source_target_pairs={{0,16},{1,17},{2,18},{3,19},{4,20},{5,21},{6,22},{7,23},{8,24},{9,... | collective-permute-start | bytes 786440 | tf_op jit(solution)/shard_map/ppermute | solution.py:305
  82.9 18.9 %copy-start = (bf16[2,256,256]{2,1,0:T(8,128)(2,1)}, bf16[2,256,256]{2,1,0:T(8,128)(2,1)S(1)}, u32[]{:S(2)}) copy-start(bf16[2,256,256]{2,1,0:T(8,128)(2,1)S(1)} %broadcast_select_fusion.refs_0_) | copy-start | bytes 786436
  82.9 18.9 %collective-permute-start.16 = (bf16[2,256,256]{2,1,0:T(8,128)(2,1)S(1)}, bf16[2,256,256]{2,1,0:T(8,128)(2,1)S(1)}, u32[]{:S(2)}, u32[]{:S(2)}) collective-permute-start(bf16[2,256,256]{2,1,0:T(8,128)(2,1)S(1)} %broadcast_select_fusion.refs_0_), channel_id=1, source_target_pairs={{0,2},{1,3},{2,0},{3,1},{4,6},{5,7},{6,4},{7,5},{8,10},{9,11},{10,... | collective-permute-start | bytes 786440 | tf_op jit(solution)/shard_map/ppermute | solution.py:322
  85.2 16.6 %collective-permute-start.17 = (bf16[2,256,256]{2,1,0:T(8,128)(2,1)S(1)}, bf16[2,256,256]{2,1,0:T(8,128)(2,1)S(1)}, u32[]{:S(2)}, u32[]{:S(2)}) collective-permute-start(bf16[2,256,256]{2,1,0:T(8,128)(2,1)S(1)} %broadcast_select_fusion.refs_0_), channel_id=1, source_target_pairs={{0,4},{1,5},{2,6},{3,7},{4,0},{5,1},{6,2},{7,3},{8,12},{9,13},{10,... | collective-permute-start | bytes 786440 | tf_op jit(solution)/shard_map/ppermute | solution.py:322
  89.0 12.8 %collective-permute-start.18 = (bf16[2,256,256]{2,1,0:T(8,128)(2,1)S(1)}, bf16[2,256,256]{2,1,0:T(8,128)(2,1)S(1)}, u32[]{:S(2)}, u32[]{:S(2)}) collective-permute-start(bf16[2,256,256]{2,1,0:T(8,128)(2,1)S(1)} %broadcast_select_fusion.refs_0_), channel_id=1, source_target_pairs={{0,8},{1,9},{2,10},{3,11},{4,12},{5,13},{6,14},{7,15},{8,0},{9,1},... | collective-permute-start | bytes 786440 | tf_op jit(solution)/shard_map/ppermute | solution.py:322
  101.8 0.7 copy-start.3
  101.8 0.8 copy-start.2
  102.6 0.7 copy-start.5
  105.9 2.1 %collective-permute-start.22 = (bf16[1024,256]{1,0:T(8,128)(2,1)}, bf16[1024,256]{1,0:T(8,128)(2,1)S(1)}, u32[]{:S(2)}, u32[]{:S(2)}) collective-permute-start(bf16[1024,256]{1,0:T(8,128)(2,1)} %pick_other.3), channel_id=1, source_target_pairs={{0,1},{1,0},{2,3},{3,2},{4,5},{5,4},{6,7},{7,6},{8,9},{9,8},{10,11... | collective-permute-start | bytes 1572872 | tf_op jit(solution)/shard_map/ppermute | solution.py:312
  105.9 13.5 %collective-permute-start.19 = (bf16[2,256,256]{2,1,0:T(8,128)(2,1)}, bf16[2,256,256]{2,1,0:T(8,128)(2,1)S(1)}, u32[]{:S(2)}, u32[]{:S(2)}) collective-permute-start(bf16[2,256,256]{2,1,0:T(8,128)(2,1)} %copy-done.3), channel_id=1, source_target_pairs={{0,4},{1,5},{2,6},{3,7},{4,0},{5,1},{6,2},{7,3},{8,12},{9,13},{10,... | collective-permute-start | bytes 786440 | tf_op jit(solution)/shard_map/ppermute | solution.py:322
  106.8 12.6 %collective-permute-start.20 = (bf16[2,256,256]{2,1,0:T(8,128)(2,1)}, bf16[2,256,256]{2,1,0:T(8,128)(2,1)S(1)}, u32[]{:S(2)}, u32[]{:S(2)}) collective-permute-start(bf16[2,256,256]{2,1,0:T(8,128)(2,1)} %copy-done.5), channel_id=1, source_target_pairs={{0,2},{1,3},{2,0},{3,1},{4,6},{5,7},{6,4},{7,5},{8,10},{9,11},{10,... | collective-permute-start | bytes 786440 | tf_op jit(solution)/shard_map/ppermute | solution.py:322
  107.5 12.0 %collective-permute-start.21 = (bf16[2,256,256]{2,1,0:T(8,128)(2,1)}, bf16[2,256,256]{2,1,0:T(8,128)(2,1)S(1)}, u32[]{:S(2)}, u32[]{:S(2)}) collective-permute-start(bf16[2,256,256]{2,1,0:T(8,128)(2,1)} %copy-done.2), channel_id=1, source_target_pairs={{0,8},{1,9},{2,10},{3,11},{4,12},{5,13},{6,14},{7,15},{8,0},{9,1},... | collective-permute-start | bytes 786440 | tf_op jit(solution)/shard_map/ppermute | solution.py:322
  108.1 0.8 copy-start.10
  119.4 0.7 copy-start.4
  119.5 0.8 copy-start.6
  120.2 0.7 copy-start.7
  123.4 1.9 %collective-permute-start.24 = (bf16[768,256]{1,0:T(8,128)(2,1)}, bf16[768,256]{1,0:T(8,128)(2,1)S(1)}, u32[]{:S(2)}, u32[]{:S(2)}) collective-permute-start(bf16[768,256]{1,0:T(8,128)(2,1)} %pick_other.4), channel_id=1, source_target_pairs={{0,1},{1,0},{2,3},{3,2},{4,5},{5,4},{6,7},{7,6},{8,9},{9,8},{10,11... | collective-permute-start | bytes 1179656 | tf_op jit(solution)/shard_map/ppermute | solution.py:312
  123.6 11.0 %collective-permute-start.23 = (bf16[2,256,256]{2,1,0:T(8,128)(2,1)}, bf16[2,256,256]{2,1,0:T(8,128)(2,1)S(1)}, u32[]{:S(2)}, u32[]{:S(2)}) collective-permute-start(bf16[2,256,256]{2,1,0:T(8,128)(2,1)} %copy-done.7), channel_id=1, source_target_pairs={{0,2},{1,3},{2,0},{3,1},{4,6},{5,7},{6,4},{7,5},{8,10},{9,11},{10,... | collective-permute-start | bytes 786440 | tf_op jit(solution)/shard_map/ppermute | solution.py:322
  125.4 0.7 copy-start.11
  134.6 0.7 copy-start.1
  137.5 1.6 %collective-permute-start.25 = (bf16[256,256]{1,0:T(8,128)(2,1)}, bf16[256,256]{1,0:T(8,128)(2,1)S(1)}, u32[]{:S(2)}, u32[]{:S(2)}) collective-permute-start(bf16[256,256]{1,0:T(8,128)(2,1)} %pick_other.5), channel_id=1, source_target_pairs={{0,1},{1,0},{2,3},{3,2},{4,5},{5,4},{6,7},{7,6},{8,9},{9,8},{10,11... | collective-permute-start | bytes 393224 | tf_op jit(solution)/shard_map/ppermute | solution.py:312
  139.1 0.7 copy-start.12

commit v15 on v14

--- a/solution.py
+++ b/solution.py
@@ -13,7 +13,7 @@
 NEG = -1e30
 CHUNK = 1024
 ROWS = 512
-PARAMS = pltpu.CompilerParams(vmem_limit_bytes=58 * 1024 * 1024)
+PARAMS = pltpu.CompilerParams(vmem_limit_bytes=44 * 1024 * 1024)
 COPY_PARAMS = pltpu.CompilerParams(vmem_limit_bytes=62 * 1024 * 1024)
 
 IN_SMEM = pl.BlockSpec(memory_space=pltpu.SMEM)
@@ -85,7 +85,7 @@
         ).astype(out_ref.dtype)
 
 
-def local_kernel(factor, len_ref, q_ref, suffix_ref, own_ref, out_ref, *work):
+def local_kernel(factor, len_ref, q_ref, suffix_ref, own_ref, after_ref, out_ref, *work):
     q_stacked, max_ref, lanes_ref, sums_ref = work
     size = sums_ref.shape[1]
     suffix, own = suffix_ref.shape[0], own_ref.shape[0]
@@ -240,7 +240,7 @@
     wait_all([store(step) for step in range(chips)])
 
 
-def multicast(prefix_cache, owners, readers, ctx_len, outgoing, fold_local, fold_moved):
+def multicast(prefix_cache, owners, readers, outgoing, fold_local, fold_moved):
     replicas = lax.axis_size("replica")
     me = lax.axis_index("replica")
     half = replicas // 2
@@ -286,12 +286,11 @@
             own = jnp.where((away == step)[:, None, None], rows, own)
         return own
 
-    staged[0], ctx_len = lax.optimization_barrier((staged[0], ctx_len))
     passed = to_peers(staged[:chips], range(replicas))
     wanted = jnp.stack([readers[me], readers[me ^ 1]])
     place = jnp.where(wanted == known, 0, wanted + (wanted < known))
     passed[0], local, place, *known_staged = lax.optimization_barrier(
-        (passed[0], fold_local(ctx_len), place, *staged[chips:])
+        (passed[0], fold_local(staged[0]), place, *staged[chips:])
     )
     passed_known = to_peers(known_staged, (replicas - 2, replicas - 1))
     last_chip = jnp.full((1,), chips - 1, jnp.int32)
@@ -393,7 +392,7 @@
         compiler_params=COPY_PARAMS,
         name="pack_moved",
     )(mig_target, mig_block, mig_count, kv_pool)
-    def fold_local(ctx_len):
+    def fold_local(after):
         return pl.pallas_call(
             functools.partial(local_kernel, factor),
             out_shape=state,
@@ -403,13 +402,14 @@
                 whole(queries.shape),
                 whole(suffix_kv.shape),
                 whole(own_cache.shape),
+                IN_HBM,
             ],
             out_specs=whole(state.shape),
             scratch_shapes=work,
             compiler_params=PARAMS,
             cost_estimate=cost(row_count, tokens + own_cache.shape[0], size),
             name="local_keys",
-        )(ctx_len, queries, suffix_kv, own_cache)
+        )(ctx_len, queries, suffix_kv, own_cache, after)
 
     def fold_moved(arrived, state_now, part):
         rows = arrived.shape[1]
@@ -461,7 +461,7 @@
         )(place, queries, *pieces, others, state_now)
 
     held, place, state_now, arrived = multicast(
-        prefix_cache, owners, readers, ctx_len, outgoing, fold_local, fold_moved
+        prefix_cache, owners, readers, outgoing, fold_local, fold_moved
     )
     gathered = {0: held}
     ready = [held]

time: 146 us -> 127 us (0.87)
  Pallas kernels: 63.7 us -> 42.9 us
  waiting for transfers between devices: 19.6 us -> 28.6 us
  starting transfers between devices: 45.8 us -> 42.6 us
  other arithmetic: 5.25 us -> 3.08 us
  local copies, waits for them, and re-layouts: 7.17 us -> 5.14 us
    pallas_call x3, Pallas kernels: 24.4 us -> 16 us  [fold_prefix(): pl.pallas_call(functools.partial(prefix_kernel, factor, last, len(pieces)...]
    ppermute x14, waiting for transfers between devices: 17.2 us -> 23.8 us  [to_peers(): lax.ppermute(rows, 'replica', [(i, i ^ 2 * step) for i in senders])]
    pallas_call x3, Pallas kernels: 7.28 us -> 1.71 us  [from_other(): pl.pallas_call(pick_kernel, out_shape=jax.ShapeDtypeStruct((len(pieces) *...]
    pallas_call x2, Pallas kernels: 20.5 us -> 16 us  [fold_moved(): pl.pallas_call(functools.partial(moved_kernel, factor, steps), out_shape=...]
    ppermute x14, starting transfers between devices: 18.3 us -> 14.9 us  [to_peers(): lax.ppermute(rows, 'replica', [(i, i ^ 2 * step) for i in senders])]
    ppermute x7, waiting for transfers between devices: 0.02 us -> 2.71 us  [gather_step(): return lax.ppermute(gathered[step ^ 1 << last], 'replica', pairs)]
    pallas_call x1, Pallas kernels: 5.09 us -> 2.62 us  [fold_local(): pl.pallas_call(functools.partial(local_kernel, factor), out_shape=state,...]
    unnamed x26 -> x38, local copies, waits for them, and re-layouts: 5.91 us -> 3.93 us
  transfers between devices with their start and end apart: 27 -> 27, of which waited for: 6 -> 7; matrix products, arithmetic and copies ran while one was open for 4% -> 3% of each run, Pallas kernels for 35% -> 30%
where the time goes in v15:
time: 127 us; the launch traced here: 126 us
  Pallas kernels  42.9 us (34%)
  starting transfers between devices  42.6 us (34%)
  waiting for transfers between devices  28.6 us (23%)
  local copies, waits for them, and re-layouts  5.14 us (4%)
  between operations  3.92 us (3%)
  other arithmetic  3.08 us (2%)
    ppermute x14, waiting for transfers between devices, to_peers(): lax.ppermute(rows, 'replica', [(i, i ^ 2 * step) for i in senders])  23.8 us
    pallas_call x3, Pallas kernels, fold_prefix(): pl.pallas_call(functools.partial(prefix_kernel, factor, last, len(pieces)...  16 us
    pallas_call x2, Pallas kernels, fold_moved(): pl.pallas_call(functools.partial(moved_kernel, factor, steps), out_shape=...  16 us
    ppermute x14, starting transfers between devices, to_peers(): lax.ppermute(rows, 'replica', [(i, i ^ 2 * step) for i in senders])  14.9 us
    ppermute x7, starting transfers between devices, gather_step(): return lax.ppermute(gathered[step ^ 1 << last], 'replica', pairs)  13.4 us
    all_to_all x1, starting transfers between devices, multicast(): lax.all_to_all(outgoing, 'replica', split_axis=0, concat_axis=0, tiled=True)  7.19 us
    ppermute x1, starting transfers between devices, multicast(): lax.ppermute(found, 'replica', [(i, (i + half) % replicas) for i in range...  6.48 us
    unnamed x38, local copies, waits for them, and re-layouts  3.93 us
  transfers between devices with their start and end apart: 27, of which 7 were waited for; matrix products, arithmetic and copies ran while one was open for 3% of the time, Pallas kernels for 30%

profile of v15, /device:TPU:0, one launch (start us, length us, event | category | flops | bytes accessed | tf_op | source)
XLA Modules:
  0.0 126.3 jit_solution(8299519003241162323)
XLA Ops:
  0.0 0.5 collective-permute-start
  1.1 3.6 %pack_moved.1 = bf16[32,128,256]{2,1,0:T(8,128)(2,1)} custom-call(s32[1,32]{1,0:T(1,128)} %target_ref.1, s32[1,32]{1,0:T(1,128)} %block_ref.1, s32[1]{0:T(128)S(6)} %copy.13.count_ref, bf16[32,128,256]{2,1,0:T(8,128)(2,1)} %pool_ref.1), custom_call_target="tpu_custom_call" | custom-call | tf_op jit(solution)/shard_map/pack_moved/pallas_call | solution.py:381
  4.7 7.2 %all-to-all-start = ((bf16[32,128,256]{2,1,0:T(8,128)(2,1)}), bf16[32,128,256]{2,1,0:T(8,128)(2,1)}, u32[]{:S(2)}, u32[]{:S(2)}) async-start(bf16[32,128,256]{2,1,0:T(8,128)(2,1)} %pack_moved.1), calls=%async_computation | async-start | bytes 4194304 | tf_op jit(solution)/shard_map/all_to_all | solution.py:256
  12.6 0.6 fusion.4
  13.2 0.7 fusion.1
  13.9 2.0 %compare_select_fusion.which_ref = s32[2]{0:T(128)S(1)} fusion(s32[1]{0:T(128)} %get-tuple-element.90, s32[1]{0:T(128)} %get-tuple-element.89, s32[]{:T(128)} %fusion.1), kind=kLoop, calls=%fused_computation.6 | loop fusion | flops 12 | bytes 20 | tf_op jit(solution)/shard_map/jit(_where)/select_n | solution.py:291
  16.0 3.1 %stage_prefix.1 = (bf16[1,256,256]{2,1,0:T(8,128)(2,1)}, bf16[1,256,256]{2,1,0:T(8,128)(2,1)}, bf16[1,256,256]{2,1,0:T(8,128)(2,1)}, bf16[1,256,256]{2,1,0:T(8,1...) custom-call(s32[2]{0:T(128)} %owner_ref.1, ...), custom_call_target="tpu_custom_call" | custom-call | tf_op jit(solution)/shard_map/stage_prefix/pallas_call | solution.py:260
  19.1 1.8 %collective-permute-start.1 = (bf16[1,256,256]{2,1,0:T(8,128)(2,1)}, bf16[1,256,256]{2,1,0:T(8,128)(2,1)S(1)}, u32[]{:S(2)}, u32[]{:S(2)}) collective-permute-start(bf16[1,256,256]{2,1,0:T(8,128)(2,1)} %get-tuple-element.47), channel_id=1, source_target_pairs={{0,2},{1,3},{2,0},{3,1},{4,6},{5,7},{6,4},{7,5},{8,10},{9,11},{10,... | collective-permute-start | bytes 393224 | tf_op jit(solution)/shard_map/ppermute | solution.py:278
  20.8 2.4 %collective-permute-start.9 = (bf16[1,256,256]{2,1,0:T(8,128)(2,1)}, bf16[1,256,256]{2,1,0:T(8,128)(2,1)S(1)}, u32[]{:S(2)}, u32[]{:S(2)}) collective-permute-start(bf16[1,256,256]{2,1,0:T(8,128)(2,1)} %get-tuple-element.66), channel_id=1, source_target_pairs={{0,14},{1,15},{2,12},{3,13},{4,10},{5,11},{6,8},{7,9},{8,6},{9,7},... | collective-permute-start | bytes 393224 | tf_op jit(solution)/shard_map/ppermute | solution.py:278
  23.2 0.3 collective-permute-start.10
  23.5 2.6 %collective-permute-start.11 = (bf16[1,256,256]{2,1,0:T(8,128)(2,1)}, bf16[1,256,256]{2,1,0:T(8,128)(2,1)S(1)}, u32[]{:S(2)}, u32[]{:S(2)}) collective-permute-start(bf16[1,256,256]{2,1,0:T(8,128)(2,1)} %get-tuple-element.68), channel_id=1, source_target_pairs={{0,10},{1,11},{2,8},{3,9},{4,14},{5,15},{6,12},{7,13},{8,2},{9,3},... | collective-permute-start | bytes 393224 | tf_op jit(solution)/shard_map/ppermute | solution.py:278
  26.1 0.6 collective-permute-start.12
  26.7 0.9 copy-done
  27.7 2.6 %local_keys.1.loaded_ref = f32[2,2048,128]{2,1,0:T(8,128)S(1)} custom-call(s32[1]{0:T(128)S(6)} %copy.12.len_ref, bf16[256,1024]{1,0:T(8,128)(2,1)S(1)} %copy-done.2, bf16[256,256]{1,0:T(8,128)(2,1)S(1)} %copy-done.4, bf16[512,256]{1,0:T(8,128)(2,1)S(1)} %copy-done.3, bf16[1,256,256]{2,1,0:T(8,128)(2,1)S(1)} %copy-done), custom_call_target="tpu_custom_call" | custom-call | flops 2415919104 | bytes 393216 | tf_op jit(solution)/shard_map/local_keys/pallas_call | solution.py:396
  30.3 1.4 %copy-done.5 = f32[2,2048,128]{2,1,0:T(8,128)} copy-done((f32[2,2048,128]{2,1,0:T(8,128)}, f32[2,2048,128]{2,1,0:T(8,128)S(1)}, u32[]{:S(2)}) %copy-start.5) | copy-done | bytes 2097176
  31.7 1.5 %collective-permute-start.13 = (bf16[1,256,256]{2,1,0:T(8,128)(2,1)}, bf16[1,256,256]{2,1,0:T(8,128)(2,1)S(1)}, u32[]{:S(2)}, u32[]{:S(2)}) collective-permute-start(bf16[1,256,256]{2,1,0:T(8,128)(2,1)} %get-tuple-element.70), channel_id=1, source_target_pairs={{0,6},{1,7},{2,4},{3,5},{4,2},{5,3},{6,0},{7,1},{8,14},{9,15},{10,... | collective-permute-start | bytes 393224 | tf_op jit(solution)/shard_map/ppermute | solution.py:278
  33.1 17.2 %collective-permute-done.9 = bf16[1,256,256]{2,1,0:T(8,128)(2,1)S(1)} collective-permute-done((bf16[1,256,256]{2,1,0:T(8,128)(2,1)}, bf16[1,256,256]{2,1,0:T(8,128)(2,1)S(1)}, u32[]{:S(2)}, u32[]{:S(2)}) %collective-permute-start.9) | collective-permute-done | bytes 131104 | tf_op jit(solution)/shard_map/ppermute | solution.py:278
  50.3 1.2 collective-permute-start.14
  51.5 3.4 %collective-permute-done.10 = bf16[1,256,256]{2,1,0:T(8,128)(2,1)S(1)} collective-permute-done((bf16[1,256,256]{2,1,0:T(8,128)(2,1)}, bf16[1,256,256]{2,1,0:T(8,128)(2,1)S(1)}, u32[]{:S(2)}, u32[]{:S(2)}) %collective-permute-start.10) | collective-permute-done | bytes 131104 | tf_op jit(solution)/shard_map/ppermute | solution.py:278
  54.9 0.7 collective-permute-start.2
  55.5 3.2 %collective-permute-done.11 = bf16[1,256,256]{2,1,0:T(8,128)(2,1)S(1)} collective-permute-done((bf16[1,256,256]{2,1,0:T(8,128)(2,1)}, bf16[1,256,256]{2,1,0:T(8,128)(2,1)S(1)}, u32[]{:S(2)}, u32[]{:S(2)}) %collective-permute-start.11) | collective-permute-done | bytes 131104 | tf_op jit(solution)/shard_map/ppermute | solution.py:278
  58.7 0.7 collective-permute-start.3
  59.4 0.6 fusion.3
  62.2 0.7 collective-permute-start.4
  62.9 0.7 collective-permute-start.5
  63.6 0.7 collective-permute-start.6
  64.3 0.7 collective-permute-start.7
  65.0 0.7 collective-permute-start.8
  65.9 6.5 %collective-permute-start.15 = (bf16[2,256,256]{2,1,0:T(8,128)(2,1)S(1)}, bf16[2,256,256]{2,1,0:T(8,128)(2,1)S(1)}, u32[]{:S(2)}, u32[]{:S(2)}) collective-permute-start(bf16[2,256,256]{2,1,0:T(8,128)(2,1)S(1)} %pad_maximum_fusion), channel_id=1, source_target_pairs={{0,16},{1,17},{2,18},{3,19},{4,20},{5,21},{6,22},{7,23},{8,24},{9,... | collective-permute-start | bytes 786440 | tf_op jit(solution)/shard_map/ppermute | solution.py:304
  72.4 1.6 %copy-done.6 = f32[2,2048,128]{2,1,0:T(8,128)S(1)} copy-done((f32[2,2048,128]{2,1,0:T(8,128)S(1)}, f32[2,2048,128]{2,1,0:T(8,128)}, u32[]{:S(2)}) %copy-start.6) | copy-done | bytes 2097176
  74.0 8.0 %moved_keys.2.loaded_ref = f32[2,2048,128]{2,1,0:T(8,128)S(1)} custom-call(bf16[256,1024]{1,0:T(8,128)(2,1)S(1)} %copy-done.2, bf16[32,128,256]{2,1,0:T(8,128)(2,1)} %all-to-all-done.kv_ref, f32[2,2048,128]{2,1,0:T(8,128)S(1)} %copy-done.6), custom_call_target="tpu_custom_call" | custom-call | flops 6442450944 | bytes 1048576 | tf_op jit(solution)/shard_map/moved_keys/pallas_call | solution.py:418
  82.0 0.1 broadcast_select_fusion.refs_0_
  82.1 7.4 %collective-permute-start.18 = (bf16[2,256,256]{2,1,0:T(8,128)(2,1)S(1)}, bf16[2,256,256]{2,1,0:T(8,128)(2,1)S(1)}, u32[]{:S(2)}, u32[]{:S(2)}) collective-permute-start(bf16[2,256,256]{2,1,0:T(8,128)(2,1)S(1)} %broadcast_select_fusion.refs_0_), channel_id=1, source_target_pairs={{0,8},{1,9},{2,10},{3,11},{4,12},{5,13},{6,14},{7,15},{8,0},{9,1},... | collective-permute-start | bytes 786440 | tf_op jit(solution)/shard_map/ppermute | solution.py:321
  89.4 2.8 %collective-permute-start.17 = (bf16[2,256,256]{2,1,0:T(8,128)(2,1)S(1)}, bf16[2,256,256]{2,1,0:T(8,128)(2,1)S(1)}, u32[]{:S(2)}, u32[]{:S(2)}) collective-permute-start(bf16[2,256,256]{2,1,0:T(8,128)(2,1)S(1)} %broadcast_select_fusion.refs_0_), channel_id=1, source_target_pairs={{0,4},{1,5},{2,6},{3,7},{4,0},{5,1},{6,2},{7,3},{8,12},{9,13},{10,... | collective-permute-start | bytes 786440 | tf_op jit(solution)/shard_map/ppermute | solution.py:321
  92.2 8.0 %moved_keys.3.refs_5_ = f32[2,2048,128]{2,1,0:T(8,128)S(1)} custom-call(bf16[256,1024]{1,0:T(8,128)(2,1)S(1)} %copy-done.2, bf16[32,128,256]{2,1,0:T(8,128)(2,1)} %all-to-all-done.kv_ref, f32[2,2048,128]{2,1,0:T(8,128)S(1)} %moved_keys.2.loaded_ref), custom_call_target="tpu_custom_call" | custom-call | flops 6442450944 | bytes 1048576 | tf_op jit(solution)/shard_map/moved_keys/pallas_call | solution.py:418
  100.3 0.6 pick_other.3
  100.9 0.6 collective-permute-start.19
  101.5 1.6 %collective-permute-start.20 = (bf16[2,256,256]{2,1,0:T(8,128)(2,1)S(1)}, bf16[2,256,256]{2,1,0:T(8,128)(2,1)S(1)}, u32[]{:S(2)}, u32[]{:S(2)}) collective-permute-start(bf16[2,256,256]{2,1,0:T(8,128)(2,1)S(1)} %collective-permute-done.18.refs_3_), channel_id=1, source_target_pairs={{0,2},{1,3},{2,0},{3,1},{4,6},{5,7},{6,4},{7,5},{8,10},{9,11},{10,... | collective-permute-start | bytes 786440 | tf_op jit(solution)/shard_map/ppermute | solution.py:321
  103.2 7.3 %prefix_keys.3.refs_4_ = f32[2,2048,128]{2,1,0:T(8,128)S(1)} custom-call(s32[2]{0:T(128)S(1)} %compare_select_fusion.which_ref, bf16[256,1024]{1,0:T(8,128)(2,1)S(1)} %copy-done.2, bf16[2,256,256]{2,1,0:T(8,128)(2,1)S(1)} %broadcast_select_fusion.refs_0_, bf16[2,256,256]{2,1,0:T(8,128)(2,1)S(1)} %collective-permute-done.16.refs_1_, ...), custom_call_target="tpu_custom_call" | custom-call | flops 6442450944 | bytes 1048576 | tf_op jit(solution)/shard_map/prefix_keys/pallas_call | solution.py:442
  110.6 0.8 collective-permute-done.21.refs_2_
  111.4 0.6 pick_other.4
  112.0 1.0 collective-permute-start.23
  113.0 0.7 collective-permute-done.24.refs_3_
  113.7 5.1 %prefix_keys.4.refs_2_ = f32[2,2048,128]{2,1,0:T(8,128)S(1)} custom-call(s32[2]{0:T(128)S(1)} %compare_select_fusion.which_ref, bf16[256,1024]{1,0:T(8,128)(2,1)S(1)} %copy-done.2, bf16[2,256,256]{2,1,0:T(8,128)(2,1)S(1)} %collective-permute-done.19.refs_0_, bf16[2,256,256]{2,1,0:T(8,128)(2,1)S(1)} %collective-permute-done.20.refs_1_, ...), custom_call_target="tpu_custom_call" | custom-call | flops 4831838208 | bytes 786432 | tf_op jit(solution)/shard_map/prefix_keys/pallas_call | solution.py:442
  118.9 1.9 %collective-permute-done.23.refs_0_ = bf16[2,256,256]{2,1,0:T(8,128)(2,1)S(1)} collective-permute-done((bf16[2,256,256]{2,1,0:T(8,128)(2,1)S(1)}, bf16[2,256,256]{2,1,0:T(8,128)(2,1)S(1)}, u32[]{:S(2)}, u32[]{:S(2)}) %collective-permute-start.23) | collective-permute-done | bytes 262176 | tf_op jit(solution)/shard_map/ppermute | solution.py:321
  120.8 0.6 pick_other.5
  121.4 1.3 %collective-permute-done.25.refs_1_ = bf16[256,256]{1,0:T(8,128)(2,1)S(1)} collective-permute-done((bf16[256,256]{1,0:T(8,128)(2,1)S(1)}, bf16[256,256]{1,0:T(8,128)(2,1)S(1)}, u32[]{:S(2)}, u32[]{:S(2)}) %collective-permute-start.25) | collective-permute-done | bytes 131104 | tf_op jit(solution)/shard_map/ppermute | solution.py:311
  122.7 3.5 %prefix_keys.5 = bf16[256,1024]{1,0:T(8,128)(2,1)} custom-call(s32[2]{0:T(128)S(1)} %compare_select_fusion.which_ref, bf16[256,1024]{1,0:T(8,128)(2,1)S(1)} %copy-done.2, bf16[2,256,256]{2,1,0:T(8,128)(2,1)S(1)} %collective-permute-done.23.refs_0_, bf16[256,256]{1,0:T(8,128)(2,1)S(1)} %collective-permute-done.25.refs_1_, f32[2,2048,128]{2,1,0:T(8,128)S(1)} %prefix_keys.4.refs_2_), custom_call_target="tpu_custom_call" | custom-call | flops 1610612736 | bytes 262144 | tf_op jit(solution)/shard_map/prefix_keys/pallas_call | solution.py:442
  (65 shorter events, 0.7 us)
Async XLA Ops:
  0.0 4.7 %collective-permute-start = (bf16[4096,256]{1,0:T(8,128)(2,1)}, bf16[4096,256]{1,0:T(8,128)(2,1)}, u32[]{:S(2)}, u32[]{:S(2)}) collective-permute-start(bf16[4096,256]{1,0:T(8,128)(2,1)} %param.15), channel_id=1, source_target_pairs={{0,1},{1,0},{2,3},{3,2},{4,5},{5,4},{6,7},{7,6},{8,9},{9,8},{10,11... | collective-permute-start | bytes 6291464 | tf_op jit(solution)/shard_map/ppermute | solution.py:311
  4.7 7.9 %copy-start.10 = (s32[32]{0:T(128)S(1)}, s32[32]{0:T(128)}, u32[]{:S(2)}) copy-start(s32[32]{0:T(128)} %param.17) | copy-start | bytes 388
  4.7 8.5 %copy-start.8 = (s32[2]{0:T(128)S(1)}, s32[2]{0:T(128)}, u32[]{:S(2)}) copy-start(s32[2]{0:T(128)} %owner_ref.1) | copy-start | bytes 28
  4.7 67.6 %all-to-all-start = ((bf16[32,128,256]{2,1,0:T(8,128)(2,1)}), bf16[32,128,256]{2,1,0:T(8,128)(2,1)}, u32[]{:S(2)}, u32[]{:S(2)}) async-start(bf16[32,128,256]{2,1,0:T(8,128)(2,1)} %pack_moved.1), calls=%async_computation | async-start | bytes 4194304 | tf_op jit(solution)/shard_map/all_to_all | solution.py:256
  16.0 10.7 %copy-start.2 = (bf16[256,1024]{1,0:T(8,128)(2,1)S(1)}, bf16[256,1024]{1,0:T(8,128)(2,1)}, u32[]{:S(2)}) copy-start(bf16[256,1024]{1,0:T(8,128)(2,1)} %q_ref.11) | copy-start | bytes 1572868
  16.0 10.7 %copy-start.3 = (bf16[512,256]{1,0:T(8,128)(2,1)S(1)}, bf16[512,256]{1,0:T(8,128)(2,1)}, u32[]{:S(2)}) copy-start(bf16[512,256]{1,0:T(8,128)(2,1)} %own_ref.1) | copy-start | bytes 786436
  16.0 10.7 %copy-start.4 = (bf16[256,256]{1,0:T(8,128)(2,1)S(1)}, bf16[256,256]{1,0:T(8,128)(2,1)}, u32[]{:S(2)}) copy-start(bf16[256,256]{1,0:T(8,128)(2,1)} %suffix_ref.1) | copy-start | bytes 393220
  19.1 12.6 %collective-permute-start.1 = (bf16[1,256,256]{2,1,0:T(8,128)(2,1)}, bf16[1,256,256]{2,1,0:T(8,128)(2,1)S(1)}, u32[]{:S(2)}, u32[]{:S(2)}) collective-permute-start(bf16[1,256,256]{2,1,0:T(8,128)(2,1)} %get-tuple-element.47), channel_id=1, source_target_pairs={{0,2},{1,3},{2,0},{3,1},{4,6},{5,7},{6,4},{7,5},{8,10},{9,11},{10,... | collective-permute-start | bytes 393224 | tf_op jit(solution)/shard_map/ppermute | solution.py:278
  20.8 29.5 %collective-permute-start.9 = (bf16[1,256,256]{2,1,0:T(8,128)(2,1)}, bf16[1,256,256]{2,1,0:T(8,128)(2,1)S(1)}, u32[]{:S(2)}, u32[]{:S(2)}) collective-permute-start(bf16[1,256,256]{2,1,0:T(8,128)(2,1)} %get-tuple-element.66), channel_id=1, source_target_pairs={{0,14},{1,15},{2,12},{3,13},{4,10},{5,11},{6,8},{7,9},{8,6},{9,7},... | collective-permute-start | bytes 393224 | tf_op jit(solution)/shard_map/ppermute | solution.py:278
  23.2 31.7 %collective-permute-start.10 = (bf16[1,256,256]{2,1,0:T(8,128)(2,1)}, bf16[1,256,256]{2,1,0:T(8,128)(2,1)S(1)}, u32[]{:S(2)}, u32[]{:S(2)}) collective-permute-start(bf16[1,256,256]{2,1,0:T(8,128)(2,1)} %get-tuple-element.67), channel_id=1, source_target_pairs={{0,12},{1,13},{2,14},{3,15},{4,8},{5,9},{6,10},{7,11},{8,4},{9,5},... | collective-permute-start | bytes 393224 | tf_op jit(solution)/shard_map/ppermute | solution.py:278
  23.5 35.2 %collective-permute-start.11 = (bf16[1,256,256]{2,1,0:T(8,128)(2,1)}, bf16[1,256,256]{2,1,0:T(8,128)(2,1)S(1)}, u32[]{:S(2)}, u32[]{:S(2)}) collective-permute-start(bf16[1,256,256]{2,1,0:T(8,128)(2,1)} %get-tuple-element.68), channel_id=1, source_target_pairs={{0,10},{1,11},{2,8},{3,9},{4,14},{5,15},{6,12},{7,13},{8,2},{9,3},... | collective-permute-start | bytes 393224 | tf_op jit(solution)/shard_map/ppermute | solution.py:278
  26.1 36.1 %collective-permute-start.12 = (bf16[1,256,256]{2,1,0:T(8,128)(2,1)}, bf16[1,256,256]{2,1,0:T(8,128)(2,1)S(1)}, u32[]{:S(2)}, u32[]{:S(2)}) collective-permute-start(bf16[1,256,256]{2,1,0:T(8,128)(2,1)} %get-tuple-element.69), channel_id=1, source_target_pairs={{0,8},{1,9},{2,10},{3,11},{4,12},{5,13},{6,14},{7,15},{8,0},{9,1},... | collective-permute-start | bytes 393224 | tf_op jit(solution)/shard_map/ppermute | solution.py:278
  26.7 0.9 copy-start
  27.6 22.7 %copy-start.18 = (bf16[1,256,256]{2,1,0:T(8,128)(2,1)S(1)}, bf16[1,256,256]{2,1,0:T(8,128)(2,1)}, u32[]{:S(2)}) copy-start(bf16[1,256,256]{2,1,0:T(8,128)(2,1)} %get-tuple-element.71) | copy-start | bytes 393220
  27.6 27.3 %copy-start.17 = (bf16[1,256,256]{2,1,0:T(8,128)(2,1)S(1)}, bf16[1,256,256]{2,1,0:T(8,128)(2,1)}, u32[]{:S(2)}) copy-start(bf16[1,256,256]{2,1,0:T(8,128)(2,1)} %get-tuple-element.58) | copy-start | bytes 393220
  27.6 31.1 %copy-start.16 = (bf16[1,256,256]{2,1,0:T(8,128)(2,1)S(1)}, bf16[1,256,256]{2,1,0:T(8,128)(2,1)}, u32[]{:S(2)}) copy-start(bf16[1,256,256]{2,1,0:T(8,128)(2,1)} %get-tuple-element.59) | copy-start | bytes 393220
  27.6 31.8 %copy-start.9 = (s32[2]{0:T(128)S(1)}, s32[2]{0:T(128)}, u32[]{:S(2)}) copy-start(s32[2]{0:T(128)} %owner_ref.1) | copy-start | bytes 28
  27.6 34.6 %copy-start.15 = (bf16[1,256,256]{2,1,0:T(8,128)(2,1)S(1)}, bf16[1,256,256]{2,1,0:T(8,128)(2,1)}, u32[]{:S(2)}) copy-start(bf16[1,256,256]{2,1,0:T(8,128)(2,1)} %get-tuple-element.60) | copy-start | bytes 393220
  27.6 35.3 %copy-start.14 = (bf16[1,256,256]{2,1,0:T(8,128)(2,1)S(1)}, bf16[1,256,256]{2,1,0:T(8,128)(2,1)}, u32[]{:S(2)}) copy-start(bf16[1,256,256]{2,1,0:T(8,128)(2,1)} %get-tuple-element.61) | copy-start | bytes 393220
  27.6 36.0 %copy-start.13 = (bf16[1,256,256]{2,1,0:T(8,128)(2,1)S(1)}, bf16[1,256,256]{2,1,0:T(8,128)(2,1)}, u32[]{:S(2)}) copy-start(bf16[1,256,256]{2,1,0:T(8,128)(2,1)} %get-tuple-element.62) | copy-start | bytes 393220
  27.6 36.7 %copy-start.12 = (bf16[1,256,256]{2,1,0:T(8,128)(2,1)S(1)}, bf16[1,256,256]{2,1,0:T(8,128)(2,1)}, u32[]{:S(2)}) copy-start(bf16[1,256,256]{2,1,0:T(8,128)(2,1)} %get-tuple-element.63) | copy-start | bytes 393220
  27.6 37.3 %copy-start.11 = (bf16[1,256,256]{2,1,0:T(8,128)(2,1)S(1)}, bf16[1,256,256]{2,1,0:T(8,128)(2,1)}, u32[]{:S(2)}) copy-start(bf16[1,256,256]{2,1,0:T(8,128)(2,1)} %get-tuple-element.64) | copy-start | bytes 393220
  27.6 38.0 %copy-start.1 = (bf16[1,256,256]{2,1,0:T(8,128)(2,1)S(1)}, bf16[1,256,256]{2,1,0:T(8,128)(2,1)}, u32[]{:S(2)}) copy-start(bf16[1,256,256]{2,1,0:T(8,128)(2,1)} %get-tuple-element.48.after_ref) | copy-start | bytes 393220
  27.6 38.1 %copy-start.7 = (bf16[1,256,256]{2,1,0:T(8,128)(2,1)S(1)}, bf16[1,256,256]{2,1,0:T(8,128)(2,1)}, u32[]{:S(2)}) copy-start(bf16[1,256,256]{2,1,0:T(8,128)(2,1)} %get-tuple-element.65) | copy-start | bytes 393220
  30.3 1.4 %copy-start.5 = (f32[2,2048,128]{2,1,0:T(8,128)}, f32[2,2048,128]{2,1,0:T(8,128)S(1)}, u32[]{:S(2)}) copy-start(f32[2,2048,128]{2,1,0:T(8,128)S(1)} %local_keys.1.loaded_ref) | copy-start | bytes 6291460
  31.7 31.2 %collective-permute-start.13 = (bf16[1,256,256]{2,1,0:T(8,128)(2,1)}, bf16[1,256,256]{2,1,0:T(8,128)(2,1)S(1)}, u32[]{:S(2)}, u32[]{:S(2)}) collective-permute-start(bf16[1,256,256]{2,1,0:T(8,128)(2,1)} %get-tuple-element.70), channel_id=1, source_target_pairs={{0,6},{1,7},{2,4},{3,5},{4,2},{5,3},{6,0},{7,1},{8,14},{9,15},{10,... | collective-permute-start | bytes 393224 | tf_op jit(solution)/shard_map/ppermute | solution.py:278
  50.3 13.2 %collective-permute-start.14 = (bf16[1,256,256]{2,1,0:T(8,128)(2,1)S(1)}, bf16[1,256,256]{2,1,0:T(8,128)(2,1)S(1)}, u32[]{:S(2)}, u32[]{:S(2)}) collective-permute-start(bf16[1,256,256]{2,1,0:T(8,128)(2,1)S(1)} %copy-done.18), channel_id=1, source_target_pairs={{0,4},{1,5},{2,6},{3,7},{4,0},{5,1},{6,2},{7,3},{8,12},{9,13},{10,... | collective-permute-start | bytes 393224 | tf_op jit(solution)/shard_map/ppermute | solution.py:278
  54.9 9.4 %collective-permute-start.2 = (bf16[1,256,256]{2,1,0:T(8,128)(2,1)S(1)}, bf16[1,256,256]{2,1,0:T(8,128)(2,1)S(1)}, u32[]{:S(2)}, u32[]{:S(2)}) collective-permute-start(bf16[1,256,256]{2,1,0:T(8,128)(2,1)S(1)} %copy-done.17), channel_id=1, source_target_pairs={{30,16},{31,17}} | collective-permute-start | bytes 393224 | tf_op jit(solution)/shard_map/ppermute | solution.py:278
  58.7 6.3 %collective-permute-start.3 = (bf16[1,256,256]{2,1,0:T(8,128)(2,1)S(1)}, bf16[1,256,256]{2,1,0:T(8,128)(2,1)S(1)}, u32[]{:S(2)}, u32[]{:S(2)}) collective-permute-start(bf16[1,256,256]{2,1,0:T(8,128)(2,1)S(1)} %copy-done.16), channel_id=1, source_target_pairs={{30,18},{31,19}} | collective-permute-start | bytes 393224 | tf_op jit(solution)/shard_map/ppermute | solution.py:278
  62.2 3.5 %collective-permute-start.4 = (bf16[1,256,256]{2,1,0:T(8,128)(2,1)S(1)}, bf16[1,256,256]{2,1,0:T(8,128)(2,1)S(1)}, u32[]{:S(2)}, u32[]{:S(2)}) collective-permute-start(bf16[1,256,256]{2,1,0:T(8,128)(2,1)S(1)} %copy-done.15), channel_id=1, source_target_pairs={{30,20},{31,21}} | collective-permute-start | bytes 393224 | tf_op jit(solution)/shard_map/ppermute | solution.py:278
  62.9 2.9 %collective-permute-start.5 = (bf16[1,256,256]{2,1,0:T(8,128)(2,1)S(1)}, bf16[1,256,256]{2,1,0:T(8,128)(2,1)S(1)}, u32[]{:S(2)}, u32[]{:S(2)}) collective-permute-start(bf16[1,256,256]{2,1,0:T(8,128)(2,1)S(1)} %copy-done.14), channel_id=1, source_target_pairs={{30,22},{31,23}} | collective-permute-start | bytes 393224 | tf_op jit(solution)/shard_map/ppermute | solution.py:278
  63.6 2.2 %collective-permute-start.6 = (bf16[1,256,256]{2,1,0:T(8,128)(2,1)S(1)}, bf16[1,256,256]{2,1,0:T(8,128)(2,1)S(1)}, u32[]{:S(2)}, u32[]{:S(2)}) collective-permute-start(bf16[1,256,256]{2,1,0:T(8,128)(2,1)S(1)} %copy-done.13), channel_id=1, source_target_pairs={{30,24},{31,25}} | collective-permute-start | bytes 393224 | tf_op jit(solution)/shard_map/ppermute | solution.py:278
  64.3 1.5 %collective-permute-start.7 = (bf16[1,256,256]{2,1,0:T(8,128)(2,1)S(1)}, bf16[1,256,256]{2,1,0:T(8,128)(2,1)S(1)}, u32[]{:S(2)}, u32[]{:S(2)}) collective-permute-start(bf16[1,256,256]{2,1,0:T(8,128)(2,1)S(1)} %copy-done.12), channel_id=1, source_target_pairs={{30,26},{31,27}} | collective-permute-start | bytes 393224 | tf_op jit(solution)/shard_map/ppermute | solution.py:278
  65.0 0.8 collective-permute-start.8
  65.9 16.1 %collective-permute-start.15 = (bf16[2,256,256]{2,1,0:T(8,128)(2,1)S(1)}, bf16[2,256,256]{2,1,0:T(8,128)(2,1)S(1)}, u32[]{:S(2)}, u32[]{:S(2)}) collective-permute-start(bf16[2,256,256]{2,1,0:T(8,128)(2,1)S(1)} %pad_maximum_fusion), channel_id=1, source_target_pairs={{0,16},{1,17},{2,18},{3,19},{4,20},{5,21},{6,22},{7,23},{8,24},{9,... | collective-permute-start | bytes 786440 | tf_op jit(solution)/shard_map/ppermute | solution.py:304
  72.4 1.6 %copy-start.6 = (f32[2,2048,128]{2,1,0:T(8,128)S(1)}, f32[2,2048,128]{2,1,0:T(8,128)}, u32[]{:S(2)}) copy-start(f32[2,2048,128]{2,1,0:T(8,128)} %copy-done.5) | copy-start | bytes 6291460
  82.1 18.2 %collective-permute-start.18 = (bf16[2,256,256]{2,1,0:T(8,128)(2,1)S(1)}, bf16[2,256,256]{2,1,0:T(8,128)(2,1)S(1)}, u32[]{:S(2)}, u32[]{:S(2)}) collective-permute-start(bf16[2,256,256]{2,1,0:T(8,128)(2,1)S(1)} %broadcast_select_fusion.refs_0_), channel_id=1, source_target_pairs={{0,8},{1,9},{2,10},{3,11},{4,12},{5,13},{6,14},{7,15},{8,0},{9,1},... | collective-permute-start | bytes 786440 | tf_op jit(solution)/shard_map/ppermute | solution.py:321
  89.4 10.8 %collective-permute-start.17 = (bf16[2,256,256]{2,1,0:T(8,128)(2,1)S(1)}, bf16[2,256,256]{2,1,0:T(8,128)(2,1)S(1)}, u32[]{:S(2)}, u32[]{:S(2)}) collective-permute-start(bf16[2,256,256]{2,1,0:T(8,128)(2,1)S(1)} %broadcast_select_fusion.refs_0_), channel_id=1, source_target_pairs={{0,4},{1,5},{2,6},{3,7},{4,0},{5,1},{6,2},{7,3},{8,12},{9,13},{10,... | collective-permute-start | bytes 786440 | tf_op jit(solution)/shard_map/ppermute | solution.py:321
  92.2 8.0 %collective-permute-start.16 = (bf16[2,256,256]{2,1,0:T(8,128)(2,1)S(1)}, bf16[2,256,256]{2,1,0:T(8,128)(2,1)S(1)}, u32[]{:S(2)}, u32[]{:S(2)}) collective-permute-start(bf16[2,256,256]{2,1,0:T(8,128)(2,1)S(1)} %broadcast_select_fusion.refs_0_), channel_id=1, source_target_pairs={{0,2},{1,3},{2,0},{3,1},{4,6},{5,7},{6,4},{7,5},{8,10},{9,11},{10,... | collective-permute-start | bytes 786440 | tf_op jit(solution)/shard_map/ppermute | solution.py:321
  100.8 2.3 %collective-permute-start.22 = (bf16[1024,256]{1,0:T(8,128)(2,1)S(1)}, bf16[1024,256]{1,0:T(8,128)(2,1)S(1)}, u32[]{:S(2)}, u32[]{:S(2)}) collective-permute-start(bf16[1024,256]{1,0:T(8,128)(2,1)S(1)} %pick_other.3), channel_id=1, source_target_pairs={{0,1},{1,0},{2,3},{3,2},{4,5},{5,4},{6,7},{7,6},{8,9},{9,8},{10,11... | collective-permute-start | bytes 1572872 | tf_op jit(solution)/shard_map/ppermute | solution.py:311
  100.9 9.6 %collective-permute-start.19 = (bf16[2,256,256]{2,1,0:T(8,128)(2,1)S(1)}, bf16[2,256,256]{2,1,0:T(8,128)(2,1)S(1)}, u32[]{:S(2)}, u32[]{:S(2)}) collective-permute-start(bf16[2,256,256]{2,1,0:T(8,128)(2,1)S(1)} %collective-permute-done.16.refs_1_), channel_id=1, source_target_pairs={{0,4},{1,5},{2,6},{3,7},{4,0},{5,1},{6,2},{7,3},{8,12},{9,13},{10,... | collective-permute-start | bytes 786440 | tf_op jit(solution)/shard_map/ppermute | solution.py:321
  101.5 9.0 %collective-permute-start.20 = (bf16[2,256,256]{2,1,0:T(8,128)(2,1)S(1)}, bf16[2,256,256]{2,1,0:T(8,128)(2,1)S(1)}, u32[]{:S(2)}, u32[]{:S(2)}) collective-permute-start(bf16[2,256,256]{2,1,0:T(8,128)(2,1)S(1)} %collective-permute-done.18.refs_3_), channel_id=1, source_target_pairs={{0,2},{1,3},{2,0},{3,1},{4,6},{5,7},{6,4},{7,5},{8,10},{9,11},{10,... | collective-permute-start | bytes 786440 | tf_op jit(solution)/shard_map/ppermute | solution.py:321
  103.1 8.3 %collective-permute-start.21 = (bf16[2,256,256]{2,1,0:T(8,128)(2,1)S(1)}, bf16[2,256,256]{2,1,0:T(8,128)(2,1)S(1)}, u32[]{:S(2)}, u32[]{:S(2)}) collective-permute-start(bf16[2,256,256]{2,1,0:T(8,128)(2,1)S(1)} %collective-permute-done.17.refs_2_), channel_id=1, source_target_pairs={{0,8},{1,9},{2,10},{3,11},{4,12},{5,13},{6,14},{7,15},{8,0},{9,1},... | collective-permute-start | bytes 786440 | tf_op jit(solution)/shard_map/ppermute | solution.py:321
  112.0 1.8 %collective-permute-start.24 = (bf16[768,256]{1,0:T(8,128)(2,1)S(1)}, bf16[768,256]{1,0:T(8,128)(2,1)S(1)}, u32[]{:S(2)}, u32[]{:S(2)}) collective-permute-start(bf16[768,256]{1,0:T(8,128)(2,1)S(1)} %pick_other.4), channel_id=1, source_target_pairs={{0,1},{1,0},{2,3},{3,2},{4,5},{5,4},{6,7},{7,6},{8,9},{9,8},{10,11... | collective-permute-start | bytes 1179656 | tf_op jit(solution)/shard_map/ppermute | solution.py:311
  112.0 8.7 %collective-permute-start.23 = (bf16[2,256,256]{2,1,0:T(8,128)(2,1)S(1)}, bf16[2,256,256]{2,1,0:T(8,128)(2,1)S(1)}, u32[]{:S(2)}, u32[]{:S(2)}) collective-permute-start(bf16[2,256,256]{2,1,0:T(8,128)(2,1)S(1)} %collective-permute-done.21.refs_2_), channel_id=1, source_target_pairs={{0,2},{1,3},{2,0},{3,1},{4,6},{5,7},{6,4},{7,5},{8,10},{9,11},{10,... | collective-permute-start | bytes 786440 | tf_op jit(solution)/shard_map/ppermute | solution.py:321
  121.3 1.4 %collective-permute-start.25 = (bf16[256,256]{1,0:T(8,128)(2,1)S(1)}, bf16[256,256]{1,0:T(8,128)(2,1)S(1)}, u32[]{:S(2)}, u32[]{:S(2)}) collective-permute-start(bf16[256,256]{1,0:T(8,128)(2,1)S(1)} %pick_other.5), channel_id=1, source_target_pairs={{0,1},{1,0},{2,3},{3,2},{4,5},{5,4},{6,7},{7,6},{8,9},{9,8},{10,11... | collective-permute-start | bytes 393224 | tf_op jit(solution)/shard_map/ppermute | solution.py:311

commit v16 on v15

--- a/solution.py
+++ b/solution.py
@@ -192,17 +192,19 @@
         store(entry, mark_ref).wait()
 
 
-def stage_kernel(owner_ref, kept_ref, swapped_ref, *refs):
+def stage_kernel(owner_ref, reader_ref, kept_ref, swapped_ref, info_ref, *refs):
     outs, (sought_ref, known_ref, in_sems, out_sems) = refs[:-4], refs[-4:]
     chips, sought = sought_ref.shape[:2]
     replicas = 4 * chips
     me = lax.axis_index("replica")
     core, chip, is_last = me % 2, me // 2 % chips, me // 2 == replicas // 2 - 1
     owners = [owner_ref[prefix] for prefix in range(sought + 1)]
-    after = False
-    for prefix in range(sought):
-        after |= owners[prefix] == replicas - 1
-        owners[prefix] = jnp.where(after, owners[prefix + 1], owners[prefix])
+    known = sum(
+        jnp.where(owner == replicas - 1, prefix, 0) for prefix, owner in enumerate(owners)
+    )
+    owners = [
+        jnp.where(known <= prefix, owners[prefix + 1], owners[prefix]) for prefix in range(sought)
+    ]
 
     def load(source, step, prefix):
         target = sought_ref.at[step, prefix] if prefix < sought else known_ref.at[step, 0]
@@ -224,6 +226,14 @@
     def _():
         for step in range(chips):
             start(step, sought, core == 1)
+
+    for place, wanted in enumerate((reader_ref[me], reader_ref[me ^ 1])):
+        ahead = jnp.where(wanted < known, wanted + 1, wanted)
+        info_ref[place] = jnp.where(wanted == known, 0, ahead)
+    for place, owner in enumerate([replicas - 1, *owners]):
+        info_ref[2 + place] = chip ^ (owner // 2 % chips)
+        same = owner // (replicas // 2) == me // (replicas // 2)
+        info_ref[3 + sought + place] = jnp.where(same, 1, 0)
 
     for step in range(chips):
         for prefix in range(sought):
@@ -242,14 +252,10 @@
 
 def multicast(prefix_cache, owners, readers, outgoing, fold_local, fold_moved):
     replicas = lax.axis_size("replica")
-    me = lax.axis_index("replica")
     half = replicas // 2
     chips = half // 2
-    chip = me // 2 % chips
     width = prefix_cache.shape[1]
-    ids = jnp.arange(owners.shape[0], dtype=jnp.int32)
-    known = jnp.sum(jnp.where(owners == replicas - 1, ids, 0))
-    sought = jnp.where(ids[:-1] >= known, owners[1:], owners[:-1])
+    prefixes = owners.shape[0]
 
     split = prefix_cache.reshape(2, chips, -1, width)
     swapped, outgoing = lax.optimization_barrier((swap_cores(prefix_cache), outgoing))
@@ -257,11 +263,13 @@
     swapped = swapped.reshape(split.shape)
     pieces = jax.ShapeDtypeStruct((owners.shape[0] - 1, *split.shape[2:]), split.dtype)
     piece = jax.ShapeDtypeStruct((1, *split.shape[2:]), split.dtype)
-    staged = pl.pallas_call(
+    info, *staged = pl.pallas_call(
         stage_kernel,
-        out_shape=(pieces,) * chips + (piece,) * chips,
-        in_specs=[IN_SMEM] + [IN_HBM] * 2,
-        out_specs=(IN_HBM,) * (2 * chips),
+        out_shape=(jax.ShapeDtypeStruct((2 + 2 * prefixes,), jnp.int32),)
+        + (pieces,) * chips
+        + (piece,) * chips,
+        in_specs=[IN_SMEM] * 2 + [IN_HBM] * 2,
+        out_specs=(IN_SMEM,) + (IN_HBM,) * (2 * chips),
         scratch_shapes=[
             pltpu.VMEM((chips, *pieces.shape), split.dtype),
             pltpu.VMEM((chips, *piece.shape), split.dtype),
@@ -270,8 +278,8 @@
         ],
         compiler_params=COPY_PARAMS,
         name="stage_prefix",
-    )(owners, split, swapped)
-    staged = list(staged)
+    )(owners, readers, split, swapped)
+    place, away, same_half = info[:2], info[2:2 + prefixes], info[2 + prefixes:] == 1
 
     def to_peers(staged, senders):
         return [
@@ -280,30 +288,28 @@
             if step
         ]
 
-    def choose(own, passed, source):
-        away = chip ^ source
+    def choose(own, passed, away):
         for step, rows in enumerate(passed, 1):
             own = jnp.where((away == step)[:, None, None], rows, own)
         return own
 
     passed = to_peers(staged[:chips], range(replicas))
-    wanted = jnp.stack([readers[me], readers[me ^ 1]])
-    place = jnp.where(wanted == known, 0, wanted + (wanted < known))
-    passed[0], local, place, *known_staged = lax.optimization_barrier(
-        (passed[0], fold_local(staged[0]), place, *staged[chips:])
+    passed[0], local, *known_staged = lax.optimization_barrier(
+        (passed[0], fold_local(staged[0]), *staged[chips:])
     )
     passed_known = to_peers(known_staged, (replicas - 2, replicas - 1))
-    last_chip = jnp.full((1,), chips - 1, jnp.int32)
-    found = jnp.concatenate(
-        [
-            choose(known_staged[0], passed_known, last_chip),
-            choose(staged[0], passed, sought // 2 % chips),
-        ]
-    )
-    source = jnp.concatenate([jnp.full((1,), replicas - 1, jnp.int32), sought])
+    found = choose(staged[0], passed, away[1:])
     passed = lax.ppermute(found, "replica", [(i, (i + half) % replicas) for i in range(replicas)])
-    passed, state_now = lax.optimization_barrier((passed, fold_moved(arrived, local, 0)))
-    held = jnp.where((source // half == me // half)[:, None, None], found, passed)
+    found_known = choose(known_staged[0], passed_known, away[:1])
+    passed_known = lax.ppermute(found_known, "replica", [(i + half, i) for i in range(half)])
+    passed, passed_known, state_now = lax.optimization_barrier(
+        (passed, passed_known, fold_moved(arrived, local, 0))
+    )
+    held = jnp.where(
+        same_half[:, None, None],
+        jnp.concatenate([found_known, found]),
+        jnp.concatenate([passed_known, passed]),
+    )
     return held, place, state_now, arrived
 
 

time: 127 us -> 124 us (0.976)
  between operations: 3.92 us -> 10.4 us
  waiting for transfers between devices: 28.6 us -> 22.7 us
  other arithmetic: 3.08 us -> 0.29 us
    ppermute x14, waiting for transfers between devices: 23.8 us -> 17.8 us  [to_peers(): lax.ppermute(rows, 'replica', [(i, i ^ 2 * step) for i in senders])]
    ppermute x7, starting transfers between devices: 13.4 us -> 9.07 us  [gather_step(): return lax.ppermute(gathered[step ^ 1 << last], 'replica', pairs)]
    select_n x2 -> x1, other arithmetic: 2.14 us -> 0.1 us  [multicast(): jnp.where(same_half[:, None, None], jnp.concatenate([found_known, found])...]
    ppermute x0 -> x1, starting transfers between devices: none -> 1.47 us  [multicast(): lax.ppermute(found_known, 'replica', [(i + half, i) for i in range(half)])]
    unnamed x38 -> x34, local copies, waits for them, and re-layouts: 3.93 us -> 3.92 us
  transfers between devices with their start and end apart: 27 -> 28, of which waited for: 7 -> 8; matrix products, arithmetic and copies ran while one was open for 3% -> 1% of each run, Pallas kernels for 30% -> 31%
where the time goes in v16:
time: 124 us; the launch traced here: 123 us
  Pallas kernels  43.3 us (35%)
  starting transfers between devices  41.5 us (33%)
  waiting for transfers between devices  22.7 us (18%)
  between operations  10.4 us (8%)
  local copies, waits for them, and re-layouts  5.28 us (4%)
    ppermute x14, waiting for transfers between devices, to_peers(): lax.ppermute(rows, 'replica', [(i, i ^ 2 * step) for i in senders])  17.8 us
    pallas_call x3, Pallas kernels, fold_prefix(): pl.pallas_call(functools.partial(prefix_kernel, factor, last, len(pieces)...  16 us
    pallas_call x2, Pallas kernels, fold_moved(): pl.pallas_call(functools.partial(moved_kernel, factor, steps), out_shape=...  16 us
    ppermute x14, starting transfers between devices, to_peers(): lax.ppermute(rows, 'replica', [(i, i ^ 2 * step) for i in senders])  15.4 us
    ppermute x7, starting transfers between devices, gather_step(): return lax.ppermute(gathered[step ^ 1 << last], 'replica', pairs)  9.07 us
    ppermute x1, starting transfers between devices, multicast(): lax.ppermute(found, 'replica', [(i, (i + half) % replicas) for i in range...  7.53 us
    all_to_all x1, starting transfers between devices, multicast(): lax.all_to_all(outgoing, 'replica', split_axis=0, concat_axis=0, tiled=True)  7.35 us
    unnamed x34, local copies, waits for them, and re-layouts  3.92 us
  transfers between devices with their start and end apart: 28, of which 8 were waited for; matrix products, arithmetic and copies ran while one was open for 1% of the time, Pallas kernels for 31%

profile of v16, /device:TPU:0, one launch (start us, length us, event | category | flops | bytes accessed | tf_op | source)
XLA Modules:
  0.0 123.4 jit_solution(5680442199382137157)
XLA Ops:
  0.0 0.5 collective-permute-start
  1.1 3.4 %pack_moved.1 = bf16[32,128,256]{2,1,0:T(8,128)(2,1)} custom-call(s32[1,32]{1,0:T(1,128)} %target_ref.1, s32[1,32]{1,0:T(1,128)} %block_ref.1, s32[1]{0:T(128)S(6)} %copy.13.count_ref, bf16[32,128,256]{2,1,0:T(8,128)(2,1)} %pool_ref.1), custom_call_target="tpu_custom_call" | custom-call | tf_op jit(solution)/shard_map/pack_moved/pallas_call | solution.py:387
  4.6 7.3 %all-to-all-start = ((bf16[32,128,256]{2,1,0:T(8,128)(2,1)}), bf16[32,128,256]{2,1,0:T(8,128)(2,1)}, u32[]{:S(2)}, u32[]{:S(2)}) async-start(bf16[32,128,256]{2,1,0:T(8,128)(2,1)} %pack_moved.1), calls=%async_computation | async-start | bytes 4194304 | tf_op jit(solution)/shard_map/all_to_all | solution.py:262
  12.6 3.6 %stage_prefix.1 = (s32[6]{0:T(128)}, bf16[1,256,256]{2,1,0:T(8,128)(2,1)}, bf16[1,256,256]{2,1,0:T(8,128)(2,1)}, bf16[1,256,256]{2,1,0:T(8,128)(2,1)}, bf16[1,25...) custom-call(s32[2]{0:T(128)} %owner_ref.1, ...), custom_call_target="tpu_custom_call" | custom-call | tf_op jit(solution)/shard_map/stage_prefix/pallas_call | solution.py:266
  16.2 1.4 %fusion = (s32[1]{0:T(128)}, s32[1]{0:T(128)}) fusion(s32[6]{0:T(128)} %get-tuple-element.48), kind=kLoop, calls=%fused_computation.4 | loop fusion | bytes 16 | tf_op jit(solution)/shard_map/slice | solution.py:303
  26.1 1.8 %collective-permute-start.1 = (bf16[1,256,256]{2,1,0:T(8,128)(2,1)}, bf16[1,256,256]{2,1,0:T(8,128)(2,1)S(1)}, u32[]{:S(2)}, u32[]{:S(2)}) collective-permute-start(bf16[1,256,256]{2,1,0:T(8,128)(2,1)} %get-tuple-element.49), channel_id=1, source_target_pairs={{0,2},{1,3},{2,0},{3,1},{4,6},{5,7},{6,4},{7,5},{8,10},{9,11},{10,... | collective-permute-start | bytes 393224 | tf_op jit(solution)/shard_map/ppermute | solution.py:286
  27.9 2.4 %collective-permute-start.9 = (bf16[1,256,256]{2,1,0:T(8,128)(2,1)}, bf16[1,256,256]{2,1,0:T(8,128)(2,1)S(1)}, u32[]{:S(2)}, u32[]{:S(2)}) collective-permute-start(bf16[1,256,256]{2,1,0:T(8,128)(2,1)} %get-tuple-element.67), channel_id=1, source_target_pairs={{0,14},{1,15},{2,12},{3,13},{4,10},{5,11},{6,8},{7,9},{8,6},{9,7},... | collective-permute-start | bytes 393224 | tf_op jit(solution)/shard_map/ppermute | solution.py:286
  30.3 0.3 collective-permute-start.10
  30.6 2.6 %collective-permute-start.11 = (bf16[1,256,256]{2,1,0:T(8,128)(2,1)}, bf16[1,256,256]{2,1,0:T(8,128)(2,1)S(1)}, u32[]{:S(2)}, u32[]{:S(2)}) collective-permute-start(bf16[1,256,256]{2,1,0:T(8,128)(2,1)} %get-tuple-element.69), channel_id=1, source_target_pairs={{0,10},{1,11},{2,8},{3,9},{4,14},{5,15},{6,12},{7,13},{8,2},{9,3},... | collective-permute-start | bytes 393224 | tf_op jit(solution)/shard_map/ppermute | solution.py:286
  33.2 0.6 collective-permute-start.12
  33.8 0.9 copy-done
  34.8 2.6 %local_keys.1.loaded_ref = f32[2,2048,128]{2,1,0:T(8,128)S(1)} custom-call(s32[1]{0:T(128)S(6)} %copy.12.len_ref, bf16[256,1024]{1,0:T(8,128)(2,1)S(1)} %copy-done.2, bf16[256,256]{1,0:T(8,128)(2,1)S(1)} %copy-done.4, bf16[512,256]{1,0:T(8,128)(2,1)S(1)} %copy-done.3, bf16[1,256,256]{2,1,0:T(8,128)(2,1)S(1)} %copy-done), custom_call_target="tpu_custom_call" | custom-call | flops 2415919104 | bytes 393216 | tf_op jit(solution)/shard_map/local_keys/pallas_call | solution.py:402
  37.4 1.4 %copy-done.5 = f32[2,2048,128]{2,1,0:T(8,128)} copy-done((f32[2,2048,128]{2,1,0:T(8,128)}, f32[2,2048,128]{2,1,0:T(8,128)S(1)}, u32[]{:S(2)}) %copy-start.5) | copy-done | bytes 2097176
  38.7 2.1 %collective-permute-start.13 = (bf16[1,256,256]{2,1,0:T(8,128)(2,1)S(1)}, bf16[1,256,256]{2,1,0:T(8,128)(2,1)S(1)}, u32[]{:S(2)}, u32[]{:S(2)}) collective-permute-start(bf16[1,256,256]{2,1,0:T(8,128)(2,1)S(1)} %copy-done.16), channel_id=1, source_target_pairs={{0,6},{1,7},{2,4},{3,5},{4,2},{5,3},{6,0},{7,1},{8,14},{9,15},{10,... | collective-permute-start | bytes 393224 | tf_op jit(solution)/shard_map/ppermute | solution.py:286
  40.8 9.5 %collective-permute-done.9 = bf16[1,256,256]{2,1,0:T(8,128)(2,1)S(1)} collective-permute-done((bf16[1,256,256]{2,1,0:T(8,128)(2,1)}, bf16[1,256,256]{2,1,0:T(8,128)(2,1)S(1)}, u32[]{:S(2)}, u32[]{:S(2)}) %collective-permute-start.9) | collective-permute-done | bytes 131104 | tf_op jit(solution)/shard_map/ppermute | solution.py:286
  50.3 1.1 collective-permute-start.14
  51.5 3.4 %collective-permute-done.10 = bf16[1,256,256]{2,1,0:T(8,128)(2,1)S(1)} collective-permute-done((bf16[1,256,256]{2,1,0:T(8,128)(2,1)}, bf16[1,256,256]{2,1,0:T(8,128)(2,1)S(1)}, u32[]{:S(2)}, u32[]{:S(2)}) %collective-permute-start.10) | collective-permute-done | bytes 131104 | tf_op jit(solution)/shard_map/ppermute | solution.py:286
  54.8 0.7 collective-permute-start.2
  55.5 3.2 %collective-permute-done.11 = bf16[1,256,256]{2,1,0:T(8,128)(2,1)S(1)} collective-permute-done((bf16[1,256,256]{2,1,0:T(8,128)(2,1)}, bf16[1,256,256]{2,1,0:T(8,128)(2,1)S(1)}, u32[]{:S(2)}, u32[]{:S(2)}) %collective-permute-start.11) | collective-permute-done | bytes 131104 | tf_op jit(solution)/shard_map/ppermute | solution.py:286
  58.7 0.7 collective-permute-start.3
  59.3 0.1 slice_compare_fusion
  59.4 1.7 %collective-permute-done.12 = bf16[1,256,256]{2,1,0:T(8,128)(2,1)S(1)} collective-permute-done((bf16[1,256,256]{2,1,0:T(8,128)(2,1)}, bf16[1,256,256]{2,1,0:T(8,128)(2,1)S(1)}, u32[]{:S(2)}, u32[]{:S(2)}) %collective-permute-start.12) | collective-permute-done | bytes 131104 | tf_op jit(solution)/shard_map/ppermute | solution.py:286
  61.2 0.7 collective-permute-start.4
  61.9 0.7 collective-permute-start.5
  62.6 0.7 collective-permute-start.6
  63.2 0.7 collective-permute-start.7
  63.9 0.7 collective-permute-start.8
  64.7 7.5 %collective-permute-start.15 = (bf16[1,256,256]{2,1,0:T(8,128)(2,1)S(1)}, bf16[1,256,256]{2,1,0:T(8,128)(2,1)S(1)}, u32[]{:S(2)}, u32[]{:S(2)}) collective-permute-start(bf16[1,256,256]{2,1,0:T(8,128)(2,1)S(1)} %select_select_fusion), channel_id=1, source_target_pairs={{0,16},{1,17},{2,18},{3,19},{4,20},{5,21},{6,22},{7,23},{8,24},{9,... | collective-permute-start | bytes 393224 | tf_op jit(solution)/shard_map/ppermute | solution.py:302
  72.3 1.5 %collective-permute-start.16 = (bf16[1,256,256]{2,1,0:T(8,128)(2,1)S(1)}, bf16[1,256,256]{2,1,0:T(8,128)(2,1)S(1)}, u32[]{:S(2)}, u32[]{:S(2)}) collective-permute-start(bf16[1,256,256]{2,1,0:T(8,128)(2,1)S(1)} %select_select_fusion.1), channel_id=1, source_target_pairs={{16,0},{17,1},{18,2},{19,3},{20,4},{21,5},{22,6},{23,7},{24,8},{25... | collective-permute-start | bytes 393224 | tf_op jit(solution)/shard_map/ppermute | solution.py:304
  73.8 1.6 %copy-done.6 = f32[2,2048,128]{2,1,0:T(8,128)S(1)} copy-done((f32[2,2048,128]{2,1,0:T(8,128)S(1)}, f32[2,2048,128]{2,1,0:T(8,128)}, u32[]{:S(2)}) %copy-start.6) | copy-done | bytes 2097176
  75.4 8.0 %moved_keys.2.loaded_ref = f32[2,2048,128]{2,1,0:T(8,128)S(1)} custom-call(bf16[256,1024]{1,0:T(8,128)(2,1)S(1)} %copy-done.2, bf16[32,128,256]{2,1,0:T(8,128)(2,1)} %all-to-all-done.kv_ref, f32[2,2048,128]{2,1,0:T(8,128)S(1)} %copy-done.6), custom_call_target="tpu_custom_call" | custom-call | flops 6442450944 | bytes 1048576 | tf_op jit(solution)/shard_map/moved_keys/pallas_call | solution.py:424
  83.4 0.1 maximum_select_fusion.refs_0_
  83.5 0.1 collective-permute-start.19
  83.6 4.7 %collective-permute-start.18 = (bf16[2,256,256]{2,1,0:T(8,128)(2,1)S(1)}, bf16[2,256,256]{2,1,0:T(8,128)(2,1)S(1)}, u32[]{:S(2)}, u32[]{:S(2)}) collective-permute-start(bf16[2,256,256]{2,1,0:T(8,128)(2,1)S(1)} %maximum_select_fusion.refs_0_), channel_id=1, source_target_pairs={{0,4},{1,5},{2,6},{3,7},{4,0},{5,1},{6,2},{7,3},{8,12},{9,13},{10,... | collective-permute-start | bytes 786440 | tf_op jit(solution)/shard_map/ppermute | solution.py:327
  88.3 0.2 collective-permute-start.17
  88.5 8.0 %moved_keys.3.refs_5_ = f32[2,2048,128]{2,1,0:T(8,128)S(1)} custom-call(bf16[256,1024]{1,0:T(8,128)(2,1)S(1)} %copy-done.2, bf16[32,128,256]{2,1,0:T(8,128)(2,1)} %all-to-all-done.kv_ref, f32[2,2048,128]{2,1,0:T(8,128)S(1)} %moved_keys.2.loaded_ref), custom_call_target="tpu_custom_call" | custom-call | flops 6442450944 | bytes 1048576 | tf_op jit(solution)/shard_map/moved_keys/pallas_call | solution.py:424
  96.6 0.6 pick_other.3
  97.3 1.9 %collective-permute-start.21 = (bf16[2,256,256]{2,1,0:T(8,128)(2,1)S(1)}, bf16[2,256,256]{2,1,0:T(8,128)(2,1)S(1)}, u32[]{:S(2)}, u32[]{:S(2)}) collective-permute-start(bf16[2,256,256]{2,1,0:T(8,128)(2,1)S(1)} %collective-permute-done.19.refs_3_), channel_id=1, source_target_pairs={{0,2},{1,3},{2,0},{3,1},{4,6},{5,7},{6,4},{7,5},{8,10},{9,11},{10,... | collective-permute-start | bytes 786440 | tf_op jit(solution)/shard_map/ppermute | solution.py:327
  99.2 1.9 %collective-permute-start.22 = (bf16[2,256,256]{2,1,0:T(8,128)(2,1)S(1)}, bf16[2,256,256]{2,1,0:T(8,128)(2,1)S(1)}, u32[]{:S(2)}, u32[]{:S(2)}) collective-permute-start(bf16[2,256,256]{2,1,0:T(8,128)(2,1)S(1)} %collective-permute-done.18.refs_2_), channel_id=1, source_target_pairs={{0,8},{1,9},{2,10},{3,11},{4,12},{5,13},{6,14},{7,15},{8,0},{9,1},... | collective-permute-start | bytes 786440 | tf_op jit(solution)/shard_map/ppermute | solution.py:327
  101.2 7.3 %prefix_keys.3.refs_4_ = f32[2,2048,128]{2,1,0:T(8,128)S(1)} custom-call(s32[2]{0:T(128)S(1)} %bitcast.18, bf16[256,1024]{1,0:T(8,128)(2,1)S(1)} %copy-done.2, bf16[2,256,256]{2,1,0:T(8,128)(2,1)S(1)} %maximum_select_fusion.refs_0_, bf16[2,256,256]{2,1,0:T(8,128)(2,1)S(1)} %collective-permute-done.17.refs_1_, ...), custom_call_target="tpu_custom_call" | custom-call | flops 6442450944 | bytes 1048576 | tf_op jit(solution)/shard_map/prefix_keys/pallas_call | solution.py:448
  108.5 0.6 pick_other.4
  109.2 0.1 collective-permute-start.24
  109.4 1.6 %collective-permute-done.25.refs_3_ = bf16[768,256]{1,0:T(8,128)(2,1)S(1)} collective-permute-done((bf16[768,256]{1,0:T(8,128)(2,1)S(1)}, bf16[768,256]{1,0:T(8,128)(2,1)S(1)}, u32[]{:S(2)}, u32[]{:S(2)}) %collective-permute-start.25) | collective-permute-done | bytes 393248 | tf_op jit(solution)/shard_map/ppermute | solution.py:317
  110.9 5.1 %prefix_keys.4.refs_2_ = f32[2,2048,128]{2,1,0:T(8,128)S(1)} custom-call(s32[2]{0:T(128)S(1)} %bitcast.20, bf16[256,1024]{1,0:T(8,128)(2,1)S(1)} %copy-done.2, bf16[2,256,256]{2,1,0:T(8,128)(2,1)S(1)} %collective-permute-done.20.refs_0_, bf16[2,256,256]{2,1,0:T(8,128)(2,1)S(1)} %collective-permute-done.21.refs_1_, ...), custom_call_target="tpu_custom_call" | custom-call | flops 4831838208 | bytes 786432 | tf_op jit(solution)/shard_map/prefix_keys/pallas_call | solution.py:448
  116.1 1.9 %collective-permute-done.24.refs_0_ = bf16[2,256,256]{2,1,0:T(8,128)(2,1)S(1)} collective-permute-done((bf16[2,256,256]{2,1,0:T(8,128)(2,1)S(1)}, bf16[2,256,256]{2,1,0:T(8,128)(2,1)S(1)}, u32[]{:S(2)}, u32[]{:S(2)}) %collective-permute-start.24) | collective-permute-done | bytes 262176 | tf_op jit(solution)/shard_map/ppermute | solution.py:327
  117.9 0.6 pick_other.5
  118.6 1.3 %collective-permute-done.26.refs_1_ = bf16[256,256]{1,0:T(8,128)(2,1)S(1)} collective-permute-done((bf16[256,256]{1,0:T(8,128)(2,1)S(1)}, bf16[256,256]{1,0:T(8,128)(2,1)S(1)}, u32[]{:S(2)}, u32[]{:S(2)}) %collective-permute-start.26) | collective-permute-done | bytes 131104 | tf_op jit(solution)/shard_map/ppermute | solution.py:317
  119.9 3.5 %prefix_keys.5 = bf16[256,1024]{1,0:T(8,128)(2,1)} custom-call(s32[2]{0:T(128)S(1)} %bitcast.22, bf16[256,1024]{1,0:T(8,128)(2,1)S(1)} %copy-done.2, bf16[2,256,256]{2,1,0:T(8,128)(2,1)S(1)} %collective-permute-done.24.refs_0_, bf16[256,256]{1,0:T(8,128)(2,1)S(1)} %collective-permute-done.26.refs_1_, f32[2,2048,128]{2,1,0:T(8,128)S(1)} %prefix_keys.4.refs_2_), custom_call_target="tpu_custom_call" | custom-call | flops 1610612736 | bytes 262144 | tf_op jit(solution)/shard_map/prefix_keys/pallas_call | solution.py:448
  (58 shorter events, 0.6 us)
Async XLA Ops:
  0.0 4.6 %collective-permute-start = (bf16[4096,256]{1,0:T(8,128)(2,1)}, bf16[4096,256]{1,0:T(8,128)(2,1)}, u32[]{:S(2)}, u32[]{:S(2)}) collective-permute-start(bf16[4096,256]{1,0:T(8,128)(2,1)} %param.15), channel_id=1, source_target_pairs={{0,1},{1,0},{2,3},{3,2},{4,5},{5,4},{6,7},{7,6},{8,9},{9,8},{10,11... | collective-permute-start | bytes 6291464 | tf_op jit(solution)/shard_map/ppermute | solution.py:317
  4.6 69.2 %all-to-all-start = ((bf16[32,128,256]{2,1,0:T(8,128)(2,1)}), bf16[32,128,256]{2,1,0:T(8,128)(2,1)}, u32[]{:S(2)}, u32[]{:S(2)}) async-start(bf16[32,128,256]{2,1,0:T(8,128)(2,1)} %pack_moved.1), calls=%async_computation | async-start | bytes 4194304 | tf_op jit(solution)/shard_map/all_to_all | solution.py:262
  12.6 21.2 %copy-start.2 = (bf16[256,1024]{1,0:T(8,128)(2,1)S(1)}, bf16[256,1024]{1,0:T(8,128)(2,1)}, u32[]{:S(2)}) copy-start(bf16[256,1024]{1,0:T(8,128)(2,1)} %q_ref.11) | copy-start | bytes 1572868
  12.6 21.2 %copy-start.3 = (bf16[512,256]{1,0:T(8,128)(2,1)S(1)}, bf16[512,256]{1,0:T(8,128)(2,1)}, u32[]{:S(2)}) copy-start(bf16[512,256]{1,0:T(8,128)(2,1)} %own_ref.1) | copy-start | bytes 786436
  12.6 21.2 %copy-start.4 = (bf16[256,256]{1,0:T(8,128)(2,1)S(1)}, bf16[256,256]{1,0:T(8,128)(2,1)}, u32[]{:S(2)}) copy-start(bf16[256,256]{1,0:T(8,128)(2,1)} %suffix_ref.1) | copy-start | bytes 393220
  26.1 12.6 %collective-permute-start.1 = (bf16[1,256,256]{2,1,0:T(8,128)(2,1)}, bf16[1,256,256]{2,1,0:T(8,128)(2,1)S(1)}, u32[]{:S(2)}, u32[]{:S(2)}) collective-permute-start(bf16[1,256,256]{2,1,0:T(8,128)(2,1)} %get-tuple-element.49), channel_id=1, source_target_pairs={{0,2},{1,3},{2,0},{3,1},{4,6},{5,7},{6,4},{7,5},{8,10},{9,11},{10,... | collective-permute-start | bytes 393224 | tf_op jit(solution)/shard_map/ppermute | solution.py:286
  27.9 22.4 %collective-permute-start.9 = (bf16[1,256,256]{2,1,0:T(8,128)(2,1)}, bf16[1,256,256]{2,1,0:T(8,128)(2,1)S(1)}, u32[]{:S(2)}, u32[]{:S(2)}) collective-permute-start(bf16[1,256,256]{2,1,0:T(8,128)(2,1)} %get-tuple-element.67), channel_id=1, source_target_pairs={{0,14},{1,15},{2,12},{3,13},{4,10},{5,11},{6,8},{7,9},{8,6},{9,7},... | collective-permute-start | bytes 393224 | tf_op jit(solution)/shard_map/ppermute | solution.py:286
  30.3 24.5 %collective-permute-start.10 = (bf16[1,256,256]{2,1,0:T(8,128)(2,1)}, bf16[1,256,256]{2,1,0:T(8,128)(2,1)S(1)}, u32[]{:S(2)}, u32[]{:S(2)}) collective-permute-start(bf16[1,256,256]{2,1,0:T(8,128)(2,1)} %get-tuple-element.68), channel_id=1, source_target_pairs={{0,12},{1,13},{2,14},{3,15},{4,8},{5,9},{6,10},{7,11},{8,4},{9,5},... | collective-permute-start | bytes 393224 | tf_op jit(solution)/shard_map/ppermute | solution.py:286
  30.6 28.1 %collective-permute-start.11 = (bf16[1,256,256]{2,1,0:T(8,128)(2,1)}, bf16[1,256,256]{2,1,0:T(8,128)(2,1)S(1)}, u32[]{:S(2)}, u32[]{:S(2)}) collective-permute-start(bf16[1,256,256]{2,1,0:T(8,128)(2,1)} %get-tuple-element.69), channel_id=1, source_target_pairs={{0,10},{1,11},{2,8},{3,9},{4,14},{5,15},{6,12},{7,13},{8,2},{9,3},... | collective-permute-start | bytes 393224 | tf_op jit(solution)/shard_map/ppermute | solution.py:286
  33.2 28.0 %collective-permute-start.12 = (bf16[1,256,256]{2,1,0:T(8,128)(2,1)}, bf16[1,256,256]{2,1,0:T(8,128)(2,1)S(1)}, u32[]{:S(2)}, u32[]{:S(2)}) collective-permute-start(bf16[1,256,256]{2,1,0:T(8,128)(2,1)} %get-tuple-element.70), channel_id=1, source_target_pairs={{0,8},{1,9},{2,10},{3,11},{4,12},{5,13},{6,14},{7,15},{8,0},{9,1},... | collective-permute-start | bytes 393224 | tf_op jit(solution)/shard_map/ppermute | solution.py:286
  33.8 0.9 copy-start
  34.7 4.1 %copy-start.16 = (bf16[1,256,256]{2,1,0:T(8,128)(2,1)S(1)}, bf16[1,256,256]{2,1,0:T(8,128)(2,1)}, u32[]{:S(2)}) copy-start(bf16[1,256,256]{2,1,0:T(8,128)(2,1)} %get-tuple-element.71) | copy-start | bytes 393220
  34.7 15.7 %copy-start.15 = (bf16[1,256,256]{2,1,0:T(8,128)(2,1)S(1)}, bf16[1,256,256]{2,1,0:T(8,128)(2,1)}, u32[]{:S(2)}) copy-start(bf16[1,256,256]{2,1,0:T(8,128)(2,1)} %get-tuple-element.72) | copy-start | bytes 393220
  34.7 20.1 %copy-start.14 = (bf16[1,256,256]{2,1,0:T(8,128)(2,1)S(1)}, bf16[1,256,256]{2,1,0:T(8,128)(2,1)}, u32[]{:S(2)}) copy-start(bf16[1,256,256]{2,1,0:T(8,128)(2,1)} %get-tuple-element.59) | copy-start | bytes 393220
  34.7 24.0 %copy-start.13 = (bf16[1,256,256]{2,1,0:T(8,128)(2,1)S(1)}, bf16[1,256,256]{2,1,0:T(8,128)(2,1)}, u32[]{:S(2)}) copy-start(bf16[1,256,256]{2,1,0:T(8,128)(2,1)} %get-tuple-element.60) | copy-start | bytes 393220
  34.7 24.6 %copy-start.1 = (s32[6]{0:T(128)S(1)}, s32[6]{0:T(128)}, u32[]{:S(2)}) copy-start(s32[6]{0:T(128)} %get-tuple-element.48) | copy-start | bytes 76
  34.7 26.5 %copy-start.12 = (bf16[1,256,256]{2,1,0:T(8,128)(2,1)S(1)}, bf16[1,256,256]{2,1,0:T(8,128)(2,1)}, u32[]{:S(2)}) copy-start(bf16[1,256,256]{2,1,0:T(8,128)(2,1)} %get-tuple-element.61) | copy-start | bytes 393220
  34.7 27.1 %copy-start.11 = (bf16[1,256,256]{2,1,0:T(8,128)(2,1)S(1)}, bf16[1,256,256]{2,1,0:T(8,128)(2,1)}, u32[]{:S(2)}) copy-start(bf16[1,256,256]{2,1,0:T(8,128)(2,1)} %get-tuple-element.62) | copy-start | bytes 393220
  34.7 27.8 %copy-start.10 = (bf16[1,256,256]{2,1,0:T(8,128)(2,1)S(1)}, bf16[1,256,256]{2,1,0:T(8,128)(2,1)}, u32[]{:S(2)}) copy-start(bf16[1,256,256]{2,1,0:T(8,128)(2,1)} %get-tuple-element.63) | copy-start | bytes 393220
  34.7 28.5 %copy-start.9 = (bf16[1,256,256]{2,1,0:T(8,128)(2,1)S(1)}, bf16[1,256,256]{2,1,0:T(8,128)(2,1)}, u32[]{:S(2)}) copy-start(bf16[1,256,256]{2,1,0:T(8,128)(2,1)} %get-tuple-element.64) | copy-start | bytes 393220
  34.7 29.2 %copy-start.8 = (bf16[1,256,256]{2,1,0:T(8,128)(2,1)S(1)}, bf16[1,256,256]{2,1,0:T(8,128)(2,1)}, u32[]{:S(2)}) copy-start(bf16[1,256,256]{2,1,0:T(8,128)(2,1)} %get-tuple-element.65) | copy-start | bytes 393220
  34.7 37.5 %copy-start.7 = (bf16[1,256,256]{2,1,0:T(8,128)(2,1)S(1)}, bf16[1,256,256]{2,1,0:T(8,128)(2,1)}, u32[]{:S(2)}) copy-start(bf16[1,256,256]{2,1,0:T(8,128)(2,1)} %get-tuple-element.66) | copy-start | bytes 393220
  37.4 1.4 %copy-start.5 = (f32[2,2048,128]{2,1,0:T(8,128)}, f32[2,2048,128]{2,1,0:T(8,128)S(1)}, u32[]{:S(2)}) copy-start(f32[2,2048,128]{2,1,0:T(8,128)S(1)} %local_keys.1.loaded_ref) | copy-start | bytes 6291460
  38.7 23.1 %collective-permute-start.13 = (bf16[1,256,256]{2,1,0:T(8,128)(2,1)S(1)}, bf16[1,256,256]{2,1,0:T(8,128)(2,1)S(1)}, u32[]{:S(2)}, u32[]{:S(2)}) collective-permute-start(bf16[1,256,256]{2,1,0:T(8,128)(2,1)S(1)} %copy-done.16), channel_id=1, source_target_pairs={{0,6},{1,7},{2,4},{3,5},{4,2},{5,3},{6,0},{7,1},{8,14},{9,15},{10,... | collective-permute-start | bytes 393224 | tf_op jit(solution)/shard_map/ppermute | solution.py:286
  50.3 12.2 %collective-permute-start.14 = (bf16[1,256,256]{2,1,0:T(8,128)(2,1)S(1)}, bf16[1,256,256]{2,1,0:T(8,128)(2,1)S(1)}, u32[]{:S(2)}, u32[]{:S(2)}) collective-permute-start(bf16[1,256,256]{2,1,0:T(8,128)(2,1)S(1)} %copy-done.15), channel_id=1, source_target_pairs={{0,4},{1,5},{2,6},{3,7},{4,0},{5,1},{6,2},{7,3},{8,12},{9,13},{10,... | collective-permute-start | bytes 393224 | tf_op jit(solution)/shard_map/ppermute | solution.py:286
  54.8 8.4 %collective-permute-start.2 = (bf16[1,256,256]{2,1,0:T(8,128)(2,1)S(1)}, bf16[1,256,256]{2,1,0:T(8,128)(2,1)S(1)}, u32[]{:S(2)}, u32[]{:S(2)}) collective-permute-start(bf16[1,256,256]{2,1,0:T(8,128)(2,1)S(1)} %copy-done.14), channel_id=1, source_target_pairs={{30,16},{31,17}} | collective-permute-start | bytes 393224 | tf_op jit(solution)/shard_map/ppermute | solution.py:286
  58.7 5.3 %collective-permute-start.3 = (bf16[1,256,256]{2,1,0:T(8,128)(2,1)S(1)}, bf16[1,256,256]{2,1,0:T(8,128)(2,1)S(1)}, u32[]{:S(2)}, u32[]{:S(2)}) collective-permute-start(bf16[1,256,256]{2,1,0:T(8,128)(2,1)S(1)} %copy-done.13), channel_id=1, source_target_pairs={{30,18},{31,19}} | collective-permute-start | bytes 393224 | tf_op jit(solution)/shard_map/ppermute | solution.py:286
  61.2 3.5 %collective-permute-start.4 = (bf16[1,256,256]{2,1,0:T(8,128)(2,1)S(1)}, bf16[1,256,256]{2,1,0:T(8,128)(2,1)S(1)}, u32[]{:S(2)}, u32[]{:S(2)}) collective-permute-start(bf16[1,256,256]{2,1,0:T(8,128)(2,1)S(1)} %copy-done.12), channel_id=1, source_target_pairs={{30,20},{31,21}} | collective-permute-start | bytes 393224 | tf_op jit(solution)/shard_map/ppermute | solution.py:286
  61.9 10.4 %collective-permute-start.5 = (bf16[1,256,256]{2,1,0:T(8,128)(2,1)S(1)}, bf16[1,256,256]{2,1,0:T(8,128)(2,1)S(1)}, u32[]{:S(2)}, u32[]{:S(2)}) collective-permute-start(bf16[1,256,256]{2,1,0:T(8,128)(2,1)S(1)} %copy-done.11), channel_id=1, source_target_pairs={{30,22},{31,23}} | collective-permute-start | bytes 393224 | tf_op jit(solution)/shard_map/ppermute | solution.py:286
  62.6 9.7 %collective-permute-start.6 = (bf16[1,256,256]{2,1,0:T(8,128)(2,1)S(1)}, bf16[1,256,256]{2,1,0:T(8,128)(2,1)S(1)}, u32[]{:S(2)}, u32[]{:S(2)}) collective-permute-start(bf16[1,256,256]{2,1,0:T(8,128)(2,1)S(1)} %copy-done.10), channel_id=1, source_target_pairs={{30,24},{31,25}} | collective-permute-start | bytes 393224 | tf_op jit(solution)/shard_map/ppermute | solution.py:286
  63.2 9.0 %collective-permute-start.7 = (bf16[1,256,256]{2,1,0:T(8,128)(2,1)S(1)}, bf16[1,256,256]{2,1,0:T(8,128)(2,1)S(1)}, u32[]{:S(2)}, u32[]{:S(2)}) collective-permute-start(bf16[1,256,256]{2,1,0:T(8,128)(2,1)S(1)} %copy-done.9), channel_id=1, source_target_pairs={{30,26},{31,27}} | collective-permute-start | bytes 393224 | tf_op jit(solution)/shard_map/ppermute | solution.py:286
  63.9 8.3 %collective-permute-start.8 = (bf16[1,256,256]{2,1,0:T(8,128)(2,1)S(1)}, bf16[1,256,256]{2,1,0:T(8,128)(2,1)S(1)}, u32[]{:S(2)}, u32[]{:S(2)}) collective-permute-start(bf16[1,256,256]{2,1,0:T(8,128)(2,1)S(1)} %copy-done.8), channel_id=1, source_target_pairs={{30,28},{31,29}} | collective-permute-start | bytes 393224 | tf_op jit(solution)/shard_map/ppermute | solution.py:286
  64.7 18.7 %collective-permute-start.15 = (bf16[1,256,256]{2,1,0:T(8,128)(2,1)S(1)}, bf16[1,256,256]{2,1,0:T(8,128)(2,1)S(1)}, u32[]{:S(2)}, u32[]{:S(2)}) collective-permute-start(bf16[1,256,256]{2,1,0:T(8,128)(2,1)S(1)} %select_select_fusion), channel_id=1, source_target_pairs={{0,16},{1,17},{2,18},{3,19},{4,20},{5,21},{6,22},{7,23},{8,24},{9,... | collective-permute-start | bytes 393224 | tf_op jit(solution)/shard_map/ppermute | solution.py:302
  72.3 11.1 %collective-permute-start.16 = (bf16[1,256,256]{2,1,0:T(8,128)(2,1)S(1)}, bf16[1,256,256]{2,1,0:T(8,128)(2,1)S(1)}, u32[]{:S(2)}, u32[]{:S(2)}) collective-permute-start(bf16[1,256,256]{2,1,0:T(8,128)(2,1)S(1)} %select_select_fusion.1), channel_id=1, source_target_pairs={{16,0},{17,1},{18,2},{19,3},{20,4},{21,5},{22,6},{23,7},{24,8},{25... | collective-permute-start | bytes 393224 | tf_op jit(solution)/shard_map/ppermute | solution.py:304
  73.8 1.6 %copy-start.6 = (f32[2,2048,128]{2,1,0:T(8,128)S(1)}, f32[2,2048,128]{2,1,0:T(8,128)}, u32[]{:S(2)}) copy-start(f32[2,2048,128]{2,1,0:T(8,128)} %copy-done.5) | copy-start | bytes 6291460
  83.5 13.0 %collective-permute-start.19 = (bf16[2,256,256]{2,1,0:T(8,128)(2,1)S(1)}, bf16[2,256,256]{2,1,0:T(8,128)(2,1)S(1)}, u32[]{:S(2)}, u32[]{:S(2)}) collective-permute-start(bf16[2,256,256]{2,1,0:T(8,128)(2,1)S(1)} %maximum_select_fusion.refs_0_), channel_id=1, source_target_pairs={{0,8},{1,9},{2,10},{3,11},{4,12},{5,13},{6,14},{7,15},{8,0},{9,1},... | collective-permute-start | bytes 786440 | tf_op jit(solution)/shard_map/ppermute | solution.py:327
  83.6 12.9 %collective-permute-start.18 = (bf16[2,256,256]{2,1,0:T(8,128)(2,1)S(1)}, bf16[2,256,256]{2,1,0:T(8,128)(2,1)S(1)}, u32[]{:S(2)}, u32[]{:S(2)}) collective-permute-start(bf16[2,256,256]{2,1,0:T(8,128)(2,1)S(1)} %maximum_select_fusion.refs_0_), channel_id=1, source_target_pairs={{0,4},{1,5},{2,6},{3,7},{4,0},{5,1},{6,2},{7,3},{8,12},{9,13},{10,... | collective-permute-start | bytes 786440 | tf_op jit(solution)/shard_map/ppermute | solution.py:327
  88.3 8.2 %collective-permute-start.17 = (bf16[2,256,256]{2,1,0:T(8,128)(2,1)S(1)}, bf16[2,256,256]{2,1,0:T(8,128)(2,1)S(1)}, u32[]{:S(2)}, u32[]{:S(2)}) collective-permute-start(bf16[2,256,256]{2,1,0:T(8,128)(2,1)S(1)} %maximum_select_fusion.refs_0_), channel_id=1, source_target_pairs={{0,2},{1,3},{2,0},{3,1},{4,6},{5,7},{6,4},{7,5},{8,10},{9,11},{10,... | collective-permute-start | bytes 786440 | tf_op jit(solution)/shard_map/ppermute | solution.py:327
  97.2 4.0 %collective-permute-start.23 = (bf16[1024,256]{1,0:T(8,128)(2,1)S(1)}, bf16[1024,256]{1,0:T(8,128)(2,1)S(1)}, u32[]{:S(2)}, u32[]{:S(2)}) collective-permute-start(bf16[1024,256]{1,0:T(8,128)(2,1)S(1)} %pick_other.3), channel_id=1, source_target_pairs={{0,1},{1,0},{2,3},{3,2},{4,5},{5,4},{6,7},{7,6},{8,9},{9,8},{10,11... | collective-permute-start | bytes 1572872 | tf_op jit(solution)/shard_map/ppermute | solution.py:317
  97.2 11.3 %collective-permute-start.20 = (bf16[2,256,256]{2,1,0:T(8,128)(2,1)S(1)}, bf16[2,256,256]{2,1,0:T(8,128)(2,1)S(1)}, u32[]{:S(2)}, u32[]{:S(2)}) collective-permute-start(bf16[2,256,256]{2,1,0:T(8,128)(2,1)S(1)} %collective-permute-done.17.refs_1_), channel_id=1, source_target_pairs={{0,4},{1,5},{2,6},{3,7},{4,0},{5,1},{6,2},{7,3},{8,12},{9,13},{10,... | collective-permute-start | bytes 786440 | tf_op jit(solution)/shard_map/ppermute | solution.py:327
  97.3 11.2 %collective-permute-start.21 = (bf16[2,256,256]{2,1,0:T(8,128)(2,1)S(1)}, bf16[2,256,256]{2,1,0:T(8,128)(2,1)S(1)}, u32[]{:S(2)}, u32[]{:S(2)}) collective-permute-start(bf16[2,256,256]{2,1,0:T(8,128)(2,1)S(1)} %collective-permute-done.19.refs_3_), channel_id=1, source_target_pairs={{0,2},{1,3},{2,0},{3,1},{4,6},{5,7},{6,4},{7,5},{8,10},{9,11},{10,... | collective-permute-start | bytes 786440 | tf_op jit(solution)/shard_map/ppermute | solution.py:327
  99.2 9.3 %collective-permute-start.22 = (bf16[2,256,256]{2,1,0:T(8,128)(2,1)S(1)}, bf16[2,256,256]{2,1,0:T(8,128)(2,1)S(1)}, u32[]{:S(2)}, u32[]{:S(2)}) collective-permute-start(bf16[2,256,256]{2,1,0:T(8,128)(2,1)S(1)} %collective-permute-done.18.refs_2_), channel_id=1, source_target_pairs={{0,8},{1,9},{2,10},{3,11},{4,12},{5,13},{6,14},{7,15},{8,0},{9,1},... | collective-permute-start | bytes 786440 | tf_op jit(solution)/shard_map/ppermute | solution.py:327
  109.1 1.8 %collective-permute-start.25 = (bf16[768,256]{1,0:T(8,128)(2,1)S(1)}, bf16[768,256]{1,0:T(8,128)(2,1)S(1)}, u32[]{:S(2)}, u32[]{:S(2)}) collective-permute-start(bf16[768,256]{1,0:T(8,128)(2,1)S(1)} %pick_other.4), channel_id=1, source_target_pairs={{0,1},{1,0},{2,3},{3,2},{4,5},{5,4},{6,7},{7,6},{8,9},{9,8},{10,11... | collective-permute-start | bytes 1179656 | tf_op jit(solution)/shard_map/ppermute | solution.py:317
  109.2 8.7 %collective-permute-start.24 = (bf16[2,256,256]{2,1,0:T(8,128)(2,1)S(1)}, bf16[2,256,256]{2,1,0:T(8,128)(2,1)S(1)}, u32[]{:S(2)}, u32[]{:S(2)}) collective-permute-start(bf16[2,256,256]{2,1,0:T(8,128)(2,1)S(1)} %collective-permute-done.22.refs_2_), channel_id=1, source_target_pairs={{0,2},{1,3},{2,0},{3,1},{4,6},{5,7},{6,4},{7,5},{8,10},{9,11},{10,... | collective-permute-start | bytes 786440 | tf_op jit(solution)/shard_map/ppermute | solution.py:327
  118.5 1.4 %collective-permute-start.26 = (bf16[256,256]{1,0:T(8,128)(2,1)S(1)}, bf16[256,256]{1,0:T(8,128)(2,1)S(1)}, u32[]{:S(2)}, u32[]{:S(2)}) collective-permute-start(bf16[256,256]{1,0:T(8,128)(2,1)S(1)} %pick_other.5), channel_id=1, source_target_pairs={{0,1},{1,0},{2,3},{3,2},{4,5},{5,4},{6,7},{7,6},{8,9},{9,8},{10,11... | collective-permute-start | bytes 393224 | tf_op jit(solution)/shard_map/ppermute | solution.py:317

commit v17 on v16

--- a/solution.py
+++ b/solution.py
@@ -12,7 +12,7 @@
 DEAD_ABOVE = 512.0
 NEG = -1e30
 CHUNK = 1024
-ROWS = 512
+ROWS = 256
 PARAMS = pltpu.CompilerParams(vmem_limit_bytes=44 * 1024 * 1024)
 COPY_PARAMS = pltpu.CompilerParams(vmem_limit_bytes=62 * 1024 * 1024)
 
@@ -148,6 +148,11 @@
             save_state(*work[1:], out_ref)
 
 
+def start_all(copies):
+    for copy in copies:
+        copy.start()
+
+
 def wait_all(copies):
     for copy in copies:
         copy.wait()
@@ -159,8 +164,8 @@
         out_ref[pl.ds(place * piece.shape[0], piece.shape[0]), :] = piece[...]
 
 
-def pack_kernel(target_ref, block_ref, count_ref, pool_ref, out_ref, held_ref, mark_ref, *sems):
-    in_sems, out_sems = sems
+def pack_kernel(target_ref, block_ref, count_ref, pool_ref, *refs):
+    parts, (held_ref, mark_ref, in_sems, out_sems) = refs[:-4], refs[-4:]
     entries = target_ref.shape[1]
     mark_ref[...] = jnp.full(mark_ref.shape, DEAD_MARK, mark_ref.dtype)
 
@@ -169,30 +174,53 @@
             pool_ref.at[block_ref[0, entry]], held_ref.at[entry], in_sems.at[entry]
         )
 
-    def store(entry, source):
-        return pltpu.make_async_copy(
-            source, out_ref.at[target_ref[0, entry]], out_sems.at[entry]
-        )
+    def stores(entry, source):
+        rows = parts[0].shape[1]
+        return [
+            pltpu.make_async_copy(
+                source.at[pl.ds(place * rows, rows)],
+                part.at[target_ref[0, entry]],
+                out_sems.at[place, entry],
+            )
+            for place, part in enumerate(parts)
+        ]
 
     @pl.loop(0, entries)
     def _(entry):
         live = entry < count_ref[0]
         pl.when(live)(lambda: load(entry).start())
-        pl.when(jnp.logical_not(live))(lambda: store(entry, mark_ref).start())
+        pl.when(jnp.logical_not(live))(lambda: start_all(stores(entry, mark_ref)))
 
     @pl.loop(0, entries)
     def _(entry):
         @pl.when(entry < count_ref[0])
         def _():
             load(entry).wait()
-            store(entry, held_ref.at[entry]).start()
+            start_all(stores(entry, held_ref.at[entry]))
 
     @pl.loop(0, entries)
     def _(entry):
-        store(entry, mark_ref).wait()
-
-
-def stage_kernel(owner_ref, reader_ref, kept_ref, swapped_ref, info_ref, *refs):
+        wait_all(stores(entry, mark_ref))
+
+
+def gate_kernel(*refs):
+    pass
+
+
+def gate(rows, *after):
+    return pl.pallas_call(
+        gate_kernel,
+        out_shape=jax.ShapeDtypeStruct(rows.shape, rows.dtype),
+        in_specs=[IN_HBM] * (1 + len(after)),
+        out_specs=IN_HBM,
+        input_output_aliases={0: 0},
+        compiler_params=PARAMS,
+        name="gate",
+    )(rows, *after)
+
+
+def stage_kernel(owner_ref, reader_ref, kept_ref, swapped_ref, *refs):
+    mine_ref, other_ref, known_away_ref, away_ref, same_ref, *refs = refs
     outs, (sought_ref, known_ref, in_sems, out_sems) = refs[:-4], refs[-4:]
     chips, sought = sought_ref.shape[:2]
     replicas = 4 * chips
@@ -227,13 +255,15 @@
         for step in range(chips):
             start(step, sought, core == 1)
 
-    for place, wanted in enumerate((reader_ref[me], reader_ref[me ^ 1])):
+    for place_ref, wanted in ((mine_ref, reader_ref[me]), (other_ref, reader_ref[me ^ 1])):
         ahead = jnp.where(wanted < known, wanted + 1, wanted)
-        info_ref[place] = jnp.where(wanted == known, 0, ahead)
+        place_ref[0] = jnp.where(wanted == known, 0, ahead)
+    known_away_ref[0] = chip ^ (chips - 1)
     for place, owner in enumerate([replicas - 1, *owners]):
-        info_ref[2 + place] = chip ^ (owner // 2 % chips)
+        if place:
+            away_ref[place - 1] = chip ^ (owner // 2 % chips)
         same = owner // (replicas // 2) == me // (replicas // 2)
-        info_ref[3 + sought + place] = jnp.where(same, 1, 0)
+        same_ref[place] = jnp.where(same, 1, 0)
 
     for step in range(chips):
         for prefix in range(sought):
@@ -258,18 +288,19 @@
     prefixes = owners.shape[0]
 
     split = prefix_cache.reshape(2, chips, -1, width)
-    swapped, outgoing = lax.optimization_barrier((swap_cores(prefix_cache), outgoing))
-    arrived = lax.all_to_all(outgoing, "replica", split_axis=0, concat_axis=0, tiled=True)
+    swapped, *outgoing = lax.optimization_barrier((swap_cores(prefix_cache), *outgoing))
+    arrived = send_blocks(outgoing[0])
     swapped = swapped.reshape(split.shape)
     pieces = jax.ShapeDtypeStruct((owners.shape[0] - 1, *split.shape[2:]), split.dtype)
     piece = jax.ShapeDtypeStruct((1, *split.shape[2:]), split.dtype)
-    info, *staged = pl.pallas_call(
+    small = (1, 1, 1, prefixes - 1, prefixes)
+    mine, other, known_away, away, same_half, *staged = pl.pallas_call(
         stage_kernel,
-        out_shape=(jax.ShapeDtypeStruct((2 + 2 * prefixes,), jnp.int32),)
+        out_shape=tuple(jax.ShapeDtypeStruct((count,), jnp.int32) for count in small)
         + (pieces,) * chips
         + (piece,) * chips,
         in_specs=[IN_SMEM] * 2 + [IN_HBM] * 2,
-        out_specs=(IN_SMEM,) + (IN_HBM,) * (2 * chips),
+        out_specs=(IN_SMEM,) * len(small) + (IN_HBM,) * (2 * chips),
         scratch_shapes=[
             pltpu.VMEM((chips, *pieces.shape), split.dtype),
             pltpu.VMEM((chips, *piece.shape), split.dtype),
@@ -279,7 +310,6 @@
         compiler_params=COPY_PARAMS,
         name="stage_prefix",
     )(owners, readers, split, swapped)
-    place, away, same_half = info[:2], info[2:2 + prefixes], info[2 + prefixes:] == 1
 
     def to_peers(staged, senders):
         return [
@@ -298,19 +328,24 @@
         (passed[0], fold_local(staged[0]), *staged[chips:])
     )
     passed_known = to_peers(known_staged, (replicas - 2, replicas - 1))
-    found = choose(staged[0], passed, away[1:])
+    found = choose(staged[0], passed, away)
     passed = lax.ppermute(found, "replica", [(i, (i + half) % replicas) for i in range(replicas)])
-    found_known = choose(known_staged[0], passed_known, away[:1])
+    found_known = choose(known_staged[0], passed_known, known_away)
     passed_known = lax.ppermute(found_known, "replica", [(i + half, i) for i in range(half)])
+    later = send_blocks(gate(outgoing[1], passed, passed_known))
     passed, passed_known, state_now = lax.optimization_barrier(
-        (passed, passed_known, fold_moved(arrived, local, 0))
+        (passed, passed_known, fold_moved(arrived, local))
     )
     held = jnp.where(
-        same_half[:, None, None],
+        (same_half == 1)[:, None, None],
         jnp.concatenate([found_known, found]),
         jnp.concatenate([passed_known, passed]),
     )
-    return held, place, state_now, arrived
+    return held, mine, other, state_now, later
+
+
+def send_blocks(rows):
+    return lax.all_to_all(rows, "replica", split_axis=0, concat_axis=0, tiled=True)
 
 
 def swap_cores(rows):
@@ -329,7 +364,7 @@
 
 def from_other(pieces, place):
     rows, width = pieces[0].shape[1:]
-    spec = pl.BlockSpec((None, rows, width), lambda i, which: (which[1], 0, 0))
+    spec = pl.BlockSpec((None, rows, width), lambda i, which: (which[0], 0, 0))
     picked = pl.pallas_call(
         pick_kernel,
         out_shape=jax.ShapeDtypeStruct((len(pieces) * rows, width), pieces[0].dtype),
@@ -383,17 +418,18 @@
     ]
 
     entries = mig_target.shape[1]
-    slots = jax.ShapeDtypeStruct((replicas, *kv_pool.shape[1:]), kv_pool.dtype)
+    half_block = (replicas, kv_pool.shape[1] // 2, kv_pool.shape[2])
+    slots = (jax.ShapeDtypeStruct(half_block, kv_pool.dtype),) * 2
     outgoing = pl.pallas_call(
         pack_kernel,
         out_shape=slots,
         in_specs=[IN_SMEM] * 3 + [IN_HBM],
-        out_specs=IN_HBM,
+        out_specs=(IN_HBM,) * 2,
         scratch_shapes=[
             pltpu.VMEM((entries, *kv_pool.shape[1:]), kv_pool.dtype),
             pltpu.VMEM(kv_pool.shape[1:], kv_pool.dtype),
             pltpu.SemaphoreType.DMA((entries,)),
-            pltpu.SemaphoreType.DMA((entries,)),
+            pltpu.SemaphoreType.DMA((2, entries)),
         ],
         compiler_params=COPY_PARAMS,
         name="pack_moved",
@@ -417,17 +453,17 @@
             name="local_keys",
         )(ctx_len, queries, suffix_kv, own_cache, after)
 
-    def fold_moved(arrived, state_now, part):
+    def fold_moved(arrived, state_now):
         rows = arrived.shape[1]
         group = max(n for n in range(1, replicas + 1) if replicas % n == 0 and n * rows <= CHUNK)
-        steps = replicas // group // 2
+        steps = replicas // group
         return pl.pallas_call(
             functools.partial(moved_kernel, factor, steps),
             out_shape=state,
             grid=(steps,),
             in_specs=[
                 whole(queries.shape),
-                pl.BlockSpec((group, rows, 2 * size), lambda i: (part * steps + i, 0, 0)),
+                pl.BlockSpec((group, rows, 2 * size), lambda i: (i, 0, 0)),
                 whole(state.shape),
             ],
             out_specs=whole(state.shape),
@@ -438,7 +474,7 @@
         )(queries, arrived, state_now)
 
     def fold_prefix(pieces, state_now, last=False):
-        others = from_other(pieces, place)
+        others = from_other(pieces, other)
         rows = pieces[0].shape[1]
         keys = 2 * len(pieces) * rows
         steps = max(1, keys // CHUNK)
@@ -464,9 +500,9 @@
             compiler_params=PARAMS,
             cost_estimate=cost(row_count, keys, size),
             name="prefix_keys",
-        )(place, queries, *pieces, others, state_now)
-
-    held, place, state_now, arrived = multicast(
+        )(mine, queries, *pieces, others, state_now)
+
+    held, mine, other, state_now, later = multicast(
         prefix_cache, owners, readers, outgoing, fold_local, fold_moved
     )
     gathered = {0: held}
@@ -475,15 +511,14 @@
     for near in range(1, rounds + 1):
         steps = [step for step in range(1, replicas // 4) if step.bit_count() == near]
         coming = [gather_step(gathered, step) for step in steps]
-        if near == 1:
-            state_now = fold_moved(arrived, state_now, 1)
-        else:
-            state_now = fold_prefix(ready, state_now)
+        if near > 1:
+            *coming, state_now = lax.optimization_barrier(
+                (*coming, fold_prefix(ready, state_now))
+            )
             ready = []
-        *coming, state_now = lax.optimization_barrier((*coming, state_now))
         gathered.update(zip(steps, coming))
         ready += coming
-    return fold_prefix(ready, state_now, True)
+    return fold_prefix(ready, fold_moved(later, state_now), True)
 
 
 def solution(mesh):

time: 124 us -> 125 us (level)
  waiting for transfers between devices: 22.7 us -> 14.4 us
  starting transfers between devices: 41.5 us -> 49.1 us
  local copies, waits for them, and re-layouts: 5.28 us -> 8.38 us
  Pallas kernels: 43.3 us -> 41.2 us
    ppermute x14, waiting for transfers between devices: 17.8 us -> 3.82 us  [to_peers(): lax.ppermute(rows, 'replica', [(i, i ^ 2 * step) for i in senders])]
    ppermute x7, waiting for transfers between devices: 1.89 us -> 10.4 us  [gather_step(): return lax.ppermute(gathered[step ^ 1 << last], 'replica', pairs)]
    all_to_all x1 -> x2, starting transfers between devices: 7.35 us -> 13.8 us  [send_blocks(): lax.all_to_all(rows, 'replica', split_axis=0, concat_axis=0, tiled=True)]
    unnamed x34 -> x42, local copies, waits for them, and re-layouts: 3.92 us -> 8.38 us
    ppermute x4, waiting for transfers between devices: 2.96 us -> 0.19 us  [swap_cores(): lax.ppermute(rows, 'replica', [(i, i ^ 1) for i in range(lax.axis_size('r...]
    pallas_call x2, Pallas kernels: 16 us -> 13.3 us  [fold_moved(): pl.pallas_call(functools.partial(moved_kernel, factor, steps), out_shape=...]
    ppermute x7, starting transfers between devices: 9.07 us -> 11 us  [gather_step(): return lax.ppermute(gathered[step ^ 1 << last], 'replica', pairs)]
    ppermute x1, starting transfers between devices: 7.53 us -> 5.83 us  [multicast(): lax.ppermute(found, 'replica', [(i, (i + half) % replicas) for i in range...]
  transfers between devices with their start and end apart: 28 -> 29, of which waited for: 8 -> 8; matrix products, arithmetic and copies ran while one was open for 1% -> 0% of each run, Pallas kernels for 31% -> 30%
where the time goes in v17:
time: 125 us; the launch traced here: 123 us
  starting transfers between devices  49.1 us (39%)
  Pallas kernels  41.2 us (33%)
  waiting for transfers between devices  14.4 us (12%)
  between operations  9.93 us (8%)
  local copies, waits for them, and re-layouts  8.38 us (7%)
    ppermute x14, starting transfers between devices, to_peers(): lax.ppermute(rows, 'replica', [(i, i ^ 2 * step) for i in senders])  16.4 us
    pallas_call x3, Pallas kernels, fold_prefix(): pl.pallas_call(functools.partial(prefix_kernel, factor, last, len(pieces)...  15.6 us
    all_to_all x2, starting transfers between devices, send_blocks(): lax.all_to_all(rows, 'replica', split_axis=0, concat_axis=0, tiled=True)  13.8 us
    pallas_call x2, Pallas kernels, fold_moved(): pl.pallas_call(functools.partial(moved_kernel, factor, steps), out_shape=...  13.3 us
    ppermute x7, starting transfers between devices, gather_step(): return lax.ppermute(gathered[step ^ 1 << last], 'replica', pairs)  11 us
    ppermute x7, waiting for transfers between devices, gather_step(): return lax.ppermute(gathered[step ^ 1 << last], 'replica', pairs)  10.4 us
    unnamed x42, local copies, waits for them, and re-layouts  8.38 us
    ppermute x1, starting transfers between devices, multicast(): lax.ppermute(found, 'replica', [(i, (i + half) % replicas) for i in range...  5.83 us
  transfers between devices with their start and end apart: 29, of which 8 were waited for; matrix products, arithmetic and copies ran while one was open for 0% of the time, Pallas kernels for 30%

profile of v17, /device:TPU:0, one launch (start us, length us, event | category | flops | bytes accessed | tf_op | source)
XLA Modules:
  0.0 123.3 jit_solution(3596621658767735146)
XLA Ops:
  1.1 3.9 %pack_moved.1 = (bf16[32,64,256]{2,1,0:T(8,128)(2,1)}, bf16[32,64,256]{2,1,0:T(8,128)(2,1)}) custom-call(s32[1,32]{1,0:T(1,128)} %target_ref.1, s32[1,32]{1,0:T(1,128)} %block_ref.1, s32[1]{0:T(128)S(6)} %copy.15.count_ref, bf16[32,128,256]{2,1,0:T(8,128)(2,1)} %pool_ref.1), custom_call_target="tpu_custom_call" | custom-call | tf_op jit(solution)/shard_map/pack_moved/pallas_call | solution.py:423
  5.0 7.0 %all-to-all-start = ((bf16[32,64,256]{2,1,0:T(8,128)(2,1)}), bf16[32,64,256]{2,1,0:T(8,128)(2,1)S(1)}, u32[]{:S(2)}, u32[]{:S(2)}) async-start(bf16[32,64,256]{2,1,0:T(8,128)(2,1)} %get-tuple-element.82), calls=%async_computation | async-start | bytes 2097152 | tf_op jit(solution)/shard_map/all_to_all | solution.py:348
  12.6 3.6 %stage_prefix.1 = (s32[1]{0:T(128)}, s32[1]{0:T(128)}, s32[1]{0:T(128)}, s32[1]{0:T(128)}, s32[2]{0:T(128)}, /*index=5*/bf16[1,256,256]{2,1,0:T(8,128)(2,1)}, bf...) custom-call(s32[2]{0:T(128)} %owner_ref.1, ...), custom_call_target="tpu_custom_call" | custom-call | tf_op jit(solution)/shard_map/stage_prefix/pallas_call | solution.py:297
  24.4 1.8 %collective-permute-start.1 = (bf16[1,256,256]{2,1,0:T(8,128)(2,1)}, bf16[1,256,256]{2,1,0:T(8,128)(2,1)S(1)}, u32[]{:S(2)}, u32[]{:S(2)}) collective-permute-start(bf16[1,256,256]{2,1,0:T(8,128)(2,1)} %get-tuple-element.56), channel_id=1, source_target_pairs={{0,2},{1,3},{2,0},{3,1},{4,6},{5,7},{6,4},{7,5},{8,10},{9,11},{10,... | collective-permute-start | bytes 393224 | tf_op jit(solution)/shard_map/ppermute | solution.py:316
  26.2 2.4 %collective-permute-start.10 = (bf16[1,256,256]{2,1,0:T(8,128)(2,1)}, bf16[1,256,256]{2,1,0:T(8,128)(2,1)S(1)}, u32[]{:S(2)}, u32[]{:S(2)}) collective-permute-start(bf16[1,256,256]{2,1,0:T(8,128)(2,1)} %get-tuple-element.76), channel_id=1, source_target_pairs={{0,12},{1,13},{2,14},{3,15},{4,8},{5,9},{6,10},{7,11},{8,4},{9,5},... | collective-permute-start | bytes 393224 | tf_op jit(solution)/shard_map/ppermute | solution.py:316
  28.6 0.6 collective-permute-start.11
  29.1 1.5 %collective-permute-start.12 = (bf16[1,256,256]{2,1,0:T(8,128)(2,1)}, bf16[1,256,256]{2,1,0:T(8,128)(2,1)S(1)}, u32[]{:S(2)}, u32[]{:S(2)}) collective-permute-start(bf16[1,256,256]{2,1,0:T(8,128)(2,1)} %get-tuple-element.78), channel_id=1, source_target_pairs={{0,8},{1,9},{2,10},{3,11},{4,12},{5,13},{6,14},{7,15},{8,0},{9,1},... | collective-permute-start | bytes 393224 | tf_op jit(solution)/shard_map/ppermute | solution.py:316
  30.6 1.5 %collective-permute-start.13 = (bf16[1,256,256]{2,1,0:T(8,128)(2,1)}, bf16[1,256,256]{2,1,0:T(8,128)(2,1)S(1)}, u32[]{:S(2)}, u32[]{:S(2)}) collective-permute-start(bf16[1,256,256]{2,1,0:T(8,128)(2,1)} %get-tuple-element.79), channel_id=1, source_target_pairs={{0,6},{1,7},{2,4},{3,5},{4,2},{5,3},{6,0},{7,1},{8,14},{9,15},{10,... | collective-permute-start | bytes 393224 | tf_op jit(solution)/shard_map/ppermute | solution.py:316
  32.1 0.9 copy-done
  33.1 2.7 %local_keys.1.loaded_ref = f32[2,2048,128]{2,1,0:T(8,128)S(1)} custom-call(s32[1]{0:T(128)S(6)} %copy.14.len_ref, bf16[256,1024]{1,0:T(8,128)(2,1)S(1)} %copy-done.1, bf16[256,256]{1,0:T(8,128)(2,1)S(1)} %copy-done.3, bf16[512,256]{1,0:T(8,128)(2,1)S(1)} %copy-done.2, bf16[1,256,256]{2,1,0:T(8,128)(2,1)S(1)} %copy-done), custom_call_target="tpu_custom_call" | custom-call | flops 2415919104 | bytes 393216 | tf_op jit(solution)/shard_map/local_keys/pallas_call | solution.py:438
  35.8 1.5 %collective-permute-start.14 = (bf16[1,256,256]{2,1,0:T(8,128)(2,1)S(1)}, bf16[1,256,256]{2,1,0:T(8,128)(2,1)S(1)}, u32[]{:S(2)}, u32[]{:S(2)}) collective-permute-start(bf16[1,256,256]{2,1,0:T(8,128)(2,1)S(1)} %copy-done.19), channel_id=1, source_target_pairs={{0,4},{1,5},{2,6},{3,7},{4,0},{5,1},{6,2},{7,3},{8,12},{9,13},{10,... | collective-permute-start | bytes 393224 | tf_op jit(solution)/shard_map/ppermute | solution.py:316
  37.3 2.5 %collective-permute-start.9 = (bf16[1,256,256]{2,1,0:T(8,128)(2,1)S(1)}, bf16[1,256,256]{2,1,0:T(8,128)(2,1)S(1)}, u32[]{:S(2)}, u32[]{:S(2)}) collective-permute-start(bf16[1,256,256]{2,1,0:T(8,128)(2,1)S(1)} %copy-done.18), channel_id=1, source_target_pairs={{0,14},{1,15},{2,12},{3,13},{4,10},{5,11},{6,8},{7,9},{8,6},{9,7},... | collective-permute-start | bytes 393224 | tf_op jit(solution)/shard_map/ppermute | solution.py:316
  39.8 0.7 collective-permute-done.11
  40.5 0.7 collective-permute-start.2
  41.2 2.4 %collective-permute-done.12 = bf16[1,256,256]{2,1,0:T(8,128)(2,1)S(1)} collective-permute-done((bf16[1,256,256]{2,1,0:T(8,128)(2,1)}, bf16[1,256,256]{2,1,0:T(8,128)(2,1)S(1)}, u32[]{:S(2)}, u32[]{:S(2)}) %collective-permute-start.12) | collective-permute-done | bytes 131104 | tf_op jit(solution)/shard_map/ppermute | solution.py:316
  43.6 0.7 collective-permute-start.3
  44.3 0.7 collective-permute-start.4
  45.0 0.7 collective-permute-start.5
  45.7 0.7 collective-permute-done.9
  46.4 0.7 collective-permute-start.6
  47.1 0.7 collective-permute-start.7
  47.8 0.7 collective-permute-start.8
  48.5 5.8 %collective-permute-start.15 = (bf16[1,256,256]{2,1,0:T(8,128)(2,1)S(1)}, bf16[1,256,256]{2,1,0:T(8,128)(2,1)S(1)}, u32[]{:S(2)}, u32[]{:S(2)}) collective-permute-start(bf16[1,256,256]{2,1,0:T(8,128)(2,1)S(1)} %select_select_fusion), channel_id=1, source_target_pairs={{0,16},{1,17},{2,18},{3,19},{4,20},{5,21},{6,22},{7,23},{8,24},{9,... | collective-permute-start | bytes 393224 | tf_op jit(solution)/shard_map/ppermute | solution.py:332
  54.4 1.3 %collective-permute-start.16 = (bf16[1,256,256]{2,1,0:T(8,128)(2,1)S(1)}, bf16[1,256,256]{2,1,0:T(8,128)(2,1)S(1)}, u32[]{:S(2)}, u32[]{:S(2)}) collective-permute-start(bf16[1,256,256]{2,1,0:T(8,128)(2,1)S(1)} %select_select_fusion.1), channel_id=1, source_target_pairs={{16,0},{17,1},{18,2},{19,3},{20,4},{21,5},{22,6},{23,7},{24,8},{25... | collective-permute-start | bytes 393224 | tf_op jit(solution)/shard_map/ppermute | solution.py:334
  55.8 1.6 %copy-done.5 = f32[2,2048,128]{2,1,0:T(8,128)S(1)} copy-done((f32[2,2048,128]{2,1,0:T(8,128)S(1)}, f32[2,2048,128]{2,1,0:T(8,128)}, u32[]{:S(2)}) %copy-start.5) | copy-done | bytes 2097176
  57.3 6.6 %moved_keys.2.refs_5_ = f32[2,2048,128]{2,1,0:T(8,128)S(1)} custom-call(bf16[256,1024]{1,0:T(8,128)(2,1)S(1)} %copy-done.1, bf16[32,64,256]{2,1,0:T(8,128)(2,1)S(1)} %all-to-all-done.kv_ref, f32[2,2048,128]{2,1,0:T(8,128)S(1)} %copy-done.5), custom_call_target="tpu_custom_call" | custom-call | flops 6442450944 | bytes 1048576 | tf_op jit(solution)/shard_map/moved_keys/pallas_call | solution.py:460
  64.0 1.3 %copy-done.8 = f32[2,2048,128]{2,1,0:T(8,128)} copy-done((f32[2,2048,128]{2,1,0:T(8,128)}, f32[2,2048,128]{2,1,0:T(8,128)S(1)}, u32[]{:S(2)}) %copy-start.8) | copy-done | bytes 2097176
  65.4 2.7 %collective-permute-start.17 = (bf16[2,256,256]{2,1,0:T(8,128)(2,1)S(1)}, bf16[2,256,256]{2,1,0:T(8,128)(2,1)S(1)}, u32[]{:S(2)}, u32[]{:S(2)}) collective-permute-start(bf16[2,256,256]{2,1,0:T(8,128)(2,1)S(1)} %maximum_select_fusion.refs_0_), channel_id=1, source_target_pairs={{0,2},{1,3},{2,0},{3,1},{4,6},{5,7},{6,4},{7,5},{8,10},{9,11},{10,... | collective-permute-start | bytes 786440 | tf_op jit(solution)/shard_map/ppermute | solution.py:362
  68.2 2.2 %collective-permute-start.21 = (bf16[2,256,256]{2,1,0:T(8,128)(2,1)S(1)}, bf16[2,256,256]{2,1,0:T(8,128)(2,1)S(1)}, u32[]{:S(2)}, u32[]{:S(2)}) collective-permute-start(bf16[2,256,256]{2,1,0:T(8,128)(2,1)S(1)} %maximum_select_fusion.refs_0_), channel_id=1, source_target_pairs={{0,4},{1,5},{2,6},{3,7},{4,0},{5,1},{6,2},{7,3},{8,12},{9,13},{10,... | collective-permute-start | bytes 786440 | tf_op jit(solution)/shard_map/ppermute | solution.py:362
  70.3 6.9 %all-to-all-start.1 = ((bf16[32,64,256]{2,1,0:T(8,128)(2,1)}), bf16[32,64,256]{2,1,0:T(8,128)(2,1)S(1)}, u32[]{:S(2)}, u32[]{:S(2)}) async-start(bf16[32,64,256]{2,1,0:T(8,128)(2,1)} %gate.1), calls=%async_computation.1 | async-start | bytes 2097152 | tf_op jit(solution)/shard_map/all_to_all | solution.py:348
  77.2 0.7 pick_other.3
  78.1 1.7 %collective-permute-start.18 = (bf16[2,256,256]{2,1,0:T(8,128)(2,1)S(1)}, bf16[2,256,256]{2,1,0:T(8,128)(2,1)S(1)}, u32[]{:S(2)}, u32[]{:S(2)}) collective-permute-start(bf16[2,256,256]{2,1,0:T(8,128)(2,1)S(1)} %collective-permute-done.17.refs_1_), channel_id=1, source_target_pairs={{0,4},{1,5},{2,6},{3,7},{4,0},{5,1},{6,2},{7,3},{8,12},{9,13},{10,... | collective-permute-start | bytes 786440 | tf_op jit(solution)/shard_map/ppermute | solution.py:362
  79.8 1.5 %collective-permute-start.20 = (bf16[2,256,256]{2,1,0:T(8,128)(2,1)S(1)}, bf16[2,256,256]{2,1,0:T(8,128)(2,1)S(1)}, u32[]{:S(2)}, u32[]{:S(2)}) collective-permute-start(bf16[2,256,256]{2,1,0:T(8,128)(2,1)S(1)} %collective-permute-done.19.refs_3_), channel_id=1, source_target_pairs={{0,2},{1,3},{2,0},{3,1},{4,6},{5,7},{6,4},{7,5},{8,10},{9,11},{10,... | collective-permute-start | bytes 786440 | tf_op jit(solution)/shard_map/ppermute | solution.py:362
  81.3 1.5 %collective-permute-start.22 = (bf16[2,256,256]{2,1,0:T(8,128)(2,1)S(1)}, bf16[2,256,256]{2,1,0:T(8,128)(2,1)S(1)}, u32[]{:S(2)}, u32[]{:S(2)}) collective-permute-start(bf16[2,256,256]{2,1,0:T(8,128)(2,1)S(1)} %collective-permute-done.21.refs_2_), channel_id=1, source_target_pairs={{0,8},{1,9},{2,10},{3,11},{4,12},{5,13},{6,14},{7,15},{8,0},{9,1},... | collective-permute-start | bytes 786440 | tf_op jit(solution)/shard_map/ppermute | solution.py:362
  82.7 1.6 %copy-done.9 = f32[2,2048,128]{2,1,0:T(8,128)S(1)} copy-done((f32[2,2048,128]{2,1,0:T(8,128)S(1)}, f32[2,2048,128]{2,1,0:T(8,128)}, u32[]{:S(2)}) %copy-start.9) | copy-done | bytes 2097176
  84.3 7.0 %prefix_keys.3.refs_4_ = f32[2,2048,128]{2,1,0:T(8,128)S(1)} custom-call(s32[1]{0:T(128)} %get-tuple-element.53.which_ref, bf16[256,1024]{1,0:T(8,128)(2,1)S(1)} %copy-done.1, bf16[2,256,256]{2,1,0:T(8,128)(2,1)S(1)} %maximum_select_fusion.refs_0_, bf16[2,256,256]{2,1,0:T(8,128)(2,1)S(1)} %collective-permute-done.17.refs_1_, ...), custom_call_target="tpu_custom_call" | custom-call | flops 6442450944 | bytes 1048576 | tf_op jit(solution)/shard_map/prefix_keys/pallas_call | solution.py:484
  91.3 3.0 %collective-permute-done.18.refs_0_ = bf16[2,256,256]{2,1,0:T(8,128)(2,1)S(1)} collective-permute-done((bf16[2,256,256]{2,1,0:T(8,128)(2,1)S(1)}, bf16[2,256,256]{2,1,0:T(8,128)(2,1)S(1)}, u32[]{:S(2)}, u32[]{:S(2)}) %collective-permute-start.18) | collective-permute-done | bytes 262176 | tf_op jit(solution)/shard_map/ppermute | solution.py:362
  94.4 1.0 collective-permute-done.20.refs_1_
  95.3 5.6 %collective-permute-done.22.refs_2_ = bf16[2,256,256]{2,1,0:T(8,128)(2,1)S(1)} collective-permute-done((bf16[2,256,256]{2,1,0:T(8,128)(2,1)S(1)}, bf16[2,256,256]{2,1,0:T(8,128)(2,1)S(1)}, u32[]{:S(2)}, u32[]{:S(2)}) %collective-permute-start.22) | collective-permute-done | bytes 262176 | tf_op jit(solution)/shard_map/ppermute | solution.py:362
  101.0 0.7 pick_other.4
  101.8 1.5 %collective-permute-start.24 = (bf16[2,256,256]{2,1,0:T(8,128)(2,1)S(1)}, bf16[2,256,256]{2,1,0:T(8,128)(2,1)S(1)}, u32[]{:S(2)}, u32[]{:S(2)}) collective-permute-start(bf16[2,256,256]{2,1,0:T(8,128)(2,1)S(1)} %collective-permute-done.22.refs_2_), channel_id=1, source_target_pairs={{0,2},{1,3},{2,0},{3,1},{4,6},{5,7},{6,4},{7,5},{8,10},{9,11},{10,... | collective-permute-start | bytes 786440 | tf_op jit(solution)/shard_map/ppermute | solution.py:362
  103.5 4.9 %prefix_keys.4.loaded_ref = f32[2,2048,128]{2,1,0:T(8,128)S(1)} custom-call(s32[1]{0:T(128)} %get-tuple-element.53.which_ref, bf16[256,1024]{1,0:T(8,128)(2,1)S(1)} %copy-done.1, bf16[2,256,256]{2,1,0:T(8,128)(2,1)S(1)} %collective-permute-done.18.refs_0_, bf16[2,256,256]{2,1,0:T(8,128)(2,1)S(1)} %collective-permute-done.20.refs_1_, ...), custom_call_target="tpu_custom_call" | custom-call | flops 4831838208 | bytes 786432 | tf_op jit(solution)/shard_map/prefix_keys/pallas_call | solution.py:484
  108.4 1.3 %copy-done.6 = f32[2,2048,128]{2,1,0:T(8,128)} copy-done((f32[2,2048,128]{2,1,0:T(8,128)}, f32[2,2048,128]{2,1,0:T(8,128)S(1)}, u32[]{:S(2)}) %copy-start.6) | copy-done | bytes 2097176
  109.7 0.8 collective-permute-done.24.refs_0_
  110.5 0.7 pick_other.5
  111.3 1.6 %copy-done.7 = f32[2,2048,128]{2,1,0:T(8,128)S(1)} copy-done((f32[2,2048,128]{2,1,0:T(8,128)S(1)}, f32[2,2048,128]{2,1,0:T(8,128)}, u32[]{:S(2)}) %copy-start.7) | copy-done | bytes 2097176
  112.9 6.6 %moved_keys.3.refs_2_ = f32[2,2048,128]{2,1,0:T(8,128)S(1)} custom-call(bf16[256,1024]{1,0:T(8,128)(2,1)S(1)} %copy-done.1, bf16[32,64,256]{2,1,0:T(8,128)(2,1)S(1)} %all-to-all-done.1.kv_ref, f32[2,2048,128]{2,1,0:T(8,128)S(1)} %copy-done.7), custom_call_target="tpu_custom_call" | custom-call | flops 6442450944 | bytes 1048576 | tf_op jit(solution)/shard_map/moved_keys/pallas_call | solution.py:460
  119.5 3.7 %prefix_keys.5 = bf16[256,1024]{1,0:T(8,128)(2,1)} custom-call(s32[1]{0:T(128)} %get-tuple-element.53.which_ref, bf16[256,1024]{1,0:T(8,128)(2,1)S(1)} %copy-done.1, bf16[2,256,256]{2,1,0:T(8,128)(2,1)S(1)} %collective-permute-done.24.refs_0_, bf16[256,256]{1,0:T(8,128)(2,1)S(1)} %collective-permute-done.26.refs_1_, f32[2,2048,128]{2,1,0:T(8,128)S(1)} %moved_keys.3.refs_2_), custom_call_target="tpu_custom_call" | custom-call | flops 1610612736 | bytes 262144 | tf_op jit(solution)/shard_map/prefix_keys/pallas_call | solution.py:484
  (68 shorter events, 1.3 us)
Async XLA Ops:
  0.0 5.0 %collective-permute-start = (bf16[4096,256]{1,0:T(8,128)(2,1)}, bf16[4096,256]{1,0:T(8,128)(2,1)}, u32[]{:S(2)}, u32[]{:S(2)}) collective-permute-start(bf16[4096,256]{1,0:T(8,128)(2,1)} %param.15), channel_id=1, source_target_pairs={{0,1},{1,0},{2,3},{3,2},{4,5},{5,4},{6,7},{7,6},{8,9},{9,8},{10,11... | collective-permute-start | bytes 6291464 | tf_op jit(solution)/shard_map/ppermute | solution.py:352
  5.0 50.7 %all-to-all-start = ((bf16[32,64,256]{2,1,0:T(8,128)(2,1)}), bf16[32,64,256]{2,1,0:T(8,128)(2,1)S(1)}, u32[]{:S(2)}, u32[]{:S(2)}) async-start(bf16[32,64,256]{2,1,0:T(8,128)(2,1)} %get-tuple-element.82), calls=%async_computation | async-start | bytes 2097152 | tf_op jit(solution)/shard_map/all_to_all | solution.py:348
  12.6 19.5 %copy-start.1 = (bf16[256,1024]{1,0:T(8,128)(2,1)S(1)}, bf16[256,1024]{1,0:T(8,128)(2,1)}, u32[]{:S(2)}) copy-start(bf16[256,1024]{1,0:T(8,128)(2,1)} %q_ref.11) | copy-start | bytes 1572868
  12.6 19.5 %copy-start.2 = (bf16[512,256]{1,0:T(8,128)(2,1)S(1)}, bf16[512,256]{1,0:T(8,128)(2,1)}, u32[]{:S(2)}) copy-start(bf16[512,256]{1,0:T(8,128)(2,1)} %own_ref.1) | copy-start | bytes 786436
  12.6 19.5 %copy-start.3 = (bf16[256,256]{1,0:T(8,128)(2,1)S(1)}, bf16[256,256]{1,0:T(8,128)(2,1)}, u32[]{:S(2)}) copy-start(bf16[256,256]{1,0:T(8,128)(2,1)} %suffix_ref.1) | copy-start | bytes 393220
  24.4 11.4 %collective-permute-start.1 = (bf16[1,256,256]{2,1,0:T(8,128)(2,1)}, bf16[1,256,256]{2,1,0:T(8,128)(2,1)S(1)}, u32[]{:S(2)}, u32[]{:S(2)}) collective-permute-start(bf16[1,256,256]{2,1,0:T(8,128)(2,1)} %get-tuple-element.56), channel_id=1, source_target_pairs={{0,2},{1,3},{2,0},{3,1},{4,6},{5,7},{6,4},{7,5},{8,10},{9,11},{10,... | collective-permute-start | bytes 393224 | tf_op jit(solution)/shard_map/ppermute | solution.py:316
  26.2 11.1 %collective-permute-start.10 = (bf16[1,256,256]{2,1,0:T(8,128)(2,1)}, bf16[1,256,256]{2,1,0:T(8,128)(2,1)S(1)}, u32[]{:S(2)}, u32[]{:S(2)}) collective-permute-start(bf16[1,256,256]{2,1,0:T(8,128)(2,1)} %get-tuple-element.76), channel_id=1, source_target_pairs={{0,12},{1,13},{2,14},{3,15},{4,8},{5,9},{6,10},{7,11},{8,4},{9,5},... | collective-permute-start | bytes 393224 | tf_op jit(solution)/shard_map/ppermute | solution.py:316
  28.6 12.0 %collective-permute-start.11 = (bf16[1,256,256]{2,1,0:T(8,128)(2,1)}, bf16[1,256,256]{2,1,0:T(8,128)(2,1)S(1)}, u32[]{:S(2)}, u32[]{:S(2)}) collective-permute-start(bf16[1,256,256]{2,1,0:T(8,128)(2,1)} %get-tuple-element.77), channel_id=1, source_target_pairs={{0,10},{1,11},{2,8},{3,9},{4,14},{5,15},{6,12},{7,13},{8,2},{9,3},... | collective-permute-start | bytes 393224 | tf_op jit(solution)/shard_map/ppermute | solution.py:316
  29.1 14.4 %collective-permute-start.12 = (bf16[1,256,256]{2,1,0:T(8,128)(2,1)}, bf16[1,256,256]{2,1,0:T(8,128)(2,1)S(1)}, u32[]{:S(2)}, u32[]{:S(2)}) collective-permute-start(bf16[1,256,256]{2,1,0:T(8,128)(2,1)} %get-tuple-element.78), channel_id=1, source_target_pairs={{0,8},{1,9},{2,10},{3,11},{4,12},{5,13},{6,14},{7,15},{8,0},{9,1},... | collective-permute-start | bytes 393224 | tf_op jit(solution)/shard_map/ppermute | solution.py:316
  30.6 13.7 %collective-permute-start.13 = (bf16[1,256,256]{2,1,0:T(8,128)(2,1)}, bf16[1,256,256]{2,1,0:T(8,128)(2,1)S(1)}, u32[]{:S(2)}, u32[]{:S(2)}) collective-permute-start(bf16[1,256,256]{2,1,0:T(8,128)(2,1)} %get-tuple-element.79), channel_id=1, source_target_pairs={{0,6},{1,7},{2,4},{3,5},{4,2},{5,3},{6,0},{7,1},{8,14},{9,15},{10,... | collective-permute-start | bytes 393224 | tf_op jit(solution)/shard_map/ppermute | solution.py:316
  33.0 2.8 %copy-start.19 = (bf16[1,256,256]{2,1,0:T(8,128)(2,1)S(1)}, bf16[1,256,256]{2,1,0:T(8,128)(2,1)}, u32[]{:S(2)}) copy-start(bf16[1,256,256]{2,1,0:T(8,128)(2,1)} %get-tuple-element.80) | copy-start | bytes 393220
  33.0 4.3 %copy-start.18 = (bf16[1,256,256]{2,1,0:T(8,128)(2,1)S(1)}, bf16[1,256,256]{2,1,0:T(8,128)(2,1)}, u32[]{:S(2)}) copy-start(bf16[1,256,256]{2,1,0:T(8,128)(2,1)} %get-tuple-element.75) | copy-start | bytes 393220
  33.0 7.5 %copy-start.17 = (bf16[1,256,256]{2,1,0:T(8,128)(2,1)S(1)}, bf16[1,256,256]{2,1,0:T(8,128)(2,1)}, u32[]{:S(2)}) copy-start(bf16[1,256,256]{2,1,0:T(8,128)(2,1)} %get-tuple-element.66) | copy-start | bytes 393220
  33.0 10.6 %copy-start.16 = (bf16[1,256,256]{2,1,0:T(8,128)(2,1)S(1)}, bf16[1,256,256]{2,1,0:T(8,128)(2,1)}, u32[]{:S(2)}) copy-start(bf16[1,256,256]{2,1,0:T(8,128)(2,1)} %get-tuple-element.67) | copy-start | bytes 393220
  33.0 11.2 %copy-start.20 = (s32[2]{0:T(128)S(1)}, s32[2]{0:T(128)}, u32[]{:S(2)}) copy-start(s32[2]{0:T(128)} %get-tuple-element.54) | copy-start | bytes 28
  33.0 11.3 %copy-start.15 = (bf16[1,256,256]{2,1,0:T(8,128)(2,1)S(1)}, bf16[1,256,256]{2,1,0:T(8,128)(2,1)}, u32[]{:S(2)}) copy-start(bf16[1,256,256]{2,1,0:T(8,128)(2,1)} %get-tuple-element.68) | copy-start | bytes 393220
  33.0 12.0 %copy-start.14 = (bf16[1,256,256]{2,1,0:T(8,128)(2,1)S(1)}, bf16[1,256,256]{2,1,0:T(8,128)(2,1)}, u32[]{:S(2)}) copy-start(bf16[1,256,256]{2,1,0:T(8,128)(2,1)} %get-tuple-element.69) | copy-start | bytes 393220
  33.0 13.3 %copy-start.13 = (bf16[1,256,256]{2,1,0:T(8,128)(2,1)S(1)}, bf16[1,256,256]{2,1,0:T(8,128)(2,1)}, u32[]{:S(2)}) copy-start(bf16[1,256,256]{2,1,0:T(8,128)(2,1)} %get-tuple-element.70) | copy-start | bytes 393220
  33.0 14.0 %copy-start.12 = (bf16[1,256,256]{2,1,0:T(8,128)(2,1)S(1)}, bf16[1,256,256]{2,1,0:T(8,128)(2,1)}, u32[]{:S(2)}) copy-start(bf16[1,256,256]{2,1,0:T(8,128)(2,1)} %get-tuple-element.71) | copy-start | bytes 393220
  33.1 14.7 %copy-start.11 = (bf16[1,256,256]{2,1,0:T(8,128)(2,1)S(1)}, bf16[1,256,256]{2,1,0:T(8,128)(2,1)}, u32[]{:S(2)}) copy-start(bf16[1,256,256]{2,1,0:T(8,128)(2,1)} %get-tuple-element.72) | copy-start | bytes 393220
  33.1 21.3 %copy-start.10 = (bf16[1,256,256]{2,1,0:T(8,128)(2,1)S(1)}, bf16[1,256,256]{2,1,0:T(8,128)(2,1)}, u32[]{:S(2)}) copy-start(bf16[1,256,256]{2,1,0:T(8,128)(2,1)} %get-tuple-element.73) | copy-start | bytes 393220
  35.7 18.7 %copy-start.4 = (f32[2,2048,128]{2,1,0:T(8,128)}, f32[2,2048,128]{2,1,0:T(8,128)S(1)}, u32[]{:S(2)}) copy-start(f32[2,2048,128]{2,1,0:T(8,128)S(1)} %local_keys.1.loaded_ref) | copy-start | bytes 6291460
  35.8 9.2 %collective-permute-start.14 = (bf16[1,256,256]{2,1,0:T(8,128)(2,1)S(1)}, bf16[1,256,256]{2,1,0:T(8,128)(2,1)S(1)}, u32[]{:S(2)}, u32[]{:S(2)}) collective-permute-start(bf16[1,256,256]{2,1,0:T(8,128)(2,1)S(1)} %copy-done.19), channel_id=1, source_target_pairs={{0,4},{1,5},{2,6},{3,7},{4,0},{5,1},{6,2},{7,3},{8,12},{9,13},{10,... | collective-permute-start | bytes 393224 | tf_op jit(solution)/shard_map/ppermute | solution.py:316
  37.3 9.1 %collective-permute-start.9 = (bf16[1,256,256]{2,1,0:T(8,128)(2,1)S(1)}, bf16[1,256,256]{2,1,0:T(8,128)(2,1)S(1)}, u32[]{:S(2)}, u32[]{:S(2)}) collective-permute-start(bf16[1,256,256]{2,1,0:T(8,128)(2,1)S(1)} %copy-done.18), channel_id=1, source_target_pairs={{0,14},{1,15},{2,12},{3,13},{4,10},{5,11},{6,8},{7,9},{8,6},{9,7},... | collective-permute-start | bytes 393224 | tf_op jit(solution)/shard_map/ppermute | solution.py:316
  40.5 6.5 %collective-permute-start.2 = (bf16[1,256,256]{2,1,0:T(8,128)(2,1)S(1)}, bf16[1,256,256]{2,1,0:T(8,128)(2,1)S(1)}, u32[]{:S(2)}, u32[]{:S(2)}) collective-permute-start(bf16[1,256,256]{2,1,0:T(8,128)(2,1)S(1)} %copy-done.17), channel_id=1, source_target_pairs={{30,16},{31,17}} | collective-permute-start | bytes 393224 | tf_op jit(solution)/shard_map/ppermute | solution.py:316
  43.6 4.2 %collective-permute-start.3 = (bf16[1,256,256]{2,1,0:T(8,128)(2,1)S(1)}, bf16[1,256,256]{2,1,0:T(8,128)(2,1)S(1)}, u32[]{:S(2)}, u32[]{:S(2)}) collective-permute-start(bf16[1,256,256]{2,1,0:T(8,128)(2,1)S(1)} %copy-done.16), channel_id=1, source_target_pairs={{30,18},{31,19}} | collective-permute-start | bytes 393224 | tf_op jit(solution)/shard_map/ppermute | solution.py:316
  44.3 4.2 %collective-permute-start.4 = (bf16[1,256,256]{2,1,0:T(8,128)(2,1)S(1)}, bf16[1,256,256]{2,1,0:T(8,128)(2,1)S(1)}, u32[]{:S(2)}, u32[]{:S(2)}) collective-permute-start(bf16[1,256,256]{2,1,0:T(8,128)(2,1)S(1)} %copy-done.15), channel_id=1, source_target_pairs={{30,20},{31,21}} | collective-permute-start | bytes 393224 | tf_op jit(solution)/shard_map/ppermute | solution.py:316
  45.0 9.4 %collective-permute-start.5 = (bf16[1,256,256]{2,1,0:T(8,128)(2,1)S(1)}, bf16[1,256,256]{2,1,0:T(8,128)(2,1)S(1)}, u32[]{:S(2)}, u32[]{:S(2)}) collective-permute-start(bf16[1,256,256]{2,1,0:T(8,128)(2,1)S(1)} %copy-done.14), channel_id=1, source_target_pairs={{30,22},{31,23}} | collective-permute-start | bytes 393224 | tf_op jit(solution)/shard_map/ppermute | solution.py:316
  46.4 8.0 %collective-permute-start.6 = (bf16[1,256,256]{2,1,0:T(8,128)(2,1)S(1)}, bf16[1,256,256]{2,1,0:T(8,128)(2,1)S(1)}, u32[]{:S(2)}, u32[]{:S(2)}) collective-permute-start(bf16[1,256,256]{2,1,0:T(8,128)(2,1)S(1)} %copy-done.13), channel_id=1, source_target_pairs={{30,24},{31,25}} | collective-permute-start | bytes 393224 | tf_op jit(solution)/shard_map/ppermute | solution.py:316
  47.1 7.3 %collective-permute-start.7 = (bf16[1,256,256]{2,1,0:T(8,128)(2,1)S(1)}, bf16[1,256,256]{2,1,0:T(8,128)(2,1)S(1)}, u32[]{:S(2)}, u32[]{:S(2)}) collective-permute-start(bf16[1,256,256]{2,1,0:T(8,128)(2,1)S(1)} %copy-done.12), channel_id=1, source_target_pairs={{30,26},{31,27}} | collective-permute-start | bytes 393224 | tf_op jit(solution)/shard_map/ppermute | solution.py:316
  47.8 6.6 %collective-permute-start.8 = (bf16[1,256,256]{2,1,0:T(8,128)(2,1)S(1)}, bf16[1,256,256]{2,1,0:T(8,128)(2,1)S(1)}, u32[]{:S(2)}, u32[]{:S(2)}) collective-permute-start(bf16[1,256,256]{2,1,0:T(8,128)(2,1)S(1)} %copy-done.11), channel_id=1, source_target_pairs={{30,28},{31,29}} | collective-permute-start | bytes 393224 | tf_op jit(solution)/shard_map/ppermute | solution.py:316
  48.5 16.8 %collective-permute-start.15 = (bf16[1,256,256]{2,1,0:T(8,128)(2,1)S(1)}, bf16[1,256,256]{2,1,0:T(8,128)(2,1)S(1)}, u32[]{:S(2)}, u32[]{:S(2)}) collective-permute-start(bf16[1,256,256]{2,1,0:T(8,128)(2,1)S(1)} %select_select_fusion), channel_id=1, source_target_pairs={{0,16},{1,17},{2,18},{3,19},{4,20},{5,21},{6,22},{7,23},{8,24},{9,... | collective-permute-start | bytes 393224 | tf_op jit(solution)/shard_map/ppermute | solution.py:332
  54.4 10.9 %collective-permute-start.16 = (bf16[1,256,256]{2,1,0:T(8,128)(2,1)S(1)}, bf16[1,256,256]{2,1,0:T(8,128)(2,1)S(1)}, u32[]{:S(2)}, u32[]{:S(2)}) collective-permute-start(bf16[1,256,256]{2,1,0:T(8,128)(2,1)S(1)} %select_select_fusion.1), channel_id=1, source_target_pairs={{16,0},{17,1},{18,2},{19,3},{20,4},{21,5},{22,6},{23,7},{24,8},{25... | collective-permute-start | bytes 393224 | tf_op jit(solution)/shard_map/ppermute | solution.py:334
  55.8 1.6 %copy-start.5 = (f32[2,2048,128]{2,1,0:T(8,128)S(1)}, f32[2,2048,128]{2,1,0:T(8,128)}, u32[]{:S(2)}) copy-start(f32[2,2048,128]{2,1,0:T(8,128)} %copy-done.4) | copy-start | bytes 6291460
  65.4 11.8 %collective-permute-start.17 = (bf16[2,256,256]{2,1,0:T(8,128)(2,1)S(1)}, bf16[2,256,256]{2,1,0:T(8,128)(2,1)S(1)}, u32[]{:S(2)}, u32[]{:S(2)}) collective-permute-start(bf16[2,256,256]{2,1,0:T(8,128)(2,1)S(1)} %maximum_select_fusion.refs_0_), channel_id=1, source_target_pairs={{0,2},{1,3},{2,0},{3,1},{4,6},{5,7},{6,4},{7,5},{8,10},{9,11},{10,... | collective-permute-start | bytes 786440 | tf_op jit(solution)/shard_map/ppermute | solution.py:362
  68.2 9.0 %collective-permute-start.19 = (bf16[2,256,256]{2,1,0:T(8,128)(2,1)S(1)}, bf16[2,256,256]{2,1,0:T(8,128)(2,1)S(1)}, u32[]{:S(2)}, u32[]{:S(2)}) collective-permute-start(bf16[2,256,256]{2,1,0:T(8,128)(2,1)S(1)} %maximum_select_fusion.refs_0_), channel_id=1, source_target_pairs={{0,8},{1,9},{2,10},{3,11},{4,12},{5,13},{6,14},{7,15},{8,0},{9,1},... | collective-permute-start | bytes 786440 | tf_op jit(solution)/shard_map/ppermute | solution.py:362
  68.2 9.1 %collective-permute-start.21 = (bf16[2,256,256]{2,1,0:T(8,128)(2,1)S(1)}, bf16[2,256,256]{2,1,0:T(8,128)(2,1)S(1)}, u32[]{:S(2)}, u32[]{:S(2)}) collective-permute-start(bf16[2,256,256]{2,1,0:T(8,128)(2,1)S(1)} %maximum_select_fusion.refs_0_), channel_id=1, source_target_pairs={{0,4},{1,5},{2,6},{3,7},{4,0},{5,1},{6,2},{7,3},{8,12},{9,13},{10,... | collective-permute-start | bytes 786440 | tf_op jit(solution)/shard_map/ppermute | solution.py:362
  70.3 40.9 %all-to-all-start.1 = ((bf16[32,64,256]{2,1,0:T(8,128)(2,1)}), bf16[32,64,256]{2,1,0:T(8,128)(2,1)S(1)}, u32[]{:S(2)}, u32[]{:S(2)}) async-start(bf16[32,64,256]{2,1,0:T(8,128)(2,1)} %gate.1), calls=%async_computation.1 | async-start | bytes 2097152 | tf_op jit(solution)/shard_map/all_to_all | solution.py:348
  78.0 4.8 %collective-permute-start.23 = (bf16[1024,256]{1,0:T(8,128)(2,1)S(1)}, bf16[1024,256]{1,0:T(8,128)(2,1)S(1)}, u32[]{:S(2)}, u32[]{:S(2)}) collective-permute-start(bf16[1024,256]{1,0:T(8,128)(2,1)S(1)} %pick_other.3), channel_id=1, source_target_pairs={{0,1},{1,0},{2,3},{3,2},{4,5},{5,4},{6,7},{7,6},{8,9},{9,8},{10,11... | collective-permute-start | bytes 1572872 | tf_op jit(solution)/shard_map/ppermute | solution.py:352
  78.1 16.2 %collective-permute-start.18 = (bf16[2,256,256]{2,1,0:T(8,128)(2,1)S(1)}, bf16[2,256,256]{2,1,0:T(8,128)(2,1)S(1)}, u32[]{:S(2)}, u32[]{:S(2)}) collective-permute-start(bf16[2,256,256]{2,1,0:T(8,128)(2,1)S(1)} %collective-permute-done.17.refs_1_), channel_id=1, source_target_pairs={{0,4},{1,5},{2,6},{3,7},{4,0},{5,1},{6,2},{7,3},{8,12},{9,13},{10,... | collective-permute-start | bytes 786440 | tf_op jit(solution)/shard_map/ppermute | solution.py:362
  79.8 15.5 %collective-permute-start.20 = (bf16[2,256,256]{2,1,0:T(8,128)(2,1)S(1)}, bf16[2,256,256]{2,1,0:T(8,128)(2,1)S(1)}, u32[]{:S(2)}, u32[]{:S(2)}) collective-permute-start(bf16[2,256,256]{2,1,0:T(8,128)(2,1)S(1)} %collective-permute-done.19.refs_3_), channel_id=1, source_target_pairs={{0,2},{1,3},{2,0},{3,1},{4,6},{5,7},{6,4},{7,5},{8,10},{9,11},{10,... | collective-permute-start | bytes 786440 | tf_op jit(solution)/shard_map/ppermute | solution.py:362
  81.3 19.7 %collective-permute-start.22 = (bf16[2,256,256]{2,1,0:T(8,128)(2,1)S(1)}, bf16[2,256,256]{2,1,0:T(8,128)(2,1)S(1)}, u32[]{:S(2)}, u32[]{:S(2)}) collective-permute-start(bf16[2,256,256]{2,1,0:T(8,128)(2,1)S(1)} %collective-permute-done.21.refs_2_), channel_id=1, source_target_pairs={{0,8},{1,9},{2,10},{3,11},{4,12},{5,13},{6,14},{7,15},{8,0},{9,1},... | collective-permute-start | bytes 786440 | tf_op jit(solution)/shard_map/ppermute | solution.py:362
  82.7 1.6 %copy-start.9 = (f32[2,2048,128]{2,1,0:T(8,128)S(1)}, f32[2,2048,128]{2,1,0:T(8,128)}, u32[]{:S(2)}) copy-start(f32[2,2048,128]{2,1,0:T(8,128)} %copy-done.8) | copy-start | bytes 6291460
  101.7 1.8 %collective-permute-start.25 = (bf16[768,256]{1,0:T(8,128)(2,1)S(1)}, bf16[768,256]{1,0:T(8,128)(2,1)S(1)}, u32[]{:S(2)}, u32[]{:S(2)}) collective-permute-start(bf16[768,256]{1,0:T(8,128)(2,1)S(1)} %pick_other.4), channel_id=1, source_target_pairs={{0,1},{1,0},{2,3},{3,2},{4,5},{5,4},{6,7},{7,6},{8,9},{9,8},{10,11... | collective-permute-start | bytes 1179656 | tf_op jit(solution)/shard_map/ppermute | solution.py:352
  101.8 8.7 %collective-permute-start.24 = (bf16[2,256,256]{2,1,0:T(8,128)(2,1)S(1)}, bf16[2,256,256]{2,1,0:T(8,128)(2,1)S(1)}, u32[]{:S(2)}, u32[]{:S(2)}) collective-permute-start(bf16[2,256,256]{2,1,0:T(8,128)(2,1)S(1)} %collective-permute-done.22.refs_2_), channel_id=1, source_target_pairs={{0,2},{1,3},{2,0},{3,1},{4,6},{5,7},{6,4},{7,5},{8,10},{9,11},{10,... | collective-permute-start | bytes 786440 | tf_op jit(solution)/shard_map/ppermute | solution.py:362
  108.4 1.3 %copy-start.6 = (f32[2,2048,128]{2,1,0:T(8,128)}, f32[2,2048,128]{2,1,0:T(8,128)S(1)}, u32[]{:S(2)}) copy-start(f32[2,2048,128]{2,1,0:T(8,128)S(1)} %prefix_keys.4.loaded_ref) | copy-start | bytes 6291460
  111.2 8.3 %collective-permute-start.26 = (bf16[256,256]{1,0:T(8,128)(2,1)S(1)}, bf16[256,256]{1,0:T(8,128)(2,1)S(1)}, u32[]{:S(2)}, u32[]{:S(2)}) collective-permute-start(bf16[256,256]{1,0:T(8,128)(2,1)S(1)} %pick_other.5), channel_id=1, source_target_pairs={{0,1},{1,0},{2,3},{3,2},{4,5},{5,4},{6,7},{7,6},{8,9},{9,8},{10,11... | collective-permute-start | bytes 393224 | tf_op jit(solution)/shard_map/ppermute | solution.py:352
  111.3 1.6 %copy-start.7 = (f32[2,2048,128]{2,1,0:T(8,128)S(1)}, f32[2,2048,128]{2,1,0:T(8,128)}, u32[]{:S(2)}) copy-start(f32[2,2048,128]{2,1,0:T(8,128)} %copy-done.6) | copy-start | bytes 6291460
  (2 other events, 2.2 us)

commit v18 on v17

--- a/solution.py
+++ b/solution.py
@@ -11,7 +11,7 @@
 DEAD_MARK = 1024.0
 DEAD_ABOVE = 512.0
 NEG = -1e30
-CHUNK = 1024
+CHUNK = 1280
 ROWS = 256
 PARAMS = pltpu.CompilerParams(vmem_limit_bytes=44 * 1024 * 1024)
 COPY_PARAMS = pltpu.CompilerParams(vmem_limit_bytes=62 * 1024 * 1024)
@@ -175,10 +175,10 @@
         )
 
     def stores(entry, source):
-        rows = parts[0].shape[1]
+        early = parts[0].shape[1]
         return [
             pltpu.make_async_copy(
-                source.at[pl.ds(place * rows, rows)],
+                source.at[pl.ds(place * early, part.shape[1])],
                 part.at[target_ref[0, entry]],
                 out_sems.at[place, entry],
             )
@@ -219,8 +219,7 @@
     )(rows, *after)
 
 
-def stage_kernel(owner_ref, reader_ref, kept_ref, swapped_ref, *refs):
-    mine_ref, other_ref, known_away_ref, away_ref, same_ref, *refs = refs
+def stage_kernel(owner_ref, kept_ref, swapped_ref, *refs):
     outs, (sought_ref, known_ref, in_sems, out_sems) = refs[:-4], refs[-4:]
     chips, sought = sought_ref.shape[:2]
     replicas = 4 * chips
@@ -255,16 +254,6 @@
         for step in range(chips):
             start(step, sought, core == 1)
 
-    for place_ref, wanted in ((mine_ref, reader_ref[me]), (other_ref, reader_ref[me ^ 1])):
-        ahead = jnp.where(wanted < known, wanted + 1, wanted)
-        place_ref[0] = jnp.where(wanted == known, 0, ahead)
-    known_away_ref[0] = chip ^ (chips - 1)
-    for place, owner in enumerate([replicas - 1, *owners]):
-        if place:
-            away_ref[place - 1] = chip ^ (owner // 2 % chips)
-        same = owner // (replicas // 2) == me // (replicas // 2)
-        same_ref[place] = jnp.where(same, 1, 0)
-
     for step in range(chips):
         for prefix in range(sought):
             load(kept_ref, step, prefix).wait()
@@ -293,14 +282,12 @@
     swapped = swapped.reshape(split.shape)
     pieces = jax.ShapeDtypeStruct((owners.shape[0] - 1, *split.shape[2:]), split.dtype)
     piece = jax.ShapeDtypeStruct((1, *split.shape[2:]), split.dtype)
-    small = (1, 1, 1, prefixes - 1, prefixes)
-    mine, other, known_away, away, same_half, *staged = pl.pallas_call(
+    staged = pl.pallas_call(
         stage_kernel,
-        out_shape=tuple(jax.ShapeDtypeStruct((count,), jnp.int32) for count in small)
-        + (pieces,) * chips
+        out_shape=(pieces,) * chips
         + (piece,) * chips,
-        in_specs=[IN_SMEM] * 2 + [IN_HBM] * 2,
-        out_specs=(IN_SMEM,) * len(small) + (IN_HBM,) * (2 * chips),
+        in_specs=[IN_SMEM] + [IN_HBM] * 2,
+        out_specs=(IN_HBM,) * (2 * chips),
         scratch_shapes=[
             pltpu.VMEM((chips, *pieces.shape), split.dtype),
             pltpu.VMEM((chips, *piece.shape), split.dtype),
@@ -309,7 +296,20 @@
         ],
         compiler_params=COPY_PARAMS,
         name="stage_prefix",
-    )(owners, readers, split, swapped)
+    )(owners, split, swapped)
+
+    me = lax.axis_index("replica")
+    chip = me // 2 % chips
+    owners = gate(owners, staged[0])
+    ids = jnp.arange(prefixes, dtype=jnp.int32)
+    known = jnp.sum(jnp.where(owners == replicas - 1, ids, 0))
+    sought = jnp.where(ids[:-1] >= known, owners[1:], owners[:-1])
+    away, known_away = chip ^ (sought // 2 % chips), (chip ^ (chips - 1))[None]
+    held_by = jnp.concatenate([jnp.full((1,), replicas - 1, jnp.int32), sought])
+    same_half = held_by // half == me // half
+    wanted = jnp.stack([readers[me], readers[me ^ 1]])
+    place = jnp.where(wanted == known, 0, wanted + (wanted < known))
+    mine, other = place[:1], place[1:]
 
     def to_peers(staged, senders):
         return [
@@ -337,7 +337,7 @@
         (passed, passed_known, fold_moved(arrived, local))
     )
     held = jnp.where(
-        (same_half == 1)[:, None, None],
+        same_half[:, None, None],
         jnp.concatenate([found_known, found]),
         jnp.concatenate([passed_known, passed]),
     )
@@ -418,8 +418,12 @@
     ]
 
     entries = mig_target.shape[1]
-    half_block = (replicas, kv_pool.shape[1] // 2, kv_pool.shape[2])
-    slots = (jax.ShapeDtypeStruct(half_block, kv_pool.dtype),) * 2
+    block = kv_pool.shape[1]
+    early = block * 5 // 8
+    slots = tuple(
+        jax.ShapeDtypeStruct((replicas, rows, kv_pool.shape[2]), kv_pool.dtype)
+        for rows in (early, block - early)
+    )
     outgoing = pl.pallas_call(
         pack_kernel,
         out_shape=slots,

time: 125 us -> 133 us (1.064)
  between operations: 9.93 us -> 3.83 us
  waiting for transfers between devices: 14.4 us -> 19.9 us
  local copies, waits for them, and re-layouts: 8.38 us -> 12.4 us
  other arithmetic: 0.21 us -> 3.05 us
  starting transfers between devices: 49.1 us -> 51.4 us
    ppermute x14, waiting for transfers between devices: 3.82 us -> 9.95 us  [to_peers(): lax.ppermute(rows, 'replica', [(i, i ^ 2 * step) for i in senders])]
    unnamed x42 -> x47, local copies, waits for them, and re-layouts: 8.38 us -> 10.6 us
    select_n x1 -> x2, other arithmetic: 0.1 us -> 2.05 us  [the longest x1 1.95 us: multicast(): place = jnp.where(wanted == known, 0, wanted + (wanted < known))]
    ppermute x14, starting transfers between devices: 16.4 us -> 18.2 us  [to_peers(): lax.ppermute(rows, 'replica', [(i, i ^ 2 * step) for i in senders])]
    ppermute x7, starting transfers between devices: 11 us -> 12.8 us  [gather_step(): return lax.ppermute(gathered[step ^ 1 << last], 'replica', pairs)]
  transfers between devices with their start and end apart: 29 -> 29, of which waited for: 8 -> 9; matrix products, arithmetic and copies ran while one was open for 0% -> 4% of each run, Pallas kernels for 30% -> 28%
where the time goes in v18:
time: 133 us; the launch traced here: 132 us
  starting transfers between devices  51.4 us (39%)
  Pallas kernels  41.2 us (31%)
  waiting for transfers between devices  19.9 us (15%)
  local copies, waits for them, and re-layouts  12.4 us (9%)
  between operations  3.83 us (3%)
  other arithmetic  3.05 us (2%)
    ppermute x14, starting transfers between devices, to_peers(): lax.ppermute(rows, 'replica', [(i, i ^ 2 * step) for i in senders])  18.2 us
    pallas_call x3, Pallas kernels, fold_prefix(): pl.pallas_call(functools.partial(prefix_kernel, factor, last, len(pieces)...  15.6 us
    pallas_call x2, Pallas kernels, fold_moved(): pl.pallas_call(functools.partial(moved_kernel, factor, steps), out_shape=...  13.9 us
    all_to_all x2, starting transfers between devices, send_blocks(): lax.all_to_all(rows, 'replica', split_axis=0, concat_axis=0, tiled=True)  13.8 us
    ppermute x7, starting transfers between devices, gather_step(): return lax.ppermute(gathered[step ^ 1 << last], 'replica', pairs)  12.8 us
    unnamed x47, local copies, waits for them, and re-layouts  10.6 us
    ppermute x14, waiting for transfers between devices, to_peers(): lax.ppermute(rows, 'replica', [(i, i ^ 2 * step) for i in senders])  9.95 us
    ppermute x7, waiting for transfers between devices, gather_step(): return lax.ppermute(gathered[step ^ 1 << last], 'replica', pairs)  9.79 us
  transfers between devices with their start and end apart: 29, of which 9 were waited for; matrix products, arithmetic and copies ran while one was open for 4% of the time, Pallas kernels for 28%

profile of v18, /device:TPU:0, one launch (start us, length us, event | category | flops | bytes accessed | tf_op | source)
XLA Modules:
  0.0 131.8 jit_solution(7559255806062648441)
XLA Ops:
  0.0 1.2 copy.19.owner_ref.refs_0_
  2.3 3.9 %pack_moved.1 = (bf16[32,80,256]{2,1,0:T(8,128)(2,1)}, bf16[32,48,256]{2,1,0:T(8,128)(2,1)}) custom-call(s32[1,32]{1,0:T(1,128)} %target_ref.1, s32[1,32]{1,0:T(1,128)} %block_ref.1, s32[1]{0:T(128)S(6)} %copy.18.count_ref, bf16[32,128,256]{2,1,0:T(8,128)(2,1)} %pool_ref.1), custom_call_target="tpu_custom_call" | custom-call | tf_op jit(solution)/shard_map/pack_moved/pallas_call | solution.py:427
  6.2 7.0 %all-to-all-start = ((bf16[32,80,256]{2,1,0:T(8,128)(2,1)}), bf16[32,80,256]{2,1,0:T(8,128)(2,1)S(1)}, u32[]{:S(2)}, u32[]{:S(2)}) async-start(bf16[32,80,256]{2,1,0:T(8,128)(2,1)} %get-tuple-element.73), calls=%async_computation | async-start | bytes 2621440 | tf_op jit(solution)/shard_map/all_to_all | solution.py:348
  13.9 3.1 %stage_prefix.1 = (bf16[1,256,256]{2,1,0:T(8,128)(2,1)}, bf16[1,256,256]{2,1,0:T(8,128)(2,1)}, bf16[1,256,256]{2,1,0:T(8,128)(2,1)}, bf16[1,256,256]{2,1,0:T(8,1...) custom-call(s32[2]{0:T(128)} %copy.19.owner_ref.refs_0_, ...), custom_call_target="tpu_custom_call" | custom-call | tf_op jit(solution)/shard_map/stage_prefix/pallas_call | solution.py:285
  17.0 1.8 %collective-permute-start.1 = (bf16[1,256,256]{2,1,0:T(8,128)(2,1)}, bf16[1,256,256]{2,1,0:T(8,128)(2,1)S(1)}, u32[]{:S(2)}, u32[]{:S(2)}) collective-permute-start(bf16[1,256,256]{2,1,0:T(8,128)(2,1)} %get-tuple-element.49), channel_id=1, source_target_pairs={{0,2},{1,3},{2,0},{3,1},{4,6},{5,7},{6,4},{7,5},{8,10},{9,11},{10,... | collective-permute-start | bytes 393224 | tf_op jit(solution)/shard_map/ppermute | solution.py:316
  18.8 2.4 %collective-permute-start.10 = (bf16[1,256,256]{2,1,0:T(8,128)(2,1)}, bf16[1,256,256]{2,1,0:T(8,128)(2,1)S(1)}, u32[]{:S(2)}, u32[]{:S(2)}) collective-permute-start(bf16[1,256,256]{2,1,0:T(8,128)(2,1)} %get-tuple-element.67), channel_id=1, source_target_pairs={{0,12},{1,13},{2,14},{3,15},{4,8},{5,9},{6,10},{7,11},{8,4},{9,5},... | collective-permute-start | bytes 393224 | tf_op jit(solution)/shard_map/ppermute | solution.py:316
  21.8 1.5 %collective-permute-start.12 = (bf16[1,256,256]{2,1,0:T(8,128)(2,1)}, bf16[1,256,256]{2,1,0:T(8,128)(2,1)S(1)}, u32[]{:S(2)}, u32[]{:S(2)}) collective-permute-start(bf16[1,256,256]{2,1,0:T(8,128)(2,1)} %get-tuple-element.69), channel_id=1, source_target_pairs={{0,8},{1,9},{2,10},{3,11},{4,12},{5,13},{6,14},{7,15},{8,0},{9,1},... | collective-permute-start | bytes 393224 | tf_op jit(solution)/shard_map/ppermute | solution.py:316
  23.2 1.5 %collective-permute-start.13 = (bf16[1,256,256]{2,1,0:T(8,128)(2,1)}, bf16[1,256,256]{2,1,0:T(8,128)(2,1)S(1)}, u32[]{:S(2)}, u32[]{:S(2)}) collective-permute-start(bf16[1,256,256]{2,1,0:T(8,128)(2,1)} %get-tuple-element.70), channel_id=1, source_target_pairs={{0,6},{1,7},{2,4},{3,5},{4,2},{5,3},{6,0},{7,1},{8,14},{9,15},{10,... | collective-permute-start | bytes 393224 | tf_op jit(solution)/shard_map/ppermute | solution.py:316
  24.7 0.9 copy-done
  25.6 0.9 copy-done.4
  26.6 2.8 %local_keys.1.loaded_ref = f32[2,2048,128]{2,1,0:T(8,128)S(1)} custom-call(s32[1]{0:T(128)S(6)} %copy.17.len_ref, bf16[256,1024]{1,0:T(8,128)(2,1)S(1)} %copy-done.3, bf16[256,256]{1,0:T(8,128)(2,1)S(1)} %copy-done.5, bf16[512,256]{1,0:T(8,128)(2,1)S(1)} %copy-done.4, bf16[1,256,256]{2,1,0:T(8,128)(2,1)S(1)} %copy-done), custom_call_target="tpu_custom_call" | custom-call | flops 2415919104 | bytes 393216 | tf_op jit(solution)/shard_map/local_keys/pallas_call | solution.py:442
  29.5 0.8 fusion.1
  30.2 1.5 %collective-permute-start.14 = (bf16[1,256,256]{2,1,0:T(8,128)(2,1)S(1)}, bf16[1,256,256]{2,1,0:T(8,128)(2,1)S(1)}, u32[]{:S(2)}, u32[]{:S(2)}) collective-permute-start(bf16[1,256,256]{2,1,0:T(8,128)(2,1)S(1)} %copy-done.22), channel_id=1, source_target_pairs={{0,4},{1,5},{2,6},{3,7},{4,0},{5,1},{6,2},{7,3},{8,12},{9,13},{10,... | collective-permute-start | bytes 393224 | tf_op jit(solution)/shard_map/ppermute | solution.py:316
  31.7 7.2 %collective-permute-done.10 = bf16[1,256,256]{2,1,0:T(8,128)(2,1)S(1)} collective-permute-done((bf16[1,256,256]{2,1,0:T(8,128)(2,1)}, bf16[1,256,256]{2,1,0:T(8,128)(2,1)S(1)}, u32[]{:S(2)}, u32[]{:S(2)}) %collective-permute-start.10) | collective-permute-done | bytes 131104 | tf_op jit(solution)/shard_map/ppermute | solution.py:316
  38.9 4.4 %collective-permute-start.9 = (bf16[1,256,256]{2,1,0:T(8,128)(2,1)S(1)}, bf16[1,256,256]{2,1,0:T(8,128)(2,1)S(1)}, u32[]{:S(2)}, u32[]{:S(2)}) collective-permute-start(bf16[1,256,256]{2,1,0:T(8,128)(2,1)S(1)} %copy-done.21), channel_id=1, source_target_pairs={{0,14},{1,15},{2,12},{3,13},{4,10},{5,11},{6,8},{7,9},{8,6},{9,7},... | collective-permute-start | bytes 393224 | tf_op jit(solution)/shard_map/ppermute | solution.py:316
  43.3 0.7 collective-permute-start.2
  44.0 2.3 %collective-permute-done.12 = bf16[1,256,256]{2,1,0:T(8,128)(2,1)S(1)} collective-permute-done((bf16[1,256,256]{2,1,0:T(8,128)(2,1)}, bf16[1,256,256]{2,1,0:T(8,128)(2,1)S(1)}, u32[]{:S(2)}, u32[]{:S(2)}) %collective-permute-start.12) | collective-permute-done | bytes 131104 | tf_op jit(solution)/shard_map/ppermute | solution.py:316
  49.7 0.7 collective-permute-start.4
  50.3 0.7 collective-permute-start.5
  51.4 0.7 collective-permute-start.6
  52.1 0.7 collective-permute-start.7
  52.8 0.7 collective-permute-start.8
  53.6 4.6 %collective-permute-start.15 = (bf16[1,256,256]{2,1,0:T(8,128)(2,1)S(1)}, bf16[1,256,256]{2,1,0:T(8,128)(2,1)S(1)}, u32[]{:S(2)}, u32[]{:S(2)}) collective-permute-start(bf16[1,256,256]{2,1,0:T(8,128)(2,1)S(1)} %select_select_fusion), channel_id=1, source_target_pairs={{0,16},{1,17},{2,18},{3,19},{4,20},{5,21},{6,22},{7,23},{8,24},{9,... | collective-permute-start | bytes 393224 | tf_op jit(solution)/shard_map/ppermute | solution.py:332
  58.3 1.3 collective-permute-start.16
  59.7 1.6 %copy-done.7 = f32[2,2048,128]{2,1,0:T(8,128)S(1)} copy-done((f32[2,2048,128]{2,1,0:T(8,128)S(1)}, f32[2,2048,128]{2,1,0:T(8,128)}, u32[]{:S(2)}) %copy-start.7) | copy-done | bytes 2097176
  61.2 8.4 %moved_keys.2.refs_5_ = f32[2,2048,128]{2,1,0:T(8,128)S(1)} custom-call(bf16[256,1024]{1,0:T(8,128)(2,1)S(1)} %copy-done.3, bf16[32,80,256]{2,1,0:T(8,128)(2,1)S(1)} %all-to-all-done.kv_ref, f32[2,2048,128]{2,1,0:T(8,128)S(1)} %copy-done.7), custom_call_target="tpu_custom_call" | custom-call | flops 8053063680 | bytes 1310720 | tf_op jit(solution)/shard_map/moved_keys/pallas_call | solution.py:464
  69.6 1.3 %copy-done.10 = f32[2,2048,128]{2,1,0:T(8,128)} copy-done((f32[2,2048,128]{2,1,0:T(8,128)}, f32[2,2048,128]{2,1,0:T(8,128)S(1)}, u32[]{:S(2)}) %copy-start.10) | copy-done | bytes 2097176
  71.1 2.3 %collective-permute-start.17 = (bf16[2,256,256]{2,1,0:T(8,128)(2,1)S(1)}, bf16[2,256,256]{2,1,0:T(8,128)(2,1)S(1)}, u32[]{:S(2)}, u32[]{:S(2)}) collective-permute-start(bf16[2,256,256]{2,1,0:T(8,128)(2,1)S(1)} %maximum_select_fusion.refs_0_), channel_id=1, source_target_pairs={{0,2},{1,3},{2,0},{3,1},{4,6},{5,7},{6,4},{7,5},{8,10},{9,11},{10,... | collective-permute-start | bytes 786440 | tf_op jit(solution)/shard_map/ppermute | solution.py:362
  73.4 4.4 %collective-permute-start.21 = (bf16[2,256,256]{2,1,0:T(8,128)(2,1)S(1)}, bf16[2,256,256]{2,1,0:T(8,128)(2,1)S(1)}, u32[]{:S(2)}, u32[]{:S(2)}) collective-permute-start(bf16[2,256,256]{2,1,0:T(8,128)(2,1)S(1)} %maximum_select_fusion.refs_0_), channel_id=1, source_target_pairs={{0,4},{1,5},{2,6},{3,7},{4,0},{5,1},{6,2},{7,3},{8,12},{9,13},{10,... | collective-permute-start | bytes 786440 | tf_op jit(solution)/shard_map/ppermute | solution.py:362
  78.4 2.0 %compare_select_fusion = s32[2]{0:T(128)S(1)} fusion(s32[1]{0:T(128)} %get-tuple-element.90, s32[1]{0:T(128)} %get-tuple-element.89, s32[]{:T(128)} %fusion.1), kind=kLoop, calls=%fused_computation.5 | loop fusion | flops 12 | bytes 20 | tf_op jit(solution)/shard_map/jit(_where)/select_n | solution.py:311
  80.9 1.4 %collective-permute-done.21.refs_2_ = bf16[2,256,256]{2,1,0:T(8,128)(2,1)S(1)} collective-permute-done((bf16[2,256,256]{2,1,0:T(8,128)(2,1)S(1)}, bf16[2,256,256]{2,1,0:T(8,128)(2,1)S(1)}, u32[]{:S(2)}, u32[]{:S(2)}) %collective-permute-start.21) | collective-permute-done | bytes 262176 | tf_op jit(solution)/shard_map/ppermute | solution.py:362
  82.3 0.7 pick_other.3
  83.0 6.8 %all-to-all-start.1 = ((bf16[32,48,256]{2,1,0:T(8,128)(2,1)}), bf16[32,48,256]{2,1,0:T(8,128)(2,1)S(1)}, u32[]{:S(2)}, u32[]{:S(2)}) async-start(bf16[32,48,256]{2,1,0:T(8,128)(2,1)} %gate.3), calls=%async_computation.1 | async-start | bytes 1572864 | tf_op jit(solution)/shard_map/all_to_all | solution.py:348
  89.8 1.7 %collective-permute-start.18 = (bf16[2,256,256]{2,1,0:T(8,128)(2,1)S(1)}, bf16[2,256,256]{2,1,0:T(8,128)(2,1)S(1)}, u32[]{:S(2)}, u32[]{:S(2)}) collective-permute-start(bf16[2,256,256]{2,1,0:T(8,128)(2,1)S(1)} %collective-permute-done.17.refs_1_), channel_id=1, source_target_pairs={{0,4},{1,5},{2,6},{3,7},{4,0},{5,1},{6,2},{7,3},{8,12},{9,13},{10,... | collective-permute-start | bytes 786440 | tf_op jit(solution)/shard_map/ppermute | solution.py:362
  91.5 1.5 %collective-permute-start.20 = (bf16[2,256,256]{2,1,0:T(8,128)(2,1)S(1)}, bf16[2,256,256]{2,1,0:T(8,128)(2,1)S(1)}, u32[]{:S(2)}, u32[]{:S(2)}) collective-permute-start(bf16[2,256,256]{2,1,0:T(8,128)(2,1)S(1)} %collective-permute-done.19.refs_3_), channel_id=1, source_target_pairs={{0,2},{1,3},{2,0},{3,1},{4,6},{5,7},{6,4},{7,5},{8,10},{9,11},{10,... | collective-permute-start | bytes 786440 | tf_op jit(solution)/shard_map/ppermute | solution.py:362
  92.9 1.5 %collective-permute-start.22 = (bf16[2,256,256]{2,1,0:T(8,128)(2,1)S(1)}, bf16[2,256,256]{2,1,0:T(8,128)(2,1)S(1)}, u32[]{:S(2)}, u32[]{:S(2)}) collective-permute-start(bf16[2,256,256]{2,1,0:T(8,128)(2,1)S(1)} %collective-permute-done.21.refs_2_), channel_id=1, source_target_pairs={{0,8},{1,9},{2,10},{3,11},{4,12},{5,13},{6,14},{7,15},{8,0},{9,1},... | collective-permute-start | bytes 786440 | tf_op jit(solution)/shard_map/ppermute | solution.py:362
  94.4 1.6 %copy-done.11 = f32[2,2048,128]{2,1,0:T(8,128)S(1)} copy-done((f32[2,2048,128]{2,1,0:T(8,128)S(1)}, f32[2,2048,128]{2,1,0:T(8,128)}, u32[]{:S(2)}) %copy-start.11) | copy-done | bytes 2097176
  96.0 7.1 %prefix_keys.3.refs_4_ = f32[2,2048,128]{2,1,0:T(8,128)S(1)} custom-call(s32[1]{0:T(128)} %get-tuple-element.86.which_ref, bf16[256,1024]{1,0:T(8,128)(2,1)S(1)} %copy-done.3, bf16[2,256,256]{2,1,0:T(8,128)(2,1)S(1)} %maximum_select_fusion.refs_0_, bf16[2,256,256]{2,1,0:T(8,128)(2,1)S(1)} %collective-permute-done.17.refs_1_, ...), custom_call_target="tpu_custom_call" | custom-call | flops 6442450944 | bytes 1048576 | tf_op jit(solution)/shard_map/prefix_keys/pallas_call | solution.py:488
  103.2 2.1 %collective-permute-done.18.refs_0_ = bf16[2,256,256]{2,1,0:T(8,128)(2,1)S(1)} collective-permute-done((bf16[2,256,256]{2,1,0:T(8,128)(2,1)S(1)}, bf16[2,256,256]{2,1,0:T(8,128)(2,1)S(1)}, u32[]{:S(2)}, u32[]{:S(2)}) %collective-permute-start.18) | collective-permute-done | bytes 262176 | tf_op jit(solution)/shard_map/ppermute | solution.py:362
  105.5 5.3 %collective-permute-done.22.refs_2_ = bf16[2,256,256]{2,1,0:T(8,128)(2,1)S(1)} collective-permute-done((bf16[2,256,256]{2,1,0:T(8,128)(2,1)S(1)}, bf16[2,256,256]{2,1,0:T(8,128)(2,1)S(1)}, u32[]{:S(2)}, u32[]{:S(2)}) %collective-permute-start.22) | collective-permute-done | bytes 262176 | tf_op jit(solution)/shard_map/ppermute | solution.py:362
  110.8 0.7 pick_other.4
  111.5 1.5 %collective-permute-start.24 = (bf16[2,256,256]{2,1,0:T(8,128)(2,1)S(1)}, bf16[2,256,256]{2,1,0:T(8,128)(2,1)S(1)}, u32[]{:S(2)}, u32[]{:S(2)}) collective-permute-start(bf16[2,256,256]{2,1,0:T(8,128)(2,1)S(1)} %collective-permute-done.22.refs_2_), channel_id=1, source_target_pairs={{0,2},{1,3},{2,0},{3,1},{4,6},{5,7},{6,4},{7,5},{8,10},{9,11},{10,... | collective-permute-start | bytes 786440 | tf_op jit(solution)/shard_map/ppermute | solution.py:362
  113.2 4.8 %prefix_keys.4.loaded_ref = f32[2,2048,128]{2,1,0:T(8,128)S(1)} custom-call(s32[1]{0:T(128)} %get-tuple-element.86.which_ref, bf16[256,1024]{1,0:T(8,128)(2,1)S(1)} %copy-done.3, bf16[2,256,256]{2,1,0:T(8,128)(2,1)S(1)} %collective-permute-done.18.refs_0_, bf16[2,256,256]{2,1,0:T(8,128)(2,1)S(1)} %collective-permute-done.20.refs_1_, ...), custom_call_target="tpu_custom_call" | custom-call | flops 4831838208 | bytes 786432 | tf_op jit(solution)/shard_map/prefix_keys/pallas_call | solution.py:488
  118.1 1.4 %copy-done.8 = f32[2,2048,128]{2,1,0:T(8,128)} copy-done((f32[2,2048,128]{2,1,0:T(8,128)}, f32[2,2048,128]{2,1,0:T(8,128)S(1)}, u32[]{:S(2)}) %copy-start.8) | copy-done | bytes 2097176
  119.4 0.8 collective-permute-done.24.refs_0_
  121.0 1.6 %copy-done.9 = f32[2,2048,128]{2,1,0:T(8,128)S(1)} copy-done((f32[2,2048,128]{2,1,0:T(8,128)S(1)}, f32[2,2048,128]{2,1,0:T(8,128)}, u32[]{:S(2)}) %copy-start.9) | copy-done | bytes 2097176
  122.6 5.5 %moved_keys.3.refs_2_ = f32[2,2048,128]{2,1,0:T(8,128)S(1)} custom-call(bf16[256,1024]{1,0:T(8,128)(2,1)S(1)} %copy-done.3, bf16[32,48,256]{2,1,0:T(8,128)(2,1)S(1)} %all-to-all-done.1.kv_ref, f32[2,2048,128]{2,1,0:T(8,128)S(1)} %copy-done.9), custom_call_target="tpu_custom_call" | custom-call | flops 4831838208 | bytes 786432 | tf_op jit(solution)/shard_map/moved_keys/pallas_call | solution.py:464
  128.1 3.7 %prefix_keys.5 = bf16[256,1024]{1,0:T(8,128)(2,1)} custom-call(s32[1]{0:T(128)} %get-tuple-element.86.which_ref, bf16[256,1024]{1,0:T(8,128)(2,1)S(1)} %copy-done.3, bf16[2,256,256]{2,1,0:T(8,128)(2,1)S(1)} %collective-permute-done.24.refs_0_, bf16[256,256]{1,0:T(8,128)(2,1)S(1)} %collective-permute-done.26.refs_1_, f32[2,2048,128]{2,1,0:T(8,128)S(1)} %moved_keys.3.refs_2_), custom_call_target="tpu_custom_call" | custom-call | flops 1610612736 | bytes 262144 | tf_op jit(solution)/shard_map/prefix_keys/pallas_call | solution.py:488
  (80 shorter events, 5.7 us)
Async XLA Ops:
  1.2 5.0 %collective-permute-start = (bf16[4096,256]{1,0:T(8,128)(2,1)}, bf16[4096,256]{1,0:T(8,128)(2,1)}, u32[]{:S(2)}, u32[]{:S(2)}) collective-permute-start(bf16[4096,256]{1,0:T(8,128)(2,1)} %param.15), channel_id=1, source_target_pairs={{0,1},{1,0},{2,3},{3,2},{4,5},{5,4},{6,7},{7,6},{8,9},{9,8},{10,11... | collective-permute-start | bytes 6291464 | tf_op jit(solution)/shard_map/ppermute | solution.py:352
  6.2 53.5 %all-to-all-start = ((bf16[32,80,256]{2,1,0:T(8,128)(2,1)}), bf16[32,80,256]{2,1,0:T(8,128)(2,1)S(1)}, u32[]{:S(2)}, u32[]{:S(2)}) async-start(bf16[32,80,256]{2,1,0:T(8,128)(2,1)} %get-tuple-element.73), calls=%async_computation | async-start | bytes 2621440 | tf_op jit(solution)/shard_map/all_to_all | solution.py:348
  13.9 10.8 %copy-start.3 = (bf16[256,1024]{1,0:T(8,128)(2,1)S(1)}, bf16[256,1024]{1,0:T(8,128)(2,1)}, u32[]{:S(2)}) copy-start(bf16[256,1024]{1,0:T(8,128)(2,1)} %q_ref.11) | copy-start | bytes 1572868
  13.9 10.8 %copy-start.5 = (bf16[256,256]{1,0:T(8,128)(2,1)S(1)}, bf16[256,256]{1,0:T(8,128)(2,1)}, u32[]{:S(2)}) copy-start(bf16[256,256]{1,0:T(8,128)(2,1)} %suffix_ref.1) | copy-start | bytes 393220
  17.0 13.2 %collective-permute-start.1 = (bf16[1,256,256]{2,1,0:T(8,128)(2,1)}, bf16[1,256,256]{2,1,0:T(8,128)(2,1)S(1)}, u32[]{:S(2)}, u32[]{:S(2)}) collective-permute-start(bf16[1,256,256]{2,1,0:T(8,128)(2,1)} %get-tuple-element.49), channel_id=1, source_target_pairs={{0,2},{1,3},{2,0},{3,1},{4,6},{5,7},{6,4},{7,5},{8,10},{9,11},{10,... | collective-permute-start | bytes 393224 | tf_op jit(solution)/shard_map/ppermute | solution.py:316
  18.8 20.1 %collective-permute-start.10 = (bf16[1,256,256]{2,1,0:T(8,128)(2,1)}, bf16[1,256,256]{2,1,0:T(8,128)(2,1)S(1)}, u32[]{:S(2)}, u32[]{:S(2)}) collective-permute-start(bf16[1,256,256]{2,1,0:T(8,128)(2,1)} %get-tuple-element.67), channel_id=1, source_target_pairs={{0,12},{1,13},{2,14},{3,15},{4,8},{5,9},{6,10},{7,11},{8,4},{9,5},... | collective-permute-start | bytes 393224 | tf_op jit(solution)/shard_map/ppermute | solution.py:316
  21.2 22.1 %collective-permute-start.11 = (bf16[1,256,256]{2,1,0:T(8,128)(2,1)}, bf16[1,256,256]{2,1,0:T(8,128)(2,1)S(1)}, u32[]{:S(2)}, u32[]{:S(2)}) collective-permute-start(bf16[1,256,256]{2,1,0:T(8,128)(2,1)} %get-tuple-element.68), channel_id=1, source_target_pairs={{0,10},{1,11},{2,8},{3,9},{4,14},{5,15},{6,12},{7,13},{8,2},{9,3},... | collective-permute-start | bytes 393224 | tf_op jit(solution)/shard_map/ppermute | solution.py:316
  21.8 24.5 %collective-permute-start.12 = (bf16[1,256,256]{2,1,0:T(8,128)(2,1)}, bf16[1,256,256]{2,1,0:T(8,128)(2,1)S(1)}, u32[]{:S(2)}, u32[]{:S(2)}) collective-permute-start(bf16[1,256,256]{2,1,0:T(8,128)(2,1)} %get-tuple-element.69), channel_id=1, source_target_pairs={{0,8},{1,9},{2,10},{3,11},{4,12},{5,13},{6,14},{7,15},{8,0},{9,1},... | collective-permute-start | bytes 393224 | tf_op jit(solution)/shard_map/ppermute | solution.py:316
  23.2 26.4 %collective-permute-start.13 = (bf16[1,256,256]{2,1,0:T(8,128)(2,1)}, bf16[1,256,256]{2,1,0:T(8,128)(2,1)S(1)}, u32[]{:S(2)}, u32[]{:S(2)}) collective-permute-start(bf16[1,256,256]{2,1,0:T(8,128)(2,1)} %get-tuple-element.70), channel_id=1, source_target_pairs={{0,6},{1,7},{2,4},{3,5},{4,2},{5,3},{6,0},{7,1},{8,14},{9,15},{10,... | collective-permute-start | bytes 393224 | tf_op jit(solution)/shard_map/ppermute | solution.py:316
  26.6 2.9 %copy-start.1 = (bf16[1,256,256]{2,1,0:T(8,128)(2,1)S(1)}, bf16[1,256,256]{2,1,0:T(8,128)(2,1)}, u32[]{:S(2)}) copy-start(bf16[1,256,256]{2,1,0:T(8,128)(2,1)} %get-tuple-element.48.refs_1_.after_ref) | copy-start | bytes 393220
  26.6 2.9 %copy-start.2 = (s32[2]{0:T(128)S(1)}, s32[2]{0:T(128)}, u32[]{:S(2)}) copy-start(s32[2]{0:T(128)} %copy.19.owner_ref.refs_0_) | copy-start | bytes 28
  26.6 3.7 %copy-start.22 = (bf16[1,256,256]{2,1,0:T(8,128)(2,1)S(1)}, bf16[1,256,256]{2,1,0:T(8,128)(2,1)}, u32[]{:S(2)}) copy-start(bf16[1,256,256]{2,1,0:T(8,128)(2,1)} %get-tuple-element.71) | copy-start | bytes 393220
  26.6 12.4 %copy-start.21 = (bf16[1,256,256]{2,1,0:T(8,128)(2,1)S(1)}, bf16[1,256,256]{2,1,0:T(8,128)(2,1)}, u32[]{:S(2)}) copy-start(bf16[1,256,256]{2,1,0:T(8,128)(2,1)} %get-tuple-element.66) | copy-start | bytes 393220
  26.6 16.8 %copy-start.20 = (bf16[1,256,256]{2,1,0:T(8,128)(2,1)S(1)}, bf16[1,256,256]{2,1,0:T(8,128)(2,1)}, u32[]{:S(2)}) copy-start(bf16[1,256,256]{2,1,0:T(8,128)(2,1)} %get-tuple-element.58) | copy-start | bytes 393220
  26.6 19.7 %copy-start.19 = (bf16[1,256,256]{2,1,0:T(8,128)(2,1)S(1)}, bf16[1,256,256]{2,1,0:T(8,128)(2,1)}, u32[]{:S(2)}) copy-start(bf16[1,256,256]{2,1,0:T(8,128)(2,1)} %get-tuple-element.59) | copy-start | bytes 393220
  26.6 23.1 %copy-start.18 = (bf16[1,256,256]{2,1,0:T(8,128)(2,1)S(1)}, bf16[1,256,256]{2,1,0:T(8,128)(2,1)}, u32[]{:S(2)}) copy-start(bf16[1,256,256]{2,1,0:T(8,128)(2,1)} %get-tuple-element.60) | copy-start | bytes 393220
  26.6 23.7 %copy-start.17 = (bf16[1,256,256]{2,1,0:T(8,128)(2,1)S(1)}, bf16[1,256,256]{2,1,0:T(8,128)(2,1)}, u32[]{:S(2)}) copy-start(bf16[1,256,256]{2,1,0:T(8,128)(2,1)} %get-tuple-element.61) | copy-start | bytes 393220
  26.6 24.8 %copy-start.16 = (bf16[1,256,256]{2,1,0:T(8,128)(2,1)S(1)}, bf16[1,256,256]{2,1,0:T(8,128)(2,1)}, u32[]{:S(2)}) copy-start(bf16[1,256,256]{2,1,0:T(8,128)(2,1)} %get-tuple-element.62) | copy-start | bytes 393220
  26.6 25.5 %copy-start.15 = (bf16[1,256,256]{2,1,0:T(8,128)(2,1)S(1)}, bf16[1,256,256]{2,1,0:T(8,128)(2,1)}, u32[]{:S(2)}) copy-start(bf16[1,256,256]{2,1,0:T(8,128)(2,1)} %get-tuple-element.63) | copy-start | bytes 393220
  26.6 26.2 %copy-start.14 = (bf16[1,256,256]{2,1,0:T(8,128)(2,1)S(1)}, bf16[1,256,256]{2,1,0:T(8,128)(2,1)}, u32[]{:S(2)}) copy-start(bf16[1,256,256]{2,1,0:T(8,128)(2,1)} %get-tuple-element.64) | copy-start | bytes 393220
  26.6 31.6 %copy-start.12 = (bf16[1,256,256]{2,1,0:T(8,128)(2,1)S(1)}, bf16[1,256,256]{2,1,0:T(8,128)(2,1)}, u32[]{:S(2)}) copy-start(bf16[1,256,256]{2,1,0:T(8,128)(2,1)} %get-tuple-element.65) | copy-start | bytes 393220
  29.4 28.9 %copy-start.6 = (f32[2,2048,128]{2,1,0:T(8,128)}, f32[2,2048,128]{2,1,0:T(8,128)S(1)}, u32[]{:S(2)}) copy-start(f32[2,2048,128]{2,1,0:T(8,128)S(1)} %local_keys.1.loaded_ref) | copy-start | bytes 6291460
  30.2 20.1 %collective-permute-start.14 = (bf16[1,256,256]{2,1,0:T(8,128)(2,1)S(1)}, bf16[1,256,256]{2,1,0:T(8,128)(2,1)S(1)}, u32[]{:S(2)}, u32[]{:S(2)}) collective-permute-start(bf16[1,256,256]{2,1,0:T(8,128)(2,1)S(1)} %copy-done.22), channel_id=1, source_target_pairs={{0,4},{1,5},{2,6},{3,7},{4,0},{5,1},{6,2},{7,3},{8,12},{9,13},{10,... | collective-permute-start | bytes 393224 | tf_op jit(solution)/shard_map/ppermute | solution.py:316
  38.9 12.5 %collective-permute-start.9 = (bf16[1,256,256]{2,1,0:T(8,128)(2,1)S(1)}, bf16[1,256,256]{2,1,0:T(8,128)(2,1)S(1)}, u32[]{:S(2)}, u32[]{:S(2)}) collective-permute-start(bf16[1,256,256]{2,1,0:T(8,128)(2,1)S(1)} %copy-done.21), channel_id=1, source_target_pairs={{0,14},{1,15},{2,12},{3,13},{4,10},{5,11},{6,8},{7,9},{8,6},{9,7},... | collective-permute-start | bytes 393224 | tf_op jit(solution)/shard_map/ppermute | solution.py:316
  43.3 8.8 %collective-permute-start.2 = (bf16[1,256,256]{2,1,0:T(8,128)(2,1)S(1)}, bf16[1,256,256]{2,1,0:T(8,128)(2,1)S(1)}, u32[]{:S(2)}, u32[]{:S(2)}) collective-permute-start(bf16[1,256,256]{2,1,0:T(8,128)(2,1)S(1)} %copy-done.20), channel_id=1, source_target_pairs={{30,16},{31,17}} | collective-permute-start | bytes 393224 | tf_op jit(solution)/shard_map/ppermute | solution.py:316
  46.3 6.5 %collective-permute-start.3 = (bf16[1,256,256]{2,1,0:T(8,128)(2,1)S(1)}, bf16[1,256,256]{2,1,0:T(8,128)(2,1)S(1)}, u32[]{:S(2)}, u32[]{:S(2)}) collective-permute-start(bf16[1,256,256]{2,1,0:T(8,128)(2,1)S(1)} %copy-done.19), channel_id=1, source_target_pairs={{30,18},{31,19}} | collective-permute-start | bytes 393224 | tf_op jit(solution)/shard_map/ppermute | solution.py:316
  49.7 3.9 %collective-permute-start.4 = (bf16[1,256,256]{2,1,0:T(8,128)(2,1)S(1)}, bf16[1,256,256]{2,1,0:T(8,128)(2,1)S(1)}, u32[]{:S(2)}, u32[]{:S(2)}) collective-permute-start(bf16[1,256,256]{2,1,0:T(8,128)(2,1)S(1)} %copy-done.18), channel_id=1, source_target_pairs={{30,20},{31,21}} | collective-permute-start | bytes 393224 | tf_op jit(solution)/shard_map/ppermute | solution.py:316
  50.3 7.9 %collective-permute-start.5 = (bf16[1,256,256]{2,1,0:T(8,128)(2,1)S(1)}, bf16[1,256,256]{2,1,0:T(8,128)(2,1)S(1)}, u32[]{:S(2)}, u32[]{:S(2)}) collective-permute-start(bf16[1,256,256]{2,1,0:T(8,128)(2,1)S(1)} %copy-done.17), channel_id=1, source_target_pairs={{30,22},{31,23}} | collective-permute-start | bytes 393224 | tf_op jit(solution)/shard_map/ppermute | solution.py:316
  51.4 6.8 %collective-permute-start.6 = (bf16[1,256,256]{2,1,0:T(8,128)(2,1)S(1)}, bf16[1,256,256]{2,1,0:T(8,128)(2,1)S(1)}, u32[]{:S(2)}, u32[]{:S(2)}) collective-permute-start(bf16[1,256,256]{2,1,0:T(8,128)(2,1)S(1)} %copy-done.16), channel_id=1, source_target_pairs={{30,24},{31,25}} | collective-permute-start | bytes 393224 | tf_op jit(solution)/shard_map/ppermute | solution.py:316
  52.1 6.1 %collective-permute-start.7 = (bf16[1,256,256]{2,1,0:T(8,128)(2,1)S(1)}, bf16[1,256,256]{2,1,0:T(8,128)(2,1)S(1)}, u32[]{:S(2)}, u32[]{:S(2)}) collective-permute-start(bf16[1,256,256]{2,1,0:T(8,128)(2,1)S(1)} %copy-done.15), channel_id=1, source_target_pairs={{30,26},{31,27}} | collective-permute-start | bytes 393224 | tf_op jit(solution)/shard_map/ppermute | solution.py:316
  52.8 5.4 %collective-permute-start.8 = (bf16[1,256,256]{2,1,0:T(8,128)(2,1)S(1)}, bf16[1,256,256]{2,1,0:T(8,128)(2,1)S(1)}, u32[]{:S(2)}, u32[]{:S(2)}) collective-permute-start(bf16[1,256,256]{2,1,0:T(8,128)(2,1)S(1)} %copy-done.14), channel_id=1, source_target_pairs={{30,28},{31,29}} | collective-permute-start | bytes 393224 | tf_op jit(solution)/shard_map/ppermute | solution.py:316
  53.6 17.4 %collective-permute-start.15 = (bf16[1,256,256]{2,1,0:T(8,128)(2,1)S(1)}, bf16[1,256,256]{2,1,0:T(8,128)(2,1)S(1)}, u32[]{:S(2)}, u32[]{:S(2)}) collective-permute-start(bf16[1,256,256]{2,1,0:T(8,128)(2,1)S(1)} %select_select_fusion), channel_id=1, source_target_pairs={{0,16},{1,17},{2,18},{3,19},{4,20},{5,21},{6,22},{7,23},{8,24},{9,... | collective-permute-start | bytes 393224 | tf_op jit(solution)/shard_map/ppermute | solution.py:332
  58.2 19.5 %copy-start.13 = (s32[32]{0:T(128)S(1)}, s32[32]{0:T(128)}, u32[]{:S(2)}) copy-start(s32[32]{0:T(128)} %param.17) | copy-start | bytes 388
  58.3 12.7 %collective-permute-start.16 = (bf16[1,256,256]{2,1,0:T(8,128)(2,1)S(1)}, bf16[1,256,256]{2,1,0:T(8,128)(2,1)S(1)}, u32[]{:S(2)}, u32[]{:S(2)}) collective-permute-start(bf16[1,256,256]{2,1,0:T(8,128)(2,1)S(1)} %select_select_fusion.1), channel_id=1, source_target_pairs={{16,0},{17,1},{18,2},{19,3},{20,4},{21,5},{22,6},{23,7},{24,8},{25... | collective-permute-start | bytes 393224 | tf_op jit(solution)/shard_map/ppermute | solution.py:334
  59.6 1.6 %copy-start.7 = (f32[2,2048,128]{2,1,0:T(8,128)S(1)}, f32[2,2048,128]{2,1,0:T(8,128)}, u32[]{:S(2)}) copy-start(f32[2,2048,128]{2,1,0:T(8,128)} %copy-done.6) | copy-start | bytes 6291460
  71.1 9.8 %collective-permute-start.17 = (bf16[2,256,256]{2,1,0:T(8,128)(2,1)S(1)}, bf16[2,256,256]{2,1,0:T(8,128)(2,1)S(1)}, u32[]{:S(2)}, u32[]{:S(2)}) collective-permute-start(bf16[2,256,256]{2,1,0:T(8,128)(2,1)S(1)} %maximum_select_fusion.refs_0_), channel_id=1, source_target_pairs={{0,2},{1,3},{2,0},{3,1},{4,6},{5,7},{6,4},{7,5},{8,10},{9,11},{10,... | collective-permute-start | bytes 786440 | tf_op jit(solution)/shard_map/ppermute | solution.py:362
  73.4 7.5 %collective-permute-start.19 = (bf16[2,256,256]{2,1,0:T(8,128)(2,1)S(1)}, bf16[2,256,256]{2,1,0:T(8,128)(2,1)S(1)}, u32[]{:S(2)}, u32[]{:S(2)}) collective-permute-start(bf16[2,256,256]{2,1,0:T(8,128)(2,1)S(1)} %maximum_select_fusion.refs_0_), channel_id=1, source_target_pairs={{0,8},{1,9},{2,10},{3,11},{4,12},{5,13},{6,14},{7,15},{8,0},{9,1},... | collective-permute-start | bytes 786440 | tf_op jit(solution)/shard_map/ppermute | solution.py:362
  73.4 8.9 %collective-permute-start.21 = (bf16[2,256,256]{2,1,0:T(8,128)(2,1)S(1)}, bf16[2,256,256]{2,1,0:T(8,128)(2,1)S(1)}, u32[]{:S(2)}, u32[]{:S(2)}) collective-permute-start(bf16[2,256,256]{2,1,0:T(8,128)(2,1)S(1)} %maximum_select_fusion.refs_0_), channel_id=1, source_target_pairs={{0,4},{1,5},{2,6},{3,7},{4,0},{5,1},{6,2},{7,3},{8,12},{9,13},{10,... | collective-permute-start | bytes 786440 | tf_op jit(solution)/shard_map/ppermute | solution.py:362
  83.0 11.5 %collective-permute-start.23 = (bf16[1024,256]{1,0:T(8,128)(2,1)S(1)}, bf16[1024,256]{1,0:T(8,128)(2,1)}, u32[]{:S(2)}, u32[]{:S(2)}) collective-permute-start(bf16[1024,256]{1,0:T(8,128)(2,1)S(1)} %pick_other.3), channel_id=1, source_target_pairs={{0,1},{1,0},{2,3},{3,2},{4,5},{5,4},{6,7},{7,6},{8,9},{9,8},{10,11... | collective-permute-start | bytes 1572872 | tf_op jit(solution)/shard_map/ppermute | solution.py:352
  83.0 37.9 %all-to-all-start.1 = ((bf16[32,48,256]{2,1,0:T(8,128)(2,1)}), bf16[32,48,256]{2,1,0:T(8,128)(2,1)S(1)}, u32[]{:S(2)}, u32[]{:S(2)}) async-start(bf16[32,48,256]{2,1,0:T(8,128)(2,1)} %gate.3), calls=%async_computation.1 | async-start | bytes 1572864 | tf_op jit(solution)/shard_map/all_to_all | solution.py:348
  89.8 15.4 %collective-permute-start.18 = (bf16[2,256,256]{2,1,0:T(8,128)(2,1)S(1)}, bf16[2,256,256]{2,1,0:T(8,128)(2,1)S(1)}, u32[]{:S(2)}, u32[]{:S(2)}) collective-permute-start(bf16[2,256,256]{2,1,0:T(8,128)(2,1)S(1)} %collective-permute-done.17.refs_1_), channel_id=1, source_target_pairs={{0,4},{1,5},{2,6},{3,7},{4,0},{5,1},{6,2},{7,3},{8,12},{9,13},{10,... | collective-permute-start | bytes 786440 | tf_op jit(solution)/shard_map/ppermute | solution.py:362
  91.5 14.0 %collective-permute-start.20 = (bf16[2,256,256]{2,1,0:T(8,128)(2,1)S(1)}, bf16[2,256,256]{2,1,0:T(8,128)(2,1)S(1)}, u32[]{:S(2)}, u32[]{:S(2)}) collective-permute-start(bf16[2,256,256]{2,1,0:T(8,128)(2,1)S(1)} %collective-permute-done.19.refs_3_), channel_id=1, source_target_pairs={{0,2},{1,3},{2,0},{3,1},{4,6},{5,7},{6,4},{7,5},{8,10},{9,11},{10,... | collective-permute-start | bytes 786440 | tf_op jit(solution)/shard_map/ppermute | solution.py:362
  92.9 17.8 %collective-permute-start.22 = (bf16[2,256,256]{2,1,0:T(8,128)(2,1)S(1)}, bf16[2,256,256]{2,1,0:T(8,128)(2,1)S(1)}, u32[]{:S(2)}, u32[]{:S(2)}) collective-permute-start(bf16[2,256,256]{2,1,0:T(8,128)(2,1)S(1)} %collective-permute-done.21.refs_2_), channel_id=1, source_target_pairs={{0,8},{1,9},{2,10},{3,11},{4,12},{5,13},{6,14},{7,15},{8,0},{9,1},... | collective-permute-start | bytes 786440 | tf_op jit(solution)/shard_map/ppermute | solution.py:362
  94.4 1.6 %copy-start.11 = (f32[2,2048,128]{2,1,0:T(8,128)S(1)}, f32[2,2048,128]{2,1,0:T(8,128)}, u32[]{:S(2)}) copy-start(f32[2,2048,128]{2,1,0:T(8,128)} %copy-done.10) | copy-start | bytes 6291460
  111.4 1.8 %collective-permute-start.25 = (bf16[768,256]{1,0:T(8,128)(2,1)S(1)}, bf16[768,256]{1,0:T(8,128)(2,1)S(1)}, u32[]{:S(2)}, u32[]{:S(2)}) collective-permute-start(bf16[768,256]{1,0:T(8,128)(2,1)S(1)} %pick_other.4), channel_id=1, source_target_pairs={{0,1},{1,0},{2,3},{3,2},{4,5},{5,4},{6,7},{7,6},{8,9},{9,8},{10,11... | collective-permute-start | bytes 1179656 | tf_op jit(solution)/shard_map/ppermute | solution.py:352
  111.5 8.7 %collective-permute-start.24 = (bf16[2,256,256]{2,1,0:T(8,128)(2,1)S(1)}, bf16[2,256,256]{2,1,0:T(8,128)(2,1)S(1)}, u32[]{:S(2)}, u32[]{:S(2)}) collective-permute-start(bf16[2,256,256]{2,1,0:T(8,128)(2,1)S(1)} %collective-permute-done.22.refs_2_), channel_id=1, source_target_pairs={{0,2},{1,3},{2,0},{3,1},{4,6},{5,7},{6,4},{7,5},{8,10},{9,11},{10,... | collective-permute-start | bytes 786440 | tf_op jit(solution)/shard_map/ppermute | solution.py:362
  120.9 7.2 %collective-permute-start.26 = (bf16[256,256]{1,0:T(8,128)(2,1)S(1)}, bf16[256,256]{1,0:T(8,128)(2,1)S(1)}, u32[]{:S(2)}, u32[]{:S(2)}) collective-permute-start(bf16[256,256]{1,0:T(8,128)(2,1)S(1)} %pick_other.5), channel_id=1, source_target_pairs={{0,1},{1,0},{2,3},{3,2},{4,5},{5,4},{6,7},{7,6},{8,9},{9,8},{10,11... | collective-permute-start | bytes 393224 | tf_op jit(solution)/shard_map/ppermute | solution.py:352
  121.0 1.6 %copy-start.9 = (f32[2,2048,128]{2,1,0:T(8,128)S(1)}, f32[2,2048,128]{2,1,0:T(8,128)}, u32[]{:S(2)}) copy-start(f32[2,2048,128]{2,1,0:T(8,128)} %copy-done.8) | copy-start | bytes 6291460
  (4 other events, 4.6 us)

commit v19 on v18

--- a/solution.py
+++ b/solution.py
@@ -11,7 +11,7 @@
 DEAD_MARK = 1024.0
 DEAD_ABOVE = 512.0
 NEG = -1e30
-CHUNK = 1280
+CHUNK = 1024
 ROWS = 256
 PARAMS = pltpu.CompilerParams(vmem_limit_bytes=44 * 1024 * 1024)
 COPY_PARAMS = pltpu.CompilerParams(vmem_limit_bytes=62 * 1024 * 1024)
@@ -121,7 +121,7 @@
         save_state(*work[1:], out_ref)
 
 
-def prefix_kernel(factor, last, count, steps, which_ref, q_ref, *refs):
+def prefix_kernel(factor, last, count, steps, owner_ref, reader_ref, me_ref, q_ref, *refs):
     pieces = refs[:count]
     loaded_ref, out_ref, *work, rows_ref = refs[count:]
     step = pl.program_id(0)
@@ -158,7 +158,7 @@
         copy.wait()
 
 
-def pick_kernel(which_ref, *refs):
+def pick_kernel(owner_ref, reader_ref, me_ref, *refs):
     pieces, out_ref = refs[:-1], refs[-1]
     for place, piece in enumerate(pieces):
         out_ref[pl.ds(place * piece.shape[0], piece.shape[0]), :] = piece[...]
@@ -175,10 +175,10 @@
         )
 
     def stores(entry, source):
-        early = parts[0].shape[1]
+        rows = parts[0].shape[1]
         return [
             pltpu.make_async_copy(
-                source.at[pl.ds(place * early, part.shape[1])],
+                source.at[pl.ds(place * rows, rows)],
                 part.at[target_ref[0, entry]],
                 out_sems.at[place, entry],
             )
@@ -269,7 +269,7 @@
     wait_all([store(step) for step in range(chips)])
 
 
-def multicast(prefix_cache, owners, readers, outgoing, fold_local, fold_moved):
+def multicast(prefix_cache, owners, outgoing, fold_local, fold_moved):
     replicas = lax.axis_size("replica")
     half = replicas // 2
     chips = half // 2
@@ -300,16 +300,12 @@
 
     me = lax.axis_index("replica")
     chip = me // 2 % chips
-    owners = gate(owners, staged[0])
     ids = jnp.arange(prefixes, dtype=jnp.int32)
     known = jnp.sum(jnp.where(owners == replicas - 1, ids, 0))
     sought = jnp.where(ids[:-1] >= known, owners[1:], owners[:-1])
     away, known_away = chip ^ (sought // 2 % chips), (chip ^ (chips - 1))[None]
     held_by = jnp.concatenate([jnp.full((1,), replicas - 1, jnp.int32), sought])
     same_half = held_by // half == me // half
-    wanted = jnp.stack([readers[me], readers[me ^ 1]])
-    place = jnp.where(wanted == known, 0, wanted + (wanted < known))
-    mine, other = place[:1], place[1:]
 
     def to_peers(staged, senders):
         return [
@@ -341,7 +337,7 @@
         jnp.concatenate([found_known, found]),
         jnp.concatenate([passed_known, passed]),
     )
-    return held, mine, other, state_now, later
+    return held, state_now, later
 
 
 def send_blocks(rows):
@@ -362,21 +358,33 @@
     return lax.ppermute(gathered[step ^ 1 << last], "replica", pairs)
 
 
-def from_other(pieces, place):
+def wanted_place(owner_ref, reader_ref, who):
+    last = reader_ref.shape[0] - 1
+    known = sum(
+        jnp.where(owner_ref[prefix] == last, prefix, 0) for prefix in range(owner_ref.shape[0])
+    )
+    wanted = reader_ref[who]
+    return jnp.where(wanted == known, 0, jnp.where(wanted < known, wanted + 1, wanted))
+
+
+def from_other(pieces, scalars):
     rows, width = pieces[0].shape[1:]
-    spec = pl.BlockSpec((None, rows, width), lambda i, which: (which[0], 0, 0))
+    spec = pl.BlockSpec(
+        (None, rows, width),
+        lambda i, owner, reader, me: (wanted_place(owner, reader, me[0] ^ 1), 0, 0),
+    )
     picked = pl.pallas_call(
         pick_kernel,
         out_shape=jax.ShapeDtypeStruct((len(pieces) * rows, width), pieces[0].dtype),
         grid_spec=pltpu.PrefetchScalarGridSpec(
-            num_scalar_prefetch=1,
+            num_scalar_prefetch=3,
             grid=(1,),
             in_specs=[spec] * len(pieces),
-            out_specs=pl.BlockSpec((len(pieces) * rows, width), lambda i, which: (0, 0)),
+            out_specs=whole((len(pieces) * rows, width)),
         ),
         compiler_params=PARAMS,
         name="pick_other",
-    )(place, *pieces)
+    )(*scalars, *pieces)
     return swap_cores(picked)
 
 
@@ -418,12 +426,8 @@
     ]
 
     entries = mig_target.shape[1]
-    block = kv_pool.shape[1]
-    early = block * 5 // 8
-    slots = tuple(
-        jax.ShapeDtypeStruct((replicas, rows, kv_pool.shape[2]), kv_pool.dtype)
-        for rows in (early, block - early)
-    )
+    half_block = (replicas, kv_pool.shape[1] // 2, kv_pool.shape[2])
+    slots = (jax.ShapeDtypeStruct(half_block, kv_pool.dtype),) * 2
     outgoing = pl.pallas_call(
         pack_kernel,
         out_shape=slots,
@@ -478,7 +482,7 @@
         )(queries, arrived, state_now)
 
     def fold_prefix(pieces, state_now, last=False):
-        others = from_other(pieces, other)
+        others = from_other(pieces, scalars)
         rows = pieces[0].shape[1]
         keys = 2 * len(pieces) * rows
         steps = max(1, keys // CHUNK)
@@ -489,11 +493,16 @@
             functools.partial(prefix_kernel, factor, last, len(pieces) + 1, steps),
             out_shape=target,
             grid_spec=pltpu.PrefetchScalarGridSpec(
-                num_scalar_prefetch=1,
+                num_scalar_prefetch=3,
                 grid=(steps,),
                 in_specs=[
                     whole(queries.shape),
-                    *[pl.BlockSpec((None, rows, 2 * size), lambda i, which: (which[0], 0, 0))]
+                    *[
+                        pl.BlockSpec(
+                            (None, rows, 2 * size),
+                            lambda i, owner, reader, me: (wanted_place(owner, reader, me[0]), 0, 0),
+                        )
+                    ]
                     * len(pieces),
                     whole(others.shape),
                     whole(state.shape),
@@ -504,11 +513,10 @@
             compiler_params=PARAMS,
             cost_estimate=cost(row_count, keys, size),
             name="prefix_keys",
-        )(mine, queries, *pieces, others, state_now)
-
-    held, mine, other, state_now, later = multicast(
-        prefix_cache, owners, readers, outgoing, fold_local, fold_moved
-    )
+        )(*scalars, queries, *pieces, others, state_now)
+
+    held, state_now, later = multicast(prefix_cache, owners, outgoing, fold_local, fold_moved)
+    scalars = (owners, readers, lax.axis_index("replica")[None])
     gathered = {0: held}
     ready = [held]
     rounds = (replicas // 4).bit_length() - 1

time: 133 us -> 123 us (0.925)
  waiting for transfers between devices: 19.9 us -> 16.8 us
  local copies, waits for them, and re-layouts: 12.4 us -> 10.3 us
  other arithmetic: 3.05 us -> 1.01 us
  starting transfers between devices: 51.4 us -> 49.8 us
    ppermute x14, waiting for transfers between devices: 9.95 us -> 6.09 us  [to_peers(): lax.ppermute(rows, 'replica', [(i, i ^ 2 * step) for i in senders])]
    select_n x1 -> x0, other arithmetic: 1.95 us -> none  [multicast(): place = jnp.where(wanted == known, 0, wanted + (wanted < known))]
    unnamed x47 -> x32, local copies, waits for them, and re-layouts: 10.6 us -> 9.7 us
  transfers between devices with their start and end apart: 29 -> 29, of which waited for: 9 -> 7; matrix products, arithmetic and copies ran while one was open for 4% -> 1% of each run, Pallas kernels for 28% -> 30%
where the time goes in v19:
time: 123 us; the launch traced here: 122 us
  starting transfers between devices  49.8 us (40%)
  Pallas kernels  40.4 us (33%)
  waiting for transfers between devices  16.8 us (14%)
  local copies, waits for them, and re-layouts  10.3 us (8%)
  between operations  3.7 us (3%)
    ppermute x14, starting transfers between devices, to_peers(): lax.ppermute(rows, 'replica', [(i, i ^ 2 * step) for i in senders])  17.5 us
    pallas_call x3, Pallas kernels, fold_prefix(): pl.pallas_call(functools.partial(prefix_kernel, factor, last, len(pieces)...  15.5 us
    pallas_call x2, Pallas kernels, fold_moved(): pl.pallas_call(functools.partial(moved_kernel, factor, steps), out_shape=...  13.3 us
    ppermute x7, starting transfers between devices, gather_step(): return lax.ppermute(gathered[step ^ 1 << last], 'replica', pairs)  12.7 us
    all_to_all x2, starting transfers between devices, send_blocks(): lax.all_to_all(rows, 'replica', split_axis=0, concat_axis=0, tiled=True)  12.6 us
    ppermute x7, waiting for transfers between devices, gather_step(): return lax.ppermute(gathered[step ^ 1 << last], 'replica', pairs)  10.5 us
    unnamed x32, local copies, waits for them, and re-layouts  9.7 us
    ppermute x14, waiting for transfers between devices, to_peers(): lax.ppermute(rows, 'replica', [(i, i ^ 2 * step) for i in senders])  6.09 us
  transfers between devices with their start and end apart: 29, of which 7 were waited for; matrix products, arithmetic and copies ran while one was open for 1% of the time, Pallas kernels for 30%

profile of v19, /device:TPU:0, one launch (start us, length us, event | category | flops | bytes accessed | tf_op | source)
XLA Modules:
  0.0 122.0 jit_solution(14037701533666220908)
XLA Ops:
  1.1 4.0 %pack_moved.1 = (bf16[32,64,256]{2,1,0:T(8,128)(2,1)}, bf16[32,64,256]{2,1,0:T(8,128)(2,1)}) custom-call(s32[1,32]{1,0:T(1,128)} %target_ref.1, s32[1,32]{1,0:T(1,128)} %block_ref.1, s32[1]{0:T(128)S(6)} %copy.15.count_ref, bf16[32,128,256]{2,1,0:T(8,128)(2,1)} %pool_ref.1), custom_call_target="tpu_custom_call" | custom-call | tf_op jit(solution)/shard_map/pack_moved/pallas_call | solution.py:431
  5.1 7.0 %all-to-all-start = ((bf16[32,64,256]{2,1,0:T(8,128)(2,1)}), bf16[32,64,256]{2,1,0:T(8,128)(2,1)S(1)}, u32[]{:S(2)}, u32[]{:S(2)}) async-start(bf16[32,64,256]{2,1,0:T(8,128)(2,1)} %get-tuple-element.73), calls=%async_computation | async-start | bytes 2097152 | tf_op jit(solution)/shard_map/all_to_all | solution.py:344
  12.8 0.6 fusion.2
  13.4 3.0 %stage_prefix.1 = (bf16[1,256,256]{2,1,0:T(8,128)(2,1)}, bf16[1,256,256]{2,1,0:T(8,128)(2,1)}, bf16[1,256,256]{2,1,0:T(8,128)(2,1)}, bf16[1,256,256]{2,1,0:T(8,1...) custom-call(s32[2]{0:T(128)} %owner_ref.13, ...), custom_call_target="tpu_custom_call" | custom-call | tf_op jit(solution)/shard_map/stage_prefix/pallas_call | solution.py:285
  16.4 1.8 %collective-permute-start.1 = (bf16[1,256,256]{2,1,0:T(8,128)(2,1)}, bf16[1,256,256]{2,1,0:T(8,128)(2,1)S(1)}, u32[]{:S(2)}, u32[]{:S(2)}) collective-permute-start(bf16[1,256,256]{2,1,0:T(8,128)(2,1)} %get-tuple-element.48), channel_id=1, source_target_pairs={{0,2},{1,3},{2,0},{3,1},{4,6},{5,7},{6,4},{7,5},{8,10},{9,11},{10,... | collective-permute-start | bytes 393224 | tf_op jit(solution)/shard_map/ppermute | solution.py:312
  18.3 2.4 %collective-permute-start.10 = (bf16[1,256,256]{2,1,0:T(8,128)(2,1)}, bf16[1,256,256]{2,1,0:T(8,128)(2,1)S(1)}, u32[]{:S(2)}, u32[]{:S(2)}) collective-permute-start(bf16[1,256,256]{2,1,0:T(8,128)(2,1)} %get-tuple-element.67), channel_id=1, source_target_pairs={{0,12},{1,13},{2,14},{3,15},{4,8},{5,9},{6,10},{7,11},{8,4},{9,5},... | collective-permute-start | bytes 393224 | tf_op jit(solution)/shard_map/ppermute | solution.py:312
  21.2 1.5 %collective-permute-start.12 = (bf16[1,256,256]{2,1,0:T(8,128)(2,1)}, bf16[1,256,256]{2,1,0:T(8,128)(2,1)S(1)}, u32[]{:S(2)}, u32[]{:S(2)}) collective-permute-start(bf16[1,256,256]{2,1,0:T(8,128)(2,1)} %get-tuple-element.69), channel_id=1, source_target_pairs={{0,8},{1,9},{2,10},{3,11},{4,12},{5,13},{6,14},{7,15},{8,0},{9,1},... | collective-permute-start | bytes 393224 | tf_op jit(solution)/shard_map/ppermute | solution.py:312
  22.7 1.5 %collective-permute-start.13 = (bf16[1,256,256]{2,1,0:T(8,128)(2,1)}, bf16[1,256,256]{2,1,0:T(8,128)(2,1)S(1)}, u32[]{:S(2)}, u32[]{:S(2)}) collective-permute-start(bf16[1,256,256]{2,1,0:T(8,128)(2,1)} %get-tuple-element.70), channel_id=1, source_target_pairs={{0,6},{1,7},{2,4},{3,5},{4,2},{5,3},{6,0},{7,1},{8,14},{9,15},{10,... | collective-permute-start | bytes 393224 | tf_op jit(solution)/shard_map/ppermute | solution.py:312
  24.1 0.9 copy-done
  25.0 2.8 %local_keys.1.loaded_ref = f32[2,2048,128]{2,1,0:T(8,128)S(1)} custom-call(s32[1]{0:T(128)S(6)} %copy.14.len_ref, bf16[256,1024]{1,0:T(8,128)(2,1)S(1)} %copy-done.5, bf16[256,256]{1,0:T(8,128)(2,1)S(1)} %copy-done.7, bf16[512,256]{1,0:T(8,128)(2,1)S(1)} %copy-done.6, bf16[1,256,256]{2,1,0:T(8,128)(2,1)S(1)} %copy-done), custom_call_target="tpu_custom_call" | custom-call | flops 2415919104 | bytes 393216 | tf_op jit(solution)/shard_map/local_keys/pallas_call | solution.py:446
  27.8 1.3 %copy-done.8 = f32[2,2048,128]{2,1,0:T(8,128)} copy-done((f32[2,2048,128]{2,1,0:T(8,128)}, f32[2,2048,128]{2,1,0:T(8,128)S(1)}, u32[]{:S(2)}) %copy-start.8) | copy-done | bytes 2097176
  29.2 1.5 %collective-permute-start.14 = (bf16[1,256,256]{2,1,0:T(8,128)(2,1)}, bf16[1,256,256]{2,1,0:T(8,128)(2,1)S(1)}, u32[]{:S(2)}, u32[]{:S(2)}) collective-permute-start(bf16[1,256,256]{2,1,0:T(8,128)(2,1)} %get-tuple-element.71), channel_id=1, source_target_pairs={{0,4},{1,5},{2,6},{3,7},{4,0},{5,1},{6,2},{7,3},{8,12},{9,13},{10,... | collective-permute-start | bytes 393224 | tf_op jit(solution)/shard_map/ppermute | solution.py:312
  30.6 3.7 %collective-permute-done.10 = bf16[1,256,256]{2,1,0:T(8,128)(2,1)S(1)} collective-permute-done((bf16[1,256,256]{2,1,0:T(8,128)(2,1)}, bf16[1,256,256]{2,1,0:T(8,128)(2,1)S(1)}, u32[]{:S(2)}, u32[]{:S(2)}) %collective-permute-start.10) | collective-permute-done | bytes 131104 | tf_op jit(solution)/shard_map/ppermute | solution.py:312
  34.4 3.7 %collective-permute-start.9 = (bf16[1,256,256]{2,1,0:T(8,128)(2,1)}, bf16[1,256,256]{2,1,0:T(8,128)(2,1)S(1)}, u32[]{:S(2)}, u32[]{:S(2)}) collective-permute-start(bf16[1,256,256]{2,1,0:T(8,128)(2,1)} %get-tuple-element.66), channel_id=1, source_target_pairs={{0,14},{1,15},{2,12},{3,13},{4,10},{5,11},{6,8},{7,9},{8,6},{9,7},... | collective-permute-start | bytes 393224 | tf_op jit(solution)/shard_map/ppermute | solution.py:312
  38.1 0.7 collective-permute-start.2
  38.8 2.3 %collective-permute-done.12 = bf16[1,256,256]{2,1,0:T(8,128)(2,1)S(1)} collective-permute-done((bf16[1,256,256]{2,1,0:T(8,128)(2,1)}, bf16[1,256,256]{2,1,0:T(8,128)(2,1)S(1)}, u32[]{:S(2)}, u32[]{:S(2)}) %collective-permute-start.12) | collective-permute-done | bytes 131104 | tf_op jit(solution)/shard_map/ppermute | solution.py:312
  41.1 0.7 collective-permute-start.3
  41.8 0.7 fusion
  44.6 0.7 collective-permute-start.4
  45.2 0.7 collective-permute-start.5
  45.9 0.7 collective-permute-start.6
  46.6 0.7 collective-permute-start.7
  47.3 0.7 collective-permute-start.8
  48.1 5.0 %collective-permute-start.15 = (bf16[1,256,256]{2,1,0:T(8,128)(2,1)S(1)}, bf16[1,256,256]{2,1,0:T(8,128)(2,1)S(1)}, u32[]{:S(2)}, u32[]{:S(2)}) collective-permute-start(bf16[1,256,256]{2,1,0:T(8,128)(2,1)S(1)} %select_select_fusion), channel_id=1, source_target_pairs={{0,16},{1,17},{2,18},{3,19},{4,20},{5,21},{6,22},{7,23},{8,24},{9,... | collective-permute-start | bytes 393224 | tf_op jit(solution)/shard_map/ppermute | solution.py:328
  53.2 1.3 %collective-permute-start.16 = (bf16[1,256,256]{2,1,0:T(8,128)(2,1)S(1)}, bf16[1,256,256]{2,1,0:T(8,128)(2,1)S(1)}, u32[]{:S(2)}, u32[]{:S(2)}) collective-permute-start(bf16[1,256,256]{2,1,0:T(8,128)(2,1)S(1)} %select_select_fusion.1), channel_id=1, source_target_pairs={{16,0},{17,1},{18,2},{19,3},{20,4},{21,5},{22,6},{23,7},{24,8},{25... | collective-permute-start | bytes 393224 | tf_op jit(solution)/shard_map/ppermute | solution.py:330
  54.5 1.6 %copy-done.9 = f32[2,2048,128]{2,1,0:T(8,128)S(1)} copy-done((f32[2,2048,128]{2,1,0:T(8,128)S(1)}, f32[2,2048,128]{2,1,0:T(8,128)}, u32[]{:S(2)}) %copy-start.9) | copy-done | bytes 2097176
  56.1 6.6 %moved_keys.2.refs_5_ = f32[2,2048,128]{2,1,0:T(8,128)S(1)} custom-call(bf16[256,1024]{1,0:T(8,128)(2,1)S(1)} %copy-done.5, bf16[32,64,256]{2,1,0:T(8,128)(2,1)S(1)} %all-to-all-done.kv_ref, f32[2,2048,128]{2,1,0:T(8,128)S(1)} %copy-done.9), custom_call_target="tpu_custom_call" | custom-call | flops 6442450944 | bytes 1048576 | tf_op jit(solution)/shard_map/moved_keys/pallas_call | solution.py:468
  62.7 1.3 %copy-done.12 = f32[2,2048,128]{2,1,0:T(8,128)} copy-done((f32[2,2048,128]{2,1,0:T(8,128)}, f32[2,2048,128]{2,1,0:T(8,128)S(1)}, u32[]{:S(2)}) %copy-start.12) | copy-done | bytes 2097176
  64.2 2.3 %collective-permute-start.17 = (bf16[2,256,256]{2,1,0:T(8,128)(2,1)S(1)}, bf16[2,256,256]{2,1,0:T(8,128)(2,1)S(1)}, u32[]{:S(2)}, u32[]{:S(2)}) collective-permute-start(bf16[2,256,256]{2,1,0:T(8,128)(2,1)S(1)} %maximum_select_fusion.refs_0_), channel_id=1, source_target_pairs={{0,2},{1,3},{2,0},{3,1},{4,6},{5,7},{6,4},{7,5},{8,10},{9,11},{10,... | collective-permute-start | bytes 786440 | tf_op jit(solution)/shard_map/ppermute | solution.py:358
  66.5 4.2 %collective-permute-start.21 = (bf16[2,256,256]{2,1,0:T(8,128)(2,1)S(1)}, bf16[2,256,256]{2,1,0:T(8,128)(2,1)S(1)}, u32[]{:S(2)}, u32[]{:S(2)}) collective-permute-start(bf16[2,256,256]{2,1,0:T(8,128)(2,1)S(1)} %maximum_select_fusion.refs_0_), channel_id=1, source_target_pairs={{0,4},{1,5},{2,6},{3,7},{4,0},{5,1},{6,2},{7,3},{8,12},{9,13},{10,... | collective-permute-start | bytes 786440 | tf_op jit(solution)/shard_map/ppermute | solution.py:358
  70.7 5.6 %all-to-all-start.1 = ((bf16[32,64,256]{2,1,0:T(8,128)(2,1)}), bf16[32,64,256]{2,1,0:T(8,128)(2,1)S(1)}, u32[]{:S(2)}, u32[]{:S(2)}) async-start(bf16[32,64,256]{2,1,0:T(8,128)(2,1)} %gate.1), calls=%async_computation.1 | async-start | bytes 2097152 | tf_op jit(solution)/shard_map/all_to_all | solution.py:344
  76.4 0.6 pick_other.3
  77.1 1.7 %collective-permute-start.18 = (bf16[2,256,256]{2,1,0:T(8,128)(2,1)S(1)}, bf16[2,256,256]{2,1,0:T(8,128)(2,1)S(1)}, u32[]{:S(2)}, u32[]{:S(2)}) collective-permute-start(bf16[2,256,256]{2,1,0:T(8,128)(2,1)S(1)} %collective-permute-done.17.refs_1_), channel_id=1, source_target_pairs={{0,4},{1,5},{2,6},{3,7},{4,0},{5,1},{6,2},{7,3},{8,12},{9,13},{10,... | collective-permute-start | bytes 786440 | tf_op jit(solution)/shard_map/ppermute | solution.py:358
  78.8 1.5 %collective-permute-start.20 = (bf16[2,256,256]{2,1,0:T(8,128)(2,1)S(1)}, bf16[2,256,256]{2,1,0:T(8,128)(2,1)S(1)}, u32[]{:S(2)}, u32[]{:S(2)}) collective-permute-start(bf16[2,256,256]{2,1,0:T(8,128)(2,1)S(1)} %collective-permute-done.19.refs_3_), channel_id=1, source_target_pairs={{0,2},{1,3},{2,0},{3,1},{4,6},{5,7},{6,4},{7,5},{8,10},{9,11},{10,... | collective-permute-start | bytes 786440 | tf_op jit(solution)/shard_map/ppermute | solution.py:358
  80.3 1.5 %collective-permute-start.22 = (bf16[2,256,256]{2,1,0:T(8,128)(2,1)S(1)}, bf16[2,256,256]{2,1,0:T(8,128)(2,1)S(1)}, u32[]{:S(2)}, u32[]{:S(2)}) collective-permute-start(bf16[2,256,256]{2,1,0:T(8,128)(2,1)S(1)} %collective-permute-done.21.refs_2_), channel_id=1, source_target_pairs={{0,8},{1,9},{2,10},{3,11},{4,12},{5,13},{6,14},{7,15},{8,0},{9,1},... | collective-permute-start | bytes 786440 | tf_op jit(solution)/shard_map/ppermute | solution.py:358
  81.7 1.6 %copy-done.13 = f32[2,2048,128]{2,1,0:T(8,128)S(1)} copy-done((f32[2,2048,128]{2,1,0:T(8,128)S(1)}, f32[2,2048,128]{2,1,0:T(8,128)}, u32[]{:S(2)}) %copy-start.13) | copy-done | bytes 2097176
  83.3 6.9 %prefix_keys.3.refs_4_ = f32[2,2048,128]{2,1,0:T(8,128)S(1)} custom-call(s32[2]{0:T(128)S(1)} %copy-done.3, s32[32]{0:T(128)S(1)} %copy-done.4, s32[1]{0:T(128)} %bitcast.me_ref, bf16[256,1024]{1,0:T(8,128)(2,1)S(1)} %copy-done.5, bf16[2,256,256]{2,1,0:T(8,128)(2,1)S(1)} %maximum_select_fusion.refs_0_, ...), custom_call_target="tpu_custom_call" | custom-call | flops 6442450944 | bytes 1048576 | tf_op jit(solution)/shard_map/prefix_keys/pallas_call | solution.py:492
  90.3 3.2 %collective-permute-done.18.refs_0_ = bf16[2,256,256]{2,1,0:T(8,128)(2,1)S(1)} collective-permute-done((bf16[2,256,256]{2,1,0:T(8,128)(2,1)S(1)}, bf16[2,256,256]{2,1,0:T(8,128)(2,1)S(1)}, u32[]{:S(2)}, u32[]{:S(2)}) %collective-permute-start.18) | collective-permute-done | bytes 262176 | tf_op jit(solution)/shard_map/ppermute | solution.py:358
  93.5 1.0 collective-permute-done.20.refs_1_
  94.5 5.6 %collective-permute-done.22.refs_2_ = bf16[2,256,256]{2,1,0:T(8,128)(2,1)S(1)} collective-permute-done((bf16[2,256,256]{2,1,0:T(8,128)(2,1)S(1)}, bf16[2,256,256]{2,1,0:T(8,128)(2,1)S(1)}, u32[]{:S(2)}, u32[]{:S(2)}) %collective-permute-start.22) | collective-permute-done | bytes 262176 | tf_op jit(solution)/shard_map/ppermute | solution.py:358
  100.1 0.6 pick_other.4
  100.8 1.5 %collective-permute-start.24 = (bf16[2,256,256]{2,1,0:T(8,128)(2,1)S(1)}, bf16[2,256,256]{2,1,0:T(8,128)(2,1)S(1)}, u32[]{:S(2)}, u32[]{:S(2)}) collective-permute-start(bf16[2,256,256]{2,1,0:T(8,128)(2,1)S(1)} %collective-permute-done.22.refs_2_), channel_id=1, source_target_pairs={{0,2},{1,3},{2,0},{3,1},{4,6},{5,7},{6,4},{7,5},{8,10},{9,11},{10,... | collective-permute-start | bytes 786440 | tf_op jit(solution)/shard_map/ppermute | solution.py:358
  102.5 5.0 %prefix_keys.4.loaded_ref = f32[2,2048,128]{2,1,0:T(8,128)S(1)} custom-call(s32[2]{0:T(128)S(1)} %copy-done.3, s32[32]{0:T(128)S(1)} %copy-done.4, s32[1]{0:T(128)} %bitcast.me_ref, bf16[256,1024]{1,0:T(8,128)(2,1)S(1)} %copy-done.5, bf16[2,256,256]{2,1,0:T(8,128)(2,1)S(1)} %collective-permute-done.18.refs_0_, ...), custom_call_target="tpu_custom_call" | custom-call | flops 4831838208 | bytes 786432 | tf_op jit(solution)/shard_map/prefix_keys/pallas_call | solution.py:492
  107.5 1.3 %copy-done.10 = f32[2,2048,128]{2,1,0:T(8,128)} copy-done((f32[2,2048,128]{2,1,0:T(8,128)}, f32[2,2048,128]{2,1,0:T(8,128)S(1)}, u32[]{:S(2)}) %copy-start.10) | copy-done | bytes 2097176
  108.8 0.7 collective-permute-done.24.refs_0_
  110.1 1.6 %copy-done.11 = f32[2,2048,128]{2,1,0:T(8,128)S(1)} copy-done((f32[2,2048,128]{2,1,0:T(8,128)S(1)}, f32[2,2048,128]{2,1,0:T(8,128)}, u32[]{:S(2)}) %copy-start.11) | copy-done | bytes 2097176
  111.7 6.7 %moved_keys.3.refs_2_ = f32[2,2048,128]{2,1,0:T(8,128)S(1)} custom-call(bf16[256,1024]{1,0:T(8,128)(2,1)S(1)} %copy-done.5, bf16[32,64,256]{2,1,0:T(8,128)(2,1)S(1)} %all-to-all-done.1.kv_ref, f32[2,2048,128]{2,1,0:T(8,128)S(1)} %copy-done.11), custom_call_target="tpu_custom_call" | custom-call | flops 6442450944 | bytes 1048576 | tf_op jit(solution)/shard_map/moved_keys/pallas_call | solution.py:468
  118.4 3.6 %prefix_keys.5 = bf16[256,1024]{1,0:T(8,128)(2,1)} custom-call(s32[2]{0:T(128)S(1)} %copy-done.3, s32[32]{0:T(128)S(1)} %copy-done.4, s32[1]{0:T(128)} %bitcast.me_ref, bf16[256,1024]{1,0:T(8,128)(2,1)S(1)} %copy-done.5, bf16[2,256,256]{2,1,0:T(8,128)(2,1)S(1)} %collective-permute-done.24.refs_0_, bf16[256,256]{1,0:T(8,128)(2,1)S(1)} %collective-permute-done.26.refs_1_, ...), custom_call_target="tpu_custom_call" | custom-call | flops 1610612736 | bytes 262144 | tf_op jit(solution)/shard_map/prefix_keys/pallas_call | solution.py:492
  (61 shorter events, 2.5 us)
Async XLA Ops:
  0.0 5.1 %collective-permute-start = (bf16[4096,256]{1,0:T(8,128)(2,1)}, bf16[4096,256]{1,0:T(8,128)(2,1)}, u32[]{:S(2)}, u32[]{:S(2)}) collective-permute-start(bf16[4096,256]{1,0:T(8,128)(2,1)} %param.15), channel_id=1, source_target_pairs={{0,1},{1,0},{2,3},{3,2},{4,5},{5,4},{6,7},{7,6},{8,9},{9,8},{10,11... | collective-permute-start | bytes 6291464 | tf_op jit(solution)/shard_map/ppermute | solution.py:348
  1.1 11.6 %copy-start.2 = (s32[2]{0:T(128)S(1)}, s32[2]{0:T(128)}, u32[]{:S(2)}) copy-start(s32[2]{0:T(128)} %owner_ref.13) | copy-start | bytes 28
  5.1 49.3 %all-to-all-start = ((bf16[32,64,256]{2,1,0:T(8,128)(2,1)}), bf16[32,64,256]{2,1,0:T(8,128)(2,1)S(1)}, u32[]{:S(2)}, u32[]{:S(2)}) async-start(bf16[32,64,256]{2,1,0:T(8,128)(2,1)} %get-tuple-element.73), calls=%async_computation | async-start | bytes 2097152 | tf_op jit(solution)/shard_map/all_to_all | solution.py:344
  13.4 10.7 %copy-start.5 = (bf16[256,1024]{1,0:T(8,128)(2,1)S(1)}, bf16[256,1024]{1,0:T(8,128)(2,1)}, u32[]{:S(2)}) copy-start(bf16[256,1024]{1,0:T(8,128)(2,1)} %q_ref.11) | copy-start | bytes 1572868
  13.4 10.7 %copy-start.6 = (bf16[512,256]{1,0:T(8,128)(2,1)S(1)}, bf16[512,256]{1,0:T(8,128)(2,1)}, u32[]{:S(2)}) copy-start(bf16[512,256]{1,0:T(8,128)(2,1)} %own_ref.1) | copy-start | bytes 786436
  13.4 10.7 %copy-start.7 = (bf16[256,256]{1,0:T(8,128)(2,1)S(1)}, bf16[256,256]{1,0:T(8,128)(2,1)}, u32[]{:S(2)}) copy-start(bf16[256,256]{1,0:T(8,128)(2,1)} %suffix_ref.1) | copy-start | bytes 393220
  16.4 12.7 %collective-permute-start.1 = (bf16[1,256,256]{2,1,0:T(8,128)(2,1)}, bf16[1,256,256]{2,1,0:T(8,128)(2,1)S(1)}, u32[]{:S(2)}, u32[]{:S(2)}) collective-permute-start(bf16[1,256,256]{2,1,0:T(8,128)(2,1)} %get-tuple-element.48), channel_id=1, source_target_pairs={{0,2},{1,3},{2,0},{3,1},{4,6},{5,7},{6,4},{7,5},{8,10},{9,11},{10,... | collective-permute-start | bytes 393224 | tf_op jit(solution)/shard_map/ppermute | solution.py:312
  18.3 16.1 %collective-permute-start.10 = (bf16[1,256,256]{2,1,0:T(8,128)(2,1)}, bf16[1,256,256]{2,1,0:T(8,128)(2,1)S(1)}, u32[]{:S(2)}, u32[]{:S(2)}) collective-permute-start(bf16[1,256,256]{2,1,0:T(8,128)(2,1)} %get-tuple-element.67), channel_id=1, source_target_pairs={{0,12},{1,13},{2,14},{3,15},{4,8},{5,9},{6,10},{7,11},{8,4},{9,5},... | collective-permute-start | bytes 393224 | tf_op jit(solution)/shard_map/ppermute | solution.py:312
  20.6 17.5 %collective-permute-start.11 = (bf16[1,256,256]{2,1,0:T(8,128)(2,1)}, bf16[1,256,256]{2,1,0:T(8,128)(2,1)S(1)}, u32[]{:S(2)}, u32[]{:S(2)}) collective-permute-start(bf16[1,256,256]{2,1,0:T(8,128)(2,1)} %get-tuple-element.68), channel_id=1, source_target_pairs={{0,10},{1,11},{2,8},{3,9},{4,14},{5,15},{6,12},{7,13},{8,2},{9,3},... | collective-permute-start | bytes 393224 | tf_op jit(solution)/shard_map/ppermute | solution.py:312
  21.2 19.9 %collective-permute-start.12 = (bf16[1,256,256]{2,1,0:T(8,128)(2,1)}, bf16[1,256,256]{2,1,0:T(8,128)(2,1)S(1)}, u32[]{:S(2)}, u32[]{:S(2)}) collective-permute-start(bf16[1,256,256]{2,1,0:T(8,128)(2,1)} %get-tuple-element.69), channel_id=1, source_target_pairs={{0,8},{1,9},{2,10},{3,11},{4,12},{5,13},{6,14},{7,15},{8,0},{9,1},... | collective-permute-start | bytes 393224 | tf_op jit(solution)/shard_map/ppermute | solution.py:312
  22.7 21.9 %collective-permute-start.13 = (bf16[1,256,256]{2,1,0:T(8,128)(2,1)}, bf16[1,256,256]{2,1,0:T(8,128)(2,1)S(1)}, u32[]{:S(2)}, u32[]{:S(2)}) collective-permute-start(bf16[1,256,256]{2,1,0:T(8,128)(2,1)} %get-tuple-element.70), channel_id=1, source_target_pairs={{0,6},{1,7},{2,4},{3,5},{4,2},{5,3},{6,0},{7,1},{8,14},{9,15},{10,... | collective-permute-start | bytes 393224 | tf_op jit(solution)/shard_map/ppermute | solution.py:312
  24.1 0.9 copy-start
  25.0 16.1 %copy-start.15 = (bf16[1,256,256]{2,1,0:T(8,128)(2,1)S(1)}, bf16[1,256,256]{2,1,0:T(8,128)(2,1)}, u32[]{:S(2)}) copy-start(bf16[1,256,256]{2,1,0:T(8,128)(2,1)} %get-tuple-element.59) | copy-start | bytes 393220
  25.0 16.7 %copy-start.3 = (s32[2]{0:T(128)S(1)}, s32[2]{0:T(128)}, u32[]{:S(2)}) copy-start(s32[2]{0:T(128)} %owner_ref.13) | copy-start | bytes 28
  25.0 22.9 %copy-start.1 = (bf16[1,256,256]{2,1,0:T(8,128)(2,1)S(1)}, bf16[1,256,256]{2,1,0:T(8,128)(2,1)}, u32[]{:S(2)}) copy-start(bf16[1,256,256]{2,1,0:T(8,128)(2,1)} %get-tuple-element.49.after_ref) | copy-start | bytes 393220
  25.0 28.1 %copy-start.14 = (bf16[1,256,256]{2,1,0:T(8,128)(2,1)S(1)}, bf16[1,256,256]{2,1,0:T(8,128)(2,1)}, u32[]{:S(2)}) copy-start(bf16[1,256,256]{2,1,0:T(8,128)(2,1)} %get-tuple-element.65) | copy-start | bytes 393220
  27.8 1.3 %copy-start.8 = (f32[2,2048,128]{2,1,0:T(8,128)}, f32[2,2048,128]{2,1,0:T(8,128)S(1)}, u32[]{:S(2)}) copy-start(f32[2,2048,128]{2,1,0:T(8,128)S(1)} %local_keys.1.loaded_ref) | copy-start | bytes 6291460
  29.2 16.1 %collective-permute-start.14 = (bf16[1,256,256]{2,1,0:T(8,128)(2,1)}, bf16[1,256,256]{2,1,0:T(8,128)(2,1)S(1)}, u32[]{:S(2)}, u32[]{:S(2)}) collective-permute-start(bf16[1,256,256]{2,1,0:T(8,128)(2,1)} %get-tuple-element.71), channel_id=1, source_target_pairs={{0,4},{1,5},{2,6},{3,7},{4,0},{5,1},{6,2},{7,3},{8,12},{9,13},{10,... | collective-permute-start | bytes 393224 | tf_op jit(solution)/shard_map/ppermute | solution.py:312
  34.4 11.6 %collective-permute-start.9 = (bf16[1,256,256]{2,1,0:T(8,128)(2,1)}, bf16[1,256,256]{2,1,0:T(8,128)(2,1)S(1)}, u32[]{:S(2)}, u32[]{:S(2)}) collective-permute-start(bf16[1,256,256]{2,1,0:T(8,128)(2,1)} %get-tuple-element.66), channel_id=1, source_target_pairs={{0,14},{1,15},{2,12},{3,13},{4,10},{5,11},{6,8},{7,9},{8,6},{9,7},... | collective-permute-start | bytes 393224 | tf_op jit(solution)/shard_map/ppermute | solution.py:312
  38.1 8.5 %collective-permute-start.2 = (bf16[1,256,256]{2,1,0:T(8,128)(2,1)}, bf16[1,256,256]{2,1,0:T(8,128)(2,1)S(1)}, u32[]{:S(2)}, u32[]{:S(2)}) collective-permute-start(bf16[1,256,256]{2,1,0:T(8,128)(2,1)} %get-tuple-element.58), channel_id=1, source_target_pairs={{30,16},{31,17}} | collective-permute-start | bytes 393224 | tf_op jit(solution)/shard_map/ppermute | solution.py:312
  41.1 6.2 %collective-permute-start.3 = (bf16[1,256,256]{2,1,0:T(8,128)(2,1)S(1)}, bf16[1,256,256]{2,1,0:T(8,128)(2,1)S(1)}, u32[]{:S(2)}, u32[]{:S(2)}) collective-permute-start(bf16[1,256,256]{2,1,0:T(8,128)(2,1)S(1)} %copy-done.15), channel_id=1, source_target_pairs={{30,18},{31,19}} | collective-permute-start | bytes 393224 | tf_op jit(solution)/shard_map/ppermute | solution.py:312
  44.6 3.5 %collective-permute-start.4 = (bf16[1,256,256]{2,1,0:T(8,128)(2,1)}, bf16[1,256,256]{2,1,0:T(8,128)(2,1)S(1)}, u32[]{:S(2)}, u32[]{:S(2)}) collective-permute-start(bf16[1,256,256]{2,1,0:T(8,128)(2,1)} %get-tuple-element.60), channel_id=1, source_target_pairs={{30,20},{31,21}} | collective-permute-start | bytes 393224 | tf_op jit(solution)/shard_map/ppermute | solution.py:312
  45.2 7.8 %collective-permute-start.5 = (bf16[1,256,256]{2,1,0:T(8,128)(2,1)}, bf16[1,256,256]{2,1,0:T(8,128)(2,1)S(1)}, u32[]{:S(2)}, u32[]{:S(2)}) collective-permute-start(bf16[1,256,256]{2,1,0:T(8,128)(2,1)} %get-tuple-element.61), channel_id=1, source_target_pairs={{30,22},{31,23}} | collective-permute-start | bytes 393224 | tf_op jit(solution)/shard_map/ppermute | solution.py:312
  45.9 7.2 %collective-permute-start.6 = (bf16[1,256,256]{2,1,0:T(8,128)(2,1)}, bf16[1,256,256]{2,1,0:T(8,128)(2,1)S(1)}, u32[]{:S(2)}, u32[]{:S(2)}) collective-permute-start(bf16[1,256,256]{2,1,0:T(8,128)(2,1)} %get-tuple-element.62), channel_id=1, source_target_pairs={{30,24},{31,25}} | collective-permute-start | bytes 393224 | tf_op jit(solution)/shard_map/ppermute | solution.py:312
  46.6 6.5 %collective-permute-start.7 = (bf16[1,256,256]{2,1,0:T(8,128)(2,1)}, bf16[1,256,256]{2,1,0:T(8,128)(2,1)S(1)}, u32[]{:S(2)}, u32[]{:S(2)}) collective-permute-start(bf16[1,256,256]{2,1,0:T(8,128)(2,1)} %get-tuple-element.63), channel_id=1, source_target_pairs={{30,26},{31,27}} | collective-permute-start | bytes 393224 | tf_op jit(solution)/shard_map/ppermute | solution.py:312
  47.3 5.8 %collective-permute-start.8 = (bf16[1,256,256]{2,1,0:T(8,128)(2,1)}, bf16[1,256,256]{2,1,0:T(8,128)(2,1)S(1)}, u32[]{:S(2)}, u32[]{:S(2)}) collective-permute-start(bf16[1,256,256]{2,1,0:T(8,128)(2,1)} %get-tuple-element.64), channel_id=1, source_target_pairs={{30,28},{31,29}} | collective-permute-start | bytes 393224 | tf_op jit(solution)/shard_map/ppermute | solution.py:312
  48.1 16.0 %collective-permute-start.15 = (bf16[1,256,256]{2,1,0:T(8,128)(2,1)S(1)}, bf16[1,256,256]{2,1,0:T(8,128)(2,1)S(1)}, u32[]{:S(2)}, u32[]{:S(2)}) collective-permute-start(bf16[1,256,256]{2,1,0:T(8,128)(2,1)S(1)} %select_select_fusion), channel_id=1, source_target_pairs={{0,16},{1,17},{2,18},{3,19},{4,20},{5,21},{6,22},{7,23},{8,24},{9,... | collective-permute-start | bytes 393224 | tf_op jit(solution)/shard_map/ppermute | solution.py:328
  53.2 10.9 %collective-permute-start.16 = (bf16[1,256,256]{2,1,0:T(8,128)(2,1)S(1)}, bf16[1,256,256]{2,1,0:T(8,128)(2,1)S(1)}, u32[]{:S(2)}, u32[]{:S(2)}) collective-permute-start(bf16[1,256,256]{2,1,0:T(8,128)(2,1)S(1)} %select_select_fusion.1), channel_id=1, source_target_pairs={{16,0},{17,1},{18,2},{19,3},{20,4},{21,5},{22,6},{23,7},{24,8},{25... | collective-permute-start | bytes 393224 | tf_op jit(solution)/shard_map/ppermute | solution.py:330
  54.5 1.6 %copy-start.9 = (f32[2,2048,128]{2,1,0:T(8,128)S(1)}, f32[2,2048,128]{2,1,0:T(8,128)}, u32[]{:S(2)}) copy-start(f32[2,2048,128]{2,1,0:T(8,128)} %copy-done.8) | copy-start | bytes 6291460
  62.7 1.3 %copy-start.12 = (f32[2,2048,128]{2,1,0:T(8,128)}, f32[2,2048,128]{2,1,0:T(8,128)S(1)}, u32[]{:S(2)}) copy-start(f32[2,2048,128]{2,1,0:T(8,128)S(1)} %moved_keys.2.refs_5_) | copy-start | bytes 6291460
  64.2 12.2 %copy-start.4 = (s32[32]{0:T(128)S(1)}, s32[32]{0:T(128)}, u32[]{:S(2)}) copy-start(s32[32]{0:T(128)} %reader_ref.11) | copy-start | bytes 388
  64.2 12.2 %collective-permute-start.17 = (bf16[2,256,256]{2,1,0:T(8,128)(2,1)S(1)}, bf16[2,256,256]{2,1,0:T(8,128)(2,1)S(1)}, u32[]{:S(2)}, u32[]{:S(2)}) collective-permute-start(bf16[2,256,256]{2,1,0:T(8,128)(2,1)S(1)} %maximum_select_fusion.refs_0_), channel_id=1, source_target_pairs={{0,2},{1,3},{2,0},{3,1},{4,6},{5,7},{6,4},{7,5},{8,10},{9,11},{10,... | collective-permute-start | bytes 786440 | tf_op jit(solution)/shard_map/ppermute | solution.py:358
  66.5 9.9 %collective-permute-start.19 = (bf16[2,256,256]{2,1,0:T(8,128)(2,1)S(1)}, bf16[2,256,256]{2,1,0:T(8,128)(2,1)S(1)}, u32[]{:S(2)}, u32[]{:S(2)}) collective-permute-start(bf16[2,256,256]{2,1,0:T(8,128)(2,1)S(1)} %maximum_select_fusion.refs_0_), channel_id=1, source_target_pairs={{0,8},{1,9},{2,10},{3,11},{4,12},{5,13},{6,14},{7,15},{8,0},{9,1},... | collective-permute-start | bytes 786440 | tf_op jit(solution)/shard_map/ppermute | solution.py:358
  66.5 9.9 %collective-permute-start.21 = (bf16[2,256,256]{2,1,0:T(8,128)(2,1)S(1)}, bf16[2,256,256]{2,1,0:T(8,128)(2,1)S(1)}, u32[]{:S(2)}, u32[]{:S(2)}) collective-permute-start(bf16[2,256,256]{2,1,0:T(8,128)(2,1)S(1)} %maximum_select_fusion.refs_0_), channel_id=1, source_target_pairs={{0,4},{1,5},{2,6},{3,7},{4,0},{5,1},{6,2},{7,3},{8,12},{9,13},{10,... | collective-permute-start | bytes 786440 | tf_op jit(solution)/shard_map/ppermute | solution.py:358
  70.7 39.4 %all-to-all-start.1 = ((bf16[32,64,256]{2,1,0:T(8,128)(2,1)}), bf16[32,64,256]{2,1,0:T(8,128)(2,1)S(1)}, u32[]{:S(2)}, u32[]{:S(2)}) async-start(bf16[32,64,256]{2,1,0:T(8,128)(2,1)} %gate.1), calls=%async_computation.1 | async-start | bytes 2097152 | tf_op jit(solution)/shard_map/all_to_all | solution.py:344
  77.0 4.8 %collective-permute-start.23 = (bf16[1024,256]{1,0:T(8,128)(2,1)S(1)}, bf16[1024,256]{1,0:T(8,128)(2,1)S(1)}, u32[]{:S(2)}, u32[]{:S(2)}) collective-permute-start(bf16[1024,256]{1,0:T(8,128)(2,1)S(1)} %pick_other.3), channel_id=1, source_target_pairs={{0,1},{1,0},{2,3},{3,2},{4,5},{5,4},{6,7},{7,6},{8,9},{9,8},{10,11... | collective-permute-start | bytes 1572872 | tf_op jit(solution)/shard_map/ppermute | solution.py:348
  77.1 16.4 %collective-permute-start.18 = (bf16[2,256,256]{2,1,0:T(8,128)(2,1)S(1)}, bf16[2,256,256]{2,1,0:T(8,128)(2,1)S(1)}, u32[]{:S(2)}, u32[]{:S(2)}) collective-permute-start(bf16[2,256,256]{2,1,0:T(8,128)(2,1)S(1)} %collective-permute-done.17.refs_1_), channel_id=1, source_target_pairs={{0,4},{1,5},{2,6},{3,7},{4,0},{5,1},{6,2},{7,3},{8,12},{9,13},{10,... | collective-permute-start | bytes 786440 | tf_op jit(solution)/shard_map/ppermute | solution.py:358
  78.8 15.7 %collective-permute-start.20 = (bf16[2,256,256]{2,1,0:T(8,128)(2,1)S(1)}, bf16[2,256,256]{2,1,0:T(8,128)(2,1)S(1)}, u32[]{:S(2)}, u32[]{:S(2)}) collective-permute-start(bf16[2,256,256]{2,1,0:T(8,128)(2,1)S(1)} %collective-permute-done.19.refs_3_), channel_id=1, source_target_pairs={{0,2},{1,3},{2,0},{3,1},{4,6},{5,7},{6,4},{7,5},{8,10},{9,11},{10,... | collective-permute-start | bytes 786440 | tf_op jit(solution)/shard_map/ppermute | solution.py:358
  80.3 19.8 %collective-permute-start.22 = (bf16[2,256,256]{2,1,0:T(8,128)(2,1)S(1)}, bf16[2,256,256]{2,1,0:T(8,128)(2,1)S(1)}, u32[]{:S(2)}, u32[]{:S(2)}) collective-permute-start(bf16[2,256,256]{2,1,0:T(8,128)(2,1)S(1)} %collective-permute-done.21.refs_2_), channel_id=1, source_target_pairs={{0,8},{1,9},{2,10},{3,11},{4,12},{5,13},{6,14},{7,15},{8,0},{9,1},... | collective-permute-start | bytes 786440 | tf_op jit(solution)/shard_map/ppermute | solution.py:358
  81.7 1.6 %copy-start.13 = (f32[2,2048,128]{2,1,0:T(8,128)S(1)}, f32[2,2048,128]{2,1,0:T(8,128)}, u32[]{:S(2)}) copy-start(f32[2,2048,128]{2,1,0:T(8,128)} %copy-done.12) | copy-start | bytes 6291460
  100.7 1.8 %collective-permute-start.25 = (bf16[768,256]{1,0:T(8,128)(2,1)S(1)}, bf16[768,256]{1,0:T(8,128)(2,1)S(1)}, u32[]{:S(2)}, u32[]{:S(2)}) collective-permute-start(bf16[768,256]{1,0:T(8,128)(2,1)S(1)} %pick_other.4), channel_id=1, source_target_pairs={{0,1},{1,0},{2,3},{3,2},{4,5},{5,4},{6,7},{7,6},{8,9},{9,8},{10,11... | collective-permute-start | bytes 1179656 | tf_op jit(solution)/shard_map/ppermute | solution.py:348
  100.8 8.7 %collective-permute-start.24 = (bf16[2,256,256]{2,1,0:T(8,128)(2,1)S(1)}, bf16[2,256,256]{2,1,0:T(8,128)(2,1)S(1)}, u32[]{:S(2)}, u32[]{:S(2)}) collective-permute-start(bf16[2,256,256]{2,1,0:T(8,128)(2,1)S(1)} %collective-permute-done.22.refs_2_), channel_id=1, source_target_pairs={{0,2},{1,3},{2,0},{3,1},{4,6},{5,7},{6,4},{7,5},{8,10},{9,11},{10,... | collective-permute-start | bytes 786440 | tf_op jit(solution)/shard_map/ppermute | solution.py:358
  107.5 1.3 %copy-start.10 = (f32[2,2048,128]{2,1,0:T(8,128)}, f32[2,2048,128]{2,1,0:T(8,128)S(1)}, u32[]{:S(2)}) copy-start(f32[2,2048,128]{2,1,0:T(8,128)S(1)} %prefix_keys.4.loaded_ref) | copy-start | bytes 6291460
  110.0 8.3 %collective-permute-start.26 = (bf16[256,256]{1,0:T(8,128)(2,1)S(1)}, bf16[256,256]{1,0:T(8,128)(2,1)S(1)}, u32[]{:S(2)}, u32[]{:S(2)}) collective-permute-start(bf16[256,256]{1,0:T(8,128)(2,1)S(1)} %pick_other.5), channel_id=1, source_target_pairs={{0,1},{1,0},{2,3},{3,2},{4,5},{5,4},{6,7},{7,6},{8,9},{9,8},{10,11... | collective-permute-start | bytes 393224 | tf_op jit(solution)/shard_map/ppermute | solution.py:348
  110.1 1.6 %copy-start.11 = (f32[2,2048,128]{2,1,0:T(8,128)S(1)}, f32[2,2048,128]{2,1,0:T(8,128)}, u32[]{:S(2)}) copy-start(f32[2,2048,128]{2,1,0:T(8,128)} %copy-done.10) | copy-start | bytes 6291460

commit v20 on v19

--- a/solution.py
+++ b/solution.py
@@ -121,7 +121,7 @@
         save_state(*work[1:], out_ref)
 
 
-def prefix_kernel(factor, last, count, steps, owner_ref, reader_ref, me_ref, q_ref, *refs):
+def prefix_kernel(factor, count, steps, owner_ref, reader_ref, me_ref, q_ref, *refs):
     pieces = refs[:count]
     loaded_ref, out_ref, *work, rows_ref = refs[count:]
     step = pl.program_id(0)
@@ -142,20 +142,37 @@
 
     @pl.when(step == steps - 1)
     def _():
-        if last:
-            finish(*work[2:], out_ref)
-        else:
-            save_state(*work[1:], out_ref)
-
-
-def start_all(copies):
-    for copy in copies:
-        copy.start()
+        save_state(*work[1:], out_ref)
 
 
 def wait_all(copies):
     for copy in copies:
         copy.wait()
+
+
+def last_kernel(factor, steps, owner_ref, reader_ref, me_ref, q_ref, kv_ref, *refs):
+    *pieces, loaded_ref, out_ref = refs[:-5]
+    *work, rows_ref = refs[-5:]
+    step = pl.program_id(0)
+    size = work[3].shape[1]
+
+    @pl.when(step == 0)
+    def _():
+        stack_queries(q_ref, work[0])
+        load_state(loaded_ref, *work[1:])
+        place = 0
+        for piece in pieces:
+            rows_ref[pl.ds(place, piece.shape[0]), :] = piece[...]
+            place += piece.shape[0]
+
+    rows = kv_ref[...].reshape(-1, kv_ref.shape[-1])
+    dead = jnp.where(rows[:, size:].astype(jnp.float32) > DEAD_ABOVE, NEG, 0.0).T[:1]
+    fold_keys(work, rows[:, :size], rows[:, size:], factor, dead)
+
+    @pl.when(step == steps - 1)
+    def _():
+        fold_keys(work, rows_ref[:, :size], rows_ref[:, size:], factor)
+        finish(*work[2:], out_ref)
 
 
 def pick_kernel(owner_ref, reader_ref, me_ref, *refs):
@@ -164,43 +181,34 @@
         out_ref[pl.ds(place * piece.shape[0], piece.shape[0]), :] = piece[...]
 
 
-def pack_kernel(target_ref, block_ref, count_ref, pool_ref, *refs):
-    parts, (held_ref, mark_ref, in_sems, out_sems) = refs[:-4], refs[-4:]
-    entries = target_ref.shape[1]
+def pack_kernel(first, target_ref, block_ref, count_ref, pool_ref, *refs):
+    out_ref, held_ref, mark_ref, in_sems, out_sems = refs[-5:]
+    entries, rows = held_ref.shape[:2]
     mark_ref[...] = jnp.full(mark_ref.shape, DEAD_MARK, mark_ref.dtype)
 
     def load(entry):
-        return pltpu.make_async_copy(
-            pool_ref.at[block_ref[0, entry]], held_ref.at[entry], in_sems.at[entry]
-        )
-
-    def stores(entry, source):
-        rows = parts[0].shape[1]
-        return [
-            pltpu.make_async_copy(
-                source.at[pl.ds(place * rows, rows)],
-                part.at[target_ref[0, entry]],
-                out_sems.at[place, entry],
-            )
-            for place, part in enumerate(parts)
-        ]
+        source = pool_ref.at[block_ref[0, entry], pl.ds(first, rows)]
+        return pltpu.make_async_copy(source, held_ref.at[entry], in_sems.at[entry])
+
+    def store(entry, source):
+        return pltpu.make_async_copy(source, out_ref.at[target_ref[0, entry]], out_sems.at[entry])
 
     @pl.loop(0, entries)
     def _(entry):
         live = entry < count_ref[0]
         pl.when(live)(lambda: load(entry).start())
-        pl.when(jnp.logical_not(live))(lambda: start_all(stores(entry, mark_ref)))
+        pl.when(jnp.logical_not(live))(lambda: store(entry, mark_ref).start())
 
     @pl.loop(0, entries)
     def _(entry):
         @pl.when(entry < count_ref[0])
         def _():
             load(entry).wait()
-            start_all(stores(entry, held_ref.at[entry]))
+            store(entry, held_ref.at[entry]).start()
 
     @pl.loop(0, entries)
     def _(entry):
-        wait_all(stores(entry, mark_ref))
+        store(entry, mark_ref).wait()
 
 
 def gate_kernel(*refs):
@@ -269,7 +277,7 @@
     wait_all([store(step) for step in range(chips)])
 
 
-def multicast(prefix_cache, owners, outgoing, fold_local, fold_moved):
+def multicast(prefix_cache, owners, pack, fold_local, fold_moved):
     replicas = lax.axis_size("replica")
     half = replicas // 2
     chips = half // 2
@@ -277,8 +285,8 @@
     prefixes = owners.shape[0]
 
     split = prefix_cache.reshape(2, chips, -1, width)
-    swapped, *outgoing = lax.optimization_barrier((swap_cores(prefix_cache), *outgoing))
-    arrived = send_blocks(outgoing[0])
+    swapped, outgoing = lax.optimization_barrier((swap_cores(prefix_cache), pack(0)))
+    arrived = send_blocks(outgoing)
     swapped = swapped.reshape(split.shape)
     pieces = jax.ShapeDtypeStruct((owners.shape[0] - 1, *split.shape[2:]), split.dtype)
     piece = jax.ShapeDtypeStruct((1, *split.shape[2:]), split.dtype)
@@ -328,7 +336,7 @@
     passed = lax.ppermute(found, "replica", [(i, (i + half) % replicas) for i in range(replicas)])
     found_known = choose(known_staged[0], passed_known, known_away)
     passed_known = lax.ppermute(found_known, "replica", [(i + half, i) for i in range(half)])
-    later = send_blocks(gate(outgoing[1], passed, passed_known))
+    later = send_blocks(gate(pack(1, staged[0]), passed, passed_known))
     passed, passed_known, state_now = lax.optimization_barrier(
         (passed, passed_known, fold_moved(arrived, local))
     )
@@ -426,22 +434,24 @@
     ]
 
     entries = mig_target.shape[1]
-    half_block = (replicas, kv_pool.shape[1] // 2, kv_pool.shape[2])
-    slots = (jax.ShapeDtypeStruct(half_block, kv_pool.dtype),) * 2
-    outgoing = pl.pallas_call(
-        pack_kernel,
-        out_shape=slots,
-        in_specs=[IN_SMEM] * 3 + [IN_HBM],
-        out_specs=(IN_HBM,) * 2,
-        scratch_shapes=[
-            pltpu.VMEM((entries, *kv_pool.shape[1:]), kv_pool.dtype),
-            pltpu.VMEM(kv_pool.shape[1:], kv_pool.dtype),
-            pltpu.SemaphoreType.DMA((entries,)),
-            pltpu.SemaphoreType.DMA((2, entries)),
-        ],
-        compiler_params=COPY_PARAMS,
-        name="pack_moved",
-    )(mig_target, mig_block, mig_count, kv_pool)
+    half_block = (kv_pool.shape[1] // 2, kv_pool.shape[2])
+
+    def pack(part, *after):
+        return pl.pallas_call(
+            functools.partial(pack_kernel, part * half_block[0]),
+            out_shape=jax.ShapeDtypeStruct((replicas, *half_block), kv_pool.dtype),
+            in_specs=[IN_SMEM] * 3 + [IN_HBM] * (1 + len(after)),
+            out_specs=IN_HBM,
+            scratch_shapes=[
+                pltpu.VMEM((entries, *half_block), kv_pool.dtype),
+                pltpu.VMEM(half_block, kv_pool.dtype),
+                pltpu.SemaphoreType.DMA((entries,)),
+                pltpu.SemaphoreType.DMA((entries,)),
+            ],
+            compiler_params=COPY_PARAMS,
+            name="pack_moved",
+        )(mig_target, mig_block, mig_count, kv_pool, *after)
+
     def fold_local(after):
         return pl.pallas_call(
             functools.partial(local_kernel, factor),
@@ -481,33 +491,32 @@
             name="moved_keys",
         )(queries, arrived, state_now)
 
-    def fold_prefix(pieces, state_now, last=False):
+    def wanted_pieces(pieces):
+        spec = pl.BlockSpec(
+            (None, *pieces[0].shape[1:]),
+            lambda i, owner, reader, me: (wanted_place(owner, reader, me[0]), 0, 0),
+        )
+        return [spec] * len(pieces)
+
+    def fold_prefix(pieces, state_now):
         others = from_other(pieces, scalars)
-        rows = pieces[0].shape[1]
-        keys = 2 * len(pieces) * rows
+        keys = 2 * len(pieces) * pieces[0].shape[1]
         steps = max(1, keys // CHUNK)
         while keys % (steps * size):
             steps -= 1
-        target = result if last else state
         return pl.pallas_call(
-            functools.partial(prefix_kernel, factor, last, len(pieces) + 1, steps),
-            out_shape=target,
+            functools.partial(prefix_kernel, factor, len(pieces) + 1, steps),
+            out_shape=state,
             grid_spec=pltpu.PrefetchScalarGridSpec(
                 num_scalar_prefetch=3,
                 grid=(steps,),
                 in_specs=[
                     whole(queries.shape),
-                    *[
-                        pl.BlockSpec(
-                            (None, rows, 2 * size),
-                            lambda i, owner, reader, me: (wanted_place(owner, reader, me[0]), 0, 0),
-                        )
-                    ]
-                    * len(pieces),
+                    *wanted_pieces(pieces),
                     whole(others.shape),
                     whole(state.shape),
                 ],
-                out_specs=whole(target.shape),
+                out_specs=whole(state.shape),
                 scratch_shapes=[*work, pltpu.VMEM((keys, 2 * size), jnp.bfloat16)],
             ),
             compiler_params=PARAMS,
@@ -515,7 +524,34 @@
             name="prefix_keys",
         )(*scalars, queries, *pieces, others, state_now)
 
-    held, state_now, later = multicast(prefix_cache, owners, outgoing, fold_local, fold_moved)
+    def fold_last(arrived, pieces, state_now):
+        others = from_other(pieces, scalars)
+        keys = 2 * len(pieces) * pieces[0].shape[1]
+        rows = arrived.shape[1]
+        group = max(n for n in range(1, replicas + 1) if replicas % n == 0 and n * rows <= CHUNK)
+        steps = replicas // group
+        return pl.pallas_call(
+            functools.partial(last_kernel, factor, steps),
+            out_shape=result,
+            grid_spec=pltpu.PrefetchScalarGridSpec(
+                num_scalar_prefetch=3,
+                grid=(steps,),
+                in_specs=[
+                    whole(queries.shape),
+                    pl.BlockSpec((group, rows, 2 * size), lambda i, *scalars: (i, 0, 0)),
+                    *wanted_pieces(pieces),
+                    whole(others.shape),
+                    whole(state.shape),
+                ],
+                out_specs=whole(queries.shape),
+                scratch_shapes=[*work, pltpu.VMEM((keys, 2 * size), jnp.bfloat16)],
+            ),
+            compiler_params=PARAMS,
+            cost_estimate=cost(row_count, replicas * rows + keys, size),
+            name="last_keys",
+        )(*scalars, queries, arrived, *pieces, others, state_now)
+
+    held, state_now, later = multicast(prefix_cache, owners, pack, fold_local, fold_moved)
     scalars = (owners, readers, lax.axis_index("replica")[None])
     gathered = {0: held}
     ready = [held]
@@ -530,7 +566,7 @@
             ready = []
         gathered.update(zip(steps, coming))
         ready += coming
-    return fold_prefix(ready, fold_moved(later, state_now), True)
+    return fold_last(later, ready, state_now)
 
 
 def solution(mesh):

time: 123 us -> 139 us (1.13)
  waiting for transfers between devices: 16.8 us -> 28.2 us
  local copies, waits for them, and re-layouts: 10.3 us -> 14.5 us
  Pallas kernels: 40.4 us -> 43.1 us
  starting transfers between devices: 49.8 us -> 47.7 us
    pallas_call x4 -> x5, Pallas kernels: 19.5 us -> 29 us  [the longest x2 12.9 us: fold_prefix(): pl.pallas_call(functools.partial(prefix_kernel, factor, len(pieces) + 1,...]
    pallas_call x2 -> x1, Pallas kernels: 13.3 us -> 6.65 us  [fold_moved(): pl.pallas_call(functools.partial(moved_kernel, factor, steps), out_shape=...]
    unnamed x32 -> x42, local copies, waits for them, and re-layouts: 9.7 us -> 13.9 us
    ppermute x1, waiting for transfers between devices: 0.01 us -> 4.18 us  [multicast(): lax.ppermute(found_known, 'replica', [(i + half, i) for i in range(half)])]
    ppermute x7, waiting for transfers between devices: 10.5 us -> 13.8 us  [gather_step(): return lax.ppermute(gathered[step ^ 1 << last], 'replica', pairs)]
    all_to_all x2, starting transfers between devices: 12.6 us -> 15.3 us  [send_blocks(): lax.all_to_all(rows, 'replica', split_axis=0, concat_axis=0, tiled=True)]
    ppermute x14, waiting for transfers between devices: 6.09 us -> 8.63 us  [to_peers(): lax.ppermute(rows, 'replica', [(i, i ^ 2 * step) for i in senders])]
    ppermute x14, starting transfers between devices: 17.5 us -> 15.1 us  [to_peers(): lax.ppermute(rows, 'replica', [(i, i ^ 2 * step) for i in senders])]
  transfers between devices with their start and end apart: 29 -> 29, of which waited for: 7 -> 14; matrix products, arithmetic and copies ran while one was open for 1% -> 1% of each run, Pallas kernels for 30% -> 24%
where the time goes in v20:
time: 139 us; the launch traced here: 138 us
  starting transfers between devices  47.7 us (34%)
  Pallas kernels  43.1 us (31%)
  waiting for transfers between devices  28.2 us (20%)
  local copies, waits for them, and re-layouts  14.5 us (10%)
  between operations  3.68 us (3%)
    all_to_all x2, starting transfers between devices, send_blocks(): lax.all_to_all(rows, 'replica', split_axis=0, concat_axis=0, tiled=True)  15.3 us
    ppermute x14, starting transfers between devices, to_peers(): lax.ppermute(rows, 'replica', [(i, i ^ 2 * step) for i in senders])  15.1 us
    unnamed x42, local copies, waits for them, and re-layouts  13.9 us
    ppermute x7, waiting for transfers between devices, gather_step(): return lax.ppermute(gathered[step ^ 1 << last], 'replica', pairs)  13.8 us
    pallas_call x2, Pallas kernels, fold_prefix(): pl.pallas_call(functools.partial(prefix_kernel, factor, len(pieces) + 1,...  12.9 us
    ppermute x7, starting transfers between devices, gather_step(): return lax.ppermute(gathered[step ^ 1 << last], 'replica', pairs)  10.3 us
    pallas_call x1, Pallas kernels, fold_last(): pl.pallas_call(functools.partial(last_kernel, factor, steps), out_shape=r...  9.67 us
    ppermute x14, waiting for transfers between devices, to_peers(): lax.ppermute(rows, 'replica', [(i, i ^ 2 * step) for i in senders])  8.63 us
  transfers between devices with their start and end apart: 29, of which 14 were waited for; matrix products, arithmetic and copies ran while one was open for 1% of the time, Pallas kernels for 24%

profile of v20, /device:TPU:0, one launch (start us, length us, event | category | flops | bytes accessed | tf_op | source)
XLA Modules:
  0.0 138.1 jit_solution(2744427691328590423)
XLA Ops:
  1.1 3.3 %pack_moved.2 = bf16[32,64,256]{2,1,0:T(8,128)(2,1)} custom-call(s32[1,32]{1,0:T(1,128)} %target_ref.3, s32[1,32]{1,0:T(1,128)} %block_ref.3, s32[1]{0:T(128)S(6)} %copy.15.count_ref, bf16[32,128,256]{2,1,0:T(8,128)(2,1)} %pool_ref.3), custom_call_target="tpu_custom_call" | custom-call | tf_op jit(solution)/shard_map/pack_moved/pallas_call | solution.py:440
  4.6 7.2 %all-to-all-start.1 = ((bf16[32,64,256]{2,1,0:T(8,128)(2,1)}), bf16[32,64,256]{2,1,0:T(8,128)(2,1)S(1)}, u32[]{:S(2)}, u32[]{:S(2)}) async-start(bf16[32,64,256]{2,1,0:T(8,128)(2,1)} %pack_moved.2), calls=%async_computation.1 | async-start | bytes 2097152 | tf_op jit(solution)/shard_map/all_to_all | solution.py:352
  13.1 3.0 %stage_prefix.1 = (bf16[1,256,256]{2,1,0:T(8,128)(2,1)}, bf16[1,256,256]{2,1,0:T(8,128)(2,1)}, bf16[1,256,256]{2,1,0:T(8,128)(2,1)}, bf16[1,256,256]{2,1,0:T(8,1...) custom-call(s32[2]{0:T(128)} %owner_ref.13, ...), custom_call_target="tpu_custom_call" | custom-call | tf_op jit(solution)/shard_map/stage_prefix/pallas_call | solution.py:293
  16.1 1.8 %collective-permute-start.7 = (bf16[1,256,256]{2,1,0:T(8,128)(2,1)}, bf16[1,256,256]{2,1,0:T(8,128)(2,1)S(1)}, u32[]{:S(2)}, u32[]{:S(2)}) collective-permute-start(bf16[1,256,256]{2,1,0:T(8,128)(2,1)} %get-tuple-element.50), channel_id=1, source_target_pairs={{0,2},{1,3},{2,0},{3,1},{4,6},{5,7},{6,4},{7,5},{8,10},{9,11},{10,... | collective-permute-start | bytes 393224 | tf_op jit(solution)/shard_map/ppermute | solution.py:320
  17.9 2.4 %collective-permute-start.1 = (bf16[1,256,256]{2,1,0:T(8,128)(2,1)}, bf16[1,256,256]{2,1,0:T(8,128)(2,1)S(1)}, u32[]{:S(2)}, u32[]{:S(2)}) collective-permute-start(bf16[1,256,256]{2,1,0:T(8,128)(2,1)} %get-tuple-element.44), channel_id=1, source_target_pairs={{0,14},{1,15},{2,12},{3,13},{4,10},{5,11},{6,8},{7,9},{8,6},{9,7},... | collective-permute-start | bytes 393224 | tf_op jit(solution)/shard_map/ppermute | solution.py:320
  20.6 2.7 %collective-permute-start.3 = (bf16[1,256,256]{2,1,0:T(8,128)(2,1)}, bf16[1,256,256]{2,1,0:T(8,128)(2,1)S(1)}, u32[]{:S(2)}, u32[]{:S(2)}) collective-permute-start(bf16[1,256,256]{2,1,0:T(8,128)(2,1)} %get-tuple-element.46), channel_id=1, source_target_pairs={{0,10},{1,11},{2,8},{3,9},{4,14},{5,15},{6,12},{7,13},{8,2},{9,3},... | collective-permute-start | bytes 393224 | tf_op jit(solution)/shard_map/ppermute | solution.py:320
  23.8 0.9 copy-done.2
  24.7 0.9 copy-done.10
  25.7 2.7 %local_keys.1.loaded_ref = f32[2,2048,128]{2,1,0:T(8,128)S(1)} custom-call(s32[1]{0:T(128)S(6)} %copy.14.len_ref, bf16[256,1024]{1,0:T(8,128)(2,1)S(1)} %copy-done.7, bf16[256,256]{1,0:T(8,128)(2,1)S(1)} %copy-done.11, bf16[512,256]{1,0:T(8,128)(2,1)S(1)} %copy-done.10, bf16[1,256,256]{2,1,0:T(8,128)(2,1)S(1)} %copy-done.2), custom_call_target="tpu_custom_call" | custom-call | flops 2415919104 | bytes 393216 | tf_op jit(solution)/shard_map/local_keys/pallas_call | solution.py:456
  28.4 1.3 copy-done.12
  29.7 1.5 %collective-permute-start.5 = (bf16[1,256,256]{2,1,0:T(8,128)(2,1)}, bf16[1,256,256]{2,1,0:T(8,128)(2,1)S(1)}, u32[]{:S(2)}, u32[]{:S(2)}) collective-permute-start(bf16[1,256,256]{2,1,0:T(8,128)(2,1)} %get-tuple-element.48), channel_id=1, source_target_pairs={{0,6},{1,7},{2,4},{3,5},{4,2},{5,3},{6,0},{7,1},{8,14},{9,15},{10,... | collective-permute-start | bytes 393224 | tf_op jit(solution)/shard_map/ppermute | solution.py:320
  31.2 2.1 %collective-permute-done.1 = bf16[1,256,256]{2,1,0:T(8,128)(2,1)S(1)} collective-permute-done((bf16[1,256,256]{2,1,0:T(8,128)(2,1)}, bf16[1,256,256]{2,1,0:T(8,128)(2,1)S(1)}, u32[]{:S(2)}, u32[]{:S(2)}) %collective-permute-start.1) | collective-permute-done | bytes 131104 | tf_op jit(solution)/shard_map/ppermute | solution.py:320
  33.3 1.3 collective-permute-start.6
  34.6 4.5 %collective-permute-done.2 = bf16[1,256,256]{2,1,0:T(8,128)(2,1)S(1)} collective-permute-done((bf16[1,256,256]{2,1,0:T(8,128)(2,1)}, bf16[1,256,256]{2,1,0:T(8,128)(2,1)S(1)}, u32[]{:S(2)}, u32[]{:S(2)}) %collective-permute-start.2) | collective-permute-done | bytes 131104 | tf_op jit(solution)/shard_map/ppermute | solution.py:320
  39.7 2.0 %collective-permute-done.3 = bf16[1,256,256]{2,1,0:T(8,128)(2,1)S(1)} collective-permute-done((bf16[1,256,256]{2,1,0:T(8,128)(2,1)}, bf16[1,256,256]{2,1,0:T(8,128)(2,1)S(1)}, u32[]{:S(2)}, u32[]{:S(2)}) %collective-permute-start.3) | collective-permute-done | bytes 131104 | tf_op jit(solution)/shard_map/ppermute | solution.py:320
  45.1 0.7 collective-permute-start.12
  45.8 0.7 collective-permute-start.13
  46.5 0.7 collective-permute-start.14
  47.8 0.7 collective-permute-start.9
  48.6 5.1 %collective-permute-start.8 = (bf16[1,256,256]{2,1,0:T(8,128)(2,1)S(1)}, bf16[1,256,256]{2,1,0:T(8,128)(2,1)S(1)}, u32[]{:S(2)}, u32[]{:S(2)}) collective-permute-start(bf16[1,256,256]{2,1,0:T(8,128)(2,1)S(1)} %select_select_fusion.1), channel_id=1, source_target_pairs={{0,16},{1,17},{2,18},{3,19},{4,20},{5,21},{6,22},{7,23},{8,24},{9,... | collective-permute-start | bytes 393224 | tf_op jit(solution)/shard_map/ppermute | solution.py:336
  53.8 1.3 collective-permute-start.16
  55.1 1.6 %copy-done.13 = f32[2,2048,128]{2,1,0:T(8,128)S(1)} copy-done((f32[2,2048,128]{2,1,0:T(8,128)S(1)}, f32[2,2048,128]{2,1,0:T(8,128)}, u32[]{:S(2)}) %copy-start.13) | copy-done | bytes 2097176
  56.7 6.6 %moved_keys.1.refs_5_ = f32[2,2048,128]{2,1,0:T(8,128)S(1)} custom-call(bf16[256,1024]{1,0:T(8,128)(2,1)S(1)} %copy-done.7, bf16[32,64,256]{2,1,0:T(8,128)(2,1)S(1)} %all-to-all-done.1.kv_ref, f32[2,2048,128]{2,1,0:T(8,128)S(1)} %copy-done.13), custom_call_target="tpu_custom_call" | custom-call | flops 6442450944 | bytes 1048576 | tf_op jit(solution)/shard_map/moved_keys/pallas_call | solution.py:478
  63.4 1.3 copy-done.16
  64.7 4.2 %collective-permute-done.16.refs_2_ = bf16[1,256,256]{2,1,0:T(8,128)(2,1)S(1)} collective-permute-done((bf16[1,256,256]{2,1,0:T(8,128)(2,1)S(1)}, bf16[1,256,256]{2,1,0:T(8,128)(2,1)S(1)}, u32[]{:S(2)}, u32[]{:S(2)}) %collective-permute-start.16) | collective-permute-done | bytes 131104 | tf_op jit(solution)/shard_map/ppermute | solution.py:338
  69.2 4.0 %collective-permute-start.21 = (bf16[2,256,256]{2,1,0:T(8,128)(2,1)S(1)}, bf16[2,256,256]{2,1,0:T(8,128)(2,1)S(1)}, u32[]{:S(2)}, u32[]{:S(2)}) collective-permute-start(bf16[2,256,256]{2,1,0:T(8,128)(2,1)S(1)} %maximum_select_fusion.refs_0_), channel_id=1, source_target_pairs={{0,4},{1,5},{2,6},{3,7},{4,0},{5,1},{6,2},{7,3},{8,12},{9,13},{10,... | collective-permute-start | bytes 786440 | tf_op jit(solution)/shard_map/ppermute | solution.py:366
  73.1 2.3 %collective-permute-done.17.refs_1_ = bf16[2,256,256]{2,1,0:T(8,128)(2,1)S(1)} collective-permute-done((bf16[2,256,256]{2,1,0:T(8,128)(2,1)S(1)}, bf16[2,256,256]{2,1,0:T(8,128)(2,1)S(1)}, u32[]{:S(2)}, u32[]{:S(2)}) %collective-permute-start.17) | collective-permute-done | bytes 262176 | tf_op jit(solution)/shard_map/ppermute | solution.py:366
  75.5 2.1 %collective-permute-done.21.refs_2_ = bf16[2,256,256]{2,1,0:T(8,128)(2,1)S(1)} collective-permute-done((bf16[2,256,256]{2,1,0:T(8,128)(2,1)S(1)}, bf16[2,256,256]{2,1,0:T(8,128)(2,1)S(1)}, u32[]{:S(2)}, u32[]{:S(2)}) %collective-permute-start.21) | collective-permute-done | bytes 262176 | tf_op jit(solution)/shard_map/ppermute | solution.py:366
  78.3 3.2 %pack_moved.3.refs_0_ = bf16[32,64,256]{2,1,0:T(8,128)(2,1)} custom-call(s32[1,32]{1,0:T(1,128)} %target_ref.3, s32[1,32]{1,0:T(1,128)} %block_ref.3, s32[1]{0:T(128)S(6)} %copy.15.count_ref, bf16[32,128,256]{2,1,0:T(8,128)(2,1)} %pool_ref.3, bf16[1,256,256]{2,1,0:T(8,128)(2,1)} %get-tuple-element.43.refs_0_.after_ref), custom_call_target="tpu_custom_call" | custom-call | tf_op jit(solution)/shard_map/pack_moved/pallas_call | solution.py:440
  81.5 1.2 copy-done
  82.7 1.0 copy-done.1
  83.7 8.1 %all-to-all-start = ((bf16[32,64,256]{2,1,0:T(8,128)(2,1)}), bf16[32,64,256]{2,1,0:T(8,128)(2,1)S(1)}, u32[]{:S(2)}, u32[]{:S(2)}) async-start(bf16[32,64,256]{2,1,0:T(8,128)(2,1)} %copy-done.1), calls=%async_computation | async-start | bytes 2097152 | tf_op jit(solution)/shard_map/all_to_all | solution.py:352
  91.7 1.7 %collective-permute-start.18 = (bf16[2,256,256]{2,1,0:T(8,128)(2,1)S(1)}, bf16[2,256,256]{2,1,0:T(8,128)(2,1)S(1)}, u32[]{:S(2)}, u32[]{:S(2)}) collective-permute-start(bf16[2,256,256]{2,1,0:T(8,128)(2,1)S(1)} %collective-permute-done.17.refs_1_), channel_id=1, source_target_pairs={{0,4},{1,5},{2,6},{3,7},{4,0},{5,1},{6,2},{7,3},{8,12},{9,13},{10,... | collective-permute-start | bytes 786440 | tf_op jit(solution)/shard_map/ppermute | solution.py:366
  93.4 1.5 %collective-permute-start.20 = (bf16[2,256,256]{2,1,0:T(8,128)(2,1)S(1)}, bf16[2,256,256]{2,1,0:T(8,128)(2,1)S(1)}, u32[]{:S(2)}, u32[]{:S(2)}) collective-permute-start(bf16[2,256,256]{2,1,0:T(8,128)(2,1)S(1)} %collective-permute-done.19.refs_3_), channel_id=1, source_target_pairs={{0,2},{1,3},{2,0},{3,1},{4,6},{5,7},{6,4},{7,5},{8,10},{9,11},{10,... | collective-permute-start | bytes 786440 | tf_op jit(solution)/shard_map/ppermute | solution.py:366
  94.9 1.5 %collective-permute-start.22 = (bf16[2,256,256]{2,1,0:T(8,128)(2,1)S(1)}, bf16[2,256,256]{2,1,0:T(8,128)(2,1)S(1)}, u32[]{:S(2)}, u32[]{:S(2)}) collective-permute-start(bf16[2,256,256]{2,1,0:T(8,128)(2,1)S(1)} %collective-permute-done.21.refs_2_), channel_id=1, source_target_pairs={{0,8},{1,9},{2,10},{3,11},{4,12},{5,13},{6,14},{7,15},{8,0},{9,1},... | collective-permute-start | bytes 786440 | tf_op jit(solution)/shard_map/ppermute | solution.py:366
  96.3 1.0 copy-done.8
  97.4 1.6 %copy-done.17 = f32[2,2048,128]{2,1,0:T(8,128)S(1)} copy-done((f32[2,2048,128]{2,1,0:T(8,128)S(1)}, f32[2,2048,128]{2,1,0:T(8,128)}, u32[]{:S(2)}) %copy-start.17) | copy-done | bytes 2097176
  99.0 8.0 %prefix_keys.2.refs_4_ = f32[2,2048,128]{2,1,0:T(8,128)S(1)} custom-call(s32[2]{0:T(128)S(1)} %copy-done.5, s32[32]{0:T(128)S(1)} %copy-done.6, s32[1]{0:T(128)} %bitcast.me_ref, bf16[256,1024]{1,0:T(8,128)(2,1)S(1)} %copy-done.8, bf16[2,256,256]{2,1,0:T(8,128)(2,1)S(1)} %maximum_select_fusion.refs_0_, ...), custom_call_target="tpu_custom_call" | custom-call | flops 6442450944 | bytes 1048576 | tf_op jit(solution)/shard_map/prefix_keys/pallas_call | solution.py:507
  106.9 1.9 %collective-permute-done.18.refs_0_ = bf16[2,256,256]{2,1,0:T(8,128)(2,1)S(1)} collective-permute-done((bf16[2,256,256]{2,1,0:T(8,128)(2,1)S(1)}, bf16[2,256,256]{2,1,0:T(8,128)(2,1)S(1)}, u32[]{:S(2)}, u32[]{:S(2)}) %collective-permute-start.18) | collective-permute-done | bytes 262176 | tf_op jit(solution)/shard_map/ppermute | solution.py:366
  108.9 1.0 collective-permute-done.20.refs_1_
  109.9 5.6 %collective-permute-done.22.refs_2_ = bf16[2,256,256]{2,1,0:T(8,128)(2,1)S(1)} collective-permute-done((bf16[2,256,256]{2,1,0:T(8,128)(2,1)S(1)}, bf16[2,256,256]{2,1,0:T(8,128)(2,1)S(1)}, u32[]{:S(2)}, u32[]{:S(2)}) %collective-permute-start.22) | collective-permute-done | bytes 262176 | tf_op jit(solution)/shard_map/ppermute | solution.py:366
  116.2 1.5 %collective-permute-start.24 = (bf16[2,256,256]{2,1,0:T(8,128)(2,1)S(1)}, bf16[2,256,256]{2,1,0:T(8,128)(2,1)S(1)}, u32[]{:S(2)}, u32[]{:S(2)}) collective-permute-start(bf16[2,256,256]{2,1,0:T(8,128)(2,1)S(1)} %collective-permute-done.22.refs_2_), channel_id=1, source_target_pairs={{0,2},{1,3},{2,0},{3,1},{4,6},{5,7},{6,4},{7,5},{8,10},{9,11},{10,... | collective-permute-start | bytes 786440 | tf_op jit(solution)/shard_map/ppermute | solution.py:366
  117.9 5.0 %prefix_keys.3.refs_2_ = f32[2,2048,128]{2,1,0:T(8,128)S(1)} custom-call(s32[2]{0:T(128)S(1)} %copy-done.5, s32[32]{0:T(128)S(1)} %copy-done.6, s32[1]{0:T(128)} %bitcast.me_ref, bf16[256,1024]{1,0:T(8,128)(2,1)S(1)} %copy-done.8, bf16[2,256,256]{2,1,0:T(8,128)(2,1)S(1)} %collective-permute-done.18.refs_0_, ...), custom_call_target="tpu_custom_call" | custom-call | flops 4831838208 | bytes 786432 | tf_op jit(solution)/shard_map/prefix_keys/pallas_call | solution.py:507
  122.8 1.3 copy-done.14
  124.2 0.7 collective-permute-done.24.refs_0_
  125.5 1.3 collective-permute-done.26.refs_1_
  126.9 1.6 %copy-done.15 = f32[2,2048,128]{2,1,0:T(8,128)S(1)} copy-done((f32[2,2048,128]{2,1,0:T(8,128)S(1)}, f32[2,2048,128]{2,1,0:T(8,128)}, u32[]{:S(2)}) %copy-start.15) | copy-done | bytes 2097176
  128.5 9.7 %last_keys.1 = bf16[256,1024]{1,0:T(8,128)(2,1)} custom-call(s32[2]{0:T(128)S(1)} %copy-done.5, s32[32]{0:T(128)S(1)} %copy-done.6, s32[1]{0:T(128)} %bitcast.me_ref, bf16[256,1024]{1,0:T(8,128)(2,1)S(1)} %copy-done.9, bf16[32,64,256]{2,1,0:T(8,128)(2,1)S(1)} %all-to-all-done.kv_ref, bf16[2,256,256]{2,1,0:T(8,128)(2,1)S(1)} %collective-permute-done.24.refs_0_, ...), custom_call_target="tpu_custom_call" | custom-call | flops 8053063680 | bytes 1310720 | tf_op jit(solution)/shard_map/last_keys/pallas_call | solution.py:533
  (71 shorter events, 7.4 us)
Async XLA Ops:
  0.0 4.6 %collective-permute-start = (bf16[4096,256]{1,0:T(8,128)(2,1)}, bf16[4096,256]{1,0:T(8,128)(2,1)}, u32[]{:S(2)}, u32[]{:S(2)}) collective-permute-start(bf16[4096,256]{1,0:T(8,128)(2,1)} %param.15), channel_id=1, source_target_pairs={{0,1},{1,0},{2,3},{3,2},{4,5},{5,4},{6,7},{7,6},{8,9},{9,8},{10,11... | collective-permute-start | bytes 6291464 | tf_op jit(solution)/shard_map/ppermute | solution.py:356
  1.1 11.4 %copy-start.4 = (s32[2]{0:T(128)S(1)}, s32[2]{0:T(128)}, u32[]{:S(2)}) copy-start(s32[2]{0:T(128)} %owner_ref.13) | copy-start | bytes 28
  4.6 50.5 %all-to-all-start.1 = ((bf16[32,64,256]{2,1,0:T(8,128)(2,1)}), bf16[32,64,256]{2,1,0:T(8,128)(2,1)S(1)}, u32[]{:S(2)}, u32[]{:S(2)}) async-start(bf16[32,64,256]{2,1,0:T(8,128)(2,1)} %pack_moved.2), calls=%async_computation.1 | async-start | bytes 2097152 | tf_op jit(solution)/shard_map/all_to_all | solution.py:352
  13.1 10.7 %copy-start.7 = (bf16[256,1024]{1,0:T(8,128)(2,1)S(1)}, bf16[256,1024]{1,0:T(8,128)(2,1)}, u32[]{:S(2)}) copy-start(bf16[256,1024]{1,0:T(8,128)(2,1)} %q_ref.9) | copy-start | bytes 1572868
  13.1 10.7 %copy-start.11 = (bf16[256,256]{1,0:T(8,128)(2,1)S(1)}, bf16[256,256]{1,0:T(8,128)(2,1)}, u32[]{:S(2)}) copy-start(bf16[256,256]{1,0:T(8,128)(2,1)} %suffix_ref.1) | copy-start | bytes 393220
  16.1 13.6 %collective-permute-start.7 = (bf16[1,256,256]{2,1,0:T(8,128)(2,1)}, bf16[1,256,256]{2,1,0:T(8,128)(2,1)S(1)}, u32[]{:S(2)}, u32[]{:S(2)}) collective-permute-start(bf16[1,256,256]{2,1,0:T(8,128)(2,1)} %get-tuple-element.50), channel_id=1, source_target_pairs={{0,2},{1,3},{2,0},{3,1},{4,6},{5,7},{6,4},{7,5},{8,10},{9,11},{10,... | collective-permute-start | bytes 393224 | tf_op jit(solution)/shard_map/ppermute | solution.py:320
  17.9 15.4 %collective-permute-start.1 = (bf16[1,256,256]{2,1,0:T(8,128)(2,1)}, bf16[1,256,256]{2,1,0:T(8,128)(2,1)S(1)}, u32[]{:S(2)}, u32[]{:S(2)}) collective-permute-start(bf16[1,256,256]{2,1,0:T(8,128)(2,1)} %get-tuple-element.44), channel_id=1, source_target_pairs={{0,14},{1,15},{2,12},{3,13},{4,10},{5,11},{6,8},{7,9},{8,6},{9,7},... | collective-permute-start | bytes 393224 | tf_op jit(solution)/shard_map/ppermute | solution.py:320
  20.3 18.7 %collective-permute-start.2 = (bf16[1,256,256]{2,1,0:T(8,128)(2,1)}, bf16[1,256,256]{2,1,0:T(8,128)(2,1)S(1)}, u32[]{:S(2)}, u32[]{:S(2)}) collective-permute-start(bf16[1,256,256]{2,1,0:T(8,128)(2,1)} %get-tuple-element.45), channel_id=1, source_target_pairs={{0,12},{1,13},{2,14},{3,15},{4,8},{5,9},{6,10},{7,11},{8,4},{9,5},... | collective-permute-start | bytes 393224 | tf_op jit(solution)/shard_map/ppermute | solution.py:320
  20.6 21.1 %collective-permute-start.3 = (bf16[1,256,256]{2,1,0:T(8,128)(2,1)}, bf16[1,256,256]{2,1,0:T(8,128)(2,1)S(1)}, u32[]{:S(2)}, u32[]{:S(2)}) collective-permute-start(bf16[1,256,256]{2,1,0:T(8,128)(2,1)} %get-tuple-element.46), channel_id=1, source_target_pairs={{0,10},{1,11},{2,8},{3,9},{4,14},{5,15},{6,12},{7,13},{8,2},{9,3},... | collective-permute-start | bytes 393224 | tf_op jit(solution)/shard_map/ppermute | solution.py:320
  23.2 21.8 %collective-permute-start.4 = (bf16[1,256,256]{2,1,0:T(8,128)(2,1)}, bf16[1,256,256]{2,1,0:T(8,128)(2,1)S(1)}, u32[]{:S(2)}, u32[]{:S(2)}) collective-permute-start(bf16[1,256,256]{2,1,0:T(8,128)(2,1)} %get-tuple-element.47), channel_id=1, source_target_pairs={{0,8},{1,9},{2,10},{3,11},{4,12},{5,13},{6,14},{7,15},{8,0},{9,1},... | collective-permute-start | bytes 393224 | tf_op jit(solution)/shard_map/ppermute | solution.py:320
  25.7 16.1 %copy-start.20 = (bf16[1,256,256]{2,1,0:T(8,128)(2,1)S(1)}, bf16[1,256,256]{2,1,0:T(8,128)(2,1)}, u32[]{:S(2)}) copy-start(bf16[1,256,256]{2,1,0:T(8,128)(2,1)} %get-tuple-element.62) | copy-start | bytes 393220
  25.7 16.7 %copy-start.5 = (s32[2]{0:T(128)S(1)}, s32[2]{0:T(128)}, u32[]{:S(2)}) copy-start(s32[2]{0:T(128)} %owner_ref.13) | copy-start | bytes 28
  25.7 22.2 %copy-start.19 = (bf16[1,256,256]{2,1,0:T(8,128)(2,1)S(1)}, bf16[1,256,256]{2,1,0:T(8,128)(2,1)}, u32[]{:S(2)}) copy-start(bf16[1,256,256]{2,1,0:T(8,128)(2,1)} %get-tuple-element.60) | copy-start | bytes 393220
  25.7 22.9 %copy-start.3 = (bf16[1,256,256]{2,1,0:T(8,128)(2,1)S(1)}, bf16[1,256,256]{2,1,0:T(8,128)(2,1)}, u32[]{:S(2)}) copy-start(bf16[1,256,256]{2,1,0:T(8,128)(2,1)} %get-tuple-element.43.refs_0_.after_ref) | copy-start | bytes 393220
  25.7 28.0 %copy-start.18 = (bf16[1,256,256]{2,1,0:T(8,128)(2,1)S(1)}, bf16[1,256,256]{2,1,0:T(8,128)(2,1)}, u32[]{:S(2)}) copy-start(bf16[1,256,256]{2,1,0:T(8,128)(2,1)} %get-tuple-element.67) | copy-start | bytes 393220
  28.4 1.3 copy-start.12
  29.7 16.1 %collective-permute-start.5 = (bf16[1,256,256]{2,1,0:T(8,128)(2,1)}, bf16[1,256,256]{2,1,0:T(8,128)(2,1)S(1)}, u32[]{:S(2)}, u32[]{:S(2)}) collective-permute-start(bf16[1,256,256]{2,1,0:T(8,128)(2,1)} %get-tuple-element.48), channel_id=1, source_target_pairs={{0,6},{1,7},{2,4},{3,5},{4,2},{5,3},{6,0},{7,1},{8,14},{9,15},{10,... | collective-permute-start | bytes 393224 | tf_op jit(solution)/shard_map/ppermute | solution.py:320
  33.3 13.1 %collective-permute-start.6 = (bf16[1,256,256]{2,1,0:T(8,128)(2,1)}, bf16[1,256,256]{2,1,0:T(8,128)(2,1)S(1)}, u32[]{:S(2)}, u32[]{:S(2)}) collective-permute-start(bf16[1,256,256]{2,1,0:T(8,128)(2,1)} %get-tuple-element.49), channel_id=1, source_target_pairs={{0,4},{1,5},{2,6},{3,7},{4,0},{5,1},{6,2},{7,3},{8,12},{9,13},{10,... | collective-permute-start | bytes 393224 | tf_op jit(solution)/shard_map/ppermute | solution.py:320
  39.0 8.1 %collective-permute-start.10 = (bf16[1,256,256]{2,1,0:T(8,128)(2,1)}, bf16[1,256,256]{2,1,0:T(8,128)(2,1)S(1)}, u32[]{:S(2)}, u32[]{:S(2)}) collective-permute-start(bf16[1,256,256]{2,1,0:T(8,128)(2,1)} %get-tuple-element.61), channel_id=1, source_target_pairs={{30,18},{31,19}} | collective-permute-start | bytes 393224 | tf_op jit(solution)/shard_map/ppermute | solution.py:320
  41.7 6.1 %collective-permute-start.11 = (bf16[1,256,256]{2,1,0:T(8,128)(2,1)S(1)}, bf16[1,256,256]{2,1,0:T(8,128)(2,1)S(1)}, u32[]{:S(2)}, u32[]{:S(2)}) collective-permute-start(bf16[1,256,256]{2,1,0:T(8,128)(2,1)S(1)} %copy-done.20), channel_id=1, source_target_pairs={{30,20},{31,21}} | collective-permute-start | bytes 393224 | tf_op jit(solution)/shard_map/ppermute | solution.py:320
  45.1 3.5 %collective-permute-start.12 = (bf16[1,256,256]{2,1,0:T(8,128)(2,1)}, bf16[1,256,256]{2,1,0:T(8,128)(2,1)S(1)}, u32[]{:S(2)}, u32[]{:S(2)}) collective-permute-start(bf16[1,256,256]{2,1,0:T(8,128)(2,1)} %get-tuple-element.63), channel_id=1, source_target_pairs={{30,22},{31,23}} | collective-permute-start | bytes 393224 | tf_op jit(solution)/shard_map/ppermute | solution.py:320
  45.8 7.9 %collective-permute-start.13 = (bf16[1,256,256]{2,1,0:T(8,128)(2,1)}, bf16[1,256,256]{2,1,0:T(8,128)(2,1)S(1)}, u32[]{:S(2)}, u32[]{:S(2)}) collective-permute-start(bf16[1,256,256]{2,1,0:T(8,128)(2,1)} %get-tuple-element.64), channel_id=1, source_target_pairs={{30,24},{31,25}} | collective-permute-start | bytes 393224 | tf_op jit(solution)/shard_map/ppermute | solution.py:320
  46.5 7.2 %collective-permute-start.14 = (bf16[1,256,256]{2,1,0:T(8,128)(2,1)}, bf16[1,256,256]{2,1,0:T(8,128)(2,1)S(1)}, u32[]{:S(2)}, u32[]{:S(2)}) collective-permute-start(bf16[1,256,256]{2,1,0:T(8,128)(2,1)} %get-tuple-element.65), channel_id=1, source_target_pairs={{30,26},{31,27}} | collective-permute-start | bytes 393224 | tf_op jit(solution)/shard_map/ppermute | solution.py:320
  47.1 6.6 %collective-permute-start.15 = (bf16[1,256,256]{2,1,0:T(8,128)(2,1)}, bf16[1,256,256]{2,1,0:T(8,128)(2,1)S(1)}, u32[]{:S(2)}, u32[]{:S(2)}) collective-permute-start(bf16[1,256,256]{2,1,0:T(8,128)(2,1)} %get-tuple-element.66), channel_id=1, source_target_pairs={{30,28},{31,29}} | collective-permute-start | bytes 393224 | tf_op jit(solution)/shard_map/ppermute | solution.py:320
  47.8 5.9 %collective-permute-start.9 = (bf16[1,256,256]{2,1,0:T(8,128)(2,1)S(1)}, bf16[1,256,256]{2,1,0:T(8,128)(2,1)S(1)}, u32[]{:S(2)}, u32[]{:S(2)}) collective-permute-start(bf16[1,256,256]{2,1,0:T(8,128)(2,1)S(1)} %copy-done.19), channel_id=1, source_target_pairs={{30,16},{31,17}} | collective-permute-start | bytes 393224 | tf_op jit(solution)/shard_map/ppermute | solution.py:320
  48.6 16.1 %collective-permute-start.8 = (bf16[1,256,256]{2,1,0:T(8,128)(2,1)S(1)}, bf16[1,256,256]{2,1,0:T(8,128)(2,1)S(1)}, u32[]{:S(2)}, u32[]{:S(2)}) collective-permute-start(bf16[1,256,256]{2,1,0:T(8,128)(2,1)S(1)} %select_select_fusion.1), channel_id=1, source_target_pairs={{0,16},{1,17},{2,18},{3,19},{4,20},{5,21},{6,22},{7,23},{8,24},{9,... | collective-permute-start | bytes 393224 | tf_op jit(solution)/shard_map/ppermute | solution.py:336
  53.8 23.8 %copy-start.6 = (s32[32]{0:T(128)S(1)}, s32[32]{0:T(128)}, u32[]{:S(2)}) copy-start(s32[32]{0:T(128)} %reader_ref.11) | copy-start | bytes 388
  53.8 15.1 %collective-permute-start.16 = (bf16[1,256,256]{2,1,0:T(8,128)(2,1)S(1)}, bf16[1,256,256]{2,1,0:T(8,128)(2,1)S(1)}, u32[]{:S(2)}, u32[]{:S(2)}) collective-permute-start(bf16[1,256,256]{2,1,0:T(8,128)(2,1)S(1)} %select_select_fusion), channel_id=1, source_target_pairs={{16,0},{17,1},{18,2},{19,3},{20,4},{21,5},{22,6},{23,7},{24,8},{25... | collective-permute-start | bytes 393224 | tf_op jit(solution)/shard_map/ppermute | solution.py:338
  55.1 1.6 %copy-start.13 = (f32[2,2048,128]{2,1,0:T(8,128)S(1)}, f32[2,2048,128]{2,1,0:T(8,128)}, u32[]{:S(2)}) copy-start(f32[2,2048,128]{2,1,0:T(8,128)} %copy-done.12) | copy-start | bytes 6291460
  63.4 1.3 copy-start.16
  69.0 6.4 %collective-permute-start.17 = (bf16[2,256,256]{2,1,0:T(8,128)(2,1)S(1)}, bf16[2,256,256]{2,1,0:T(8,128)(2,1)S(1)}, u32[]{:S(2)}, u32[]{:S(2)}) collective-permute-start(bf16[2,256,256]{2,1,0:T(8,128)(2,1)S(1)} %maximum_select_fusion.refs_0_), channel_id=1, source_target_pairs={{0,2},{1,3},{2,0},{3,1},{4,6},{5,7},{6,4},{7,5},{8,10},{9,11},{10,... | collective-permute-start | bytes 786440 | tf_op jit(solution)/shard_map/ppermute | solution.py:366
  69.1 6.4 %collective-permute-start.19 = (bf16[2,256,256]{2,1,0:T(8,128)(2,1)S(1)}, bf16[2,256,256]{2,1,0:T(8,128)(2,1)S(1)}, u32[]{:S(2)}, u32[]{:S(2)}) collective-permute-start(bf16[2,256,256]{2,1,0:T(8,128)(2,1)S(1)} %maximum_select_fusion.refs_0_), channel_id=1, source_target_pairs={{0,8},{1,9},{2,10},{3,11},{4,12},{5,13},{6,14},{7,15},{8,0},{9,1},... | collective-permute-start | bytes 786440 | tf_op jit(solution)/shard_map/ppermute | solution.py:366
  69.2 8.5 %collective-permute-start.21 = (bf16[2,256,256]{2,1,0:T(8,128)(2,1)S(1)}, bf16[2,256,256]{2,1,0:T(8,128)(2,1)S(1)}, u32[]{:S(2)}, u32[]{:S(2)}) collective-permute-start(bf16[2,256,256]{2,1,0:T(8,128)(2,1)S(1)} %maximum_select_fusion.refs_0_), channel_id=1, source_target_pairs={{0,4},{1,5},{2,6},{3,7},{4,0},{5,1},{6,2},{7,3},{8,12},{9,13},{10,... | collective-permute-start | bytes 786440 | tf_op jit(solution)/shard_map/ppermute | solution.py:366
  78.2 18.1 %collective-permute-start.23 = (bf16[1024,256]{1,0:T(8,128)(2,1)S(1)}, bf16[1024,256]{1,0:T(8,128)(2,1)}, u32[]{:S(2)}, u32[]{:S(2)}) collective-permute-start(bf16[1024,256]{1,0:T(8,128)(2,1)S(1)} %pick_other.3), channel_id=1, source_target_pairs={{0,1},{1,0},{2,3},{3,2},{4,5},{5,4},{6,7},{7,6},{8,9},{9,8},{10,11... | collective-permute-start | bytes 1572872 | tf_op jit(solution)/shard_map/ppermute | solution.py:356
  81.5 1.2 copy-start
  82.7 1.0 copy-start.1
  83.7 41.9 %all-to-all-start = ((bf16[32,64,256]{2,1,0:T(8,128)(2,1)}), bf16[32,64,256]{2,1,0:T(8,128)(2,1)S(1)}, u32[]{:S(2)}, u32[]{:S(2)}) async-start(bf16[32,64,256]{2,1,0:T(8,128)(2,1)} %copy-done.1), calls=%async_computation | async-start | bytes 2097152 | tf_op jit(solution)/shard_map/all_to_all | solution.py:352
  91.7 17.2 %collective-permute-start.18 = (bf16[2,256,256]{2,1,0:T(8,128)(2,1)S(1)}, bf16[2,256,256]{2,1,0:T(8,128)(2,1)S(1)}, u32[]{:S(2)}, u32[]{:S(2)}) collective-permute-start(bf16[2,256,256]{2,1,0:T(8,128)(2,1)S(1)} %collective-permute-done.17.refs_1_), channel_id=1, source_target_pairs={{0,4},{1,5},{2,6},{3,7},{4,0},{5,1},{6,2},{7,3},{8,12},{9,13},{10,... | collective-permute-start | bytes 786440 | tf_op jit(solution)/shard_map/ppermute | solution.py:366
  93.4 16.5 %collective-permute-start.20 = (bf16[2,256,256]{2,1,0:T(8,128)(2,1)S(1)}, bf16[2,256,256]{2,1,0:T(8,128)(2,1)S(1)}, u32[]{:S(2)}, u32[]{:S(2)}) collective-permute-start(bf16[2,256,256]{2,1,0:T(8,128)(2,1)S(1)} %collective-permute-done.19.refs_3_), channel_id=1, source_target_pairs={{0,2},{1,3},{2,0},{3,1},{4,6},{5,7},{6,4},{7,5},{8,10},{9,11},{10,... | collective-permute-start | bytes 786440 | tf_op jit(solution)/shard_map/ppermute | solution.py:366
  94.9 20.6 %collective-permute-start.22 = (bf16[2,256,256]{2,1,0:T(8,128)(2,1)S(1)}, bf16[2,256,256]{2,1,0:T(8,128)(2,1)S(1)}, u32[]{:S(2)}, u32[]{:S(2)}) collective-permute-start(bf16[2,256,256]{2,1,0:T(8,128)(2,1)S(1)} %collective-permute-done.21.refs_2_), channel_id=1, source_target_pairs={{0,8},{1,9},{2,10},{3,11},{4,12},{5,13},{6,14},{7,15},{8,0},{9,1},... | collective-permute-start | bytes 786440 | tf_op jit(solution)/shard_map/ppermute | solution.py:366
  96.3 1.0 copy-start.8
  97.4 1.6 %copy-start.17 = (f32[2,2048,128]{2,1,0:T(8,128)S(1)}, f32[2,2048,128]{2,1,0:T(8,128)}, u32[]{:S(2)}) copy-start(f32[2,2048,128]{2,1,0:T(8,128)} %copy-done.16) | copy-start | bytes 6291460
  116.1 10.8 %copy-start.9 = (bf16[256,1024]{1,0:T(8,128)(2,1)S(1)}, bf16[256,1024]{1,0:T(8,128)(2,1)}, u32[]{:S(2)}) copy-start(bf16[256,1024]{1,0:T(8,128)(2,1)} %q_ref.9) | copy-start | bytes 1572868
  116.1 1.8 %collective-permute-start.25 = (bf16[768,256]{1,0:T(8,128)(2,1)S(1)}, bf16[768,256]{1,0:T(8,128)(2,1)S(1)}, u32[]{:S(2)}, u32[]{:S(2)}) collective-permute-start(bf16[768,256]{1,0:T(8,128)(2,1)S(1)} %pick_other.4), channel_id=1, source_target_pairs={{0,1},{1,0},{2,3},{3,2},{4,5},{5,4},{6,7},{7,6},{8,9},{9,8},{10,11... | collective-permute-start | bytes 1179656 | tf_op jit(solution)/shard_map/ppermute | solution.py:356
  116.2 8.7 %collective-permute-start.24 = (bf16[2,256,256]{2,1,0:T(8,128)(2,1)S(1)}, bf16[2,256,256]{2,1,0:T(8,128)(2,1)S(1)}, u32[]{:S(2)}, u32[]{:S(2)}) collective-permute-start(bf16[2,256,256]{2,1,0:T(8,128)(2,1)S(1)} %collective-permute-done.22.refs_2_), channel_id=1, source_target_pairs={{0,2},{1,3},{2,0},{3,1},{4,6},{5,7},{6,4},{7,5},{8,10},{9,11},{10,... | collective-permute-start | bytes 786440 | tf_op jit(solution)/shard_map/ppermute | solution.py:366
  122.8 1.3 copy-start.14
  125.5 1.4 %collective-permute-start.26 = (bf16[256,256]{1,0:T(8,128)(2,1)S(1)}, bf16[256,256]{1,0:T(8,128)(2,1)S(1)}, u32[]{:S(2)}, u32[]{:S(2)}) collective-permute-start(bf16[256,256]{1,0:T(8,128)(2,1)S(1)} %pick_other.5), channel_id=1, source_target_pairs={{0,1},{1,0},{2,3},{3,2},{4,5},{5,4},{6,7},{7,6},{8,9},{9,8},{10,11... | collective-permute-start | bytes 393224 | tf_op jit(solution)/shard_map/ppermute | solution.py:356
  126.9 1.6 %copy-start.15 = (f32[2,2048,128]{2,1,0:T(8,128)S(1)}, f32[2,2048,128]{2,1,0:T(8,128)}, u32[]{:S(2)}) copy-start(f32[2,2048,128]{2,1,0:T(8,128)} %copy-done.14) | copy-start | bytes 6291460
  (2 other events, 1.9 us)

commit v21 on v20

--- a/solution.py
+++ b/solution.py
@@ -145,6 +145,11 @@
         save_state(*work[1:], out_ref)
 
 
+def start_all(copies):
+    for copy in copies:
+        copy.start()
+
+
 def wait_all(copies):
     for copy in copies:
         copy.wait()
@@ -181,34 +186,43 @@
         out_ref[pl.ds(place * piece.shape[0], piece.shape[0]), :] = piece[...]
 
 
-def pack_kernel(first, target_ref, block_ref, count_ref, pool_ref, *refs):
-    out_ref, held_ref, mark_ref, in_sems, out_sems = refs[-5:]
-    entries, rows = held_ref.shape[:2]
+def pack_kernel(target_ref, block_ref, count_ref, pool_ref, *refs):
+    parts, (held_ref, mark_ref, in_sems, out_sems) = refs[:-4], refs[-4:]
+    entries = target_ref.shape[1]
     mark_ref[...] = jnp.full(mark_ref.shape, DEAD_MARK, mark_ref.dtype)
 
     def load(entry):
-        source = pool_ref.at[block_ref[0, entry], pl.ds(first, rows)]
-        return pltpu.make_async_copy(source, held_ref.at[entry], in_sems.at[entry])
-
-    def store(entry, source):
-        return pltpu.make_async_copy(source, out_ref.at[target_ref[0, entry]], out_sems.at[entry])
+        return pltpu.make_async_copy(
+            pool_ref.at[block_ref[0, entry]], held_ref.at[entry], in_sems.at[entry]
+        )
+
+    def stores(entry, source):
+        rows = parts[0].shape[1]
+        return [
+            pltpu.make_async_copy(
+                source.at[pl.ds(place * rows, rows)],
+                part.at[target_ref[0, entry]],
+                out_sems.at[place, entry],
+            )
+            for place, part in enumerate(parts)
+        ]
 
     @pl.loop(0, entries)
     def _(entry):
         live = entry < count_ref[0]
         pl.when(live)(lambda: load(entry).start())
-        pl.when(jnp.logical_not(live))(lambda: store(entry, mark_ref).start())
+        pl.when(jnp.logical_not(live))(lambda: start_all(stores(entry, mark_ref)))
 
     @pl.loop(0, entries)
     def _(entry):
         @pl.when(entry < count_ref[0])
         def _():
             load(entry).wait()
-            store(entry, held_ref.at[entry]).start()
+            start_all(stores(entry, held_ref.at[entry]))
 
     @pl.loop(0, entries)
     def _(entry):
-        store(entry, mark_ref).wait()
+        wait_all(stores(entry, mark_ref))
 
 
 def gate_kernel(*refs):
@@ -277,7 +291,7 @@
     wait_all([store(step) for step in range(chips)])
 
 
-def multicast(prefix_cache, owners, pack, fold_local, fold_moved):
+def multicast(prefix_cache, owners, outgoing, fold_local, fold_moved):
     replicas = lax.axis_size("replica")
     half = replicas // 2
     chips = half // 2
@@ -285,8 +299,8 @@
     prefixes = owners.shape[0]
 
     split = prefix_cache.reshape(2, chips, -1, width)
-    swapped, outgoing = lax.optimization_barrier((swap_cores(prefix_cache), pack(0)))
-    arrived = send_blocks(outgoing)
+    swapped, *outgoing = lax.optimization_barrier((swap_cores(prefix_cache), *outgoing))
+    arrived = send_blocks(outgoing[0])
     swapped = swapped.reshape(split.shape)
     pieces = jax.ShapeDtypeStruct((owners.shape[0] - 1, *split.shape[2:]), split.dtype)
     piece = jax.ShapeDtypeStruct((1, *split.shape[2:]), split.dtype)
@@ -336,7 +350,7 @@
     passed = lax.ppermute(found, "replica", [(i, (i + half) % replicas) for i in range(replicas)])
     found_known = choose(known_staged[0], passed_known, known_away)
     passed_known = lax.ppermute(found_known, "replica", [(i + half, i) for i in range(half)])
-    later = send_blocks(gate(pack(1, staged[0]), passed, passed_known))
+    later = send_blocks(gate(outgoing[1], passed, passed_known))
     passed, passed_known, state_now = lax.optimization_barrier(
         (passed, passed_known, fold_moved(arrived, local))
     )
@@ -434,24 +448,22 @@
     ]
 
     entries = mig_target.shape[1]
-    half_block = (kv_pool.shape[1] // 2, kv_pool.shape[2])
-
-    def pack(part, *after):
-        return pl.pallas_call(
-            functools.partial(pack_kernel, part * half_block[0]),
-            out_shape=jax.ShapeDtypeStruct((replicas, *half_block), kv_pool.dtype),
-            in_specs=[IN_SMEM] * 3 + [IN_HBM] * (1 + len(after)),
-            out_specs=IN_HBM,
-            scratch_shapes=[
-                pltpu.VMEM((entries, *half_block), kv_pool.dtype),
-                pltpu.VMEM(half_block, kv_pool.dtype),
-                pltpu.SemaphoreType.DMA((entries,)),
-                pltpu.SemaphoreType.DMA((entries,)),
-            ],
-            compiler_params=COPY_PARAMS,
-            name="pack_moved",
-        )(mig_target, mig_block, mig_count, kv_pool, *after)
-
+    half_block = (replicas, kv_pool.shape[1] // 2, kv_pool.shape[2])
+    slots = (jax.ShapeDtypeStruct(half_block, kv_pool.dtype),) * 2
+    outgoing = pl.pallas_call(
+        pack_kernel,
+        out_shape=slots,
+        in_specs=[IN_SMEM] * 3 + [IN_HBM],
+        out_specs=(IN_HBM,) * 2,
+        scratch_shapes=[
+            pltpu.VMEM((entries, *kv_pool.shape[1:]), kv_pool.dtype),
+            pltpu.VMEM(kv_pool.shape[1:], kv_pool.dtype),
+            pltpu.SemaphoreType.DMA((entries,)),
+            pltpu.SemaphoreType.DMA((2, entries)),
+        ],
+        compiler_params=COPY_PARAMS,
+        name="pack_moved",
+    )(mig_target, mig_block, mig_count, kv_pool)
     def fold_local(after):
         return pl.pallas_call(
             functools.partial(local_kernel, factor),
@@ -551,7 +563,7 @@
             name="last_keys",
         )(*scalars, queries, arrived, *pieces, others, state_now)
 
-    held, state_now, later = multicast(prefix_cache, owners, pack, fold_local, fold_moved)
+    held, state_now, later = multicast(prefix_cache, owners, outgoing, fold_local, fold_moved)
     scalars = (owners, readers, lax.axis_index("replica")[None])
     gathered = {0: held}
     ready = [held]

time: 139 us -> 133 us (0.957)
  local copies, waits for them, and re-layouts: 14.5 us -> 9 us
  waiting for transfers between devices: 28.2 us -> 31.4 us
  Pallas kernels: 43.1 us -> 40.9 us
  starting transfers between devices: 47.7 us -> 46 us
    unnamed x42 -> x32, local copies, waits for them, and re-layouts: 13.9 us -> 8.38 us
    pallas_call x2 -> x1, Pallas kernels: 6.45 us -> 4.02 us  [on_device(): pl.pallas_call(pack_kernel, out_shape=slots, in_specs=[IN_SMEM] * 3 + [IN...]
    ppermute x7, starting transfers between devices: 10.3 us -> 8.7 us  [gather_step(): return lax.ppermute(gathered[step ^ 1 << last], 'replica', pairs)]
    ppermute x1, waiting for transfers between devices: 4.18 us -> 5.7 us  [multicast(): lax.ppermute(found_known, 'replica', [(i + half, i) for i in range(half)])]
  transfers between devices with their start and end apart: 29 -> 29, of which waited for: 14 -> 13; matrix products, arithmetic and copies ran while one was open for 1% -> 1% of each run, Pallas kernels for 24% -> 23%
where the time goes in v21:
time: 133 us; the launch traced here: 132 us
  starting transfers between devices  46 us (35%)
  Pallas kernels  40.9 us (31%)
  waiting for transfers between devices  31.4 us (24%)
  local copies, waits for them, and re-layouts  9 us (7%)
  between operations  3.69 us (3%)
    all_to_all x2, starting transfers between devices, send_blocks(): lax.all_to_all(rows, 'replica', split_axis=0, concat_axis=0, tiled=True)  15.2 us
    ppermute x14, starting transfers between devices, to_peers(): lax.ppermute(rows, 'replica', [(i, i ^ 2 * step) for i in senders])  15.1 us
    ppermute x7, waiting for transfers between devices, gather_step(): return lax.ppermute(gathered[step ^ 1 << last], 'replica', pairs)  14.8 us
    pallas_call x2, Pallas kernels, fold_prefix(): pl.pallas_call(functools.partial(prefix_kernel, factor, len(pieces) + 1,...  13 us
    pallas_call x1, Pallas kernels, fold_last(): pl.pallas_call(functools.partial(last_kernel, factor, steps), out_shape=r...  9.67 us
    ppermute x14, waiting for transfers between devices, to_peers(): lax.ppermute(rows, 'replica', [(i, i ^ 2 * step) for i in senders])  9.42 us
    ppermute x7, starting transfers between devices, gather_step(): return lax.ppermute(gathered[step ^ 1 << last], 'replica', pairs)  8.7 us
    unnamed x32, local copies, waits for them, and re-layouts  8.38 us
  transfers between devices with their start and end apart: 29, of which 13 were waited for; matrix products, arithmetic and copies ran while one was open for 1% of the time, Pallas kernels for 23%

profile of v21, /device:TPU:0, one launch (start us, length us, event | category | flops | bytes accessed | tf_op | source)
XLA Modules:
  0.0 132.1 jit_solution(16730502699456872018)
XLA Ops:
  1.1 4.0 %pack_moved.1 = (bf16[32,64,256]{2,1,0:T(8,128)(2,1)}, bf16[32,64,256]{2,1,0:T(8,128)(2,1)}) custom-call(s32[1,32]{1,0:T(1,128)} %target_ref.1, s32[1,32]{1,0:T(1,128)} %block_ref.1, s32[1]{0:T(128)S(6)} %copy.15.count_ref, bf16[32,128,256]{2,1,0:T(8,128)(2,1)} %pool_ref.1), custom_call_target="tpu_custom_call" | custom-call | tf_op jit(solution)/shard_map/pack_moved/pallas_call | solution.py:453
  5.2 7.0 %all-to-all-start.1 = ((bf16[32,64,256]{2,1,0:T(8,128)(2,1)}), bf16[32,64,256]{2,1,0:T(8,128)(2,1)S(1)}, u32[]{:S(2)}, u32[]{:S(2)}) async-start(bf16[32,64,256]{2,1,0:T(8,128)(2,1)} %get-tuple-element.74), calls=%async_computation.1 | async-start | bytes 2097152 | tf_op jit(solution)/shard_map/all_to_all | solution.py:366
  12.8 0.6 fusion.2
  13.4 3.0 %stage_prefix.1 = (bf16[1,256,256]{2,1,0:T(8,128)(2,1)}, bf16[1,256,256]{2,1,0:T(8,128)(2,1)}, bf16[1,256,256]{2,1,0:T(8,128)(2,1)}, bf16[1,256,256]{2,1,0:T(8,1...) custom-call(s32[2]{0:T(128)} %owner_ref.13, ...), custom_call_target="tpu_custom_call" | custom-call | tf_op jit(solution)/shard_map/stage_prefix/pallas_call | solution.py:307
  16.5 1.8 %collective-permute-start.7 = (bf16[1,256,256]{2,1,0:T(8,128)(2,1)}, bf16[1,256,256]{2,1,0:T(8,128)(2,1)S(1)}, u32[]{:S(2)}, u32[]{:S(2)}) collective-permute-start(bf16[1,256,256]{2,1,0:T(8,128)(2,1)} %get-tuple-element.55), channel_id=1, source_target_pairs={{0,2},{1,3},{2,0},{3,1},{4,6},{5,7},{6,4},{7,5},{8,10},{9,11},{10,... | collective-permute-start | bytes 393224 | tf_op jit(solution)/shard_map/ppermute | solution.py:334
  18.3 2.4 %collective-permute-start.1 = (bf16[1,256,256]{2,1,0:T(8,128)(2,1)}, bf16[1,256,256]{2,1,0:T(8,128)(2,1)S(1)}, u32[]{:S(2)}, u32[]{:S(2)}) collective-permute-start(bf16[1,256,256]{2,1,0:T(8,128)(2,1)} %get-tuple-element.49), channel_id=1, source_target_pairs={{0,14},{1,15},{2,12},{3,13},{4,10},{5,11},{6,8},{7,9},{8,6},{9,7},... | collective-permute-start | bytes 393224 | tf_op jit(solution)/shard_map/ppermute | solution.py:334
  20.9 2.7 %collective-permute-start.3 = (bf16[1,256,256]{2,1,0:T(8,128)(2,1)}, bf16[1,256,256]{2,1,0:T(8,128)(2,1)S(1)}, u32[]{:S(2)}, u32[]{:S(2)}) collective-permute-start(bf16[1,256,256]{2,1,0:T(8,128)(2,1)} %get-tuple-element.51), channel_id=1, source_target_pairs={{0,10},{1,11},{2,8},{3,9},{4,14},{5,15},{6,12},{7,13},{8,2},{9,3},... | collective-permute-start | bytes 393224 | tf_op jit(solution)/shard_map/ppermute | solution.py:334
  24.2 0.9 copy-done
  25.1 2.8 %local_keys.1.loaded_ref = f32[2,2048,128]{2,1,0:T(8,128)S(1)} custom-call(s32[1]{0:T(128)S(6)} %copy.14.len_ref, bf16[256,1024]{1,0:T(8,128)(2,1)S(1)} %copy-done.5, bf16[256,256]{1,0:T(8,128)(2,1)S(1)} %copy-done.7, bf16[512,256]{1,0:T(8,128)(2,1)S(1)} %copy-done.6, bf16[1,256,256]{2,1,0:T(8,128)(2,1)S(1)} %copy-done), custom_call_target="tpu_custom_call" | custom-call | flops 2415919104 | bytes 393216 | tf_op jit(solution)/shard_map/local_keys/pallas_call | solution.py:468
  27.9 1.3 %copy-done.8 = f32[2,2048,128]{2,1,0:T(8,128)} copy-done((f32[2,2048,128]{2,1,0:T(8,128)}, f32[2,2048,128]{2,1,0:T(8,128)S(1)}, u32[]{:S(2)}) %copy-start.8) | copy-done | bytes 2097176
  29.3 1.5 %collective-permute-start.5 = (bf16[1,256,256]{2,1,0:T(8,128)(2,1)}, bf16[1,256,256]{2,1,0:T(8,128)(2,1)S(1)}, u32[]{:S(2)}, u32[]{:S(2)}) collective-permute-start(bf16[1,256,256]{2,1,0:T(8,128)(2,1)} %get-tuple-element.53), channel_id=1, source_target_pairs={{0,6},{1,7},{2,4},{3,5},{4,2},{5,3},{6,0},{7,1},{8,14},{9,15},{10,... | collective-permute-start | bytes 393224 | tf_op jit(solution)/shard_map/ppermute | solution.py:334
  30.7 3.1 %collective-permute-done.1 = bf16[1,256,256]{2,1,0:T(8,128)(2,1)S(1)} collective-permute-done((bf16[1,256,256]{2,1,0:T(8,128)(2,1)}, bf16[1,256,256]{2,1,0:T(8,128)(2,1)S(1)}, u32[]{:S(2)}, u32[]{:S(2)}) %collective-permute-start.1) | collective-permute-done | bytes 131104 | tf_op jit(solution)/shard_map/ppermute | solution.py:334
  33.8 1.3 collective-permute-start.6
  35.1 4.4 %collective-permute-done.2 = bf16[1,256,256]{2,1,0:T(8,128)(2,1)S(1)} collective-permute-done((bf16[1,256,256]{2,1,0:T(8,128)(2,1)}, bf16[1,256,256]{2,1,0:T(8,128)(2,1)S(1)}, u32[]{:S(2)}, u32[]{:S(2)}) %collective-permute-start.2) | collective-permute-done | bytes 131104 | tf_op jit(solution)/shard_map/ppermute | solution.py:334
  39.5 0.7 collective-permute-start.10
  40.2 1.9 %collective-permute-done.3 = bf16[1,256,256]{2,1,0:T(8,128)(2,1)S(1)} collective-permute-done((bf16[1,256,256]{2,1,0:T(8,128)(2,1)}, bf16[1,256,256]{2,1,0:T(8,128)(2,1)S(1)}, u32[]{:S(2)}, u32[]{:S(2)}) %collective-permute-start.3) | collective-permute-done | bytes 131104 | tf_op jit(solution)/shard_map/ppermute | solution.py:334
  42.1 0.7 collective-permute-start.11
  42.7 0.7 fusion
  45.5 0.7 collective-permute-start.12
  46.2 0.7 collective-permute-start.13
  46.9 0.7 collective-permute-start.14
  47.6 0.7 collective-permute-start.15
  48.3 0.7 collective-permute-start.9
  49.0 5.1 %collective-permute-start.8 = (bf16[1,256,256]{2,1,0:T(8,128)(2,1)S(1)}, bf16[1,256,256]{2,1,0:T(8,128)(2,1)S(1)}, u32[]{:S(2)}, u32[]{:S(2)}) collective-permute-start(bf16[1,256,256]{2,1,0:T(8,128)(2,1)S(1)} %select_select_fusion.1), channel_id=1, source_target_pairs={{0,16},{1,17},{2,18},{3,19},{4,20},{5,21},{6,22},{7,23},{8,24},{9,... | collective-permute-start | bytes 393224 | tf_op jit(solution)/shard_map/ppermute | solution.py:350
  54.3 1.3 collective-permute-start.16
  55.6 1.6 %copy-done.9 = f32[2,2048,128]{2,1,0:T(8,128)S(1)} copy-done((f32[2,2048,128]{2,1,0:T(8,128)S(1)}, f32[2,2048,128]{2,1,0:T(8,128)}, u32[]{:S(2)}) %copy-start.9) | copy-done | bytes 2097176
  57.2 6.7 %moved_keys.1.refs_5_ = f32[2,2048,128]{2,1,0:T(8,128)S(1)} custom-call(bf16[256,1024]{1,0:T(8,128)(2,1)S(1)} %copy-done.5, bf16[32,64,256]{2,1,0:T(8,128)(2,1)S(1)} %all-to-all-done.1.kv_ref, f32[2,2048,128]{2,1,0:T(8,128)S(1)} %copy-done.9), custom_call_target="tpu_custom_call" | custom-call | flops 6442450944 | bytes 1048576 | tf_op jit(solution)/shard_map/moved_keys/pallas_call | solution.py:490
  63.8 5.7 %collective-permute-done.16.refs_2_ = bf16[1,256,256]{2,1,0:T(8,128)(2,1)S(1)} collective-permute-done((bf16[1,256,256]{2,1,0:T(8,128)(2,1)S(1)}, bf16[1,256,256]{2,1,0:T(8,128)(2,1)S(1)}, u32[]{:S(2)}, u32[]{:S(2)}) %collective-permute-start.16) | collective-permute-done | bytes 131104 | tf_op jit(solution)/shard_map/ppermute | solution.py:352
  69.8 2.4 %collective-permute-start.21 = (bf16[2,256,256]{2,1,0:T(8,128)(2,1)S(1)}, bf16[2,256,256]{2,1,0:T(8,128)(2,1)S(1)}, u32[]{:S(2)}, u32[]{:S(2)}) collective-permute-start(bf16[2,256,256]{2,1,0:T(8,128)(2,1)S(1)} %maximum_select_fusion.refs_0_), channel_id=1, source_target_pairs={{0,4},{1,5},{2,6},{3,7},{4,0},{5,1},{6,2},{7,3},{8,12},{9,13},{10,... | collective-permute-start | bytes 786440 | tf_op jit(solution)/shard_map/ppermute | solution.py:380
  72.2 3.8 %collective-permute-done.17.refs_1_ = bf16[2,256,256]{2,1,0:T(8,128)(2,1)S(1)} collective-permute-done((bf16[2,256,256]{2,1,0:T(8,128)(2,1)S(1)}, bf16[2,256,256]{2,1,0:T(8,128)(2,1)S(1)}, u32[]{:S(2)}, u32[]{:S(2)}) %collective-permute-start.17) | collective-permute-done | bytes 262176 | tf_op jit(solution)/shard_map/ppermute | solution.py:380
  76.2 0.6 collective-permute-done.21.refs_2_
  76.8 0.6 pick_other.3
  77.4 8.2 %all-to-all-start = ((bf16[32,64,256]{2,1,0:T(8,128)(2,1)}), bf16[32,64,256]{2,1,0:T(8,128)(2,1)S(1)}, u32[]{:S(2)}, u32[]{:S(2)}) async-start(bf16[32,64,256]{2,1,0:T(8,128)(2,1)} %gate.1), calls=%async_computation | async-start | bytes 2097152 | tf_op jit(solution)/shard_map/all_to_all | solution.py:366
  85.7 1.7 %collective-permute-start.18 = (bf16[2,256,256]{2,1,0:T(8,128)(2,1)S(1)}, bf16[2,256,256]{2,1,0:T(8,128)(2,1)S(1)}, u32[]{:S(2)}, u32[]{:S(2)}) collective-permute-start(bf16[2,256,256]{2,1,0:T(8,128)(2,1)S(1)} %collective-permute-done.17.refs_1_), channel_id=1, source_target_pairs={{0,4},{1,5},{2,6},{3,7},{4,0},{5,1},{6,2},{7,3},{8,12},{9,13},{10,... | collective-permute-start | bytes 786440 | tf_op jit(solution)/shard_map/ppermute | solution.py:380
  87.3 1.5 %collective-permute-start.20 = (bf16[2,256,256]{2,1,0:T(8,128)(2,1)S(1)}, bf16[2,256,256]{2,1,0:T(8,128)(2,1)S(1)}, u32[]{:S(2)}, u32[]{:S(2)}) collective-permute-start(bf16[2,256,256]{2,1,0:T(8,128)(2,1)S(1)} %collective-permute-done.19.refs_3_), channel_id=1, source_target_pairs={{0,2},{1,3},{2,0},{3,1},{4,6},{5,7},{6,4},{7,5},{8,10},{9,11},{10,... | collective-permute-start | bytes 786440 | tf_op jit(solution)/shard_map/ppermute | solution.py:380
  88.8 1.5 %collective-permute-start.22 = (bf16[2,256,256]{2,1,0:T(8,128)(2,1)S(1)}, bf16[2,256,256]{2,1,0:T(8,128)(2,1)S(1)}, u32[]{:S(2)}, u32[]{:S(2)}) collective-permute-start(bf16[2,256,256]{2,1,0:T(8,128)(2,1)S(1)} %collective-permute-done.21.refs_2_), channel_id=1, source_target_pairs={{0,8},{1,9},{2,10},{3,11},{4,12},{5,13},{6,14},{7,15},{8,0},{9,1},... | collective-permute-start | bytes 786440 | tf_op jit(solution)/shard_map/ppermute | solution.py:380
  90.3 1.6 %copy-done.13 = f32[2,2048,128]{2,1,0:T(8,128)S(1)} copy-done((f32[2,2048,128]{2,1,0:T(8,128)S(1)}, f32[2,2048,128]{2,1,0:T(8,128)}, u32[]{:S(2)}) %copy-start.13) | copy-done | bytes 2097176
  91.9 8.0 %prefix_keys.2.refs_4_ = f32[2,2048,128]{2,1,0:T(8,128)S(1)} custom-call(s32[2]{0:T(128)S(1)} %copy-done.3, s32[32]{0:T(128)S(1)} %copy-done.4, s32[1]{0:T(128)} %bitcast.me_ref, bf16[256,1024]{1,0:T(8,128)(2,1)S(1)} %copy-done.5, bf16[2,256,256]{2,1,0:T(8,128)(2,1)S(1)} %maximum_select_fusion.refs_0_, ...), custom_call_target="tpu_custom_call" | custom-call | flops 6442450944 | bytes 1048576 | tf_op jit(solution)/shard_map/prefix_keys/pallas_call | solution.py:519
  99.9 3.0 %collective-permute-done.18.refs_0_ = bf16[2,256,256]{2,1,0:T(8,128)(2,1)S(1)} collective-permute-done((bf16[2,256,256]{2,1,0:T(8,128)(2,1)S(1)}, bf16[2,256,256]{2,1,0:T(8,128)(2,1)S(1)}, u32[]{:S(2)}, u32[]{:S(2)}) %collective-permute-start.18) | collective-permute-done | bytes 262176 | tf_op jit(solution)/shard_map/ppermute | solution.py:380
  102.8 1.0 collective-permute-done.20.refs_1_
  103.8 5.6 %collective-permute-done.22.refs_2_ = bf16[2,256,256]{2,1,0:T(8,128)(2,1)S(1)} collective-permute-done((bf16[2,256,256]{2,1,0:T(8,128)(2,1)S(1)}, bf16[2,256,256]{2,1,0:T(8,128)(2,1)S(1)}, u32[]{:S(2)}, u32[]{:S(2)}) %collective-permute-start.22) | collective-permute-done | bytes 262176 | tf_op jit(solution)/shard_map/ppermute | solution.py:380
  110.1 1.5 %collective-permute-start.24 = (bf16[2,256,256]{2,1,0:T(8,128)(2,1)S(1)}, bf16[2,256,256]{2,1,0:T(8,128)(2,1)S(1)}, u32[]{:S(2)}, u32[]{:S(2)}) collective-permute-start(bf16[2,256,256]{2,1,0:T(8,128)(2,1)S(1)} %collective-permute-done.22.refs_2_), channel_id=1, source_target_pairs={{0,2},{1,3},{2,0},{3,1},{4,6},{5,7},{6,4},{7,5},{8,10},{9,11},{10,... | collective-permute-start | bytes 786440 | tf_op jit(solution)/shard_map/ppermute | solution.py:380
  111.8 5.0 %prefix_keys.3.refs_2_ = f32[2,2048,128]{2,1,0:T(8,128)S(1)} custom-call(s32[2]{0:T(128)S(1)} %copy-done.3, s32[32]{0:T(128)S(1)} %copy-done.4, s32[1]{0:T(128)} %bitcast.me_ref, bf16[256,1024]{1,0:T(8,128)(2,1)S(1)} %copy-done.5, bf16[2,256,256]{2,1,0:T(8,128)(2,1)S(1)} %collective-permute-done.18.refs_0_, ...), custom_call_target="tpu_custom_call" | custom-call | flops 4831838208 | bytes 786432 | tf_op jit(solution)/shard_map/prefix_keys/pallas_call | solution.py:519
  116.8 1.3 %copy-done.10 = f32[2,2048,128]{2,1,0:T(8,128)} copy-done((f32[2,2048,128]{2,1,0:T(8,128)}, f32[2,2048,128]{2,1,0:T(8,128)S(1)}, u32[]{:S(2)}) %copy-start.10) | copy-done | bytes 2097176
  118.2 0.7 collective-permute-done.24.refs_0_
  119.5 1.3 %collective-permute-done.26.refs_1_ = bf16[256,256]{1,0:T(8,128)(2,1)S(1)} collective-permute-done((bf16[256,256]{1,0:T(8,128)(2,1)S(1)}, bf16[256,256]{1,0:T(8,128)(2,1)S(1)}, u32[]{:S(2)}, u32[]{:S(2)}) %collective-permute-start.26) | collective-permute-done | bytes 131104 | tf_op jit(solution)/shard_map/ppermute | solution.py:370
  120.8 1.6 %copy-done.11 = f32[2,2048,128]{2,1,0:T(8,128)S(1)} copy-done((f32[2,2048,128]{2,1,0:T(8,128)S(1)}, f32[2,2048,128]{2,1,0:T(8,128)}, u32[]{:S(2)}) %copy-start.11) | copy-done | bytes 2097176
  122.4 9.7 %last_keys.1 = bf16[256,1024]{1,0:T(8,128)(2,1)} custom-call(s32[2]{0:T(128)S(1)} %copy-done.3, s32[32]{0:T(128)S(1)} %copy-done.4, s32[1]{0:T(128)} %bitcast.me_ref, bf16[256,1024]{1,0:T(8,128)(2,1)S(1)} %copy-done.5, bf16[32,64,256]{2,1,0:T(8,128)(2,1)S(1)} %all-to-all-done.kv_ref, bf16[2,256,256]{2,1,0:T(8,128)(2,1)S(1)} %collective-permute-done.24.refs_0_, ...), custom_call_target="tpu_custom_call" | custom-call | flops 8053063680 | bytes 1310720 | tf_op jit(solution)/shard_map/last_keys/pallas_call | solution.py:545
  (60 shorter events, 3.4 us)
Async XLA Ops:
  0.0 5.2 %collective-permute-start = (bf16[4096,256]{1,0:T(8,128)(2,1)}, bf16[4096,256]{1,0:T(8,128)(2,1)}, u32[]{:S(2)}, u32[]{:S(2)}) collective-permute-start(bf16[4096,256]{1,0:T(8,128)(2,1)} %param.15), channel_id=1, source_target_pairs={{0,1},{1,0},{2,3},{3,2},{4,5},{5,4},{6,7},{7,6},{8,9},{9,8},{10,11... | collective-permute-start | bytes 6291464 | tf_op jit(solution)/shard_map/ppermute | solution.py:370
  1.1 11.7 %copy-start.2 = (s32[2]{0:T(128)S(1)}, s32[2]{0:T(128)}, u32[]{:S(2)}) copy-start(s32[2]{0:T(128)} %owner_ref.13) | copy-start | bytes 28
  5.2 50.4 %all-to-all-start.1 = ((bf16[32,64,256]{2,1,0:T(8,128)(2,1)}), bf16[32,64,256]{2,1,0:T(8,128)(2,1)S(1)}, u32[]{:S(2)}, u32[]{:S(2)}) async-start(bf16[32,64,256]{2,1,0:T(8,128)(2,1)} %get-tuple-element.74), calls=%async_computation.1 | async-start | bytes 2097152 | tf_op jit(solution)/shard_map/all_to_all | solution.py:366
  13.4 10.7 %copy-start.5 = (bf16[256,1024]{1,0:T(8,128)(2,1)S(1)}, bf16[256,1024]{1,0:T(8,128)(2,1)}, u32[]{:S(2)}) copy-start(bf16[256,1024]{1,0:T(8,128)(2,1)} %q_ref.9) | copy-start | bytes 1572868
  13.4 10.7 %copy-start.6 = (bf16[512,256]{1,0:T(8,128)(2,1)S(1)}, bf16[512,256]{1,0:T(8,128)(2,1)}, u32[]{:S(2)}) copy-start(bf16[512,256]{1,0:T(8,128)(2,1)} %own_ref.1) | copy-start | bytes 786436
  13.4 10.7 %copy-start.7 = (bf16[256,256]{1,0:T(8,128)(2,1)S(1)}, bf16[256,256]{1,0:T(8,128)(2,1)}, u32[]{:S(2)}) copy-start(bf16[256,256]{1,0:T(8,128)(2,1)} %suffix_ref.1) | copy-start | bytes 393220
  16.5 12.8 %collective-permute-start.7 = (bf16[1,256,256]{2,1,0:T(8,128)(2,1)}, bf16[1,256,256]{2,1,0:T(8,128)(2,1)S(1)}, u32[]{:S(2)}, u32[]{:S(2)}) collective-permute-start(bf16[1,256,256]{2,1,0:T(8,128)(2,1)} %get-tuple-element.55), channel_id=1, source_target_pairs={{0,2},{1,3},{2,0},{3,1},{4,6},{5,7},{6,4},{7,5},{8,10},{9,11},{10,... | collective-permute-start | bytes 393224 | tf_op jit(solution)/shard_map/ppermute | solution.py:334
  18.3 15.5 %collective-permute-start.1 = (bf16[1,256,256]{2,1,0:T(8,128)(2,1)}, bf16[1,256,256]{2,1,0:T(8,128)(2,1)S(1)}, u32[]{:S(2)}, u32[]{:S(2)}) collective-permute-start(bf16[1,256,256]{2,1,0:T(8,128)(2,1)} %get-tuple-element.49), channel_id=1, source_target_pairs={{0,14},{1,15},{2,12},{3,13},{4,10},{5,11},{6,8},{7,9},{8,6},{9,7},... | collective-permute-start | bytes 393224 | tf_op jit(solution)/shard_map/ppermute | solution.py:334
  20.7 18.8 %collective-permute-start.2 = (bf16[1,256,256]{2,1,0:T(8,128)(2,1)}, bf16[1,256,256]{2,1,0:T(8,128)(2,1)S(1)}, u32[]{:S(2)}, u32[]{:S(2)}) collective-permute-start(bf16[1,256,256]{2,1,0:T(8,128)(2,1)} %get-tuple-element.50), channel_id=1, source_target_pairs={{0,12},{1,13},{2,14},{3,15},{4,8},{5,9},{6,10},{7,11},{8,4},{9,5},... | collective-permute-start | bytes 393224 | tf_op jit(solution)/shard_map/ppermute | solution.py:334
  20.9 21.1 %collective-permute-start.3 = (bf16[1,256,256]{2,1,0:T(8,128)(2,1)}, bf16[1,256,256]{2,1,0:T(8,128)(2,1)S(1)}, u32[]{:S(2)}, u32[]{:S(2)}) collective-permute-start(bf16[1,256,256]{2,1,0:T(8,128)(2,1)} %get-tuple-element.51), channel_id=1, source_target_pairs={{0,10},{1,11},{2,8},{3,9},{4,14},{5,15},{6,12},{7,13},{8,2},{9,3},... | collective-permute-start | bytes 393224 | tf_op jit(solution)/shard_map/ppermute | solution.py:334
  23.6 21.9 %collective-permute-start.4 = (bf16[1,256,256]{2,1,0:T(8,128)(2,1)}, bf16[1,256,256]{2,1,0:T(8,128)(2,1)S(1)}, u32[]{:S(2)}, u32[]{:S(2)}) collective-permute-start(bf16[1,256,256]{2,1,0:T(8,128)(2,1)} %get-tuple-element.52), channel_id=1, source_target_pairs={{0,8},{1,9},{2,10},{3,11},{4,12},{5,13},{6,14},{7,15},{8,0},{9,1},... | collective-permute-start | bytes 393224 | tf_op jit(solution)/shard_map/ppermute | solution.py:334
  24.2 0.9 copy-start
  25.1 17.0 %copy-start.15 = (bf16[1,256,256]{2,1,0:T(8,128)(2,1)S(1)}, bf16[1,256,256]{2,1,0:T(8,128)(2,1)}, u32[]{:S(2)}) copy-start(bf16[1,256,256]{2,1,0:T(8,128)(2,1)} %get-tuple-element.68) | copy-start | bytes 393220
  25.1 17.7 %copy-start.3 = (s32[2]{0:T(128)S(1)}, s32[2]{0:T(128)}, u32[]{:S(2)}) copy-start(s32[2]{0:T(128)} %owner_ref.13) | copy-start | bytes 28
  25.1 23.9 %copy-start.1 = (bf16[1,256,256]{2,1,0:T(8,128)(2,1)S(1)}, bf16[1,256,256]{2,1,0:T(8,128)(2,1)}, u32[]{:S(2)}) copy-start(bf16[1,256,256]{2,1,0:T(8,128)(2,1)} %get-tuple-element.56.after_ref) | copy-start | bytes 393220
  25.1 29.1 %copy-start.14 = (bf16[1,256,256]{2,1,0:T(8,128)(2,1)S(1)}, bf16[1,256,256]{2,1,0:T(8,128)(2,1)}, u32[]{:S(2)}) copy-start(bf16[1,256,256]{2,1,0:T(8,128)(2,1)} %get-tuple-element.73) | copy-start | bytes 393220
  27.9 1.3 %copy-start.8 = (f32[2,2048,128]{2,1,0:T(8,128)}, f32[2,2048,128]{2,1,0:T(8,128)S(1)}, u32[]{:S(2)}) copy-start(f32[2,2048,128]{2,1,0:T(8,128)S(1)} %local_keys.1.loaded_ref) | copy-start | bytes 6291460
  29.3 16.9 %collective-permute-start.5 = (bf16[1,256,256]{2,1,0:T(8,128)(2,1)}, bf16[1,256,256]{2,1,0:T(8,128)(2,1)S(1)}, u32[]{:S(2)}, u32[]{:S(2)}) collective-permute-start(bf16[1,256,256]{2,1,0:T(8,128)(2,1)} %get-tuple-element.53), channel_id=1, source_target_pairs={{0,6},{1,7},{2,4},{3,5},{4,2},{5,3},{6,0},{7,1},{8,14},{9,15},{10,... | collective-permute-start | bytes 393224 | tf_op jit(solution)/shard_map/ppermute | solution.py:334
  33.8 13.0 %collective-permute-start.6 = (bf16[1,256,256]{2,1,0:T(8,128)(2,1)}, bf16[1,256,256]{2,1,0:T(8,128)(2,1)S(1)}, u32[]{:S(2)}, u32[]{:S(2)}) collective-permute-start(bf16[1,256,256]{2,1,0:T(8,128)(2,1)} %get-tuple-element.54), channel_id=1, source_target_pairs={{0,4},{1,5},{2,6},{3,7},{4,0},{5,1},{6,2},{7,3},{8,12},{9,13},{10,... | collective-permute-start | bytes 393224 | tf_op jit(solution)/shard_map/ppermute | solution.py:334
  39.5 8.0 %collective-permute-start.10 = (bf16[1,256,256]{2,1,0:T(8,128)(2,1)}, bf16[1,256,256]{2,1,0:T(8,128)(2,1)S(1)}, u32[]{:S(2)}, u32[]{:S(2)}) collective-permute-start(bf16[1,256,256]{2,1,0:T(8,128)(2,1)} %get-tuple-element.67), channel_id=1, source_target_pairs={{30,18},{31,19}} | collective-permute-start | bytes 393224 | tf_op jit(solution)/shard_map/ppermute | solution.py:334
  42.1 6.2 %collective-permute-start.11 = (bf16[1,256,256]{2,1,0:T(8,128)(2,1)S(1)}, bf16[1,256,256]{2,1,0:T(8,128)(2,1)S(1)}, u32[]{:S(2)}, u32[]{:S(2)}) collective-permute-start(bf16[1,256,256]{2,1,0:T(8,128)(2,1)S(1)} %copy-done.15), channel_id=1, source_target_pairs={{30,20},{31,21}} | collective-permute-start | bytes 393224 | tf_op jit(solution)/shard_map/ppermute | solution.py:334
  45.5 3.5 %collective-permute-start.12 = (bf16[1,256,256]{2,1,0:T(8,128)(2,1)}, bf16[1,256,256]{2,1,0:T(8,128)(2,1)S(1)}, u32[]{:S(2)}, u32[]{:S(2)}) collective-permute-start(bf16[1,256,256]{2,1,0:T(8,128)(2,1)} %get-tuple-element.69), channel_id=1, source_target_pairs={{30,22},{31,23}} | collective-permute-start | bytes 393224 | tf_op jit(solution)/shard_map/ppermute | solution.py:334
  46.2 7.9 %collective-permute-start.13 = (bf16[1,256,256]{2,1,0:T(8,128)(2,1)}, bf16[1,256,256]{2,1,0:T(8,128)(2,1)S(1)}, u32[]{:S(2)}, u32[]{:S(2)}) collective-permute-start(bf16[1,256,256]{2,1,0:T(8,128)(2,1)} %get-tuple-element.70), channel_id=1, source_target_pairs={{30,24},{31,25}} | collective-permute-start | bytes 393224 | tf_op jit(solution)/shard_map/ppermute | solution.py:334
  46.9 7.3 %collective-permute-start.14 = (bf16[1,256,256]{2,1,0:T(8,128)(2,1)}, bf16[1,256,256]{2,1,0:T(8,128)(2,1)S(1)}, u32[]{:S(2)}, u32[]{:S(2)}) collective-permute-start(bf16[1,256,256]{2,1,0:T(8,128)(2,1)} %get-tuple-element.71), channel_id=1, source_target_pairs={{30,26},{31,27}} | collective-permute-start | bytes 393224 | tf_op jit(solution)/shard_map/ppermute | solution.py:334
  47.6 6.6 %collective-permute-start.15 = (bf16[1,256,256]{2,1,0:T(8,128)(2,1)}, bf16[1,256,256]{2,1,0:T(8,128)(2,1)S(1)}, u32[]{:S(2)}, u32[]{:S(2)}) collective-permute-start(bf16[1,256,256]{2,1,0:T(8,128)(2,1)} %get-tuple-element.72), channel_id=1, source_target_pairs={{30,28},{31,29}} | collective-permute-start | bytes 393224 | tf_op jit(solution)/shard_map/ppermute | solution.py:334
  48.3 5.9 %collective-permute-start.9 = (bf16[1,256,256]{2,1,0:T(8,128)(2,1)}, bf16[1,256,256]{2,1,0:T(8,128)(2,1)S(1)}, u32[]{:S(2)}, u32[]{:S(2)}) collective-permute-start(bf16[1,256,256]{2,1,0:T(8,128)(2,1)} %get-tuple-element.66), channel_id=1, source_target_pairs={{30,16},{31,17}} | collective-permute-start | bytes 393224 | tf_op jit(solution)/shard_map/ppermute | solution.py:334
  49.0 14.8 %collective-permute-start.8 = (bf16[1,256,256]{2,1,0:T(8,128)(2,1)S(1)}, bf16[1,256,256]{2,1,0:T(8,128)(2,1)S(1)}, u32[]{:S(2)}, u32[]{:S(2)}) collective-permute-start(bf16[1,256,256]{2,1,0:T(8,128)(2,1)S(1)} %select_select_fusion.1), channel_id=1, source_target_pairs={{0,16},{1,17},{2,18},{3,19},{4,20},{5,21},{6,22},{7,23},{8,24},{9,... | collective-permute-start | bytes 393224 | tf_op jit(solution)/shard_map/ppermute | solution.py:350
  54.2 22.5 %copy-start.4 = (s32[32]{0:T(128)S(1)}, s32[32]{0:T(128)}, u32[]{:S(2)}) copy-start(s32[32]{0:T(128)} %reader_ref.11) | copy-start | bytes 388
  54.3 15.3 %collective-permute-start.16 = (bf16[1,256,256]{2,1,0:T(8,128)(2,1)S(1)}, bf16[1,256,256]{2,1,0:T(8,128)(2,1)S(1)}, u32[]{:S(2)}, u32[]{:S(2)}) collective-permute-start(bf16[1,256,256]{2,1,0:T(8,128)(2,1)S(1)} %select_select_fusion), channel_id=1, source_target_pairs={{16,0},{17,1},{18,2},{19,3},{20,4},{21,5},{22,6},{23,7},{24,8},{25... | collective-permute-start | bytes 393224 | tf_op jit(solution)/shard_map/ppermute | solution.py:352
  55.6 1.6 %copy-start.9 = (f32[2,2048,128]{2,1,0:T(8,128)S(1)}, f32[2,2048,128]{2,1,0:T(8,128)}, u32[]{:S(2)}) copy-start(f32[2,2048,128]{2,1,0:T(8,128)} %copy-done.8) | copy-start | bytes 6291460
  63.8 13.6 %copy-start.12 = (f32[2,2048,128]{2,1,0:T(8,128)}, f32[2,2048,128]{2,1,0:T(8,128)S(1)}, u32[]{:S(2)}) copy-start(f32[2,2048,128]{2,1,0:T(8,128)S(1)} %moved_keys.1.refs_5_) | copy-start | bytes 6291460
  69.6 6.4 %collective-permute-start.17 = (bf16[2,256,256]{2,1,0:T(8,128)(2,1)S(1)}, bf16[2,256,256]{2,1,0:T(8,128)(2,1)S(1)}, u32[]{:S(2)}, u32[]{:S(2)}) collective-permute-start(bf16[2,256,256]{2,1,0:T(8,128)(2,1)S(1)} %maximum_select_fusion.refs_0_), channel_id=1, source_target_pairs={{0,2},{1,3},{2,0},{3,1},{4,6},{5,7},{6,4},{7,5},{8,10},{9,11},{10,... | collective-permute-start | bytes 786440 | tf_op jit(solution)/shard_map/ppermute | solution.py:380
  69.7 6.4 %collective-permute-start.19 = (bf16[2,256,256]{2,1,0:T(8,128)(2,1)S(1)}, bf16[2,256,256]{2,1,0:T(8,128)(2,1)S(1)}, u32[]{:S(2)}, u32[]{:S(2)}) collective-permute-start(bf16[2,256,256]{2,1,0:T(8,128)(2,1)S(1)} %maximum_select_fusion.refs_0_), channel_id=1, source_target_pairs={{0,8},{1,9},{2,10},{3,11},{4,12},{5,13},{6,14},{7,15},{8,0},{9,1},... | collective-permute-start | bytes 786440 | tf_op jit(solution)/shard_map/ppermute | solution.py:380
  69.8 7.0 %collective-permute-start.21 = (bf16[2,256,256]{2,1,0:T(8,128)(2,1)S(1)}, bf16[2,256,256]{2,1,0:T(8,128)(2,1)S(1)}, u32[]{:S(2)}, u32[]{:S(2)}) collective-permute-start(bf16[2,256,256]{2,1,0:T(8,128)(2,1)S(1)} %maximum_select_fusion.refs_0_), channel_id=1, source_target_pairs={{0,4},{1,5},{2,6},{3,7},{4,0},{5,1},{6,2},{7,3},{8,12},{9,13},{10,... | collective-permute-start | bytes 786440 | tf_op jit(solution)/shard_map/ppermute | solution.py:380
  77.3 12.9 %collective-permute-start.23 = (bf16[1024,256]{1,0:T(8,128)(2,1)S(1)}, bf16[1024,256]{1,0:T(8,128)(2,1)}, u32[]{:S(2)}, u32[]{:S(2)}) collective-permute-start(bf16[1024,256]{1,0:T(8,128)(2,1)S(1)} %pick_other.3), channel_id=1, source_target_pairs={{0,1},{1,0},{2,3},{3,2},{4,5},{5,4},{6,7},{7,6},{8,9},{9,8},{10,11... | collective-permute-start | bytes 1572872 | tf_op jit(solution)/shard_map/ppermute | solution.py:370
  77.4 42.0 %all-to-all-start = ((bf16[32,64,256]{2,1,0:T(8,128)(2,1)}), bf16[32,64,256]{2,1,0:T(8,128)(2,1)S(1)}, u32[]{:S(2)}, u32[]{:S(2)}) async-start(bf16[32,64,256]{2,1,0:T(8,128)(2,1)} %gate.1), calls=%async_computation | async-start | bytes 2097152 | tf_op jit(solution)/shard_map/all_to_all | solution.py:366
  85.7 17.2 %collective-permute-start.18 = (bf16[2,256,256]{2,1,0:T(8,128)(2,1)S(1)}, bf16[2,256,256]{2,1,0:T(8,128)(2,1)S(1)}, u32[]{:S(2)}, u32[]{:S(2)}) collective-permute-start(bf16[2,256,256]{2,1,0:T(8,128)(2,1)S(1)} %collective-permute-done.17.refs_1_), channel_id=1, source_target_pairs={{0,4},{1,5},{2,6},{3,7},{4,0},{5,1},{6,2},{7,3},{8,12},{9,13},{10,... | collective-permute-start | bytes 786440 | tf_op jit(solution)/shard_map/ppermute | solution.py:380
  87.3 16.5 %collective-permute-start.20 = (bf16[2,256,256]{2,1,0:T(8,128)(2,1)S(1)}, bf16[2,256,256]{2,1,0:T(8,128)(2,1)S(1)}, u32[]{:S(2)}, u32[]{:S(2)}) collective-permute-start(bf16[2,256,256]{2,1,0:T(8,128)(2,1)S(1)} %collective-permute-done.19.refs_3_), channel_id=1, source_target_pairs={{0,2},{1,3},{2,0},{3,1},{4,6},{5,7},{6,4},{7,5},{8,10},{9,11},{10,... | collective-permute-start | bytes 786440 | tf_op jit(solution)/shard_map/ppermute | solution.py:380
  88.8 20.6 %collective-permute-start.22 = (bf16[2,256,256]{2,1,0:T(8,128)(2,1)S(1)}, bf16[2,256,256]{2,1,0:T(8,128)(2,1)S(1)}, u32[]{:S(2)}, u32[]{:S(2)}) collective-permute-start(bf16[2,256,256]{2,1,0:T(8,128)(2,1)S(1)} %collective-permute-done.21.refs_2_), channel_id=1, source_target_pairs={{0,8},{1,9},{2,10},{3,11},{4,12},{5,13},{6,14},{7,15},{8,0},{9,1},... | collective-permute-start | bytes 786440 | tf_op jit(solution)/shard_map/ppermute | solution.py:380
  90.3 1.6 %copy-start.13 = (f32[2,2048,128]{2,1,0:T(8,128)S(1)}, f32[2,2048,128]{2,1,0:T(8,128)}, u32[]{:S(2)}) copy-start(f32[2,2048,128]{2,1,0:T(8,128)} %copy-done.12) | copy-start | bytes 6291460
  110.0 1.8 %collective-permute-start.25 = (bf16[768,256]{1,0:T(8,128)(2,1)S(1)}, bf16[768,256]{1,0:T(8,128)(2,1)S(1)}, u32[]{:S(2)}, u32[]{:S(2)}) collective-permute-start(bf16[768,256]{1,0:T(8,128)(2,1)S(1)} %pick_other.4), channel_id=1, source_target_pairs={{0,1},{1,0},{2,3},{3,2},{4,5},{5,4},{6,7},{7,6},{8,9},{9,8},{10,11... | collective-permute-start | bytes 1179656 | tf_op jit(solution)/shard_map/ppermute | solution.py:370
  110.1 8.7 %collective-permute-start.24 = (bf16[2,256,256]{2,1,0:T(8,128)(2,1)S(1)}, bf16[2,256,256]{2,1,0:T(8,128)(2,1)S(1)}, u32[]{:S(2)}, u32[]{:S(2)}) collective-permute-start(bf16[2,256,256]{2,1,0:T(8,128)(2,1)S(1)} %collective-permute-done.22.refs_2_), channel_id=1, source_target_pairs={{0,2},{1,3},{2,0},{3,1},{4,6},{5,7},{6,4},{7,5},{8,10},{9,11},{10,... | collective-permute-start | bytes 786440 | tf_op jit(solution)/shard_map/ppermute | solution.py:380
  116.8 1.3 %copy-start.10 = (f32[2,2048,128]{2,1,0:T(8,128)}, f32[2,2048,128]{2,1,0:T(8,128)S(1)}, u32[]{:S(2)}) copy-start(f32[2,2048,128]{2,1,0:T(8,128)S(1)} %prefix_keys.3.refs_2_) | copy-start | bytes 6291460
  119.4 1.4 %collective-permute-start.26 = (bf16[256,256]{1,0:T(8,128)(2,1)S(1)}, bf16[256,256]{1,0:T(8,128)(2,1)S(1)}, u32[]{:S(2)}, u32[]{:S(2)}) collective-permute-start(bf16[256,256]{1,0:T(8,128)(2,1)S(1)} %pick_other.5), channel_id=1, source_target_pairs={{0,1},{1,0},{2,3},{3,2},{4,5},{5,4},{6,7},{7,6},{8,9},{9,8},{10,11... | collective-permute-start | bytes 393224 | tf_op jit(solution)/shard_map/ppermute | solution.py:370
  120.8 1.6 %copy-start.11 = (f32[2,2048,128]{2,1,0:T(8,128)S(1)}, f32[2,2048,128]{2,1,0:T(8,128)}, u32[]{:S(2)}) copy-start(f32[2,2048,128]{2,1,0:T(8,128)} %copy-done.10) | copy-start | bytes 6291460
